TPU v7x, 32 devices: a whole 2x2x4 slice. The times are simulated.
32 devices in a mesh: section: 4 (over y, x), depth: 8 (over z, core).
Axes of the slice: x: 2, y: 2, z: 4, core: 2. Of those that a mesh axis runs over, the one named last changes fastest.
Arguments:
- resident: bfloat16 [4, 2, 32, 16, 8, 256], P('section', None, 'depth'), may hold values from -6 to 6
- previous: bfloat16 [4, 2, 32, 16, 8, 256], P('section', None, 'depth'), may hold values from -6 to 6
- incoming: bfloat16 [3, 2, 32, 16, 8, 256], P(None, None, 'depth'), may hold values from -6 to 6
- first_weights: bfloat16 [4, 3, 3, 3, 256, 256], P('section'), may hold values from -0.078125 to 0.078125
- second_weights: bfloat16 [4, 3, 3, 3, 256, 256], P('section'), may hold values from -0.078125 to 0.078125
Outputs:
- emitted: bfloat16 [4, 2, 32, 16, 8, 256], P('section', None, 'depth')
All inputs are finite; a program needn't handle non-finite values.
Results may differ from a plain program's by a relative error of at most 0.014.
Values may be sent and summed in bfloat16 or wider, within the bound.
No kernel may reach another device: no remote copies, remote signals or barrier semaphores. Data moves between devices by JAX's collectives and lax.ppermute only.
A program may use at most 64 MiB of HBM per device.

v0:
```python
import functools

import jax
import jax.numpy as jnp
from jax import lax
from jax.experimental import pallas as pl
from jax.experimental.pallas import tpu as pltpu
from jax.sharding import PartitionSpec as P

EPS = 1e-05
VMEM_LIMIT = 48 * 1024 * 1024


def act(values):
    values = values.astype(jnp.float32)
    scaled = values * lax.rsqrt(jnp.mean(values * values, axis=-1, keepdims=True) + EPS)
    return scaled / (1.0 + jnp.exp(-scaled))


def fill(even, odd, at, values, width):
    planes, voxels, chans = values.shape
    rows = voxels // width
    field = act(values).reshape(planes * rows, width, chans)
    column = lax.broadcasted_iota(jnp.int32, field.shape, 1)
    shifted = (
        jnp.where(column == 0, 0.0, pltpu.roll(field, 1, 1)),
        field,
        jnp.where(column == width - 1, 0.0, pltpu.roll(field, width - 1, 1)),
    )
    edge = jnp.zeros((planes, width, chans), jnp.float32)
    for k, part in enumerate(shifted):
        part = part.reshape(planes, voxels, chans)
        columns = pl.ds(k * chans, chans)
        even[pl.ds(at, planes), :, columns] = part.astype(jnp.bfloat16)
        odd[pl.ds(at, planes), :, columns] = jnp.concatenate([edge, part, edge], axis=1).astype(jnp.bfloat16)


def convolve(even, odd, weights, copies, planes, width):
    voxels = even.shape[1]
    total = None
    for i in range(3):
        copies[i].wait()
        taps = [odd[i : i + planes, 0:voxels], even[i : i + planes], odd[i : i + planes, 2 * width : 2 * width + voxels]]
        slab = jnp.concatenate(taps, axis=-1)
        part = jnp.dot(
            slab.reshape(planes * voxels, slab.shape[-1]), weights[i], preferred_element_type=jnp.float32
        )
        total = part if total is None else total + part
    return total.reshape(planes, voxels, -1)


def fetch(weights_hbm, weights, sems):
    copies = [pltpu.make_async_copy(weights_hbm.at[i], weights.at[i], sems.at[i]) for i in range(3)]
    for copy in copies:
        copy.start()
    return copies


def first_kernel(width, flags, q_low, q_mid, q_high, p_low, p_mid, p_high, weights_hbm, low, mid, high, even, odd, weights, sems):
    copies = fetch(weights_hbm, weights, sems)
    planes = q_mid.shape[0]
    fill(even, odd, 0, q_low[...], width)
    fill(even, odd, 2, q_mid[...], width)
    fill(even, odd, 2 + planes, q_high[...], width)
    total = convolve(even, odd, weights, copies, planes + 2, width)
    low[...] = jnp.where(flags[0] > 0, p_low[...].astype(jnp.float32) + total[:1], 0.0).astype(low.dtype)
    mid[...] = (p_mid[...].astype(jnp.float32) + total[1:-1]).astype(mid.dtype)
    high[...] = jnp.where(flags[1] > 0, p_high[...].astype(jnp.float32) + total[-1:], 0.0).astype(high.dtype)


def second_kernel(width, first_low, first_mid, first_high, q_mid, weights_hbm, out, even, odd, weights, sems):
    copies = fetch(weights_hbm, weights, sems)
    planes = q_mid.shape[0]
    fill(even, odd, 0, first_low[...], width)
    fill(even, odd, 1, first_mid[...], width)
    fill(even, odd, 1 + planes, first_high[...], width)
    total = convolve(even, odd, weights, copies, planes, width)
    out[...] = (q_mid[...].astype(jnp.float32) + total).astype(out.dtype)


def scratch(planes, voxels, chans, width):
    return [
        pltpu.VMEM((planes, voxels, 3 * chans), jnp.bfloat16),
        pltpu.VMEM((planes, voxels + 2 * width, 3 * chans), jnp.bfloat16),
        pltpu.VMEM((3, 9 * chans, chans), jnp.bfloat16),
        pltpu.SemaphoreType.DMA((3,)),
    ]


VMEM = pl.BlockSpec(memory_space=pltpu.VMEM)
SMEM = pl.BlockSpec(memory_space=pltpu.SMEM)
ANY = pl.BlockSpec(memory_space=pl.ANY)


def first_half(flags, q, q_halo, p, p_halo, weights, width):
    planes, voxels, chans = q.shape
    shape = lambda n: jax.ShapeDtypeStruct((n, voxels, chans), jnp.bfloat16)
    return pl.pallas_call(
        functools.partial(first_kernel, width),
        out_shape=(shape(1), shape(planes), shape(1)),
        in_specs=[SMEM] + [VMEM] * 6 + [ANY],
        out_specs=(VMEM, VMEM, VMEM),
        scratch_shapes=scratch(planes + 4, voxels, chans, width),
        compiler_params=pltpu.CompilerParams(vmem_limit_bytes=VMEM_LIMIT),
        cost_estimate=pl.CostEstimate(
            flops=(planes + 2) * voxels * 54 * chans * chans, bytes_accessed=8 * weights.size // 3, transcendentals=0
        ),
    )(flags, q_halo[0], q, q_halo[1], p_halo[0], p, p_halo[1], weights)


def second_half(first, q, weights, width):
    planes, voxels, chans = q.shape
    return pl.pallas_call(
        functools.partial(second_kernel, width),
        out_shape=jax.ShapeDtypeStruct(q.shape, jnp.bfloat16),
        in_specs=[VMEM] * 4 + [ANY],
        out_specs=VMEM,
        scratch_shapes=scratch(planes + 2, voxels, chans, width),
        compiler_params=pltpu.CompilerParams(vmem_limit_bytes=VMEM_LIMIT),
        cost_estimate=pl.CostEstimate(
            flops=planes * voxels * 54 * chans * chans, bytes_accessed=8 * weights.size // 3, transcendentals=0
        ),
    )(*first, q, weights)


def halo(block, width):
    count = lax.axis_size("depth")
    upward = [(i, i + 1) for i in range(count - 1)]
    downward = [(i + 1, i) for i in range(count - 1)]
    low = lax.ppermute(block[-width:], "depth", upward)
    high = lax.ppermute(block[:width], "depth", downward)
    return low, high


def local(resident, previous, incoming, first_weights, second_weights):
    section = lax.axis_index("section")
    sections = lax.axis_size("section")
    half = sections // 2
    depth = lax.axis_index("depth")
    ticks = incoming.shape[0] + 1
    _, _, planes, rows, width, chans = resident.shape
    voxels = rows * width
    flat = lambda a: a.reshape(a.shape[0], 2, planes, voxels, chans)
    resident, previous, incoming = flat(resident)[0], flat(previous)[0], flat(incoming)
    w_one = first_weights.reshape(3, 9 * chans, chans)
    w_two = second_weights.reshape(3, 9 * chans, chans)
    flags = jnp.stack([depth > 0, depth < lax.axis_size("depth") - 1]).astype(jnp.int32)

    def send(block, pairs):
        return lax.ppermute(block, "section", pairs) if pairs else block

    mirrored = send(previous, [(j, sections - 1 - j) for j in range(half)])
    across = [(j, sections - 1 - j) for j in range(1, half - 1)]
    decoder = section >= half

    def join(held, skip):
        total = (held.astype(jnp.float32) + skip.astype(jnp.float32)).astype(jnp.bfloat16)
        return jnp.where(decoder, total, held)

    out = emitted = None
    newer, older, relayed, direct = {}, {}, {}, {}
    for slot in range(ticks + 1):
        inputs = []
        for stream in range(2):
            fresh = resident[stream] if slot == 0 else incoming[min(slot, ticks - 1) - 1, stream]
            if slot == 0:
                value = fresh
            elif slot == 1:
                value = jnp.where(section == 0, fresh, join(resident[stream], mirrored[stream]))
            else:
                held = jnp.where(section == 1, older[stream], newer[stream])
                skip = jnp.where(section == sections - 1, relayed[stream], newer[stream])
                if across:
                    skip = jnp.where((section > half) & (section < sections - 1), direct[stream], skip)
                value = jnp.where(section == 0, fresh, join(held, skip))
            inputs.append(value)
        p, q = inputs
        onward = []
        if slot < ticks:
            onward = [(0, 1)] if slot < ticks - 1 else []
            if slot > 0:
                onward += [(j, j + 1) for j in range(1, sections - 1)]
        received = {}
        relays = {}
        first = first_half(flags, q, halo(q, 2), p, halo(p, 1), w_one, width)
        if onward:
            received[0] = send(first[1], onward)
        second = second_half(first, q, w_two, width)
        if onward:
            received[1] = send(second, onward)
        if 0 < slot < ticks:
            relays = {k: send(newer[k], [(1, sections - 1)]) for k in range(2)}
        if across and 0 < slot < ticks:
            direct = {0: send(first[1], across), 1: send(second, across)}
        older, newer, relayed = newer, received, relays
        out = jnp.stack([first[1], second])
        if slot == ticks - 1:
            emitted = out
    result = jnp.where(section == 0, emitted, out)
    return result.reshape(1, 2, planes, rows, width, chans)


def solution(mesh):
    in_specs = (
        P("section", None, "depth", None, None, None),
        P("section", None, "depth", None, None, None),
        P(None, None, "depth", None, None, None),
        P("section", None, None, None, None, None),
        P("section", None, None, None, None, None),
    )
    out_specs = P("section", None, "depth", None, None, None)
    return jax.shard_map(local, mesh=mesh, in_specs=in_specs, out_specs=out_specs, check_vma=False)
```

profile of v0, /device:TPU:13, one launch (start us, length us, event | category | flops | bytes accessed | tf_op | source)
XLA Modules:
  0.0 189.7 jit_solution(7972093014983413845)
XLA Ops:
  0.9 2.6 %collective-permute-start.9 = (bf16[1,128,256]{2,1,0:T(8,128)(2,1)S(1)}, bf16[1,128,256]{2,1,0:T(8,128)(2,1)S(1)}, u32[]{:S(2)}, u32[]{:S(2)}) collective-permute-start(bf16[1,128,256]{2,1,0:T(8,128)(2,1)S(1)} %get-tuple-element.43), channel_id=1, source_target_pairs={{1,0},{2,1},{3,2},{4,3},{5,4},{6,5},{7,6},{9,8},{10,9},{11,10},{12... | collective-permute-start | bytes 196616 | tf_op jit(solution)/shard_map/ppermute | solution.py:131
  3.5 3.1 %collective-permute-start.8 = (bf16[1,128,256]{2,1,0:T(8,128)(2,1)S(1)}, bf16[1,128,256]{2,1,0:T(8,128)(2,1)S(1)}, u32[]{:S(2)}, u32[]{:S(2)}) collective-permute-start(bf16[1,128,256]{2,1,0:T(8,128)(2,1)S(1)} %get-tuple-element.44), channel_id=1, source_target_pairs={{0,1},{1,2},{2,3},{3,4},{4,5},{5,6},{6,7},{8,9},{9,10},{10,11},{11... | collective-permute-start | bytes 196616 | tf_op jit(solution)/shard_map/ppermute | solution.py:130
  7.6 1.9 %collective-permute-start.7 = (bf16[2,128,256]{2,1,0:T(8,128)(2,1)S(1)}, bf16[2,128,256]{2,1,0:T(8,128)(2,1)S(1)}, u32[]{:S(2)}, u32[]{:S(2)}) collective-permute-start(bf16[2,128,256]{2,1,0:T(8,128)(2,1)S(1)} %get-tuple-element.47), channel_id=1, source_target_pairs={{1,0},{2,1},{3,2},{4,3},{5,4},{6,5},{7,6},{9,8},{10,9},{11,10},{12... | collective-permute-start | bytes 393224 | tf_op jit(solution)/shard_map/ppermute | solution.py:131
  9.5 3.6 %collective-permute-start.6 = (bf16[2,128,256]{2,1,0:T(8,128)(2,1)S(1)}, bf16[2,128,256]{2,1,0:T(8,128)(2,1)S(1)}, u32[]{:S(2)}, u32[]{:S(2)}) collective-permute-start(bf16[2,128,256]{2,1,0:T(8,128)(2,1)S(1)} %get-tuple-element.48), channel_id=1, source_target_pairs={{0,1},{1,2},{2,3},{3,4},{4,5},{5,6},{6,7},{8,9},{9,10},{10,11},{11... | collective-permute-start | bytes 393224 | tf_op jit(solution)/shard_map/ppermute | solution.py:130
  15.7 2.0 %copy-done = bf16[1,3,3,3,256,256]{5,4,3,2,1,0:T(8,128)(2,1)S(1)} copy-done((bf16[1,3,3,3,256,256]{5,4,3,2,1,0:T(8,128)(2,1)S(1)}, bf16[1,3,3,3,256,256]{5,4,3,2,1,0:T(8,128)(2,1)}, u32[]{:S(2)}) %copy-start) | copy-done | bytes 3538968
  17.6 6.8 %shard_map.57 = (bf16[1,128,256]{2,1,0:T(8,128)(2,1)S(1)}, bf16[4,128,256]{2,1,0:T(8,128)(2,1)S(1)}, bf16[1,128,256]{2,1,0:T(8,128)(2,1)S(1)}) custom-call(s32[2]{0:T(128)S(1)} %add_convert_fusion.6.flags, bf16[2,128,256]{2,1,0:T(8,128)(2,1)S(1)} %collective-permute-done.6.q_low, bf16[4,128,256]{2,1,0:T(8,128)(2,1)S(1)} %get-tuple-element.46.q_mid, ...), custom_call_target="tpu_custom_call" | custom-call | flops 2717908992 | bytes 4718592 | tf_op jit(solution)/shard_map/pallas_call | solution.py:98
  24.5 1.4 collective-permute-start.14
  25.8 4.6 %shard_map.58 = bf16[4,128,256]{2,1,0:T(8,128)(2,1)S(1)} custom-call(bf16[1,128,256]{2,1,0:T(8,128)(2,1)S(1)} %get-tuple-element.23.first_low, bf16[4,128,256]{2,1,0:T(8,128)(2,1)S(1)} %get-tuple-element.24.first_mid, bf16[1,128,256]{2,1,0:T(8,128)(2,1)S(1)} %get-tuple-element.25.first_high, bf16[4,128,256]{2,1,0:T(8,128)(2,1)S(1)} %get-tuple-element.46.q_mid, ...), custom_call_target="tpu_custom_call" | custom-call | flops 1811939328 | bytes 4718592 | tf_op jit(solution)/shard_map/pallas_call | solution.py:113
  30.5 1.4 collective-permute-start.10
  33.1 2.6 %collective-permute-start.2 = (bf16[2,128,256]{2,1,0:T(8,128)(2,1)S(1)}, bf16[2,128,256]{2,1,0:T(8,128)(2,1)S(1)}, u32[]{:S(2)}, u32[]{:S(2)}) collective-permute-start(bf16[2,128,256]{2,1,0:T(8,128)(2,1)S(1)} %get-tuple-element.63), channel_id=1, source_target_pairs={{1,0},{2,1},{3,2},{4,3},{5,4},{6,5},{7,6},{9,8},{10,9},{11,10},{12... | collective-permute-start | bytes 393224 | tf_op jit(solution)/shard_map/ppermute | solution.py:131
  35.7 3.1 %collective-permute-start.1 = (bf16[2,128,256]{2,1,0:T(8,128)(2,1)S(1)}, bf16[2,128,256]{2,1,0:T(8,128)(2,1)S(1)}, u32[]{:S(2)}, u32[]{:S(2)}) collective-permute-start(bf16[2,128,256]{2,1,0:T(8,128)(2,1)S(1)} %get-tuple-element.64), channel_id=1, source_target_pairs={{0,1},{1,2},{2,3},{3,4},{4,5},{5,6},{6,7},{8,9},{9,10},{10,11},{11... | collective-permute-start | bytes 393224 | tf_op jit(solution)/shard_map/ppermute | solution.py:130
  38.9 1.9 %collective-permute-start.4 = (bf16[1,128,256]{2,1,0:T(8,128)(2,1)S(1)}, bf16[1,128,256]{2,1,0:T(8,128)(2,1)S(1)}, u32[]{:S(2)}, u32[]{:S(2)}) collective-permute-start(bf16[1,128,256]{2,1,0:T(8,128)(2,1)S(1)} %get-tuple-element.61), channel_id=1, source_target_pairs={{1,0},{2,1},{3,2},{4,3},{5,4},{6,5},{7,6},{9,8},{10,9},{11,10},{12... | collective-permute-start | bytes 196616 | tf_op jit(solution)/shard_map/ppermute | solution.py:131
  40.8 3.6 %collective-permute-start.3 = (bf16[1,128,256]{2,1,0:T(8,128)(2,1)S(1)}, bf16[1,128,256]{2,1,0:T(8,128)(2,1)S(1)}, u32[]{:S(2)}, u32[]{:S(2)}) collective-permute-start(bf16[1,128,256]{2,1,0:T(8,128)(2,1)S(1)} %get-tuple-element.62), channel_id=1, source_target_pairs={{0,1},{1,2},{2,3},{3,4},{4,5},{5,6},{6,7},{8,9},{9,10},{10,11},{11... | collective-permute-start | bytes 196616 | tf_op jit(solution)/shard_map/ppermute | solution.py:130
  44.5 1.4 collective-permute-start.11
  45.9 1.4 collective-permute-start.16
  47.2 7.5 %shard_map.55 = (bf16[1,128,256]{2,1,0:T(8,128)(2,1)S(1)}, bf16[4,128,256]{2,1,0:T(8,128)(2,1)}, bf16[1,128,256]{2,1,0:T(8,128)(2,1)S(1)}) custom-call(s32[2]{0:T(128)S(1)} %add_convert_fusion.6.flags, bf16[2,128,256]{2,1,0:T(8,128)(2,1)S(1)} %collective-permute-done.1.q_low, bf16[4,128,256]{2,1,0:T(8,128)(2,1)S(1)} %get-tuple-element.36.q_mid, ...), custom_call_target="tpu_custom_call" | custom-call | flops 2717908992 | bytes 4718592 | tf_op jit(solution)/shard_map/pallas_call | solution.py:98
  54.7 6.4 %shard_map.56 = bf16[4,128,256]{2,1,0:T(8,128)(2,1)} custom-call(bf16[1,128,256]{2,1,0:T(8,128)(2,1)S(1)} %get-tuple-element.20.first_low, bf16[4,128,256]{2,1,0:T(8,128)(2,1)} %get-tuple-element.21.first_mid, bf16[1,128,256]{2,1,0:T(8,128)(2,1)S(1)} %get-tuple-element.22.first_high, bf16[4,128,256]{2,1,0:T(8,128)(2,1)S(1)} %get-tuple-element.36.q_mid, ...), custom_call_target="tpu_custom_call" | custom-call | flops 1811939328 | bytes 4718592 | tf_op jit(solution)/shard_map/pallas_call | solution.py:113
  61.1 3.2 %collective-permute-start.5 = (bf16[4,128,256]{2,1,0:T(8,128)(2,1)}, bf16[4,128,256]{2,1,0:T(8,128)(2,1)}, u32[]{:S(2)}, u32[]{:S(2)}) collective-permute-start(bf16[4,128,256]{2,1,0:T(8,128)(2,1)} %shard_map.56), channel_id=1, source_target_pairs={{0,8},{8,16},{16,24},{1,9},{9,17},{17,25},{2,10},{10,18},{18,26},{... | collective-permute-start | bytes 786440 | tf_op jit(solution)/shard_map/ppermute | solution.py:150
  64.3 1.9 %collective-permute-start.15 = (bf16[4,128,256]{2,1,0:T(8,128)(2,1)}, bf16[4,128,256]{2,1,0:T(8,128)(2,1)}, u32[]{:S(2)}, u32[]{:S(2)}) collective-permute-start(bf16[4,128,256]{2,1,0:T(8,128)(2,1)} %get-tuple-element.21.first_mid), channel_id=1, source_target_pairs={{0,8},{8,16},{16,24},{1,9},{9,17},{17,25},{2,10},{10,18},{18,26},{... | collective-permute-start | bytes 786440 | tf_op jit(solution)/shard_map/ppermute | solution.py:150
  66.3 8.2 %collective-permute-done.5 = bf16[4,128,256]{2,1,0:T(8,128)(2,1)} collective-permute-done((bf16[4,128,256]{2,1,0:T(8,128)(2,1)}, bf16[4,128,256]{2,1,0:T(8,128)(2,1)}, u32[]{:S(2)}, u32[]{:S(2)}) %collective-permute-start.5) | collective-permute-done | bytes 262176 | tf_op jit(solution)/shard_map/ppermute | solution.py:150
  74.5 4.7 %collective-permute-done.15 = bf16[4,128,256]{2,1,0:T(8,128)(2,1)} collective-permute-done((bf16[4,128,256]{2,1,0:T(8,128)(2,1)}, bf16[4,128,256]{2,1,0:T(8,128)(2,1)}, u32[]{:S(2)}, u32[]{:S(2)}) %collective-permute-start.15) | collective-permute-done | bytes 262176 | tf_op jit(solution)/shard_map/ppermute | solution.py:150
  79.1 1.4 fusion.16
  80.5 1.9 %collective-permute-start.13 = (bf16[2,128,256]{2,1,0:T(8,128)(2,1)S(1)}, bf16[2,128,256]{2,1,0:T(8,128)(2,1)S(1)}, u32[]{:S(2)}, u32[]{:S(2)}) collective-permute-start(bf16[2,128,256]{2,1,0:T(8,128)(2,1)S(1)} %get-tuple-element.59), channel_id=1, source_target_pairs={{1,0},{2,1},{3,2},{4,3},{5,4},{6,5},{7,6},{9,8},{10,9},{11,10},{12... | collective-permute-start | bytes 393224 | tf_op jit(solution)/shard_map/ppermute | solution.py:131
  82.5 3.6 %collective-permute-start.12 = (bf16[2,128,256]{2,1,0:T(8,128)(2,1)S(1)}, bf16[2,128,256]{2,1,0:T(8,128)(2,1)S(1)}, u32[]{:S(2)}, u32[]{:S(2)}) collective-permute-start(bf16[2,128,256]{2,1,0:T(8,128)(2,1)S(1)} %get-tuple-element.60), channel_id=1, source_target_pairs={{0,1},{1,2},{2,3},{3,4},{4,5},{5,6},{6,7},{8,9},{9,10},{10,11},{11... | collective-permute-start | bytes 393224 | tf_op jit(solution)/shard_map/ppermute | solution.py:130
  86.1 1.9 %collective-permute-start.18 = (bf16[1,128,256]{2,1,0:T(8,128)(2,1)S(1)}, bf16[1,128,256]{2,1,0:T(8,128)(2,1)S(1)}, u32[]{:S(2)}, u32[]{:S(2)}) collective-permute-start(bf16[1,128,256]{2,1,0:T(8,128)(2,1)S(1)} %get-tuple-element.57), channel_id=1, source_target_pairs={{1,0},{2,1},{3,2},{4,3},{5,4},{6,5},{7,6},{9,8},{10,9},{11,10},{12... | collective-permute-start | bytes 196616 | tf_op jit(solution)/shard_map/ppermute | solution.py:131
  88.1 3.9 %collective-permute-start.17 = (bf16[1,128,256]{2,1,0:T(8,128)(2,1)S(1)}, bf16[1,128,256]{2,1,0:T(8,128)(2,1)S(1)}, u32[]{:S(2)}, u32[]{:S(2)}) collective-permute-start(bf16[1,128,256]{2,1,0:T(8,128)(2,1)S(1)} %get-tuple-element.58), channel_id=1, source_target_pairs={{0,1},{1,2},{2,3},{3,4},{4,5},{5,6},{6,7},{8,9},{9,10},{10,11},{11... | collective-permute-start | bytes 196616 | tf_op jit(solution)/shard_map/ppermute | solution.py:130
  93.6 6.8 %shard_map.59 = (bf16[1,128,256]{2,1,0:T(8,128)(2,1)S(1)}, bf16[4,128,256]{2,1,0:T(8,128)(2,1)S(1)}, bf16[1,128,256]{2,1,0:T(8,128)(2,1)S(1)}) custom-call(s32[2]{0:T(128)S(1)} %add_convert_fusion.6.flags, bf16[2,128,256]{2,1,0:T(8,128)(2,1)S(1)} %collective-permute-done.12.q_low, bf16[4,128,256]{2,1,0:T(8,128)(2,1)S(1)} %get-tuple-element.42.q_mid, ...), custom_call_target="tpu_custom_call" | custom-call | flops 2717908992 | bytes 4718592 | tf_op jit(solution)/shard_map/pallas_call | solution.py:98
  100.5 4.6 %shard_map.60 = bf16[4,128,256]{2,1,0:T(8,128)(2,1)S(1)} custom-call(bf16[1,128,256]{2,1,0:T(8,128)(2,1)S(1)} %get-tuple-element.26.first_low, bf16[4,128,256]{2,1,0:T(8,128)(2,1)S(1)} %get-tuple-element.27.first_mid, bf16[1,128,256]{2,1,0:T(8,128)(2,1)S(1)} %get-tuple-element.28.first_high, bf16[4,128,256]{2,1,0:T(8,128)(2,1)S(1)} %get-tuple-element.42.q_mid, ...), custom_call_target="tpu_custom_call" | custom-call | flops 1811939328 | bytes 4718592 | tf_op jit(solution)/shard_map/pallas_call | solution.py:113
  105.1 2.6 %collective-permute-start.19 = (bf16[4,128,256]{2,1,0:T(8,128)(2,1)S(1)}, bf16[4,128,256]{2,1,0:T(8,128)(2,1)S(1)}, u32[]{:S(2)}, u32[]{:S(2)}) collective-permute-start(bf16[4,128,256]{2,1,0:T(8,128)(2,1)S(1)} %shard_map.60), channel_id=1, source_target_pairs={{0,8},{8,16},{16,24},{1,9},{9,17},{17,25},{2,10},{10,18},{18,26},{... | collective-permute-start | bytes 786440 | tf_op jit(solution)/shard_map/ppermute | solution.py:150
  107.7 1.9 %collective-permute-start.23 = (bf16[4,128,256]{2,1,0:T(8,128)(2,1)S(1)}, bf16[4,128,256]{2,1,0:T(8,128)(2,1)S(1)}, u32[]{:S(2)}, u32[]{:S(2)}) collective-permute-start(bf16[4,128,256]{2,1,0:T(8,128)(2,1)S(1)} %get-tuple-element.27.first_mid), channel_id=1, source_target_pairs={{0,8},{8,16},{16,24},{1,9},{9,17},{17,25},{2,10},{10,18},{18,26},{... | collective-permute-start | bytes 786440 | tf_op jit(solution)/shard_map/ppermute | solution.py:150
  109.7 7.3 %collective-permute-done.19 = bf16[4,128,256]{2,1,0:T(8,128)(2,1)S(1)} collective-permute-done((bf16[4,128,256]{2,1,0:T(8,128)(2,1)S(1)}, bf16[4,128,256]{2,1,0:T(8,128)(2,1)S(1)}, u32[]{:S(2)}, u32[]{:S(2)}) %collective-permute-start.19) | collective-permute-done | bytes 262176 | tf_op jit(solution)/shard_map/ppermute | solution.py:150
  116.9 5.6 %collective-permute-done.23 = bf16[4,128,256]{2,1,0:T(8,128)(2,1)S(1)} collective-permute-done((bf16[4,128,256]{2,1,0:T(8,128)(2,1)S(1)}, bf16[4,128,256]{2,1,0:T(8,128)(2,1)S(1)}, u32[]{:S(2)}, u32[]{:S(2)}) %collective-permute-start.23) | collective-permute-done | bytes 262176 | tf_op jit(solution)/shard_map/ppermute | solution.py:150
  122.8 2.6 %collective-permute-start.22 = (bf16[2,128,256]{2,1,0:T(8,128)(2,1)S(1)}, bf16[2,128,256]{2,1,0:T(8,128)(2,1)S(1)}, u32[]{:S(2)}, u32[]{:S(2)}) collective-permute-start(bf16[2,128,256]{2,1,0:T(8,128)(2,1)S(1)} %get-tuple-element.55), channel_id=1, source_target_pairs={{1,0},{2,1},{3,2},{4,3},{5,4},{6,5},{7,6},{9,8},{10,9},{11,10},{12... | collective-permute-start | bytes 393224 | tf_op jit(solution)/shard_map/ppermute | solution.py:131
  125.4 3.1 %collective-permute-start.21 = (bf16[2,128,256]{2,1,0:T(8,128)(2,1)S(1)}, bf16[2,128,256]{2,1,0:T(8,128)(2,1)S(1)}, u32[]{:S(2)}, u32[]{:S(2)}) collective-permute-start(bf16[2,128,256]{2,1,0:T(8,128)(2,1)S(1)} %get-tuple-element.56), channel_id=1, source_target_pairs={{0,1},{1,2},{2,3},{3,4},{4,5},{5,6},{6,7},{8,9},{9,10},{10,11},{11... | collective-permute-start | bytes 393224 | tf_op jit(solution)/shard_map/ppermute | solution.py:130
  128.5 1.9 %collective-permute-start.26 = (bf16[1,128,256]{2,1,0:T(8,128)(2,1)S(1)}, bf16[1,128,256]{2,1,0:T(8,128)(2,1)S(1)}, u32[]{:S(2)}, u32[]{:S(2)}) collective-permute-start(bf16[1,128,256]{2,1,0:T(8,128)(2,1)S(1)} %get-tuple-element.53), channel_id=1, source_target_pairs={{1,0},{2,1},{3,2},{4,3},{5,4},{6,5},{7,6},{9,8},{10,9},{11,10},{12... | collective-permute-start | bytes 196616 | tf_op jit(solution)/shard_map/ppermute | solution.py:131
  130.5 3.6 %collective-permute-start.25 = (bf16[1,128,256]{2,1,0:T(8,128)(2,1)S(1)}, bf16[1,128,256]{2,1,0:T(8,128)(2,1)S(1)}, u32[]{:S(2)}, u32[]{:S(2)}) collective-permute-start(bf16[1,128,256]{2,1,0:T(8,128)(2,1)S(1)} %get-tuple-element.54), channel_id=1, source_target_pairs={{0,1},{1,2},{2,3},{3,4},{4,5},{5,6},{6,7},{8,9},{9,10},{10,11},{11... | collective-permute-start | bytes 196616 | tf_op jit(solution)/shard_map/ppermute | solution.py:130
  135.8 6.8 %shard_map.61 = (bf16[1,128,256]{2,1,0:T(8,128)(2,1)S(1)}, bf16[4,128,256]{2,1,0:T(8,128)(2,1)S(1)}, bf16[1,128,256]{2,1,0:T(8,128)(2,1)S(1)}) custom-call(s32[2]{0:T(128)S(1)} %add_convert_fusion.6.flags, bf16[2,128,256]{2,1,0:T(8,128)(2,1)S(1)} %collective-permute-done.21.q_low, bf16[4,128,256]{2,1,0:T(8,128)(2,1)S(1)} %get-tuple-element.40.q_mid, ...), custom_call_target="tpu_custom_call" | custom-call | flops 2717908992 | bytes 4718592 | tf_op jit(solution)/shard_map/pallas_call | solution.py:98
  142.6 4.6 %shard_map.62 = bf16[4,128,256]{2,1,0:T(8,128)(2,1)S(1)} custom-call(bf16[1,128,256]{2,1,0:T(8,128)(2,1)S(1)} %get-tuple-element.30.first_low, bf16[4,128,256]{2,1,0:T(8,128)(2,1)S(1)} %get-tuple-element.29.first_mid, bf16[1,128,256]{2,1,0:T(8,128)(2,1)S(1)} %get-tuple-element.31.first_high, bf16[4,128,256]{2,1,0:T(8,128)(2,1)S(1)} %get-tuple-element.40.q_mid, ...), custom_call_target="tpu_custom_call" | custom-call | flops 1811939328 | bytes 4718592 | tf_op jit(solution)/shard_map/pallas_call | solution.py:113
  147.2 2.0 %collective-permute-start.27 = (bf16[4,128,256]{2,1,0:T(8,128)(2,1)S(1)}, bf16[4,128,256]{2,1,0:T(8,128)(2,1)S(1)}, u32[]{:S(2)}, u32[]{:S(2)}) collective-permute-start(bf16[4,128,256]{2,1,0:T(8,128)(2,1)S(1)} %shard_map.62), channel_id=1, source_target_pairs={{8,16},{16,24},{9,17},{17,25},{10,18},{18,26},{11,19},{19,27},{12,... | collective-permute-start | bytes 786440 | tf_op jit(solution)/shard_map/ppermute | solution.py:150
  149.2 1.9 %collective-permute-start.31 = (bf16[4,128,256]{2,1,0:T(8,128)(2,1)S(1)}, bf16[4,128,256]{2,1,0:T(8,128)(2,1)S(1)}, u32[]{:S(2)}, u32[]{:S(2)}) collective-permute-start(bf16[4,128,256]{2,1,0:T(8,128)(2,1)S(1)} %get-tuple-element.29.first_mid), channel_id=1, source_target_pairs={{8,16},{16,24},{9,17},{17,25},{10,18},{18,26},{11,19},{19,27},{12,... | collective-permute-start | bytes 786440 | tf_op jit(solution)/shard_map/ppermute | solution.py:150
  151.1 7.5 %collective-permute-done.27 = bf16[4,128,256]{2,1,0:T(8,128)(2,1)S(1)} collective-permute-done((bf16[4,128,256]{2,1,0:T(8,128)(2,1)S(1)}, bf16[4,128,256]{2,1,0:T(8,128)(2,1)S(1)}, u32[]{:S(2)}, u32[]{:S(2)}) %collective-permute-start.27) | collective-permute-done | bytes 262176 | tf_op jit(solution)/shard_map/ppermute | solution.py:150
  158.6 5.6 %collective-permute-done.31 = bf16[4,128,256]{2,1,0:T(8,128)(2,1)S(1)} collective-permute-done((bf16[4,128,256]{2,1,0:T(8,128)(2,1)S(1)}, bf16[4,128,256]{2,1,0:T(8,128)(2,1)S(1)}, u32[]{:S(2)}, u32[]{:S(2)}) %collective-permute-start.31) | collective-permute-done | bytes 262176 | tf_op jit(solution)/shard_map/ppermute | solution.py:150
  164.5 2.8 %collective-permute-start.30 = (bf16[2,128,256]{2,1,0:T(8,128)(2,1)S(1)}, bf16[2,128,256]{2,1,0:T(8,128)(2,1)S(1)}, u32[]{:S(2)}, u32[]{:S(2)}) collective-permute-start(bf16[2,128,256]{2,1,0:T(8,128)(2,1)S(1)} %get-tuple-element.51), channel_id=1, source_target_pairs={{1,0},{2,1},{3,2},{4,3},{5,4},{6,5},{7,6},{9,8},{10,9},{11,10},{12... | collective-permute-start | bytes 393224 | tf_op jit(solution)/shard_map/ppermute | solution.py:131
  167.2 3.2 %collective-permute-start.29 = (bf16[2,128,256]{2,1,0:T(8,128)(2,1)S(1)}, bf16[2,128,256]{2,1,0:T(8,128)(2,1)S(1)}, u32[]{:S(2)}, u32[]{:S(2)}) collective-permute-start(bf16[2,128,256]{2,1,0:T(8,128)(2,1)S(1)} %get-tuple-element.52), channel_id=1, source_target_pairs={{0,1},{1,2},{2,3},{3,4},{4,5},{5,6},{6,7},{8,9},{9,10},{10,11},{11... | collective-permute-start | bytes 393224 | tf_op jit(solution)/shard_map/ppermute | solution.py:130
  170.5 1.9 %collective-permute-start.34 = (bf16[1,128,256]{2,1,0:T(8,128)(2,1)S(1)}, bf16[1,128,256]{2,1,0:T(8,128)(2,1)S(1)}, u32[]{:S(2)}, u32[]{:S(2)}) collective-permute-start(bf16[1,128,256]{2,1,0:T(8,128)(2,1)S(1)} %get-tuple-element.49), channel_id=1, source_target_pairs={{1,0},{2,1},{3,2},{4,3},{5,4},{6,5},{7,6},{9,8},{10,9},{11,10},{12... | collective-permute-start | bytes 196616 | tf_op jit(solution)/shard_map/ppermute | solution.py:131
  172.4 3.9 %collective-permute-start.33 = (bf16[1,128,256]{2,1,0:T(8,128)(2,1)S(1)}, bf16[1,128,256]{2,1,0:T(8,128)(2,1)S(1)}, u32[]{:S(2)}, u32[]{:S(2)}) collective-permute-start(bf16[1,128,256]{2,1,0:T(8,128)(2,1)S(1)} %get-tuple-element.50), channel_id=1, source_target_pairs={{0,1},{1,2},{2,3},{3,4},{4,5},{5,6},{6,7},{8,9},{9,10},{10,11},{11... | collective-permute-start | bytes 196616 | tf_op jit(solution)/shard_map/ppermute | solution.py:130
  177.4 6.8 %shard_map.63 = (bf16[1,128,256]{2,1,0:T(8,128)(2,1)S(1)}, bf16[4,128,256]{2,1,0:T(8,128)(2,1)S(1)}, bf16[1,128,256]{2,1,0:T(8,128)(2,1)S(1)}) custom-call(s32[2]{0:T(128)S(1)} %add_convert_fusion.6.flags, bf16[2,128,256]{2,1,0:T(8,128)(2,1)S(1)} %collective-permute-done.29.q_low, bf16[4,128,256]{2,1,0:T(8,128)(2,1)S(1)} %get-tuple-element.38.q_mid, ...), custom_call_target="tpu_custom_call" | custom-call | flops 2717908992 | bytes 4718592 | tf_op jit(solution)/shard_map/pallas_call | solution.py:98
  184.2 4.6 %shard_map.64 = bf16[4,128,256]{2,1,0:T(8,128)(2,1)S(1)} custom-call(bf16[1,128,256]{2,1,0:T(8,128)(2,1)S(1)} %get-tuple-element.33.first_low, bf16[4,128,256]{2,1,0:T(8,128)(2,1)S(1)} %get-tuple-element.32.first_mid, bf16[1,128,256]{2,1,0:T(8,128)(2,1)S(1)} %get-tuple-element.34.first_high, bf16[4,128,256]{2,1,0:T(8,128)(2,1)S(1)} %get-tuple-element.38.q_mid, ...), custom_call_target="tpu_custom_call" | custom-call | flops 1811939328 | bytes 4718592 | tf_op jit(solution)/shard_map/pallas_call | solution.py:113
  (63 shorter events, 11.3 us)
Async XLA Ops:
  0.9 14.7 %collective-permute-start.9 = (bf16[1,128,256]{2,1,0:T(8,128)(2,1)S(1)}, bf16[1,128,256]{2,1,0:T(8,128)(2,1)S(1)}, u32[]{:S(2)}, u32[]{:S(2)}) collective-permute-start(bf16[1,128,256]{2,1,0:T(8,128)(2,1)S(1)} %get-tuple-element.43), channel_id=1, source_target_pairs={{1,0},{2,1},{3,2},{4,3},{5,4},{6,5},{7,6},{9,8},{10,9},{11,10},{12... | collective-permute-start | bytes 196616 | tf_op jit(solution)/shard_map/ppermute | solution.py:131
  3.5 12.1 %collective-permute-start.8 = (bf16[1,128,256]{2,1,0:T(8,128)(2,1)S(1)}, bf16[1,128,256]{2,1,0:T(8,128)(2,1)S(1)}, u32[]{:S(2)}, u32[]{:S(2)}) collective-permute-start(bf16[1,128,256]{2,1,0:T(8,128)(2,1)S(1)} %get-tuple-element.44), channel_id=1, source_target_pairs={{0,1},{1,2},{2,3},{3,4},{4,5},{5,6},{6,7},{8,9},{9,10},{10,11},{11... | collective-permute-start | bytes 196616 | tf_op jit(solution)/shard_map/ppermute | solution.py:130
  7.6 8.0 %collective-permute-start.7 = (bf16[2,128,256]{2,1,0:T(8,128)(2,1)S(1)}, bf16[2,128,256]{2,1,0:T(8,128)(2,1)S(1)}, u32[]{:S(2)}, u32[]{:S(2)}) collective-permute-start(bf16[2,128,256]{2,1,0:T(8,128)(2,1)S(1)} %get-tuple-element.47), channel_id=1, source_target_pairs={{1,0},{2,1},{3,2},{4,3},{5,4},{6,5},{7,6},{9,8},{10,9},{11,10},{12... | collective-permute-start | bytes 393224 | tf_op jit(solution)/shard_map/ppermute | solution.py:131
  9.5 6.1 %collective-permute-start.6 = (bf16[2,128,256]{2,1,0:T(8,128)(2,1)S(1)}, bf16[2,128,256]{2,1,0:T(8,128)(2,1)S(1)}, u32[]{:S(2)}, u32[]{:S(2)}) collective-permute-start(bf16[2,128,256]{2,1,0:T(8,128)(2,1)S(1)} %get-tuple-element.48), channel_id=1, source_target_pairs={{0,1},{1,2},{2,3},{3,4},{4,5},{5,6},{6,7},{8,9},{9,10},{10,11},{11... | collective-permute-start | bytes 393224 | tf_op jit(solution)/shard_map/ppermute | solution.py:130
  13.2 18.7 %collective-permute-start = (bf16[2,4,128,256]{3,2,1,0:T(8,128)(2,1)}, bf16[2,4,128,256]{3,2,1,0:T(8,128)(2,1)S(1)}, u32[]{:S(2)}, u32[]{:S(2)}) collective-permute-start(bf16[2,4,128,256]{3,2,1,0:T(8,128)(2,1)} %bitcast.82), channel_id=1, source_target_pairs={{0,24},{8,16},{1,25},{9,17},{2,26},{10,18},{3,27},{11,19},{4,28},{... | collective-permute-start | bytes 1572872 | tf_op jit(solution)/shard_map/ppermute | solution.py:150
  15.6 2.0 %copy-start = (bf16[1,3,3,3,256,256]{5,4,3,2,1,0:T(8,128)(2,1)S(1)}, bf16[1,3,3,3,256,256]{5,4,3,2,1,0:T(8,128)(2,1)}, u32[]{:S(2)}) copy-start(bf16[1,3,3,3,256,256]{5,4,3,2,1,0:T(8,128)(2,1)} %param.8) | copy-start | bytes 10616836
  17.6 8.2 %copy-start.3 = (bf16[1,3,3,3,256,256]{5,4,3,2,1,0:T(8,128)(2,1)S(1)}, bf16[1,3,3,3,256,256]{5,4,3,2,1,0:T(8,128)(2,1)}, u32[]{:S(2)}) copy-start(bf16[1,3,3,3,256,256]{5,4,3,2,1,0:T(8,128)(2,1)} %param.9) | copy-start | bytes 10616836
  24.5 20.0 %collective-permute-start.14 = (bf16[4,128,256]{2,1,0:T(8,128)(2,1)S(1)}, bf16[4,128,256]{2,1,0:T(8,128)(2,1)}, u32[]{:S(2)}, u32[]{:S(2)}) collective-permute-start(bf16[4,128,256]{2,1,0:T(8,128)(2,1)S(1)} %get-tuple-element.24.first_mid), channel_id=1, source_target_pairs={{0,8},{1,9},{2,10},{3,11},{4,12},{5,13},{6,14},{7,15}} | collective-permute-start | bytes 786440 | tf_op jit(solution)/shard_map/ppermute | solution.py:150
  25.8 6.0 %copy-start.5 = (bf16[1,2,4,16,8,256]{5,4,3,2,1,0:T(8,128)(2,1)S(1)}, bf16[1,2,4,16,8,256]{5,4,3,2,1,0:T(8,128)(2,1)}, u32[]{:S(2)}) copy-start(bf16[1,2,4,16,8,256]{5,4,3,2,1,0:T(8,128)(2,1)} %param.5) | copy-start | bytes 1572868
  25.8 21.4 %copy-start.1 = (bf16[1,3,3,3,256,256]{5,4,3,2,1,0:T(8,128)(2,1)S(1)}, bf16[1,3,3,3,256,256]{5,4,3,2,1,0:T(8,128)(2,1)}, u32[]{:S(2)}) copy-start(bf16[1,3,3,3,256,256]{5,4,3,2,1,0:T(8,128)(2,1)} %param.8) | copy-start | bytes 10616836
  30.5 10.4 %collective-permute-start.10 = (bf16[4,128,256]{2,1,0:T(8,128)(2,1)S(1)}, bf16[4,128,256]{2,1,0:T(8,128)(2,1)}, u32[]{:S(2)}, u32[]{:S(2)}) collective-permute-start(bf16[4,128,256]{2,1,0:T(8,128)(2,1)S(1)} %shard_map.58), channel_id=1, source_target_pairs={{0,8},{1,9},{2,10},{3,11},{4,12},{5,13},{6,14},{7,15}} | collective-permute-start | bytes 786440 | tf_op jit(solution)/shard_map/ppermute | solution.py:150
  33.1 14.1 %collective-permute-start.2 = (bf16[2,128,256]{2,1,0:T(8,128)(2,1)S(1)}, bf16[2,128,256]{2,1,0:T(8,128)(2,1)S(1)}, u32[]{:S(2)}, u32[]{:S(2)}) collective-permute-start(bf16[2,128,256]{2,1,0:T(8,128)(2,1)S(1)} %get-tuple-element.63), channel_id=1, source_target_pairs={{1,0},{2,1},{3,2},{4,3},{5,4},{6,5},{7,6},{9,8},{10,9},{11,10},{12... | collective-permute-start | bytes 393224 | tf_op jit(solution)/shard_map/ppermute | solution.py:131
  35.7 11.5 %collective-permute-start.1 = (bf16[2,128,256]{2,1,0:T(8,128)(2,1)S(1)}, bf16[2,128,256]{2,1,0:T(8,128)(2,1)S(1)}, u32[]{:S(2)}, u32[]{:S(2)}) collective-permute-start(bf16[2,128,256]{2,1,0:T(8,128)(2,1)S(1)} %get-tuple-element.64), channel_id=1, source_target_pairs={{0,1},{1,2},{2,3},{3,4},{4,5},{5,6},{6,7},{8,9},{9,10},{10,11},{11... | collective-permute-start | bytes 393224 | tf_op jit(solution)/shard_map/ppermute | solution.py:130
  38.9 7.0 %collective-permute-start.4 = (bf16[1,128,256]{2,1,0:T(8,128)(2,1)S(1)}, bf16[1,128,256]{2,1,0:T(8,128)(2,1)S(1)}, u32[]{:S(2)}, u32[]{:S(2)}) collective-permute-start(bf16[1,128,256]{2,1,0:T(8,128)(2,1)S(1)} %get-tuple-element.61), channel_id=1, source_target_pairs={{1,0},{2,1},{3,2},{4,3},{5,4},{6,5},{7,6},{9,8},{10,9},{11,10},{12... | collective-permute-start | bytes 196616 | tf_op jit(solution)/shard_map/ppermute | solution.py:131
  40.8 6.4 %collective-permute-start.3 = (bf16[1,128,256]{2,1,0:T(8,128)(2,1)S(1)}, bf16[1,128,256]{2,1,0:T(8,128)(2,1)S(1)}, u32[]{:S(2)}, u32[]{:S(2)}) collective-permute-start(bf16[1,128,256]{2,1,0:T(8,128)(2,1)S(1)} %get-tuple-element.62), channel_id=1, source_target_pairs={{0,1},{1,2},{2,3},{3,4},{4,5},{5,6},{6,7},{8,9},{9,10},{10,11},{11... | collective-permute-start | bytes 196616 | tf_op jit(solution)/shard_map/ppermute | solution.py:130
  44.5 21.8 %collective-permute-start.11 = (bf16[4,128,256]{2,1,0:T(8,128)(2,1)}, bf16[4,128,256]{2,1,0:T(8,128)(2,1)}, u32[]{:S(2)}, u32[]{:S(2)}) collective-permute-start(bf16[4,128,256]{2,1,0:T(8,128)(2,1)} %collective-permute-done.10), channel_id=1, source_target_pairs={{8,24},{9,25},{10,26},{11,27},{12,28},{13,29},{14,30},{15,31}} | collective-permute-start | bytes 786440 | tf_op jit(solution)/shard_map/ppermute | solution.py:150
  45.9 20.4 %collective-permute-start.16 = (bf16[4,128,256]{2,1,0:T(8,128)(2,1)}, bf16[4,128,256]{2,1,0:T(8,128)(2,1)}, u32[]{:S(2)}, u32[]{:S(2)}) collective-permute-start(bf16[4,128,256]{2,1,0:T(8,128)(2,1)} %collective-permute-done.14), channel_id=1, source_target_pairs={{8,24},{9,25},{10,26},{11,27},{12,28},{13,29},{14,30},{15,31}} | collective-permute-start | bytes 786440 | tf_op jit(solution)/shard_map/ppermute | solution.py:150
  54.7 38.9 %copy-start.2 = (bf16[1,3,3,3,256,256]{5,4,3,2,1,0:T(8,128)(2,1)S(1)}, bf16[1,3,3,3,256,256]{5,4,3,2,1,0:T(8,128)(2,1)}, u32[]{:S(2)}) copy-start(bf16[1,3,3,3,256,256]{5,4,3,2,1,0:T(8,128)(2,1)} %param.8) | copy-start | bytes 10616836
  61.1 13.3 %collective-permute-start.5 = (bf16[4,128,256]{2,1,0:T(8,128)(2,1)}, bf16[4,128,256]{2,1,0:T(8,128)(2,1)}, u32[]{:S(2)}, u32[]{:S(2)}) collective-permute-start(bf16[4,128,256]{2,1,0:T(8,128)(2,1)} %shard_map.56), channel_id=1, source_target_pairs={{0,8},{8,16},{16,24},{1,9},{9,17},{17,25},{2,10},{10,18},{18,26},{... | collective-permute-start | bytes 786440 | tf_op jit(solution)/shard_map/ppermute | solution.py:150
  64.3 14.8 %collective-permute-start.15 = (bf16[4,128,256]{2,1,0:T(8,128)(2,1)}, bf16[4,128,256]{2,1,0:T(8,128)(2,1)}, u32[]{:S(2)}, u32[]{:S(2)}) collective-permute-start(bf16[4,128,256]{2,1,0:T(8,128)(2,1)} %get-tuple-element.21.first_mid), channel_id=1, source_target_pairs={{0,8},{8,16},{16,24},{1,9},{9,17},{17,25},{2,10},{10,18},{18,26},{... | collective-permute-start | bytes 786440 | tf_op jit(solution)/shard_map/ppermute | solution.py:150
  80.5 13.1 %collective-permute-start.13 = (bf16[2,128,256]{2,1,0:T(8,128)(2,1)S(1)}, bf16[2,128,256]{2,1,0:T(8,128)(2,1)S(1)}, u32[]{:S(2)}, u32[]{:S(2)}) collective-permute-start(bf16[2,128,256]{2,1,0:T(8,128)(2,1)S(1)} %get-tuple-element.59), channel_id=1, source_target_pairs={{1,0},{2,1},{3,2},{4,3},{5,4},{6,5},{7,6},{9,8},{10,9},{11,10},{12... | collective-permute-start | bytes 393224 | tf_op jit(solution)/shard_map/ppermute | solution.py:131
  82.5 11.1 %collective-permute-start.12 = (bf16[2,128,256]{2,1,0:T(8,128)(2,1)S(1)}, bf16[2,128,256]{2,1,0:T(8,128)(2,1)S(1)}, u32[]{:S(2)}, u32[]{:S(2)}) collective-permute-start(bf16[2,128,256]{2,1,0:T(8,128)(2,1)S(1)} %get-tuple-element.60), channel_id=1, source_target_pairs={{0,1},{1,2},{2,3},{3,4},{4,5},{5,6},{6,7},{8,9},{9,10},{10,11},{11... | collective-permute-start | bytes 393224 | tf_op jit(solution)/shard_map/ppermute | solution.py:130
  86.1 6.5 %collective-permute-start.18 = (bf16[1,128,256]{2,1,0:T(8,128)(2,1)S(1)}, bf16[1,128,256]{2,1,0:T(8,128)(2,1)S(1)}, u32[]{:S(2)}, u32[]{:S(2)}) collective-permute-start(bf16[1,128,256]{2,1,0:T(8,128)(2,1)S(1)} %get-tuple-element.57), channel_id=1, source_target_pairs={{1,0},{2,1},{3,2},{4,3},{5,4},{6,5},{7,6},{9,8},{10,9},{11,10},{12... | collective-permute-start | bytes 196616 | tf_op jit(solution)/shard_map/ppermute | solution.py:131
  88.1 12.4 %copy-start.4 = (bf16[1,3,3,3,256,256]{5,4,3,2,1,0:T(8,128)(2,1)S(1)}, bf16[1,3,3,3,256,256]{5,4,3,2,1,0:T(8,128)(2,1)}, u32[]{:S(2)}) copy-start(bf16[1,3,3,3,256,256]{5,4,3,2,1,0:T(8,128)(2,1)} %param.9) | copy-start | bytes 10616836
  88.1 5.5 %collective-permute-start.17 = (bf16[1,128,256]{2,1,0:T(8,128)(2,1)S(1)}, bf16[1,128,256]{2,1,0:T(8,128)(2,1)S(1)}, u32[]{:S(2)}, u32[]{:S(2)}) collective-permute-start(bf16[1,128,256]{2,1,0:T(8,128)(2,1)S(1)} %get-tuple-element.58), channel_id=1, source_target_pairs={{0,1},{1,2},{2,3},{3,4},{4,5},{5,6},{6,7},{8,9},{9,10},{10,11},{11... | collective-permute-start | bytes 196616 | tf_op jit(solution)/shard_map/ppermute | solution.py:130
  92.0 17.7 %collective-permute-start.20 = (bf16[4,128,256]{2,1,0:T(8,128)(2,1)}, bf16[4,128,256]{2,1,0:T(8,128)(2,1)S(1)}, u32[]{:S(2)}, u32[]{:S(2)}) collective-permute-start(bf16[4,128,256]{2,1,0:T(8,128)(2,1)} %collective-permute-done.5), channel_id=1, source_target_pairs={{8,24},{9,25},{10,26},{11,27},{12,28},{13,29},{14,30},{15,31}} | collective-permute-start | bytes 786440 | tf_op jit(solution)/shard_map/ppermute | solution.py:150
  92.7 17.0 %collective-permute-start.24 = (bf16[4,128,256]{2,1,0:T(8,128)(2,1)}, bf16[4,128,256]{2,1,0:T(8,128)(2,1)S(1)}, u32[]{:S(2)}, u32[]{:S(2)}) collective-permute-start(bf16[4,128,256]{2,1,0:T(8,128)(2,1)} %collective-permute-done.15), channel_id=1, source_target_pairs={{8,24},{9,25},{10,26},{11,27},{12,28},{13,29},{14,30},{15,31}} | collective-permute-start | bytes 786440 | tf_op jit(solution)/shard_map/ppermute | solution.py:150
  100.4 22.1 %copy-start.6 = (bf16[3,2,4,16,8,256]{5,4,3,2,1,0:T(8,128)(2,1)S(1)}, bf16[3,2,4,16,8,256]{5,4,3,2,1,0:T(8,128)(2,1)}, u32[]{:S(2)}) copy-start(bf16[3,2,4,16,8,256]{5,4,3,2,1,0:T(8,128)(2,1)} %param.7) | copy-start | bytes 4718596
  105.1 11.9 %collective-permute-start.19 = (bf16[4,128,256]{2,1,0:T(8,128)(2,1)S(1)}, bf16[4,128,256]{2,1,0:T(8,128)(2,1)S(1)}, u32[]{:S(2)}, u32[]{:S(2)}) collective-permute-start(bf16[4,128,256]{2,1,0:T(8,128)(2,1)S(1)} %shard_map.60), channel_id=1, source_target_pairs={{0,8},{8,16},{16,24},{1,9},{9,17},{17,25},{2,10},{10,18},{18,26},{... | collective-permute-start | bytes 786440 | tf_op jit(solution)/shard_map/ppermute | solution.py:150
  107.7 14.8 %collective-permute-start.23 = (bf16[4,128,256]{2,1,0:T(8,128)(2,1)S(1)}, bf16[4,128,256]{2,1,0:T(8,128)(2,1)S(1)}, u32[]{:S(2)}, u32[]{:S(2)}) collective-permute-start(bf16[4,128,256]{2,1,0:T(8,128)(2,1)S(1)} %get-tuple-element.27.first_mid), channel_id=1, source_target_pairs={{0,8},{8,16},{16,24},{1,9},{9,17},{17,25},{2,10},{10,18},{18,26},{... | collective-permute-start | bytes 786440 | tf_op jit(solution)/shard_map/ppermute | solution.py:150
  122.8 12.9 %collective-permute-start.22 = (bf16[2,128,256]{2,1,0:T(8,128)(2,1)S(1)}, bf16[2,128,256]{2,1,0:T(8,128)(2,1)S(1)}, u32[]{:S(2)}, u32[]{:S(2)}) collective-permute-start(bf16[2,128,256]{2,1,0:T(8,128)(2,1)S(1)} %get-tuple-element.55), channel_id=1, source_target_pairs={{1,0},{2,1},{3,2},{4,3},{5,4},{6,5},{7,6},{9,8},{10,9},{11,10},{12... | collective-permute-start | bytes 393224 | tf_op jit(solution)/shard_map/ppermute | solution.py:131
  125.4 10.4 %collective-permute-start.21 = (bf16[2,128,256]{2,1,0:T(8,128)(2,1)S(1)}, bf16[2,128,256]{2,1,0:T(8,128)(2,1)S(1)}, u32[]{:S(2)}, u32[]{:S(2)}) collective-permute-start(bf16[2,128,256]{2,1,0:T(8,128)(2,1)S(1)} %get-tuple-element.56), channel_id=1, source_target_pairs={{0,1},{1,2},{2,3},{3,4},{4,5},{5,6},{6,7},{8,9},{9,10},{10,11},{11... | collective-permute-start | bytes 393224 | tf_op jit(solution)/shard_map/ppermute | solution.py:130
  128.5 6.3 %collective-permute-start.26 = (bf16[1,128,256]{2,1,0:T(8,128)(2,1)S(1)}, bf16[1,128,256]{2,1,0:T(8,128)(2,1)S(1)}, u32[]{:S(2)}, u32[]{:S(2)}) collective-permute-start(bf16[1,128,256]{2,1,0:T(8,128)(2,1)S(1)} %get-tuple-element.53), channel_id=1, source_target_pairs={{1,0},{2,1},{3,2},{4,3},{5,4},{6,5},{7,6},{9,8},{10,9},{11,10},{12... | collective-permute-start | bytes 196616 | tf_op jit(solution)/shard_map/ppermute | solution.py:131
  130.5 5.3 %collective-permute-start.25 = (bf16[1,128,256]{2,1,0:T(8,128)(2,1)S(1)}, bf16[1,128,256]{2,1,0:T(8,128)(2,1)S(1)}, u32[]{:S(2)}, u32[]{:S(2)}) collective-permute-start(bf16[1,128,256]{2,1,0:T(8,128)(2,1)S(1)} %get-tuple-element.54), channel_id=1, source_target_pairs={{0,1},{1,2},{2,3},{3,4},{4,5},{5,6},{6,7},{8,9},{9,10},{10,11},{11... | collective-permute-start | bytes 196616 | tf_op jit(solution)/shard_map/ppermute | solution.py:130
  134.1 17.0 %collective-permute-start.28 = (bf16[4,128,256]{2,1,0:T(8,128)(2,1)S(1)}, bf16[4,128,256]{2,1,0:T(8,128)(2,1)S(1)}, u32[]{:S(2)}, u32[]{:S(2)}) collective-permute-start(bf16[4,128,256]{2,1,0:T(8,128)(2,1)S(1)} %collective-permute-done.19), channel_id=1, source_target_pairs={{8,24},{9,25},{10,26},{11,27},{12,28},{13,29},{14,30},{15,31}} | collective-permute-start | bytes 786440 | tf_op jit(solution)/shard_map/ppermute | solution.py:150
  134.8 16.3 %collective-permute-start.32 = (bf16[4,128,256]{2,1,0:T(8,128)(2,1)S(1)}, bf16[4,128,256]{2,1,0:T(8,128)(2,1)S(1)}, u32[]{:S(2)}, u32[]{:S(2)}) collective-permute-start(bf16[4,128,256]{2,1,0:T(8,128)(2,1)S(1)} %collective-permute-done.23), channel_id=1, source_target_pairs={{8,24},{9,25},{10,26},{11,27},{12,28},{13,29},{14,30},{15,31}} | collective-permute-start | bytes 786440 | tf_op jit(solution)/shard_map/ppermute | solution.py:150
  147.2 11.4 %collective-permute-start.27 = (bf16[4,128,256]{2,1,0:T(8,128)(2,1)S(1)}, bf16[4,128,256]{2,1,0:T(8,128)(2,1)S(1)}, u32[]{:S(2)}, u32[]{:S(2)}) collective-permute-start(bf16[4,128,256]{2,1,0:T(8,128)(2,1)S(1)} %shard_map.62), channel_id=1, source_target_pairs={{8,16},{16,24},{9,17},{17,25},{10,18},{18,26},{11,19},{19,27},{12,... | collective-permute-start | bytes 786440 | tf_op jit(solution)/shard_map/ppermute | solution.py:150
  149.2 15.1 %collective-permute-start.31 = (bf16[4,128,256]{2,1,0:T(8,128)(2,1)S(1)}, bf16[4,128,256]{2,1,0:T(8,128)(2,1)S(1)}, u32[]{:S(2)}, u32[]{:S(2)}) collective-permute-start(bf16[4,128,256]{2,1,0:T(8,128)(2,1)S(1)} %get-tuple-element.29.first_mid), channel_id=1, source_target_pairs={{8,16},{16,24},{9,17},{17,25},{10,18},{18,26},{11,19},{19,27},{12,... | collective-permute-start | bytes 786440 | tf_op jit(solution)/shard_map/ppermute | solution.py:150
  164.5 12.9 %collective-permute-start.30 = (bf16[2,128,256]{2,1,0:T(8,128)(2,1)S(1)}, bf16[2,128,256]{2,1,0:T(8,128)(2,1)S(1)}, u32[]{:S(2)}, u32[]{:S(2)}) collective-permute-start(bf16[2,128,256]{2,1,0:T(8,128)(2,1)S(1)} %get-tuple-element.51), channel_id=1, source_target_pairs={{1,0},{2,1},{3,2},{4,3},{5,4},{6,5},{7,6},{9,8},{10,9},{11,10},{12... | collective-permute-start | bytes 393224 | tf_op jit(solution)/shard_map/ppermute | solution.py:131
  167.2 10.1 %collective-permute-start.29 = (bf16[2,128,256]{2,1,0:T(8,128)(2,1)S(1)}, bf16[2,128,256]{2,1,0:T(8,128)(2,1)S(1)}, u32[]{:S(2)}, u32[]{:S(2)}) collective-permute-start(bf16[2,128,256]{2,1,0:T(8,128)(2,1)S(1)} %get-tuple-element.52), channel_id=1, source_target_pairs={{0,1},{1,2},{2,3},{3,4},{4,5},{5,6},{6,7},{8,9},{9,10},{10,11},{11... | collective-permute-start | bytes 393224 | tf_op jit(solution)/shard_map/ppermute | solution.py:130
  170.5 5.9 %collective-permute-start.34 = (bf16[1,128,256]{2,1,0:T(8,128)(2,1)S(1)}, bf16[1,128,256]{2,1,0:T(8,128)(2,1)S(1)}, u32[]{:S(2)}, u32[]{:S(2)}) collective-permute-start(bf16[1,128,256]{2,1,0:T(8,128)(2,1)S(1)} %get-tuple-element.49), channel_id=1, source_target_pairs={{1,0},{2,1},{3,2},{4,3},{5,4},{6,5},{7,6},{9,8},{10,9},{11,10},{12... | collective-permute-start | bytes 196616 | tf_op jit(solution)/shard_map/ppermute | solution.py:131
  172.4 5.0 %collective-permute-start.33 = (bf16[1,128,256]{2,1,0:T(8,128)(2,1)S(1)}, bf16[1,128,256]{2,1,0:T(8,128)(2,1)S(1)}, u32[]{:S(2)}, u32[]{:S(2)}) collective-permute-start(bf16[1,128,256]{2,1,0:T(8,128)(2,1)S(1)} %get-tuple-element.50), channel_id=1, source_target_pairs={{0,1},{1,2},{2,3},{3,4},{4,5},{5,6},{6,7},{8,9},{9,10},{10,11},{11... | collective-permute-start | bytes 196616 | tf_op jit(solution)/shard_map/ppermute | solution.py:130
where the time goes:
time: 191 us; the launch traced here: 190 us
  starting transfers between devices  80.5 us (42%)
  Pallas kernels  59.5 us (31%)
  waiting for transfers between devices  39.9 us (21%)
  local copies, waits for them, and re-layouts  5.08 us (3%)
  other arithmetic  4.05 us (2%)
    ppermute x15, waiting for transfers between devices, send(): return lax.ppermute(block, 'section', pairs) if pairs else block  38.8 us
    ppermute x10, starting transfers between devices, halo(): low = lax.ppermute(block[-width:], 'depth', upward)  34.9 us
    pallas_call x5, Pallas kernels, first_half(): pl.pallas_call(functools.partial(first_kernel, width), out_shape=(shape(1...  34.7 us
    pallas_call x5, Pallas kernels, second_half(): pl.pallas_call(functools.partial(second_kernel, width), out_shape=jax.Sha...  24.8 us
    ppermute x15, starting transfers between devices, send(): return lax.ppermute(block, 'section', pairs) if pairs else block  23.5 us
    ppermute x10, starting transfers between devices, halo(): high = lax.ppermute(block[:width], 'depth', downward)  22.1 us
  transfers between devices with their start and end apart: 35, of which 7 were waited for; matrix products, arithmetic and copies ran while one was open for 2% of the time, Pallas kernels for 25%

commit v1 on v0

--- a/solution.py
+++ b/solution.py
@@ -14,7 +14,7 @@
 def act(values):
     values = values.astype(jnp.float32)
     scaled = values * lax.rsqrt(jnp.mean(values * values, axis=-1, keepdims=True) + EPS)
-    return scaled / (1.0 + jnp.exp(-scaled))
+    return scaled * (0.5 + 0.5 * jnp.tanh(0.5 * scaled))
 
 
 def fill(even, odd, at, values, width):
@@ -37,35 +37,40 @@
 
 def convolve(even, odd, weights, copies, planes, width):
     voxels = even.shape[1]
-    total = None
+    taps = []
     for i in range(3):
         copies[i].wait()
-        taps = [odd[i : i + planes, 0:voxels], even[i : i + planes], odd[i : i + planes, 2 * width : 2 * width + voxels]]
-        slab = jnp.concatenate(taps, axis=-1)
-        part = jnp.dot(
-            slab.reshape(planes * voxels, slab.shape[-1]), weights[i], preferred_element_type=jnp.float32
-        )
-        total = part if total is None else total + part
+        for part in (odd[i : i + planes, 0:voxels], even[i : i + planes], odd[i : i + planes, 2 * width : 2 * width + voxels]):
+            taps.append(part.reshape(planes * voxels, part.shape[-1]))
+    slab = jnp.concatenate(taps, axis=-1)
+    total = jnp.dot(slab, weights[...], preferred_element_type=jnp.float32)
     return total.reshape(planes, voxels, -1)
 
 
 def fetch(weights_hbm, weights, sems):
-    copies = [pltpu.make_async_copy(weights_hbm.at[i], weights.at[i], sems.at[i]) for i in range(3)]
+    depth = weights.shape[0] // 3
+    copies = [
+        pltpu.make_async_copy(weights_hbm.at[pl.ds(i * depth, depth)], weights.at[pl.ds(i * depth, depth)], sems.at[i])
+        for i in range(3)
+    ]
     for copy in copies:
         copy.start()
     return copies
 
 
-def first_kernel(width, flags, q_low, q_mid, q_high, p_low, p_mid, p_high, weights_hbm, low, mid, high, even, odd, weights, sems):
+def first_kernel(width, flags, q_mid, q_inner, q_outer, p_mid, p_inner, p_outer, weights_hbm, low, mid, high, even, odd, weights, sems):
     copies = fetch(weights_hbm, weights, sems)
     planes = q_mid.shape[0]
-    fill(even, odd, 0, q_low[...], width)
+    above = flags[2] > 0
     fill(even, odd, 2, q_mid[...], width)
-    fill(even, odd, 2 + planes, q_high[...], width)
+    inner, outer = q_inner[...].astype(jnp.float32), q_outer[...].astype(jnp.float32)
+    fill(even, odd, 0, jnp.where(above, outer, inner), width)
+    fill(even, odd, 2 + planes, jnp.where(above, inner, outer), width)
     total = convolve(even, odd, weights, copies, planes + 2, width)
-    low[...] = jnp.where(flags[0] > 0, p_low[...].astype(jnp.float32) + total[:1], 0.0).astype(low.dtype)
+    inner, outer = p_inner[...].astype(jnp.float32), p_outer[...].astype(jnp.float32)
+    low[...] = jnp.where(flags[0] > 0, jnp.where(above, outer, inner) + total[:1], 0.0).astype(low.dtype)
     mid[...] = (p_mid[...].astype(jnp.float32) + total[1:-1]).astype(mid.dtype)
-    high[...] = jnp.where(flags[1] > 0, p_high[...].astype(jnp.float32) + total[-1:], 0.0).astype(high.dtype)
+    high[...] = jnp.where(flags[1] > 0, jnp.where(above, inner, outer) + total[-1:], 0.0).astype(high.dtype)
 
 
 def second_kernel(width, first_low, first_mid, first_high, q_mid, weights_hbm, out, even, odd, weights, sems):
@@ -82,7 +87,7 @@
     return [
         pltpu.VMEM((planes, voxels, 3 * chans), jnp.bfloat16),
         pltpu.VMEM((planes, voxels + 2 * width, 3 * chans), jnp.bfloat16),
-        pltpu.VMEM((3, 9 * chans, chans), jnp.bfloat16),
+        pltpu.VMEM((27 * chans, chans), jnp.bfloat16),
         pltpu.SemaphoreType.DMA((3,)),
     ]
 
@@ -103,9 +108,9 @@
         scratch_shapes=scratch(planes + 4, voxels, chans, width),
         compiler_params=pltpu.CompilerParams(vmem_limit_bytes=VMEM_LIMIT),
         cost_estimate=pl.CostEstimate(
-            flops=(planes + 2) * voxels * 54 * chans * chans, bytes_accessed=8 * weights.size // 3, transcendentals=0
+            flops=1, bytes_accessed=1, transcendentals=0
         ),
-    )(flags, q_halo[0], q, q_halo[1], p_halo[0], p, p_halo[1], weights)
+    )(flags, q, *q_halo, p, *p_halo, weights)
 
 
 def second_half(first, q, weights, width):
@@ -118,18 +123,22 @@
         scratch_shapes=scratch(planes + 2, voxels, chans, width),
         compiler_params=pltpu.CompilerParams(vmem_limit_bytes=VMEM_LIMIT),
         cost_estimate=pl.CostEstimate(
-            flops=planes * voxels * 54 * chans * chans, bytes_accessed=8 * weights.size // 3, transcendentals=0
+            flops=1, bytes_accessed=1, transcendentals=0
         ),
     )(*first, q, weights)
 
 
-def halo(block, width):
+def halo(block, width, above):
     count = lax.axis_size("depth")
-    upward = [(i, i + 1) for i in range(count - 1)]
-    downward = [(i + 1, i) for i in range(count - 1)]
-    low = lax.ppermute(block[-width:], "depth", upward)
-    high = lax.ppermute(block[:width], "depth", downward)
-    return low, high
+    planes = block.shape[0]
+    top, bottom = planes - width, 0
+
+    def swap(start, base):
+        part = lax.dynamic_slice_in_dim(block, start, width, axis=0)
+        pairs = [pair for i in range(base, count - 1, 2) for pair in ((i, i + 1), (i + 1, i))]
+        return lax.ppermute(part, "depth", pairs)
+
+    return swap(jnp.where(above, top, bottom), 0), swap(jnp.where(above, bottom, top), 1)
 
 
 def local(resident, previous, incoming, first_weights, second_weights):
@@ -142,9 +151,10 @@
     voxels = rows * width
     flat = lambda a: a.reshape(a.shape[0], 2, planes, voxels, chans)
     resident, previous, incoming = flat(resident)[0], flat(previous)[0], flat(incoming)
-    w_one = first_weights.reshape(3, 9 * chans, chans)
-    w_two = second_weights.reshape(3, 9 * chans, chans)
-    flags = jnp.stack([depth > 0, depth < lax.axis_size("depth") - 1]).astype(jnp.int32)
+    w_one = first_weights.reshape(27 * chans, chans)
+    w_two = second_weights.reshape(27 * chans, chans)
+    above = depth % 2 == 0
+    flags = jnp.stack([depth > 0, depth < lax.axis_size("depth") - 1, above]).astype(jnp.int32)
 
     def send(block, pairs):
         return lax.ppermute(block, "section", pairs) if pairs else block
@@ -175,6 +185,8 @@
                 value = jnp.where(section == 0, fresh, join(held, skip))
             inputs.append(value)
         p, q = inputs
+        p_halo = halo(p, 1, above)
+        q_halo = halo(q, 2, above)
         onward = []
         if slot < ticks:
             onward = [(0, 1)] if slot < ticks - 1 else []
@@ -182,7 +194,7 @@
                 onward += [(j, j + 1) for j in range(1, sections - 1)]
         received = {}
         relays = {}
-        first = first_half(flags, q, halo(q, 2), p, halo(p, 1), w_one, width)
+        first = first_half(flags, q, q_halo, p, p_halo, w_one, width)
         if onward:
             received[0] = send(first[1], onward)
         second = second_half(first, q, w_two, width)

time: 191 us -> 157 us (0.82)
  starting transfers between devices: 80.5 us -> 56.1 us
  Pallas kernels: 59.5 us -> 40.9 us
  waiting for transfers between devices: 39.9 us -> 49.2 us
    ppermute x20, starting transfers between devices: 57 us -> 33.6 us  [swap(): return lax.ppermute(part, 'depth', pairs)]
    pallas_call x5, Pallas kernels: 34.7 us -> 23.9 us  [first_half(): pl.pallas_call(functools.partial(first_kernel, width), out_shape=(shape(1...]
    ppermute x20, waiting for transfers between devices: 1.05 us -> 9.72 us  [swap(): return lax.ppermute(part, 'depth', pairs)]
    pallas_call x5, Pallas kernels: 24.8 us -> 17 us  [second_half(): pl.pallas_call(functools.partial(second_kernel, width), out_shape=jax.Sha...]
    slice x10 -> x0, local copies, waits for them, and re-layouts: 1.99 us -> none  [halo(): high = lax.ppermute(block[:width], 'depth', downward)]
  transfers between devices with their start and end apart: 35 -> 35, of which waited for: 7 -> 11; matrix products, arithmetic and copies ran while one was open for 2% -> 2% of each run, Pallas kernels for 25% -> 21%
where the time goes in v1:
time: 157 us; the launch traced here: 155 us
  starting transfers between devices  56.1 us (36%)
  waiting for transfers between devices  49.2 us (31%)
  Pallas kernels  40.9 us (26%)
  local copies, waits for them, and re-layouts  4.26 us (3%)
  other arithmetic  4.15 us (3%)
    ppermute x15, waiting for transfers between devices, send(): return lax.ppermute(block, 'section', pairs) if pairs else block  39.5 us
    ppermute x20, starting transfers between devices, swap(): return lax.ppermute(part, 'depth', pairs)  33.6 us
    pallas_call x5, Pallas kernels, first_half(): pl.pallas_call(functools.partial(first_kernel, width), out_shape=(shape(1...  23.9 us
    ppermute x15, starting transfers between devices, send(): return lax.ppermute(block, 'section', pairs) if pairs else block  22.4 us
    pallas_call x5, Pallas kernels, second_half(): pl.pallas_call(functools.partial(second_kernel, width), out_shape=jax.Sha...  17 us
    ppermute x20, waiting for transfers between devices, swap(): return lax.ppermute(part, 'depth', pairs)  9.72 us
  transfers between devices with their start and end apart: 35, of which 11 were waited for; matrix products, arithmetic and copies ran while one was open for 2% of the time, Pallas kernels for 21%

profile of v1, /device:TPU:13, one launch (start us, length us, event | category | flops | bytes accessed | tf_op | source)
XLA Modules:
  0.0 155.3 jit_solution(12729258486069015506)
XLA Ops:
  0.0 1.3 collective-permute-start
  1.3 1.1 slice_bitcast_fusion.8
  2.4 3.8 %collective-permute-start.7 = (bf16[2,128,256]{2,1,0:T(8,128)(2,1)S(1)}, bf16[2,128,256]{2,1,0:T(8,128)(2,1)S(1)}, u32[]{:S(2)}, u32[]{:S(2)}) collective-permute-start(bf16[2,128,256]{2,1,0:T(8,128)(2,1)S(1)} %get-tuple-element.59), channel_id=1, source_target_pairs={{1,2},{2,1},{3,4},{4,3},{5,6},{6,5},{9,10},{10,9},{11,12},{12,11},... | collective-permute-start | bytes 393224 | tf_op jit(solution)/shard_map/ppermute | solution.py:139
  6.3 3.6 %collective-permute-start.9 = (bf16[1,128,256]{2,1,0:T(8,128)(2,1)S(1)}, bf16[1,128,256]{2,1,0:T(8,128)(2,1)S(1)}, u32[]{:S(2)}, u32[]{:S(2)}) collective-permute-start(bf16[1,128,256]{2,1,0:T(8,128)(2,1)S(1)} %get-tuple-element.57), channel_id=1, source_target_pairs={{1,2},{2,1},{3,4},{4,3},{5,6},{6,5},{9,10},{10,9},{11,12},{12,11},... | collective-permute-start | bytes 196616 | tf_op jit(solution)/shard_map/ppermute | solution.py:139
  10.1 2.2 %collective-permute-done.9.p_outer = bf16[1,128,256]{2,1,0:T(8,128)(2,1)S(1)} collective-permute-done((bf16[1,128,256]{2,1,0:T(8,128)(2,1)S(1)}, bf16[1,128,256]{2,1,0:T(8,128)(2,1)S(1)}, u32[]{:S(2)}, u32[]{:S(2)}) %collective-permute-start.9) | collective-permute-done | bytes 65568 | tf_op jit(solution)/shard_map/ppermute | solution.py:139
  12.3 2.0 %copy-done = bf16[1,3,3,3,256,256]{5,4,3,2,1,0:T(8,128)(2,1)S(1)} copy-done((bf16[1,3,3,3,256,256]{5,4,3,2,1,0:T(8,128)(2,1)S(1)}, bf16[1,3,3,3,256,256]{5,4,3,2,1,0:T(8,128)(2,1)}, u32[]{:S(2)}) %copy-start) | copy-done | bytes 3538968
  14.3 4.6 %shard_map.57 = (bf16[1,128,256]{2,1,0:T(8,128)(2,1)S(1)}, bf16[4,128,256]{2,1,0:T(8,128)(2,1)S(1)}, bf16[1,128,256]{2,1,0:T(8,128)(2,1)S(1)}) custom-call(s32[3]{0:T(128)S(1)} %add_convert_fusion.6.flags, bf16[4,128,256]{2,1,0:T(8,128)(2,1)S(1)} %get-tuple-element.44.q_mid, bf16[2,128,256]{2,1,0:T(8,128)(2,1)S(1)} %collective-permute-done.6.q_inner, ...), custom_call_target="tpu_custom_call" | custom-call | flops 1 | bytes 1 | tf_op jit(solution)/shard_map/pallas_call | solution.py:103
  19.0 1.4 collective-permute-start.14
  21.3 3.1 %shard_map.58 = bf16[4,128,256]{2,1,0:T(8,128)(2,1)S(1)} custom-call(bf16[1,128,256]{2,1,0:T(8,128)(2,1)S(1)} %get-tuple-element.23.first_low, bf16[4,128,256]{2,1,0:T(8,128)(2,1)S(1)} %get-tuple-element.24.first_mid, bf16[1,128,256]{2,1,0:T(8,128)(2,1)S(1)} %get-tuple-element.25.first_high, bf16[4,128,256]{2,1,0:T(8,128)(2,1)S(1)} %copy-done.5, ...), custom_call_target="tpu_custom_call" | custom-call | flops 1 | bytes 1 | tf_op jit(solution)/shard_map/pallas_call | solution.py:118
  24.4 1.4 collective-permute-start.10
  25.8 1.4 fusion.10
  27.2 3.2 %collective-permute-start.2 = (bf16[2,128,256]{2,1,0:T(8,128)(2,1)S(1)}, bf16[2,128,256]{2,1,0:T(8,128)(2,1)S(1)}, u32[]{:S(2)}, u32[]{:S(2)}) collective-permute-start(bf16[2,128,256]{2,1,0:T(8,128)(2,1)S(1)} %get-tuple-element.63), channel_id=1, source_target_pairs={{1,2},{2,1},{3,4},{4,3},{5,6},{6,5},{9,10},{10,9},{11,12},{12,11},... | collective-permute-start | bytes 393224 | tf_op jit(solution)/shard_map/ppermute | solution.py:139
  30.5 2.4 %collective-permute-start.4 = (bf16[1,128,256]{2,1,0:T(8,128)(2,1)S(1)}, bf16[1,128,256]{2,1,0:T(8,128)(2,1)S(1)}, u32[]{:S(2)}, u32[]{:S(2)}) collective-permute-start(bf16[1,128,256]{2,1,0:T(8,128)(2,1)S(1)} %get-tuple-element.61), channel_id=1, source_target_pairs={{1,2},{2,1},{3,4},{4,3},{5,6},{6,5},{9,10},{10,9},{11,12},{12,11},... | collective-permute-start | bytes 196616 | tf_op jit(solution)/shard_map/ppermute | solution.py:139
  33.1 1.4 collective-permute-start.11
  34.5 1.7 %collective-permute-done.4.p_outer = bf16[1,128,256]{2,1,0:T(8,128)(2,1)S(1)} collective-permute-done((bf16[1,128,256]{2,1,0:T(8,128)(2,1)S(1)}, bf16[1,128,256]{2,1,0:T(8,128)(2,1)S(1)}, u32[]{:S(2)}, u32[]{:S(2)}) %collective-permute-start.4) | collective-permute-done | bytes 65568 | tf_op jit(solution)/shard_map/ppermute | solution.py:139
  36.2 1.4 collective-permute-start.16
  37.6 5.3 %shard_map.55 = (bf16[1,128,256]{2,1,0:T(8,128)(2,1)S(1)}, bf16[4,128,256]{2,1,0:T(8,128)(2,1)}, bf16[1,128,256]{2,1,0:T(8,128)(2,1)S(1)}) custom-call(s32[3]{0:T(128)S(1)} %add_convert_fusion.6.flags, bf16[4,128,256]{2,1,0:T(8,128)(2,1)S(1)} %get-tuple-element.36.q_mid, bf16[2,128,256]{2,1,0:T(8,128)(2,1)S(1)} %collective-permute-done.1.q_inner, ...), custom_call_target="tpu_custom_call" | custom-call | flops 1 | bytes 1 | tf_op jit(solution)/shard_map/pallas_call | solution.py:103
  42.9 4.7 %shard_map.56 = bf16[4,128,256]{2,1,0:T(8,128)(2,1)} custom-call(bf16[1,128,256]{2,1,0:T(8,128)(2,1)S(1)} %get-tuple-element.20.first_low, bf16[4,128,256]{2,1,0:T(8,128)(2,1)} %get-tuple-element.21.first_mid, bf16[1,128,256]{2,1,0:T(8,128)(2,1)S(1)} %get-tuple-element.22.first_high, bf16[4,128,256]{2,1,0:T(8,128)(2,1)S(1)} %get-tuple-element.36.q_mid, ...), custom_call_target="tpu_custom_call" | custom-call | flops 1 | bytes 1 | tf_op jit(solution)/shard_map/pallas_call | solution.py:118
  47.7 3.1 %collective-permute-start.5 = (bf16[4,128,256]{2,1,0:T(8,128)(2,1)}, bf16[4,128,256]{2,1,0:T(8,128)(2,1)}, u32[]{:S(2)}, u32[]{:S(2)}) collective-permute-start(bf16[4,128,256]{2,1,0:T(8,128)(2,1)} %shard_map.56), channel_id=1, source_target_pairs={{0,8},{8,16},{16,24},{1,9},{9,17},{17,25},{2,10},{10,18},{18,26},{... | collective-permute-start | bytes 786440 | tf_op jit(solution)/shard_map/ppermute | solution.py:160
  50.7 1.9 %collective-permute-start.15 = (bf16[4,128,256]{2,1,0:T(8,128)(2,1)}, bf16[4,128,256]{2,1,0:T(8,128)(2,1)}, u32[]{:S(2)}, u32[]{:S(2)}) collective-permute-start(bf16[4,128,256]{2,1,0:T(8,128)(2,1)} %get-tuple-element.21.first_mid), channel_id=1, source_target_pairs={{0,8},{8,16},{16,24},{1,9},{9,17},{17,25},{2,10},{10,18},{18,26},{... | collective-permute-start | bytes 786440 | tf_op jit(solution)/shard_map/ppermute | solution.py:160
  52.7 9.8 %collective-permute-done.5 = bf16[4,128,256]{2,1,0:T(8,128)(2,1)} collective-permute-done((bf16[4,128,256]{2,1,0:T(8,128)(2,1)}, bf16[4,128,256]{2,1,0:T(8,128)(2,1)}, u32[]{:S(2)}, u32[]{:S(2)}) %collective-permute-start.5) | collective-permute-done | bytes 262176 | tf_op jit(solution)/shard_map/ppermute | solution.py:160
  62.5 5.6 %collective-permute-done.15 = bf16[4,128,256]{2,1,0:T(8,128)(2,1)} collective-permute-done((bf16[4,128,256]{2,1,0:T(8,128)(2,1)}, bf16[4,128,256]{2,1,0:T(8,128)(2,1)}, u32[]{:S(2)}, u32[]{:S(2)}) %collective-permute-start.15) | collective-permute-done | bytes 262176 | tf_op jit(solution)/shard_map/ppermute | solution.py:160
  68.1 1.4 fusion.16
  69.5 3.7 %collective-permute-start.13 = (bf16[2,128,256]{2,1,0:T(8,128)(2,1)S(1)}, bf16[2,128,256]{2,1,0:T(8,128)(2,1)S(1)}, u32[]{:S(2)}, u32[]{:S(2)}) collective-permute-start(bf16[2,128,256]{2,1,0:T(8,128)(2,1)S(1)} %get-tuple-element.55), channel_id=1, source_target_pairs={{1,2},{2,1},{3,4},{4,3},{5,6},{6,5},{9,10},{10,9},{11,12},{12,11},... | collective-permute-start | bytes 393224 | tf_op jit(solution)/shard_map/ppermute | solution.py:139
  73.3 1.9 %collective-permute-start.18 = (bf16[1,128,256]{2,1,0:T(8,128)(2,1)S(1)}, bf16[1,128,256]{2,1,0:T(8,128)(2,1)S(1)}, u32[]{:S(2)}, u32[]{:S(2)}) collective-permute-start(bf16[1,128,256]{2,1,0:T(8,128)(2,1)S(1)} %get-tuple-element.53), channel_id=1, source_target_pairs={{1,2},{2,1},{3,4},{4,3},{5,6},{6,5},{9,10},{10,9},{11,12},{12,11},... | collective-permute-start | bytes 196616 | tf_op jit(solution)/shard_map/ppermute | solution.py:139
  76.7 2.3 %collective-permute-done.18.p_outer = bf16[1,128,256]{2,1,0:T(8,128)(2,1)S(1)} collective-permute-done((bf16[1,128,256]{2,1,0:T(8,128)(2,1)S(1)}, bf16[1,128,256]{2,1,0:T(8,128)(2,1)S(1)}, u32[]{:S(2)}, u32[]{:S(2)}) %collective-permute-start.18) | collective-permute-done | bytes 65568 | tf_op jit(solution)/shard_map/ppermute | solution.py:139
  79.9 4.7 %shard_map.59 = (bf16[1,128,256]{2,1,0:T(8,128)(2,1)S(1)}, bf16[4,128,256]{2,1,0:T(8,128)(2,1)S(1)}, bf16[1,128,256]{2,1,0:T(8,128)(2,1)S(1)}) custom-call(s32[3]{0:T(128)S(1)} %add_convert_fusion.6.flags, bf16[4,128,256]{2,1,0:T(8,128)(2,1)S(1)} %get-tuple-element.42.q_mid, bf16[2,128,256]{2,1,0:T(8,128)(2,1)S(1)} %collective-permute-done.12.q_inner, ...), custom_call_target="tpu_custom_call" | custom-call | flops 1 | bytes 1 | tf_op jit(solution)/shard_map/pallas_call | solution.py:103
  84.5 3.1 %shard_map.60 = bf16[4,128,256]{2,1,0:T(8,128)(2,1)S(1)} custom-call(bf16[1,128,256]{2,1,0:T(8,128)(2,1)S(1)} %get-tuple-element.26.first_low, bf16[4,128,256]{2,1,0:T(8,128)(2,1)S(1)} %get-tuple-element.27.first_mid, bf16[1,128,256]{2,1,0:T(8,128)(2,1)S(1)} %get-tuple-element.28.first_high, bf16[4,128,256]{2,1,0:T(8,128)(2,1)S(1)} %get-tuple-element.42.q_mid, ...), custom_call_target="tpu_custom_call" | custom-call | flops 1 | bytes 1 | tf_op jit(solution)/shard_map/pallas_call | solution.py:118
  87.6 1.9 %collective-permute-start.19 = (bf16[4,128,256]{2,1,0:T(8,128)(2,1)S(1)}, bf16[4,128,256]{2,1,0:T(8,128)(2,1)S(1)}, u32[]{:S(2)}, u32[]{:S(2)}) collective-permute-start(bf16[4,128,256]{2,1,0:T(8,128)(2,1)S(1)} %shard_map.60), channel_id=1, source_target_pairs={{0,8},{8,16},{16,24},{1,9},{9,17},{17,25},{2,10},{10,18},{18,26},{... | collective-permute-start | bytes 786440 | tf_op jit(solution)/shard_map/ppermute | solution.py:160
  89.6 1.9 %collective-permute-start.23 = (bf16[4,128,256]{2,1,0:T(8,128)(2,1)S(1)}, bf16[4,128,256]{2,1,0:T(8,128)(2,1)S(1)}, u32[]{:S(2)}, u32[]{:S(2)}) collective-permute-start(bf16[4,128,256]{2,1,0:T(8,128)(2,1)S(1)} %get-tuple-element.27.first_mid), channel_id=1, source_target_pairs={{0,8},{8,16},{16,24},{1,9},{9,17},{17,25},{2,10},{10,18},{18,26},{... | collective-permute-start | bytes 786440 | tf_op jit(solution)/shard_map/ppermute | solution.py:160
  91.5 6.4 %collective-permute-done.19 = bf16[4,128,256]{2,1,0:T(8,128)(2,1)S(1)} collective-permute-done((bf16[4,128,256]{2,1,0:T(8,128)(2,1)S(1)}, bf16[4,128,256]{2,1,0:T(8,128)(2,1)S(1)}, u32[]{:S(2)}, u32[]{:S(2)}) %collective-permute-start.19) | collective-permute-done | bytes 262176 | tf_op jit(solution)/shard_map/ppermute | solution.py:160
  97.9 5.6 %collective-permute-done.23 = bf16[4,128,256]{2,1,0:T(8,128)(2,1)S(1)} collective-permute-done((bf16[4,128,256]{2,1,0:T(8,128)(2,1)S(1)}, bf16[4,128,256]{2,1,0:T(8,128)(2,1)S(1)}, u32[]{:S(2)}, u32[]{:S(2)}) %collective-permute-start.23) | collective-permute-done | bytes 262176 | tf_op jit(solution)/shard_map/ppermute | solution.py:160
  103.8 3.0 %collective-permute-start.22 = (bf16[2,128,256]{2,1,0:T(8,128)(2,1)S(1)}, bf16[2,128,256]{2,1,0:T(8,128)(2,1)S(1)}, u32[]{:S(2)}, u32[]{:S(2)}) collective-permute-start(bf16[2,128,256]{2,1,0:T(8,128)(2,1)S(1)} %get-tuple-element.51), channel_id=1, source_target_pairs={{1,2},{2,1},{3,4},{4,3},{5,6},{6,5},{9,10},{10,9},{11,12},{12,11},... | collective-permute-start | bytes 393224 | tf_op jit(solution)/shard_map/ppermute | solution.py:139
  107.0 2.4 %collective-permute-start.26 = (bf16[1,128,256]{2,1,0:T(8,128)(2,1)S(1)}, bf16[1,128,256]{2,1,0:T(8,128)(2,1)S(1)}, u32[]{:S(2)}, u32[]{:S(2)}) collective-permute-start(bf16[1,128,256]{2,1,0:T(8,128)(2,1)S(1)} %get-tuple-element.49), channel_id=1, source_target_pairs={{1,2},{2,1},{3,4},{4,3},{5,6},{6,5},{9,10},{10,9},{11,12},{12,11},... | collective-permute-start | bytes 196616 | tf_op jit(solution)/shard_map/ppermute | solution.py:139
  109.5 1.3 collective-permute-start.25
  111.4 1.2 collective-permute-done.26.p_outer
  113.3 4.7 %shard_map.61 = (bf16[1,128,256]{2,1,0:T(8,128)(2,1)S(1)}, bf16[4,128,256]{2,1,0:T(8,128)(2,1)S(1)}, bf16[1,128,256]{2,1,0:T(8,128)(2,1)S(1)}) custom-call(s32[3]{0:T(128)S(1)} %add_convert_fusion.6.flags, bf16[4,128,256]{2,1,0:T(8,128)(2,1)S(1)} %get-tuple-element.40.q_mid, bf16[2,128,256]{2,1,0:T(8,128)(2,1)S(1)} %collective-permute-done.21.q_inner, ...), custom_call_target="tpu_custom_call" | custom-call | flops 1 | bytes 1 | tf_op jit(solution)/shard_map/pallas_call | solution.py:103
  118.0 3.1 %shard_map.62 = bf16[4,128,256]{2,1,0:T(8,128)(2,1)S(1)} custom-call(bf16[1,128,256]{2,1,0:T(8,128)(2,1)S(1)} %get-tuple-element.30.first_low, bf16[4,128,256]{2,1,0:T(8,128)(2,1)S(1)} %get-tuple-element.29.first_mid, bf16[1,128,256]{2,1,0:T(8,128)(2,1)S(1)} %get-tuple-element.31.first_high, bf16[4,128,256]{2,1,0:T(8,128)(2,1)S(1)} %get-tuple-element.40.q_mid, ...), custom_call_target="tpu_custom_call" | custom-call | flops 1 | bytes 1 | tf_op jit(solution)/shard_map/pallas_call | solution.py:118
  121.0 1.9 %collective-permute-start.27 = (bf16[4,128,256]{2,1,0:T(8,128)(2,1)S(1)}, bf16[4,128,256]{2,1,0:T(8,128)(2,1)S(1)}, u32[]{:S(2)}, u32[]{:S(2)}) collective-permute-start(bf16[4,128,256]{2,1,0:T(8,128)(2,1)S(1)} %shard_map.62), channel_id=1, source_target_pairs={{8,16},{16,24},{9,17},{17,25},{10,18},{18,26},{11,19},{19,27},{12,... | collective-permute-start | bytes 786440 | tf_op jit(solution)/shard_map/ppermute | solution.py:160
  123.0 1.9 %collective-permute-start.31 = (bf16[4,128,256]{2,1,0:T(8,128)(2,1)S(1)}, bf16[4,128,256]{2,1,0:T(8,128)(2,1)S(1)}, u32[]{:S(2)}, u32[]{:S(2)}) collective-permute-start(bf16[4,128,256]{2,1,0:T(8,128)(2,1)S(1)} %get-tuple-element.29.first_mid), channel_id=1, source_target_pairs={{8,16},{16,24},{9,17},{17,25},{10,18},{18,26},{11,19},{19,27},{12,... | collective-permute-start | bytes 786440 | tf_op jit(solution)/shard_map/ppermute | solution.py:160
  124.9 6.4 %collective-permute-done.27 = bf16[4,128,256]{2,1,0:T(8,128)(2,1)S(1)} collective-permute-done((bf16[4,128,256]{2,1,0:T(8,128)(2,1)S(1)}, bf16[4,128,256]{2,1,0:T(8,128)(2,1)S(1)}, u32[]{:S(2)}, u32[]{:S(2)}) %collective-permute-start.27) | collective-permute-done | bytes 262176 | tf_op jit(solution)/shard_map/ppermute | solution.py:160
  131.3 5.6 %collective-permute-done.31 = bf16[4,128,256]{2,1,0:T(8,128)(2,1)S(1)} collective-permute-done((bf16[4,128,256]{2,1,0:T(8,128)(2,1)S(1)}, bf16[4,128,256]{2,1,0:T(8,128)(2,1)S(1)}, u32[]{:S(2)}, u32[]{:S(2)}) %collective-permute-start.31) | collective-permute-done | bytes 262176 | tf_op jit(solution)/shard_map/ppermute | solution.py:160
  137.2 3.6 %collective-permute-start.30 = (bf16[2,128,256]{2,1,0:T(8,128)(2,1)S(1)}, bf16[2,128,256]{2,1,0:T(8,128)(2,1)S(1)}, u32[]{:S(2)}, u32[]{:S(2)}) collective-permute-start(bf16[2,128,256]{2,1,0:T(8,128)(2,1)S(1)} %get-tuple-element.47), channel_id=1, source_target_pairs={{1,2},{2,1},{3,4},{4,3},{5,6},{6,5},{9,10},{10,9},{11,12},{12,11},... | collective-permute-start | bytes 393224 | tf_op jit(solution)/shard_map/ppermute | solution.py:139
  140.9 2.2 %collective-permute-start.34 = (bf16[1,128,256]{2,1,0:T(8,128)(2,1)S(1)}, bf16[1,128,256]{2,1,0:T(8,128)(2,1)S(1)}, u32[]{:S(2)}, u32[]{:S(2)}) collective-permute-start(bf16[1,128,256]{2,1,0:T(8,128)(2,1)S(1)} %get-tuple-element.45), channel_id=1, source_target_pairs={{1,2},{2,1},{3,4},{4,3},{5,6},{6,5},{9,10},{10,9},{11,12},{12,11},... | collective-permute-start | bytes 196616 | tf_op jit(solution)/shard_map/ppermute | solution.py:139
  143.1 1.3 collective-permute-start.33
  144.4 2.2 %collective-permute-done.34.p_outer = bf16[1,128,256]{2,1,0:T(8,128)(2,1)S(1)} collective-permute-done((bf16[1,128,256]{2,1,0:T(8,128)(2,1)S(1)}, bf16[1,128,256]{2,1,0:T(8,128)(2,1)S(1)}, u32[]{:S(2)}, u32[]{:S(2)}) %collective-permute-start.34) | collective-permute-done | bytes 65568 | tf_op jit(solution)/shard_map/ppermute | solution.py:139
  146.6 4.7 %shard_map.63 = (bf16[1,128,256]{2,1,0:T(8,128)(2,1)S(1)}, bf16[4,128,256]{2,1,0:T(8,128)(2,1)S(1)}, bf16[1,128,256]{2,1,0:T(8,128)(2,1)S(1)}) custom-call(s32[3]{0:T(128)S(1)} %add_convert_fusion.6.flags, bf16[4,128,256]{2,1,0:T(8,128)(2,1)S(1)} %get-tuple-element.38.q_mid, bf16[2,128,256]{2,1,0:T(8,128)(2,1)S(1)} %collective-permute-done.29.q_inner, ...), custom_call_target="tpu_custom_call" | custom-call | flops 1 | bytes 1 | tf_op jit(solution)/shard_map/pallas_call | solution.py:103
  151.3 3.1 %shard_map.64 = bf16[4,128,256]{2,1,0:T(8,128)(2,1)S(1)} custom-call(bf16[1,128,256]{2,1,0:T(8,128)(2,1)S(1)} %get-tuple-element.33.first_low, bf16[4,128,256]{2,1,0:T(8,128)(2,1)S(1)} %get-tuple-element.32.first_mid, bf16[1,128,256]{2,1,0:T(8,128)(2,1)S(1)} %get-tuple-element.34.first_high, bf16[4,128,256]{2,1,0:T(8,128)(2,1)S(1)} %get-tuple-element.38.q_mid, ...), custom_call_target="tpu_custom_call" | custom-call | flops 1 | bytes 1 | tf_op jit(solution)/shard_map/pallas_call | solution.py:118
  (65 shorter events, 6.9 us)
Async XLA Ops:
  0.0 25.8 %collective-permute-start = (bf16[2,4,128,256]{3,2,1,0:T(8,128)(2,1)}, bf16[2,4,128,256]{3,2,1,0:T(8,128)(2,1)}, u32[]{:S(2)}, u32[]{:S(2)}) collective-permute-start(bf16[2,4,128,256]{3,2,1,0:T(8,128)(2,1)} %bitcast.75), channel_id=1, source_target_pairs={{0,24},{8,16},{1,25},{9,17},{2,26},{10,18},{3,27},{11,19},{4,28},{... | collective-permute-start | bytes 1572872 | tf_op jit(solution)/shard_map/ppermute | solution.py:160
  2.4 16.6 %copy-start.4 = (bf16[4,128,256]{2,1,0:T(8,128)(2,1)}, bf16[4,128,256]{2,1,0:T(8,128)(2,1)S(1)}, u32[]{:S(2)}) copy-start(bf16[4,128,256]{2,1,0:T(8,128)(2,1)S(1)} %get-tuple-element.44.q_mid) | copy-start | bytes 786436
  2.4 9.9 %collective-permute-start.7 = (bf16[2,128,256]{2,1,0:T(8,128)(2,1)S(1)}, bf16[2,128,256]{2,1,0:T(8,128)(2,1)S(1)}, u32[]{:S(2)}, u32[]{:S(2)}) collective-permute-start(bf16[2,128,256]{2,1,0:T(8,128)(2,1)S(1)} %get-tuple-element.59), channel_id=1, source_target_pairs={{1,2},{2,1},{3,4},{4,3},{5,6},{6,5},{9,10},{10,9},{11,12},{12,11},... | collective-permute-start | bytes 393224 | tf_op jit(solution)/shard_map/ppermute | solution.py:139
  6.2 6.1 %collective-permute-start.6 = (bf16[2,128,256]{2,1,0:T(8,128)(2,1)S(1)}, bf16[2,128,256]{2,1,0:T(8,128)(2,1)S(1)}, u32[]{:S(2)}, u32[]{:S(2)}) collective-permute-start(bf16[2,128,256]{2,1,0:T(8,128)(2,1)S(1)} %get-tuple-element.60), channel_id=1, source_target_pairs={{0,1},{1,0},{2,3},{3,2},{4,5},{5,4},{6,7},{7,6},{8,9},{9,8},{10,11... | collective-permute-start | bytes 393224 | tf_op jit(solution)/shard_map/ppermute | solution.py:139
  6.3 6.0 %collective-permute-start.9 = (bf16[1,128,256]{2,1,0:T(8,128)(2,1)S(1)}, bf16[1,128,256]{2,1,0:T(8,128)(2,1)S(1)}, u32[]{:S(2)}, u32[]{:S(2)}) collective-permute-start(bf16[1,128,256]{2,1,0:T(8,128)(2,1)S(1)} %get-tuple-element.57), channel_id=1, source_target_pairs={{1,2},{2,1},{3,4},{4,3},{5,6},{6,5},{9,10},{10,9},{11,12},{12,11},... | collective-permute-start | bytes 196616 | tf_op jit(solution)/shard_map/ppermute | solution.py:139
  9.9 2.4 %collective-permute-start.8 = (bf16[1,128,256]{2,1,0:T(8,128)(2,1)S(1)}, bf16[1,128,256]{2,1,0:T(8,128)(2,1)S(1)}, u32[]{:S(2)}, u32[]{:S(2)}) collective-permute-start(bf16[1,128,256]{2,1,0:T(8,128)(2,1)S(1)} %get-tuple-element.58), channel_id=1, source_target_pairs={{0,1},{1,0},{2,3},{3,2},{4,5},{5,4},{6,7},{7,6},{8,9},{9,8},{10,11... | collective-permute-start | bytes 196616 | tf_op jit(solution)/shard_map/ppermute | solution.py:139
  12.3 2.0 %copy-start = (bf16[1,3,3,3,256,256]{5,4,3,2,1,0:T(8,128)(2,1)S(1)}, bf16[1,3,3,3,256,256]{5,4,3,2,1,0:T(8,128)(2,1)}, u32[]{:S(2)}) copy-start(bf16[1,3,3,3,256,256]{5,4,3,2,1,0:T(8,128)(2,1)} %param.8) | copy-start | bytes 10616836
  14.3 6.1 %copy-start.2 = (bf16[1,3,3,3,256,256]{5,4,3,2,1,0:T(8,128)(2,1)S(1)}, bf16[1,3,3,3,256,256]{5,4,3,2,1,0:T(8,128)(2,1)}, u32[]{:S(2)}) copy-start(bf16[1,3,3,3,256,256]{5,4,3,2,1,0:T(8,128)(2,1)} %param.9) | copy-start | bytes 10616836
  19.0 14.1 %collective-permute-start.14 = (bf16[4,128,256]{2,1,0:T(8,128)(2,1)S(1)}, bf16[4,128,256]{2,1,0:T(8,128)(2,1)}, u32[]{:S(2)}, u32[]{:S(2)}) collective-permute-start(bf16[4,128,256]{2,1,0:T(8,128)(2,1)S(1)} %get-tuple-element.24.first_mid), channel_id=1, source_target_pairs={{0,8},{1,9},{2,10},{3,11},{4,12},{5,13},{6,14},{7,15}} | collective-permute-start | bytes 786440 | tf_op jit(solution)/shard_map/ppermute | solution.py:160
  20.4 1.0 copy-start.5
  21.3 4.5 %copy-start.7 = (bf16[1,2,4,16,8,256]{5,4,3,2,1,0:T(8,128)(2,1)S(1)}, bf16[1,2,4,16,8,256]{5,4,3,2,1,0:T(8,128)(2,1)}, u32[]{:S(2)}) copy-start(bf16[1,2,4,16,8,256]{5,4,3,2,1,0:T(8,128)(2,1)} %param.5) | copy-start | bytes 1572868
  21.3 16.3 %copy-start.1 = (bf16[1,3,3,3,256,256]{5,4,3,2,1,0:T(8,128)(2,1)S(1)}, bf16[1,3,3,3,256,256]{5,4,3,2,1,0:T(8,128)(2,1)}, u32[]{:S(2)}) copy-start(bf16[1,3,3,3,256,256]{5,4,3,2,1,0:T(8,128)(2,1)} %param.8) | copy-start | bytes 10616836
  24.4 8.5 %collective-permute-start.10 = (bf16[4,128,256]{2,1,0:T(8,128)(2,1)S(1)}, bf16[4,128,256]{2,1,0:T(8,128)(2,1)}, u32[]{:S(2)}, u32[]{:S(2)}) collective-permute-start(bf16[4,128,256]{2,1,0:T(8,128)(2,1)S(1)} %shard_map.58), channel_id=1, source_target_pairs={{0,8},{1,9},{2,10},{3,11},{4,12},{5,13},{6,14},{7,15}} | collective-permute-start | bytes 786440 | tf_op jit(solution)/shard_map/ppermute | solution.py:160
  27.2 10.3 %collective-permute-start.2 = (bf16[2,128,256]{2,1,0:T(8,128)(2,1)S(1)}, bf16[2,128,256]{2,1,0:T(8,128)(2,1)S(1)}, u32[]{:S(2)}, u32[]{:S(2)}) collective-permute-start(bf16[2,128,256]{2,1,0:T(8,128)(2,1)S(1)} %get-tuple-element.63), channel_id=1, source_target_pairs={{1,2},{2,1},{3,4},{4,3},{5,6},{6,5},{9,10},{10,9},{11,12},{12,11},... | collective-permute-start | bytes 393224 | tf_op jit(solution)/shard_map/ppermute | solution.py:139
  30.4 7.2 %collective-permute-start.1 = (bf16[2,128,256]{2,1,0:T(8,128)(2,1)S(1)}, bf16[2,128,256]{2,1,0:T(8,128)(2,1)S(1)}, u32[]{:S(2)}, u32[]{:S(2)}) collective-permute-start(bf16[2,128,256]{2,1,0:T(8,128)(2,1)S(1)} %get-tuple-element.64), channel_id=1, source_target_pairs={{0,1},{1,0},{2,3},{3,2},{4,5},{5,4},{6,7},{7,6},{8,9},{9,8},{10,11... | collective-permute-start | bytes 393224 | tf_op jit(solution)/shard_map/ppermute | solution.py:139
  30.5 5.7 %collective-permute-start.4 = (bf16[1,128,256]{2,1,0:T(8,128)(2,1)S(1)}, bf16[1,128,256]{2,1,0:T(8,128)(2,1)S(1)}, u32[]{:S(2)}, u32[]{:S(2)}) collective-permute-start(bf16[1,128,256]{2,1,0:T(8,128)(2,1)S(1)} %get-tuple-element.61), channel_id=1, source_target_pairs={{1,2},{2,1},{3,4},{4,3},{5,6},{6,5},{9,10},{10,9},{11,12},{12,11},... | collective-permute-start | bytes 196616 | tf_op jit(solution)/shard_map/ppermute | solution.py:139
  32.9 4.6 %collective-permute-start.3 = (bf16[1,128,256]{2,1,0:T(8,128)(2,1)S(1)}, bf16[1,128,256]{2,1,0:T(8,128)(2,1)S(1)}, u32[]{:S(2)}, u32[]{:S(2)}) collective-permute-start(bf16[1,128,256]{2,1,0:T(8,128)(2,1)S(1)} %get-tuple-element.62), channel_id=1, source_target_pairs={{0,1},{1,0},{2,3},{3,2},{4,5},{5,4},{6,7},{7,6},{8,9},{9,8},{10,11... | collective-permute-start | bytes 196616 | tf_op jit(solution)/shard_map/ppermute | solution.py:139
  33.1 19.6 %collective-permute-start.11 = (bf16[4,128,256]{2,1,0:T(8,128)(2,1)}, bf16[4,128,256]{2,1,0:T(8,128)(2,1)}, u32[]{:S(2)}, u32[]{:S(2)}) collective-permute-start(bf16[4,128,256]{2,1,0:T(8,128)(2,1)} %collective-permute-done.10), channel_id=1, source_target_pairs={{8,24},{9,25},{10,26},{11,27},{12,28},{13,29},{14,30},{15,31}} | collective-permute-start | bytes 786440 | tf_op jit(solution)/shard_map/ppermute | solution.py:160
  36.2 16.5 %collective-permute-start.16 = (bf16[4,128,256]{2,1,0:T(8,128)(2,1)}, bf16[4,128,256]{2,1,0:T(8,128)(2,1)}, u32[]{:S(2)}, u32[]{:S(2)}) collective-permute-start(bf16[4,128,256]{2,1,0:T(8,128)(2,1)} %collective-permute-done.14), channel_id=1, source_target_pairs={{8,24},{9,25},{10,26},{11,27},{12,28},{13,29},{14,30},{15,31}} | collective-permute-start | bytes 786440 | tf_op jit(solution)/shard_map/ppermute | solution.py:160
  47.7 14.8 %collective-permute-start.5 = (bf16[4,128,256]{2,1,0:T(8,128)(2,1)}, bf16[4,128,256]{2,1,0:T(8,128)(2,1)}, u32[]{:S(2)}, u32[]{:S(2)}) collective-permute-start(bf16[4,128,256]{2,1,0:T(8,128)(2,1)} %shard_map.56), channel_id=1, source_target_pairs={{0,8},{8,16},{16,24},{1,9},{9,17},{17,25},{2,10},{10,18},{18,26},{... | collective-permute-start | bytes 786440 | tf_op jit(solution)/shard_map/ppermute | solution.py:160
  50.7 17.4 %collective-permute-start.15 = (bf16[4,128,256]{2,1,0:T(8,128)(2,1)}, bf16[4,128,256]{2,1,0:T(8,128)(2,1)}, u32[]{:S(2)}, u32[]{:S(2)}) collective-permute-start(bf16[4,128,256]{2,1,0:T(8,128)(2,1)} %get-tuple-element.21.first_mid), channel_id=1, source_target_pairs={{0,8},{8,16},{16,24},{1,9},{9,17},{17,25},{2,10},{10,18},{18,26},{... | collective-permute-start | bytes 786440 | tf_op jit(solution)/shard_map/ppermute | solution.py:160
  69.5 10.3 %collective-permute-start.13 = (bf16[2,128,256]{2,1,0:T(8,128)(2,1)S(1)}, bf16[2,128,256]{2,1,0:T(8,128)(2,1)S(1)}, u32[]{:S(2)}, u32[]{:S(2)}) collective-permute-start(bf16[2,128,256]{2,1,0:T(8,128)(2,1)S(1)} %get-tuple-element.55), channel_id=1, source_target_pairs={{1,2},{2,1},{3,4},{4,3},{5,6},{6,5},{9,10},{10,9},{11,12},{12,11},... | collective-permute-start | bytes 393224 | tf_op jit(solution)/shard_map/ppermute | solution.py:139
  73.2 6.7 %collective-permute-start.12 = (bf16[2,128,256]{2,1,0:T(8,128)(2,1)S(1)}, bf16[2,128,256]{2,1,0:T(8,128)(2,1)S(1)}, u32[]{:S(2)}, u32[]{:S(2)}) collective-permute-start(bf16[2,128,256]{2,1,0:T(8,128)(2,1)S(1)} %get-tuple-element.56), channel_id=1, source_target_pairs={{0,1},{1,0},{2,3},{3,2},{4,5},{5,4},{6,7},{7,6},{8,9},{9,8},{10,11... | collective-permute-start | bytes 393224 | tf_op jit(solution)/shard_map/ppermute | solution.py:139
  73.3 5.7 %collective-permute-start.18 = (bf16[1,128,256]{2,1,0:T(8,128)(2,1)S(1)}, bf16[1,128,256]{2,1,0:T(8,128)(2,1)S(1)}, u32[]{:S(2)}, u32[]{:S(2)}) collective-permute-start(bf16[1,128,256]{2,1,0:T(8,128)(2,1)S(1)} %get-tuple-element.53), channel_id=1, source_target_pairs={{1,2},{2,1},{3,4},{4,3},{5,6},{6,5},{9,10},{10,9},{11,12},{12,11},... | collective-permute-start | bytes 196616 | tf_op jit(solution)/shard_map/ppermute | solution.py:139
  75.2 9.3 %copy-start.3 = (bf16[1,3,3,3,256,256]{5,4,3,2,1,0:T(8,128)(2,1)S(1)}, bf16[1,3,3,3,256,256]{5,4,3,2,1,0:T(8,128)(2,1)}, u32[]{:S(2)}) copy-start(bf16[1,3,3,3,256,256]{5,4,3,2,1,0:T(8,128)(2,1)} %param.9) | copy-start | bytes 10616836
  75.2 4.6 %collective-permute-start.17 = (bf16[1,128,256]{2,1,0:T(8,128)(2,1)S(1)}, bf16[1,128,256]{2,1,0:T(8,128)(2,1)S(1)}, u32[]{:S(2)}, u32[]{:S(2)}) collective-permute-start(bf16[1,128,256]{2,1,0:T(8,128)(2,1)S(1)} %get-tuple-element.54), channel_id=1, source_target_pairs={{0,1},{1,0},{2,3},{3,2},{4,5},{5,4},{6,7},{7,6},{8,9},{9,8},{10,11... | collective-permute-start | bytes 196616 | tf_op jit(solution)/shard_map/ppermute | solution.py:139
  75.9 15.6 %collective-permute-start.20 = (bf16[4,128,256]{2,1,0:T(8,128)(2,1)}, bf16[4,128,256]{2,1,0:T(8,128)(2,1)S(1)}, u32[]{:S(2)}, u32[]{:S(2)}) collective-permute-start(bf16[4,128,256]{2,1,0:T(8,128)(2,1)} %collective-permute-done.5), channel_id=1, source_target_pairs={{8,24},{9,25},{10,26},{11,27},{12,28},{13,29},{14,30},{15,31}} | collective-permute-start | bytes 786440 | tf_op jit(solution)/shard_map/ppermute | solution.py:160
  79.0 12.5 %collective-permute-start.24 = (bf16[4,128,256]{2,1,0:T(8,128)(2,1)}, bf16[4,128,256]{2,1,0:T(8,128)(2,1)S(1)}, u32[]{:S(2)}, u32[]{:S(2)}) collective-permute-start(bf16[4,128,256]{2,1,0:T(8,128)(2,1)} %collective-permute-done.15), channel_id=1, source_target_pairs={{8,24},{9,25},{10,26},{11,27},{12,28},{13,29},{14,30},{15,31}} | collective-permute-start | bytes 786440 | tf_op jit(solution)/shard_map/ppermute | solution.py:160
  84.5 19.0 %copy-start.6 = (bf16[3,2,4,16,8,256]{5,4,3,2,1,0:T(8,128)(2,1)S(1)}, bf16[3,2,4,16,8,256]{5,4,3,2,1,0:T(8,128)(2,1)}, u32[]{:S(2)}) copy-start(bf16[3,2,4,16,8,256]{5,4,3,2,1,0:T(8,128)(2,1)} %param.7) | copy-start | bytes 4718596
  87.6 10.3 %collective-permute-start.19 = (bf16[4,128,256]{2,1,0:T(8,128)(2,1)S(1)}, bf16[4,128,256]{2,1,0:T(8,128)(2,1)S(1)}, u32[]{:S(2)}, u32[]{:S(2)}) collective-permute-start(bf16[4,128,256]{2,1,0:T(8,128)(2,1)S(1)} %shard_map.60), channel_id=1, source_target_pairs={{0,8},{8,16},{16,24},{1,9},{9,17},{17,25},{2,10},{10,18},{18,26},{... | collective-permute-start | bytes 786440 | tf_op jit(solution)/shard_map/ppermute | solution.py:160
  89.6 14.0 %collective-permute-start.23 = (bf16[4,128,256]{2,1,0:T(8,128)(2,1)S(1)}, bf16[4,128,256]{2,1,0:T(8,128)(2,1)S(1)}, u32[]{:S(2)}, u32[]{:S(2)}) collective-permute-start(bf16[4,128,256]{2,1,0:T(8,128)(2,1)S(1)} %get-tuple-element.27.first_mid), channel_id=1, source_target_pairs={{0,8},{8,16},{16,24},{1,9},{9,17},{17,25},{2,10},{10,18},{18,26},{... | collective-permute-start | bytes 786440 | tf_op jit(solution)/shard_map/ppermute | solution.py:160
  103.8 9.5 %collective-permute-start.22 = (bf16[2,128,256]{2,1,0:T(8,128)(2,1)S(1)}, bf16[2,128,256]{2,1,0:T(8,128)(2,1)S(1)}, u32[]{:S(2)}, u32[]{:S(2)}) collective-permute-start(bf16[2,128,256]{2,1,0:T(8,128)(2,1)S(1)} %get-tuple-element.51), channel_id=1, source_target_pairs={{1,2},{2,1},{3,4},{4,3},{5,6},{6,5},{9,10},{10,9},{11,12},{12,11},... | collective-permute-start | bytes 393224 | tf_op jit(solution)/shard_map/ppermute | solution.py:139
  106.8 6.5 %collective-permute-start.21 = (bf16[2,128,256]{2,1,0:T(8,128)(2,1)S(1)}, bf16[2,128,256]{2,1,0:T(8,128)(2,1)S(1)}, u32[]{:S(2)}, u32[]{:S(2)}) collective-permute-start(bf16[2,128,256]{2,1,0:T(8,128)(2,1)S(1)} %get-tuple-element.52), channel_id=1, source_target_pairs={{0,1},{1,0},{2,3},{3,2},{4,5},{5,4},{6,7},{7,6},{8,9},{9,8},{10,11... | collective-permute-start | bytes 393224 | tf_op jit(solution)/shard_map/ppermute | solution.py:139
  107.0 5.6 %collective-permute-start.26 = (bf16[1,128,256]{2,1,0:T(8,128)(2,1)S(1)}, bf16[1,128,256]{2,1,0:T(8,128)(2,1)S(1)}, u32[]{:S(2)}, u32[]{:S(2)}) collective-permute-start(bf16[1,128,256]{2,1,0:T(8,128)(2,1)S(1)} %get-tuple-element.49), channel_id=1, source_target_pairs={{1,2},{2,1},{3,4},{4,3},{5,6},{6,5},{9,10},{10,9},{11,12},{12,11},... | collective-permute-start | bytes 196616 | tf_op jit(solution)/shard_map/ppermute | solution.py:139
  109.5 3.8 %collective-permute-start.25 = (bf16[1,128,256]{2,1,0:T(8,128)(2,1)S(1)}, bf16[1,128,256]{2,1,0:T(8,128)(2,1)S(1)}, u32[]{:S(2)}, u32[]{:S(2)}) collective-permute-start(bf16[1,128,256]{2,1,0:T(8,128)(2,1)S(1)} %get-tuple-element.50), channel_id=1, source_target_pairs={{0,1},{1,0},{2,3},{3,2},{4,5},{5,4},{6,7},{7,6},{8,9},{9,8},{10,11... | collective-permute-start | bytes 196616 | tf_op jit(solution)/shard_map/ppermute | solution.py:139
  110.7 14.2 %collective-permute-start.28 = (bf16[4,128,256]{2,1,0:T(8,128)(2,1)S(1)}, bf16[4,128,256]{2,1,0:T(8,128)(2,1)S(1)}, u32[]{:S(2)}, u32[]{:S(2)}) collective-permute-start(bf16[4,128,256]{2,1,0:T(8,128)(2,1)S(1)} %collective-permute-done.19), channel_id=1, source_target_pairs={{8,24},{9,25},{10,26},{11,27},{12,28},{13,29},{14,30},{15,31}} | collective-permute-start | bytes 786440 | tf_op jit(solution)/shard_map/ppermute | solution.py:160
  112.6 12.3 %collective-permute-start.32 = (bf16[4,128,256]{2,1,0:T(8,128)(2,1)S(1)}, bf16[4,128,256]{2,1,0:T(8,128)(2,1)S(1)}, u32[]{:S(2)}, u32[]{:S(2)}) collective-permute-start(bf16[4,128,256]{2,1,0:T(8,128)(2,1)S(1)} %collective-permute-done.23), channel_id=1, source_target_pairs={{8,24},{9,25},{10,26},{11,27},{12,28},{13,29},{14,30},{15,31}} | collective-permute-start | bytes 786440 | tf_op jit(solution)/shard_map/ppermute | solution.py:160
  121.0 10.3 %collective-permute-start.27 = (bf16[4,128,256]{2,1,0:T(8,128)(2,1)S(1)}, bf16[4,128,256]{2,1,0:T(8,128)(2,1)S(1)}, u32[]{:S(2)}, u32[]{:S(2)}) collective-permute-start(bf16[4,128,256]{2,1,0:T(8,128)(2,1)S(1)} %shard_map.62), channel_id=1, source_target_pairs={{8,16},{16,24},{9,17},{17,25},{10,18},{18,26},{11,19},{19,27},{12,... | collective-permute-start | bytes 786440 | tf_op jit(solution)/shard_map/ppermute | solution.py:160
  123.0 14.0 %collective-permute-start.31 = (bf16[4,128,256]{2,1,0:T(8,128)(2,1)S(1)}, bf16[4,128,256]{2,1,0:T(8,128)(2,1)S(1)}, u32[]{:S(2)}, u32[]{:S(2)}) collective-permute-start(bf16[4,128,256]{2,1,0:T(8,128)(2,1)S(1)} %get-tuple-element.29.first_mid), channel_id=1, source_target_pairs={{8,16},{16,24},{9,17},{17,25},{10,18},{18,26},{11,19},{19,27},{12,... | collective-permute-start | bytes 786440 | tf_op jit(solution)/shard_map/ppermute | solution.py:160
  137.2 9.4 %collective-permute-start.30 = (bf16[2,128,256]{2,1,0:T(8,128)(2,1)S(1)}, bf16[2,128,256]{2,1,0:T(8,128)(2,1)S(1)}, u32[]{:S(2)}, u32[]{:S(2)}) collective-permute-start(bf16[2,128,256]{2,1,0:T(8,128)(2,1)S(1)} %get-tuple-element.47), channel_id=1, source_target_pairs={{1,2},{2,1},{3,4},{4,3},{5,6},{6,5},{9,10},{10,9},{11,12},{12,11},... | collective-permute-start | bytes 393224 | tf_op jit(solution)/shard_map/ppermute | solution.py:139
  140.8 5.8 %collective-permute-start.29 = (bf16[2,128,256]{2,1,0:T(8,128)(2,1)S(1)}, bf16[2,128,256]{2,1,0:T(8,128)(2,1)S(1)}, u32[]{:S(2)}, u32[]{:S(2)}) collective-permute-start(bf16[2,128,256]{2,1,0:T(8,128)(2,1)S(1)} %get-tuple-element.48), channel_id=1, source_target_pairs={{0,1},{1,0},{2,3},{3,2},{4,5},{5,4},{6,7},{7,6},{8,9},{9,8},{10,11... | collective-permute-start | bytes 393224 | tf_op jit(solution)/shard_map/ppermute | solution.py:139
  140.9 5.7 %collective-permute-start.34 = (bf16[1,128,256]{2,1,0:T(8,128)(2,1)S(1)}, bf16[1,128,256]{2,1,0:T(8,128)(2,1)S(1)}, u32[]{:S(2)}, u32[]{:S(2)}) collective-permute-start(bf16[1,128,256]{2,1,0:T(8,128)(2,1)S(1)} %get-tuple-element.45), channel_id=1, source_target_pairs={{1,2},{2,1},{3,4},{4,3},{5,6},{6,5},{9,10},{10,9},{11,12},{12,11},... | collective-permute-start | bytes 196616 | tf_op jit(solution)/shard_map/ppermute | solution.py:139
  143.1 3.5 %collective-permute-start.33 = (bf16[1,128,256]{2,1,0:T(8,128)(2,1)S(1)}, bf16[1,128,256]{2,1,0:T(8,128)(2,1)S(1)}, u32[]{:S(2)}, u32[]{:S(2)}) collective-permute-start(bf16[1,128,256]{2,1,0:T(8,128)(2,1)S(1)} %get-tuple-element.46), channel_id=1, source_target_pairs={{0,1},{1,0},{2,3},{3,2},{4,5},{5,4},{6,7},{7,6},{8,9},{9,8},{10,11... | collective-permute-start | bytes 196616 | tf_op jit(solution)/shard_map/ppermute | solution.py:139

commit v2 on v1

--- a/solution.py
+++ b/solution.py
@@ -8,6 +8,7 @@
 from jax.sharding import PartitionSpec as P
 
 EPS = 1e-05
+LANES = 128
 VMEM_LIMIT = 48 * 1024 * 1024
 
 
@@ -30,18 +31,25 @@
     edge = jnp.zeros((planes, width, chans), jnp.float32)
     for k, part in enumerate(shifted):
         part = part.reshape(planes, voxels, chans)
-        columns = pl.ds(k * chans, chans)
-        even[pl.ds(at, planes), :, columns] = part.astype(jnp.bfloat16)
-        odd[pl.ds(at, planes), :, columns] = jnp.concatenate([edge, part, edge], axis=1).astype(jnp.bfloat16)
+        moved = jnp.concatenate([edge, part, edge], axis=1).astype(jnp.bfloat16)
+        part = part.astype(jnp.bfloat16)
+        for c in range(chans // LANES):
+            piece = k * (chans // LANES) + c
+            columns = slice(c * LANES, (c + 1) * LANES)
+            even[piece, pl.ds(at, planes)] = part[:, :, columns]
+            odd[piece, pl.ds(at, planes)] = moved[:, :, columns]
 
 
 def convolve(even, odd, weights, copies, planes, width):
-    voxels = even.shape[1]
+    pieces, _, voxels, _ = even.shape
     taps = []
     for i in range(3):
         copies[i].wait()
-        for part in (odd[i : i + planes, 0:voxels], even[i : i + planes], odd[i : i + planes, 2 * width : 2 * width + voxels]):
-            taps.append(part.reshape(planes * voxels, part.shape[-1]))
+        for j in range(3):
+            for piece in range(pieces):
+                source, row = (even, 0) if j == 1 else (odd, j * width)
+                part = source[piece, i : i + planes, row : row + voxels]
+                taps.append(part.reshape(planes * voxels, LANES))
     slab = jnp.concatenate(taps, axis=-1)
     total = jnp.dot(slab, weights[...], preferred_element_type=jnp.float32)
     return total.reshape(planes, voxels, -1)
@@ -63,11 +71,11 @@
     planes = q_mid.shape[0]
     above = flags[2] > 0
     fill(even, odd, 2, q_mid[...], width)
-    inner, outer = q_inner[...].astype(jnp.float32), q_outer[...].astype(jnp.float32)
+    inner, outer = q_inner[:2].astype(jnp.float32), q_outer[:2].astype(jnp.float32)
     fill(even, odd, 0, jnp.where(above, outer, inner), width)
     fill(even, odd, 2 + planes, jnp.where(above, inner, outer), width)
     total = convolve(even, odd, weights, copies, planes + 2, width)
-    inner, outer = p_inner[...].astype(jnp.float32), p_outer[...].astype(jnp.float32)
+    inner, outer = p_inner[-1:].astype(jnp.float32), p_outer[-1:].astype(jnp.float32)
     low[...] = jnp.where(flags[0] > 0, jnp.where(above, outer, inner) + total[:1], 0.0).astype(low.dtype)
     mid[...] = (p_mid[...].astype(jnp.float32) + total[1:-1]).astype(mid.dtype)
     high[...] = jnp.where(flags[1] > 0, jnp.where(above, inner, outer) + total[-1:], 0.0).astype(high.dtype)
@@ -85,8 +93,8 @@
 
 def scratch(planes, voxels, chans, width):
     return [
-        pltpu.VMEM((planes, voxels, 3 * chans), jnp.bfloat16),
-        pltpu.VMEM((planes, voxels + 2 * width, 3 * chans), jnp.bfloat16),
+        pltpu.VMEM((3 * chans // LANES, planes, voxels, LANES), jnp.bfloat16),
+        pltpu.VMEM((3 * chans // LANES, planes, voxels + 2 * width, LANES), jnp.bfloat16),
         pltpu.VMEM((27 * chans, chans), jnp.bfloat16),
         pltpu.SemaphoreType.DMA((3,)),
     ]
@@ -128,17 +136,18 @@
     )(*first, q, weights)
 
 
-def halo(block, width, above):
+def halo(blocks, widths, above):
     count = lax.axis_size("depth")
-    planes = block.shape[0]
-    top, bottom = planes - width, 0
-
-    def swap(start, base):
-        part = lax.dynamic_slice_in_dim(block, start, width, axis=0)
+
+    def swap(upward, base):
+        parts = [
+            lax.dynamic_slice_in_dim(block, jnp.where(upward, block.shape[0] - width, 0), width, axis=0)
+            for block, width in zip(blocks, widths)
+        ]
         pairs = [pair for i in range(base, count - 1, 2) for pair in ((i, i + 1), (i + 1, i))]
-        return lax.ppermute(part, "depth", pairs)
-
-    return swap(jnp.where(above, top, bottom), 0), swap(jnp.where(above, bottom, top), 1)
+        return lax.ppermute(jnp.concatenate(parts, axis=0), "depth", pairs)
+
+    return swap(above, 0), swap(jnp.logical_not(above), 1)
 
 
 def local(resident, previous, incoming, first_weights, second_weights):
@@ -169,31 +178,33 @@
 
     out = emitted = None
     newer, older, relayed, direct = {}, {}, {}, {}
+
+    def arrived(slot, stream):
+        fresh = incoming[min(slot, ticks - 1) - 1, stream]
+        if slot == 1:
+            return jnp.where(section == 0, fresh, join(resident[stream], mirrored[stream]))
+        held = jnp.where(section == 1, older[stream], newer[stream])
+        skip = jnp.where(section == sections - 1, relayed[stream], newer[stream])
+        if across:
+            skip = jnp.where((section > half) & (section < sections - 1), direct[stream], skip)
+        return jnp.where(section == 0, fresh, join(held, skip))
+
     for slot in range(ticks + 1):
-        inputs = []
-        for stream in range(2):
-            fresh = resident[stream] if slot == 0 else incoming[min(slot, ticks - 1) - 1, stream]
-            if slot == 0:
-                value = fresh
-            elif slot == 1:
-                value = jnp.where(section == 0, fresh, join(resident[stream], mirrored[stream]))
-            else:
-                held = jnp.where(section == 1, older[stream], newer[stream])
-                skip = jnp.where(section == sections - 1, relayed[stream], newer[stream])
-                if across:
-                    skip = jnp.where((section > half) & (section < sections - 1), direct[stream], skip)
-                value = jnp.where(section == 0, fresh, join(held, skip))
-            inputs.append(value)
-        p, q = inputs
-        p_halo = halo(p, 1, above)
-        q_halo = halo(q, 2, above)
+        if slot < 2:
+            p, q = resident if slot == 0 else (arrived(slot, 0), arrived(slot, 1))
+            p_halo = q_halo = halo((q, p), (2, 1), above)
+        else:
+            p = arrived(slot, 0)
+            p_halo = halo((p,), (1,), above)
+            p, p_halo, newer[1] = lax.optimization_barrier((p, p_halo, newer[1]))
+            q = arrived(slot, 1)
+            q_halo = halo((q,), (2,), above)
         onward = []
         if slot < ticks:
             onward = [(0, 1)] if slot < ticks - 1 else []
             if slot > 0:
                 onward += [(j, j + 1) for j in range(1, sections - 1)]
-        received = {}
-        relays = {}
+        received, relays = {}, {}
         first = first_half(flags, q, q_halo, p, p_halo, w_one, width)
         if onward:
             received[0] = send(first[1], onward)
@@ -201,7 +212,8 @@
         if onward:
             received[1] = send(second, onward)
         if 0 < slot < ticks:
-            relays = {k: send(newer[k], [(1, sections - 1)]) for k in range(2)}
+            held_q, second = lax.optimization_barrier((newer[1], second))
+            relays = {k: send(held, [(1, sections - 1)]) for k, held in enumerate((newer[0], held_q))}
         if across and 0 < slot < ticks:
             direct = {0: send(first[1], across), 1: send(second, across)}
         older, newer, relayed = newer, received, relays

time: 157 us -> 153 us (0.975)
  waiting for transfers between devices: 49.2 us -> 33.3 us
  Pallas kernels: 40.9 us -> 48.3 us
  local copies, waits for them, and re-layouts: 4.26 us -> 7.96 us
    ppermute x15, waiting for transfers between devices: 39.5 us -> 24.4 us  [send(): return lax.ppermute(block, 'section', pairs) if pairs else block]
    pallas_call x5, Pallas kernels: 23.9 us -> 28.2 us  [first_half(): pl.pallas_call(functools.partial(first_kernel, width), out_shape=(shape(1...]
    unnamed x16 -> x24, local copies, waits for them, and re-layouts: 2.98 us -> 6.68 us
    pallas_call x5, Pallas kernels: 17 us -> 20.1 us  [second_half(): pl.pallas_call(functools.partial(second_kernel, width), out_shape=jax.Sha...]
    ppermute x15, starting transfers between devices: 22.4 us -> 25.2 us  [send(): return lax.ppermute(block, 'section', pairs) if pairs else block]
    ppermute x20 -> x16, starting transfers between devices: 33.6 us -> 31.5 us  [swap(): return lax.ppermute(jnp.concatenate(parts, axis=0), 'depth', pairs)]
    ppermute x20 -> x16, waiting for transfers between devices: 9.72 us -> 8.84 us  [swap(): return lax.ppermute(jnp.concatenate(parts, axis=0), 'depth', pairs)]
    select_n x4 -> x7, other arithmetic: 3.19 us -> 3.37 us  [the longest x1 1.72 us: arrived(): jnp.where(section == 0, fresh, join(resident[stream], mirrored[stream]))]
  transfers between devices with their start and end apart: 35 -> 31, of which waited for: 11 -> 11; matrix products, arithmetic and copies ran while one was open for 2% -> 2% of each run, Pallas kernels for 21% -> 26%
where the time goes in v2:
time: 153 us; the launch traced here: 151 us
  starting transfers between devices  56.7 us (37%)
  Pallas kernels  48.3 us (32%)
  waiting for transfers between devices  33.3 us (22%)
  local copies, waits for them, and re-layouts  7.96 us (5%)
  other arithmetic  4.41 us (3%)
    ppermute x16, starting transfers between devices, swap(): return lax.ppermute(jnp.concatenate(parts, axis=0), 'depth', pairs)  31.5 us
    pallas_call x5, Pallas kernels, first_half(): pl.pallas_call(functools.partial(first_kernel, width), out_shape=(shape(1...  28.2 us
    ppermute x15, starting transfers between devices, send(): return lax.ppermute(block, 'section', pairs) if pairs else block  25.2 us
    ppermute x15, waiting for transfers between devices, send(): return lax.ppermute(block, 'section', pairs) if pairs else block  24.4 us
    pallas_call x5, Pallas kernels, second_half(): pl.pallas_call(functools.partial(second_kernel, width), out_shape=jax.Sha...  20.1 us
    ppermute x16, waiting for transfers between devices, swap(): return lax.ppermute(jnp.concatenate(parts, axis=0), 'depth', pairs)  8.84 us
    unnamed x24, local copies, waits for them, and re-layouts  6.68 us
  transfers between devices with their start and end apart: 31, of which 11 were waited for; matrix products, arithmetic and copies ran while one was open for 2% of the time, Pallas kernels for 26%

profile of v2, /device:TPU:13, one launch (start us, length us, event | category | flops | bytes accessed | tf_op | source)
XLA Modules:
  0.0 151.2 jit_solution(14707678006796255722)
XLA Ops:
  0.0 1.3 collective-permute-start.3
  1.3 1.1 slice_bitcast_fusion.8
  2.4 13.4 %collective-permute-done.3 = bf16[2,4,128,256]{3,2,1,0:T(8,128)(2,1)S(1)} collective-permute-done((bf16[2,4,128,256]{3,2,1,0:T(8,128)(2,1)}, bf16[2,4,128,256]{3,2,1,0:T(8,128)(2,1)S(1)}, u32[]{:S(2)}, u32[]{:S(2)}) %collective-permute-start.3) | collective-permute-done | bytes 524320 | tf_op jit(solution)/shard_map/ppermute | solution.py:169
  15.8 0.8 copy-done.11
  16.6 1.7 %fusion.10 = (bf16[4,128,256]{2,1,0:T(8,128)(2,1)S(1)}, bf16[4,128,256]{2,1,0:T(8,128)(2,1)S(1)}) fusion(bf16[2,4,128,256]{3,2,1,0:T(8,128)(2,1)} %copy-done.11, bf16[3,2,4,128,256]{4,3,2,1,0:T(8,128)(2,1)} %bitcast.71, pred[]{:T(512)S(6)} %ge.3, pred[]{:T(512)S(6)} %eq.10, bf16[1,2,4,16,8,256]{5,4,3,2,1,0:T(8,128)(2,1)} %param.5), kind=kLoop, calls=%fused_computation.19 | loop fusion | flops 1572864 | bytes 2097154 | tf_op jit(solution)/shard_map/jit(_where)/select_n | solution.py:185
  18.4 4.6 %collective-permute-start.1 = (bf16[3,128,256]{2,1,0:T(8,128)(2,1)S(1)}, bf16[3,128,256]{2,1,0:T(8,128)(2,1)S(1)}, u32[]{:S(2)}, u32[]{:S(2)}) collective-permute-start(bf16[3,128,256]{2,1,0:T(8,128)(2,1)S(1)} %pad_maximum_fusion.1), channel_id=1, source_target_pairs={{1,2},{2,1},{3,4},{4,3},{5,6},{6,5},{9,10},{10,9},{11,12},{12,11},... | collective-permute-start | bytes 589832 | tf_op jit(solution)/shard_map/ppermute | solution.py:148
  23.8 2.7 %collective-permute-done.1.q_outer.p_outer = bf16[3,128,256]{2,1,0:T(8,128)(2,1)S(1)} collective-permute-done((bf16[3,128,256]{2,1,0:T(8,128)(2,1)S(1)}, bf16[3,128,256]{2,1,0:T(8,128)(2,1)S(1)}, u32[]{:S(2)}, u32[]{:S(2)}) %collective-permute-start.1) | collective-permute-done | bytes 196640 | tf_op jit(solution)/shard_map/ppermute | solution.py:148
  26.6 5.5 %shard_map.55 = (bf16[1,128,256]{2,1,0:T(8,128)(2,1)S(1)}, bf16[4,128,256]{2,1,0:T(8,128)(2,1)S(1)}, bf16[1,128,256]{2,1,0:T(8,128)(2,1)S(1)}) custom-call(s32[3]{0:T(128)S(1)} %add_convert_fusion.6.flags, bf16[4,128,256]{2,1,0:T(8,128)(2,1)S(1)} %get-tuple-element.70.q_mid, bf16[3,128,256]{2,1,0:T(8,128)(2,1)S(1)} %collective-permute-done.q_inner.p_inner, ...), custom_call_target="tpu_custom_call" | custom-call | flops 1 | bytes 1 | tf_op jit(solution)/shard_map/pallas_call | solution.py:111
  32.1 1.4 collective-permute-start.2
  33.5 3.5 %collective-permute-start.5 = (bf16[3,128,256]{2,1,0:T(8,128)(2,1)S(1)}, bf16[3,128,256]{2,1,0:T(8,128)(2,1)S(1)}, u32[]{:S(2)}, u32[]{:S(2)}) collective-permute-start(bf16[3,128,256]{2,1,0:T(8,128)(2,1)S(1)} %pad_maximum_fusion.3), channel_id=1, source_target_pairs={{1,2},{2,1},{3,4},{4,3},{5,6},{6,5},{9,10},{10,9},{11,12},{12,11},... | collective-permute-start | bytes 589832 | tf_op jit(solution)/shard_map/ppermute | solution.py:148
  37.0 4.4 %shard_map.58 = bf16[4,128,256]{2,1,0:T(8,128)(2,1)} custom-call(bf16[1,128,256]{2,1,0:T(8,128)(2,1)S(1)} %get-tuple-element.41.first_low, bf16[4,128,256]{2,1,0:T(8,128)(2,1)S(1)} %get-tuple-element.36.first_mid, bf16[1,128,256]{2,1,0:T(8,128)(2,1)S(1)} %get-tuple-element.42.first_high, bf16[4,128,256]{2,1,0:T(8,128)(2,1)S(1)} %get-tuple-element.70.q_mid, ...), custom_call_target="tpu_custom_call" | custom-call | flops 1 | bytes 1 | tf_op jit(solution)/shard_map/pallas_call | solution.py:126
  41.3 1.4 collective-permute-start.11
  42.7 6.2 %shard_map.56 = (bf16[1,128,256]{2,1,0:T(8,128)(2,1)S(1)}, bf16[4,128,256]{2,1,0:T(8,128)(2,1)}, bf16[1,128,256]{2,1,0:T(8,128)(2,1)S(1)}) custom-call(s32[3]{0:T(128)S(1)} %add_convert_fusion.6.flags, bf16[4,128,256]{2,1,0:T(8,128)(2,1)S(1)} %get-tuple-element.68.q_mid, bf16[3,128,256]{2,1,0:T(8,128)(2,1)S(1)} %collective-permute-done.4.q_inner.p_inner, ...), custom_call_target="tpu_custom_call" | custom-call | flops 1 | bytes 1 | tf_op jit(solution)/shard_map/pallas_call | solution.py:111
  50.2 3.1 %collective-permute-start.6 = (bf16[4,128,256]{2,1,0:T(8,128)(2,1)}, bf16[4,128,256]{2,1,0:T(8,128)(2,1)}, u32[]{:S(2)}, u32[]{:S(2)}) collective-permute-start(bf16[4,128,256]{2,1,0:T(8,128)(2,1)} %get-tuple-element.37.first_mid), channel_id=1, source_target_pairs={{0,8},{8,16},{16,24},{1,9},{9,17},{17,25},{2,10},{10,18},{18,26},{... | collective-permute-start | bytes 786440 | tf_op jit(solution)/shard_map/ppermute | solution.py:169
  53.3 1.4 collective-permute-start.7
  54.7 2.0 %copy-done.2 = bf16[1,3,3,3,256,256]{5,4,3,2,1,0:T(8,128)(2,1)S(1)} copy-done((bf16[1,3,3,3,256,256]{5,4,3,2,1,0:T(8,128)(2,1)S(1)}, bf16[1,3,3,3,256,256]{5,4,3,2,1,0:T(8,128)(2,1)}, u32[]{:S(2)}) %copy-start.2) | copy-done | bytes 3538968
  56.7 0.9 copy-done.5
  57.6 0.8 copy-done.7
  58.5 0.8 copy-done.9
  59.3 4.7 %shard_map.57 = bf16[4,128,256]{2,1,0:T(8,128)(2,1)S(1)} custom-call(bf16[1,128,256]{2,1,0:T(8,128)(2,1)S(1)} %copy-done.7, bf16[4,128,256]{2,1,0:T(8,128)(2,1)} %get-tuple-element.37.first_mid, bf16[1,128,256]{2,1,0:T(8,128)(2,1)S(1)} %copy-done.9, bf16[4,128,256]{2,1,0:T(8,128)(2,1)S(1)} %copy-done.5, bf16[6912,256]{1,0:T(8,128)(2,1)S(1)} %bitcast.63), custom_call_target="tpu_custom_call" | custom-call | flops 1 | bytes 1 | tf_op jit(solution)/shard_map/pallas_call | solution.py:126
  64.0 1.9 %collective-permute-start.10 = (bf16[4,128,256]{2,1,0:T(8,128)(2,1)S(1)}, bf16[4,128,256]{2,1,0:T(8,128)(2,1)S(1)}, u32[]{:S(2)}, u32[]{:S(2)}) collective-permute-start(bf16[4,128,256]{2,1,0:T(8,128)(2,1)S(1)} %shard_map.57), channel_id=1, source_target_pairs={{0,8},{8,16},{16,24},{1,9},{9,17},{17,25},{2,10},{10,18},{18,26},{... | collective-permute-start | bytes 786440 | tf_op jit(solution)/shard_map/ppermute | solution.py:169
  66.7 1.1 fusion.17.p_mid
  67.8 2.4 %collective-permute-start.9 = (bf16[1,128,256]{2,1,0:T(8,128)(2,1)S(1)}, bf16[1,128,256]{2,1,0:T(8,128)(2,1)S(1)}, u32[]{:S(2)}, u32[]{:S(2)}) collective-permute-start(bf16[1,128,256]{2,1,0:T(8,128)(2,1)S(1)} %get-tuple-element.81), channel_id=1, source_target_pairs={{1,2},{2,1},{3,4},{4,3},{5,6},{6,5},{9,10},{10,9},{11,12},{12,11},... | collective-permute-start | bytes 196616 | tf_op jit(solution)/shard_map/ppermute | solution.py:148
  70.3 4.1 %collective-permute-done.10 = bf16[4,128,256]{2,1,0:T(8,128)(2,1)S(1)} collective-permute-done((bf16[4,128,256]{2,1,0:T(8,128)(2,1)S(1)}, bf16[4,128,256]{2,1,0:T(8,128)(2,1)S(1)}, u32[]{:S(2)}, u32[]{:S(2)}) %collective-permute-start.10) | collective-permute-done | bytes 262176 | tf_op jit(solution)/shard_map/ppermute | solution.py:169
  74.6 3.7 %collective-permute-start.14 = (bf16[2,128,256]{2,1,0:T(8,128)(2,1)S(1)}, bf16[2,128,256]{2,1,0:T(8,128)(2,1)S(1)}, u32[]{:S(2)}, u32[]{:S(2)}) collective-permute-start(bf16[2,128,256]{2,1,0:T(8,128)(2,1)S(1)} %get-tuple-element.79), channel_id=1, source_target_pairs={{1,2},{2,1},{3,4},{4,3},{5,6},{6,5},{9,10},{10,9},{11,12},{12,11},... | collective-permute-start | bytes 393224 | tf_op jit(solution)/shard_map/ppermute | solution.py:148
  78.4 0.8 collective-permute-start.16
  79.2 1.7 %collective-permute-done.14.q_outer = bf16[2,128,256]{2,1,0:T(8,128)(2,1)S(1)} collective-permute-done((bf16[2,128,256]{2,1,0:T(8,128)(2,1)S(1)}, bf16[2,128,256]{2,1,0:T(8,128)(2,1)S(1)}, u32[]{:S(2)}, u32[]{:S(2)}) %collective-permute-start.14) | collective-permute-done | bytes 131104 | tf_op jit(solution)/shard_map/ppermute | solution.py:148
  80.9 5.5 %shard_map.59 = (bf16[1,128,256]{2,1,0:T(8,128)(2,1)S(1)}, bf16[4,128,256]{2,1,0:T(8,128)(2,1)S(1)}, bf16[1,128,256]{2,1,0:T(8,128)(2,1)S(1)}) custom-call(s32[3]{0:T(128)S(1)} %add_convert_fusion.6.flags, bf16[4,128,256]{2,1,0:T(8,128)(2,1)S(1)} %fusion.16.q_mid, bf16[2,128,256]{2,1,0:T(8,128)(2,1)S(1)} %collective-permute-done.13.q_inner, ...), custom_call_target="tpu_custom_call" | custom-call | flops 1 | bytes 1 | tf_op jit(solution)/shard_map/pallas_call | solution.py:111
  86.4 3.7 %collective-permute-start.15 = (bf16[4,128,256]{2,1,0:T(8,128)(2,1)S(1)}, bf16[4,128,256]{2,1,0:T(8,128)(2,1)S(1)}, u32[]{:S(2)}, u32[]{:S(2)}) collective-permute-start(bf16[4,128,256]{2,1,0:T(8,128)(2,1)S(1)} %get-tuple-element.47.first_mid), channel_id=1, source_target_pairs={{0,8},{8,16},{16,24},{1,9},{9,17},{17,25},{2,10},{10,18},{18,26},{... | collective-permute-start | bytes 786440 | tf_op jit(solution)/shard_map/ppermute | solution.py:169
  90.1 3.7 %shard_map.60 = bf16[4,128,256]{2,1,0:T(8,128)(2,1)S(1)} custom-call(bf16[1,128,256]{2,1,0:T(8,128)(2,1)S(1)} %get-tuple-element.48.first_low, bf16[4,128,256]{2,1,0:T(8,128)(2,1)S(1)} %get-tuple-element.47.first_mid, bf16[1,128,256]{2,1,0:T(8,128)(2,1)S(1)} %get-tuple-element.49.first_high, bf16[4,128,256]{2,1,0:T(8,128)(2,1)S(1)} %fusion.16.q_mid, ...), custom_call_target="tpu_custom_call" | custom-call | flops 1 | bytes 1 | tf_op jit(solution)/shard_map/pallas_call | solution.py:126
  93.8 1.9 %collective-permute-start.19 = (bf16[4,128,256]{2,1,0:T(8,128)(2,1)S(1)}, bf16[4,128,256]{2,1,0:T(8,128)(2,1)S(1)}, u32[]{:S(2)}, u32[]{:S(2)}) collective-permute-start(bf16[4,128,256]{2,1,0:T(8,128)(2,1)S(1)} %shard_map.60), channel_id=1, source_target_pairs={{0,8},{8,16},{16,24},{1,9},{9,17},{17,25},{2,10},{10,18},{18,26},{... | collective-permute-start | bytes 786440 | tf_op jit(solution)/shard_map/ppermute | solution.py:169
  96.4 1.4 collective-permute-done.15
  97.9 3.8 %collective-permute-start.18 = (bf16[1,128,256]{2,1,0:T(8,128)(2,1)S(1)}, bf16[1,128,256]{2,1,0:T(8,128)(2,1)S(1)}, u32[]{:S(2)}, u32[]{:S(2)}) collective-permute-start(bf16[1,128,256]{2,1,0:T(8,128)(2,1)S(1)} %get-tuple-element.77), channel_id=1, source_target_pairs={{1,2},{2,1},{3,4},{4,3},{5,6},{6,5},{9,10},{10,9},{11,12},{12,11},... | collective-permute-start | bytes 196616 | tf_op jit(solution)/shard_map/ppermute | solution.py:148
  101.8 2.0 %collective-permute-done.19 = bf16[4,128,256]{2,1,0:T(8,128)(2,1)S(1)} collective-permute-done((bf16[4,128,256]{2,1,0:T(8,128)(2,1)S(1)}, bf16[4,128,256]{2,1,0:T(8,128)(2,1)S(1)}, u32[]{:S(2)}, u32[]{:S(2)}) %collective-permute-start.19) | collective-permute-done | bytes 262176 | tf_op jit(solution)/shard_map/ppermute | solution.py:169
  104.1 4.6 %collective-permute-start.22 = (bf16[2,128,256]{2,1,0:T(8,128)(2,1)S(1)}, bf16[2,128,256]{2,1,0:T(8,128)(2,1)S(1)}, u32[]{:S(2)}, u32[]{:S(2)}) collective-permute-start(bf16[2,128,256]{2,1,0:T(8,128)(2,1)S(1)} %get-tuple-element.75), channel_id=1, source_target_pairs={{1,2},{2,1},{3,4},{4,3},{5,6},{6,5},{9,10},{10,9},{11,12},{12,11},... | collective-permute-start | bytes 393224 | tf_op jit(solution)/shard_map/ppermute | solution.py:148
  108.8 0.9 collective-permute-start.24
  109.7 1.7 %collective-permute-done.22.q_outer = bf16[2,128,256]{2,1,0:T(8,128)(2,1)S(1)} collective-permute-done((bf16[2,128,256]{2,1,0:T(8,128)(2,1)S(1)}, bf16[2,128,256]{2,1,0:T(8,128)(2,1)S(1)}, u32[]{:S(2)}, u32[]{:S(2)}) %collective-permute-start.22) | collective-permute-done | bytes 131104 | tf_op jit(solution)/shard_map/ppermute | solution.py:148
  111.4 5.5 %shard_map.61 = (bf16[1,128,256]{2,1,0:T(8,128)(2,1)S(1)}, bf16[4,128,256]{2,1,0:T(8,128)(2,1)S(1)}, bf16[1,128,256]{2,1,0:T(8,128)(2,1)S(1)}) custom-call(s32[3]{0:T(128)S(1)} %add_convert_fusion.6.flags, bf16[4,128,256]{2,1,0:T(8,128)(2,1)S(1)} %fusion.14.q_mid, bf16[2,128,256]{2,1,0:T(8,128)(2,1)S(1)} %collective-permute-done.21.q_inner, ...), custom_call_target="tpu_custom_call" | custom-call | flops 1 | bytes 1 | tf_op jit(solution)/shard_map/pallas_call | solution.py:111
  116.9 3.5 %collective-permute-start.23 = (bf16[4,128,256]{2,1,0:T(8,128)(2,1)S(1)}, bf16[4,128,256]{2,1,0:T(8,128)(2,1)S(1)}, u32[]{:S(2)}, u32[]{:S(2)}) collective-permute-start(bf16[4,128,256]{2,1,0:T(8,128)(2,1)S(1)} %get-tuple-element.55.first_mid), channel_id=1, source_target_pairs={{8,16},{16,24},{9,17},{17,25},{10,18},{18,26},{11,19},{19,27},{12,... | collective-permute-start | bytes 786440 | tf_op jit(solution)/shard_map/ppermute | solution.py:169
  120.4 3.7 %shard_map.62 = bf16[4,128,256]{2,1,0:T(8,128)(2,1)S(1)} custom-call(bf16[1,128,256]{2,1,0:T(8,128)(2,1)S(1)} %get-tuple-element.56.first_low, bf16[4,128,256]{2,1,0:T(8,128)(2,1)S(1)} %get-tuple-element.55.first_mid, bf16[1,128,256]{2,1,0:T(8,128)(2,1)S(1)} %get-tuple-element.57.first_high, bf16[4,128,256]{2,1,0:T(8,128)(2,1)S(1)} %fusion.14.q_mid, ...), custom_call_target="tpu_custom_call" | custom-call | flops 1 | bytes 1 | tf_op jit(solution)/shard_map/pallas_call | solution.py:126
  124.0 1.9 %collective-permute-start.27 = (bf16[4,128,256]{2,1,0:T(8,128)(2,1)S(1)}, bf16[4,128,256]{2,1,0:T(8,128)(2,1)S(1)}, u32[]{:S(2)}, u32[]{:S(2)}) collective-permute-start(bf16[4,128,256]{2,1,0:T(8,128)(2,1)S(1)} %shard_map.62), channel_id=1, source_target_pairs={{8,16},{16,24},{9,17},{17,25},{10,18},{18,26},{11,19},{19,27},{12,... | collective-permute-start | bytes 786440 | tf_op jit(solution)/shard_map/ppermute | solution.py:169
  127.3 3.6 %collective-permute-start.26 = (bf16[1,128,256]{2,1,0:T(8,128)(2,1)S(1)}, bf16[1,128,256]{2,1,0:T(8,128)(2,1)S(1)}, u32[]{:S(2)}, u32[]{:S(2)}) collective-permute-start(bf16[1,128,256]{2,1,0:T(8,128)(2,1)S(1)} %get-tuple-element.73), channel_id=1, source_target_pairs={{1,2},{2,1},{3,4},{4,3},{5,6},{6,5},{9,10},{10,9},{11,12},{12,11},... | collective-permute-start | bytes 196616 | tf_op jit(solution)/shard_map/ppermute | solution.py:148
  131.0 3.0 %collective-permute-done.27 = bf16[4,128,256]{2,1,0:T(8,128)(2,1)S(1)} collective-permute-done((bf16[4,128,256]{2,1,0:T(8,128)(2,1)S(1)}, bf16[4,128,256]{2,1,0:T(8,128)(2,1)S(1)}, u32[]{:S(2)}, u32[]{:S(2)}) %collective-permute-start.27) | collective-permute-done | bytes 262176 | tf_op jit(solution)/shard_map/ppermute | solution.py:169
  134.2 4.2 %collective-permute-start.30 = (bf16[2,128,256]{2,1,0:T(8,128)(2,1)S(1)}, bf16[2,128,256]{2,1,0:T(8,128)(2,1)S(1)}, u32[]{:S(2)}, u32[]{:S(2)}) collective-permute-start(bf16[2,128,256]{2,1,0:T(8,128)(2,1)S(1)} %get-tuple-element.71), channel_id=1, source_target_pairs={{1,2},{2,1},{3,4},{4,3},{5,6},{6,5},{9,10},{10,9},{11,12},{12,11},... | collective-permute-start | bytes 393224 | tf_op jit(solution)/shard_map/ppermute | solution.py:148
  138.5 2.6 %collective-permute-done.30.q_outer = bf16[2,128,256]{2,1,0:T(8,128)(2,1)S(1)} collective-permute-done((bf16[2,128,256]{2,1,0:T(8,128)(2,1)S(1)}, bf16[2,128,256]{2,1,0:T(8,128)(2,1)S(1)}, u32[]{:S(2)}, u32[]{:S(2)}) %collective-permute-start.30) | collective-permute-done | bytes 131104 | tf_op jit(solution)/shard_map/ppermute | solution.py:148
  141.1 5.5 %shard_map.63 = (bf16[1,128,256]{2,1,0:T(8,128)(2,1)S(1)}, bf16[4,128,256]{2,1,0:T(8,128)(2,1)S(1)}, bf16[1,128,256]{2,1,0:T(8,128)(2,1)S(1)}) custom-call(s32[3]{0:T(128)S(1)} %add_convert_fusion.6.flags, bf16[4,128,256]{2,1,0:T(8,128)(2,1)S(1)} %fusion.12.q_mid, bf16[2,128,256]{2,1,0:T(8,128)(2,1)S(1)} %collective-permute-done.29.q_inner, ...), custom_call_target="tpu_custom_call" | custom-call | flops 1 | bytes 1 | tf_op jit(solution)/shard_map/pallas_call | solution.py:111
  146.6 3.7 %shard_map.64 = bf16[4,128,256]{2,1,0:T(8,128)(2,1)S(1)} custom-call(bf16[1,128,256]{2,1,0:T(8,128)(2,1)S(1)} %get-tuple-element.65.first_low, bf16[4,128,256]{2,1,0:T(8,128)(2,1)S(1)} %get-tuple-element.64.first_mid, bf16[1,128,256]{2,1,0:T(8,128)(2,1)S(1)} %get-tuple-element.66.first_high, bf16[4,128,256]{2,1,0:T(8,128)(2,1)S(1)} %fusion.12.q_mid, ...), custom_call_target="tpu_custom_call" | custom-call | flops 1 | bytes 1 | tf_op jit(solution)/shard_map/pallas_call | solution.py:126
  150.3 0.9 maximum_select_fusion
  (70 shorter events, 6.1 us)
Async XLA Ops:
  0.0 15.8 %collective-permute-start.3 = (bf16[2,4,128,256]{3,2,1,0:T(8,128)(2,1)}, bf16[2,4,128,256]{3,2,1,0:T(8,128)(2,1)S(1)}, u32[]{:S(2)}, u32[]{:S(2)}) collective-permute-start(bf16[2,4,128,256]{3,2,1,0:T(8,128)(2,1)} %bitcast.78), channel_id=1, source_target_pairs={{0,24},{8,16},{1,25},{9,17},{2,26},{10,18},{3,27},{11,19},{4,28},{... | collective-permute-start | bytes 1572872 | tf_op jit(solution)/shard_map/ppermute | solution.py:169
  15.8 0.8 copy-start.11
  16.6 10.0 %copy-start = (bf16[1,3,3,3,256,256]{5,4,3,2,1,0:T(8,128)(2,1)S(1)}, bf16[1,3,3,3,256,256]{5,4,3,2,1,0:T(8,128)(2,1)}, u32[]{:S(2)}) copy-start(bf16[1,3,3,3,256,256]{5,4,3,2,1,0:T(8,128)(2,1)} %param.8) | copy-start | bytes 10616836
  18.3 24.4 %copy-start.4 = (bf16[4,128,256]{2,1,0:T(8,128)(2,1)}, bf16[4,128,256]{2,1,0:T(8,128)(2,1)S(1)}, u32[]{:S(2)}) copy-start(bf16[4,128,256]{2,1,0:T(8,128)(2,1)S(1)} %get-tuple-element.68.q_mid) | copy-start | bytes 786436
  18.4 8.1 %collective-permute-start.1 = (bf16[3,128,256]{2,1,0:T(8,128)(2,1)S(1)}, bf16[3,128,256]{2,1,0:T(8,128)(2,1)S(1)}, u32[]{:S(2)}, u32[]{:S(2)}) collective-permute-start(bf16[3,128,256]{2,1,0:T(8,128)(2,1)S(1)} %pad_maximum_fusion.1), channel_id=1, source_target_pairs={{1,2},{2,1},{3,4},{4,3},{5,6},{6,5},{9,10},{10,9},{11,12},{12,11},... | collective-permute-start | bytes 589832 | tf_op jit(solution)/shard_map/ppermute | solution.py:148
  23.1 3.5 %collective-permute-start = (bf16[3,128,256]{2,1,0:T(8,128)(2,1)S(1)}, bf16[3,128,256]{2,1,0:T(8,128)(2,1)S(1)}, u32[]{:S(2)}, u32[]{:S(2)}) collective-permute-start(bf16[3,128,256]{2,1,0:T(8,128)(2,1)S(1)} %pad_maximum_fusion), channel_id=1, source_target_pairs={{0,1},{1,0},{2,3},{3,2},{4,5},{5,4},{6,7},{7,6},{8,9},{9,8},{10,11... | collective-permute-start | bytes 589832 | tf_op jit(solution)/shard_map/ppermute | solution.py:148
  23.3 19.4 %collective-permute-start.4 = (bf16[3,128,256]{2,1,0:T(8,128)(2,1)S(1)}, bf16[3,128,256]{2,1,0:T(8,128)(2,1)S(1)}, u32[]{:S(2)}, u32[]{:S(2)}) collective-permute-start(bf16[3,128,256]{2,1,0:T(8,128)(2,1)S(1)} %pad_maximum_fusion.2), channel_id=1, source_target_pairs={{0,1},{1,0},{2,3},{3,2},{4,5},{5,4},{6,7},{7,6},{8,9},{9,8},{10,11... | collective-permute-start | bytes 589832 | tf_op jit(solution)/shard_map/ppermute | solution.py:148
  26.6 10.4 %copy-start.1 = (bf16[1,3,3,3,256,256]{5,4,3,2,1,0:T(8,128)(2,1)S(1)}, bf16[1,3,3,3,256,256]{5,4,3,2,1,0:T(8,128)(2,1)}, u32[]{:S(2)}) copy-start(bf16[1,3,3,3,256,256]{5,4,3,2,1,0:T(8,128)(2,1)} %param.9) | copy-start | bytes 10616836
  32.1 21.2 %collective-permute-start.2 = (bf16[4,128,256]{2,1,0:T(8,128)(2,1)S(1)}, bf16[4,128,256]{2,1,0:T(8,128)(2,1)}, u32[]{:S(2)}, u32[]{:S(2)}) collective-permute-start(bf16[4,128,256]{2,1,0:T(8,128)(2,1)S(1)} %get-tuple-element.36.first_mid), channel_id=1, source_target_pairs={{0,8},{1,9},{2,10},{3,11},{4,12},{5,13},{6,14},{7,15}} | collective-permute-start | bytes 786440 | tf_op jit(solution)/shard_map/ppermute | solution.py:169
  33.5 9.2 %collective-permute-start.5 = (bf16[3,128,256]{2,1,0:T(8,128)(2,1)S(1)}, bf16[3,128,256]{2,1,0:T(8,128)(2,1)S(1)}, u32[]{:S(2)}, u32[]{:S(2)}) collective-permute-start(bf16[3,128,256]{2,1,0:T(8,128)(2,1)S(1)} %pad_maximum_fusion.3), channel_id=1, source_target_pairs={{1,2},{2,1},{3,4},{4,3},{5,6},{6,5},{9,10},{10,9},{11,12},{12,11},... | collective-permute-start | bytes 589832 | tf_op jit(solution)/shard_map/ppermute | solution.py:148
  41.3 24.6 %collective-permute-start.11 = (bf16[4,128,256]{2,1,0:T(8,128)(2,1)}, bf16[4,128,256]{2,1,0:T(8,128)(2,1)}, u32[]{:S(2)}, u32[]{:S(2)}) collective-permute-start(bf16[4,128,256]{2,1,0:T(8,128)(2,1)} %shard_map.58), channel_id=1, source_target_pairs={{0,8},{1,9},{2,10},{3,11},{4,12},{5,13},{6,14},{7,15}} | collective-permute-start | bytes 786440 | tf_op jit(solution)/shard_map/ppermute | solution.py:169
  48.9 0.6 copy-start.6
  49.5 0.6 copy-start.8
  50.2 16.5 %collective-permute-start.6 = (bf16[4,128,256]{2,1,0:T(8,128)(2,1)}, bf16[4,128,256]{2,1,0:T(8,128)(2,1)}, u32[]{:S(2)}, u32[]{:S(2)}) collective-permute-start(bf16[4,128,256]{2,1,0:T(8,128)(2,1)} %get-tuple-element.37.first_mid), channel_id=1, source_target_pairs={{0,8},{8,16},{16,24},{1,9},{9,17},{17,25},{2,10},{10,18},{18,26},{... | collective-permute-start | bytes 786440 | tf_op jit(solution)/shard_map/ppermute | solution.py:169
  53.3 13.4 %collective-permute-start.7 = (bf16[4,128,256]{2,1,0:T(8,128)(2,1)}, bf16[4,128,256]{2,1,0:T(8,128)(2,1)}, u32[]{:S(2)}, u32[]{:S(2)}) collective-permute-start(bf16[4,128,256]{2,1,0:T(8,128)(2,1)} %collective-permute-done.2), channel_id=1, source_target_pairs={{8,24},{9,25},{10,26},{11,27},{12,28},{13,29},{14,30},{15,31}} | collective-permute-start | bytes 786440 | tf_op jit(solution)/shard_map/ppermute | solution.py:169
  54.7 2.0 %copy-start.2 = (bf16[1,3,3,3,256,256]{5,4,3,2,1,0:T(8,128)(2,1)S(1)}, bf16[1,3,3,3,256,256]{5,4,3,2,1,0:T(8,128)(2,1)}, u32[]{:S(2)}) copy-start(bf16[1,3,3,3,256,256]{5,4,3,2,1,0:T(8,128)(2,1)} %param.9) | copy-start | bytes 10616836
  56.7 0.9 copy-start.5
  57.6 0.8 copy-start.7
  58.5 0.8 copy-start.9
  59.3 7.4 %copy-start.10 = (bf16[3,2,4,16,8,256]{5,4,3,2,1,0:T(8,128)(2,1)S(1)}, bf16[3,2,4,16,8,256]{5,4,3,2,1,0:T(8,128)(2,1)}, u32[]{:S(2)}) copy-start(bf16[3,2,4,16,8,256]{5,4,3,2,1,0:T(8,128)(2,1)} %param.7) | copy-start | bytes 4718596
  64.0 10.4 %collective-permute-start.10 = (bf16[4,128,256]{2,1,0:T(8,128)(2,1)S(1)}, bf16[4,128,256]{2,1,0:T(8,128)(2,1)S(1)}, u32[]{:S(2)}, u32[]{:S(2)}) collective-permute-start(bf16[4,128,256]{2,1,0:T(8,128)(2,1)S(1)} %shard_map.57), channel_id=1, source_target_pairs={{0,8},{8,16},{16,24},{1,9},{9,17},{17,25},{2,10},{10,18},{18,26},{... | collective-permute-start | bytes 786440 | tf_op jit(solution)/shard_map/ppermute | solution.py:169
  66.0 8.5 %collective-permute-start.12 = (bf16[4,128,256]{2,1,0:T(8,128)(2,1)}, bf16[4,128,256]{2,1,0:T(8,128)(2,1)S(1)}, u32[]{:S(2)}, u32[]{:S(2)}) collective-permute-start(bf16[4,128,256]{2,1,0:T(8,128)(2,1)} %collective-permute-done.11), channel_id=1, source_target_pairs={{8,24},{9,25},{10,26},{11,27},{12,28},{13,29},{14,30},{15,31}} | collective-permute-start | bytes 786440 | tf_op jit(solution)/shard_map/ppermute | solution.py:169
  67.8 6.6 %collective-permute-start.9 = (bf16[1,128,256]{2,1,0:T(8,128)(2,1)S(1)}, bf16[1,128,256]{2,1,0:T(8,128)(2,1)S(1)}, u32[]{:S(2)}, u32[]{:S(2)}) collective-permute-start(bf16[1,128,256]{2,1,0:T(8,128)(2,1)S(1)} %get-tuple-element.81), channel_id=1, source_target_pairs={{1,2},{2,1},{3,4},{4,3},{5,6},{6,5},{9,10},{10,9},{11,12},{12,11},... | collective-permute-start | bytes 196616 | tf_op jit(solution)/shard_map/ppermute | solution.py:148
  70.1 4.3 %collective-permute-start.8 = (bf16[1,128,256]{2,1,0:T(8,128)(2,1)S(1)}, bf16[1,128,256]{2,1,0:T(8,128)(2,1)S(1)}, u32[]{:S(2)}, u32[]{:S(2)}) collective-permute-start(bf16[1,128,256]{2,1,0:T(8,128)(2,1)S(1)} %get-tuple-element.82), channel_id=1, source_target_pairs={{0,1},{1,0},{2,3},{3,2},{4,5},{5,4},{6,7},{7,6},{8,9},{9,8},{10,11... | collective-permute-start | bytes 196616 | tf_op jit(solution)/shard_map/ppermute | solution.py:148
  74.6 6.3 %collective-permute-start.14 = (bf16[2,128,256]{2,1,0:T(8,128)(2,1)S(1)}, bf16[2,128,256]{2,1,0:T(8,128)(2,1)S(1)}, u32[]{:S(2)}, u32[]{:S(2)}) collective-permute-start(bf16[2,128,256]{2,1,0:T(8,128)(2,1)S(1)} %get-tuple-element.79), channel_id=1, source_target_pairs={{1,2},{2,1},{3,4},{4,3},{5,6},{6,5},{9,10},{10,9},{11,12},{12,11},... | collective-permute-start | bytes 393224 | tf_op jit(solution)/shard_map/ppermute | solution.py:148
  78.3 11.9 %copy-start.3 = (bf16[1,3,3,3,256,256]{5,4,3,2,1,0:T(8,128)(2,1)S(1)}, bf16[1,3,3,3,256,256]{5,4,3,2,1,0:T(8,128)(2,1)}, u32[]{:S(2)}) copy-start(bf16[1,3,3,3,256,256]{5,4,3,2,1,0:T(8,128)(2,1)} %param.9) | copy-start | bytes 10616836
  78.3 2.6 %collective-permute-start.13 = (bf16[2,128,256]{2,1,0:T(8,128)(2,1)S(1)}, bf16[2,128,256]{2,1,0:T(8,128)(2,1)S(1)}, u32[]{:S(2)}, u32[]{:S(2)}) collective-permute-start(bf16[2,128,256]{2,1,0:T(8,128)(2,1)S(1)} %get-tuple-element.80), channel_id=1, source_target_pairs={{0,1},{1,0},{2,3},{3,2},{4,5},{5,4},{6,7},{7,6},{8,9},{9,8},{10,11... | collective-permute-start | bytes 393224 | tf_op jit(solution)/shard_map/ppermute | solution.py:148
  78.4 18.1 %collective-permute-start.16 = (bf16[4,128,256]{2,1,0:T(8,128)(2,1)}, bf16[4,128,256]{2,1,0:T(8,128)(2,1)S(1)}, u32[]{:S(2)}, u32[]{:S(2)}) collective-permute-start(bf16[4,128,256]{2,1,0:T(8,128)(2,1)} %collective-permute-done.6), channel_id=1, source_target_pairs={{8,24},{9,25},{10,26},{11,27},{12,28},{13,29},{14,30},{15,31}} | collective-permute-start | bytes 786440 | tf_op jit(solution)/shard_map/ppermute | solution.py:169
  86.4 11.4 %collective-permute-start.15 = (bf16[4,128,256]{2,1,0:T(8,128)(2,1)S(1)}, bf16[4,128,256]{2,1,0:T(8,128)(2,1)S(1)}, u32[]{:S(2)}, u32[]{:S(2)}) collective-permute-start(bf16[4,128,256]{2,1,0:T(8,128)(2,1)S(1)} %get-tuple-element.47.first_mid), channel_id=1, source_target_pairs={{0,8},{8,16},{16,24},{1,9},{9,17},{17,25},{2,10},{10,18},{18,26},{... | collective-permute-start | bytes 786440 | tf_op jit(solution)/shard_map/ppermute | solution.py:169
  93.8 10.1 %collective-permute-start.19 = (bf16[4,128,256]{2,1,0:T(8,128)(2,1)S(1)}, bf16[4,128,256]{2,1,0:T(8,128)(2,1)S(1)}, u32[]{:S(2)}, u32[]{:S(2)}) collective-permute-start(bf16[4,128,256]{2,1,0:T(8,128)(2,1)S(1)} %shard_map.60), channel_id=1, source_target_pairs={{0,8},{8,16},{16,24},{1,9},{9,17},{17,25},{2,10},{10,18},{18,26},{... | collective-permute-start | bytes 786440 | tf_op jit(solution)/shard_map/ppermute | solution.py:169
  95.7 8.2 %collective-permute-start.20 = (bf16[4,128,256]{2,1,0:T(8,128)(2,1)S(1)}, bf16[4,128,256]{2,1,0:T(8,128)(2,1)S(1)}, u32[]{:S(2)}, u32[]{:S(2)}) collective-permute-start(bf16[4,128,256]{2,1,0:T(8,128)(2,1)S(1)} %collective-permute-done.10), channel_id=1, source_target_pairs={{8,24},{9,25},{10,26},{11,27},{12,28},{13,29},{14,30},{15,31}} | collective-permute-start | bytes 786440 | tf_op jit(solution)/shard_map/ppermute | solution.py:169
  97.9 6.0 %collective-permute-start.18 = (bf16[1,128,256]{2,1,0:T(8,128)(2,1)S(1)}, bf16[1,128,256]{2,1,0:T(8,128)(2,1)S(1)}, u32[]{:S(2)}, u32[]{:S(2)}) collective-permute-start(bf16[1,128,256]{2,1,0:T(8,128)(2,1)S(1)} %get-tuple-element.77), channel_id=1, source_target_pairs={{1,2},{2,1},{3,4},{4,3},{5,6},{6,5},{9,10},{10,9},{11,12},{12,11},... | collective-permute-start | bytes 196616 | tf_op jit(solution)/shard_map/ppermute | solution.py:148
  101.7 2.2 %collective-permute-start.17 = (bf16[1,128,256]{2,1,0:T(8,128)(2,1)S(1)}, bf16[1,128,256]{2,1,0:T(8,128)(2,1)S(1)}, u32[]{:S(2)}, u32[]{:S(2)}) collective-permute-start(bf16[1,128,256]{2,1,0:T(8,128)(2,1)S(1)} %get-tuple-element.78), channel_id=1, source_target_pairs={{0,1},{1,0},{2,3},{3,2},{4,5},{5,4},{6,7},{7,6},{8,9},{9,8},{10,11... | collective-permute-start | bytes 196616 | tf_op jit(solution)/shard_map/ppermute | solution.py:148
  104.1 7.3 %collective-permute-start.22 = (bf16[2,128,256]{2,1,0:T(8,128)(2,1)S(1)}, bf16[2,128,256]{2,1,0:T(8,128)(2,1)S(1)}, u32[]{:S(2)}, u32[]{:S(2)}) collective-permute-start(bf16[2,128,256]{2,1,0:T(8,128)(2,1)S(1)} %get-tuple-element.75), channel_id=1, source_target_pairs={{1,2},{2,1},{3,4},{4,3},{5,6},{6,5},{9,10},{10,9},{11,12},{12,11},... | collective-permute-start | bytes 393224 | tf_op jit(solution)/shard_map/ppermute | solution.py:148
  108.7 2.6 %collective-permute-start.21 = (bf16[2,128,256]{2,1,0:T(8,128)(2,1)S(1)}, bf16[2,128,256]{2,1,0:T(8,128)(2,1)S(1)}, u32[]{:S(2)}, u32[]{:S(2)}) collective-permute-start(bf16[2,128,256]{2,1,0:T(8,128)(2,1)S(1)} %get-tuple-element.76), channel_id=1, source_target_pairs={{0,1},{1,0},{2,3},{3,2},{4,5},{5,4},{6,7},{7,6},{8,9},{9,8},{10,11... | collective-permute-start | bytes 393224 | tf_op jit(solution)/shard_map/ppermute | solution.py:148
  108.8 17.8 %collective-permute-start.24 = (bf16[4,128,256]{2,1,0:T(8,128)(2,1)S(1)}, bf16[4,128,256]{2,1,0:T(8,128)(2,1)S(1)}, u32[]{:S(2)}, u32[]{:S(2)}) collective-permute-start(bf16[4,128,256]{2,1,0:T(8,128)(2,1)S(1)} %collective-permute-done.15), channel_id=1, source_target_pairs={{8,24},{9,25},{10,26},{11,27},{12,28},{13,29},{14,30},{15,31}} | collective-permute-start | bytes 786440 | tf_op jit(solution)/shard_map/ppermute | solution.py:169
  116.9 10.3 %collective-permute-start.23 = (bf16[4,128,256]{2,1,0:T(8,128)(2,1)S(1)}, bf16[4,128,256]{2,1,0:T(8,128)(2,1)S(1)}, u32[]{:S(2)}, u32[]{:S(2)}) collective-permute-start(bf16[4,128,256]{2,1,0:T(8,128)(2,1)S(1)} %get-tuple-element.55.first_mid), channel_id=1, source_target_pairs={{8,16},{16,24},{9,17},{17,25},{10,18},{18,26},{11,19},{19,27},{12,... | collective-permute-start | bytes 786440 | tf_op jit(solution)/shard_map/ppermute | solution.py:169
  124.0 10.0 %collective-permute-start.27 = (bf16[4,128,256]{2,1,0:T(8,128)(2,1)S(1)}, bf16[4,128,256]{2,1,0:T(8,128)(2,1)S(1)}, u32[]{:S(2)}, u32[]{:S(2)}) collective-permute-start(bf16[4,128,256]{2,1,0:T(8,128)(2,1)S(1)} %shard_map.62), channel_id=1, source_target_pairs={{8,16},{16,24},{9,17},{17,25},{10,18},{18,26},{11,19},{19,27},{12,... | collective-permute-start | bytes 786440 | tf_op jit(solution)/shard_map/ppermute | solution.py:169
  126.0 8.0 %collective-permute-start.28 = (bf16[4,128,256]{2,1,0:T(8,128)(2,1)S(1)}, bf16[4,128,256]{2,1,0:T(8,128)(2,1)S(1)}, u32[]{:S(2)}, u32[]{:S(2)}) collective-permute-start(bf16[4,128,256]{2,1,0:T(8,128)(2,1)S(1)} %collective-permute-done.19), channel_id=1, source_target_pairs={{8,24},{9,25},{10,26},{11,27},{12,28},{13,29},{14,30},{15,31}} | collective-permute-start | bytes 786440 | tf_op jit(solution)/shard_map/ppermute | solution.py:169
  127.3 6.7 %collective-permute-start.26 = (bf16[1,128,256]{2,1,0:T(8,128)(2,1)S(1)}, bf16[1,128,256]{2,1,0:T(8,128)(2,1)S(1)}, u32[]{:S(2)}, u32[]{:S(2)}) collective-permute-start(bf16[1,128,256]{2,1,0:T(8,128)(2,1)S(1)} %get-tuple-element.73), channel_id=1, source_target_pairs={{1,2},{2,1},{3,4},{4,3},{5,6},{6,5},{9,10},{10,9},{11,12},{12,11},... | collective-permute-start | bytes 196616 | tf_op jit(solution)/shard_map/ppermute | solution.py:148
  130.9 3.1 %collective-permute-start.25 = (bf16[1,128,256]{2,1,0:T(8,128)(2,1)S(1)}, bf16[1,128,256]{2,1,0:T(8,128)(2,1)S(1)}, u32[]{:S(2)}, u32[]{:S(2)}) collective-permute-start(bf16[1,128,256]{2,1,0:T(8,128)(2,1)S(1)} %get-tuple-element.74), channel_id=1, source_target_pairs={{0,1},{1,0},{2,3},{3,2},{4,5},{5,4},{6,7},{7,6},{8,9},{9,8},{10,11... | collective-permute-start | bytes 196616 | tf_op jit(solution)/shard_map/ppermute | solution.py:148
  134.2 6.9 %collective-permute-start.30 = (bf16[2,128,256]{2,1,0:T(8,128)(2,1)S(1)}, bf16[2,128,256]{2,1,0:T(8,128)(2,1)S(1)}, u32[]{:S(2)}, u32[]{:S(2)}) collective-permute-start(bf16[2,128,256]{2,1,0:T(8,128)(2,1)S(1)} %get-tuple-element.71), channel_id=1, source_target_pairs={{1,2},{2,1},{3,4},{4,3},{5,6},{6,5},{9,10},{10,9},{11,12},{12,11},... | collective-permute-start | bytes 393224 | tf_op jit(solution)/shard_map/ppermute | solution.py:148
  138.4 2.7 %collective-permute-start.29 = (bf16[2,128,256]{2,1,0:T(8,128)(2,1)S(1)}, bf16[2,128,256]{2,1,0:T(8,128)(2,1)S(1)}, u32[]{:S(2)}, u32[]{:S(2)}) collective-permute-start(bf16[2,128,256]{2,1,0:T(8,128)(2,1)S(1)} %get-tuple-element.72), channel_id=1, source_target_pairs={{0,1},{1,0},{2,3},{3,2},{4,5},{5,4},{6,7},{7,6},{8,9},{9,8},{10,11... | collective-permute-start | bytes 393224 | tf_op jit(solution)/shard_map/ppermute | solution.py:148

commit v3 on v2

--- a/solution.py
+++ b/solution.py
@@ -8,8 +8,7 @@
 from jax.sharding import PartitionSpec as P
 
 EPS = 1e-05
-LANES = 128
-VMEM_LIMIT = 48 * 1024 * 1024
+VMEM_LIMIT = 24 * 1024 * 1024
 
 
 def act(values):
@@ -19,90 +18,70 @@
 
 
 def fill(even, odd, at, values, width):
-    planes, voxels, chans = values.shape
-    rows = voxels // width
-    field = act(values).reshape(planes * rows, width, chans)
-    column = lax.broadcasted_iota(jnp.int32, field.shape, 1)
-    shifted = (
-        jnp.where(column == 0, 0.0, pltpu.roll(field, 1, 1)),
-        field,
-        jnp.where(column == width - 1, 0.0, pltpu.roll(field, width - 1, 1)),
-    )
+    planes, _, chans = values.shape
+    field = act(values)
     edge = jnp.zeros((planes, width, chans), jnp.float32)
-    for k, part in enumerate(shifted):
-        part = part.reshape(planes, voxels, chans)
-        moved = jnp.concatenate([edge, part, edge], axis=1).astype(jnp.bfloat16)
-        part = part.astype(jnp.bfloat16)
-        for c in range(chans // LANES):
-            piece = k * (chans // LANES) + c
-            columns = slice(c * LANES, (c + 1) * LANES)
-            even[piece, pl.ds(at, planes)] = part[:, :, columns]
-            odd[piece, pl.ds(at, planes)] = moved[:, :, columns]
-
-
-def convolve(even, odd, weights, copies, planes, width):
-    pieces, _, voxels, _ = even.shape
+    even[pl.ds(at, planes)] = field.astype(jnp.bfloat16)
+    odd[pl.ds(at, planes)] = jnp.concatenate([edge, field, edge], axis=1).astype(jnp.bfloat16)
+
+
+def convolve(even, odd, weights, planes, width):
+    _, voxels, chans = even.shape
     taps = []
     for i in range(3):
-        copies[i].wait()
         for j in range(3):
-            for piece in range(pieces):
-                source, row = (even, 0) if j == 1 else (odd, j * width)
-                part = source[piece, i : i + planes, row : row + voxels]
-                taps.append(part.reshape(planes * voxels, LANES))
+            part = even[i : i + planes] if j == 1 else odd[i : i + planes, j * width : j * width + voxels]
+            taps.append(part.reshape(planes * voxels, chans))
     slab = jnp.concatenate(taps, axis=-1)
-    total = jnp.dot(slab, weights[...], preferred_element_type=jnp.float32)
-    return total.reshape(planes, voxels, -1)
-
-
-def fetch(weights_hbm, weights, sems):
-    depth = weights.shape[0] // 3
-    copies = [
-        pltpu.make_async_copy(weights_hbm.at[pl.ds(i * depth, depth)], weights.at[pl.ds(i * depth, depth)], sems.at[i])
-        for i in range(3)
-    ]
-    for copy in copies:
-        copy.start()
-    return copies
-
-
-def first_kernel(width, flags, q_mid, q_inner, q_outer, p_mid, p_inner, p_outer, weights_hbm, low, mid, high, even, odd, weights, sems):
-    copies = fetch(weights_hbm, weights, sems)
+    total = None
+    for k in (1, 0, 2):
+        columns = jnp.concatenate([weights[(3 * n + k) * chans : (3 * n + k + 1) * chans] for n in range(9)], axis=0)
+        part = jnp.dot(slab, columns, preferred_element_type=jnp.float32).reshape(-1, width, chans)
+        column = lax.broadcasted_iota(jnp.int32, part.shape, 1)
+        if k == 0:
+            part = jnp.where(column == 0, 0.0, pltpu.roll(part, 1, 1))
+        elif k == 2:
+            part = jnp.where(column == width - 1, 0.0, pltpu.roll(part, width - 1, 1))
+        total = part if total is None else total + part
+    return total.reshape(planes, voxels, chans)
+
+
+def first_kernel(width, flags, q_mid, q_inner, q_outer, p_mid, p_inner, p_outer, weights, low, mid, high, even, odd):
     planes = q_mid.shape[0]
     above = flags[2] > 0
     fill(even, odd, 2, q_mid[...], width)
     inner, outer = q_inner[:2].astype(jnp.float32), q_outer[:2].astype(jnp.float32)
     fill(even, odd, 0, jnp.where(above, outer, inner), width)
     fill(even, odd, 2 + planes, jnp.where(above, inner, outer), width)
-    total = convolve(even, odd, weights, copies, planes + 2, width)
-    inner, outer = p_inner[-1:].astype(jnp.float32), p_outer[-1:].astype(jnp.float32)
+    total = convolve(even, odd, weights, planes + 2, width)
+    if p_inner.shape[0] == 2:
+        inner, outer = p_inner[pl.ds(flags[2], 1)], p_outer[pl.ds(1 - flags[2], 1)]
+    else:
+        inner, outer = p_inner[2:], p_outer[2:]
+    inner, outer = inner.astype(jnp.float32), outer.astype(jnp.float32)
     low[...] = jnp.where(flags[0] > 0, jnp.where(above, outer, inner) + total[:1], 0.0).astype(low.dtype)
     mid[...] = (p_mid[...].astype(jnp.float32) + total[1:-1]).astype(mid.dtype)
     high[...] = jnp.where(flags[1] > 0, jnp.where(above, inner, outer) + total[-1:], 0.0).astype(high.dtype)
 
 
-def second_kernel(width, first_low, first_mid, first_high, q_mid, weights_hbm, out, even, odd, weights, sems):
-    copies = fetch(weights_hbm, weights, sems)
+def second_kernel(width, first_low, first_mid, first_high, q_mid, weights, out, even, odd):
     planes = q_mid.shape[0]
     fill(even, odd, 0, first_low[...], width)
     fill(even, odd, 1, first_mid[...], width)
     fill(even, odd, 1 + planes, first_high[...], width)
-    total = convolve(even, odd, weights, copies, planes, width)
+    total = convolve(even, odd, weights, planes, width)
     out[...] = (q_mid[...].astype(jnp.float32) + total).astype(out.dtype)
 
 
 def scratch(planes, voxels, chans, width):
     return [
-        pltpu.VMEM((3 * chans // LANES, planes, voxels, LANES), jnp.bfloat16),
-        pltpu.VMEM((3 * chans // LANES, planes, voxels + 2 * width, LANES), jnp.bfloat16),
-        pltpu.VMEM((27 * chans, chans), jnp.bfloat16),
-        pltpu.SemaphoreType.DMA((3,)),
+        pltpu.VMEM((planes, voxels, chans), jnp.bfloat16),
+        pltpu.VMEM((planes, voxels + 2 * width, chans), jnp.bfloat16),
     ]
 
 
 VMEM = pl.BlockSpec(memory_space=pltpu.VMEM)
 SMEM = pl.BlockSpec(memory_space=pltpu.SMEM)
-ANY = pl.BlockSpec(memory_space=pl.ANY)
 
 
 def first_half(flags, q, q_halo, p, p_halo, weights, width):
@@ -111,7 +90,7 @@
     return pl.pallas_call(
         functools.partial(first_kernel, width),
         out_shape=(shape(1), shape(planes), shape(1)),
-        in_specs=[SMEM] + [VMEM] * 6 + [ANY],
+        in_specs=[SMEM] + [VMEM] * 7,
         out_specs=(VMEM, VMEM, VMEM),
         scratch_shapes=scratch(planes + 4, voxels, chans, width),
         compiler_params=pltpu.CompilerParams(vmem_limit_bytes=VMEM_LIMIT),
@@ -126,7 +105,7 @@
     return pl.pallas_call(
         functools.partial(second_kernel, width),
         out_shape=jax.ShapeDtypeStruct(q.shape, jnp.bfloat16),
-        in_specs=[VMEM] * 4 + [ANY],
+        in_specs=[VMEM] * 5,
         out_specs=VMEM,
         scratch_shapes=scratch(planes + 2, voxels, chans, width),
         compiler_params=pltpu.CompilerParams(vmem_limit_bytes=VMEM_LIMIT),
@@ -136,18 +115,29 @@
     )(*first, q, weights)
 
 
-def halo(blocks, widths, above):
+def boundary(block, upward, width):
+    return lax.dynamic_slice_in_dim(block, jnp.where(upward, block.shape[0] - width, 0), width, axis=0)
+
+
+def swapped(blocks, widths, above):
     count = lax.axis_size("depth")
 
     def swap(upward, base):
-        parts = [
-            lax.dynamic_slice_in_dim(block, jnp.where(upward, block.shape[0] - width, 0), width, axis=0)
-            for block, width in zip(blocks, widths)
-        ]
+        parts = [boundary(block, upward, width) for block, width in zip(blocks, widths)]
         pairs = [pair for i in range(base, count - 1, 2) for pair in ((i, i + 1), (i + 1, i))]
         return lax.ppermute(jnp.concatenate(parts, axis=0), "depth", pairs)
 
     return swap(above, 0), swap(jnp.logical_not(above), 1)
+
+
+def gathered(block, above):
+    count = lax.axis_size("depth")
+
+    def gather(upward, base):
+        groups = [[i, (i + 1) % count] for i in range(base, count, 2)]
+        return lax.all_gather(boundary(block, upward, 1), "depth", axis_index_groups=groups, tiled=True)
+
+    return gather(above, 0), gather(jnp.logical_not(above), 1)
 
 
 def local(resident, previous, incoming, first_weights, second_weights):
@@ -179,7 +169,7 @@
     out = emitted = None
     newer, older, relayed, direct = {}, {}, {}, {}
 
-    def arrived(slot, stream):
+    def arrived(slot, stream, mirrored=None):
         fresh = incoming[min(slot, ticks - 1) - 1, stream]
         if slot == 1:
             return jnp.where(section == 0, fresh, join(resident[stream], mirrored[stream]))
@@ -191,14 +181,16 @@
 
     for slot in range(ticks + 1):
         if slot < 2:
-            p, q = resident if slot == 0 else (arrived(slot, 0), arrived(slot, 1))
-            p_halo = q_halo = halo((q, p), (2, 1), above)
+            if slot == 1:
+                mirrored, _ = lax.optimization_barrier((mirrored, first[1]))
+            p, q = resident if slot == 0 else (arrived(slot, 0, mirrored), arrived(slot, 1, mirrored))
+            p_halo = q_halo = swapped((q, p), (2, 1), above)
         else:
             p = arrived(slot, 0)
-            p_halo = halo((p,), (1,), above)
-            p, p_halo, newer[1] = lax.optimization_barrier((p, p_halo, newer[1]))
+            p_halo = gathered(p, above)
+            p, newer[1] = lax.optimization_barrier((p, newer[1]))
             q = arrived(slot, 1)
-            q_halo = halo((q,), (2,), above)
+            q_halo = swapped((q,), (2,), above)
         onward = []
         if slot < ticks:
             onward = [(0, 1)] if slot < ticks - 1 else []

time: 153 us -> 136 us (0.89)
  blocking collectives: 0 us -> 20.4 us
  Pallas kernels: 48.3 us -> 31 us
  starting transfers between devices: 56.7 us -> 44.2 us
  waiting for transfers between devices: 33.3 us -> 28.5 us
  local copies, waits for them, and re-layouts: 7.96 us -> 4.27 us
    all_gather x0 -> x6, blocking collectives: none -> 20.4 us  [gather(): lax.all_gather(boundary(block, upward, 1), 'depth', axis_index_groups=gro...]
    ppermute x16 -> x10, starting transfers between devices: 31.5 us -> 18.4 us  [swap(): return lax.ppermute(jnp.concatenate(parts, axis=0), 'depth', pairs)]
    pallas_call x5, Pallas kernels: 28.2 us -> 18.8 us  [first_half(): pl.pallas_call(functools.partial(first_kernel, width), out_shape=(shape(1...]
    pallas_call x5, Pallas kernels: 20.1 us -> 12.2 us  [second_half(): pl.pallas_call(functools.partial(second_kernel, width), out_shape=jax.Sha...]
    ppermute x16 -> x10, waiting for transfers between devices: 8.84 us -> 4.09 us  [swap(): return lax.ppermute(jnp.concatenate(parts, axis=0), 'depth', pairs)]
    unnamed x24 -> x16, local copies, waits for them, and re-layouts: 6.68 us -> 2.97 us
  transfers between devices with their start and end apart: 31 -> 25, of which waited for: 11 -> 7; matrix products, arithmetic and copies ran while one was open for 2% -> 3% of each run, Pallas kernels for 26% -> 19%
where the time goes in v3:
time: 136 us; the launch traced here: 134 us
  starting transfers between devices  44.2 us (32%)
  Pallas kernels  31 us (23%)
  waiting for transfers between devices  28.5 us (21%)
  blocking collectives  20.4 us (15%)
  other arithmetic  5.14 us (4%)
  local copies, waits for them, and re-layouts  4.27 us (3%)
    ppermute x15, starting transfers between devices, send(): return lax.ppermute(block, 'section', pairs) if pairs else block  25.9 us
    ppermute x15, waiting for transfers between devices, send(): return lax.ppermute(block, 'section', pairs) if pairs else block  24.4 us
    all_gather x6, blocking collectives, gather(): lax.all_gather(boundary(block, upward, 1), 'depth', axis_index_groups=gro...  20.4 us
    pallas_call x5, Pallas kernels, first_half(): pl.pallas_call(functools.partial(first_kernel, width), out_shape=(shape(1...  18.8 us
    ppermute x10, starting transfers between devices, swap(): return lax.ppermute(jnp.concatenate(parts, axis=0), 'depth', pairs)  18.4 us
    pallas_call x5, Pallas kernels, second_half(): pl.pallas_call(functools.partial(second_kernel, width), out_shape=jax.Sha...  12.2 us
    ppermute x10, waiting for transfers between devices, swap(): return lax.ppermute(jnp.concatenate(parts, axis=0), 'depth', pairs)  4.09 us
    unnamed x16, local copies, waits for them, and re-layouts  2.97 us
  transfers between devices with their start and end apart: 25, of which 7 were waited for; matrix products, arithmetic and copies ran while one was open for 3% of the time, Pallas kernels for 19%

profile of v3, /device:TPU:13, one launch (start us, length us, event | category | flops | bytes accessed | tf_op | source)
XLA Modules:
  0.0 134.0 jit_solution(6805306987608758366)
XLA Ops:
  0.0 1.3 collective-permute-start.3
  1.3 1.1 slice_bitcast_fusion.6
  2.5 0.7 collective-permute-start
  3.2 3.1 %collective-permute-start.1 = (bf16[3,128,256]{2,1,0:T(8,128)(2,1)S(1)}, bf16[3,128,256]{2,1,0:T(8,128)(2,1)S(1)}, u32[]{:S(2)}, u32[]{:S(2)}) collective-permute-start(bf16[3,128,256]{2,1,0:T(8,128)(2,1)S(1)} %pad_maximum_fusion.1), channel_id=1, source_target_pairs={{1,2},{2,1},{3,4},{4,3},{5,6},{6,5},{9,10},{10,9},{11,12},{12,11},... | collective-permute-start | bytes 589832 | tf_op jit(solution)/shard_map/ppermute | solution.py:128
  6.5 4.1 %collective-permute-done.1.q_outer.p_outer = bf16[3,128,256]{2,1,0:T(8,128)(2,1)S(1)} collective-permute-done((bf16[3,128,256]{2,1,0:T(8,128)(2,1)S(1)}, bf16[3,128,256]{2,1,0:T(8,128)(2,1)S(1)}, u32[]{:S(2)}, u32[]{:S(2)}) %collective-permute-start.1) | collective-permute-done | bytes 196640 | tf_op jit(solution)/shard_map/ppermute | solution.py:128
  10.5 2.0 %copy-done = bf16[1,3,3,3,256,256]{5,4,3,2,1,0:T(8,128)(2,1)S(1)} copy-done((bf16[1,3,3,3,256,256]{5,4,3,2,1,0:T(8,128)(2,1)S(1)}, bf16[1,3,3,3,256,256]{5,4,3,2,1,0:T(8,128)(2,1)}, u32[]{:S(2)}) %copy-start) | copy-done | bytes 3538968
  12.5 3.6 %shard_map.55 = (bf16[1,128,256]{2,1,0:T(8,128)(2,1)S(1)}, bf16[4,128,256]{2,1,0:T(8,128)(2,1)S(1)}, bf16[1,128,256]{2,1,0:T(8,128)(2,1)S(1)}) custom-call(s32[3]{0:T(128)S(1)} %add_convert_fusion.6.flags, bf16[4,128,256]{2,1,0:T(8,128)(2,1)S(1)} %get-tuple-element.60.q_mid, bf16[3,128,256]{2,1,0:T(8,128)(2,1)S(1)} %collective-permute-done.q_inner.p_inner, ...), custom_call_target="tpu_custom_call" | custom-call | flops 1 | bytes 1 | tf_op jit(solution)/shard_map/pallas_call | solution.py:90
  16.2 1.4 %collective-permute-start.2 = (bf16[4,128,256]{2,1,0:T(8,128)(2,1)S(1)}, bf16[4,128,256]{2,1,0:T(8,128)(2,1)}, u32[]{:S(2)}, u32[]{:S(2)}) collective-permute-start(bf16[4,128,256]{2,1,0:T(8,128)(2,1)S(1)} %get-tuple-element.31.first_mid), channel_id=1, source_target_pairs={{0,8},{1,9},{2,10},{3,11},{4,12},{5,13},{6,14},{7,15}} | collective-permute-start | bytes 786440 | tf_op jit(solution)/shard_map/ppermute | solution.py:159
  17.5 1.4 %fusion.10 = (bf16[4,128,256]{2,1,0:T(8,128)(2,1)S(1)}, bf16[4,128,256]{2,1,0:T(8,128)(2,1)S(1)}) fusion(bf16[3,2,4,128,256]{4,3,2,1,0:T(8,128)(2,1)} %bitcast.67, bf16[2,4,128,256]{3,2,1,0:T(8,128)(2,1)S(1)} %collective-permute-done.3, pred[]{:T(512)S(6)} %ge.3, pred[]{:T(512)S(6)} %eq.10, bf16[1,2,4,16,8,256]{5,4,3,2,1,0:T(8,128)(2,1)S(1)} %copy-done.7), kind=kLoop, calls=%fused_computation.19 | loop fusion | flops 1572864 | bytes 2097154 | tf_op jit(solution)/shard_map/jit(_where)/select_n | solution.py:175
  19.2 3.6 %collective-permute-start.5 = (bf16[3,128,256]{2,1,0:T(8,128)(2,1)S(1)}, bf16[3,128,256]{2,1,0:T(8,128)(2,1)S(1)}, u32[]{:S(2)}, u32[]{:S(2)}) collective-permute-start(bf16[3,128,256]{2,1,0:T(8,128)(2,1)S(1)} %pad_maximum_fusion.3), channel_id=1, source_target_pairs={{1,2},{2,1},{3,4},{4,3},{5,6},{6,5},{9,10},{10,9},{11,12},{12,11},... | collective-permute-start | bytes 589832 | tf_op jit(solution)/shard_map/ppermute | solution.py:128
  22.8 0.9 copy-done.5
  23.7 2.1 %shard_map.58 = bf16[4,128,256]{2,1,0:T(8,128)(2,1)S(1)} custom-call(bf16[1,128,256]{2,1,0:T(8,128)(2,1)S(1)} %get-tuple-element.37.first_low, bf16[4,128,256]{2,1,0:T(8,128)(2,1)S(1)} %get-tuple-element.31.first_mid, bf16[1,128,256]{2,1,0:T(8,128)(2,1)S(1)} %get-tuple-element.38.first_high, bf16[4,128,256]{2,1,0:T(8,128)(2,1)S(1)} %copy-done.5, ...), custom_call_target="tpu_custom_call" | custom-call | flops 1 | bytes 1 | tf_op jit(solution)/shard_map/pallas_call | solution.py:105
  25.8 1.4 %collective-permute-start.9 = (bf16[4,128,256]{2,1,0:T(8,128)(2,1)S(1)}, bf16[4,128,256]{2,1,0:T(8,128)(2,1)}, u32[]{:S(2)}, u32[]{:S(2)}) collective-permute-start(bf16[4,128,256]{2,1,0:T(8,128)(2,1)S(1)} %shard_map.58), channel_id=1, source_target_pairs={{0,8},{1,9},{2,10},{3,11},{4,12},{5,13},{6,14},{7,15}} | collective-permute-start | bytes 786440 | tf_op jit(solution)/shard_map/ppermute | solution.py:159
  27.2 1.4 %collective-permute-start.7 = (bf16[4,128,256]{2,1,0:T(8,128)(2,1)}, bf16[4,128,256]{2,1,0:T(8,128)(2,1)}, u32[]{:S(2)}, u32[]{:S(2)}) collective-permute-start(bf16[4,128,256]{2,1,0:T(8,128)(2,1)} %collective-permute-done.2), channel_id=1, source_target_pairs={{8,24},{9,25},{10,26},{11,27},{12,28},{13,29},{14,30},{15,31}} | collective-permute-start | bytes 786440 | tf_op jit(solution)/shard_map/ppermute | solution.py:159
  28.6 4.3 %shard_map.56 = (bf16[1,128,256]{2,1,0:T(8,128)(2,1)S(1)}, bf16[4,128,256]{2,1,0:T(8,128)(2,1)}, bf16[1,128,256]{2,1,0:T(8,128)(2,1)S(1)}) custom-call(s32[3]{0:T(128)S(1)} %add_convert_fusion.6.flags, bf16[4,128,256]{2,1,0:T(8,128)(2,1)S(1)} %get-tuple-element.58.q_mid, bf16[3,128,256]{2,1,0:T(8,128)(2,1)S(1)} %collective-permute-done.4.q_inner.p_inner, ...), custom_call_target="tpu_custom_call" | custom-call | flops 1 | bytes 1 | tf_op jit(solution)/shard_map/pallas_call | solution.py:90
  32.9 3.1 %collective-permute-start.6 = (bf16[4,128,256]{2,1,0:T(8,128)(2,1)}, bf16[4,128,256]{2,1,0:T(8,128)(2,1)}, u32[]{:S(2)}, u32[]{:S(2)}) collective-permute-start(bf16[4,128,256]{2,1,0:T(8,128)(2,1)} %get-tuple-element.33.first_mid), channel_id=1, source_target_pairs={{0,8},{8,16},{16,24},{1,9},{9,17},{17,25},{2,10},{10,18},{18,26},{... | collective-permute-start | bytes 786440 | tf_op jit(solution)/shard_map/ppermute | solution.py:159
  35.9 3.8 %shard_map.57 = bf16[4,128,256]{2,1,0:T(8,128)(2,1)} custom-call(bf16[1,128,256]{2,1,0:T(8,128)(2,1)S(1)} %get-tuple-element.34.first_low, bf16[4,128,256]{2,1,0:T(8,128)(2,1)} %get-tuple-element.33.first_mid, bf16[1,128,256]{2,1,0:T(8,128)(2,1)S(1)} %get-tuple-element.35.first_high, bf16[4,128,256]{2,1,0:T(8,128)(2,1)S(1)} %get-tuple-element.58.q_mid, ...), custom_call_target="tpu_custom_call" | custom-call | flops 1 | bytes 1 | tf_op jit(solution)/shard_map/pallas_call | solution.py:105
  39.7 1.9 %collective-permute-start.8 = (bf16[4,128,256]{2,1,0:T(8,128)(2,1)}, bf16[4,128,256]{2,1,0:T(8,128)(2,1)}, u32[]{:S(2)}, u32[]{:S(2)}) collective-permute-start(bf16[4,128,256]{2,1,0:T(8,128)(2,1)} %shard_map.57), channel_id=1, source_target_pairs={{0,8},{8,16},{16,24},{1,9},{9,17},{17,25},{2,10},{10,18},{18,26},{... | collective-permute-start | bytes 786440 | tf_op jit(solution)/shard_map/ppermute | solution.py:159
  41.6 1.4 %collective-permute-start.10 = (bf16[4,128,256]{2,1,0:T(8,128)(2,1)}, bf16[4,128,256]{2,1,0:T(8,128)(2,1)}, u32[]{:S(2)}, u32[]{:S(2)}) collective-permute-start(bf16[4,128,256]{2,1,0:T(8,128)(2,1)} %collective-permute-done.9), channel_id=1, source_target_pairs={{8,24},{9,25},{10,26},{11,27},{12,28},{13,29},{14,30},{15,31}} | collective-permute-start | bytes 786440 | tf_op jit(solution)/shard_map/ppermute | solution.py:159
  43.0 2.2 %collective-permute-done.6 = bf16[4,128,256]{2,1,0:T(8,128)(2,1)} collective-permute-done((bf16[4,128,256]{2,1,0:T(8,128)(2,1)}, bf16[4,128,256]{2,1,0:T(8,128)(2,1)}, u32[]{:S(2)}, u32[]{:S(2)}) %collective-permute-start.6) | collective-permute-done | bytes 262176 | tf_op jit(solution)/shard_map/ppermute | solution.py:159
  45.3 1.1 fusion.17.p_mid
  46.4 4.6 %collective-permute-done.8 = bf16[4,128,256]{2,1,0:T(8,128)(2,1)} collective-permute-done((bf16[4,128,256]{2,1,0:T(8,128)(2,1)}, bf16[4,128,256]{2,1,0:T(8,128)(2,1)}, u32[]{:S(2)}, u32[]{:S(2)}) %collective-permute-start.8) | collective-permute-done | bytes 262176 | tf_op jit(solution)/shard_map/ppermute | solution.py:159
  51.0 1.1 fusion.16.q_mid
  52.6 2.9 %collective-permute-start.12 = (bf16[2,128,256]{2,1,0:T(8,128)(2,1)S(1)}, bf16[2,128,256]{2,1,0:T(8,128)(2,1)S(1)}, u32[]{:S(2)}, u32[]{:S(2)}) collective-permute-start(bf16[2,128,256]{2,1,0:T(8,128)(2,1)S(1)} %get-tuple-element.71), channel_id=1, source_target_pairs={{1,2},{2,1},{3,4},{4,3},{5,6},{6,5},{9,10},{10,9},{11,12},{12,11},... | collective-permute-start | bytes 393224 | tf_op jit(solution)/shard_map/ppermute | solution.py:128
  56.3 1.9 %all_gather.18.p_inner = bf16[2,128,256]{2,1,0:T(8,128)(2,1)S(1)} all-gather(bf16[1,128,256]{2,1,0:T(8,128)(2,1)S(1)} %get-tuple-element.70), channel_id=1, replica_groups={{0,1},{2,3},{4,5},{6,7},{8,9},{10,11},{12,13},{14,15},{16,17},{18,19},{..., dimensions={0}, use_global_device_ids=true | all-gather | bytes 196608 | tf_op jit(solution)/shard_map/all_gather | solution.py:138
  58.2 4.7 %all_gather.19.p_outer = bf16[2,128,256]{2,1,0:T(8,128)(2,1)S(1)} all-gather(bf16[1,128,256]{2,1,0:T(8,128)(2,1)S(1)} %get-tuple-element.69), channel_id=1, replica_groups={{1,2},{3,4},{5,6},{7,0},{9,10},{11,12},{13,14},{15,8},{17,18},{19,20},{..., dimensions={0}, use_global_device_ids=true | all-gather | bytes 196608 | tf_op jit(solution)/shard_map/all_gather | solution.py:138
  62.9 3.6 %shard_map.59 = (bf16[1,128,256]{2,1,0:T(8,128)(2,1)S(1)}, bf16[4,128,256]{2,1,0:T(8,128)(2,1)S(1)}, bf16[1,128,256]{2,1,0:T(8,128)(2,1)S(1)}) custom-call(s32[3]{0:T(128)S(1)} %add_convert_fusion.6.flags, bf16[4,128,256]{2,1,0:T(8,128)(2,1)S(1)} %fusion.16.q_mid, bf16[2,128,256]{2,1,0:T(8,128)(2,1)S(1)} %collective-permute-done.11.q_inner, ...), custom_call_target="tpu_custom_call" | custom-call | flops 1 | bytes 1 | tf_op jit(solution)/shard_map/pallas_call | solution.py:90
  66.6 4.5 %collective-permute-start.13 = (bf16[4,128,256]{2,1,0:T(8,128)(2,1)S(1)}, bf16[4,128,256]{2,1,0:T(8,128)(2,1)S(1)}, u32[]{:S(2)}, u32[]{:S(2)}) collective-permute-start(bf16[4,128,256]{2,1,0:T(8,128)(2,1)S(1)} %get-tuple-element.41.first_mid), channel_id=1, source_target_pairs={{0,8},{8,16},{16,24},{1,9},{9,17},{17,25},{2,10},{10,18},{18,26},{... | collective-permute-start | bytes 786440 | tf_op jit(solution)/shard_map/ppermute | solution.py:159
  71.1 2.1 %shard_map.60 = bf16[4,128,256]{2,1,0:T(8,128)(2,1)S(1)} custom-call(bf16[1,128,256]{2,1,0:T(8,128)(2,1)S(1)} %get-tuple-element.42.first_low, bf16[4,128,256]{2,1,0:T(8,128)(2,1)S(1)} %get-tuple-element.41.first_mid, bf16[1,128,256]{2,1,0:T(8,128)(2,1)S(1)} %get-tuple-element.43.first_high, bf16[4,128,256]{2,1,0:T(8,128)(2,1)S(1)} %fusion.16.q_mid, ...), custom_call_target="tpu_custom_call" | custom-call | flops 1 | bytes 1 | tf_op jit(solution)/shard_map/pallas_call | solution.py:105
  73.2 1.9 %collective-permute-start.15 = (bf16[4,128,256]{2,1,0:T(8,128)(2,1)S(1)}, bf16[4,128,256]{2,1,0:T(8,128)(2,1)S(1)}, u32[]{:S(2)}, u32[]{:S(2)}) collective-permute-start(bf16[4,128,256]{2,1,0:T(8,128)(2,1)S(1)} %shard_map.60), channel_id=1, source_target_pairs={{0,8},{8,16},{16,24},{1,9},{9,17},{17,25},{2,10},{10,18},{18,26},{... | collective-permute-start | bytes 786440 | tf_op jit(solution)/shard_map/ppermute | solution.py:159
  75.8 3.5 %collective-permute-done.13 = bf16[4,128,256]{2,1,0:T(8,128)(2,1)S(1)} collective-permute-done((bf16[4,128,256]{2,1,0:T(8,128)(2,1)S(1)}, bf16[4,128,256]{2,1,0:T(8,128)(2,1)S(1)}, u32[]{:S(2)}, u32[]{:S(2)}) %collective-permute-start.13) | collective-permute-done | bytes 262176 | tf_op jit(solution)/shard_map/ppermute | solution.py:159
  79.4 5.5 %collective-permute-done.15 = bf16[4,128,256]{2,1,0:T(8,128)(2,1)S(1)} collective-permute-done((bf16[4,128,256]{2,1,0:T(8,128)(2,1)S(1)}, bf16[4,128,256]{2,1,0:T(8,128)(2,1)S(1)}, u32[]{:S(2)}, u32[]{:S(2)}) %collective-permute-start.15) | collective-permute-done | bytes 262176 | tf_op jit(solution)/shard_map/ppermute | solution.py:159
  85.7 2.9 %collective-permute-start.18 = (bf16[2,128,256]{2,1,0:T(8,128)(2,1)S(1)}, bf16[2,128,256]{2,1,0:T(8,128)(2,1)S(1)}, u32[]{:S(2)}, u32[]{:S(2)}) collective-permute-start(bf16[2,128,256]{2,1,0:T(8,128)(2,1)S(1)} %get-tuple-element.67), channel_id=1, source_target_pairs={{1,2},{2,1},{3,4},{4,3},{5,6},{6,5},{9,10},{10,9},{11,12},{12,11},... | collective-permute-start | bytes 393224 | tf_op jit(solution)/shard_map/ppermute | solution.py:128
  89.2 1.9 %all_gather.20.p_inner = bf16[2,128,256]{2,1,0:T(8,128)(2,1)S(1)} all-gather(bf16[1,128,256]{2,1,0:T(8,128)(2,1)S(1)} %get-tuple-element.66), channel_id=1, replica_groups={{0,1},{2,3},{4,5},{6,7},{8,9},{10,11},{12,13},{14,15},{16,17},{18,19},{..., dimensions={0}, use_global_device_ids=true | all-gather | bytes 196608 | tf_op jit(solution)/shard_map/all_gather | solution.py:138
  91.1 4.7 %all_gather.21.p_outer = bf16[2,128,256]{2,1,0:T(8,128)(2,1)S(1)} all-gather(bf16[1,128,256]{2,1,0:T(8,128)(2,1)S(1)} %get-tuple-element.65), channel_id=1, replica_groups={{1,2},{3,4},{5,6},{7,0},{9,10},{11,12},{13,14},{15,8},{17,18},{19,20},{..., dimensions={0}, use_global_device_ids=true | all-gather | bytes 196608 | tf_op jit(solution)/shard_map/all_gather | solution.py:138
  95.9 3.6 %shard_map.61 = (bf16[1,128,256]{2,1,0:T(8,128)(2,1)S(1)}, bf16[4,128,256]{2,1,0:T(8,128)(2,1)S(1)}, bf16[1,128,256]{2,1,0:T(8,128)(2,1)S(1)}) custom-call(s32[3]{0:T(128)S(1)} %add_convert_fusion.6.flags, bf16[4,128,256]{2,1,0:T(8,128)(2,1)S(1)} %fusion.14.q_mid, bf16[2,128,256]{2,1,0:T(8,128)(2,1)S(1)} %collective-permute-done.17.q_inner, ...), custom_call_target="tpu_custom_call" | custom-call | flops 1 | bytes 1 | tf_op jit(solution)/shard_map/pallas_call | solution.py:90
  99.5 3.1 %collective-permute-start.19 = (bf16[4,128,256]{2,1,0:T(8,128)(2,1)S(1)}, bf16[4,128,256]{2,1,0:T(8,128)(2,1)S(1)}, u32[]{:S(2)}, u32[]{:S(2)}) collective-permute-start(bf16[4,128,256]{2,1,0:T(8,128)(2,1)S(1)} %get-tuple-element.47.first_mid), channel_id=1, source_target_pairs={{8,16},{16,24},{9,17},{17,25},{10,18},{18,26},{11,19},{19,27},{12,... | collective-permute-start | bytes 786440 | tf_op jit(solution)/shard_map/ppermute | solution.py:159
  102.6 2.1 %shard_map.62 = bf16[4,128,256]{2,1,0:T(8,128)(2,1)S(1)} custom-call(bf16[1,128,256]{2,1,0:T(8,128)(2,1)S(1)} %get-tuple-element.48.first_low, bf16[4,128,256]{2,1,0:T(8,128)(2,1)S(1)} %get-tuple-element.47.first_mid, bf16[1,128,256]{2,1,0:T(8,128)(2,1)S(1)} %get-tuple-element.49.first_high, bf16[4,128,256]{2,1,0:T(8,128)(2,1)S(1)} %fusion.14.q_mid, ...), custom_call_target="tpu_custom_call" | custom-call | flops 1 | bytes 1 | tf_op jit(solution)/shard_map/pallas_call | solution.py:105
  104.7 1.9 %collective-permute-start.21 = (bf16[4,128,256]{2,1,0:T(8,128)(2,1)S(1)}, bf16[4,128,256]{2,1,0:T(8,128)(2,1)S(1)}, u32[]{:S(2)}, u32[]{:S(2)}) collective-permute-start(bf16[4,128,256]{2,1,0:T(8,128)(2,1)S(1)} %shard_map.62), channel_id=1, source_target_pairs={{8,16},{16,24},{9,17},{17,25},{10,18},{18,26},{11,19},{19,27},{12,... | collective-permute-start | bytes 786440 | tf_op jit(solution)/shard_map/ppermute | solution.py:159
  107.3 3.0 %collective-permute-done.19 = bf16[4,128,256]{2,1,0:T(8,128)(2,1)S(1)} collective-permute-done((bf16[4,128,256]{2,1,0:T(8,128)(2,1)S(1)}, bf16[4,128,256]{2,1,0:T(8,128)(2,1)S(1)}, u32[]{:S(2)}, u32[]{:S(2)}) %collective-permute-start.19) | collective-permute-done | bytes 262176 | tf_op jit(solution)/shard_map/ppermute | solution.py:159
  110.5 5.5 %collective-permute-done.21 = bf16[4,128,256]{2,1,0:T(8,128)(2,1)S(1)} collective-permute-done((bf16[4,128,256]{2,1,0:T(8,128)(2,1)S(1)}, bf16[4,128,256]{2,1,0:T(8,128)(2,1)S(1)}, u32[]{:S(2)}, u32[]{:S(2)}) %collective-permute-start.21) | collective-permute-done | bytes 262176 | tf_op jit(solution)/shard_map/ppermute | solution.py:159
  116.1 0.7 collective-permute-start.23
  116.9 3.3 %collective-permute-start.24 = (bf16[2,128,256]{2,1,0:T(8,128)(2,1)S(1)}, bf16[2,128,256]{2,1,0:T(8,128)(2,1)S(1)}, u32[]{:S(2)}, u32[]{:S(2)}) collective-permute-start(bf16[2,128,256]{2,1,0:T(8,128)(2,1)S(1)} %get-tuple-element.63), channel_id=1, source_target_pairs={{1,2},{2,1},{3,4},{4,3},{5,6},{6,5},{9,10},{10,9},{11,12},{12,11},... | collective-permute-start | bytes 393224 | tf_op jit(solution)/shard_map/ppermute | solution.py:128
  120.2 1.9 %all_gather.22.p_inner = bf16[2,128,256]{2,1,0:T(8,128)(2,1)S(1)} all-gather(bf16[1,128,256]{2,1,0:T(8,128)(2,1)S(1)} %get-tuple-element.62), channel_id=1, replica_groups={{0,1},{2,3},{4,5},{6,7},{8,9},{10,11},{12,13},{14,15},{16,17},{18,19},{..., dimensions={0}, use_global_device_ids=true | all-gather | bytes 196608 | tf_op jit(solution)/shard_map/all_gather | solution.py:138
  122.1 5.3 %all_gather.23.p_outer = bf16[2,128,256]{2,1,0:T(8,128)(2,1)S(1)} all-gather(bf16[1,128,256]{2,1,0:T(8,128)(2,1)S(1)} %get-tuple-element.61), channel_id=1, replica_groups={{1,2},{3,4},{5,6},{7,0},{9,10},{11,12},{13,14},{15,8},{17,18},{19,20},{..., dimensions={0}, use_global_device_ids=true | all-gather | bytes 196608 | tf_op jit(solution)/shard_map/all_gather | solution.py:138
  127.4 3.6 %shard_map.63 = (bf16[1,128,256]{2,1,0:T(8,128)(2,1)S(1)}, bf16[4,128,256]{2,1,0:T(8,128)(2,1)S(1)}, bf16[1,128,256]{2,1,0:T(8,128)(2,1)S(1)}) custom-call(s32[3]{0:T(128)S(1)} %add_convert_fusion.6.flags, bf16[4,128,256]{2,1,0:T(8,128)(2,1)S(1)} %fusion.12.q_mid, bf16[2,128,256]{2,1,0:T(8,128)(2,1)S(1)} %collective-permute-done.23.q_inner, ...), custom_call_target="tpu_custom_call" | custom-call | flops 1 | bytes 1 | tf_op jit(solution)/shard_map/pallas_call | solution.py:90
  131.0 2.1 %shard_map.64 = bf16[4,128,256]{2,1,0:T(8,128)(2,1)S(1)} custom-call(bf16[1,128,256]{2,1,0:T(8,128)(2,1)S(1)} %get-tuple-element.55.first_low, bf16[4,128,256]{2,1,0:T(8,128)(2,1)S(1)} %get-tuple-element.54.first_mid, bf16[1,128,256]{2,1,0:T(8,128)(2,1)S(1)} %get-tuple-element.56.first_high, bf16[4,128,256]{2,1,0:T(8,128)(2,1)S(1)} %fusion.12.q_mid, ...), custom_call_target="tpu_custom_call" | custom-call | flops 1 | bytes 1 | tf_op jit(solution)/shard_map/pallas_call | solution.py:105
  133.1 0.9 maximum_select_fusion
  (58 shorter events, 4.7 us)
Async XLA Ops:
  0.0 17.5 %collective-permute-start.3 = (bf16[2,4,128,256]{3,2,1,0:T(8,128)(2,1)}, bf16[2,4,128,256]{3,2,1,0:T(8,128)(2,1)S(1)}, u32[]{:S(2)}, u32[]{:S(2)}) collective-permute-start(bf16[2,4,128,256]{3,2,1,0:T(8,128)(2,1)} %bitcast.74), channel_id=1, source_target_pairs={{0,24},{8,16},{1,25},{9,17},{2,26},{10,18},{3,27},{11,19},{4,28},{... | collective-permute-start | bytes 1572872 | tf_op jit(solution)/shard_map/ppermute | solution.py:159
  2.4 13.8 %copy-start.4 = (bf16[4,128,256]{2,1,0:T(8,128)(2,1)}, bf16[4,128,256]{2,1,0:T(8,128)(2,1)S(1)}, u32[]{:S(2)}) copy-start(bf16[4,128,256]{2,1,0:T(8,128)(2,1)S(1)} %get-tuple-element.60.q_mid) | copy-start | bytes 786436
  2.5 4.0 %collective-permute-start = (bf16[3,128,256]{2,1,0:T(8,128)(2,1)S(1)}, bf16[3,128,256]{2,1,0:T(8,128)(2,1)S(1)}, u32[]{:S(2)}, u32[]{:S(2)}) collective-permute-start(bf16[3,128,256]{2,1,0:T(8,128)(2,1)S(1)} %pad_maximum_fusion), channel_id=1, source_target_pairs={{0,1},{1,0},{2,3},{3,2},{4,5},{5,4},{6,7},{7,6},{8,9},{9,8},{10,11... | collective-permute-start | bytes 589832 | tf_op jit(solution)/shard_map/ppermute | solution.py:128
  3.2 7.3 %collective-permute-start.1 = (bf16[3,128,256]{2,1,0:T(8,128)(2,1)S(1)}, bf16[3,128,256]{2,1,0:T(8,128)(2,1)S(1)}, u32[]{:S(2)}, u32[]{:S(2)}) collective-permute-start(bf16[3,128,256]{2,1,0:T(8,128)(2,1)S(1)} %pad_maximum_fusion.1), channel_id=1, source_target_pairs={{1,2},{2,1},{3,4},{4,3},{5,6},{6,5},{9,10},{10,9},{11,12},{12,11},... | collective-permute-start | bytes 589832 | tf_op jit(solution)/shard_map/ppermute | solution.py:128
  10.5 2.0 %copy-start = (bf16[1,3,3,3,256,256]{5,4,3,2,1,0:T(8,128)(2,1)S(1)}, bf16[1,3,3,3,256,256]{5,4,3,2,1,0:T(8,128)(2,1)}, u32[]{:S(2)}) copy-start(bf16[1,3,3,3,256,256]{5,4,3,2,1,0:T(8,128)(2,1)} %param.8) | copy-start | bytes 10616836
  12.5 5.0 %copy-start.7 = (bf16[1,2,4,16,8,256]{5,4,3,2,1,0:T(8,128)(2,1)S(1)}, bf16[1,2,4,16,8,256]{5,4,3,2,1,0:T(8,128)(2,1)}, u32[]{:S(2)}) copy-start(bf16[1,2,4,16,8,256]{5,4,3,2,1,0:T(8,128)(2,1)} %param.5) | copy-start | bytes 1572868
  16.2 11.0 %collective-permute-start.2 = (bf16[4,128,256]{2,1,0:T(8,128)(2,1)S(1)}, bf16[4,128,256]{2,1,0:T(8,128)(2,1)}, u32[]{:S(2)}, u32[]{:S(2)}) collective-permute-start(bf16[4,128,256]{2,1,0:T(8,128)(2,1)S(1)} %get-tuple-element.31.first_mid), channel_id=1, source_target_pairs={{0,8},{1,9},{2,10},{3,11},{4,12},{5,13},{6,14},{7,15}} | collective-permute-start | bytes 786440 | tf_op jit(solution)/shard_map/ppermute | solution.py:159
  17.5 5.2 %copy-start.2 = (bf16[1,3,3,3,256,256]{5,4,3,2,1,0:T(8,128)(2,1)S(1)}, bf16[1,3,3,3,256,256]{5,4,3,2,1,0:T(8,128)(2,1)}, u32[]{:S(2)}) copy-start(bf16[1,3,3,3,256,256]{5,4,3,2,1,0:T(8,128)(2,1)} %param.9) | copy-start | bytes 10616836
  19.0 9.5 %collective-permute-start.4 = (bf16[3,128,256]{2,1,0:T(8,128)(2,1)S(1)}, bf16[3,128,256]{2,1,0:T(8,128)(2,1)S(1)}, u32[]{:S(2)}, u32[]{:S(2)}) collective-permute-start(bf16[3,128,256]{2,1,0:T(8,128)(2,1)S(1)} %pad_maximum_fusion.2), channel_id=1, source_target_pairs={{0,1},{1,0},{2,3},{3,2},{4,5},{5,4},{6,7},{7,6},{8,9},{9,8},{10,11... | collective-permute-start | bytes 589832 | tf_op jit(solution)/shard_map/ppermute | solution.py:128
  19.2 9.4 %collective-permute-start.5 = (bf16[3,128,256]{2,1,0:T(8,128)(2,1)S(1)}, bf16[3,128,256]{2,1,0:T(8,128)(2,1)S(1)}, u32[]{:S(2)}, u32[]{:S(2)}) collective-permute-start(bf16[3,128,256]{2,1,0:T(8,128)(2,1)S(1)} %pad_maximum_fusion.3), channel_id=1, source_target_pairs={{1,2},{2,1},{3,4},{4,3},{5,6},{6,5},{9,10},{10,9},{11,12},{12,11},... | collective-permute-start | bytes 589832 | tf_op jit(solution)/shard_map/ppermute | solution.py:128
  22.8 1.0 copy-start.5
  23.7 4.9 %copy-start.1 = (bf16[1,3,3,3,256,256]{5,4,3,2,1,0:T(8,128)(2,1)S(1)}, bf16[1,3,3,3,256,256]{5,4,3,2,1,0:T(8,128)(2,1)}, u32[]{:S(2)}) copy-start(bf16[1,3,3,3,256,256]{5,4,3,2,1,0:T(8,128)(2,1)} %param.8) | copy-start | bytes 10616836
  25.8 15.8 %collective-permute-start.9 = (bf16[4,128,256]{2,1,0:T(8,128)(2,1)S(1)}, bf16[4,128,256]{2,1,0:T(8,128)(2,1)}, u32[]{:S(2)}, u32[]{:S(2)}) collective-permute-start(bf16[4,128,256]{2,1,0:T(8,128)(2,1)S(1)} %shard_map.58), channel_id=1, source_target_pairs={{0,8},{1,9},{2,10},{3,11},{4,12},{5,13},{6,14},{7,15}} | collective-permute-start | bytes 786440 | tf_op jit(solution)/shard_map/ppermute | solution.py:159
  27.2 15.8 %collective-permute-start.7 = (bf16[4,128,256]{2,1,0:T(8,128)(2,1)}, bf16[4,128,256]{2,1,0:T(8,128)(2,1)}, u32[]{:S(2)}, u32[]{:S(2)}) collective-permute-start(bf16[4,128,256]{2,1,0:T(8,128)(2,1)} %collective-permute-done.2), channel_id=1, source_target_pairs={{8,24},{9,25},{10,26},{11,27},{12,28},{13,29},{14,30},{15,31}} | collective-permute-start | bytes 786440 | tf_op jit(solution)/shard_map/ppermute | solution.py:159
  32.9 12.4 %collective-permute-start.6 = (bf16[4,128,256]{2,1,0:T(8,128)(2,1)}, bf16[4,128,256]{2,1,0:T(8,128)(2,1)}, u32[]{:S(2)}, u32[]{:S(2)}) collective-permute-start(bf16[4,128,256]{2,1,0:T(8,128)(2,1)} %get-tuple-element.33.first_mid), channel_id=1, source_target_pairs={{0,8},{8,16},{16,24},{1,9},{9,17},{17,25},{2,10},{10,18},{18,26},{... | collective-permute-start | bytes 786440 | tf_op jit(solution)/shard_map/ppermute | solution.py:159
  39.7 11.3 %collective-permute-start.8 = (bf16[4,128,256]{2,1,0:T(8,128)(2,1)}, bf16[4,128,256]{2,1,0:T(8,128)(2,1)}, u32[]{:S(2)}, u32[]{:S(2)}) collective-permute-start(bf16[4,128,256]{2,1,0:T(8,128)(2,1)} %shard_map.57), channel_id=1, source_target_pairs={{0,8},{8,16},{16,24},{1,9},{9,17},{17,25},{2,10},{10,18},{18,26},{... | collective-permute-start | bytes 786440 | tf_op jit(solution)/shard_map/ppermute | solution.py:159
  41.6 9.3 %collective-permute-start.10 = (bf16[4,128,256]{2,1,0:T(8,128)(2,1)}, bf16[4,128,256]{2,1,0:T(8,128)(2,1)}, u32[]{:S(2)}, u32[]{:S(2)}) collective-permute-start(bf16[4,128,256]{2,1,0:T(8,128)(2,1)} %collective-permute-done.9), channel_id=1, source_target_pairs={{8,24},{9,25},{10,26},{11,27},{12,28},{13,29},{14,30},{15,31}} | collective-permute-start | bytes 786440 | tf_op jit(solution)/shard_map/ppermute | solution.py:159
  52.2 10.8 %collective-permute-start.11 = (bf16[2,128,256]{2,1,0:T(8,128)(2,1)S(1)}, bf16[2,128,256]{2,1,0:T(8,128)(2,1)S(1)}, u32[]{:S(2)}, u32[]{:S(2)}) collective-permute-start(bf16[2,128,256]{2,1,0:T(8,128)(2,1)S(1)} %get-tuple-element.72), channel_id=1, source_target_pairs={{0,1},{1,0},{2,3},{3,2},{4,5},{5,4},{6,7},{7,6},{8,9},{9,8},{10,11... | collective-permute-start | bytes 393224 | tf_op jit(solution)/shard_map/ppermute | solution.py:128
  52.6 10.3 %collective-permute-start.12 = (bf16[2,128,256]{2,1,0:T(8,128)(2,1)S(1)}, bf16[2,128,256]{2,1,0:T(8,128)(2,1)S(1)}, u32[]{:S(2)}, u32[]{:S(2)}) collective-permute-start(bf16[2,128,256]{2,1,0:T(8,128)(2,1)S(1)} %get-tuple-element.71), channel_id=1, source_target_pairs={{1,2},{2,1},{3,4},{4,3},{5,6},{6,5},{9,10},{10,9},{11,12},{12,11},... | collective-permute-start | bytes 393224 | tf_op jit(solution)/shard_map/ppermute | solution.py:128
  55.6 20.2 %collective-permute-start.14 = (bf16[4,128,256]{2,1,0:T(8,128)(2,1)}, bf16[4,128,256]{2,1,0:T(8,128)(2,1)S(1)}, u32[]{:S(2)}, u32[]{:S(2)}) collective-permute-start(bf16[4,128,256]{2,1,0:T(8,128)(2,1)} %collective-permute-done.6), channel_id=1, source_target_pairs={{8,24},{9,25},{10,26},{11,27},{12,28},{13,29},{14,30},{15,31}} | collective-permute-start | bytes 786440 | tf_op jit(solution)/shard_map/ppermute | solution.py:159
  62.9 8.2 %copy-start.3 = (bf16[1,3,3,3,256,256]{5,4,3,2,1,0:T(8,128)(2,1)S(1)}, bf16[1,3,3,3,256,256]{5,4,3,2,1,0:T(8,128)(2,1)}, u32[]{:S(2)}) copy-start(bf16[1,3,3,3,256,256]{5,4,3,2,1,0:T(8,128)(2,1)} %param.9) | copy-start | bytes 10616836
  66.6 12.7 %collective-permute-start.13 = (bf16[4,128,256]{2,1,0:T(8,128)(2,1)S(1)}, bf16[4,128,256]{2,1,0:T(8,128)(2,1)S(1)}, u32[]{:S(2)}, u32[]{:S(2)}) collective-permute-start(bf16[4,128,256]{2,1,0:T(8,128)(2,1)S(1)} %get-tuple-element.41.first_mid), channel_id=1, source_target_pairs={{0,8},{8,16},{16,24},{1,9},{9,17},{17,25},{2,10},{10,18},{18,26},{... | collective-permute-start | bytes 786440 | tf_op jit(solution)/shard_map/ppermute | solution.py:159
  71.1 8.2 %copy-start.6 = (bf16[3,2,4,16,8,256]{5,4,3,2,1,0:T(8,128)(2,1)S(1)}, bf16[3,2,4,16,8,256]{5,4,3,2,1,0:T(8,128)(2,1)}, u32[]{:S(2)}) copy-start(bf16[3,2,4,16,8,256]{5,4,3,2,1,0:T(8,128)(2,1)} %param.7) | copy-start | bytes 4718596
  73.2 11.7 %collective-permute-start.15 = (bf16[4,128,256]{2,1,0:T(8,128)(2,1)S(1)}, bf16[4,128,256]{2,1,0:T(8,128)(2,1)S(1)}, u32[]{:S(2)}, u32[]{:S(2)}) collective-permute-start(bf16[4,128,256]{2,1,0:T(8,128)(2,1)S(1)} %shard_map.60), channel_id=1, source_target_pairs={{0,8},{8,16},{16,24},{1,9},{9,17},{17,25},{2,10},{10,18},{18,26},{... | collective-permute-start | bytes 786440 | tf_op jit(solution)/shard_map/ppermute | solution.py:159
  75.1 9.8 %collective-permute-start.16 = (bf16[4,128,256]{2,1,0:T(8,128)(2,1)}, bf16[4,128,256]{2,1,0:T(8,128)(2,1)S(1)}, u32[]{:S(2)}, u32[]{:S(2)}) collective-permute-start(bf16[4,128,256]{2,1,0:T(8,128)(2,1)} %collective-permute-done.8), channel_id=1, source_target_pairs={{8,24},{9,25},{10,26},{11,27},{12,28},{13,29},{14,30},{15,31}} | collective-permute-start | bytes 786440 | tf_op jit(solution)/shard_map/ppermute | solution.py:159
  85.0 10.8 %collective-permute-start.17 = (bf16[2,128,256]{2,1,0:T(8,128)(2,1)S(1)}, bf16[2,128,256]{2,1,0:T(8,128)(2,1)S(1)}, u32[]{:S(2)}, u32[]{:S(2)}) collective-permute-start(bf16[2,128,256]{2,1,0:T(8,128)(2,1)S(1)} %get-tuple-element.68), channel_id=1, source_target_pairs={{0,1},{1,0},{2,3},{3,2},{4,5},{5,4},{6,7},{7,6},{8,9},{9,8},{10,11... | collective-permute-start | bytes 393224 | tf_op jit(solution)/shard_map/ppermute | solution.py:128
  85.7 10.2 %collective-permute-start.18 = (bf16[2,128,256]{2,1,0:T(8,128)(2,1)S(1)}, bf16[2,128,256]{2,1,0:T(8,128)(2,1)S(1)}, u32[]{:S(2)}, u32[]{:S(2)}) collective-permute-start(bf16[2,128,256]{2,1,0:T(8,128)(2,1)S(1)} %get-tuple-element.67), channel_id=1, source_target_pairs={{1,2},{2,1},{3,4},{4,3},{5,6},{6,5},{9,10},{10,9},{11,12},{12,11},... | collective-permute-start | bytes 393224 | tf_op jit(solution)/shard_map/ppermute | solution.py:128
  88.5 18.8 %collective-permute-start.20 = (bf16[4,128,256]{2,1,0:T(8,128)(2,1)S(1)}, bf16[4,128,256]{2,1,0:T(8,128)(2,1)S(1)}, u32[]{:S(2)}, u32[]{:S(2)}) collective-permute-start(bf16[4,128,256]{2,1,0:T(8,128)(2,1)S(1)} %collective-permute-done.13), channel_id=1, source_target_pairs={{8,24},{9,25},{10,26},{11,27},{12,28},{13,29},{14,30},{15,31}} | collective-permute-start | bytes 786440 | tf_op jit(solution)/shard_map/ppermute | solution.py:159
  99.5 10.9 %collective-permute-start.19 = (bf16[4,128,256]{2,1,0:T(8,128)(2,1)S(1)}, bf16[4,128,256]{2,1,0:T(8,128)(2,1)S(1)}, u32[]{:S(2)}, u32[]{:S(2)}) collective-permute-start(bf16[4,128,256]{2,1,0:T(8,128)(2,1)S(1)} %get-tuple-element.47.first_mid), channel_id=1, source_target_pairs={{8,16},{16,24},{9,17},{17,25},{10,18},{18,26},{11,19},{19,27},{12,... | collective-permute-start | bytes 786440 | tf_op jit(solution)/shard_map/ppermute | solution.py:159
  104.7 11.3 %collective-permute-start.21 = (bf16[4,128,256]{2,1,0:T(8,128)(2,1)S(1)}, bf16[4,128,256]{2,1,0:T(8,128)(2,1)S(1)}, u32[]{:S(2)}, u32[]{:S(2)}) collective-permute-start(bf16[4,128,256]{2,1,0:T(8,128)(2,1)S(1)} %shard_map.62), channel_id=1, source_target_pairs={{8,16},{16,24},{9,17},{17,25},{10,18},{18,26},{11,19},{19,27},{12,... | collective-permute-start | bytes 786440 | tf_op jit(solution)/shard_map/ppermute | solution.py:159
  106.6 9.4 %collective-permute-start.22 = (bf16[4,128,256]{2,1,0:T(8,128)(2,1)S(1)}, bf16[4,128,256]{2,1,0:T(8,128)(2,1)S(1)}, u32[]{:S(2)}, u32[]{:S(2)}) collective-permute-start(bf16[4,128,256]{2,1,0:T(8,128)(2,1)S(1)} %collective-permute-done.15), channel_id=1, source_target_pairs={{8,24},{9,25},{10,26},{11,27},{12,28},{13,29},{14,30},{15,31}} | collective-permute-start | bytes 786440 | tf_op jit(solution)/shard_map/ppermute | solution.py:159
  116.1 11.2 %collective-permute-start.23 = (bf16[2,128,256]{2,1,0:T(8,128)(2,1)S(1)}, bf16[2,128,256]{2,1,0:T(8,128)(2,1)S(1)}, u32[]{:S(2)}, u32[]{:S(2)}) collective-permute-start(bf16[2,128,256]{2,1,0:T(8,128)(2,1)S(1)} %get-tuple-element.64), channel_id=1, source_target_pairs={{0,1},{1,0},{2,3},{3,2},{4,5},{5,4},{6,7},{7,6},{8,9},{9,8},{10,11... | collective-permute-start | bytes 393224 | tf_op jit(solution)/shard_map/ppermute | solution.py:128
  116.9 10.5 %collective-permute-start.24 = (bf16[2,128,256]{2,1,0:T(8,128)(2,1)S(1)}, bf16[2,128,256]{2,1,0:T(8,128)(2,1)S(1)}, u32[]{:S(2)}, u32[]{:S(2)}) collective-permute-start(bf16[2,128,256]{2,1,0:T(8,128)(2,1)S(1)} %get-tuple-element.63), channel_id=1, source_target_pairs={{1,2},{2,1},{3,4},{4,3},{5,6},{6,5},{9,10},{10,9},{11,12},{12,11},... | collective-permute-start | bytes 393224 | tf_op jit(solution)/shard_map/ppermute | solution.py:128

commit v4 on v3

--- a/solution.py
+++ b/solution.py
@@ -8,7 +8,7 @@
 from jax.sharding import PartitionSpec as P
 
 EPS = 1e-05
-VMEM_LIMIT = 24 * 1024 * 1024
+VMEM_LIMIT = 12 * 1024 * 1024
 
 
 def act(values):
@@ -46,19 +46,15 @@
     return total.reshape(planes, voxels, chans)
 
 
-def first_kernel(width, flags, q_mid, q_inner, q_outer, p_mid, p_inner, p_outer, weights, low, mid, high, even, odd):
+def first_kernel(width, flags, p_mid, q_mid, inner_halo, outer_halo, weights, low, mid, high, even, odd):
     planes = q_mid.shape[0]
     above = flags[2] > 0
     fill(even, odd, 2, q_mid[...], width)
-    inner, outer = q_inner[:2].astype(jnp.float32), q_outer[:2].astype(jnp.float32)
+    inner, outer = inner_halo[:2].astype(jnp.float32), outer_halo[:2].astype(jnp.float32)
     fill(even, odd, 0, jnp.where(above, outer, inner), width)
     fill(even, odd, 2 + planes, jnp.where(above, inner, outer), width)
     total = convolve(even, odd, weights, planes + 2, width)
-    if p_inner.shape[0] == 2:
-        inner, outer = p_inner[pl.ds(flags[2], 1)], p_outer[pl.ds(1 - flags[2], 1)]
-    else:
-        inner, outer = p_inner[2:], p_outer[2:]
-    inner, outer = inner.astype(jnp.float32), outer.astype(jnp.float32)
+    inner, outer = inner_halo[2:].astype(jnp.float32), outer_halo[2:].astype(jnp.float32)
     low[...] = jnp.where(flags[0] > 0, jnp.where(above, outer, inner) + total[:1], 0.0).astype(low.dtype)
     mid[...] = (p_mid[...].astype(jnp.float32) + total[1:-1]).astype(mid.dtype)
     high[...] = jnp.where(flags[1] > 0, jnp.where(above, inner, outer) + total[-1:], 0.0).astype(high.dtype)
@@ -84,20 +80,20 @@
 SMEM = pl.BlockSpec(memory_space=pltpu.SMEM)
 
 
-def first_half(flags, q, q_halo, p, p_halo, weights, width):
+def first_half(flags, p, q, halos, weights, width):
     planes, voxels, chans = q.shape
     shape = lambda n: jax.ShapeDtypeStruct((n, voxels, chans), jnp.bfloat16)
     return pl.pallas_call(
         functools.partial(first_kernel, width),
         out_shape=(shape(1), shape(planes), shape(1)),
-        in_specs=[SMEM] + [VMEM] * 7,
+        in_specs=[SMEM] + [VMEM] * 5,
         out_specs=(VMEM, VMEM, VMEM),
         scratch_shapes=scratch(planes + 4, voxels, chans, width),
         compiler_params=pltpu.CompilerParams(vmem_limit_bytes=VMEM_LIMIT),
         cost_estimate=pl.CostEstimate(
             flops=1, bytes_accessed=1, transcendentals=0
         ),
-    )(flags, q, *q_halo, p, *p_halo, weights)
+    )(flags, p, q, *halos, weights)
 
 
 def second_half(first, q, weights, width):
@@ -119,25 +115,15 @@
     return lax.dynamic_slice_in_dim(block, jnp.where(upward, block.shape[0] - width, 0), width, axis=0)
 
 
-def swapped(blocks, widths, above):
+def swapped(p, q, above):
     count = lax.axis_size("depth")
 
     def swap(upward, base):
-        parts = [boundary(block, upward, width) for block, width in zip(blocks, widths)]
+        part = jnp.concatenate([boundary(q, upward, 2), boundary(p, upward, 1)], axis=0)
         pairs = [pair for i in range(base, count - 1, 2) for pair in ((i, i + 1), (i + 1, i))]
-        return lax.ppermute(jnp.concatenate(parts, axis=0), "depth", pairs)
+        return lax.ppermute(part, "depth", pairs)
 
     return swap(above, 0), swap(jnp.logical_not(above), 1)
-
-
-def gathered(block, above):
-    count = lax.axis_size("depth")
-
-    def gather(upward, base):
-        groups = [[i, (i + 1) % count] for i in range(base, count, 2)]
-        return lax.all_gather(boundary(block, upward, 1), "depth", axis_index_groups=groups, tiled=True)
-
-    return gather(above, 0), gather(jnp.logical_not(above), 1)
 
 
 def local(resident, previous, incoming, first_weights, second_weights):
@@ -158,7 +144,6 @@
     def send(block, pairs):
         return lax.ppermute(block, "section", pairs) if pairs else block
 
-    mirrored = send(previous, [(j, sections - 1 - j) for j in range(half)])
     across = [(j, sections - 1 - j) for j in range(1, half - 1)]
     decoder = section >= half
 
@@ -166,10 +151,9 @@
         total = (held.astype(jnp.float32) + skip.astype(jnp.float32)).astype(jnp.bfloat16)
         return jnp.where(decoder, total, held)
 
-    out = emitted = None
     newer, older, relayed, direct = {}, {}, {}, {}
 
-    def arrived(slot, stream, mirrored=None):
+    def arrived(slot, stream):
         fresh = incoming[min(slot, ticks - 1) - 1, stream]
         if slot == 1:
             return jnp.where(section == 0, fresh, join(resident[stream], mirrored[stream]))
@@ -180,39 +164,40 @@
         return jnp.where(section == 0, fresh, join(held, skip))
 
     for slot in range(ticks + 1):
-        if slot < 2:
+        if slot == 0:
+            p, q = resident
+            halos = swapped(p, q, above)
+            inner, previous = lax.optimization_barrier((halos[0], previous))
+            halos = (inner, halos[1])
+            mirrored = send(previous, [(j, sections - 1 - j) for j in range(half)])
+        else:
             if slot == 1:
                 mirrored, _ = lax.optimization_barrier((mirrored, first[1]))
-            p, q = resident if slot == 0 else (arrived(slot, 0, mirrored), arrived(slot, 1, mirrored))
-            p_halo = q_halo = swapped((q, p), (2, 1), above)
-        else:
             p = arrived(slot, 0)
-            p_halo = gathered(p, above)
-            p, newer[1] = lax.optimization_barrier((p, newer[1]))
+            if slot > 1:
+                p, newer[1] = lax.optimization_barrier((p, newer[1]))
             q = arrived(slot, 1)
-            q_halo = swapped((q,), (2,), above)
-        onward = []
-        if slot < ticks:
-            onward = [(0, 1)] if slot < ticks - 1 else []
-            if slot > 0:
-                onward += [(j, j + 1) for j in range(1, sections - 1)]
-        received, relays = {}, {}
-        first = first_half(flags, q, q_halo, p, p_halo, w_one, width)
-        if onward:
-            received[0] = send(first[1], onward)
+            halos = swapped(p, q, above)
+        first = first_half(flags, p, q, halos, w_one, width)
+        onward = [(j, j + 1) for j in range(1, sections - 1)]
+        if slot < ticks - 1:
+            onward = [(0, 1)] + onward
+        received = relays = {}
+        if 0 < slot < ticks:
+            received = {0: send(first[1], onward)}
         second = second_half(first, q, w_two, width)
-        if onward:
+        if slot == 0:
+            received = send(jnp.stack([first[1], second]), [(0, 1)])
+        elif slot < ticks:
             received[1] = send(second, onward)
-        if 0 < slot < ticks:
-            held_q, second = lax.optimization_barrier((newer[1], second))
-            relays = {k: send(held, [(1, sections - 1)]) for k, held in enumerate((newer[0], held_q))}
-        if across and 0 < slot < ticks:
-            direct = {0: send(first[1], across), 1: send(second, across)}
+            held = jnp.stack([newer[0], newer[1]])
+            if slot == 1:
+                held, _ = lax.optimization_barrier((held, first[1]))
+            relays = send(held, [(1, sections - 1)])
+            if across:
+                direct = {0: send(first[1], across), 1: send(second, across)}
         older, newer, relayed = newer, received, relays
-        out = jnp.stack([first[1], second])
-        if slot == ticks - 1:
-            emitted = out
-    result = jnp.where(section == 0, emitted, out)
+    result = jnp.stack([first[1], second])
     return result.reshape(1, 2, planes, rows, width, chans)
 
 

time: 136 us -> 130 us (0.956); the launches traced: 134 us -> 130 us
  blocking collectives: 20.4 us -> 0 us
  waiting for transfers between devices: 28.5 us -> 48.4 us
  starting transfers between devices: 44.2 us -> 38.7 us
  other arithmetic: 5.14 us -> 6.82 us
    all_gather x6 -> x0, blocking collectives: 20.4 us -> none  [gather(): lax.all_gather(boundary(block, upward, 1), 'depth', axis_index_groups=gro...]
    ppermute x10, waiting for transfers between devices: 4.09 us -> 19.5 us  [swap(): return lax.ppermute(part, 'depth', pairs)]
    ppermute x15 -> x11, starting transfers between devices: 25.9 us -> 18.1 us  [send(): return lax.ppermute(block, 'section', pairs) if pairs else block]
    ppermute x15 -> x11, waiting for transfers between devices: 24.4 us -> 28.9 us  [send(): return lax.ppermute(block, 'section', pairs) if pairs else block]
    ppermute x10, starting transfers between devices: 18.4 us -> 20.6 us  [swap(): return lax.ppermute(part, 'depth', pairs)]
    another operation x0 -> x4, other arithmetic: none -> 2.02 us  [the longest x2 1.13 us: local(): held = jnp.stack([newer[0], newer[1]])]
  transfers between devices with their start and end apart: 25 -> 21, of which waited for: 7 -> 12; matrix products, arithmetic and copies ran while one was open for 3% -> 3% of each run, Pallas kernels for 19% -> 20%
where the time goes in v4:
time: 130 us
  waiting for transfers between devices  48.4 us (37%)
  starting transfers between devices  38.7 us (30%)
  Pallas kernels  31 us (24%)
  other arithmetic  6.82 us (5%)
  local copies, waits for them, and re-layouts  4.15 us (3%)
    ppermute x11, waiting for transfers between devices, send(): return lax.ppermute(block, 'section', pairs) if pairs else block  28.9 us
    ppermute x10, starting transfers between devices, swap(): return lax.ppermute(part, 'depth', pairs)  20.6 us
    ppermute x10, waiting for transfers between devices, swap(): return lax.ppermute(part, 'depth', pairs)  19.5 us
    pallas_call x5, Pallas kernels, first_half(): pl.pallas_call(functools.partial(first_kernel, width), out_shape=(shape(1...  18.8 us
    ppermute x11, starting transfers between devices, send(): return lax.ppermute(block, 'section', pairs) if pairs else block  18.1 us
    pallas_call x5, Pallas kernels, second_half(): pl.pallas_call(functools.partial(second_kernel, width), out_shape=jax.Sha...  12.2 us
    select_n x6, other arithmetic, arrived(): return jnp.where(section == 0, fresh, join(held, skip))  2.95 us
    unnamed x16, local copies, waits for them, and re-layouts  2.82 us
  transfers between devices with their start and end apart: 21, of which 12 were waited for; matrix products, arithmetic and copies ran while one was open for 3% of the time, Pallas kernels for 20%

profile of v4, /device:TPU:13, one launch (start us, length us, event | category | flops | bytes accessed | tf_op | source)
XLA Modules:
  0.0 129.5 jit_solution(17560806080448338724)
XLA Ops:
  0.0 1.1 slice_bitcast_fusion.14
  1.2 0.7 collective-permute-start
  2.0 1.1 collective-permute-done.inner_halo
  3.0 1.3 collective-permute-start.3
  4.3 3.5 %collective-permute-start.1 = (bf16[3,128,256]{2,1,0:T(8,128)(2,1)S(1)}, bf16[3,128,256]{2,1,0:T(8,128)(2,1)S(1)}, u32[]{:S(2)}, u32[]{:S(2)}) collective-permute-start(bf16[3,128,256]{2,1,0:T(8,128)(2,1)S(1)} %pad_maximum_fusion.5), channel_id=1, source_target_pairs={{1,2},{2,1},{3,4},{4,3},{5,6},{6,5},{9,10},{10,9},{11,12},{12,11},... | collective-permute-start | bytes 589832 | tf_op jit(solution)/shard_map/ppermute | solution.py:124
  7.9 3.7 %collective-permute-done.1.outer_halo = bf16[3,128,256]{2,1,0:T(8,128)(2,1)S(1)} collective-permute-done((bf16[3,128,256]{2,1,0:T(8,128)(2,1)S(1)}, bf16[3,128,256]{2,1,0:T(8,128)(2,1)S(1)}, u32[]{:S(2)}, u32[]{:S(2)}) %collective-permute-start.1) | collective-permute-done | bytes 196640 | tf_op jit(solution)/shard_map/ppermute | solution.py:124
  11.6 2.0 %copy-done = bf16[1,3,3,3,256,256]{5,4,3,2,1,0:T(8,128)(2,1)S(1)} copy-done((bf16[1,3,3,3,256,256]{5,4,3,2,1,0:T(8,128)(2,1)S(1)}, bf16[1,3,3,3,256,256]{5,4,3,2,1,0:T(8,128)(2,1)}, u32[]{:S(2)}) %copy-start) | copy-done | bytes 3538968
  13.6 3.6 %shard_map.55 = (bf16[1,128,256]{2,1,0:T(8,128)(2,1)S(1)}, bf16[4,128,256]{2,1,0:T(8,128)(2,1)S(1)}, bf16[1,128,256]{2,1,0:T(8,128)(2,1)S(1)}) custom-call(s32[3]{0:T(128)S(1)} %add_convert_fusion.6.flags, bf16[4,128,256]{2,1,0:T(8,128)(2,1)S(1)} %get-tuple-element.58.p_mid, bf16[4,128,256]{2,1,0:T(8,128)(2,1)S(1)} %get-tuple-element.57.q_mid, ...), custom_call_target="tpu_custom_call" | custom-call | flops 1 | bytes 1 | tf_op jit(solution)/shard_map/pallas_call | solution.py:86
  17.3 2.1 %shard_map.56 = bf16[4,128,256]{2,1,0:T(8,128)(2,1)S(1)} custom-call(bf16[1,128,256]{2,1,0:T(8,128)(2,1)S(1)} %get-tuple-element.32.first_low, bf16[4,128,256]{2,1,0:T(8,128)(2,1)S(1)} %get-tuple-element.31.first_mid, bf16[1,128,256]{2,1,0:T(8,128)(2,1)S(1)} %get-tuple-element.33.first_high, bf16[4,128,256]{2,1,0:T(8,128)(2,1)S(1)} %get-tuple-element.57.q_mid, ...), custom_call_target="tpu_custom_call" | custom-call | flops 1 | bytes 1 | tf_op jit(solution)/shard_map/pallas_call | solution.py:101
  19.4 1.5 %collective-permute-start.2 = (bf16[2,4,128,256]{3,2,1,0:T(8,128)(2,1)S(1)}, bf16[2,4,128,256]{3,2,1,0:T(8,128)(2,1)}, u32[]{:S(2)}, u32[]{:S(2)}) collective-permute-start(bf16[2,4,128,256]{3,2,1,0:T(8,128)(2,1)S(1)} %pad_maximum_fusion), channel_id=1, source_target_pairs={{0,8},{1,9},{2,10},{3,11},{4,12},{5,13},{6,14},{7,15}} | collective-permute-start | bytes 1572872 | tf_op jit(solution)/shard_map/ppermute | solution.py:145
  20.9 0.8 copy-done.6
  21.7 1.6 %fusion.10 = (bf16[4,128,256]{2,1,0:T(8,128)(2,1)S(1)}, bf16[4,128,256]{2,1,0:T(8,128)(2,1)S(1)}) fusion(bf16[3,2,4,128,256]{4,3,2,1,0:T(8,128)(2,1)} %bitcast.119, bf16[2,4,128,256]{3,2,1,0:T(8,128)(2,1)} %copy-done.6, pred[]{:T(512)S(6)} %ge.3, pred[]{:T(512)S(6)} %eq.11, bf16[1,2,4,16,8,256]{5,4,3,2,1,0:T(8,128)(2,1)S(1)} %copy-done.5), kind=kLoop, calls=%fused_computation.22 | loop fusion | flops 1572864 | bytes 2097154 | tf_op jit(solution)/shard_map/jit(_where)/select_n | solution.py:159
  23.5 3.5 %collective-permute-start.5 = (bf16[3,128,256]{2,1,0:T(8,128)(2,1)S(1)}, bf16[3,128,256]{2,1,0:T(8,128)(2,1)S(1)}, u32[]{:S(2)}, u32[]{:S(2)}) collective-permute-start(bf16[3,128,256]{2,1,0:T(8,128)(2,1)S(1)} %pad_maximum_fusion.7), channel_id=1, source_target_pairs={{1,2},{2,1},{3,4},{4,3},{5,6},{6,5},{9,10},{10,9},{11,12},{12,11},... | collective-permute-start | bytes 589832 | tf_op jit(solution)/shard_map/ppermute | solution.py:124
  27.1 3.5 %collective-permute-done.5.outer_halo = bf16[3,128,256]{2,1,0:T(8,128)(2,1)S(1)} collective-permute-done((bf16[3,128,256]{2,1,0:T(8,128)(2,1)S(1)}, bf16[3,128,256]{2,1,0:T(8,128)(2,1)S(1)}, u32[]{:S(2)}, u32[]{:S(2)}) %collective-permute-start.5) | collective-permute-done | bytes 196640 | tf_op jit(solution)/shard_map/ppermute | solution.py:124
  30.6 4.3 %shard_map.57 = (bf16[1,128,256]{2,1,0:T(8,128)(2,1)S(1)}, bf16[4,128,256]{2,1,0:T(8,128)(2,1)}, bf16[1,128,256]{2,1,0:T(8,128)(2,1)S(1)}) custom-call(s32[3]{0:T(128)S(1)} %add_convert_fusion.6.flags, bf16[4,128,256]{2,1,0:T(8,128)(2,1)S(1)} %get-tuple-element.56.p_mid, bf16[4,128,256]{2,1,0:T(8,128)(2,1)S(1)} %get-tuple-element.55.q_mid, ...), custom_call_target="tpu_custom_call" | custom-call | flops 1 | bytes 1 | tf_op jit(solution)/shard_map/pallas_call | solution.py:86
  34.9 1.5 %collective-permute-start.7 = (bf16[2,4,128,256]{3,2,1,0:T(8,128)(2,1)}, bf16[2,4,128,256]{3,2,1,0:T(8,128)(2,1)}, u32[]{:S(2)}, u32[]{:S(2)}) collective-permute-start(bf16[2,4,128,256]{3,2,1,0:T(8,128)(2,1)} %collective-permute-done.2), channel_id=1, source_target_pairs={{8,24},{9,25},{10,26},{11,27},{12,28},{13,29},{14,30},{15,31}} | collective-permute-start | bytes 1572872 | tf_op jit(solution)/shard_map/ppermute | solution.py:145
  36.3 2.9 %collective-permute-start.6 = (bf16[4,128,256]{2,1,0:T(8,128)(2,1)}, bf16[4,128,256]{2,1,0:T(8,128)(2,1)}, u32[]{:S(2)}, u32[]{:S(2)}) collective-permute-start(bf16[4,128,256]{2,1,0:T(8,128)(2,1)} %get-tuple-element.36.first_mid), channel_id=1, source_target_pairs={{0,8},{8,16},{16,24},{1,9},{9,17},{17,25},{2,10},{10,18},{18,26},{... | collective-permute-start | bytes 786440 | tf_op jit(solution)/shard_map/ppermute | solution.py:145
  39.3 3.8 %shard_map.58 = bf16[4,128,256]{2,1,0:T(8,128)(2,1)} custom-call(bf16[1,128,256]{2,1,0:T(8,128)(2,1)S(1)} %get-tuple-element.38.first_low, bf16[4,128,256]{2,1,0:T(8,128)(2,1)} %get-tuple-element.36.first_mid, bf16[1,128,256]{2,1,0:T(8,128)(2,1)S(1)} %get-tuple-element.39.first_high, bf16[4,128,256]{2,1,0:T(8,128)(2,1)S(1)} %get-tuple-element.55.q_mid, ...), custom_call_target="tpu_custom_call" | custom-call | flops 1 | bytes 1 | tf_op jit(solution)/shard_map/pallas_call | solution.py:101
  43.0 1.9 %collective-permute-start.8 = (bf16[4,128,256]{2,1,0:T(8,128)(2,1)}, bf16[4,128,256]{2,1,0:T(8,128)(2,1)}, u32[]{:S(2)}, u32[]{:S(2)}) collective-permute-start(bf16[4,128,256]{2,1,0:T(8,128)(2,1)} %shard_map.58), channel_id=1, source_target_pairs={{0,8},{8,16},{16,24},{1,9},{9,17},{17,25},{2,10},{10,18},{18,26},{... | collective-permute-start | bytes 786440 | tf_op jit(solution)/shard_map/ppermute | solution.py:145
  45.0 4.0 %collective-permute-done.6 = bf16[4,128,256]{2,1,0:T(8,128)(2,1)} collective-permute-done((bf16[4,128,256]{2,1,0:T(8,128)(2,1)}, bf16[4,128,256]{2,1,0:T(8,128)(2,1)}, u32[]{:S(2)}, u32[]{:S(2)}) %collective-permute-start.6) | collective-permute-done | bytes 262176 | tf_op jit(solution)/shard_map/ppermute | solution.py:145
  49.0 1.3 fusion.17.p_mid
  50.3 4.4 %collective-permute-done.8 = bf16[4,128,256]{2,1,0:T(8,128)(2,1)} collective-permute-done((bf16[4,128,256]{2,1,0:T(8,128)(2,1)}, bf16[4,128,256]{2,1,0:T(8,128)(2,1)}, u32[]{:S(2)}, u32[]{:S(2)}) %collective-permute-start.8) | collective-permute-done | bytes 262176 | tf_op jit(solution)/shard_map/ppermute | solution.py:145
  54.7 1.2 fusion.16.q_mid
  56.0 1.0 collective-permute-start.9
  57.0 1.1 pad_maximum_fusion.1
  58.8 3.5 %collective-permute-start.10 = (bf16[3,128,256]{2,1,0:T(8,128)(2,1)S(1)}, bf16[3,128,256]{2,1,0:T(8,128)(2,1)S(1)}, u32[]{:S(2)}, u32[]{:S(2)}) collective-permute-start(bf16[3,128,256]{2,1,0:T(8,128)(2,1)S(1)} %pad_maximum_fusion.9), channel_id=1, source_target_pairs={{1,2},{2,1},{3,4},{4,3},{5,6},{6,5},{9,10},{10,9},{11,12},{12,11},... | collective-permute-start | bytes 589832 | tf_op jit(solution)/shard_map/ppermute | solution.py:124
  62.4 3.7 %collective-permute-done.10.outer_halo = bf16[3,128,256]{2,1,0:T(8,128)(2,1)S(1)} collective-permute-done((bf16[3,128,256]{2,1,0:T(8,128)(2,1)S(1)}, bf16[3,128,256]{2,1,0:T(8,128)(2,1)S(1)}, u32[]{:S(2)}, u32[]{:S(2)}) %collective-permute-start.10) | collective-permute-done | bytes 196640 | tf_op jit(solution)/shard_map/ppermute | solution.py:124
  66.1 3.6 %shard_map.59 = (bf16[1,128,256]{2,1,0:T(8,128)(2,1)S(1)}, bf16[4,128,256]{2,1,0:T(8,128)(2,1)S(1)}, bf16[1,128,256]{2,1,0:T(8,128)(2,1)S(1)}) custom-call(s32[3]{0:T(128)S(1)} %add_convert_fusion.6.flags, bf16[4,128,256]{2,1,0:T(8,128)(2,1)S(1)} %fusion.17.p_mid, bf16[4,128,256]{2,1,0:T(8,128)(2,1)S(1)} %fusion.16.q_mid, ...), custom_call_target="tpu_custom_call" | custom-call | flops 1 | bytes 1 | tf_op jit(solution)/shard_map/pallas_call | solution.py:86
  69.7 1.9 %collective-permute-start.11 = (bf16[4,128,256]{2,1,0:T(8,128)(2,1)S(1)}, bf16[4,128,256]{2,1,0:T(8,128)(2,1)S(1)}, u32[]{:S(2)}, u32[]{:S(2)}) collective-permute-start(bf16[4,128,256]{2,1,0:T(8,128)(2,1)S(1)} %get-tuple-element.42.first_mid), channel_id=1, source_target_pairs={{0,8},{8,16},{16,24},{1,9},{9,17},{17,25},{2,10},{10,18},{18,26},{... | collective-permute-start | bytes 786440 | tf_op jit(solution)/shard_map/ppermute | solution.py:145
  71.6 2.1 %shard_map.60 = bf16[4,128,256]{2,1,0:T(8,128)(2,1)S(1)} custom-call(bf16[1,128,256]{2,1,0:T(8,128)(2,1)S(1)} %get-tuple-element.43.first_low, bf16[4,128,256]{2,1,0:T(8,128)(2,1)S(1)} %get-tuple-element.42.first_mid, bf16[1,128,256]{2,1,0:T(8,128)(2,1)S(1)} %get-tuple-element.44.first_high, bf16[4,128,256]{2,1,0:T(8,128)(2,1)S(1)} %fusion.16.q_mid, ...), custom_call_target="tpu_custom_call" | custom-call | flops 1 | bytes 1 | tf_op jit(solution)/shard_map/pallas_call | solution.py:101
  73.8 1.9 %collective-permute-start.13 = (bf16[4,128,256]{2,1,0:T(8,128)(2,1)S(1)}, bf16[4,128,256]{2,1,0:T(8,128)(2,1)S(1)}, u32[]{:S(2)}, u32[]{:S(2)}) collective-permute-start(bf16[4,128,256]{2,1,0:T(8,128)(2,1)S(1)} %shard_map.60), channel_id=1, source_target_pairs={{0,8},{8,16},{16,24},{1,9},{9,17},{17,25},{2,10},{10,18},{18,26},{... | collective-permute-start | bytes 786440 | tf_op jit(solution)/shard_map/ppermute | solution.py:145
  75.7 4.7 %collective-permute-done.11 = bf16[4,128,256]{2,1,0:T(8,128)(2,1)S(1)} collective-permute-done((bf16[4,128,256]{2,1,0:T(8,128)(2,1)S(1)}, bf16[4,128,256]{2,1,0:T(8,128)(2,1)S(1)}, u32[]{:S(2)}, u32[]{:S(2)}) %collective-permute-start.11) | collective-permute-done | bytes 262176 | tf_op jit(solution)/shard_map/ppermute | solution.py:145
  80.5 5.5 %collective-permute-done.13 = bf16[4,128,256]{2,1,0:T(8,128)(2,1)S(1)} collective-permute-done((bf16[4,128,256]{2,1,0:T(8,128)(2,1)S(1)}, bf16[4,128,256]{2,1,0:T(8,128)(2,1)S(1)}, u32[]{:S(2)}, u32[]{:S(2)}) %collective-permute-start.13) | collective-permute-done | bytes 262176 | tf_op jit(solution)/shard_map/ppermute | solution.py:145
  86.2 0.9 collective-permute-start.14
  87.9 3.1 %collective-permute-start.15 = (bf16[3,128,256]{2,1,0:T(8,128)(2,1)S(1)}, bf16[3,128,256]{2,1,0:T(8,128)(2,1)S(1)}, u32[]{:S(2)}, u32[]{:S(2)}) collective-permute-start(bf16[3,128,256]{2,1,0:T(8,128)(2,1)S(1)} %pad_maximum_fusion.11), channel_id=1, source_target_pairs={{1,2},{2,1},{3,4},{4,3},{5,6},{6,5},{9,10},{10,9},{11,12},{12,11},... | collective-permute-start | bytes 589832 | tf_op jit(solution)/shard_map/ppermute | solution.py:124
  91.0 3.9 %collective-permute-done.15.outer_halo = bf16[3,128,256]{2,1,0:T(8,128)(2,1)S(1)} collective-permute-done((bf16[3,128,256]{2,1,0:T(8,128)(2,1)S(1)}, bf16[3,128,256]{2,1,0:T(8,128)(2,1)S(1)}, u32[]{:S(2)}, u32[]{:S(2)}) %collective-permute-start.15) | collective-permute-done | bytes 196640 | tf_op jit(solution)/shard_map/ppermute | solution.py:124
  94.9 3.6 %shard_map.61 = (bf16[1,128,256]{2,1,0:T(8,128)(2,1)S(1)}, bf16[4,128,256]{2,1,0:T(8,128)(2,1)S(1)}, bf16[1,128,256]{2,1,0:T(8,128)(2,1)S(1)}) custom-call(s32[3]{0:T(128)S(1)} %add_convert_fusion.6.flags, bf16[4,128,256]{2,1,0:T(8,128)(2,1)S(1)} %fusion.15.p_mid, bf16[4,128,256]{2,1,0:T(8,128)(2,1)S(1)} %fusion.14.q_mid, ...), custom_call_target="tpu_custom_call" | custom-call | flops 1 | bytes 1 | tf_op jit(solution)/shard_map/pallas_call | solution.py:86
  98.5 1.9 %collective-permute-start.16 = (bf16[4,128,256]{2,1,0:T(8,128)(2,1)S(1)}, bf16[4,128,256]{2,1,0:T(8,128)(2,1)S(1)}, u32[]{:S(2)}, u32[]{:S(2)}) collective-permute-start(bf16[4,128,256]{2,1,0:T(8,128)(2,1)S(1)} %get-tuple-element.47.first_mid), channel_id=1, source_target_pairs={{8,16},{16,24},{9,17},{17,25},{10,18},{18,26},{11,19},{19,27},{12,... | collective-permute-start | bytes 786440 | tf_op jit(solution)/shard_map/ppermute | solution.py:145
  100.4 2.1 %shard_map.62 = bf16[4,128,256]{2,1,0:T(8,128)(2,1)S(1)} custom-call(bf16[1,128,256]{2,1,0:T(8,128)(2,1)S(1)} %get-tuple-element.48.first_low, bf16[4,128,256]{2,1,0:T(8,128)(2,1)S(1)} %get-tuple-element.47.first_mid, bf16[1,128,256]{2,1,0:T(8,128)(2,1)S(1)} %get-tuple-element.49.first_high, bf16[4,128,256]{2,1,0:T(8,128)(2,1)S(1)} %fusion.14.q_mid, ...), custom_call_target="tpu_custom_call" | custom-call | flops 1 | bytes 1 | tf_op jit(solution)/shard_map/pallas_call | solution.py:101
  102.6 1.9 %collective-permute-start.18 = (bf16[4,128,256]{2,1,0:T(8,128)(2,1)S(1)}, bf16[4,128,256]{2,1,0:T(8,128)(2,1)S(1)}, u32[]{:S(2)}, u32[]{:S(2)}) collective-permute-start(bf16[4,128,256]{2,1,0:T(8,128)(2,1)S(1)} %shard_map.62), channel_id=1, source_target_pairs={{8,16},{16,24},{9,17},{17,25},{10,18},{18,26},{11,19},{19,27},{12,... | collective-permute-start | bytes 786440 | tf_op jit(solution)/shard_map/ppermute | solution.py:145
  104.5 4.7 %collective-permute-done.16 = bf16[4,128,256]{2,1,0:T(8,128)(2,1)S(1)} collective-permute-done((bf16[4,128,256]{2,1,0:T(8,128)(2,1)S(1)}, bf16[4,128,256]{2,1,0:T(8,128)(2,1)S(1)}, u32[]{:S(2)}, u32[]{:S(2)}) %collective-permute-start.16) | collective-permute-done | bytes 262176 | tf_op jit(solution)/shard_map/ppermute | solution.py:145
  109.3 5.5 %collective-permute-done.18 = bf16[4,128,256]{2,1,0:T(8,128)(2,1)S(1)} collective-permute-done((bf16[4,128,256]{2,1,0:T(8,128)(2,1)S(1)}, bf16[4,128,256]{2,1,0:T(8,128)(2,1)S(1)}, u32[]{:S(2)}, u32[]{:S(2)}) %collective-permute-start.18) | collective-permute-done | bytes 262176 | tf_op jit(solution)/shard_map/ppermute | solution.py:145
  115.0 0.9 collective-permute-start.19
  115.9 3.3 %collective-permute-start.20 = (bf16[3,128,256]{2,1,0:T(8,128)(2,1)S(1)}, bf16[3,128,256]{2,1,0:T(8,128)(2,1)S(1)}, u32[]{:S(2)}, u32[]{:S(2)}) collective-permute-start(bf16[3,128,256]{2,1,0:T(8,128)(2,1)S(1)} %pad_maximum_fusion.13), channel_id=1, source_target_pairs={{1,2},{2,1},{3,4},{4,3},{5,6},{6,5},{9,10},{10,9},{11,12},{12,11},... | collective-permute-start | bytes 589832 | tf_op jit(solution)/shard_map/ppermute | solution.py:124
  119.3 3.6 %collective-permute-done.20.outer_halo = bf16[3,128,256]{2,1,0:T(8,128)(2,1)S(1)} collective-permute-done((bf16[3,128,256]{2,1,0:T(8,128)(2,1)S(1)}, bf16[3,128,256]{2,1,0:T(8,128)(2,1)S(1)}, u32[]{:S(2)}, u32[]{:S(2)}) %collective-permute-start.20) | collective-permute-done | bytes 196640 | tf_op jit(solution)/shard_map/ppermute | solution.py:124
  122.9 3.6 %shard_map.63 = (bf16[1,128,256]{2,1,0:T(8,128)(2,1)S(1)}, bf16[4,128,256]{2,1,0:T(8,128)(2,1)S(1)}, bf16[1,128,256]{2,1,0:T(8,128)(2,1)S(1)}) custom-call(s32[3]{0:T(128)S(1)} %add_convert_fusion.6.flags, bf16[4,128,256]{2,1,0:T(8,128)(2,1)S(1)} %fusion.13.p_mid, bf16[4,128,256]{2,1,0:T(8,128)(2,1)S(1)} %fusion.12.q_mid, ...), custom_call_target="tpu_custom_call" | custom-call | flops 1 | bytes 1 | tf_op jit(solution)/shard_map/pallas_call | solution.py:86
  126.5 2.1 %shard_map.64 = bf16[4,128,256]{2,1,0:T(8,128)(2,1)S(1)} custom-call(bf16[1,128,256]{2,1,0:T(8,128)(2,1)S(1)} %get-tuple-element.53.first_low, bf16[4,128,256]{2,1,0:T(8,128)(2,1)S(1)} %get-tuple-element.52.first_mid, bf16[1,128,256]{2,1,0:T(8,128)(2,1)S(1)} %get-tuple-element.54.first_high, bf16[4,128,256]{2,1,0:T(8,128)(2,1)S(1)} %fusion.12.q_mid, ...), custom_call_target="tpu_custom_call" | custom-call | flops 1 | bytes 1 | tf_op jit(solution)/shard_map/pallas_call | solution.py:101
  128.7 0.8 pad_maximum_fusion.3
  (53 shorter events, 2.6 us)
Async XLA Ops:
  0.0 3.0 %copy-start.7 = (bf16[1,2,4,16,8,256]{5,4,3,2,1,0:T(8,128)(2,1)S(1)}, bf16[1,2,4,16,8,256]{5,4,3,2,1,0:T(8,128)(2,1)}, u32[]{:S(2)}) copy-start(bf16[1,2,4,16,8,256]{5,4,3,2,1,0:T(8,128)(2,1)} %param.6) | copy-start | bytes 1572868
  1.2 1.8 %collective-permute-start = (bf16[3,128,256]{2,1,0:T(8,128)(2,1)S(1)}, bf16[3,128,256]{2,1,0:T(8,128)(2,1)S(1)}, u32[]{:S(2)}, u32[]{:S(2)}) collective-permute-start(bf16[3,128,256]{2,1,0:T(8,128)(2,1)S(1)} %pad_maximum_fusion.4), channel_id=1, source_target_pairs={{0,1},{1,0},{2,3},{3,2},{4,5},{5,4},{6,7},{7,6},{8,9},{9,8},{10,11... | collective-permute-start | bytes 589832 | tf_op jit(solution)/shard_map/ppermute | solution.py:124
  3.0 17.9 %collective-permute-start.3 = (bf16[2,4,128,256]{3,2,1,0:T(8,128)(2,1)S(1)}, bf16[2,4,128,256]{3,2,1,0:T(8,128)(2,1)S(1)}, u32[]{:S(2)}, u32[]{:S(2)}) collective-permute-start(bf16[2,4,128,256]{3,2,1,0:T(8,128)(2,1)S(1)} %bitcast.128), channel_id=1, source_target_pairs={{0,24},{8,16},{1,25},{9,17},{2,26},{10,18},{3,27},{11,19},{4,28},{... | collective-permute-start | bytes 1572872 | tf_op jit(solution)/shard_map/ppermute | solution.py:145
  4.3 7.3 %collective-permute-start.1 = (bf16[3,128,256]{2,1,0:T(8,128)(2,1)S(1)}, bf16[3,128,256]{2,1,0:T(8,128)(2,1)S(1)}, u32[]{:S(2)}, u32[]{:S(2)}) collective-permute-start(bf16[3,128,256]{2,1,0:T(8,128)(2,1)S(1)} %pad_maximum_fusion.5), channel_id=1, source_target_pairs={{1,2},{2,1},{3,4},{4,3},{5,6},{6,5},{9,10},{10,9},{11,12},{12,11},... | collective-permute-start | bytes 589832 | tf_op jit(solution)/shard_map/ppermute | solution.py:124
  11.6 2.0 %copy-start = (bf16[1,3,3,3,256,256]{5,4,3,2,1,0:T(8,128)(2,1)S(1)}, bf16[1,3,3,3,256,256]{5,4,3,2,1,0:T(8,128)(2,1)}, u32[]{:S(2)}) copy-start(bf16[1,3,3,3,256,256]{5,4,3,2,1,0:T(8,128)(2,1)} %param.8) | copy-start | bytes 10616836
  13.6 3.6 %copy-start.2 = (bf16[1,3,3,3,256,256]{5,4,3,2,1,0:T(8,128)(2,1)S(1)}, bf16[1,3,3,3,256,256]{5,4,3,2,1,0:T(8,128)(2,1)}, u32[]{:S(2)}) copy-start(bf16[1,3,3,3,256,256]{5,4,3,2,1,0:T(8,128)(2,1)} %param.9) | copy-start | bytes 10616836
  17.3 4.4 %copy-start.5 = (bf16[1,2,4,16,8,256]{5,4,3,2,1,0:T(8,128)(2,1)S(1)}, bf16[1,2,4,16,8,256]{5,4,3,2,1,0:T(8,128)(2,1)}, u32[]{:S(2)}) copy-start(bf16[1,2,4,16,8,256]{5,4,3,2,1,0:T(8,128)(2,1)} %param.5) | copy-start | bytes 1572868
  19.4 15.4 %collective-permute-start.2 = (bf16[2,4,128,256]{3,2,1,0:T(8,128)(2,1)S(1)}, bf16[2,4,128,256]{3,2,1,0:T(8,128)(2,1)}, u32[]{:S(2)}, u32[]{:S(2)}) collective-permute-start(bf16[2,4,128,256]{3,2,1,0:T(8,128)(2,1)S(1)} %pad_maximum_fusion), channel_id=1, source_target_pairs={{0,8},{1,9},{2,10},{3,11},{4,12},{5,13},{6,14},{7,15}} | collective-permute-start | bytes 1572872 | tf_op jit(solution)/shard_map/ppermute | solution.py:145
  20.9 0.8 copy-start.6
  21.7 8.9 %copy-start.1 = (bf16[1,3,3,3,256,256]{5,4,3,2,1,0:T(8,128)(2,1)S(1)}, bf16[1,3,3,3,256,256]{5,4,3,2,1,0:T(8,128)(2,1)}, u32[]{:S(2)}) copy-start(bf16[1,3,3,3,256,256]{5,4,3,2,1,0:T(8,128)(2,1)} %param.8) | copy-start | bytes 10616836
  23.4 3.7 %collective-permute-start.4 = (bf16[3,128,256]{2,1,0:T(8,128)(2,1)S(1)}, bf16[3,128,256]{2,1,0:T(8,128)(2,1)S(1)}, u32[]{:S(2)}, u32[]{:S(2)}) collective-permute-start(bf16[3,128,256]{2,1,0:T(8,128)(2,1)S(1)} %pad_maximum_fusion.6), channel_id=1, source_target_pairs={{0,1},{1,0},{2,3},{3,2},{4,5},{5,4},{6,7},{7,6},{8,9},{9,8},{10,11... | collective-permute-start | bytes 589832 | tf_op jit(solution)/shard_map/ppermute | solution.py:124
  23.5 7.0 %collective-permute-start.5 = (bf16[3,128,256]{2,1,0:T(8,128)(2,1)S(1)}, bf16[3,128,256]{2,1,0:T(8,128)(2,1)S(1)}, u32[]{:S(2)}, u32[]{:S(2)}) collective-permute-start(bf16[3,128,256]{2,1,0:T(8,128)(2,1)S(1)} %pad_maximum_fusion.7), channel_id=1, source_target_pairs={{1,2},{2,1},{3,4},{4,3},{5,6},{6,5},{9,10},{10,9},{11,12},{12,11},... | collective-permute-start | bytes 589832 | tf_op jit(solution)/shard_map/ppermute | solution.py:124
  34.9 14.2 %collective-permute-start.7 = (bf16[2,4,128,256]{3,2,1,0:T(8,128)(2,1)}, bf16[2,4,128,256]{3,2,1,0:T(8,128)(2,1)}, u32[]{:S(2)}, u32[]{:S(2)}) collective-permute-start(bf16[2,4,128,256]{3,2,1,0:T(8,128)(2,1)} %collective-permute-done.2), channel_id=1, source_target_pairs={{8,24},{9,25},{10,26},{11,27},{12,28},{13,29},{14,30},{15,31}} | collective-permute-start | bytes 1572872 | tf_op jit(solution)/shard_map/ppermute | solution.py:145
  36.3 12.7 %collective-permute-start.6 = (bf16[4,128,256]{2,1,0:T(8,128)(2,1)}, bf16[4,128,256]{2,1,0:T(8,128)(2,1)}, u32[]{:S(2)}, u32[]{:S(2)}) collective-permute-start(bf16[4,128,256]{2,1,0:T(8,128)(2,1)} %get-tuple-element.36.first_mid), channel_id=1, source_target_pairs={{0,8},{8,16},{16,24},{1,9},{9,17},{17,25},{2,10},{10,18},{18,26},{... | collective-permute-start | bytes 786440 | tf_op jit(solution)/shard_map/ppermute | solution.py:145
  43.0 11.7 %collective-permute-start.8 = (bf16[4,128,256]{2,1,0:T(8,128)(2,1)}, bf16[4,128,256]{2,1,0:T(8,128)(2,1)}, u32[]{:S(2)}, u32[]{:S(2)}) collective-permute-start(bf16[4,128,256]{2,1,0:T(8,128)(2,1)} %shard_map.58), channel_id=1, source_target_pairs={{0,8},{8,16},{16,24},{1,9},{9,17},{17,25},{2,10},{10,18},{18,26},{... | collective-permute-start | bytes 786440 | tf_op jit(solution)/shard_map/ppermute | solution.py:145
  44.9 9.8 %copy-start.4 = (bf16[3,2,4,16,8,256]{5,4,3,2,1,0:T(8,128)(2,1)S(1)}, bf16[3,2,4,16,8,256]{5,4,3,2,1,0:T(8,128)(2,1)}, u32[]{:S(2)}) copy-start(bf16[3,2,4,16,8,256]{5,4,3,2,1,0:T(8,128)(2,1)} %param.7) | copy-start | bytes 4718596
  56.0 6.4 %collective-permute-start.9 = (bf16[3,128,256]{2,1,0:T(8,128)(2,1)S(1)}, bf16[3,128,256]{2,1,0:T(8,128)(2,1)S(1)}, u32[]{:S(2)}, u32[]{:S(2)}) collective-permute-start(bf16[3,128,256]{2,1,0:T(8,128)(2,1)S(1)} %pad_maximum_fusion.8), channel_id=1, source_target_pairs={{0,1},{1,0},{2,3},{3,2},{4,5},{5,4},{6,7},{7,6},{8,9},{9,8},{10,11... | collective-permute-start | bytes 589832 | tf_op jit(solution)/shard_map/ppermute | solution.py:124
  58.1 22.3 %collective-permute-start.12 = (bf16[2,4,128,256]{3,2,1,0:T(8,128)(2,1)S(1)}, bf16[2,4,128,256]{3,2,1,0:T(8,128)(2,1)S(1)}, u32[]{:S(2)}, u32[]{:S(2)}) collective-permute-start(bf16[2,4,128,256]{3,2,1,0:T(8,128)(2,1)S(1)} %pad_maximum_fusion.1), channel_id=1, source_target_pairs={{8,24},{9,25},{10,26},{11,27},{12,28},{13,29},{14,30},{15,31}} | collective-permute-start | bytes 1572872 | tf_op jit(solution)/shard_map/ppermute | solution.py:145
  58.8 12.8 %copy-start.3 = (bf16[1,3,3,3,256,256]{5,4,3,2,1,0:T(8,128)(2,1)S(1)}, bf16[1,3,3,3,256,256]{5,4,3,2,1,0:T(8,128)(2,1)}, u32[]{:S(2)}) copy-start(bf16[1,3,3,3,256,256]{5,4,3,2,1,0:T(8,128)(2,1)} %param.9) | copy-start | bytes 10616836
  58.8 7.3 %collective-permute-start.10 = (bf16[3,128,256]{2,1,0:T(8,128)(2,1)S(1)}, bf16[3,128,256]{2,1,0:T(8,128)(2,1)S(1)}, u32[]{:S(2)}, u32[]{:S(2)}) collective-permute-start(bf16[3,128,256]{2,1,0:T(8,128)(2,1)S(1)} %pad_maximum_fusion.9), channel_id=1, source_target_pairs={{1,2},{2,1},{3,4},{4,3},{5,6},{6,5},{9,10},{10,9},{11,12},{12,11},... | collective-permute-start | bytes 589832 | tf_op jit(solution)/shard_map/ppermute | solution.py:124
  69.7 10.7 %collective-permute-start.11 = (bf16[4,128,256]{2,1,0:T(8,128)(2,1)S(1)}, bf16[4,128,256]{2,1,0:T(8,128)(2,1)S(1)}, u32[]{:S(2)}, u32[]{:S(2)}) collective-permute-start(bf16[4,128,256]{2,1,0:T(8,128)(2,1)S(1)} %get-tuple-element.42.first_mid), channel_id=1, source_target_pairs={{0,8},{8,16},{16,24},{1,9},{9,17},{17,25},{2,10},{10,18},{18,26},{... | collective-permute-start | bytes 786440 | tf_op jit(solution)/shard_map/ppermute | solution.py:145
  73.8 12.3 %collective-permute-start.13 = (bf16[4,128,256]{2,1,0:T(8,128)(2,1)S(1)}, bf16[4,128,256]{2,1,0:T(8,128)(2,1)S(1)}, u32[]{:S(2)}, u32[]{:S(2)}) collective-permute-start(bf16[4,128,256]{2,1,0:T(8,128)(2,1)S(1)} %shard_map.60), channel_id=1, source_target_pairs={{0,8},{8,16},{16,24},{1,9},{9,17},{17,25},{2,10},{10,18},{18,26},{... | collective-permute-start | bytes 786440 | tf_op jit(solution)/shard_map/ppermute | solution.py:145
  86.2 4.8 %collective-permute-start.14 = (bf16[3,128,256]{2,1,0:T(8,128)(2,1)S(1)}, bf16[3,128,256]{2,1,0:T(8,128)(2,1)S(1)}, u32[]{:S(2)}, u32[]{:S(2)}) collective-permute-start(bf16[3,128,256]{2,1,0:T(8,128)(2,1)S(1)} %pad_maximum_fusion.10), channel_id=1, source_target_pairs={{0,1},{1,0},{2,3},{3,2},{4,5},{5,4},{6,7},{7,6},{8,9},{9,8},{10,11... | collective-permute-start | bytes 589832 | tf_op jit(solution)/shard_map/ppermute | solution.py:124
  87.1 22.1 %collective-permute-start.17 = (bf16[2,4,128,256]{3,2,1,0:T(8,128)(2,1)S(1)}, bf16[2,4,128,256]{3,2,1,0:T(8,128)(2,1)S(1)}, u32[]{:S(2)}, u32[]{:S(2)}) collective-permute-start(bf16[2,4,128,256]{3,2,1,0:T(8,128)(2,1)S(1)} %pad_maximum_fusion.2), channel_id=1, source_target_pairs={{8,24},{9,25},{10,26},{11,27},{12,28},{13,29},{14,30},{15,31}} | collective-permute-start | bytes 1572872 | tf_op jit(solution)/shard_map/ppermute | solution.py:145
  87.9 7.0 %collective-permute-start.15 = (bf16[3,128,256]{2,1,0:T(8,128)(2,1)S(1)}, bf16[3,128,256]{2,1,0:T(8,128)(2,1)S(1)}, u32[]{:S(2)}, u32[]{:S(2)}) collective-permute-start(bf16[3,128,256]{2,1,0:T(8,128)(2,1)S(1)} %pad_maximum_fusion.11), channel_id=1, source_target_pairs={{1,2},{2,1},{3,4},{4,3},{5,6},{6,5},{9,10},{10,9},{11,12},{12,11},... | collective-permute-start | bytes 589832 | tf_op jit(solution)/shard_map/ppermute | solution.py:124
  98.5 10.7 %collective-permute-start.16 = (bf16[4,128,256]{2,1,0:T(8,128)(2,1)S(1)}, bf16[4,128,256]{2,1,0:T(8,128)(2,1)S(1)}, u32[]{:S(2)}, u32[]{:S(2)}) collective-permute-start(bf16[4,128,256]{2,1,0:T(8,128)(2,1)S(1)} %get-tuple-element.47.first_mid), channel_id=1, source_target_pairs={{8,16},{16,24},{9,17},{17,25},{10,18},{18,26},{11,19},{19,27},{12,... | collective-permute-start | bytes 786440 | tf_op jit(solution)/shard_map/ppermute | solution.py:145
  102.6 12.3 %collective-permute-start.18 = (bf16[4,128,256]{2,1,0:T(8,128)(2,1)S(1)}, bf16[4,128,256]{2,1,0:T(8,128)(2,1)S(1)}, u32[]{:S(2)}, u32[]{:S(2)}) collective-permute-start(bf16[4,128,256]{2,1,0:T(8,128)(2,1)S(1)} %shard_map.62), channel_id=1, source_target_pairs={{8,16},{16,24},{9,17},{17,25},{10,18},{18,26},{11,19},{19,27},{12,... | collective-permute-start | bytes 786440 | tf_op jit(solution)/shard_map/ppermute | solution.py:145
  115.0 4.2 %collective-permute-start.19 = (bf16[3,128,256]{2,1,0:T(8,128)(2,1)S(1)}, bf16[3,128,256]{2,1,0:T(8,128)(2,1)S(1)}, u32[]{:S(2)}, u32[]{:S(2)}) collective-permute-start(bf16[3,128,256]{2,1,0:T(8,128)(2,1)S(1)} %pad_maximum_fusion.12), channel_id=1, source_target_pairs={{0,1},{1,0},{2,3},{3,2},{4,5},{5,4},{6,7},{7,6},{8,9},{9,8},{10,11... | collective-permute-start | bytes 589832 | tf_op jit(solution)/shard_map/ppermute | solution.py:124
  115.9 7.0 %collective-permute-start.20 = (bf16[3,128,256]{2,1,0:T(8,128)(2,1)S(1)}, bf16[3,128,256]{2,1,0:T(8,128)(2,1)S(1)}, u32[]{:S(2)}, u32[]{:S(2)}) collective-permute-start(bf16[3,128,256]{2,1,0:T(8,128)(2,1)S(1)} %pad_maximum_fusion.13), channel_id=1, source_target_pairs={{1,2},{2,1},{3,4},{4,3},{5,6},{6,5},{9,10},{10,9},{11,12},{12,11},... | collective-permute-start | bytes 589832 | tf_op jit(solution)/shard_map/ppermute | solution.py:124

commit v5 on v4

v5 whole, which is shorter than its diff:
```python
import functools

import jax
import jax.numpy as jnp
from jax import lax
from jax.experimental import pallas as pl
from jax.experimental.pallas import tpu as pltpu
from jax.sharding import PartitionSpec as P

EPS = 1e-05
VMEM_LIMIT = 12 * 1024 * 1024


def act(values):
    values = values.astype(jnp.float32)
    scaled = values * lax.rsqrt(jnp.mean(values * values, axis=-1, keepdims=True) + EPS)
    return scaled * (0.5 + 0.5 * jnp.tanh(0.5 * scaled))


def fill(even, odd, at, values, width):
    planes, _, chans = values.shape
    field = act(values)
    edge = jnp.zeros((planes, width, chans), jnp.float32)
    even[pl.ds(at, planes)] = field.astype(jnp.bfloat16)
    odd[pl.ds(at, planes)] = jnp.concatenate([edge, field, edge], axis=1).astype(jnp.bfloat16)


def convolve(taps, weights, width):
    planes, voxels, chans = taps[0].shape
    slab = jnp.concatenate([part.reshape(planes * voxels, chans) for part in taps], axis=-1)
    total = None
    for k in (1, 0, 2):
        columns = jnp.concatenate([weights[(3 * n + k) * chans : (3 * n + k + 1) * chans] for n in range(9)], axis=0)
        part = jnp.dot(slab, columns, preferred_element_type=jnp.float32).reshape(-1, width, chans)
        column = lax.broadcasted_iota(jnp.int32, part.shape, 1)
        if k == 0:
            part = jnp.where(column == 0, 0.0, pltpu.roll(part, 1, 1))
        elif k == 2:
            part = jnp.where(column == width - 1, 0.0, pltpu.roll(part, width - 1, 1))
        total = part if total is None else total + part
    return total.reshape(planes, voxels, chans)


def planes_at(even, odd, start, count, width):
    voxels = even.shape[1]
    return [
        even[start : start + count] if j == 1 else odd[start : start + count, j * width : j * width + voxels]
        for j in range(3)
    ]


def inner_kernel(width, p, q, weights, even, odd, inner):
    planes = q.shape[0]
    fill(even, odd, 0, q[...], width)
    taps = [part for i in range(3) for part in planes_at(even, odd, i, planes - 2, width)]
    inner[...] = (p[1:-1].astype(jnp.float32) + convolve(taps, weights, width)).astype(inner.dtype)


def loading_kernel(width, p, q, weights_hbm, even, odd, inner, weights, sem):
    copy = pltpu.make_async_copy(weights_hbm, weights, sem)
    copy.start()
    planes = q.shape[0]
    fill(even, odd, 0, q[...], width)
    taps = [part for i in range(3) for part in planes_at(even, odd, i, planes - 2, width)]
    copy.wait()
    inner[...] = (p[1:-1].astype(jnp.float32) + convolve(taps, weights, width)).astype(inner.dtype)


def edge_kernel(
    width, flags, p, even, odd, inner, q_near, q_far, p_near, p_far, weights, low, mid, high, edge_even, edge_odd
):
    planes = p.shape[0]
    above = flags[2] > 0
    near, far = q_near[:2].astype(jnp.float32), q_far[:2].astype(jnp.float32)
    fill(edge_even, edge_odd, 0, jnp.where(above, far, near), width)
    fill(edge_even, edge_odd, 2, jnp.where(above, near, far), width)
    halo = lambda start, count: planes_at(edge_even, edge_odd, start, count, width)
    own = lambda start, count: planes_at(even, odd, start, count, width)
    sources = (
        (halo(0, 2), own(planes - 2, 2)),
        (halo(1, 1), own(0, 1), own(planes - 1, 1), halo(2, 1)),
        (own(0, 2), halo(2, 2)),
    )
    taps = [jnp.concatenate(parts, axis=0) for source in sources for parts in zip(*source)]
    total = convolve(taps, weights, width)
    near, far = p_near[-1:].astype(jnp.float32), p_far[-1:].astype(jnp.float32)
    low[...] = jnp.where(flags[0] > 0, jnp.where(above, far, near) + total[:1], 0.0).astype(low.dtype)
    mid[pl.ds(0, 1)] = (p[:1].astype(jnp.float32) + total[1:2]).astype(mid.dtype)
    mid[pl.ds(1, planes - 2)] = inner[...]
    mid[pl.ds(planes - 1, 1)] = (p[-1:].astype(jnp.float32) + total[2:3]).astype(mid.dtype)
    high[...] = jnp.where(flags[1] > 0, jnp.where(above, near, far) + total[3:], 0.0).astype(high.dtype)


def second_kernel(width, first_low, first_mid, first_high, q, weights, out, even, odd):
    planes = q.shape[0]
    fill(even, odd, 0, first_low[...], width)
    fill(even, odd, 1, first_mid[...], width)
    fill(even, odd, 1 + planes, first_high[...], width)
    taps = [part for i in range(3) for part in planes_at(even, odd, i, planes, width)]
    second = (q[...].astype(jnp.float32) + convolve(taps, weights, width)).astype(out.dtype)
    if len(out.shape) == 4:
        out[0] = first_mid[...]
        out[1] = second
    else:
        out[...] = second


def call(kernel, out_shape, scratch, arguments, width):
    specs = [pl.BlockSpec(memory_space=pltpu.VMEM) for _ in arguments]
    if kernel is edge_kernel:
        specs[0] = pl.BlockSpec(memory_space=pltpu.SMEM)
    if kernel is loading_kernel:
        specs[-1] = pl.BlockSpec(memory_space=pltpu.HBM)
    shapes = [jax.ShapeDtypeStruct(shape, jnp.bfloat16) for shape in out_shape]
    return pl.pallas_call(
        functools.partial(kernel, width),
        out_shape=shapes,
        in_specs=specs,
        out_specs=[pl.BlockSpec(memory_space=pltpu.VMEM) for _ in shapes],
        scratch_shapes=[pltpu.VMEM(shape, jnp.bfloat16) if shape else pltpu.SemaphoreType.DMA for shape in scratch],
        compiler_params=pltpu.CompilerParams(vmem_limit_bytes=VMEM_LIMIT),
        cost_estimate=pl.CostEstimate(flops=1, bytes_accessed=1, transcendentals=0),
    )(*arguments)


def stored(planes, voxels, chans, width):
    return (planes, voxels, chans), (planes, voxels + 2 * width, chans)


def inner_half(p, q, weights, width, load):
    planes, voxels, chans = q.shape
    shapes = [*stored(planes, voxels, chans, width), (planes - 2, voxels, chans)]
    if load:
        weights = pltpu.with_memory_space_constraint(weights, pltpu.HBM)
        return call(loading_kernel, shapes + [weights.shape], [()], (p, q, weights), width)
    return *call(inner_kernel, shapes, [], (p, q, weights), width), weights


def first_half(flags, p, kept, q_halos, p_halos, weights, width):
    planes, voxels, chans = p.shape
    return call(
        edge_kernel,
        [(1, voxels, chans), (planes, voxels, chans), (1, voxels, chans)],
        stored(4, voxels, chans, width),
        (flags, p, *kept, *q_halos, *p_halos, weights),
        width,
    )


def second_half(first, q, weights, width, both):
    planes, voxels, chans = q.shape
    (out,) = call(
        second_kernel,
        [(2, *q.shape) if both else q.shape],
        stored(planes + 2, voxels, chans, width),
        (*first, q, weights),
        width,
    )
    return out


def boundary(block, upward, width):
    return lax.dynamic_slice_in_dim(block, jnp.where(upward, block.shape[0] - width, 0), width, axis=0)


def swapped(blocks, widths, above):
    count = lax.axis_size("depth")

    def swap(upward, base):
        part = jnp.concatenate([boundary(block, upward, width) for block, width in zip(blocks, widths)], axis=0)
        pairs = [pair for i in range(base, count - 1, 2) for pair in ((i, i + 1), (i + 1, i))]
        return lax.ppermute(part, "depth", pairs)

    return swap(above, 0), swap(jnp.logical_not(above), 1)


def local(resident, previous, incoming, first_weights, second_weights):
    section = lax.axis_index("section")
    sections = lax.axis_size("section")
    half = sections // 2
    depth = lax.axis_index("depth")
    ticks = incoming.shape[0] + 1
    _, _, planes, rows, width, chans = resident.shape
    voxels = rows * width
    flat = lambda a: a.reshape(a.shape[0], 2, planes, voxels, chans)
    resident, previous, incoming = flat(resident)[0], flat(previous)[0], flat(incoming)
    w_one = first_weights.reshape(27 * chans, chans)
    w_two = second_weights.reshape(27 * chans, chans)
    above = depth % 2 == 0
    flags = jnp.stack([depth > 0, depth < lax.axis_size("depth") - 1, above]).astype(jnp.int32)

    def send(block, pairs):
        return lax.ppermute(block, "section", pairs) if pairs else block

    across = [(j, sections - 1 - j) for j in range(1, half - 1)]
    decoder = section >= half

    def join(held, skip):
        total = (held.astype(jnp.float32) + skip.astype(jnp.float32)).astype(jnp.bfloat16)
        return jnp.where(decoder, total, held)

    newer, older, relayed, direct = {}, {}, {}, {}

    def arrived(slot, stream):
        fresh = incoming[min(slot, ticks - 1) - 1, stream]
        if slot == 1:
            return jnp.where(section == 0, fresh, join(resident[stream], mirrored[stream]))
        held = jnp.where(section == 1, older[stream], newer[stream])
        skip = jnp.where(section == sections - 1, relayed[stream], newer[stream])
        if across:
            skip = jnp.where((section > half) & (section < sections - 1), direct[stream], skip)
        return jnp.where(section == 0, fresh, join(held, skip))

    p, q = resident
    mirrored = send(previous, [(j, sections - 1 - j) for j in range(half)])
    q_halos = p_halos = swapped((q, p), (2, 1), above)
    for slot in range(ticks + 1):
        if slot == 1:
            p, q, q_halos = following
            p_halos = q_halos
        elif slot > 1:
            p = arrived(slot, 0)
            p_halos = swapped((p,), (1,), above)
            p, p_halos, newer[1] = lax.optimization_barrier((p, p_halos, newer[1]))
            q = arrived(slot, 1)
            q_halos = swapped((q,), (2,), above)
        *kept, w_one = inner_half(p, q, w_one, width, slot == 0)
        first = first_half(flags, p, kept, q_halos, p_halos, w_one, width)
        onward = [(j, j + 1) for j in range(1, sections - 1)]
        if slot < ticks - 1:
            onward = [(0, 1)] + onward
        received, relays = {}, {}
        if slot == 0:
            mirrored, _ = lax.optimization_barrier((mirrored, first[1]))
            following = arrived(1, 0), arrived(1, 1)
            following = *following, swapped(following[::-1], (2, 1), above)
            first, joined = lax.optimization_barrier((first, following[:2]))
            following = *joined, following[2]
        elif slot < ticks:
            received[0] = send(first[1], onward)
        second = second_half(first, q, w_two, width, slot == ticks)
        if slot == 0:
            second, q_halos = lax.optimization_barrier((second, following[2]))
            following = *following[:2], q_halos
            received = send(jnp.stack([first[1], second]), [(0, 1)])
        elif slot < ticks:
            received[1] = send(second, onward)
            relay_p, relay_q = newer[0], newer[1]
            if slot == 1:
                relay_p, _ = lax.optimization_barrier((relay_p, first[1]))
            relay_q, second = lax.optimization_barrier((relay_q, second))
            relays = {0: send(relay_p, [(1, sections - 1)]), 1: send(relay_q, [(1, sections - 1)])}
            if across:
                direct = {0: send(first[1], across), 1: send(second, across)}
        older, newer, relayed = newer, received, relays
    result = second
    return result.reshape(1, 2, planes, rows, width, chans)


def solution(mesh):
    in_specs = (
        P("section", None, "depth", None, None, None),
        P("section", None, "depth", None, None, None),
        P(None, None, "depth", None, None, None),
        P("section", None, None, None, None, None),
        P("section", None, None, None, None, None),
    )
    out_specs = P("section", None, "depth", None, None, None)
    return jax.shard_map(local, mesh=mesh, in_specs=in_specs, out_specs=out_specs, check_vma=False)
```

time: 130 us -> 137 us (1.054)
  waiting for transfers between devices: 48.4 us -> 30.9 us
  starting transfers between devices: 38.7 us -> 49.5 us
  local copies, waits for them, and re-layouts: 4.15 us -> 14.6 us
  Pallas kernels: 31 us -> 35.2 us
  other arithmetic: 6.82 us -> 4.9 us
    ppermute x10 -> x16, waiting for transfers between devices: 19.5 us -> 9.22 us  [swap(): return lax.ppermute(part, 'depth', pairs)]
    unnamed x16 -> x48, local copies, waits for them, and re-layouts: 2.82 us -> 12.5 us
    ppermute x11 -> x14, waiting for transfers between devices: 28.9 us -> 21.7 us  [send(): return lax.ppermute(block, 'section', pairs) if pairs else block]
    ppermute x10 -> x16, starting transfers between devices: 20.6 us -> 27.5 us  [swap(): return lax.ppermute(part, 'depth', pairs)]
    pallas_call x10 -> x15, Pallas kernels: 31 us -> 35.2 us  [call(): pl.pallas_call(functools.partial(kernel, width), out_shape=shapes, in_spe...]
    ppermute x11 -> x14, starting transfers between devices: 18.1 us -> 22.1 us  [send(): return lax.ppermute(block, 'section', pairs) if pairs else block]
    another operation x3 -> x0, other arithmetic: 1.97 us -> none  [the longest x2 1.13 us: local(): held = jnp.stack([newer[0], newer[1]])]
    concatenate x10 -> x4, other arithmetic: 0.2 us -> 1.58 us  [swap(): jnp.concatenate([boundary(block, upward, width) for block, width in zip(b...]
  transfers between devices with their start and end apart: 21 -> 30, of which waited for: 12 -> 11; matrix products, arithmetic and copies ran while one was open for 3% -> 4% of each run, Pallas kernels for 20% -> 22%
where the time goes in v5:
time: 137 us; the launch traced here: 136 us
  starting transfers between devices  49.5 us (36%)
  Pallas kernels  35.2 us (26%)
  waiting for transfers between devices  30.9 us (23%)
  local copies, waits for them, and re-layouts  14.6 us (11%)
  other arithmetic  4.9 us (4%)
    pallas_call x15, Pallas kernels, call(): pl.pallas_call(functools.partial(kernel, width), out_shape=shapes, in_spe...  35.2 us
    ppermute x16, starting transfers between devices, swap(): return lax.ppermute(part, 'depth', pairs)  27.5 us
    ppermute x14, starting transfers between devices, send(): return lax.ppermute(block, 'section', pairs) if pairs else block  22.1 us
    ppermute x14, waiting for transfers between devices, send(): return lax.ppermute(block, 'section', pairs) if pairs else block  21.7 us
    unnamed x48, local copies, waits for them, and re-layouts  12.5 us
    ppermute x16, waiting for transfers between devices, swap(): return lax.ppermute(part, 'depth', pairs)  9.22 us
  transfers between devices with their start and end apart: 30, of which 11 were waited for; matrix products, arithmetic and copies ran while one was open for 4% of the time, Pallas kernels for 22%

profile of v5, /device:TPU:13, one launch (start us, length us, event | category | flops | bytes accessed | tf_op | source)
XLA Modules:
  0.0 135.8 jit_solution(5459455955820868794)
XLA Ops:
  0.0 1.3 collective-permute-start.2
  1.3 1.1 slice_bitcast_fusion.8
  4.7 3.1 %collective-permute-start.1 = (bf16[3,128,256]{2,1,0:T(8,128)(2,1)}, bf16[3,128,256]{2,1,0:T(8,128)(2,1)}, u32[]{:S(2)}, u32[]{:S(2)}) collective-permute-start(bf16[3,128,256]{2,1,0:T(8,128)(2,1)} %pad_maximum_fusion.2), channel_id=1, source_target_pairs={{1,2},{2,1},{3,4},{4,3},{5,6},{6,5},{9,10},{10,9},{11,12},{12,11},... | collective-permute-start | bytes 589832 | tf_op jit(solution)/shard_map/ppermute | solution.py:172
  7.8 3.1 %shard_map.55 = (bf16[4,128,256]{2,1,0:T(8,128)(2,1)S(1)}, bf16[4,144,256]{2,1,0:T(8,128)(2,1)S(1)}, bf16[2,128,256]{2,1,0:T(8,128)(2,1)S(1)}, bf16[6912,256]{1,0:T(8,128)(2,1)S(1)}) custom-call(bf16[4,128,256]{2,1,0:T(8,128)(2,1)S(1)} %get-tuple-element.122.p, bf16[4,128,256]{2,1,0:T(8,128)(2,1)S(1)} %get-tuple-element.121.q, bf16[6912,256]{1,0:T(8,128)(2,1)} %bitcast.67), custom_call_target="tpu_custom_call" | custom-call | flops 1 | bytes 1 | tf_op jit(solution)/shard_map/pallas_call | solution.py:115
  14.0 1.0 copy-done.10
  15.0 0.9 copy-done.12
  16.8 3.4 %shard_map.56 = (bf16[1,128,256]{2,1,0:T(8,128)(2,1)S(1)}, bf16[4,128,256]{2,1,0:T(8,128)(2,1)S(1)}, bf16[1,128,256]{2,1,0:T(8,128)(2,1)S(1)}) custom-call(s32[3]{0:T(128)S(1)} %add_convert_fusion.6.flags, bf16[4,128,256]{2,1,0:T(8,128)(2,1)S(1)} %copy-done.8, bf16[4,128,256]{2,1,0:T(8,128)(2,1)S(1)} %copy-done.12, bf16[4,144,256]{2,1,0:T(8,128)(2,1)S(1)} %copy-done.10, ...), custom_call_target="tpu_custom_call" | custom-call | flops 1 | bytes 1 | tf_op jit(solution)/shard_map/pallas_call | solution.py:115
  20.3 1.6 %fusion.10 = (bf16[4,128,256]{2,1,0:T(8,128)(2,1)S(1)}, bf16[4,128,256]{2,1,0:T(8,128)(2,1)S(1)}) fusion(bf16[3,2,4,128,256]{4,3,2,1,0:T(8,128)(2,1)} %bitcast.68, bf16[2,4,128,256]{3,2,1,0:T(8,128)(2,1)} %collective-permute-done.2, pred[]{:T(512)S(6)} %ge.3, pred[]{:T(512)S(6)} %eq.11, bf16[1,2,4,16,8,256]{5,4,3,2,1,0:T(8,128)(2,1)S(1)} %copy-done.22), kind=kLoop, calls=%fused_computation.19 | loop fusion | flops 1572864 | bytes 2097154 | tf_op jit(solution)/shard_map/jit(_where)/select_n | solution.py:207
  21.9 2.5 %collective-permute-start.4 = (bf16[3,128,256]{2,1,0:T(8,128)(2,1)S(1)}, bf16[3,128,256]{2,1,0:T(8,128)(2,1)S(1)}, u32[]{:S(2)}, u32[]{:S(2)}) collective-permute-start(bf16[3,128,256]{2,1,0:T(8,128)(2,1)S(1)} %pad_maximum_fusion.4), channel_id=1, source_target_pairs={{1,2},{2,1},{3,4},{4,3},{5,6},{6,5},{9,10},{10,9},{11,12},{12,11},... | collective-permute-start | bytes 589832 | tf_op jit(solution)/shard_map/ppermute | solution.py:172
  24.5 2.1 %shard_map.57 = bf16[4,128,256]{2,1,0:T(8,128)(2,1)S(1)} custom-call(bf16[1,128,256]{2,1,0:T(8,128)(2,1)S(1)} %get-tuple-element.70.first_low, bf16[4,128,256]{2,1,0:T(8,128)(2,1)S(1)} %get-tuple-element.69.first_mid, bf16[1,128,256]{2,1,0:T(8,128)(2,1)S(1)} %get-tuple-element.71.first_high, bf16[4,128,256]{2,1,0:T(8,128)(2,1)S(1)} %copy-done.4, ...), custom_call_target="tpu_custom_call" | custom-call | flops 1 | bytes 1 | tf_op jit(solution)/shard_map/pallas_call | solution.py:115
  26.7 2.3 %collective-permute-done.4.q_far.p_far = bf16[3,128,256]{2,1,0:T(8,128)(2,1)S(1)} collective-permute-done((bf16[3,128,256]{2,1,0:T(8,128)(2,1)S(1)}, bf16[3,128,256]{2,1,0:T(8,128)(2,1)S(1)}, u32[]{:S(2)}, u32[]{:S(2)}) %collective-permute-start.4) | collective-permute-done | bytes 196640 | tf_op jit(solution)/shard_map/ppermute | solution.py:172
  29.7 1.2 shard_map.58
  30.9 3.3 %shard_map.59 = (bf16[1,128,256]{2,1,0:T(8,128)(2,1)S(1)}, bf16[4,128,256]{2,1,0:T(8,128)(2,1)}, bf16[1,128,256]{2,1,0:T(8,128)(2,1)S(1)}) custom-call(s32[3]{0:T(128)S(1)} %add_convert_fusion.6.flags, bf16[4,128,256]{2,1,0:T(8,128)(2,1)S(1)} %get-tuple-element.73.p, bf16[4,128,256]{2,1,0:T(8,128)(2,1)S(1)} %get-tuple-element.75.even, ...), custom_call_target="tpu_custom_call" | custom-call | flops 1 | bytes 1 | tf_op jit(solution)/shard_map/pallas_call | solution.py:115
  35.5 3.1 %collective-permute-start.6 = (bf16[4,128,256]{2,1,0:T(8,128)(2,1)}, bf16[4,128,256]{2,1,0:T(8,128)(2,1)}, u32[]{:S(2)}, u32[]{:S(2)}) collective-permute-start(bf16[4,128,256]{2,1,0:T(8,128)(2,1)} %get-tuple-element.80.first_mid), channel_id=1, source_target_pairs={{0,8},{8,16},{16,24},{1,9},{9,17},{17,25},{2,10},{10,18},{18,26},{... | collective-permute-start | bytes 786440 | tf_op jit(solution)/shard_map/ppermute | solution.py:193
  40.3 1.3 collective-permute-start.7
  41.6 2.0 %copy-done.1 = bf16[1,3,3,3,256,256]{5,4,3,2,1,0:T(8,128)(2,1)S(1)} copy-done((bf16[1,3,3,3,256,256]{5,4,3,2,1,0:T(8,128)(2,1)S(1)}, bf16[1,3,3,3,256,256]{5,4,3,2,1,0:T(8,128)(2,1)}, u32[]{:S(2)}) %copy-start.1) | copy-done | bytes 3538968
  46.2 3.2 %shard_map.60 = bf16[4,128,256]{2,1,0:T(8,128)(2,1)S(1)} custom-call(bf16[1,128,256]{2,1,0:T(8,128)(2,1)S(1)} %copy-done.16, bf16[4,128,256]{2,1,0:T(8,128)(2,1)} %get-tuple-element.80.first_mid, bf16[1,128,256]{2,1,0:T(8,128)(2,1)S(1)} %copy-done.18, bf16[4,128,256]{2,1,0:T(8,128)(2,1)S(1)} %copy-done.6, bf16[6912,256]{1,0:T(8,128)(2,1)S(1)} %bitcast.61), custom_call_target="tpu_custom_call" | custom-call | flops 1 | bytes 1 | tf_op jit(solution)/shard_map/pallas_call | solution.py:115
  49.4 1.9 %collective-permute-start.10 = (bf16[4,128,256]{2,1,0:T(8,128)(2,1)S(1)}, bf16[4,128,256]{2,1,0:T(8,128)(2,1)S(1)}, u32[]{:S(2)}, u32[]{:S(2)}) collective-permute-start(bf16[4,128,256]{2,1,0:T(8,128)(2,1)S(1)} %shard_map.60), channel_id=1, source_target_pairs={{0,8},{8,16},{16,24},{1,9},{9,17},{17,25},{2,10},{10,18},{18,26},{... | collective-permute-start | bytes 786440 | tf_op jit(solution)/shard_map/ppermute | solution.py:193
  52.1 1.1 fusion.17.p
  53.3 3.6 %collective-permute-start.9 = (bf16[1,128,256]{2,1,0:T(8,128)(2,1)S(1)}, bf16[1,128,256]{2,1,0:T(8,128)(2,1)S(1)}, u32[]{:S(2)}, u32[]{:S(2)}) collective-permute-start(bf16[1,128,256]{2,1,0:T(8,128)(2,1)S(1)} %get-tuple-element.133), channel_id=1, source_target_pairs={{1,2},{2,1},{3,4},{4,3},{5,6},{6,5},{9,10},{10,9},{11,12},{12,11},... | collective-permute-start | bytes 196616 | tf_op jit(solution)/shard_map/ppermute | solution.py:172
  56.9 12.2 %collective-permute-done.10 = bf16[4,128,256]{2,1,0:T(8,128)(2,1)S(1)} collective-permute-done((bf16[4,128,256]{2,1,0:T(8,128)(2,1)S(1)}, bf16[4,128,256]{2,1,0:T(8,128)(2,1)S(1)}, u32[]{:S(2)}, u32[]{:S(2)}) %collective-permute-start.10) | collective-permute-done | bytes 262176 | tf_op jit(solution)/shard_map/ppermute | solution.py:193
  69.8 3.1 %collective-permute-start.13 = (bf16[2,128,256]{2,1,0:T(8,128)(2,1)S(1)}, bf16[2,128,256]{2,1,0:T(8,128)(2,1)S(1)}, u32[]{:S(2)}, u32[]{:S(2)}) collective-permute-start(bf16[2,128,256]{2,1,0:T(8,128)(2,1)S(1)} %get-tuple-element.131), channel_id=1, source_target_pairs={{1,2},{2,1},{3,4},{4,3},{5,6},{6,5},{9,10},{10,9},{11,12},{12,11},... | collective-permute-start | bytes 393224 | tf_op jit(solution)/shard_map/ppermute | solution.py:172
  73.8 1.2 shard_map.61
  75.0 1.1 collective-permute-done.13.q_far
  76.1 2.7 %shard_map.62 = (bf16[1,128,256]{2,1,0:T(8,128)(2,1)S(1)}, bf16[4,128,256]{2,1,0:T(8,128)(2,1)S(1)}, bf16[1,128,256]{2,1,0:T(8,128)(2,1)S(1)}) custom-call(s32[3]{0:T(128)S(1)} %add_convert_fusion.6.flags, bf16[4,128,256]{2,1,0:T(8,128)(2,1)S(1)} %fusion.17.p, bf16[4,128,256]{2,1,0:T(8,128)(2,1)S(1)} %get-tuple-element.87.even, ...), custom_call_target="tpu_custom_call" | custom-call | flops 1 | bytes 1 | tf_op jit(solution)/shard_map/pallas_call | solution.py:115
  78.8 3.5 %collective-permute-start.14 = (bf16[4,128,256]{2,1,0:T(8,128)(2,1)S(1)}, bf16[4,128,256]{2,1,0:T(8,128)(2,1)S(1)}, u32[]{:S(2)}, u32[]{:S(2)}) collective-permute-start(bf16[4,128,256]{2,1,0:T(8,128)(2,1)S(1)} %get-tuple-element.92.first_mid), channel_id=1, source_target_pairs={{0,8},{8,16},{16,24},{1,9},{9,17},{17,25},{2,10},{10,18},{18,26},{... | collective-permute-start | bytes 786440 | tf_op jit(solution)/shard_map/ppermute | solution.py:193
  82.3 2.1 %shard_map.63 = bf16[4,128,256]{2,1,0:T(8,128)(2,1)S(1)} custom-call(bf16[1,128,256]{2,1,0:T(8,128)(2,1)S(1)} %get-tuple-element.93.first_low, bf16[4,128,256]{2,1,0:T(8,128)(2,1)S(1)} %get-tuple-element.92.first_mid, bf16[1,128,256]{2,1,0:T(8,128)(2,1)S(1)} %get-tuple-element.94.first_high, bf16[4,128,256]{2,1,0:T(8,128)(2,1)S(1)} %fusion.16.q, ...), custom_call_target="tpu_custom_call" | custom-call | flops 1 | bytes 1 | tf_op jit(solution)/shard_map/pallas_call | solution.py:115
  84.4 1.9 %collective-permute-start.18 = (bf16[4,128,256]{2,1,0:T(8,128)(2,1)S(1)}, bf16[4,128,256]{2,1,0:T(8,128)(2,1)S(1)}, u32[]{:S(2)}, u32[]{:S(2)}) collective-permute-start(bf16[4,128,256]{2,1,0:T(8,128)(2,1)S(1)} %shard_map.63), channel_id=1, source_target_pairs={{0,8},{8,16},{16,24},{1,9},{9,17},{17,25},{2,10},{10,18},{18,26},{... | collective-permute-start | bytes 786440 | tf_op jit(solution)/shard_map/ppermute | solution.py:193
  87.0 3.2 %collective-permute-done.14 = bf16[4,128,256]{2,1,0:T(8,128)(2,1)S(1)} collective-permute-done((bf16[4,128,256]{2,1,0:T(8,128)(2,1)S(1)}, bf16[4,128,256]{2,1,0:T(8,128)(2,1)S(1)}, u32[]{:S(2)}, u32[]{:S(2)}) %collective-permute-start.14) | collective-permute-done | bytes 262176 | tf_op jit(solution)/shard_map/ppermute | solution.py:193
  90.9 2.7 %collective-permute-start.17 = (bf16[1,128,256]{2,1,0:T(8,128)(2,1)S(1)}, bf16[1,128,256]{2,1,0:T(8,128)(2,1)S(1)}, u32[]{:S(2)}, u32[]{:S(2)}) collective-permute-start(bf16[1,128,256]{2,1,0:T(8,128)(2,1)S(1)} %get-tuple-element.129), channel_id=1, source_target_pairs={{1,2},{2,1},{3,4},{4,3},{5,6},{6,5},{9,10},{10,9},{11,12},{12,11},... | collective-permute-start | bytes 196616 | tf_op jit(solution)/shard_map/ppermute | solution.py:172
  93.6 2.0 %collective-permute-done.18 = bf16[4,128,256]{2,1,0:T(8,128)(2,1)S(1)} collective-permute-done((bf16[4,128,256]{2,1,0:T(8,128)(2,1)S(1)}, bf16[4,128,256]{2,1,0:T(8,128)(2,1)S(1)}, u32[]{:S(2)}, u32[]{:S(2)}) %collective-permute-start.18) | collective-permute-done | bytes 262176 | tf_op jit(solution)/shard_map/ppermute | solution.py:193
  96.8 3.1 %collective-permute-start.21 = (bf16[2,128,256]{2,1,0:T(8,128)(2,1)S(1)}, bf16[2,128,256]{2,1,0:T(8,128)(2,1)S(1)}, u32[]{:S(2)}, u32[]{:S(2)}) collective-permute-start(bf16[2,128,256]{2,1,0:T(8,128)(2,1)S(1)} %get-tuple-element.127), channel_id=1, source_target_pairs={{1,2},{2,1},{3,4},{4,3},{5,6},{6,5},{9,10},{10,9},{11,12},{12,11},... | collective-permute-start | bytes 393224 | tf_op jit(solution)/shard_map/ppermute | solution.py:172
  100.6 1.2 shard_map.64
  101.8 1.3 collective-permute-done.21.q_far
  103.1 2.7 %shard_map.65 = (bf16[1,128,256]{2,1,0:T(8,128)(2,1)S(1)}, bf16[4,128,256]{2,1,0:T(8,128)(2,1)S(1)}, bf16[1,128,256]{2,1,0:T(8,128)(2,1)S(1)}) custom-call(s32[3]{0:T(128)S(1)} %add_convert_fusion.6.flags, bf16[4,128,256]{2,1,0:T(8,128)(2,1)S(1)} %fusion.15.p, bf16[4,128,256]{2,1,0:T(8,128)(2,1)S(1)} %get-tuple-element.98.even, ...), custom_call_target="tpu_custom_call" | custom-call | flops 1 | bytes 1 | tf_op jit(solution)/shard_map/pallas_call | solution.py:115
  105.7 2.9 %collective-permute-start.22 = (bf16[4,128,256]{2,1,0:T(8,128)(2,1)S(1)}, bf16[4,128,256]{2,1,0:T(8,128)(2,1)S(1)}, u32[]{:S(2)}, u32[]{:S(2)}) collective-permute-start(bf16[4,128,256]{2,1,0:T(8,128)(2,1)S(1)} %get-tuple-element.103.first_mid), channel_id=1, source_target_pairs={{8,16},{16,24},{9,17},{17,25},{10,18},{18,26},{11,19},{19,27},{12,... | collective-permute-start | bytes 786440 | tf_op jit(solution)/shard_map/ppermute | solution.py:193
  108.6 2.1 %shard_map.66 = bf16[4,128,256]{2,1,0:T(8,128)(2,1)S(1)} custom-call(bf16[1,128,256]{2,1,0:T(8,128)(2,1)S(1)} %get-tuple-element.104.first_low, bf16[4,128,256]{2,1,0:T(8,128)(2,1)S(1)} %get-tuple-element.103.first_mid, bf16[1,128,256]{2,1,0:T(8,128)(2,1)S(1)} %get-tuple-element.105.first_high, bf16[4,128,256]{2,1,0:T(8,128)(2,1)S(1)} %fusion.14.q, ...), custom_call_target="tpu_custom_call" | custom-call | flops 1 | bytes 1 | tf_op jit(solution)/shard_map/pallas_call | solution.py:115
  110.7 1.9 %collective-permute-start.26 = (bf16[4,128,256]{2,1,0:T(8,128)(2,1)S(1)}, bf16[4,128,256]{2,1,0:T(8,128)(2,1)S(1)}, u32[]{:S(2)}, u32[]{:S(2)}) collective-permute-start(bf16[4,128,256]{2,1,0:T(8,128)(2,1)S(1)} %shard_map.66), channel_id=1, source_target_pairs={{8,16},{16,24},{9,17},{17,25},{10,18},{18,26},{11,19},{19,27},{12,... | collective-permute-start | bytes 786440 | tf_op jit(solution)/shard_map/ppermute | solution.py:193
  113.4 2.7 %collective-permute-done.22 = bf16[4,128,256]{2,1,0:T(8,128)(2,1)S(1)} collective-permute-done((bf16[4,128,256]{2,1,0:T(8,128)(2,1)S(1)}, bf16[4,128,256]{2,1,0:T(8,128)(2,1)S(1)}, u32[]{:S(2)}, u32[]{:S(2)}) %collective-permute-start.22) | collective-permute-done | bytes 262176 | tf_op jit(solution)/shard_map/ppermute | solution.py:193
  116.2 1.9 %collective-permute-start.24 = (bf16[1,128,256]{2,1,0:T(8,128)(2,1)S(1)}, bf16[1,128,256]{2,1,0:T(8,128)(2,1)S(1)}, u32[]{:S(2)}, u32[]{:S(2)}) collective-permute-start(bf16[1,128,256]{2,1,0:T(8,128)(2,1)S(1)} %get-tuple-element.126), channel_id=1, source_target_pairs={{0,1},{1,0},{2,3},{3,2},{4,5},{5,4},{6,7},{7,6},{8,9},{9,8},{10,11... | collective-permute-start | bytes 196616 | tf_op jit(solution)/shard_map/ppermute | solution.py:172
  118.0 2.4 %collective-permute-start.25 = (bf16[1,128,256]{2,1,0:T(8,128)(2,1)S(1)}, bf16[1,128,256]{2,1,0:T(8,128)(2,1)S(1)}, u32[]{:S(2)}, u32[]{:S(2)}) collective-permute-start(bf16[1,128,256]{2,1,0:T(8,128)(2,1)S(1)} %get-tuple-element.125), channel_id=1, source_target_pairs={{1,2},{2,1},{3,4},{4,3},{5,6},{6,5},{9,10},{10,9},{11,12},{12,11},... | collective-permute-start | bytes 196616 | tf_op jit(solution)/shard_map/ppermute | solution.py:172
  120.4 1.5 %collective-permute-done.26 = bf16[4,128,256]{2,1,0:T(8,128)(2,1)S(1)} collective-permute-done((bf16[4,128,256]{2,1,0:T(8,128)(2,1)S(1)}, bf16[4,128,256]{2,1,0:T(8,128)(2,1)S(1)}, u32[]{:S(2)}, u32[]{:S(2)}) %collective-permute-start.26) | collective-permute-done | bytes 262176 | tf_op jit(solution)/shard_map/ppermute | solution.py:193
  121.9 1.7 %collective-permute-done.25.p_far = bf16[1,128,256]{2,1,0:T(8,128)(2,1)S(1)} collective-permute-done((bf16[1,128,256]{2,1,0:T(8,128)(2,1)S(1)}, bf16[1,128,256]{2,1,0:T(8,128)(2,1)S(1)}, u32[]{:S(2)}, u32[]{:S(2)}) %collective-permute-start.25) | collective-permute-done | bytes 65568 | tf_op jit(solution)/shard_map/ppermute | solution.py:172
  123.8 3.0 %collective-permute-start.29 = (bf16[2,128,256]{2,1,0:T(8,128)(2,1)S(1)}, bf16[2,128,256]{2,1,0:T(8,128)(2,1)S(1)}, u32[]{:S(2)}, u32[]{:S(2)}) collective-permute-start(bf16[2,128,256]{2,1,0:T(8,128)(2,1)S(1)} %get-tuple-element.123), channel_id=1, source_target_pairs={{1,2},{2,1},{3,4},{4,3},{5,6},{6,5},{9,10},{10,9},{11,12},{12,11},... | collective-permute-start | bytes 393224 | tf_op jit(solution)/shard_map/ppermute | solution.py:172
  126.9 1.2 shard_map.67
  128.1 2.1 %collective-permute-done.29.q_far = bf16[2,128,256]{2,1,0:T(8,128)(2,1)S(1)} collective-permute-done((bf16[2,128,256]{2,1,0:T(8,128)(2,1)S(1)}, bf16[2,128,256]{2,1,0:T(8,128)(2,1)S(1)}, u32[]{:S(2)}, u32[]{:S(2)}) %collective-permute-start.29) | collective-permute-done | bytes 131104 | tf_op jit(solution)/shard_map/ppermute | solution.py:172
  130.2 2.7 %shard_map.68 = (bf16[1,128,256]{2,1,0:T(8,128)(2,1)S(1)}, bf16[4,128,256]{2,1,0:T(8,128)(2,1)S(1)}, bf16[1,128,256]{2,1,0:T(8,128)(2,1)S(1)}) custom-call(s32[3]{0:T(128)S(1)} %add_convert_fusion.6.flags, bf16[4,128,256]{2,1,0:T(8,128)(2,1)S(1)} %fusion.13.p, bf16[4,128,256]{2,1,0:T(8,128)(2,1)S(1)} %get-tuple-element.109.even, ...), custom_call_target="tpu_custom_call" | custom-call | flops 1 | bytes 1 | tf_op jit(solution)/shard_map/pallas_call | solution.py:115
  132.9 2.9 %shard_map.69 = bf16[2,4,128,256]{3,2,1,0:T(8,128)(2,1)} custom-call(bf16[1,128,256]{2,1,0:T(8,128)(2,1)S(1)} %get-tuple-element.114.first_low, bf16[4,128,256]{2,1,0:T(8,128)(2,1)S(1)} %get-tuple-element.115.first_mid, bf16[1,128,256]{2,1,0:T(8,128)(2,1)S(1)} %get-tuple-element.116.first_high, bf16[4,128,256]{2,1,0:T(8,128)(2,1)S(1)} %fusion.12.q, ...), custom_call_target="tpu_custom_call" | custom-call | flops 1 | bytes 1 | tf_op jit(solution)/shard_map/pallas_call | solution.py:115
  (100 shorter events, 19.2 us)
Async XLA Ops:
  0.0 20.2 %collective-permute-start.2 = (bf16[2,4,128,256]{3,2,1,0:T(8,128)(2,1)}, bf16[2,4,128,256]{3,2,1,0:T(8,128)(2,1)}, u32[]{:S(2)}, u32[]{:S(2)}) collective-permute-start(bf16[2,4,128,256]{3,2,1,0:T(8,128)(2,1)} %bitcast.75), channel_id=1, source_target_pairs={{0,24},{8,16},{1,25},{9,17},{2,26},{10,18},{3,27},{11,19},{4,28},{... | collective-permute-start | bytes 1572872 | tf_op jit(solution)/shard_map/ppermute | solution.py:193
  2.4 5.4 %copy-start.3 = (bf16[4,128,256]{2,1,0:T(8,128)(2,1)}, bf16[4,128,256]{2,1,0:T(8,128)(2,1)S(1)}, u32[]{:S(2)}) copy-start(bf16[4,128,256]{2,1,0:T(8,128)(2,1)S(1)} %get-tuple-element.121.q) | copy-start | bytes 786436
  2.4 5.4 %copy-start.7 = (bf16[4,128,256]{2,1,0:T(8,128)(2,1)}, bf16[4,128,256]{2,1,0:T(8,128)(2,1)S(1)}, u32[]{:S(2)}) copy-start(bf16[4,128,256]{2,1,0:T(8,128)(2,1)S(1)} %get-tuple-element.122.p) | copy-start | bytes 786436
  3.3 9.8 %collective-permute-start = (bf16[3,128,256]{2,1,0:T(8,128)(2,1)}, bf16[3,128,256]{2,1,0:T(8,128)(2,1)}, u32[]{:S(2)}, u32[]{:S(2)}) collective-permute-start(bf16[3,128,256]{2,1,0:T(8,128)(2,1)} %pad_maximum_fusion.1), channel_id=1, source_target_pairs={{0,1},{1,0},{2,3},{3,2},{4,5},{5,4},{6,7},{7,6},{8,9},{9,8},{10,11... | collective-permute-start | bytes 589832 | tf_op jit(solution)/shard_map/ppermute | solution.py:172
  4.7 8.4 %collective-permute-start.1 = (bf16[3,128,256]{2,1,0:T(8,128)(2,1)}, bf16[3,128,256]{2,1,0:T(8,128)(2,1)}, u32[]{:S(2)}, u32[]{:S(2)}) collective-permute-start(bf16[3,128,256]{2,1,0:T(8,128)(2,1)} %pad_maximum_fusion.2), channel_id=1, source_target_pairs={{1,2},{2,1},{3,4},{4,3},{5,6},{6,5},{9,10},{10,9},{11,12},{12,11},... | collective-permute-start | bytes 589832 | tf_op jit(solution)/shard_map/ppermute | solution.py:172
  13.0 1.0 copy-start.8
  14.0 1.0 copy-start.10
  15.0 0.9 copy-start.12
  15.9 0.9 copy-start.14
  16.8 3.4 %copy-start.22 = (bf16[1,2,4,16,8,256]{5,4,3,2,1,0:T(8,128)(2,1)S(1)}, bf16[1,2,4,16,8,256]{5,4,3,2,1,0:T(8,128)(2,1)}, u32[]{:S(2)}) copy-start(bf16[1,2,4,16,8,256]{5,4,3,2,1,0:T(8,128)(2,1)} %param.5) | copy-start | bytes 1572868
  16.8 7.7 %copy-start.4 = (bf16[4,128,256]{2,1,0:T(8,128)(2,1)S(1)}, bf16[4,128,256]{2,1,0:T(8,128)(2,1)}, u32[]{:S(2)}) copy-start(bf16[4,128,256]{2,1,0:T(8,128)(2,1)} %copy-done.3) | copy-start | bytes 786436
  20.3 4.3 %copy-start = (bf16[1,3,3,3,256,256]{5,4,3,2,1,0:T(8,128)(2,1)S(1)}, bf16[1,3,3,3,256,256]{5,4,3,2,1,0:T(8,128)(2,1)}, u32[]{:S(2)}) copy-start(bf16[1,3,3,3,256,256]{5,4,3,2,1,0:T(8,128)(2,1)} %param.9) | copy-start | bytes 10616836
  21.8 7.9 %copy-start.5 = (bf16[4,128,256]{2,1,0:T(8,128)(2,1)}, bf16[4,128,256]{2,1,0:T(8,128)(2,1)S(1)}, u32[]{:S(2)}) copy-start(bf16[4,128,256]{2,1,0:T(8,128)(2,1)S(1)} %get-tuple-element.74.q) | copy-start | bytes 786436
  21.9 7.0 %collective-permute-start.4 = (bf16[3,128,256]{2,1,0:T(8,128)(2,1)S(1)}, bf16[3,128,256]{2,1,0:T(8,128)(2,1)S(1)}, u32[]{:S(2)}, u32[]{:S(2)}) collective-permute-start(bf16[3,128,256]{2,1,0:T(8,128)(2,1)S(1)} %pad_maximum_fusion.4), channel_id=1, source_target_pairs={{1,2},{2,1},{3,4},{4,3},{5,6},{6,5},{9,10},{10,9},{11,12},{12,11},... | collective-permute-start | bytes 589832 | tf_op jit(solution)/shard_map/ppermute | solution.py:172
  24.5 4.5 %collective-permute-start.3 = (bf16[3,128,256]{2,1,0:T(8,128)(2,1)S(1)}, bf16[3,128,256]{2,1,0:T(8,128)(2,1)S(1)}, u32[]{:S(2)}, u32[]{:S(2)}) collective-permute-start(bf16[3,128,256]{2,1,0:T(8,128)(2,1)S(1)} %pad_maximum_fusion.3), channel_id=1, source_target_pairs={{0,1},{1,0},{2,3},{3,2},{4,5},{5,4},{6,7},{7,6},{8,9},{9,8},{10,11... | collective-permute-start | bytes 589832 | tf_op jit(solution)/shard_map/ppermute | solution.py:172
  29.0 9.6 %collective-permute-start.5 = (bf16[2,4,128,256]{3,2,1,0:T(8,128)(2,1)S(1)}, bf16[2,4,128,256]{3,2,1,0:T(8,128)(2,1)S(1)}, u32[]{:S(2)}, u32[]{:S(2)}) collective-permute-start(bf16[2,4,128,256]{3,2,1,0:T(8,128)(2,1)S(1)} %pad_maximum_fusion), channel_id=1, source_target_pairs={{0,8},{1,9},{2,10},{3,11},{4,12},{5,13},{6,14},{7,15}} | collective-permute-start | bytes 1572872 | tf_op jit(solution)/shard_map/ppermute | solution.py:193
  35.5 16.6 %collective-permute-start.6 = (bf16[4,128,256]{2,1,0:T(8,128)(2,1)}, bf16[4,128,256]{2,1,0:T(8,128)(2,1)}, u32[]{:S(2)}, u32[]{:S(2)}) collective-permute-start(bf16[4,128,256]{2,1,0:T(8,128)(2,1)} %get-tuple-element.80.first_mid), channel_id=1, source_target_pairs={{0,8},{8,16},{16,24},{1,9},{9,17},{17,25},{2,10},{10,18},{18,26},{... | collective-permute-start | bytes 786440 | tf_op jit(solution)/shard_map/ppermute | solution.py:193
  40.3 11.8 %collective-permute-start.7 = (bf16[4,128,256]{2,1,0:T(8,128)(2,1)}, bf16[4,128,256]{2,1,0:T(8,128)(2,1)}, u32[]{:S(2)}, u32[]{:S(2)}) collective-permute-start(bf16[4,128,256]{2,1,0:T(8,128)(2,1)} %get-tuple-element.81), channel_id=1, source_target_pairs={{8,24},{9,25},{10,26},{11,27},{12,28},{13,29},{14,30},{15,31}} | collective-permute-start | bytes 786440 | tf_op jit(solution)/shard_map/ppermute | solution.py:193
  41.6 2.0 %copy-start.1 = (bf16[1,3,3,3,256,256]{5,4,3,2,1,0:T(8,128)(2,1)S(1)}, bf16[1,3,3,3,256,256]{5,4,3,2,1,0:T(8,128)(2,1)}, u32[]{:S(2)}) copy-start(bf16[1,3,3,3,256,256]{5,4,3,2,1,0:T(8,128)(2,1)} %param.9) | copy-start | bytes 10616836
  43.6 0.9 copy-start.6
  44.6 0.8 copy-start.16
  45.4 0.8 copy-start.18
  46.2 5.1 %copy-start.23 = (bf16[4,128,256]{2,1,0:T(8,128)(2,1)S(1)}, bf16[4,128,256]{2,1,0:T(8,128)(2,1)}, u32[]{:S(2)}) copy-start(bf16[4,128,256]{2,1,0:T(8,128)(2,1)} %get-tuple-element.86) | copy-start | bytes 786436
  46.2 5.9 %copy-start.19 = (bf16[3,2,4,16,8,256]{5,4,3,2,1,0:T(8,128)(2,1)S(1)}, bf16[3,2,4,16,8,256]{5,4,3,2,1,0:T(8,128)(2,1)}, u32[]{:S(2)}) copy-start(bf16[3,2,4,16,8,256]{5,4,3,2,1,0:T(8,128)(2,1)} %param.7) | copy-start | bytes 4718596
  46.2 5.9 %copy-start.21 = (bf16[2,4,128,256]{3,2,1,0:T(8,128)(2,1)S(1)}, bf16[2,4,128,256]{3,2,1,0:T(8,128)(2,1)}, u32[]{:S(2)}) copy-start(bf16[2,4,128,256]{3,2,1,0:T(8,128)(2,1)} %copy-done.20) | copy-start | bytes 1572868
  49.4 19.6 %collective-permute-start.10 = (bf16[4,128,256]{2,1,0:T(8,128)(2,1)S(1)}, bf16[4,128,256]{2,1,0:T(8,128)(2,1)S(1)}, u32[]{:S(2)}, u32[]{:S(2)}) collective-permute-start(bf16[4,128,256]{2,1,0:T(8,128)(2,1)S(1)} %shard_map.60), channel_id=1, source_target_pairs={{0,8},{8,16},{16,24},{1,9},{9,17},{17,25},{2,10},{10,18},{18,26},{... | collective-permute-start | bytes 786440 | tf_op jit(solution)/shard_map/ppermute | solution.py:193
  51.4 17.7 %collective-permute-start.11 = (bf16[4,128,256]{2,1,0:T(8,128)(2,1)S(1)}, bf16[4,128,256]{2,1,0:T(8,128)(2,1)S(1)}, u32[]{:S(2)}, u32[]{:S(2)}) collective-permute-start(bf16[4,128,256]{2,1,0:T(8,128)(2,1)S(1)} %copy-done.23), channel_id=1, source_target_pairs={{8,24},{9,25},{10,26},{11,27},{12,28},{13,29},{14,30},{15,31}} | collective-permute-start | bytes 786440 | tf_op jit(solution)/shard_map/ppermute | solution.py:193
  53.2 15.9 %collective-permute-start.8 = (bf16[1,128,256]{2,1,0:T(8,128)(2,1)S(1)}, bf16[1,128,256]{2,1,0:T(8,128)(2,1)S(1)}, u32[]{:S(2)}, u32[]{:S(2)}) collective-permute-start(bf16[1,128,256]{2,1,0:T(8,128)(2,1)S(1)} %get-tuple-element.134), channel_id=1, source_target_pairs={{0,1},{1,0},{2,3},{3,2},{4,5},{5,4},{6,7},{7,6},{8,9},{9,8},{10,11... | collective-permute-start | bytes 196616 | tf_op jit(solution)/shard_map/ppermute | solution.py:172
  53.3 15.8 %collective-permute-start.9 = (bf16[1,128,256]{2,1,0:T(8,128)(2,1)S(1)}, bf16[1,128,256]{2,1,0:T(8,128)(2,1)S(1)}, u32[]{:S(2)}, u32[]{:S(2)}) collective-permute-start(bf16[1,128,256]{2,1,0:T(8,128)(2,1)S(1)} %get-tuple-element.133), channel_id=1, source_target_pairs={{1,2},{2,1},{3,4},{4,3},{5,6},{6,5},{9,10},{10,9},{11,12},{12,11},... | collective-permute-start | bytes 196616 | tf_op jit(solution)/shard_map/ppermute | solution.py:172
  69.2 5.8 %collective-permute-start.12 = (bf16[2,128,256]{2,1,0:T(8,128)(2,1)S(1)}, bf16[2,128,256]{2,1,0:T(8,128)(2,1)S(1)}, u32[]{:S(2)}, u32[]{:S(2)}) collective-permute-start(bf16[2,128,256]{2,1,0:T(8,128)(2,1)S(1)} %get-tuple-element.132), channel_id=1, source_target_pairs={{0,1},{1,0},{2,3},{3,2},{4,5},{5,4},{6,7},{7,6},{8,9},{9,8},{10,11... | collective-permute-start | bytes 393224 | tf_op jit(solution)/shard_map/ppermute | solution.py:172
  69.8 6.3 %collective-permute-start.13 = (bf16[2,128,256]{2,1,0:T(8,128)(2,1)S(1)}, bf16[2,128,256]{2,1,0:T(8,128)(2,1)S(1)}, u32[]{:S(2)}, u32[]{:S(2)}) collective-permute-start(bf16[2,128,256]{2,1,0:T(8,128)(2,1)S(1)} %get-tuple-element.131), channel_id=1, source_target_pairs={{1,2},{2,1},{3,4},{4,3},{5,6},{6,5},{9,10},{10,9},{11,12},{12,11},... | collective-permute-start | bytes 393224 | tf_op jit(solution)/shard_map/ppermute | solution.py:172
  72.9 14.1 %collective-permute-start.15 = (bf16[4,128,256]{2,1,0:T(8,128)(2,1)}, bf16[4,128,256]{2,1,0:T(8,128)(2,1)S(1)}, u32[]{:S(2)}, u32[]{:S(2)}) collective-permute-start(bf16[4,128,256]{2,1,0:T(8,128)(2,1)} %collective-permute-done.6), channel_id=1, source_target_pairs={{8,24},{9,25},{10,26},{11,27},{12,28},{13,29},{14,30},{15,31}} | collective-permute-start | bytes 786440 | tf_op jit(solution)/shard_map/ppermute | solution.py:193
  76.1 6.2 %copy-start.2 = (bf16[1,3,3,3,256,256]{5,4,3,2,1,0:T(8,128)(2,1)S(1)}, bf16[1,3,3,3,256,256]{5,4,3,2,1,0:T(8,128)(2,1)}, u32[]{:S(2)}) copy-start(bf16[1,3,3,3,256,256]{5,4,3,2,1,0:T(8,128)(2,1)} %param.9) | copy-start | bytes 10616836
  78.8 11.5 %collective-permute-start.14 = (bf16[4,128,256]{2,1,0:T(8,128)(2,1)S(1)}, bf16[4,128,256]{2,1,0:T(8,128)(2,1)S(1)}, u32[]{:S(2)}, u32[]{:S(2)}) collective-permute-start(bf16[4,128,256]{2,1,0:T(8,128)(2,1)S(1)} %get-tuple-element.92.first_mid), channel_id=1, source_target_pairs={{0,8},{8,16},{16,24},{1,9},{9,17},{17,25},{2,10},{10,18},{18,26},{... | collective-permute-start | bytes 786440 | tf_op jit(solution)/shard_map/ppermute | solution.py:193
  84.4 11.2 %collective-permute-start.18 = (bf16[4,128,256]{2,1,0:T(8,128)(2,1)S(1)}, bf16[4,128,256]{2,1,0:T(8,128)(2,1)S(1)}, u32[]{:S(2)}, u32[]{:S(2)}) collective-permute-start(bf16[4,128,256]{2,1,0:T(8,128)(2,1)S(1)} %shard_map.63), channel_id=1, source_target_pairs={{0,8},{8,16},{16,24},{1,9},{9,17},{17,25},{2,10},{10,18},{18,26},{... | collective-permute-start | bytes 786440 | tf_op jit(solution)/shard_map/ppermute | solution.py:193
  86.4 10.1 %collective-permute-start.19 = (bf16[4,128,256]{2,1,0:T(8,128)(2,1)S(1)}, bf16[4,128,256]{2,1,0:T(8,128)(2,1)S(1)}, u32[]{:S(2)}, u32[]{:S(2)}) collective-permute-start(bf16[4,128,256]{2,1,0:T(8,128)(2,1)S(1)} %collective-permute-done.10), channel_id=1, source_target_pairs={{8,24},{9,25},{10,26},{11,27},{12,28},{13,29},{14,30},{15,31}} | collective-permute-start | bytes 786440 | tf_op jit(solution)/shard_map/ppermute | solution.py:193
  90.4 5.2 %collective-permute-start.16 = (bf16[1,128,256]{2,1,0:T(8,128)(2,1)S(1)}, bf16[1,128,256]{2,1,0:T(8,128)(2,1)S(1)}, u32[]{:S(2)}, u32[]{:S(2)}) collective-permute-start(bf16[1,128,256]{2,1,0:T(8,128)(2,1)S(1)} %get-tuple-element.130), channel_id=1, source_target_pairs={{0,1},{1,0},{2,3},{3,2},{4,5},{5,4},{6,7},{7,6},{8,9},{9,8},{10,11... | collective-permute-start | bytes 196616 | tf_op jit(solution)/shard_map/ppermute | solution.py:172
  90.9 5.6 %collective-permute-start.17 = (bf16[1,128,256]{2,1,0:T(8,128)(2,1)S(1)}, bf16[1,128,256]{2,1,0:T(8,128)(2,1)S(1)}, u32[]{:S(2)}, u32[]{:S(2)}) collective-permute-start(bf16[1,128,256]{2,1,0:T(8,128)(2,1)S(1)} %get-tuple-element.129), channel_id=1, source_target_pairs={{1,2},{2,1},{3,4},{4,3},{5,6},{6,5},{9,10},{10,9},{11,12},{12,11},... | collective-permute-start | bytes 196616 | tf_op jit(solution)/shard_map/ppermute | solution.py:172
  96.6 5.2 %collective-permute-start.20 = (bf16[2,128,256]{2,1,0:T(8,128)(2,1)S(1)}, bf16[2,128,256]{2,1,0:T(8,128)(2,1)S(1)}, u32[]{:S(2)}, u32[]{:S(2)}) collective-permute-start(bf16[2,128,256]{2,1,0:T(8,128)(2,1)S(1)} %get-tuple-element.128), channel_id=1, source_target_pairs={{0,1},{1,0},{2,3},{3,2},{4,5},{5,4},{6,7},{7,6},{8,9},{9,8},{10,11... | collective-permute-start | bytes 393224 | tf_op jit(solution)/shard_map/ppermute | solution.py:172
  96.8 6.3 %collective-permute-start.21 = (bf16[2,128,256]{2,1,0:T(8,128)(2,1)S(1)}, bf16[2,128,256]{2,1,0:T(8,128)(2,1)S(1)}, u32[]{:S(2)}, u32[]{:S(2)}) collective-permute-start(bf16[2,128,256]{2,1,0:T(8,128)(2,1)S(1)} %get-tuple-element.127), channel_id=1, source_target_pairs={{1,2},{2,1},{3,4},{4,3},{5,6},{6,5},{9,10},{10,9},{11,12},{12,11},... | collective-permute-start | bytes 393224 | tf_op jit(solution)/shard_map/ppermute | solution.py:172
  99.9 13.5 %collective-permute-start.23 = (bf16[4,128,256]{2,1,0:T(8,128)(2,1)S(1)}, bf16[4,128,256]{2,1,0:T(8,128)(2,1)S(1)}, u32[]{:S(2)}, u32[]{:S(2)}) collective-permute-start(bf16[4,128,256]{2,1,0:T(8,128)(2,1)S(1)} %collective-permute-done.14), channel_id=1, source_target_pairs={{8,24},{9,25},{10,26},{11,27},{12,28},{13,29},{14,30},{15,31}} | collective-permute-start | bytes 786440 | tf_op jit(solution)/shard_map/ppermute | solution.py:193
  105.7 10.3 %collective-permute-start.22 = (bf16[4,128,256]{2,1,0:T(8,128)(2,1)S(1)}, bf16[4,128,256]{2,1,0:T(8,128)(2,1)S(1)}, u32[]{:S(2)}, u32[]{:S(2)}) collective-permute-start(bf16[4,128,256]{2,1,0:T(8,128)(2,1)S(1)} %get-tuple-element.103.first_mid), channel_id=1, source_target_pairs={{8,16},{16,24},{9,17},{17,25},{10,18},{18,26},{11,19},{19,27},{12,... | collective-permute-start | bytes 786440 | tf_op jit(solution)/shard_map/ppermute | solution.py:193
  110.7 11.2 %collective-permute-start.26 = (bf16[4,128,256]{2,1,0:T(8,128)(2,1)S(1)}, bf16[4,128,256]{2,1,0:T(8,128)(2,1)S(1)}, u32[]{:S(2)}, u32[]{:S(2)}) collective-permute-start(bf16[4,128,256]{2,1,0:T(8,128)(2,1)S(1)} %shard_map.66), channel_id=1, source_target_pairs={{8,16},{16,24},{9,17},{17,25},{10,18},{18,26},{11,19},{19,27},{12,... | collective-permute-start | bytes 786440 | tf_op jit(solution)/shard_map/ppermute | solution.py:193
  112.7 10.9 %collective-permute-start.27 = (bf16[4,128,256]{2,1,0:T(8,128)(2,1)S(1)}, bf16[4,128,256]{2,1,0:T(8,128)(2,1)S(1)}, u32[]{:S(2)}, u32[]{:S(2)}) collective-permute-start(bf16[4,128,256]{2,1,0:T(8,128)(2,1)S(1)} %collective-permute-done.18), channel_id=1, source_target_pairs={{8,24},{9,25},{10,26},{11,27},{12,28},{13,29},{14,30},{15,31}} | collective-permute-start | bytes 786440 | tf_op jit(solution)/shard_map/ppermute | solution.py:193
  116.2 5.8 %collective-permute-start.24 = (bf16[1,128,256]{2,1,0:T(8,128)(2,1)S(1)}, bf16[1,128,256]{2,1,0:T(8,128)(2,1)S(1)}, u32[]{:S(2)}, u32[]{:S(2)}) collective-permute-start(bf16[1,128,256]{2,1,0:T(8,128)(2,1)S(1)} %get-tuple-element.126), channel_id=1, source_target_pairs={{0,1},{1,0},{2,3},{3,2},{4,5},{5,4},{6,7},{7,6},{8,9},{9,8},{10,11... | collective-permute-start | bytes 196616 | tf_op jit(solution)/shard_map/ppermute | solution.py:172
  118.0 5.6 %collective-permute-start.25 = (bf16[1,128,256]{2,1,0:T(8,128)(2,1)S(1)}, bf16[1,128,256]{2,1,0:T(8,128)(2,1)S(1)}, u32[]{:S(2)}, u32[]{:S(2)}) collective-permute-start(bf16[1,128,256]{2,1,0:T(8,128)(2,1)S(1)} %get-tuple-element.125), channel_id=1, source_target_pairs={{1,2},{2,1},{3,4},{4,3},{5,6},{6,5},{9,10},{10,9},{11,12},{12,11},... | collective-permute-start | bytes 196616 | tf_op jit(solution)/shard_map/ppermute | solution.py:172
  123.7 4.4 %collective-permute-start.28 = (bf16[2,128,256]{2,1,0:T(8,128)(2,1)S(1)}, bf16[2,128,256]{2,1,0:T(8,128)(2,1)S(1)}, u32[]{:S(2)}, u32[]{:S(2)}) collective-permute-start(bf16[2,128,256]{2,1,0:T(8,128)(2,1)S(1)} %get-tuple-element.124), channel_id=1, source_target_pairs={{0,1},{1,0},{2,3},{3,2},{4,5},{5,4},{6,7},{7,6},{8,9},{9,8},{10,11... | collective-permute-start | bytes 393224 | tf_op jit(solution)/shard_map/ppermute | solution.py:172
  123.8 6.4 %collective-permute-start.29 = (bf16[2,128,256]{2,1,0:T(8,128)(2,1)S(1)}, bf16[2,128,256]{2,1,0:T(8,128)(2,1)S(1)}, u32[]{:S(2)}, u32[]{:S(2)}) collective-permute-start(bf16[2,128,256]{2,1,0:T(8,128)(2,1)S(1)} %get-tuple-element.123), channel_id=1, source_target_pairs={{1,2},{2,1},{3,4},{4,3},{5,6},{6,5},{9,10},{10,9},{11,12},{12,11},... | collective-permute-start | bytes 393224 | tf_op jit(solution)/shard_map/ppermute | solution.py:172
  (6 other events, 4.1 us)

commit v6 on v5

--- a/solution.py
+++ b/solution.py
@@ -159,19 +159,17 @@
     return out
 
 
-def boundary(block, upward, width):
-    return lax.dynamic_slice_in_dim(block, jnp.where(upward, block.shape[0] - width, 0), width, axis=0)
-
-
-def swapped(blocks, widths, above):
+def swapped(blocks, widths, starts):
     count = lax.axis_size("depth")
 
-    def swap(upward, base):
-        part = jnp.concatenate([boundary(block, upward, width) for block, width in zip(blocks, widths)], axis=0)
-        pairs = [pair for i in range(base, count - 1, 2) for pair in ((i, i + 1), (i + 1, i))]
-        return lax.ppermute(part, "depth", pairs)
-
-    return swap(above, 0), swap(jnp.logical_not(above), 1)
+    def swap(turn):
+        parts = [
+            lax.dynamic_slice_in_dim(block, starts[width][turn], width, axis=0) for block, width in zip(blocks, widths)
+        ]
+        pairs = [pair for i in range(turn, count - 1, 2) for pair in ((i, i + 1), (i + 1, i))]
+        return lax.ppermute(jnp.concatenate(parts, axis=0), "depth", pairs)
+
+    return swap(0), swap(1)
 
 
 def local(resident, previous, incoming, first_weights, second_weights):
@@ -182,48 +180,62 @@
     ticks = incoming.shape[0] + 1
     _, _, planes, rows, width, chans = resident.shape
     voxels = rows * width
+    across = [(j, sections - 1 - j) for j in range(1, half - 1)]
+
+    above = depth % 2 == 0
+    places = {
+        "flags": jnp.stack([depth > 0, depth < lax.axis_size("depth") - 1, above]).astype(jnp.int32),
+        "starts": {
+            n: (jnp.where(above, planes - n, 0), jnp.where(above, 0, planes - n)) for n in (1, 2)
+        },
+        "first": section == 0,
+        "second": section == 1,
+        "last": section == sections - 1,
+        "decoder": section >= half,
+        "direct": (section > half) & (section < sections - 1) if across else (),
+    }
+    places, resident, previous, incoming, first_weights, second_weights = lax.optimization_barrier(
+        (places, resident, previous, incoming, first_weights, second_weights)
+    )
+    flags, starts = places["flags"], places["starts"]
+
     flat = lambda a: a.reshape(a.shape[0], 2, planes, voxels, chans)
     resident, previous, incoming = flat(resident)[0], flat(previous)[0], flat(incoming)
     w_one = first_weights.reshape(27 * chans, chans)
     w_two = second_weights.reshape(27 * chans, chans)
-    above = depth % 2 == 0
-    flags = jnp.stack([depth > 0, depth < lax.axis_size("depth") - 1, above]).astype(jnp.int32)
 
     def send(block, pairs):
         return lax.ppermute(block, "section", pairs) if pairs else block
 
-    across = [(j, sections - 1 - j) for j in range(1, half - 1)]
-    decoder = section >= half
-
     def join(held, skip):
         total = (held.astype(jnp.float32) + skip.astype(jnp.float32)).astype(jnp.bfloat16)
-        return jnp.where(decoder, total, held)
+        return jnp.where(places["decoder"], total, held)
 
     newer, older, relayed, direct = {}, {}, {}, {}
 
     def arrived(slot, stream):
         fresh = incoming[min(slot, ticks - 1) - 1, stream]
         if slot == 1:
-            return jnp.where(section == 0, fresh, join(resident[stream], mirrored[stream]))
-        held = jnp.where(section == 1, older[stream], newer[stream])
-        skip = jnp.where(section == sections - 1, relayed[stream], newer[stream])
+            return jnp.where(places["first"], fresh, join(resident[stream], mirrored[stream]))
+        held = jnp.where(places["second"], older[stream], newer[stream])
+        skip = jnp.where(places["last"], relayed[stream], newer[stream])
         if across:
-            skip = jnp.where((section > half) & (section < sections - 1), direct[stream], skip)
-        return jnp.where(section == 0, fresh, join(held, skip))
+            skip = jnp.where(places["direct"], direct[stream], skip)
+        return jnp.where(places["first"], fresh, join(held, skip))
 
     p, q = resident
     mirrored = send(previous, [(j, sections - 1 - j) for j in range(half)])
-    q_halos = p_halos = swapped((q, p), (2, 1), above)
+    q_halos = p_halos = swapped((q, p), (2, 1), starts)
     for slot in range(ticks + 1):
         if slot == 1:
             p, q, q_halos = following
             p_halos = q_halos
         elif slot > 1:
             p = arrived(slot, 0)
-            p_halos = swapped((p,), (1,), above)
+            p_halos = swapped((p,), (1,), starts)
             p, p_halos, newer[1] = lax.optimization_barrier((p, p_halos, newer[1]))
             q = arrived(slot, 1)
-            q_halos = swapped((q,), (2,), above)
+            q_halos = swapped((q,), (2,), starts)
         *kept, w_one = inner_half(p, q, w_one, width, slot == 0)
         first = first_half(flags, p, kept, q_halos, p_halos, w_one, width)
         onward = [(j, j + 1) for j in range(1, sections - 1)]
@@ -233,7 +245,7 @@
         if slot == 0:
             mirrored, _ = lax.optimization_barrier((mirrored, first[1]))
             following = arrived(1, 0), arrived(1, 1)
-            following = *following, swapped(following[::-1], (2, 1), above)
+            following = *following, swapped(following[::-1], (2, 1), starts)
             first, joined = lax.optimization_barrier((first, following[:2]))
             following = *joined, following[2]
         elif slot < ticks:
@@ -247,7 +259,7 @@
             received[1] = send(second, onward)
             relay_p, relay_q = newer[0], newer[1]
             if slot == 1:
-                relay_p, _ = lax.optimization_barrier((relay_p, first[1]))
+                relay_p, second = lax.optimization_barrier((relay_p, second))
             relay_q, second = lax.optimization_barrier((relay_q, second))
             relays = {0: send(relay_p, [(1, sections - 1)]), 1: send(relay_q, [(1, sections - 1)])}
             if across:

time: 137 us -> 120 us (0.88)
  local copies, waits for them, and re-layouts: 14.6 us -> 1.34 us
  starting transfers between devices: 49.5 us -> 59.4 us
  waiting for transfers between devices: 30.9 us -> 24.7 us
  other arithmetic: 4.9 us -> 1.06 us
  Pallas kernels: 35.2 us -> 32.7 us
    unnamed x48 -> x6, local copies, waits for them, and re-layouts: 12.5 us -> 0.01 us
    ppermute x14, waiting for transfers between devices: 21.7 us -> 15.5 us  [send(): return lax.ppermute(block, 'section', pairs) if pairs else block]
    ppermute x16, starting transfers between devices: 27.5 us -> 32.5 us  [swap(): return lax.ppermute(jnp.concatenate(parts, axis=0), 'depth', pairs)]
    ppermute x14, starting transfers between devices: 22.1 us -> 26.9 us  [send(): return lax.ppermute(block, 'section', pairs) if pairs else block]
    pallas_call x15, Pallas kernels: 35.2 us -> 32.7 us  [call(): pl.pallas_call(functools.partial(kernel, width), out_shape=shapes, in_spe...]
    select_n x7, other arithmetic: 3.19 us -> 0.86 us  [the longest x6 0.62 us: arrived(): return jnp.where(places['first'], fresh, join(held, skip))]
    concatenate x4, other arithmetic: 1.58 us -> 0.08 us  [swap(): return lax.ppermute(jnp.concatenate(parts, axis=0), 'depth', pairs)]
  transfers between devices with their start and end apart: 30 -> 30, of which waited for: 11 -> 14; matrix products, arithmetic and copies ran while one was open for 4% -> 1% of each run, Pallas kernels for 22% -> 23%
where the time goes in v6:
time: 120 us
  starting transfers between devices  59.4 us (50%)
  Pallas kernels  32.7 us (27%)
  waiting for transfers between devices  24.7 us (21%)
  local copies, waits for them, and re-layouts  1.34 us (1%)
    pallas_call x15, Pallas kernels, call(): pl.pallas_call(functools.partial(kernel, width), out_shape=shapes, in_spe...  32.7 us
    ppermute x16, starting transfers between devices, swap(): return lax.ppermute(jnp.concatenate(parts, axis=0), 'depth', pairs)  32.5 us
    ppermute x14, starting transfers between devices, send(): return lax.ppermute(block, 'section', pairs) if pairs else block  26.9 us
    ppermute x14, waiting for transfers between devices, send(): return lax.ppermute(block, 'section', pairs) if pairs else block  15.5 us
    ppermute x16, waiting for transfers between devices, swap(): return lax.ppermute(jnp.concatenate(parts, axis=0), 'depth', pairs)  9.14 us
  transfers between devices with their start and end apart: 30, of which 14 were waited for; matrix products, arithmetic and copies ran while one was open for 1% of the time, Pallas kernels for 23%

profile of v6, /device:TPU:13, one launch (start us, length us, event | category | flops | bytes accessed | tf_op | source)
XLA Modules:
  0.0 119.8 jit_solution(3334260484766823193)
XLA Ops:
  0.1 1.3 %collective-permute-start.2 = (bf16[2,4,128,256]{3,2,1,0:T(8,128)(2,1)}, bf16[2,4,128,256]{3,2,1,0:T(8,128)(2,1)S(1)}, u32[]{:S(2)}, u32[]{:S(2)}) collective-permute-start(bf16[2,4,128,256]{3,2,1,0:T(8,128)(2,1)} %bitcast.75), channel_id=1, source_target_pairs={{0,24},{8,16},{1,25},{9,17},{2,26},{10,18},{3,27},{11,19},{4,28},{... | collective-permute-start | bytes 1572872 | tf_op jit(solution)/shard_map/ppermute | solution.py:208
  1.4 1.1 slice_bitcast_fusion.8
  3.3 3.1 %collective-permute-start.1 = (bf16[3,128,256]{2,1,0:T(8,128)(2,1)S(1)}, bf16[3,128,256]{2,1,0:T(8,128)(2,1)S(1)}, u32[]{:S(2)}, u32[]{:S(2)}) collective-permute-start(bf16[3,128,256]{2,1,0:T(8,128)(2,1)S(1)} %pad_maximum_fusion.2), channel_id=1, source_target_pairs={{1,2},{2,1},{3,4},{4,3},{5,6},{6,5},{9,10},{10,9},{11,12},{12,11},... | collective-permute-start | bytes 589832 | tf_op jit(solution)/shard_map/ppermute | solution.py:170
  6.4 3.1 %shard_map.55 = (bf16[4,128,256]{2,1,0:T(8,128)(2,1)S(1)}, bf16[4,144,256]{2,1,0:T(8,128)(2,1)S(1)}, bf16[2,128,256]{2,1,0:T(8,128)(2,1)S(1)}, bf16[6912,256]{1,0:T(8,128)(2,1)S(1)}) custom-call(bf16[4,128,256]{2,1,0:T(8,128)(2,1)S(1)} %get-tuple-element.148.p, bf16[4,128,256]{2,1,0:T(8,128)(2,1)S(1)} %get-tuple-element.147.q, bf16[6912,256]{1,0:T(8,128)(2,1)} %bitcast.67), custom_call_target="tpu_custom_call" | custom-call | flops 1 | bytes 1 | tf_op jit(solution)/shard_map/pallas_call | solution.py:115
  9.5 1.0 collective-permute-done.1.q_far.p_far
  10.6 2.7 %shard_map.56 = (bf16[1,128,256]{2,1,0:T(8,128)(2,1)S(1)}, bf16[4,128,256]{2,1,0:T(8,128)(2,1)S(1)}, bf16[1,128,256]{2,1,0:T(8,128)(2,1)S(1)}) custom-call(s32[3]{0:T(128)S(1)} %add_convert_fusion.6.flags, bf16[4,128,256]{2,1,0:T(8,128)(2,1)S(1)} %get-tuple-element.148.p, bf16[4,128,256]{2,1,0:T(8,128)(2,1)S(1)} %get-tuple-element.81.even, ...), custom_call_target="tpu_custom_call" | custom-call | flops 1 | bytes 1 | tf_op jit(solution)/shard_map/pallas_call | solution.py:115
  13.3 2.6 %collective-permute-done.2 = bf16[2,4,128,256]{3,2,1,0:T(8,128)(2,1)S(1)} collective-permute-done((bf16[2,4,128,256]{3,2,1,0:T(8,128)(2,1)}, bf16[2,4,128,256]{3,2,1,0:T(8,128)(2,1)S(1)}, u32[]{:S(2)}, u32[]{:S(2)}) %collective-permute-start.2) | collective-permute-done | bytes 524320 | tf_op jit(solution)/shard_map/ppermute | solution.py:208
  16.2 4.8 %collective-permute-start.4 = (bf16[3,128,256]{2,1,0:T(8,128)(2,1)S(1)}, bf16[3,128,256]{2,1,0:T(8,128)(2,1)S(1)}, u32[]{:S(2)}, u32[]{:S(2)}) collective-permute-start(bf16[3,128,256]{2,1,0:T(8,128)(2,1)S(1)} %pad_maximum_fusion.4), channel_id=1, source_target_pairs={{1,2},{2,1},{3,4},{4,3},{5,6},{6,5},{9,10},{10,9},{11,12},{12,11},... | collective-permute-start | bytes 589832 | tf_op jit(solution)/shard_map/ppermute | solution.py:170
  21.1 2.1 %shard_map.57 = bf16[4,128,256]{2,1,0:T(8,128)(2,1)S(1)} custom-call(bf16[1,128,256]{2,1,0:T(8,128)(2,1)S(1)} %get-tuple-element.95.first_low, bf16[4,128,256]{2,1,0:T(8,128)(2,1)S(1)} %get-tuple-element.94.first_mid, bf16[1,128,256]{2,1,0:T(8,128)(2,1)S(1)} %get-tuple-element.96.first_high, bf16[4,128,256]{2,1,0:T(8,128)(2,1)S(1)} %get-tuple-element.147.q, ...), custom_call_target="tpu_custom_call" | custom-call | flops 1 | bytes 1 | tf_op jit(solution)/shard_map/pallas_call | solution.py:115
  23.2 1.3 %collective-permute-done.4.q_far.p_far = bf16[3,128,256]{2,1,0:T(8,128)(2,1)S(1)} collective-permute-done((bf16[3,128,256]{2,1,0:T(8,128)(2,1)S(1)}, bf16[3,128,256]{2,1,0:T(8,128)(2,1)S(1)}, u32[]{:S(2)}, u32[]{:S(2)}) %collective-permute-start.4) | collective-permute-done | bytes 196640 | tf_op jit(solution)/shard_map/ppermute | solution.py:170
  25.2 1.2 %shard_map.58 = (bf16[4,128,256]{2,1,0:T(8,128)(2,1)S(1)}, bf16[4,144,256]{2,1,0:T(8,128)(2,1)S(1)}, bf16[2,128,256]{2,1,0:T(8,128)(2,1)S(1)}) custom-call(bf16[4,128,256]{2,1,0:T(8,128)(2,1)S(1)} %get-tuple-element.99.p, bf16[4,128,256]{2,1,0:T(8,128)(2,1)S(1)} %get-tuple-element.100.q, bf16[6912,256]{1,0:T(8,128)(2,1)S(1)} %get-tuple-element.88.weights), custom_call_target="tpu_custom_call" | custom-call | flops 1 | bytes 1 | tf_op jit(solution)/shard_map/pallas_call | solution.py:115
  26.4 2.7 %shard_map.59 = (bf16[1,128,256]{2,1,0:T(8,128)(2,1)S(1)}, bf16[4,128,256]{2,1,0:T(8,128)(2,1)S(1)}, bf16[1,128,256]{2,1,0:T(8,128)(2,1)S(1)}) custom-call(s32[3]{0:T(128)S(1)} %add_convert_fusion.6.flags, bf16[4,128,256]{2,1,0:T(8,128)(2,1)S(1)} %get-tuple-element.99.p, bf16[4,128,256]{2,1,0:T(8,128)(2,1)S(1)} %get-tuple-element.101.even, ...), custom_call_target="tpu_custom_call" | custom-call | flops 1 | bytes 1 | tf_op jit(solution)/shard_map/pallas_call | solution.py:115
  29.1 3.1 %collective-permute-start.6 = (bf16[4,128,256]{2,1,0:T(8,128)(2,1)S(1)}, bf16[4,128,256]{2,1,0:T(8,128)(2,1)S(1)}, u32[]{:S(2)}, u32[]{:S(2)}) collective-permute-start(bf16[4,128,256]{2,1,0:T(8,128)(2,1)S(1)} %get-tuple-element.106.first_mid), channel_id=1, source_target_pairs={{0,8},{8,16},{16,24},{1,9},{9,17},{17,25},{2,10},{10,18},{18,26},{... | collective-permute-start | bytes 786440 | tf_op jit(solution)/shard_map/ppermute | solution.py:208
  32.3 2.1 %shard_map.60 = bf16[4,128,256]{2,1,0:T(8,128)(2,1)S(1)} custom-call(bf16[1,128,256]{2,1,0:T(8,128)(2,1)S(1)} %get-tuple-element.108.first_low, bf16[4,128,256]{2,1,0:T(8,128)(2,1)S(1)} %get-tuple-element.106.first_mid, bf16[1,128,256]{2,1,0:T(8,128)(2,1)S(1)} %get-tuple-element.109.first_high, bf16[4,128,256]{2,1,0:T(8,128)(2,1)S(1)} %get-tuple-element.100.q, ...), custom_call_target="tpu_custom_call" | custom-call | flops 1 | bytes 1 | tf_op jit(solution)/shard_map/pallas_call | solution.py:115
  35.1 1.9 %collective-permute-start.10 = (bf16[4,128,256]{2,1,0:T(8,128)(2,1)S(1)}, bf16[4,128,256]{2,1,0:T(8,128)(2,1)S(1)}, u32[]{:S(2)}, u32[]{:S(2)}) collective-permute-start(bf16[4,128,256]{2,1,0:T(8,128)(2,1)S(1)} %shard_map.60), channel_id=1, source_target_pairs={{0,8},{8,16},{16,24},{1,9},{9,17},{17,25},{2,10},{10,18},{18,26},{... | collective-permute-start | bytes 786440 | tf_op jit(solution)/shard_map/ppermute | solution.py:208
  37.7 1.7 %collective-permute-done.6 = bf16[4,128,256]{2,1,0:T(8,128)(2,1)S(1)} collective-permute-done((bf16[4,128,256]{2,1,0:T(8,128)(2,1)S(1)}, bf16[4,128,256]{2,1,0:T(8,128)(2,1)S(1)}, u32[]{:S(2)}, u32[]{:S(2)}) %collective-permute-start.6) | collective-permute-done | bytes 262176 | tf_op jit(solution)/shard_map/ppermute | solution.py:208
  39.6 1.3 %collective-permute-start.8 = (bf16[1,128,256]{2,1,0:T(8,128)(2,1)S(1)}, bf16[1,128,256]{2,1,0:T(8,128)(2,1)S(1)}, u32[]{:S(2)}, u32[]{:S(2)}) collective-permute-start(bf16[1,128,256]{2,1,0:T(8,128)(2,1)S(1)} %get-tuple-element.160), channel_id=1, source_target_pairs={{0,1},{1,0},{2,3},{3,2},{4,5},{5,4},{6,7},{7,6},{8,9},{9,8},{10,11... | collective-permute-start | bytes 196616 | tf_op jit(solution)/shard_map/ppermute | solution.py:170
  40.8 3.1 %collective-permute-start.9 = (bf16[1,128,256]{2,1,0:T(8,128)(2,1)S(1)}, bf16[1,128,256]{2,1,0:T(8,128)(2,1)S(1)}, u32[]{:S(2)}, u32[]{:S(2)}) collective-permute-start(bf16[1,128,256]{2,1,0:T(8,128)(2,1)S(1)} %get-tuple-element.159), channel_id=1, source_target_pairs={{1,2},{2,1},{3,4},{4,3},{5,6},{6,5},{9,10},{10,9},{11,12},{12,11},... | collective-permute-start | bytes 196616 | tf_op jit(solution)/shard_map/ppermute | solution.py:170
  44.0 2.8 %collective-permute-done.10 = bf16[4,128,256]{2,1,0:T(8,128)(2,1)S(1)} collective-permute-done((bf16[4,128,256]{2,1,0:T(8,128)(2,1)S(1)}, bf16[4,128,256]{2,1,0:T(8,128)(2,1)S(1)}, u32[]{:S(2)}, u32[]{:S(2)}) %collective-permute-start.10) | collective-permute-done | bytes 262176 | tf_op jit(solution)/shard_map/ppermute | solution.py:208
  46.9 2.8 %collective-permute-start.12 = (bf16[2,128,256]{2,1,0:T(8,128)(2,1)S(1)}, bf16[2,128,256]{2,1,0:T(8,128)(2,1)S(1)}, u32[]{:S(2)}, u32[]{:S(2)}) collective-permute-start(bf16[2,128,256]{2,1,0:T(8,128)(2,1)S(1)} %get-tuple-element.158), channel_id=1, source_target_pairs={{0,1},{1,0},{2,3},{3,2},{4,5},{5,4},{6,7},{7,6},{8,9},{9,8},{10,11... | collective-permute-start | bytes 393224 | tf_op jit(solution)/shard_map/ppermute | solution.py:170
  49.6 3.1 %collective-permute-start.13 = (bf16[2,128,256]{2,1,0:T(8,128)(2,1)S(1)}, bf16[2,128,256]{2,1,0:T(8,128)(2,1)S(1)}, u32[]{:S(2)}, u32[]{:S(2)}) collective-permute-start(bf16[2,128,256]{2,1,0:T(8,128)(2,1)S(1)} %get-tuple-element.157), channel_id=1, source_target_pairs={{1,2},{2,1},{3,4},{4,3},{5,6},{6,5},{9,10},{10,9},{11,12},{12,11},... | collective-permute-start | bytes 393224 | tf_op jit(solution)/shard_map/ppermute | solution.py:170
  53.6 1.2 shard_map.61
  54.8 1.1 collective-permute-done.13.q_far
  55.9 2.7 %shard_map.62 = (bf16[1,128,256]{2,1,0:T(8,128)(2,1)S(1)}, bf16[4,128,256]{2,1,0:T(8,128)(2,1)S(1)}, bf16[1,128,256]{2,1,0:T(8,128)(2,1)S(1)}) custom-call(s32[3]{0:T(128)S(1)} %add_convert_fusion.6.flags, bf16[4,128,256]{2,1,0:T(8,128)(2,1)S(1)} %fusion.17.p, bf16[4,128,256]{2,1,0:T(8,128)(2,1)S(1)} %get-tuple-element.113.even, ...), custom_call_target="tpu_custom_call" | custom-call | flops 1 | bytes 1 | tf_op jit(solution)/shard_map/pallas_call | solution.py:115
  58.6 8.4 %collective-permute-start.14 = (bf16[4,128,256]{2,1,0:T(8,128)(2,1)S(1)}, bf16[4,128,256]{2,1,0:T(8,128)(2,1)S(1)}, u32[]{:S(2)}, u32[]{:S(2)}) collective-permute-start(bf16[4,128,256]{2,1,0:T(8,128)(2,1)S(1)} %get-tuple-element.118.first_mid), channel_id=1, source_target_pairs={{0,8},{8,16},{16,24},{1,9},{9,17},{17,25},{2,10},{10,18},{18,26},{... | collective-permute-start | bytes 786440 | tf_op jit(solution)/shard_map/ppermute | solution.py:208
  67.0 2.1 %shard_map.63 = bf16[4,128,256]{2,1,0:T(8,128)(2,1)S(1)} custom-call(bf16[1,128,256]{2,1,0:T(8,128)(2,1)S(1)} %get-tuple-element.119.first_low, bf16[4,128,256]{2,1,0:T(8,128)(2,1)S(1)} %get-tuple-element.118.first_mid, bf16[1,128,256]{2,1,0:T(8,128)(2,1)S(1)} %get-tuple-element.120.first_high, bf16[4,128,256]{2,1,0:T(8,128)(2,1)S(1)} %fusion.16.q, ...), custom_call_target="tpu_custom_call" | custom-call | flops 1 | bytes 1 | tf_op jit(solution)/shard_map/pallas_call | solution.py:115
  69.2 1.9 %collective-permute-start.18 = (bf16[4,128,256]{2,1,0:T(8,128)(2,1)S(1)}, bf16[4,128,256]{2,1,0:T(8,128)(2,1)S(1)}, u32[]{:S(2)}, u32[]{:S(2)}) collective-permute-start(bf16[4,128,256]{2,1,0:T(8,128)(2,1)S(1)} %shard_map.63), channel_id=1, source_target_pairs={{0,8},{8,16},{16,24},{1,9},{9,17},{17,25},{2,10},{10,18},{18,26},{... | collective-permute-start | bytes 786440 | tf_op jit(solution)/shard_map/ppermute | solution.py:208
  71.8 2.8 %collective-permute-done.14 = bf16[4,128,256]{2,1,0:T(8,128)(2,1)S(1)} collective-permute-done((bf16[4,128,256]{2,1,0:T(8,128)(2,1)S(1)}, bf16[4,128,256]{2,1,0:T(8,128)(2,1)S(1)}, u32[]{:S(2)}, u32[]{:S(2)}) %collective-permute-start.14) | collective-permute-done | bytes 262176 | tf_op jit(solution)/shard_map/ppermute | solution.py:208
  74.8 2.8 %collective-permute-start.17 = (bf16[1,128,256]{2,1,0:T(8,128)(2,1)S(1)}, bf16[1,128,256]{2,1,0:T(8,128)(2,1)S(1)}, u32[]{:S(2)}, u32[]{:S(2)}) collective-permute-start(bf16[1,128,256]{2,1,0:T(8,128)(2,1)S(1)} %get-tuple-element.155), channel_id=1, source_target_pairs={{1,2},{2,1},{3,4},{4,3},{5,6},{6,5},{9,10},{10,9},{11,12},{12,11},... | collective-permute-start | bytes 196616 | tf_op jit(solution)/shard_map/ppermute | solution.py:170
  77.7 1.9 %collective-permute-done.18 = bf16[4,128,256]{2,1,0:T(8,128)(2,1)S(1)} collective-permute-done((bf16[4,128,256]{2,1,0:T(8,128)(2,1)S(1)}, bf16[4,128,256]{2,1,0:T(8,128)(2,1)S(1)}, u32[]{:S(2)}, u32[]{:S(2)}) %collective-permute-start.18) | collective-permute-done | bytes 262176 | tf_op jit(solution)/shard_map/ppermute | solution.py:208
  79.5 1.0 collective-permute-done.17.p_far
  81.1 2.9 %collective-permute-start.21 = (bf16[2,128,256]{2,1,0:T(8,128)(2,1)S(1)}, bf16[2,128,256]{2,1,0:T(8,128)(2,1)S(1)}, u32[]{:S(2)}, u32[]{:S(2)}) collective-permute-start(bf16[2,128,256]{2,1,0:T(8,128)(2,1)S(1)} %get-tuple-element.153), channel_id=1, source_target_pairs={{1,2},{2,1},{3,4},{4,3},{5,6},{6,5},{9,10},{10,9},{11,12},{12,11},... | collective-permute-start | bytes 393224 | tf_op jit(solution)/shard_map/ppermute | solution.py:170
  84.8 1.2 shard_map.64
  86.0 1.4 %collective-permute-done.21.q_far = bf16[2,128,256]{2,1,0:T(8,128)(2,1)S(1)} collective-permute-done((bf16[2,128,256]{2,1,0:T(8,128)(2,1)S(1)}, bf16[2,128,256]{2,1,0:T(8,128)(2,1)S(1)}, u32[]{:S(2)}, u32[]{:S(2)}) %collective-permute-start.21) | collective-permute-done | bytes 131104 | tf_op jit(solution)/shard_map/ppermute | solution.py:170
  87.4 2.7 %shard_map.65 = (bf16[1,128,256]{2,1,0:T(8,128)(2,1)S(1)}, bf16[4,128,256]{2,1,0:T(8,128)(2,1)S(1)}, bf16[1,128,256]{2,1,0:T(8,128)(2,1)S(1)}) custom-call(s32[3]{0:T(128)S(1)} %add_convert_fusion.6.flags, bf16[4,128,256]{2,1,0:T(8,128)(2,1)S(1)} %fusion.15.p, bf16[4,128,256]{2,1,0:T(8,128)(2,1)S(1)} %get-tuple-element.124.even, ...), custom_call_target="tpu_custom_call" | custom-call | flops 1 | bytes 1 | tf_op jit(solution)/shard_map/pallas_call | solution.py:115
  90.1 3.4 %collective-permute-start.22 = (bf16[4,128,256]{2,1,0:T(8,128)(2,1)S(1)}, bf16[4,128,256]{2,1,0:T(8,128)(2,1)S(1)}, u32[]{:S(2)}, u32[]{:S(2)}) collective-permute-start(bf16[4,128,256]{2,1,0:T(8,128)(2,1)S(1)} %get-tuple-element.129.first_mid), channel_id=1, source_target_pairs={{8,16},{16,24},{9,17},{17,25},{10,18},{18,26},{11,19},{19,27},{12,... | collective-permute-start | bytes 786440 | tf_op jit(solution)/shard_map/ppermute | solution.py:208
  93.5 2.1 %shard_map.66 = bf16[4,128,256]{2,1,0:T(8,128)(2,1)S(1)} custom-call(bf16[1,128,256]{2,1,0:T(8,128)(2,1)S(1)} %get-tuple-element.130.first_low, bf16[4,128,256]{2,1,0:T(8,128)(2,1)S(1)} %get-tuple-element.129.first_mid, bf16[1,128,256]{2,1,0:T(8,128)(2,1)S(1)} %get-tuple-element.131.first_high, bf16[4,128,256]{2,1,0:T(8,128)(2,1)S(1)} %fusion.14.q, ...), custom_call_target="tpu_custom_call" | custom-call | flops 1 | bytes 1 | tf_op jit(solution)/shard_map/pallas_call | solution.py:115
  95.7 1.9 %collective-permute-start.26 = (bf16[4,128,256]{2,1,0:T(8,128)(2,1)S(1)}, bf16[4,128,256]{2,1,0:T(8,128)(2,1)S(1)}, u32[]{:S(2)}, u32[]{:S(2)}) collective-permute-start(bf16[4,128,256]{2,1,0:T(8,128)(2,1)S(1)} %shard_map.66), channel_id=1, source_target_pairs={{8,16},{16,24},{9,17},{17,25},{10,18},{18,26},{11,19},{19,27},{12,... | collective-permute-start | bytes 786440 | tf_op jit(solution)/shard_map/ppermute | solution.py:208
  98.3 2.6 %collective-permute-done.22 = bf16[4,128,256]{2,1,0:T(8,128)(2,1)S(1)} collective-permute-done((bf16[4,128,256]{2,1,0:T(8,128)(2,1)S(1)}, bf16[4,128,256]{2,1,0:T(8,128)(2,1)S(1)}, u32[]{:S(2)}, u32[]{:S(2)}) %collective-permute-start.22) | collective-permute-done | bytes 262176 | tf_op jit(solution)/shard_map/ppermute | solution.py:208
  101.0 0.9 collective-permute-start.24
  102.0 2.7 %collective-permute-start.25 = (bf16[1,128,256]{2,1,0:T(8,128)(2,1)S(1)}, bf16[1,128,256]{2,1,0:T(8,128)(2,1)S(1)}, u32[]{:S(2)}, u32[]{:S(2)}) collective-permute-start(bf16[1,128,256]{2,1,0:T(8,128)(2,1)S(1)} %get-tuple-element.151), channel_id=1, source_target_pairs={{1,2},{2,1},{3,4},{4,3},{5,6},{6,5},{9,10},{10,9},{11,12},{12,11},... | collective-permute-start | bytes 196616 | tf_op jit(solution)/shard_map/ppermute | solution.py:170
  104.7 1.2 collective-permute-done.26
  105.9 1.6 %collective-permute-done.25.p_far = bf16[1,128,256]{2,1,0:T(8,128)(2,1)S(1)} collective-permute-done((bf16[1,128,256]{2,1,0:T(8,128)(2,1)S(1)}, bf16[1,128,256]{2,1,0:T(8,128)(2,1)S(1)}, u32[]{:S(2)}, u32[]{:S(2)}) %collective-permute-start.25) | collective-permute-done | bytes 65568 | tf_op jit(solution)/shard_map/ppermute | solution.py:170
  107.8 3.4 %collective-permute-start.29 = (bf16[2,128,256]{2,1,0:T(8,128)(2,1)S(1)}, bf16[2,128,256]{2,1,0:T(8,128)(2,1)S(1)}, u32[]{:S(2)}, u32[]{:S(2)}) collective-permute-start(bf16[2,128,256]{2,1,0:T(8,128)(2,1)S(1)} %get-tuple-element.149), channel_id=1, source_target_pairs={{1,2},{2,1},{3,4},{4,3},{5,6},{6,5},{9,10},{10,9},{11,12},{12,11},... | collective-permute-start | bytes 393224 | tf_op jit(solution)/shard_map/ppermute | solution.py:170
  111.2 1.2 shard_map.67
  112.4 1.7 %collective-permute-done.29.q_far = bf16[2,128,256]{2,1,0:T(8,128)(2,1)S(1)} collective-permute-done((bf16[2,128,256]{2,1,0:T(8,128)(2,1)S(1)}, bf16[2,128,256]{2,1,0:T(8,128)(2,1)S(1)}, u32[]{:S(2)}, u32[]{:S(2)}) %collective-permute-start.29) | collective-permute-done | bytes 131104 | tf_op jit(solution)/shard_map/ppermute | solution.py:170
  114.1 2.7 %shard_map.68 = (bf16[1,128,256]{2,1,0:T(8,128)(2,1)S(1)}, bf16[4,128,256]{2,1,0:T(8,128)(2,1)S(1)}, bf16[1,128,256]{2,1,0:T(8,128)(2,1)S(1)}) custom-call(s32[3]{0:T(128)S(1)} %add_convert_fusion.6.flags, bf16[4,128,256]{2,1,0:T(8,128)(2,1)S(1)} %fusion.13.p, bf16[4,128,256]{2,1,0:T(8,128)(2,1)S(1)} %get-tuple-element.135.even, ...), custom_call_target="tpu_custom_call" | custom-call | flops 1 | bytes 1 | tf_op jit(solution)/shard_map/pallas_call | solution.py:115
  116.8 2.9 %shard_map.69 = bf16[2,4,128,256]{3,2,1,0:T(8,128)(2,1)} custom-call(bf16[1,128,256]{2,1,0:T(8,128)(2,1)S(1)} %get-tuple-element.140.first_low, bf16[4,128,256]{2,1,0:T(8,128)(2,1)S(1)} %get-tuple-element.141.first_mid, bf16[1,128,256]{2,1,0:T(8,128)(2,1)S(1)} %get-tuple-element.142.first_high, bf16[4,128,256]{2,1,0:T(8,128)(2,1)S(1)} %fusion.12.q, ...), custom_call_target="tpu_custom_call" | custom-call | flops 1 | bytes 1 | tf_op jit(solution)/shard_map/pallas_call | solution.py:115
  (58 shorter events, 7.8 us)
Async XLA Ops:
  0.1 15.8 %collective-permute-start.2 = (bf16[2,4,128,256]{3,2,1,0:T(8,128)(2,1)}, bf16[2,4,128,256]{3,2,1,0:T(8,128)(2,1)S(1)}, u32[]{:S(2)}, u32[]{:S(2)}) collective-permute-start(bf16[2,4,128,256]{3,2,1,0:T(8,128)(2,1)} %bitcast.75), channel_id=1, source_target_pairs={{0,24},{8,16},{1,25},{9,17},{2,26},{10,18},{3,27},{11,19},{4,28},{... | collective-permute-start | bytes 1572872 | tf_op jit(solution)/shard_map/ppermute | solution.py:208
  2.5 7.0 %collective-permute-start = (bf16[3,128,256]{2,1,0:T(8,128)(2,1)S(1)}, bf16[3,128,256]{2,1,0:T(8,128)(2,1)S(1)}, u32[]{:S(2)}, u32[]{:S(2)}) collective-permute-start(bf16[3,128,256]{2,1,0:T(8,128)(2,1)S(1)} %pad_maximum_fusion.1), channel_id=1, source_target_pairs={{0,1},{1,0},{2,3},{3,2},{4,5},{5,4},{6,7},{7,6},{8,9},{9,8},{10,11... | collective-permute-start | bytes 589832 | tf_op jit(solution)/shard_map/ppermute | solution.py:170
  3.3 7.3 %collective-permute-start.1 = (bf16[3,128,256]{2,1,0:T(8,128)(2,1)S(1)}, bf16[3,128,256]{2,1,0:T(8,128)(2,1)S(1)}, u32[]{:S(2)}, u32[]{:S(2)}) collective-permute-start(bf16[3,128,256]{2,1,0:T(8,128)(2,1)S(1)} %pad_maximum_fusion.2), channel_id=1, source_target_pairs={{1,2},{2,1},{3,4},{4,3},{5,6},{6,5},{9,10},{10,9},{11,12},{12,11},... | collective-permute-start | bytes 589832 | tf_op jit(solution)/shard_map/ppermute | solution.py:170
  10.6 5.3 %copy-start.1 = (bf16[3,2,4,16,8,256]{5,4,3,2,1,0:T(8,128)(2,1)S(1)}, bf16[3,2,4,16,8,256]{5,4,3,2,1,0:T(8,128)(2,1)}, u32[]{:S(2)}) copy-start(bf16[3,2,4,16,8,256]{5,4,3,2,1,0:T(8,128)(2,1)} %param.7) | copy-start | bytes 4718596
  10.6 5.3 %copy-start.2 = (bf16[1,2,4,16,8,256]{5,4,3,2,1,0:T(8,128)(2,1)S(1)}, bf16[1,2,4,16,8,256]{5,4,3,2,1,0:T(8,128)(2,1)}, u32[]{:S(2)}) copy-start(bf16[1,2,4,16,8,256]{5,4,3,2,1,0:T(8,128)(2,1)} %param.5) | copy-start | bytes 1572868
  15.9 5.2 %copy-start = (bf16[1,3,3,3,256,256]{5,4,3,2,1,0:T(8,128)(2,1)S(1)}, bf16[1,3,3,3,256,256]{5,4,3,2,1,0:T(8,128)(2,1)}, u32[]{:S(2)}) copy-start(bf16[1,3,3,3,256,256]{5,4,3,2,1,0:T(8,128)(2,1)} %param.9) | copy-start | bytes 10616836
  16.2 8.3 %collective-permute-start.4 = (bf16[3,128,256]{2,1,0:T(8,128)(2,1)S(1)}, bf16[3,128,256]{2,1,0:T(8,128)(2,1)S(1)}, u32[]{:S(2)}, u32[]{:S(2)}) collective-permute-start(bf16[3,128,256]{2,1,0:T(8,128)(2,1)S(1)} %pad_maximum_fusion.4), channel_id=1, source_target_pairs={{1,2},{2,1},{3,4},{4,3},{5,6},{6,5},{9,10},{10,9},{11,12},{12,11},... | collective-permute-start | bytes 589832 | tf_op jit(solution)/shard_map/ppermute | solution.py:170
  21.0 3.5 %collective-permute-start.3 = (bf16[3,128,256]{2,1,0:T(8,128)(2,1)S(1)}, bf16[3,128,256]{2,1,0:T(8,128)(2,1)S(1)}, u32[]{:S(2)}, u32[]{:S(2)}) collective-permute-start(bf16[3,128,256]{2,1,0:T(8,128)(2,1)S(1)} %pad_maximum_fusion.3), channel_id=1, source_target_pairs={{0,1},{1,0},{2,3},{3,2},{4,5},{5,4},{6,7},{7,6},{8,9},{9,8},{10,11... | collective-permute-start | bytes 589832 | tf_op jit(solution)/shard_map/ppermute | solution.py:170
  24.5 9.9 %collective-permute-start.5 = (bf16[2,4,128,256]{3,2,1,0:T(8,128)(2,1)S(1)}, bf16[2,4,128,256]{3,2,1,0:T(8,128)(2,1)S(1)}, u32[]{:S(2)}, u32[]{:S(2)}) collective-permute-start(bf16[2,4,128,256]{3,2,1,0:T(8,128)(2,1)S(1)} %pad_maximum_fusion), channel_id=1, source_target_pairs={{0,8},{1,9},{2,10},{3,11},{4,12},{5,13},{6,14},{7,15}} | collective-permute-start | bytes 1572872 | tf_op jit(solution)/shard_map/ppermute | solution.py:208
  29.1 10.3 %collective-permute-start.6 = (bf16[4,128,256]{2,1,0:T(8,128)(2,1)S(1)}, bf16[4,128,256]{2,1,0:T(8,128)(2,1)S(1)}, u32[]{:S(2)}, u32[]{:S(2)}) collective-permute-start(bf16[4,128,256]{2,1,0:T(8,128)(2,1)S(1)} %get-tuple-element.106.first_mid), channel_id=1, source_target_pairs={{0,8},{8,16},{16,24},{1,9},{9,17},{17,25},{2,10},{10,18},{18,26},{... | collective-permute-start | bytes 786440 | tf_op jit(solution)/shard_map/ppermute | solution.py:208
  34.4 5.0 %collective-permute-start.7 = (bf16[4,128,256]{2,1,0:T(8,128)(2,1)S(1)}, bf16[4,128,256]{2,1,0:T(8,128)(2,1)S(1)}, u32[]{:S(2)}, u32[]{:S(2)}) collective-permute-start(bf16[4,128,256]{2,1,0:T(8,128)(2,1)S(1)} %get-tuple-element.110), channel_id=1, source_target_pairs={{8,24},{9,25},{10,26},{11,27},{12,28},{13,29},{14,30},{15,31}} | collective-permute-start | bytes 786440 | tf_op jit(solution)/shard_map/ppermute | solution.py:208
  35.1 11.6 %collective-permute-start.10 = (bf16[4,128,256]{2,1,0:T(8,128)(2,1)S(1)}, bf16[4,128,256]{2,1,0:T(8,128)(2,1)S(1)}, u32[]{:S(2)}, u32[]{:S(2)}) collective-permute-start(bf16[4,128,256]{2,1,0:T(8,128)(2,1)S(1)} %shard_map.60), channel_id=1, source_target_pairs={{0,8},{8,16},{16,24},{1,9},{9,17},{17,25},{2,10},{10,18},{18,26},{... | collective-permute-start | bytes 786440 | tf_op jit(solution)/shard_map/ppermute | solution.py:208
  37.1 9.7 %collective-permute-start.11 = (bf16[4,128,256]{2,1,0:T(8,128)(2,1)S(1)}, bf16[4,128,256]{2,1,0:T(8,128)(2,1)S(1)}, u32[]{:S(2)}, u32[]{:S(2)}) collective-permute-start(bf16[4,128,256]{2,1,0:T(8,128)(2,1)S(1)} %get-tuple-element.145), channel_id=1, source_target_pairs={{8,24},{9,25},{10,26},{11,27},{12,28},{13,29},{14,30},{15,31}} | collective-permute-start | bytes 786440 | tf_op jit(solution)/shard_map/ppermute | solution.py:208
  39.6 7.2 %collective-permute-start.8 = (bf16[1,128,256]{2,1,0:T(8,128)(2,1)S(1)}, bf16[1,128,256]{2,1,0:T(8,128)(2,1)S(1)}, u32[]{:S(2)}, u32[]{:S(2)}) collective-permute-start(bf16[1,128,256]{2,1,0:T(8,128)(2,1)S(1)} %get-tuple-element.160), channel_id=1, source_target_pairs={{0,1},{1,0},{2,3},{3,2},{4,5},{5,4},{6,7},{7,6},{8,9},{9,8},{10,11... | collective-permute-start | bytes 196616 | tf_op jit(solution)/shard_map/ppermute | solution.py:170
  40.8 5.9 %collective-permute-start.9 = (bf16[1,128,256]{2,1,0:T(8,128)(2,1)S(1)}, bf16[1,128,256]{2,1,0:T(8,128)(2,1)S(1)}, u32[]{:S(2)}, u32[]{:S(2)}) collective-permute-start(bf16[1,128,256]{2,1,0:T(8,128)(2,1)S(1)} %get-tuple-element.159), channel_id=1, source_target_pairs={{1,2},{2,1},{3,4},{4,3},{5,6},{6,5},{9,10},{10,9},{11,12},{12,11},... | collective-permute-start | bytes 196616 | tf_op jit(solution)/shard_map/ppermute | solution.py:170
  46.9 7.9 %collective-permute-start.12 = (bf16[2,128,256]{2,1,0:T(8,128)(2,1)S(1)}, bf16[2,128,256]{2,1,0:T(8,128)(2,1)S(1)}, u32[]{:S(2)}, u32[]{:S(2)}) collective-permute-start(bf16[2,128,256]{2,1,0:T(8,128)(2,1)S(1)} %get-tuple-element.158), channel_id=1, source_target_pairs={{0,1},{1,0},{2,3},{3,2},{4,5},{5,4},{6,7},{7,6},{8,9},{9,8},{10,11... | collective-permute-start | bytes 393224 | tf_op jit(solution)/shard_map/ppermute | solution.py:170
  49.6 6.3 %collective-permute-start.13 = (bf16[2,128,256]{2,1,0:T(8,128)(2,1)S(1)}, bf16[2,128,256]{2,1,0:T(8,128)(2,1)S(1)}, u32[]{:S(2)}, u32[]{:S(2)}) collective-permute-start(bf16[2,128,256]{2,1,0:T(8,128)(2,1)S(1)} %get-tuple-element.157), channel_id=1, source_target_pairs={{1,2},{2,1},{3,4},{4,3},{5,6},{6,5},{9,10},{10,9},{11,12},{12,11},... | collective-permute-start | bytes 393224 | tf_op jit(solution)/shard_map/ppermute | solution.py:170
  52.8 19.0 %collective-permute-start.15 = (bf16[4,128,256]{2,1,0:T(8,128)(2,1)S(1)}, bf16[4,128,256]{2,1,0:T(8,128)(2,1)S(1)}, u32[]{:S(2)}, u32[]{:S(2)}) collective-permute-start(bf16[4,128,256]{2,1,0:T(8,128)(2,1)S(1)} %collective-permute-done.6), channel_id=1, source_target_pairs={{8,24},{9,25},{10,26},{11,27},{12,28},{13,29},{14,30},{15,31}} | collective-permute-start | bytes 786440 | tf_op jit(solution)/shard_map/ppermute | solution.py:208
  58.6 16.0 %collective-permute-start.14 = (bf16[4,128,256]{2,1,0:T(8,128)(2,1)S(1)}, bf16[4,128,256]{2,1,0:T(8,128)(2,1)S(1)}, u32[]{:S(2)}, u32[]{:S(2)}) collective-permute-start(bf16[4,128,256]{2,1,0:T(8,128)(2,1)S(1)} %get-tuple-element.118.first_mid), channel_id=1, source_target_pairs={{0,8},{8,16},{16,24},{1,9},{9,17},{17,25},{2,10},{10,18},{18,26},{... | collective-permute-start | bytes 786440 | tf_op jit(solution)/shard_map/ppermute | solution.py:208
  69.2 10.4 %collective-permute-start.18 = (bf16[4,128,256]{2,1,0:T(8,128)(2,1)S(1)}, bf16[4,128,256]{2,1,0:T(8,128)(2,1)S(1)}, u32[]{:S(2)}, u32[]{:S(2)}) collective-permute-start(bf16[4,128,256]{2,1,0:T(8,128)(2,1)S(1)} %shard_map.63), channel_id=1, source_target_pairs={{0,8},{8,16},{16,24},{1,9},{9,17},{17,25},{2,10},{10,18},{18,26},{... | collective-permute-start | bytes 786440 | tf_op jit(solution)/shard_map/ppermute | solution.py:208
  71.1 9.4 %collective-permute-start.19 = (bf16[4,128,256]{2,1,0:T(8,128)(2,1)S(1)}, bf16[4,128,256]{2,1,0:T(8,128)(2,1)S(1)}, u32[]{:S(2)}, u32[]{:S(2)}) collective-permute-start(bf16[4,128,256]{2,1,0:T(8,128)(2,1)S(1)} %collective-permute-done.10), channel_id=1, source_target_pairs={{8,24},{9,25},{10,26},{11,27},{12,28},{13,29},{14,30},{15,31}} | collective-permute-start | bytes 786440 | tf_op jit(solution)/shard_map/ppermute | solution.py:208
  74.7 4.8 %collective-permute-start.16 = (bf16[1,128,256]{2,1,0:T(8,128)(2,1)S(1)}, bf16[1,128,256]{2,1,0:T(8,128)(2,1)S(1)}, u32[]{:S(2)}, u32[]{:S(2)}) collective-permute-start(bf16[1,128,256]{2,1,0:T(8,128)(2,1)S(1)} %get-tuple-element.156), channel_id=1, source_target_pairs={{0,1},{1,0},{2,3},{3,2},{4,5},{5,4},{6,7},{7,6},{8,9},{9,8},{10,11... | collective-permute-start | bytes 196616 | tf_op jit(solution)/shard_map/ppermute | solution.py:170
  74.8 5.7 %collective-permute-start.17 = (bf16[1,128,256]{2,1,0:T(8,128)(2,1)S(1)}, bf16[1,128,256]{2,1,0:T(8,128)(2,1)S(1)}, u32[]{:S(2)}, u32[]{:S(2)}) collective-permute-start(bf16[1,128,256]{2,1,0:T(8,128)(2,1)S(1)} %get-tuple-element.155), channel_id=1, source_target_pairs={{1,2},{2,1},{3,4},{4,3},{5,6},{6,5},{9,10},{10,9},{11,12},{12,11},... | collective-permute-start | bytes 196616 | tf_op jit(solution)/shard_map/ppermute | solution.py:170
  80.7 5.3 %collective-permute-start.20 = (bf16[2,128,256]{2,1,0:T(8,128)(2,1)S(1)}, bf16[2,128,256]{2,1,0:T(8,128)(2,1)S(1)}, u32[]{:S(2)}, u32[]{:S(2)}) collective-permute-start(bf16[2,128,256]{2,1,0:T(8,128)(2,1)S(1)} %get-tuple-element.154), channel_id=1, source_target_pairs={{0,1},{1,0},{2,3},{3,2},{4,5},{5,4},{6,7},{7,6},{8,9},{9,8},{10,11... | collective-permute-start | bytes 393224 | tf_op jit(solution)/shard_map/ppermute | solution.py:170
  81.1 6.3 %collective-permute-start.21 = (bf16[2,128,256]{2,1,0:T(8,128)(2,1)S(1)}, bf16[2,128,256]{2,1,0:T(8,128)(2,1)S(1)}, u32[]{:S(2)}, u32[]{:S(2)}) collective-permute-start(bf16[2,128,256]{2,1,0:T(8,128)(2,1)S(1)} %get-tuple-element.153), channel_id=1, source_target_pairs={{1,2},{2,1},{3,4},{4,3},{5,6},{6,5},{9,10},{10,9},{11,12},{12,11},... | collective-permute-start | bytes 393224 | tf_op jit(solution)/shard_map/ppermute | solution.py:170
  84.1 14.2 %collective-permute-start.23 = (bf16[4,128,256]{2,1,0:T(8,128)(2,1)S(1)}, bf16[4,128,256]{2,1,0:T(8,128)(2,1)S(1)}, u32[]{:S(2)}, u32[]{:S(2)}) collective-permute-start(bf16[4,128,256]{2,1,0:T(8,128)(2,1)S(1)} %collective-permute-done.14), channel_id=1, source_target_pairs={{8,24},{9,25},{10,26},{11,27},{12,28},{13,29},{14,30},{15,31}} | collective-permute-start | bytes 786440 | tf_op jit(solution)/shard_map/ppermute | solution.py:208
  90.1 10.8 %collective-permute-start.22 = (bf16[4,128,256]{2,1,0:T(8,128)(2,1)S(1)}, bf16[4,128,256]{2,1,0:T(8,128)(2,1)S(1)}, u32[]{:S(2)}, u32[]{:S(2)}) collective-permute-start(bf16[4,128,256]{2,1,0:T(8,128)(2,1)S(1)} %get-tuple-element.129.first_mid), channel_id=1, source_target_pairs={{8,16},{16,24},{9,17},{17,25},{10,18},{18,26},{11,19},{19,27},{12,... | collective-permute-start | bytes 786440 | tf_op jit(solution)/shard_map/ppermute | solution.py:208
  95.7 10.2 %collective-permute-start.26 = (bf16[4,128,256]{2,1,0:T(8,128)(2,1)S(1)}, bf16[4,128,256]{2,1,0:T(8,128)(2,1)S(1)}, u32[]{:S(2)}, u32[]{:S(2)}) collective-permute-start(bf16[4,128,256]{2,1,0:T(8,128)(2,1)S(1)} %shard_map.66), channel_id=1, source_target_pairs={{8,16},{16,24},{9,17},{17,25},{10,18},{18,26},{11,19},{19,27},{12,... | collective-permute-start | bytes 786440 | tf_op jit(solution)/shard_map/ppermute | solution.py:208
  97.6 9.9 %collective-permute-start.27 = (bf16[4,128,256]{2,1,0:T(8,128)(2,1)S(1)}, bf16[4,128,256]{2,1,0:T(8,128)(2,1)S(1)}, u32[]{:S(2)}, u32[]{:S(2)}) collective-permute-start(bf16[4,128,256]{2,1,0:T(8,128)(2,1)S(1)} %collective-permute-done.18), channel_id=1, source_target_pairs={{8,24},{9,25},{10,26},{11,27},{12,28},{13,29},{14,30},{15,31}} | collective-permute-start | bytes 786440 | tf_op jit(solution)/shard_map/ppermute | solution.py:208
  101.0 4.9 %collective-permute-start.24 = (bf16[1,128,256]{2,1,0:T(8,128)(2,1)S(1)}, bf16[1,128,256]{2,1,0:T(8,128)(2,1)S(1)}, u32[]{:S(2)}, u32[]{:S(2)}) collective-permute-start(bf16[1,128,256]{2,1,0:T(8,128)(2,1)S(1)} %get-tuple-element.152), channel_id=1, source_target_pairs={{0,1},{1,0},{2,3},{3,2},{4,5},{5,4},{6,7},{7,6},{8,9},{9,8},{10,11... | collective-permute-start | bytes 196616 | tf_op jit(solution)/shard_map/ppermute | solution.py:170
  102.0 5.6 %collective-permute-start.25 = (bf16[1,128,256]{2,1,0:T(8,128)(2,1)S(1)}, bf16[1,128,256]{2,1,0:T(8,128)(2,1)S(1)}, u32[]{:S(2)}, u32[]{:S(2)}) collective-permute-start(bf16[1,128,256]{2,1,0:T(8,128)(2,1)S(1)} %get-tuple-element.151), channel_id=1, source_target_pairs={{1,2},{2,1},{3,4},{4,3},{5,6},{6,5},{9,10},{10,9},{11,12},{12,11},... | collective-permute-start | bytes 196616 | tf_op jit(solution)/shard_map/ppermute | solution.py:170
  107.7 4.7 %collective-permute-start.28 = (bf16[2,128,256]{2,1,0:T(8,128)(2,1)S(1)}, bf16[2,128,256]{2,1,0:T(8,128)(2,1)S(1)}, u32[]{:S(2)}, u32[]{:S(2)}) collective-permute-start(bf16[2,128,256]{2,1,0:T(8,128)(2,1)S(1)} %get-tuple-element.150), channel_id=1, source_target_pairs={{0,1},{1,0},{2,3},{3,2},{4,5},{5,4},{6,7},{7,6},{8,9},{9,8},{10,11... | collective-permute-start | bytes 393224 | tf_op jit(solution)/shard_map/ppermute | solution.py:170
  107.8 6.4 %collective-permute-start.29 = (bf16[2,128,256]{2,1,0:T(8,128)(2,1)S(1)}, bf16[2,128,256]{2,1,0:T(8,128)(2,1)S(1)}, u32[]{:S(2)}, u32[]{:S(2)}) collective-permute-start(bf16[2,128,256]{2,1,0:T(8,128)(2,1)S(1)} %get-tuple-element.149), channel_id=1, source_target_pairs={{1,2},{2,1},{3,4},{4,3},{5,6},{6,5},{9,10},{10,9},{11,12},{12,11},... | collective-permute-start | bytes 393224 | tf_op jit(solution)/shard_map/ppermute | solution.py:170

commit v7 on v6

--- a/solution.py
+++ b/solution.py
@@ -159,17 +159,11 @@
     return out
 
 
-def swapped(blocks, widths, starts):
+def swap(turn, starts, *blocks):
     count = lax.axis_size("depth")
-
-    def swap(turn):
-        parts = [
-            lax.dynamic_slice_in_dim(block, starts[width][turn], width, axis=0) for block, width in zip(blocks, widths)
-        ]
-        pairs = [pair for i in range(turn, count - 1, 2) for pair in ((i, i + 1), (i + 1, i))]
-        return lax.ppermute(jnp.concatenate(parts, axis=0), "depth", pairs)
-
-    return swap(0), swap(1)
+    parts = [lax.dynamic_slice_in_dim(block, starts[n][turn], n, axis=0) for block, n in blocks]
+    pairs = [pair for i in range(turn, count - 1, 2) for pair in ((i, i + 1), (i + 1, i))]
+    return lax.ppermute(jnp.concatenate(parts, axis=0), "depth", pairs)
 
 
 def local(resident, previous, incoming, first_weights, second_weights):
@@ -225,43 +219,37 @@
 
     p, q = resident
     mirrored = send(previous, [(j, sections - 1 - j) for j in range(half)])
-    q_halos = p_halos = swapped((q, p), (2, 1), starts)
+    near, q_far = (swap(turn, starts, (q, 2), (p, 1)) for turn in range(2))
+    p_far = q_far
     for slot in range(ticks + 1):
         if slot == 1:
-            p, q, q_halos = following
-            p_halos = q_halos
+            p, q, near, q_far = following
+            p_far = q_far
         elif slot > 1:
             p = arrived(slot, 0)
-            p_halos = swapped((p,), (1,), starts)
-            p, p_halos, newer[1] = lax.optimization_barrier((p, p_halos, newer[1]))
+            p_far = swap(1, starts, (p, 1))
+            p, p_far, newer[1] = lax.optimization_barrier((p, p_far, newer[1]))
             q = arrived(slot, 1)
-            q_halos = swapped((q,), (2,), starts)
+            near = swap(0, starts, (q, 2), (p, 1))
+            q_far = swap(1, starts, (q, 2))
         *kept, w_one = inner_half(p, q, w_one, width, slot == 0)
-        first = first_half(flags, p, kept, q_halos, p_halos, w_one, width)
-        onward = [(j, j + 1) for j in range(1, sections - 1)]
+        first = first_half(flags, p, kept, (near, q_far), (near, p_far), w_one, width)
+        onward = [(j, j + 1) for j in range(1, sections - 1)] if slot > 0 else []
         if slot < ticks - 1:
             onward = [(0, 1)] + onward
         received, relays = {}, {}
-        if slot == 0:
-            mirrored, _ = lax.optimization_barrier((mirrored, first[1]))
-            following = arrived(1, 0), arrived(1, 1)
-            following = *following, swapped(following[::-1], (2, 1), starts)
-            first, joined = lax.optimization_barrier((first, following[:2]))
-            following = *joined, following[2]
-        elif slot < ticks:
+        if slot < ticks:
             received[0] = send(first[1], onward)
         second = second_half(first, q, w_two, width, slot == ticks)
+        if slot < ticks:
+            received[1] = send(second, onward)
         if slot == 0:
-            second, q_halos = lax.optimization_barrier((second, following[2]))
-            following = *following[:2], q_halos
-            received = send(jnp.stack([first[1], second]), [(0, 1)])
+            mirrored, _ = lax.optimization_barrier((mirrored, second))
+            following = arrived(1, 0), arrived(1, 1)
+            following += tuple(swap(turn, starts, (following[1], 2), (following[0], 1)) for turn in range(2))
         elif slot < ticks:
-            received[1] = send(second, onward)
-            relay_p, relay_q = newer[0], newer[1]
-            if slot == 1:
-                relay_p, second = lax.optimization_barrier((relay_p, second))
-            relay_q, second = lax.optimization_barrier((relay_q, second))
-            relays = {0: send(relay_p, [(1, sections - 1)]), 1: send(relay_q, [(1, sections - 1)])}
+            relay_q, second = lax.optimization_barrier((newer[1], second))
+            relays = {0: send(newer[0], [(1, sections - 1)]), 1: send(relay_q, [(1, sections - 1)])}
             if across:
                 direct = {0: send(first[1], across), 1: send(second, across)}
         older, newer, relayed = newer, received, relays

time: 120 us -> 114 us (0.950)
  starting transfers between devices: 59.4 us -> 52.6 us
    ppermute x14 -> x15, starting transfers between devices: 26.9 us -> 19.6 us  [send(): return lax.ppermute(block, 'section', pairs) if pairs else block]
    ppermute x16 -> x13, waiting for transfers between devices: 9.14 us -> 10.5 us  [swap(): return lax.ppermute(jnp.concatenate(parts, axis=0), 'depth', pairs)]
    ppermute x14 -> x15, waiting for transfers between devices: 15.5 us -> 14.4 us  [send(): return lax.ppermute(block, 'section', pairs) if pairs else block]
    ppermute x16 -> x13, starting transfers between devices: 32.5 us -> 33 us  [swap(): return lax.ppermute(jnp.concatenate(parts, axis=0), 'depth', pairs)]
  transfers between devices with their start and end apart: 30 -> 28, of which waited for: 14 -> 13; matrix products, arithmetic and copies ran while one was open for 1% -> 2% of each run, Pallas kernels for 23% -> 24%
where the time goes in v7:
time: 114 us; the launch traced here: 113 us
  starting transfers between devices  52.6 us (46%)
  Pallas kernels  32.7 us (29%)
  waiting for transfers between devices  24.9 us (22%)
  local copies, waits for them, and re-layouts  1.34 us (1%)
    ppermute x13, starting transfers between devices, swap(): return lax.ppermute(jnp.concatenate(parts, axis=0), 'depth', pairs)  33 us
    pallas_call x15, Pallas kernels, call(): pl.pallas_call(functools.partial(kernel, width), out_shape=shapes, in_spe...  32.7 us
    ppermute x15, starting transfers between devices, send(): return lax.ppermute(block, 'section', pairs) if pairs else block  19.6 us
    ppermute x15, waiting for transfers between devices, send(): return lax.ppermute(block, 'section', pairs) if pairs else block  14.4 us
    ppermute x13, waiting for transfers between devices, swap(): return lax.ppermute(jnp.concatenate(parts, axis=0), 'depth', pairs)  10.5 us
  transfers between devices with their start and end apart: 28, of which 13 were waited for; matrix products, arithmetic and copies ran while one was open for 2% of the time, Pallas kernels for 24%

profile of v7, /device:TPU:13, one launch (start us, length us, event | category | flops | bytes accessed | tf_op | source)
XLA Modules:
  0.0 113.3 jit_solution(3106326456487402773)
XLA Ops:
  0.1 1.3 %collective-permute-start.3 = (bf16[2,4,128,256]{3,2,1,0:T(8,128)(2,1)}, bf16[2,4,128,256]{3,2,1,0:T(8,128)(2,1)S(1)}, u32[]{:S(2)}, u32[]{:S(2)}) collective-permute-start(bf16[2,4,128,256]{3,2,1,0:T(8,128)(2,1)} %bitcast.63), channel_id=1, source_target_pairs={{0,24},{8,16},{1,25},{9,17},{2,26},{10,18},{3,27},{11,19},{4,28},{... | collective-permute-start | bytes 1572872 | tf_op jit(solution)/shard_map/ppermute | solution.py:202
  1.4 1.1 slice_bitcast_fusion.6
  2.5 0.7 collective-permute-start
  3.3 3.1 %collective-permute-start.1 = (bf16[3,128,256]{2,1,0:T(8,128)(2,1)S(1)}, bf16[3,128,256]{2,1,0:T(8,128)(2,1)S(1)}, u32[]{:S(2)}, u32[]{:S(2)}) collective-permute-start(bf16[3,128,256]{2,1,0:T(8,128)(2,1)S(1)} %pad_maximum_fusion.1), channel_id=1, source_target_pairs={{1,2},{2,1},{3,4},{4,3},{5,6},{6,5},{9,10},{10,9},{11,12},{12,11},... | collective-permute-start | bytes 589832 | tf_op jit(solution)/shard_map/ppermute | solution.py:166
  6.4 3.1 %shard_map.55 = (bf16[4,128,256]{2,1,0:T(8,128)(2,1)S(1)}, bf16[4,144,256]{2,1,0:T(8,128)(2,1)S(1)}, bf16[2,128,256]{2,1,0:T(8,128)(2,1)S(1)}, bf16[6912,256]{1,0:T(8,128)(2,1)S(1)}) custom-call(bf16[4,128,256]{2,1,0:T(8,128)(2,1)S(1)} %get-tuple-element.124.p, bf16[4,128,256]{2,1,0:T(8,128)(2,1)S(1)} %get-tuple-element.123.q, bf16[6912,256]{1,0:T(8,128)(2,1)} %bitcast.55), custom_call_target="tpu_custom_call" | custom-call | flops 1 | bytes 1 | tf_op jit(solution)/shard_map/pallas_call | solution.py:115
  9.5 1.0 collective-permute-done.1.q_far.p_far
  10.6 2.7 %shard_map.56 = (bf16[1,128,256]{2,1,0:T(8,128)(2,1)S(1)}, bf16[4,128,256]{2,1,0:T(8,128)(2,1)S(1)}, bf16[1,128,256]{2,1,0:T(8,128)(2,1)S(1)}) custom-call(s32[3]{0:T(128)S(1)} %add_convert_fusion.6.flags, bf16[4,128,256]{2,1,0:T(8,128)(2,1)S(1)} %get-tuple-element.124.p, bf16[4,128,256]{2,1,0:T(8,128)(2,1)S(1)} %get-tuple-element.70.even, ...), custom_call_target="tpu_custom_call" | custom-call | flops 1 | bytes 1 | tf_op jit(solution)/shard_map/pallas_call | solution.py:115
  14.0 2.1 %shard_map.57 = bf16[4,128,256]{2,1,0:T(8,128)(2,1)S(1)} custom-call(bf16[1,128,256]{2,1,0:T(8,128)(2,1)S(1)} %get-tuple-element.80.first_low, bf16[4,128,256]{2,1,0:T(8,128)(2,1)S(1)} %get-tuple-element.78.first_mid, bf16[1,128,256]{2,1,0:T(8,128)(2,1)S(1)} %get-tuple-element.81.first_high, bf16[4,128,256]{2,1,0:T(8,128)(2,1)S(1)} %get-tuple-element.123.q, ...), custom_call_target="tpu_custom_call" | custom-call | flops 1 | bytes 1 | tf_op jit(solution)/shard_map/pallas_call | solution.py:115
  16.5 4.4 %collective-permute-start.5 = (bf16[3,128,256]{2,1,0:T(8,128)(2,1)S(1)}, bf16[3,128,256]{2,1,0:T(8,128)(2,1)S(1)}, u32[]{:S(2)}, u32[]{:S(2)}) collective-permute-start(bf16[3,128,256]{2,1,0:T(8,128)(2,1)S(1)} %pad_maximum_fusion.3), channel_id=1, source_target_pairs={{1,2},{2,1},{3,4},{4,3},{5,6},{6,5},{9,10},{10,9},{11,12},{12,11},... | collective-permute-start | bytes 589832 | tf_op jit(solution)/shard_map/ppermute | solution.py:166
  20.9 0.7 collective-permute-start.10
  22.3 1.2 %shard_map.58 = (bf16[4,128,256]{2,1,0:T(8,128)(2,1)S(1)}, bf16[4,144,256]{2,1,0:T(8,128)(2,1)S(1)}, bf16[2,128,256]{2,1,0:T(8,128)(2,1)S(1)}) custom-call(bf16[4,128,256]{2,1,0:T(8,128)(2,1)S(1)} %get-tuple-element.122.p, bf16[4,128,256]{2,1,0:T(8,128)(2,1)S(1)} %get-tuple-element.121.q, bf16[6912,256]{1,0:T(8,128)(2,1)S(1)} %get-tuple-element.77.weights), custom_call_target="tpu_custom_call" | custom-call | flops 1 | bytes 1 | tf_op jit(solution)/shard_map/pallas_call | solution.py:115
  23.5 0.8 collective-permute-done.5.q_far.p_far
  24.3 2.7 %shard_map.59 = (bf16[1,128,256]{2,1,0:T(8,128)(2,1)S(1)}, bf16[4,128,256]{2,1,0:T(8,128)(2,1)S(1)}, bf16[1,128,256]{2,1,0:T(8,128)(2,1)S(1)}) custom-call(s32[3]{0:T(128)S(1)} %add_convert_fusion.6.flags, bf16[4,128,256]{2,1,0:T(8,128)(2,1)S(1)} %get-tuple-element.122.p, bf16[4,128,256]{2,1,0:T(8,128)(2,1)S(1)} %get-tuple-element.84.even, ...), custom_call_target="tpu_custom_call" | custom-call | flops 1 | bytes 1 | tf_op jit(solution)/shard_map/pallas_call | solution.py:115
  27.0 3.1 %collective-permute-start.6 = (bf16[4,128,256]{2,1,0:T(8,128)(2,1)S(1)}, bf16[4,128,256]{2,1,0:T(8,128)(2,1)S(1)}, u32[]{:S(2)}, u32[]{:S(2)}) collective-permute-start(bf16[4,128,256]{2,1,0:T(8,128)(2,1)S(1)} %get-tuple-element.87.first_mid), channel_id=1, source_target_pairs={{0,8},{8,16},{16,24},{1,9},{9,17},{17,25},{2,10},{10,18},{18,26},{... | collective-permute-start | bytes 786440 | tf_op jit(solution)/shard_map/ppermute | solution.py:202
  30.2 2.1 %shard_map.60 = bf16[4,128,256]{2,1,0:T(8,128)(2,1)S(1)} custom-call(bf16[1,128,256]{2,1,0:T(8,128)(2,1)S(1)} %get-tuple-element.89.first_low, bf16[4,128,256]{2,1,0:T(8,128)(2,1)S(1)} %get-tuple-element.87.first_mid, bf16[1,128,256]{2,1,0:T(8,128)(2,1)S(1)} %get-tuple-element.90.first_high, bf16[4,128,256]{2,1,0:T(8,128)(2,1)S(1)} %get-tuple-element.121.q, ...), custom_call_target="tpu_custom_call" | custom-call | flops 1 | bytes 1 | tf_op jit(solution)/shard_map/pallas_call | solution.py:115
  32.3 1.9 %collective-permute-start.9 = (bf16[4,128,256]{2,1,0:T(8,128)(2,1)S(1)}, bf16[4,128,256]{2,1,0:T(8,128)(2,1)S(1)}, u32[]{:S(2)}, u32[]{:S(2)}) collective-permute-start(bf16[4,128,256]{2,1,0:T(8,128)(2,1)S(1)} %shard_map.60), channel_id=1, source_target_pairs={{0,8},{8,16},{16,24},{1,9},{9,17},{17,25},{2,10},{10,18},{18,26},{... | collective-permute-start | bytes 786440 | tf_op jit(solution)/shard_map/ppermute | solution.py:202
  34.9 4.2 %collective-permute-done.6 = bf16[4,128,256]{2,1,0:T(8,128)(2,1)S(1)} collective-permute-done((bf16[4,128,256]{2,1,0:T(8,128)(2,1)S(1)}, bf16[4,128,256]{2,1,0:T(8,128)(2,1)S(1)}, u32[]{:S(2)}, u32[]{:S(2)}) %collective-permute-start.6) | collective-permute-done | bytes 262176 | tf_op jit(solution)/shard_map/ppermute | solution.py:202
  39.2 5.4 %collective-permute-start.8 = (bf16[1,128,256]{2,1,0:T(8,128)(2,1)S(1)}, bf16[1,128,256]{2,1,0:T(8,128)(2,1)S(1)}, u32[]{:S(2)}, u32[]{:S(2)}) collective-permute-start(bf16[1,128,256]{2,1,0:T(8,128)(2,1)S(1)} %constant_dynamic-slice_fusion.11), channel_id=1, source_target_pairs={{1,2},{2,1},{3,4},{4,3},{5,6},{6,5},{9,10},{10,9},{11,12},{12,11},... | collective-permute-start | bytes 196616 | tf_op jit(solution)/shard_map/ppermute | solution.py:166
  44.7 2.1 %collective-permute-done.8.p_far = bf16[1,128,256]{2,1,0:T(8,128)(2,1)S(1)} collective-permute-done((bf16[1,128,256]{2,1,0:T(8,128)(2,1)S(1)}, bf16[1,128,256]{2,1,0:T(8,128)(2,1)S(1)}, u32[]{:S(2)}, u32[]{:S(2)}) %collective-permute-start.8) | collective-permute-done | bytes 65568 | tf_op jit(solution)/shard_map/ppermute | solution.py:166
  47.4 3.1 %collective-permute-start.13 = (bf16[2,128,256]{2,1,0:T(8,128)(2,1)S(1)}, bf16[2,128,256]{2,1,0:T(8,128)(2,1)S(1)}, u32[]{:S(2)}, u32[]{:S(2)}) collective-permute-start(bf16[2,128,256]{2,1,0:T(8,128)(2,1)S(1)} %get-tuple-element.129), channel_id=1, source_target_pairs={{1,2},{2,1},{3,4},{4,3},{5,6},{6,5},{9,10},{10,9},{11,12},{12,11},... | collective-permute-start | bytes 393224 | tf_op jit(solution)/shard_map/ppermute | solution.py:166
  50.5 0.9 collective-permute-start.15
  51.4 1.2 %shard_map.61 = (bf16[4,128,256]{2,1,0:T(8,128)(2,1)S(1)}, bf16[4,144,256]{2,1,0:T(8,128)(2,1)S(1)}, bf16[2,128,256]{2,1,0:T(8,128)(2,1)S(1)}) custom-call(bf16[4,128,256]{2,1,0:T(8,128)(2,1)S(1)} %fusion.17.p, bf16[4,128,256]{2,1,0:T(8,128)(2,1)S(1)} %fusion.16.q, bf16[6912,256]{1,0:T(8,128)(2,1)S(1)} %get-tuple-element.77.weights), custom_call_target="tpu_custom_call" | custom-call | flops 1 | bytes 1 | tf_op jit(solution)/shard_map/pallas_call | solution.py:115
  52.6 1.1 collective-permute-done.13.q_far
  53.7 2.7 %shard_map.62 = (bf16[1,128,256]{2,1,0:T(8,128)(2,1)S(1)}, bf16[4,128,256]{2,1,0:T(8,128)(2,1)S(1)}, bf16[1,128,256]{2,1,0:T(8,128)(2,1)S(1)}) custom-call(s32[3]{0:T(128)S(1)} %add_convert_fusion.6.flags, bf16[4,128,256]{2,1,0:T(8,128)(2,1)S(1)} %fusion.17.p, bf16[4,128,256]{2,1,0:T(8,128)(2,1)S(1)} %get-tuple-element.94.even, ...), custom_call_target="tpu_custom_call" | custom-call | flops 1 | bytes 1 | tf_op jit(solution)/shard_map/pallas_call | solution.py:115
  56.4 1.9 %collective-permute-start.14 = (bf16[4,128,256]{2,1,0:T(8,128)(2,1)S(1)}, bf16[4,128,256]{2,1,0:T(8,128)(2,1)S(1)}, u32[]{:S(2)}, u32[]{:S(2)}) collective-permute-start(bf16[4,128,256]{2,1,0:T(8,128)(2,1)S(1)} %get-tuple-element.98.first_mid), channel_id=1, source_target_pairs={{0,8},{8,16},{16,24},{1,9},{9,17},{17,25},{2,10},{10,18},{18,26},{... | collective-permute-start | bytes 786440 | tf_op jit(solution)/shard_map/ppermute | solution.py:202
  58.3 2.1 %shard_map.63 = bf16[4,128,256]{2,1,0:T(8,128)(2,1)S(1)} custom-call(bf16[1,128,256]{2,1,0:T(8,128)(2,1)S(1)} %get-tuple-element.99.first_low, bf16[4,128,256]{2,1,0:T(8,128)(2,1)S(1)} %get-tuple-element.98.first_mid, bf16[1,128,256]{2,1,0:T(8,128)(2,1)S(1)} %get-tuple-element.100.first_high, bf16[4,128,256]{2,1,0:T(8,128)(2,1)S(1)} %fusion.16.q, ...), custom_call_target="tpu_custom_call" | custom-call | flops 1 | bytes 1 | tf_op jit(solution)/shard_map/pallas_call | solution.py:115
  60.4 1.9 %collective-permute-start.17 = (bf16[4,128,256]{2,1,0:T(8,128)(2,1)S(1)}, bf16[4,128,256]{2,1,0:T(8,128)(2,1)S(1)}, u32[]{:S(2)}, u32[]{:S(2)}) collective-permute-start(bf16[4,128,256]{2,1,0:T(8,128)(2,1)S(1)} %shard_map.63), channel_id=1, source_target_pairs={{0,8},{8,16},{16,24},{1,9},{9,17},{17,25},{2,10},{10,18},{18,26},{... | collective-permute-start | bytes 786440 | tf_op jit(solution)/shard_map/ppermute | solution.py:202
  62.4 0.7 collective-permute-start.18
  63.1 3.9 %collective-permute-done.14 = bf16[4,128,256]{2,1,0:T(8,128)(2,1)S(1)} collective-permute-done((bf16[4,128,256]{2,1,0:T(8,128)(2,1)S(1)}, bf16[4,128,256]{2,1,0:T(8,128)(2,1)S(1)}, u32[]{:S(2)}, u32[]{:S(2)}) %collective-permute-start.14) | collective-permute-done | bytes 262176 | tf_op jit(solution)/shard_map/ppermute | solution.py:202
  67.1 4.4 %collective-permute-start.16 = (bf16[1,128,256]{2,1,0:T(8,128)(2,1)S(1)}, bf16[1,128,256]{2,1,0:T(8,128)(2,1)S(1)}, u32[]{:S(2)}, u32[]{:S(2)}) collective-permute-start(bf16[1,128,256]{2,1,0:T(8,128)(2,1)S(1)} %constant_dynamic-slice_fusion.7), channel_id=1, source_target_pairs={{1,2},{2,1},{3,4},{4,3},{5,6},{6,5},{9,10},{10,9},{11,12},{12,11},... | collective-permute-start | bytes 196616 | tf_op jit(solution)/shard_map/ppermute | solution.py:166
  71.5 1.0 collective-permute-done.17
  72.6 1.2 %collective-permute-done.16.p_far = bf16[1,128,256]{2,1,0:T(8,128)(2,1)S(1)} collective-permute-done((bf16[1,128,256]{2,1,0:T(8,128)(2,1)S(1)}, bf16[1,128,256]{2,1,0:T(8,128)(2,1)S(1)}, u32[]{:S(2)}, u32[]{:S(2)}) %collective-permute-start.16) | collective-permute-done | bytes 65568 | tf_op jit(solution)/shard_map/ppermute | solution.py:166
  74.4 3.0 %collective-permute-start.20 = (bf16[2,128,256]{2,1,0:T(8,128)(2,1)S(1)}, bf16[2,128,256]{2,1,0:T(8,128)(2,1)S(1)}, u32[]{:S(2)}, u32[]{:S(2)}) collective-permute-start(bf16[2,128,256]{2,1,0:T(8,128)(2,1)S(1)} %get-tuple-element.127), channel_id=1, source_target_pairs={{1,2},{2,1},{3,4},{4,3},{5,6},{6,5},{9,10},{10,9},{11,12},{12,11},... | collective-permute-start | bytes 393224 | tf_op jit(solution)/shard_map/ppermute | solution.py:166
  78.1 1.2 %shard_map.64 = (bf16[4,128,256]{2,1,0:T(8,128)(2,1)S(1)}, bf16[4,144,256]{2,1,0:T(8,128)(2,1)S(1)}, bf16[2,128,256]{2,1,0:T(8,128)(2,1)S(1)}) custom-call(bf16[4,128,256]{2,1,0:T(8,128)(2,1)S(1)} %fusion.15.p, bf16[4,128,256]{2,1,0:T(8,128)(2,1)S(1)} %fusion.14.q, bf16[6912,256]{1,0:T(8,128)(2,1)S(1)} %get-tuple-element.77.weights), custom_call_target="tpu_custom_call" | custom-call | flops 1 | bytes 1 | tf_op jit(solution)/shard_map/pallas_call | solution.py:115
  79.3 1.4 %collective-permute-done.20.q_far = bf16[2,128,256]{2,1,0:T(8,128)(2,1)S(1)} collective-permute-done((bf16[2,128,256]{2,1,0:T(8,128)(2,1)S(1)}, bf16[2,128,256]{2,1,0:T(8,128)(2,1)S(1)}, u32[]{:S(2)}, u32[]{:S(2)}) %collective-permute-start.20) | collective-permute-done | bytes 131104 | tf_op jit(solution)/shard_map/ppermute | solution.py:166
  80.7 2.7 %shard_map.65 = (bf16[1,128,256]{2,1,0:T(8,128)(2,1)S(1)}, bf16[4,128,256]{2,1,0:T(8,128)(2,1)S(1)}, bf16[1,128,256]{2,1,0:T(8,128)(2,1)S(1)}) custom-call(s32[3]{0:T(128)S(1)} %add_convert_fusion.6.flags, bf16[4,128,256]{2,1,0:T(8,128)(2,1)S(1)} %fusion.15.p, bf16[4,128,256]{2,1,0:T(8,128)(2,1)S(1)} %get-tuple-element.104.even, ...), custom_call_target="tpu_custom_call" | custom-call | flops 1 | bytes 1 | tf_op jit(solution)/shard_map/pallas_call | solution.py:115
  83.4 1.9 %collective-permute-start.21 = (bf16[4,128,256]{2,1,0:T(8,128)(2,1)S(1)}, bf16[4,128,256]{2,1,0:T(8,128)(2,1)S(1)}, u32[]{:S(2)}, u32[]{:S(2)}) collective-permute-start(bf16[4,128,256]{2,1,0:T(8,128)(2,1)S(1)} %get-tuple-element.108.first_mid), channel_id=1, source_target_pairs={{8,16},{16,24},{9,17},{17,25},{10,18},{18,26},{11,19},{19,27},{12,... | collective-permute-start | bytes 786440 | tf_op jit(solution)/shard_map/ppermute | solution.py:202
  85.3 2.1 %shard_map.66 = bf16[4,128,256]{2,1,0:T(8,128)(2,1)S(1)} custom-call(bf16[1,128,256]{2,1,0:T(8,128)(2,1)S(1)} %get-tuple-element.109.first_low, bf16[4,128,256]{2,1,0:T(8,128)(2,1)S(1)} %get-tuple-element.108.first_mid, bf16[1,128,256]{2,1,0:T(8,128)(2,1)S(1)} %get-tuple-element.110.first_high, bf16[4,128,256]{2,1,0:T(8,128)(2,1)S(1)} %fusion.14.q, ...), custom_call_target="tpu_custom_call" | custom-call | flops 1 | bytes 1 | tf_op jit(solution)/shard_map/pallas_call | solution.py:115
  87.4 1.9 %collective-permute-start.24 = (bf16[4,128,256]{2,1,0:T(8,128)(2,1)S(1)}, bf16[4,128,256]{2,1,0:T(8,128)(2,1)S(1)}, u32[]{:S(2)}, u32[]{:S(2)}) collective-permute-start(bf16[4,128,256]{2,1,0:T(8,128)(2,1)S(1)} %shard_map.66), channel_id=1, source_target_pairs={{8,16},{16,24},{9,17},{17,25},{10,18},{18,26},{11,19},{19,27},{12,... | collective-permute-start | bytes 786440 | tf_op jit(solution)/shard_map/ppermute | solution.py:202
  90.1 4.0 %collective-permute-done.21 = bf16[4,128,256]{2,1,0:T(8,128)(2,1)S(1)} collective-permute-done((bf16[4,128,256]{2,1,0:T(8,128)(2,1)S(1)}, bf16[4,128,256]{2,1,0:T(8,128)(2,1)S(1)}, u32[]{:S(2)}, u32[]{:S(2)}) %collective-permute-start.21) | collective-permute-done | bytes 262176 | tf_op jit(solution)/shard_map/ppermute | solution.py:202
  94.2 4.2 %collective-permute-start.23 = (bf16[1,128,256]{2,1,0:T(8,128)(2,1)S(1)}, bf16[1,128,256]{2,1,0:T(8,128)(2,1)S(1)}, u32[]{:S(2)}, u32[]{:S(2)}) collective-permute-start(bf16[1,128,256]{2,1,0:T(8,128)(2,1)S(1)} %constant_dynamic-slice_fusion.3), channel_id=1, source_target_pairs={{1,2},{2,1},{3,4},{4,3},{5,6},{6,5},{9,10},{10,9},{11,12},{12,11},... | collective-permute-start | bytes 196616 | tf_op jit(solution)/shard_map/ppermute | solution.py:166
  98.4 1.3 %collective-permute-done.24 = bf16[4,128,256]{2,1,0:T(8,128)(2,1)S(1)} collective-permute-done((bf16[4,128,256]{2,1,0:T(8,128)(2,1)S(1)}, bf16[4,128,256]{2,1,0:T(8,128)(2,1)S(1)}, u32[]{:S(2)}, u32[]{:S(2)}) %collective-permute-start.24) | collective-permute-done | bytes 262176 | tf_op jit(solution)/shard_map/ppermute | solution.py:202
  99.7 0.9 collective-permute-done.23.p_far
  101.4 3.1 %collective-permute-start.27 = (bf16[2,128,256]{2,1,0:T(8,128)(2,1)S(1)}, bf16[2,128,256]{2,1,0:T(8,128)(2,1)S(1)}, u32[]{:S(2)}, u32[]{:S(2)}) collective-permute-start(bf16[2,128,256]{2,1,0:T(8,128)(2,1)S(1)} %get-tuple-element.125), channel_id=1, source_target_pairs={{1,2},{2,1},{3,4},{4,3},{5,6},{6,5},{9,10},{10,9},{11,12},{12,11},... | collective-permute-start | bytes 393224 | tf_op jit(solution)/shard_map/ppermute | solution.py:166
  104.5 1.2 %shard_map.67 = (bf16[4,128,256]{2,1,0:T(8,128)(2,1)S(1)}, bf16[4,144,256]{2,1,0:T(8,128)(2,1)S(1)}, bf16[2,128,256]{2,1,0:T(8,128)(2,1)S(1)}) custom-call(bf16[4,128,256]{2,1,0:T(8,128)(2,1)S(1)} %fusion.13.p, bf16[4,128,256]{2,1,0:T(8,128)(2,1)S(1)} %fusion.12.q, bf16[6912,256]{1,0:T(8,128)(2,1)S(1)} %get-tuple-element.77.weights), custom_call_target="tpu_custom_call" | custom-call | flops 1 | bytes 1 | tf_op jit(solution)/shard_map/pallas_call | solution.py:115
  105.7 2.0 %collective-permute-done.27.q_far = bf16[2,128,256]{2,1,0:T(8,128)(2,1)S(1)} collective-permute-done((bf16[2,128,256]{2,1,0:T(8,128)(2,1)S(1)}, bf16[2,128,256]{2,1,0:T(8,128)(2,1)S(1)}, u32[]{:S(2)}, u32[]{:S(2)}) %collective-permute-start.27) | collective-permute-done | bytes 131104 | tf_op jit(solution)/shard_map/ppermute | solution.py:166
  107.7 2.7 %shard_map.68 = (bf16[1,128,256]{2,1,0:T(8,128)(2,1)S(1)}, bf16[4,128,256]{2,1,0:T(8,128)(2,1)S(1)}, bf16[1,128,256]{2,1,0:T(8,128)(2,1)S(1)}) custom-call(s32[3]{0:T(128)S(1)} %add_convert_fusion.6.flags, bf16[4,128,256]{2,1,0:T(8,128)(2,1)S(1)} %fusion.13.p, bf16[4,128,256]{2,1,0:T(8,128)(2,1)S(1)} %get-tuple-element.114.even, ...), custom_call_target="tpu_custom_call" | custom-call | flops 1 | bytes 1 | tf_op jit(solution)/shard_map/pallas_call | solution.py:115
  110.3 2.9 %shard_map.69 = bf16[2,4,128,256]{3,2,1,0:T(8,128)(2,1)} custom-call(bf16[1,128,256]{2,1,0:T(8,128)(2,1)S(1)} %get-tuple-element.118.first_low, bf16[4,128,256]{2,1,0:T(8,128)(2,1)S(1)} %get-tuple-element.119.first_mid, bf16[1,128,256]{2,1,0:T(8,128)(2,1)S(1)} %get-tuple-element.120.first_high, bf16[4,128,256]{2,1,0:T(8,128)(2,1)S(1)} %fusion.12.q, ...), custom_call_target="tpu_custom_call" | custom-call | flops 1 | bytes 1 | tf_op jit(solution)/shard_map/pallas_call | solution.py:115
  (58 shorter events, 6.4 us)
Async XLA Ops:
  0.1 16.0 %collective-permute-start.3 = (bf16[2,4,128,256]{3,2,1,0:T(8,128)(2,1)}, bf16[2,4,128,256]{3,2,1,0:T(8,128)(2,1)S(1)}, u32[]{:S(2)}, u32[]{:S(2)}) collective-permute-start(bf16[2,4,128,256]{3,2,1,0:T(8,128)(2,1)} %bitcast.63), channel_id=1, source_target_pairs={{0,24},{8,16},{1,25},{9,17},{2,26},{10,18},{3,27},{11,19},{4,28},{... | collective-permute-start | bytes 1572872 | tf_op jit(solution)/shard_map/ppermute | solution.py:202
  2.5 7.0 %collective-permute-start = (bf16[3,128,256]{2,1,0:T(8,128)(2,1)S(1)}, bf16[3,128,256]{2,1,0:T(8,128)(2,1)S(1)}, u32[]{:S(2)}, u32[]{:S(2)}) collective-permute-start(bf16[3,128,256]{2,1,0:T(8,128)(2,1)S(1)} %pad_maximum_fusion), channel_id=1, source_target_pairs={{0,1},{1,0},{2,3},{3,2},{4,5},{5,4},{6,7},{7,6},{8,9},{9,8},{10,11... | collective-permute-start | bytes 589832 | tf_op jit(solution)/shard_map/ppermute | solution.py:166
  3.3 7.3 %collective-permute-start.1 = (bf16[3,128,256]{2,1,0:T(8,128)(2,1)S(1)}, bf16[3,128,256]{2,1,0:T(8,128)(2,1)S(1)}, u32[]{:S(2)}, u32[]{:S(2)}) collective-permute-start(bf16[3,128,256]{2,1,0:T(8,128)(2,1)S(1)} %pad_maximum_fusion.1), channel_id=1, source_target_pairs={{1,2},{2,1},{3,4},{4,3},{5,6},{6,5},{9,10},{10,9},{11,12},{12,11},... | collective-permute-start | bytes 589832 | tf_op jit(solution)/shard_map/ppermute | solution.py:166
  10.6 3.4 %copy-start = (bf16[1,3,3,3,256,256]{5,4,3,2,1,0:T(8,128)(2,1)S(1)}, bf16[1,3,3,3,256,256]{5,4,3,2,1,0:T(8,128)(2,1)}, u32[]{:S(2)}) copy-start(bf16[1,3,3,3,256,256]{5,4,3,2,1,0:T(8,128)(2,1)} %param.9) | copy-start | bytes 10616836
  13.3 8.4 %collective-permute-start.2 = (bf16[4,128,256]{2,1,0:T(8,128)(2,1)S(1)}, bf16[4,128,256]{2,1,0:T(8,128)(2,1)S(1)}, u32[]{:S(2)}, u32[]{:S(2)}) collective-permute-start(bf16[4,128,256]{2,1,0:T(8,128)(2,1)S(1)} %get-tuple-element.78.first_mid), channel_id=1, source_target_pairs={{0,8},{1,9},{2,10},{3,11},{4,12},{5,13},{6,14},{7,15}} | collective-permute-start | bytes 786440 | tf_op jit(solution)/shard_map/ppermute | solution.py:202
  14.0 2.2 %copy-start.1 = (bf16[3,2,4,16,8,256]{5,4,3,2,1,0:T(8,128)(2,1)S(1)}, bf16[3,2,4,16,8,256]{5,4,3,2,1,0:T(8,128)(2,1)}, u32[]{:S(2)}) copy-start(bf16[3,2,4,16,8,256]{5,4,3,2,1,0:T(8,128)(2,1)} %param.7) | copy-start | bytes 4718596
  14.0 2.2 %copy-start.2 = (bf16[1,2,4,16,8,256]{5,4,3,2,1,0:T(8,128)(2,1)S(1)}, bf16[1,2,4,16,8,256]{5,4,3,2,1,0:T(8,128)(2,1)}, u32[]{:S(2)}) copy-start(bf16[1,2,4,16,8,256]{5,4,3,2,1,0:T(8,128)(2,1)} %param.5) | copy-start | bytes 1572868
  16.5 7.9 %collective-permute-start.5 = (bf16[3,128,256]{2,1,0:T(8,128)(2,1)S(1)}, bf16[3,128,256]{2,1,0:T(8,128)(2,1)S(1)}, u32[]{:S(2)}, u32[]{:S(2)}) collective-permute-start(bf16[3,128,256]{2,1,0:T(8,128)(2,1)S(1)} %pad_maximum_fusion.3), channel_id=1, source_target_pairs={{1,2},{2,1},{3,4},{4,3},{5,6},{6,5},{9,10},{10,9},{11,12},{12,11},... | collective-permute-start | bytes 589832 | tf_op jit(solution)/shard_map/ppermute | solution.py:166
  20.9 3.5 %collective-permute-start.4 = (bf16[3,128,256]{2,1,0:T(8,128)(2,1)S(1)}, bf16[3,128,256]{2,1,0:T(8,128)(2,1)S(1)}, u32[]{:S(2)}, u32[]{:S(2)}) collective-permute-start(bf16[3,128,256]{2,1,0:T(8,128)(2,1)S(1)} %pad_maximum_fusion.2), channel_id=1, source_target_pairs={{0,1},{1,0},{2,3},{3,2},{4,5},{5,4},{6,7},{7,6},{8,9},{9,8},{10,11... | collective-permute-start | bytes 589832 | tf_op jit(solution)/shard_map/ppermute | solution.py:166
  20.9 13.3 %collective-permute-start.10 = (bf16[4,128,256]{2,1,0:T(8,128)(2,1)S(1)}, bf16[4,128,256]{2,1,0:T(8,128)(2,1)S(1)}, u32[]{:S(2)}, u32[]{:S(2)}) collective-permute-start(bf16[4,128,256]{2,1,0:T(8,128)(2,1)S(1)} %shard_map.57), channel_id=1, source_target_pairs={{0,8},{1,9},{2,10},{3,11},{4,12},{5,13},{6,14},{7,15}} | collective-permute-start | bytes 786440 | tf_op jit(solution)/shard_map/ppermute | solution.py:202
  21.6 13.3 %collective-permute-start.7 = (bf16[4,128,256]{2,1,0:T(8,128)(2,1)S(1)}, bf16[4,128,256]{2,1,0:T(8,128)(2,1)S(1)}, u32[]{:S(2)}, u32[]{:S(2)}) collective-permute-start(bf16[4,128,256]{2,1,0:T(8,128)(2,1)S(1)} %collective-permute-done.2), channel_id=1, source_target_pairs={{8,24},{9,25},{10,26},{11,27},{12,28},{13,29},{14,30},{15,31}} | collective-permute-start | bytes 786440 | tf_op jit(solution)/shard_map/ppermute | solution.py:202
  27.0 12.0 %collective-permute-start.6 = (bf16[4,128,256]{2,1,0:T(8,128)(2,1)S(1)}, bf16[4,128,256]{2,1,0:T(8,128)(2,1)S(1)}, u32[]{:S(2)}, u32[]{:S(2)}) collective-permute-start(bf16[4,128,256]{2,1,0:T(8,128)(2,1)S(1)} %get-tuple-element.87.first_mid), channel_id=1, source_target_pairs={{0,8},{8,16},{16,24},{1,9},{9,17},{17,25},{2,10},{10,18},{18,26},{... | collective-permute-start | bytes 786440 | tf_op jit(solution)/shard_map/ppermute | solution.py:202
  32.3 12.4 %collective-permute-start.9 = (bf16[4,128,256]{2,1,0:T(8,128)(2,1)S(1)}, bf16[4,128,256]{2,1,0:T(8,128)(2,1)S(1)}, u32[]{:S(2)}, u32[]{:S(2)}) collective-permute-start(bf16[4,128,256]{2,1,0:T(8,128)(2,1)S(1)} %shard_map.60), channel_id=1, source_target_pairs={{0,8},{8,16},{16,24},{1,9},{9,17},{17,25},{2,10},{10,18},{18,26},{... | collective-permute-start | bytes 786440 | tf_op jit(solution)/shard_map/ppermute | solution.py:202
  34.2 12.5 %collective-permute-start.11 = (bf16[4,128,256]{2,1,0:T(8,128)(2,1)S(1)}, bf16[4,128,256]{2,1,0:T(8,128)(2,1)S(1)}, u32[]{:S(2)}, u32[]{:S(2)}) collective-permute-start(bf16[4,128,256]{2,1,0:T(8,128)(2,1)S(1)} %collective-permute-done.10), channel_id=1, source_target_pairs={{8,24},{9,25},{10,26},{11,27},{12,28},{13,29},{14,30},{15,31}} | collective-permute-start | bytes 786440 | tf_op jit(solution)/shard_map/ppermute | solution.py:202
  39.2 7.5 %collective-permute-start.8 = (bf16[1,128,256]{2,1,0:T(8,128)(2,1)S(1)}, bf16[1,128,256]{2,1,0:T(8,128)(2,1)S(1)}, u32[]{:S(2)}, u32[]{:S(2)}) collective-permute-start(bf16[1,128,256]{2,1,0:T(8,128)(2,1)S(1)} %constant_dynamic-slice_fusion.11), channel_id=1, source_target_pairs={{1,2},{2,1},{3,4},{4,3},{5,6},{6,5},{9,10},{10,9},{11,12},{12,11},... | collective-permute-start | bytes 196616 | tf_op jit(solution)/shard_map/ppermute | solution.py:166
  46.9 6.7 %collective-permute-start.12 = (bf16[3,128,256]{2,1,0:T(8,128)(2,1)S(1)}, bf16[3,128,256]{2,1,0:T(8,128)(2,1)S(1)}, u32[]{:S(2)}, u32[]{:S(2)}) collective-permute-start(bf16[3,128,256]{2,1,0:T(8,128)(2,1)S(1)} %pad_maximum_fusion.4), channel_id=1, source_target_pairs={{0,1},{1,0},{2,3},{3,2},{4,5},{5,4},{6,7},{7,6},{8,9},{9,8},{10,11... | collective-permute-start | bytes 589832 | tf_op jit(solution)/shard_map/ppermute | solution.py:166
  47.4 6.3 %collective-permute-start.13 = (bf16[2,128,256]{2,1,0:T(8,128)(2,1)S(1)}, bf16[2,128,256]{2,1,0:T(8,128)(2,1)S(1)}, u32[]{:S(2)}, u32[]{:S(2)}) collective-permute-start(bf16[2,128,256]{2,1,0:T(8,128)(2,1)S(1)} %get-tuple-element.129), channel_id=1, source_target_pairs={{1,2},{2,1},{3,4},{4,3},{5,6},{6,5},{9,10},{10,9},{11,12},{12,11},... | collective-permute-start | bytes 393224 | tf_op jit(solution)/shard_map/ppermute | solution.py:166
  50.5 12.5 %collective-permute-start.15 = (bf16[4,128,256]{2,1,0:T(8,128)(2,1)S(1)}, bf16[4,128,256]{2,1,0:T(8,128)(2,1)S(1)}, u32[]{:S(2)}, u32[]{:S(2)}) collective-permute-start(bf16[4,128,256]{2,1,0:T(8,128)(2,1)S(1)} %collective-permute-done.6), channel_id=1, source_target_pairs={{8,24},{9,25},{10,26},{11,27},{12,28},{13,29},{14,30},{15,31}} | collective-permute-start | bytes 786440 | tf_op jit(solution)/shard_map/ppermute | solution.py:202
  56.4 10.6 %collective-permute-start.14 = (bf16[4,128,256]{2,1,0:T(8,128)(2,1)S(1)}, bf16[4,128,256]{2,1,0:T(8,128)(2,1)S(1)}, u32[]{:S(2)}, u32[]{:S(2)}) collective-permute-start(bf16[4,128,256]{2,1,0:T(8,128)(2,1)S(1)} %get-tuple-element.98.first_mid), channel_id=1, source_target_pairs={{0,8},{8,16},{16,24},{1,9},{9,17},{17,25},{2,10},{10,18},{18,26},{... | collective-permute-start | bytes 786440 | tf_op jit(solution)/shard_map/ppermute | solution.py:202
  60.4 12.1 %collective-permute-start.17 = (bf16[4,128,256]{2,1,0:T(8,128)(2,1)S(1)}, bf16[4,128,256]{2,1,0:T(8,128)(2,1)S(1)}, u32[]{:S(2)}, u32[]{:S(2)}) collective-permute-start(bf16[4,128,256]{2,1,0:T(8,128)(2,1)S(1)} %shard_map.63), channel_id=1, source_target_pairs={{0,8},{8,16},{16,24},{1,9},{9,17},{17,25},{2,10},{10,18},{18,26},{... | collective-permute-start | bytes 786440 | tf_op jit(solution)/shard_map/ppermute | solution.py:202
  62.4 11.4 %collective-permute-start.18 = (bf16[4,128,256]{2,1,0:T(8,128)(2,1)S(1)}, bf16[4,128,256]{2,1,0:T(8,128)(2,1)S(1)}, u32[]{:S(2)}, u32[]{:S(2)}) collective-permute-start(bf16[4,128,256]{2,1,0:T(8,128)(2,1)S(1)} %collective-permute-done.9), channel_id=1, source_target_pairs={{8,24},{9,25},{10,26},{11,27},{12,28},{13,29},{14,30},{15,31}} | collective-permute-start | bytes 786440 | tf_op jit(solution)/shard_map/ppermute | solution.py:202
  67.1 6.7 %collective-permute-start.16 = (bf16[1,128,256]{2,1,0:T(8,128)(2,1)S(1)}, bf16[1,128,256]{2,1,0:T(8,128)(2,1)S(1)}, u32[]{:S(2)}, u32[]{:S(2)}) collective-permute-start(bf16[1,128,256]{2,1,0:T(8,128)(2,1)S(1)} %constant_dynamic-slice_fusion.7), channel_id=1, source_target_pairs={{1,2},{2,1},{3,4},{4,3},{5,6},{6,5},{9,10},{10,9},{11,12},{12,11},... | collective-permute-start | bytes 196616 | tf_op jit(solution)/shard_map/ppermute | solution.py:166
  73.9 6.7 %collective-permute-start.19 = (bf16[3,128,256]{2,1,0:T(8,128)(2,1)S(1)}, bf16[3,128,256]{2,1,0:T(8,128)(2,1)S(1)}, u32[]{:S(2)}, u32[]{:S(2)}) collective-permute-start(bf16[3,128,256]{2,1,0:T(8,128)(2,1)S(1)} %pad_maximum_fusion.5), channel_id=1, source_target_pairs={{0,1},{1,0},{2,3},{3,2},{4,5},{5,4},{6,7},{7,6},{8,9},{9,8},{10,11... | collective-permute-start | bytes 589832 | tf_op jit(solution)/shard_map/ppermute | solution.py:166
  74.4 6.3 %collective-permute-start.20 = (bf16[2,128,256]{2,1,0:T(8,128)(2,1)S(1)}, bf16[2,128,256]{2,1,0:T(8,128)(2,1)S(1)}, u32[]{:S(2)}, u32[]{:S(2)}) collective-permute-start(bf16[2,128,256]{2,1,0:T(8,128)(2,1)S(1)} %get-tuple-element.127), channel_id=1, source_target_pairs={{1,2},{2,1},{3,4},{4,3},{5,6},{6,5},{9,10},{10,9},{11,12},{12,11},... | collective-permute-start | bytes 393224 | tf_op jit(solution)/shard_map/ppermute | solution.py:166
  77.4 12.7 %collective-permute-start.22 = (bf16[4,128,256]{2,1,0:T(8,128)(2,1)S(1)}, bf16[4,128,256]{2,1,0:T(8,128)(2,1)S(1)}, u32[]{:S(2)}, u32[]{:S(2)}) collective-permute-start(bf16[4,128,256]{2,1,0:T(8,128)(2,1)S(1)} %collective-permute-done.14), channel_id=1, source_target_pairs={{8,24},{9,25},{10,26},{11,27},{12,28},{13,29},{14,30},{15,31}} | collective-permute-start | bytes 786440 | tf_op jit(solution)/shard_map/ppermute | solution.py:202
  83.4 10.7 %collective-permute-start.21 = (bf16[4,128,256]{2,1,0:T(8,128)(2,1)S(1)}, bf16[4,128,256]{2,1,0:T(8,128)(2,1)S(1)}, u32[]{:S(2)}, u32[]{:S(2)}) collective-permute-start(bf16[4,128,256]{2,1,0:T(8,128)(2,1)S(1)} %get-tuple-element.108.first_mid), channel_id=1, source_target_pairs={{8,16},{16,24},{9,17},{17,25},{10,18},{18,26},{11,19},{19,27},{12,... | collective-permute-start | bytes 786440 | tf_op jit(solution)/shard_map/ppermute | solution.py:202
  87.4 12.2 %collective-permute-start.24 = (bf16[4,128,256]{2,1,0:T(8,128)(2,1)S(1)}, bf16[4,128,256]{2,1,0:T(8,128)(2,1)S(1)}, u32[]{:S(2)}, u32[]{:S(2)}) collective-permute-start(bf16[4,128,256]{2,1,0:T(8,128)(2,1)S(1)} %shard_map.66), channel_id=1, source_target_pairs={{8,16},{16,24},{9,17},{17,25},{10,18},{18,26},{11,19},{19,27},{12,... | collective-permute-start | bytes 786440 | tf_op jit(solution)/shard_map/ppermute | solution.py:202
  89.4 11.3 %collective-permute-start.25 = (bf16[4,128,256]{2,1,0:T(8,128)(2,1)S(1)}, bf16[4,128,256]{2,1,0:T(8,128)(2,1)S(1)}, u32[]{:S(2)}, u32[]{:S(2)}) collective-permute-start(bf16[4,128,256]{2,1,0:T(8,128)(2,1)S(1)} %collective-permute-done.17), channel_id=1, source_target_pairs={{8,24},{9,25},{10,26},{11,27},{12,28},{13,29},{14,30},{15,31}} | collective-permute-start | bytes 786440 | tf_op jit(solution)/shard_map/ppermute | solution.py:202
  94.2 6.4 %collective-permute-start.23 = (bf16[1,128,256]{2,1,0:T(8,128)(2,1)S(1)}, bf16[1,128,256]{2,1,0:T(8,128)(2,1)S(1)}, u32[]{:S(2)}, u32[]{:S(2)}) collective-permute-start(bf16[1,128,256]{2,1,0:T(8,128)(2,1)S(1)} %constant_dynamic-slice_fusion.3), channel_id=1, source_target_pairs={{1,2},{2,1},{3,4},{4,3},{5,6},{6,5},{9,10},{10,9},{11,12},{12,11},... | collective-permute-start | bytes 196616 | tf_op jit(solution)/shard_map/ppermute | solution.py:166
  100.8 6.8 %collective-permute-start.26 = (bf16[3,128,256]{2,1,0:T(8,128)(2,1)S(1)}, bf16[3,128,256]{2,1,0:T(8,128)(2,1)S(1)}, u32[]{:S(2)}, u32[]{:S(2)}) collective-permute-start(bf16[3,128,256]{2,1,0:T(8,128)(2,1)S(1)} %pad_maximum_fusion.6), channel_id=1, source_target_pairs={{0,1},{1,0},{2,3},{3,2},{4,5},{5,4},{6,7},{7,6},{8,9},{9,8},{10,11... | collective-permute-start | bytes 589832 | tf_op jit(solution)/shard_map/ppermute | solution.py:166
  101.4 6.3 %collective-permute-start.27 = (bf16[2,128,256]{2,1,0:T(8,128)(2,1)S(1)}, bf16[2,128,256]{2,1,0:T(8,128)(2,1)S(1)}, u32[]{:S(2)}, u32[]{:S(2)}) collective-permute-start(bf16[2,128,256]{2,1,0:T(8,128)(2,1)S(1)} %get-tuple-element.125), channel_id=1, source_target_pairs={{1,2},{2,1},{3,4},{4,3},{5,6},{6,5},{9,10},{10,9},{11,12},{12,11},... | collective-permute-start | bytes 393224 | tf_op jit(solution)/shard_map/ppermute | solution.py:166

commit v8 on v7

v8 whole, which is shorter than its diff:
```python
import functools

import jax
import jax.numpy as jnp
from jax import lax
from jax.experimental import pallas as pl
from jax.experimental.pallas import tpu as pltpu
from jax.sharding import PartitionSpec as P

EPS = 1e-05
VMEM_LIMIT = 12 * 1024 * 1024


def act(values):
    values = values.astype(jnp.float32)
    scaled = values * lax.rsqrt(jnp.mean(values * values, axis=-1, keepdims=True) + EPS)
    return scaled * (0.5 + 0.5 * jnp.tanh(0.5 * scaled))


def fill(even, odd, at, values, width):
    planes, _, chans = values.shape
    field = act(values)
    edge = jnp.zeros((planes, width, chans), jnp.float32)
    even[pl.ds(at, planes)] = field.astype(jnp.bfloat16)
    odd[pl.ds(at, planes)] = jnp.concatenate([edge, field, edge], axis=1).astype(jnp.bfloat16)


def convolve(taps, weights, width):
    planes, voxels, chans = taps[0].shape
    slab = jnp.concatenate([part.reshape(planes * voxels, chans) for part in taps], axis=-1)
    total = None
    for k in (1, 0, 2):
        columns = jnp.concatenate([weights[(3 * n + k) * chans : (3 * n + k + 1) * chans] for n in range(9)], axis=0)
        part = jnp.dot(slab, columns, preferred_element_type=jnp.float32).reshape(-1, width, chans)
        column = lax.broadcasted_iota(jnp.int32, part.shape, 1)
        if k == 0:
            part = jnp.where(column == 0, 0.0, pltpu.roll(part, 1, 1))
        elif k == 2:
            part = jnp.where(column == width - 1, 0.0, pltpu.roll(part, width - 1, 1))
        total = part if total is None else total + part
    return total.reshape(planes, voxels, chans)


def planes_at(even, odd, start, count, width):
    voxels = even.shape[1]
    return [
        even[start : start + count] if j == 1 else odd[start : start + count, j * width : j * width + voxels]
        for j in range(3)
    ]


def inner_kernel(width, field, weights, even, odd, total):
    planes = field.shape[0]
    fill(even, odd, 0, field[...], width)
    taps = [part for i in range(3) for part in planes_at(even, odd, i, planes - 2, width)]
    total[...] = convolve(taps, weights, width)


def loading_kernel(width, field, weights_hbm, even, odd, total, weights, sem):
    copy = pltpu.make_async_copy(weights_hbm, weights, sem)
    copy.start()
    planes = field.shape[0]
    fill(even, odd, 0, field[...], width)
    taps = [part for i in range(3) for part in planes_at(even, odd, i, planes - 2, width)]
    copy.wait()
    total[...] = convolve(taps, weights, width)


def edge_kernel(width, flags, near, far, even, odd, inner, weights, *rest):
    *added, out, edge_even, edge_odd = rest
    planes = even.shape[0]
    above = flags[0] > 0
    near, far = near[...].astype(jnp.float32), far[...].astype(jnp.float32)
    fill(edge_even, edge_odd, 0, jnp.where(above, far, near), width)
    fill(edge_even, edge_odd, 1, jnp.where(above, near, far), width)
    halo = lambda plane: planes_at(edge_even, edge_odd, plane, 1, width)
    own = lambda plane: planes_at(even, odd, plane, 1, width)
    sources = ((halo(0), own(planes - 2)), (own(0), own(planes - 1)), (own(1), halo(1)))
    taps = [jnp.concatenate(pair, axis=0) for source in sources for pair in zip(*source)]
    total = convolve(taps, weights, width)
    pieces = ((0, 1, total[:1]), (1, planes - 2, inner[...]), (planes - 1, 1, total[1:]))
    for start, count, piece in pieces:
        where = pl.ds(start, count)
        if added:
            piece = added[-1][where].astype(jnp.float32) + piece
        if len(added) == 2:
            out[0, where] = added[0][where]
            out[1, where] = piece.astype(out.dtype)
        else:
            out[where] = piece.astype(out.dtype)


def call(kernel, outputs, scratch, arguments, width):
    specs = [pl.BlockSpec(memory_space=pltpu.VMEM) for _ in arguments]
    if kernel is edge_kernel:
        specs[0] = pl.BlockSpec(memory_space=pltpu.SMEM)
    if kernel is loading_kernel:
        specs[-1] = pl.BlockSpec(memory_space=pltpu.HBM)
    return pl.pallas_call(
        functools.partial(kernel, width),
        out_shape=[jax.ShapeDtypeStruct(shape, dtype) for shape, dtype in outputs],
        in_specs=specs,
        out_specs=[pl.BlockSpec(memory_space=pltpu.VMEM) for _ in outputs],
        scratch_shapes=[pltpu.VMEM(shape, jnp.bfloat16) if shape else pltpu.SemaphoreType.DMA for shape in scratch],
        compiler_params=pltpu.CompilerParams(vmem_limit_bytes=VMEM_LIMIT),
        cost_estimate=pl.CostEstimate(flops=1, bytes_accessed=1, transcendentals=0),
    )(*arguments)


def stored(planes, voxels, chans, width):
    return (planes, voxels, chans), (planes, voxels + 2 * width, chans)


def inner_planes(field, weights, width, load=False):
    planes, voxels, chans = field.shape
    outputs = [(shape, jnp.bfloat16) for shape in stored(planes, voxels, chans, width)]
    outputs.append(((planes - 2, voxels, chans), jnp.float32))
    if load:
        weights = pltpu.with_memory_space_constraint(weights, pltpu.HBM)
        outputs.append((weights.shape, jnp.bfloat16))
        return call(loading_kernel, outputs, [()], (field, weights), width)
    return *call(inner_kernel, outputs, [], (field, weights), width), weights


def all_planes(flags, near, far, kept, weights, added, width):
    shape = kept[0].shape
    _, voxels, chans = shape
    output = ((2, *shape) if len(added) == 2 else shape, jnp.bfloat16 if added else jnp.float32)
    arguments = (flags, near, far, *kept, weights, *added)
    (out,) = call(edge_kernel, [output], stored(2, voxels, chans, width), arguments, width)
    return out


def swap(turn, starts, block):
    count = lax.axis_size("depth")
    pairs = [pair for i in range(turn, count - 1, 2) for pair in ((i, i + 1), (i + 1, i))]
    return lax.ppermute(lax.dynamic_slice_in_dim(block, starts[turn], 1, axis=0), "depth", pairs)


def local(resident, previous, incoming, first_weights, second_weights):
    section = lax.axis_index("section")
    sections = lax.axis_size("section")
    half = sections // 2
    depth = lax.axis_index("depth")
    ticks = incoming.shape[0] + 1
    _, _, planes, rows, width, chans = resident.shape
    voxels = rows * width
    across = [(j, sections - 1 - j) for j in range(1, half - 1)]

    above = depth % 2 == 0
    places = {
        "flags": jnp.stack([above]).astype(jnp.int32),
        "starts": (jnp.where(above, planes - 1, 0), jnp.where(above, 0, planes - 1)),
        "first": section == 0,
        "second": section == 1,
        "last": section == sections - 1,
        "decoder": section >= half,
        "direct": (section > half) & (section < sections - 1) if across else (),
    }
    places, resident, previous, incoming, first_weights, second_weights = lax.optimization_barrier(
        (places, resident, previous, incoming, first_weights, second_weights)
    )
    flags, starts = places["flags"], places["starts"]

    flat = lambda a: a.reshape(a.shape[0], 2, planes, voxels, chans)
    resident, previous, incoming = flat(resident)[0], flat(previous)[0], flat(incoming)
    w_one = first_weights.reshape(27 * chans, chans)
    w_two = second_weights.reshape(27 * chans, chans)

    def send(block, pairs):
        return lax.ppermute(block, "section", pairs) if pairs else block

    def join(held, skip):
        total = (held.astype(jnp.float32) + skip.astype(jnp.float32)).astype(jnp.bfloat16)
        return jnp.where(places["decoder"], total, held)

    newer, older, relayed, direct = {}, {}, {}, {}

    def arrived(slot, stream):
        fresh = incoming[min(slot, ticks - 1) - 1, stream]
        if slot == 1:
            return jnp.where(places["first"], fresh, join(resident[stream], mirrored[stream]))
        held = jnp.where(places["second"], older[stream], newer[stream])
        skip = jnp.where(places["last"], relayed[stream], newer[stream])
        if across:
            skip = jnp.where(places["direct"], direct[stream], skip)
        return jnp.where(places["first"], fresh, join(held, skip))

    def swaps(block):
        return swap(0, starts, block), swap(1, starts, block)

    mirrored = send(previous, [(j, sections - 1 - j) for j in range(half)])
    p, q = resident
    halos = swaps(q)
    for slot in range(ticks + 1):
        if slot > 1:
            q = arrived(slot, 1)
            halos = swaps(q)
        *kept, w_one = inner_planes(q, w_one, width, slot == 0)
        first = all_planes(flags, *halos, kept, w_one, (p,) if slot < 2 else (), width)
        if slot > 1:
            p = arrived(slot, 0)
            first = (p.astype(jnp.float32) + first).astype(jnp.bfloat16)
        halos = swaps(first)
        *kept, _ = inner_planes(first, w_two, width)
        if slot == 0:
            mirrored, _ = lax.optimization_barrier((mirrored, first))
            following = arrived(1, 0), arrived(1, 1)
            following += (swaps(following[1]),)
        second = all_planes(flags, *halos, kept, w_two, (first, q) if slot == ticks else (q,), width)
        if slot == 0:
            p, q, halos = following
            halos, second = lax.optimization_barrier((halos, second))
        if slot < ticks:
            onward = [(j, j + 1) for j in range(1, sections - 1)] if slot > 0 else []
            if slot < ticks - 1:
                onward = [(0, 1)] + onward
            first, second = lax.optimization_barrier((first, second))
            received, relays = {1: send(second, onward), 0: send(first, onward)}, {}
            if slot > 0:
                held, _ = lax.optimization_barrier((newer, second))
                relays = {k: send(held[k], [(1, sections - 1)]) for k in (1, 0)}
                if across:
                    direct = {0: send(first, across), 1: send(second, across)}
            older, newer, relayed = newer, received, relays
    result = second
    return result.reshape(1, 2, planes, rows, width, chans)


def solution(mesh):
    in_specs = (
        P("section", None, "depth", None, None, None),
        P("section", None, "depth", None, None, None),
        P(None, None, "depth", None, None, None),
        P("section", None, None, None, None, None),
        P("section", None, None, None, None, None),
    )
    out_specs = P("section", None, "depth", None, None, None)
    return jax.shard_map(local, mesh=mesh, in_specs=in_specs, out_specs=out_specs, check_vma=False)
```

time: 114 us -> 118 us (1.035)
  starting transfers between devices: 52.6 us -> 67 us
  Pallas kernels: 32.7 us -> 26.6 us
  waiting for transfers between devices: 24.9 us -> 20.8 us
    ppermute x13 -> x20, starting transfers between devices: 33 us -> 41.2 us  [swap(): lax.ppermute(lax.dynamic_slice_in_dim(block, starts[turn], 1, axis=0), 'd...]
    ppermute x15, starting transfers between devices: 19.6 us -> 25.8 us  [send(): return lax.ppermute(block, 'section', pairs) if pairs else block]
    pallas_call x15 -> x20, Pallas kernels: 32.7 us -> 26.6 us  [call(): pl.pallas_call(functools.partial(kernel, width), out_shape=[jax.ShapeDtyp...]
    ppermute x13 -> x20, waiting for transfers between devices: 10.5 us -> 8.41 us  [swap(): lax.ppermute(lax.dynamic_slice_in_dim(block, starts[turn], 1, axis=0), 'd...]
    ppermute x15, waiting for transfers between devices: 14.4 us -> 12.3 us  [send(): return lax.ppermute(block, 'section', pairs) if pairs else block]
  transfers between devices with their start and end apart: 28 -> 35, of which waited for: 13 -> 11; matrix products, arithmetic and copies ran while one was open for 2% -> 1% of each run, Pallas kernels for 24% -> 19%
where the time goes in v8:
time: 118 us; the launch traced here: 117 us
  starting transfers between devices  67 us (57%)
  Pallas kernels  26.6 us (23%)
  waiting for transfers between devices  20.8 us (18%)
  local copies, waits for them, and re-layouts  1.27 us (1%)
    ppermute x20, starting transfers between devices, swap(): lax.ppermute(lax.dynamic_slice_in_dim(block, starts[turn], 1, axis=0), 'd...  41.2 us
    pallas_call x20, Pallas kernels, call(): pl.pallas_call(functools.partial(kernel, width), out_shape=[jax.ShapeDtyp...  26.6 us
    ppermute x15, starting transfers between devices, send(): return lax.ppermute(block, 'section', pairs) if pairs else block  25.8 us
    ppermute x15, waiting for transfers between devices, send(): return lax.ppermute(block, 'section', pairs) if pairs else block  12.3 us
    ppermute x20, waiting for transfers between devices, swap(): lax.ppermute(lax.dynamic_slice_in_dim(block, starts[turn], 1, axis=0), 'd...  8.41 us
  transfers between devices with their start and end apart: 35, of which 11 were waited for; matrix products, arithmetic and copies ran while one was open for 1% of the time, Pallas kernels for 19%

profile of v8, /device:TPU:13, one launch (start us, length us, event | category | flops | bytes accessed | tf_op | source)
XLA Modules:
  0.0 117.4 jit_solution(9373341651205177280)
XLA Ops:
  0.0 1.3 %collective-permute-start.2 = (bf16[2,4,128,256]{3,2,1,0:T(8,128)(2,1)}, bf16[2,4,128,256]{3,2,1,0:T(8,128)(2,1)S(1)}, u32[]{:S(2)}, u32[]{:S(2)}) collective-permute-start(bf16[2,4,128,256]{3,2,1,0:T(8,128)(2,1)} %bitcast.66), channel_id=1, source_target_pairs={{0,24},{8,16},{1,25},{9,17},{2,26},{10,18},{3,27},{11,19},{4,28},{... | collective-permute-start | bytes 1572872 | tf_op jit(solution)/shard_map/ppermute | solution.py:171
  3.1 3.1 %collective-permute-start.1 = (bf16[1,128,256]{2,1,0:T(8,128)(2,1)S(1)}, bf16[1,128,256]{2,1,0:T(8,128)(2,1)S(1)}, u32[]{:S(2)}, u32[]{:S(2)}) collective-permute-start(bf16[1,128,256]{2,1,0:T(8,128)(2,1)S(1)} %get-tuple-element.149), channel_id=1, source_target_pairs={{1,2},{2,1},{3,4},{4,3},{5,6},{6,5},{9,10},{10,9},{11,12},{12,11},... | collective-permute-start | bytes 196616 | tf_op jit(solution)/shard_map/ppermute | solution.py:137
  6.2 3.2 %shard_map.55 = (bf16[4,128,256]{2,1,0:T(8,128)(2,1)S(1)}, bf16[4,144,256]{2,1,0:T(8,128)(2,1)S(1)}, f32[2,128,256]{2,1,0:T(8,128)S(1)}, bf16[6912,256]{1,0:T(8,128)(2,1)S(1)}) custom-call(bf16[4,128,256]{2,1,0:T(8,128)(2,1)S(1)} %get-tuple-element.130.field.rest_0_, bf16[6912,256]{1,0:T(8,128)(2,1)} %bitcast.58), custom_call_target="tpu_custom_call" | custom-call | flops 1 | bytes 1 | tf_op jit(solution)/shard_map/pallas_call | solution.py:99
  9.5 1.2 %shard_map.56.field = bf16[4,128,256]{2,1,0:T(8,128)(2,1)S(1)} custom-call(s32[1]{0:T(128)} %bitcast.flags, bf16[1,128,256]{2,1,0:T(8,128)(2,1)S(1)} %collective-permute-done.near, bf16[1,128,256]{2,1,0:T(8,128)(2,1)S(1)} %collective-permute-done.1.far, bf16[4,128,256]{2,1,0:T(8,128)(2,1)S(1)} %get-tuple-element.75.even, ...), custom_call_target="tpu_custom_call" | custom-call | flops 1 | bytes 1 | tf_op jit(solution)/shard_map/pallas_call | solution.py:99
  10.8 3.6 %collective-permute-start.6 = (bf16[1,128,256]{2,1,0:T(8,128)(2,1)S(1)}, bf16[1,128,256]{2,1,0:T(8,128)(2,1)S(1)}, u32[]{:S(2)}, u32[]{:S(2)}) collective-permute-start(bf16[1,128,256]{2,1,0:T(8,128)(2,1)S(1)} %get-tuple-element.145), channel_id=1, source_target_pairs={{1,2},{2,1},{3,4},{4,3},{5,6},{6,5},{9,10},{10,9},{11,12},{12,11},... | collective-permute-start | bytes 196616 | tf_op jit(solution)/shard_map/ppermute | solution.py:137
  14.4 1.4 %collective-permute-done.2 = bf16[2,4,128,256]{3,2,1,0:T(8,128)(2,1)S(1)} collective-permute-done((bf16[2,4,128,256]{3,2,1,0:T(8,128)(2,1)}, bf16[2,4,128,256]{3,2,1,0:T(8,128)(2,1)S(1)}, u32[]{:S(2)}, u32[]{:S(2)}) %collective-permute-start.2) | collective-permute-done | bytes 524320 | tf_op jit(solution)/shard_map/ppermute | solution.py:171
  16.1 1.6 %collective-permute-start.3 = (bf16[1,128,256]{2,1,0:T(8,128)(2,1)S(1)}, bf16[1,128,256]{2,1,0:T(8,128)(2,1)S(1)}, u32[]{:S(2)}, u32[]{:S(2)}) collective-permute-start(bf16[1,128,256]{2,1,0:T(8,128)(2,1)S(1)} %get-tuple-element.148), channel_id=1, source_target_pairs={{0,1},{1,0},{2,3},{3,2},{4,5},{5,4},{6,7},{7,6},{8,9},{9,8},{10,11... | collective-permute-start | bytes 196616 | tf_op jit(solution)/shard_map/ppermute | solution.py:137
  17.7 3.1 %collective-permute-start.4 = (bf16[1,128,256]{2,1,0:T(8,128)(2,1)S(1)}, bf16[1,128,256]{2,1,0:T(8,128)(2,1)S(1)}, u32[]{:S(2)}, u32[]{:S(2)}) collective-permute-start(bf16[1,128,256]{2,1,0:T(8,128)(2,1)S(1)} %get-tuple-element.147), channel_id=1, source_target_pairs={{1,2},{2,1},{3,4},{4,3},{5,6},{6,5},{9,10},{10,9},{11,12},{12,11},... | collective-permute-start | bytes 196616 | tf_op jit(solution)/shard_map/ppermute | solution.py:137
  20.8 1.2 %shard_map.57 = (bf16[4,128,256]{2,1,0:T(8,128)(2,1)S(1)}, bf16[4,144,256]{2,1,0:T(8,128)(2,1)S(1)}, f32[2,128,256]{2,1,0:T(8,128)S(1)}) custom-call(bf16[4,128,256]{2,1,0:T(8,128)(2,1)S(1)} %shard_map.56.field, bf16[6912,256]{1,0:T(8,128)(2,1)S(1)} %bitcast.48), custom_call_target="tpu_custom_call" | custom-call | flops 1 | bytes 1 | tf_op jit(solution)/shard_map/pallas_call | solution.py:99
  22.0 1.2 %shard_map.58 = bf16[4,128,256]{2,1,0:T(8,128)(2,1)S(1)} custom-call(s32[1]{0:T(128)} %bitcast.flags, bf16[1,128,256]{2,1,0:T(8,128)(2,1)S(1)} %collective-permute-done.5.near, bf16[1,128,256]{2,1,0:T(8,128)(2,1)S(1)} %collective-permute-done.6.far, bf16[4,128,256]{2,1,0:T(8,128)(2,1)S(1)} %get-tuple-element.82.even, ...), custom_call_target="tpu_custom_call" | custom-call | flops 1 | bytes 1 | tf_op jit(solution)/shard_map/pallas_call | solution.py:99
  24.6 1.2 %shard_map.59 = (bf16[4,128,256]{2,1,0:T(8,128)(2,1)S(1)}, bf16[4,144,256]{2,1,0:T(8,128)(2,1)S(1)}, f32[2,128,256]{2,1,0:T(8,128)S(1)}) custom-call(bf16[4,128,256]{2,1,0:T(8,128)(2,1)S(1)} %get-tuple-element.128.field.rest_0_, bf16[6912,256]{1,0:T(8,128)(2,1)S(1)} %get-tuple-element.78.weights), custom_call_target="tpu_custom_call" | custom-call | flops 1 | bytes 1 | tf_op jit(solution)/shard_map/pallas_call | solution.py:99
  25.8 1.2 %shard_map.60.field = bf16[4,128,256]{2,1,0:T(8,128)(2,1)S(1)} custom-call(s32[1]{0:T(128)} %bitcast.flags, bf16[1,128,256]{2,1,0:T(8,128)(2,1)S(1)} %collective-permute-done.3.near, bf16[1,128,256]{2,1,0:T(8,128)(2,1)S(1)} %collective-permute-done.4.far, bf16[4,128,256]{2,1,0:T(8,128)(2,1)S(1)} %get-tuple-element.89.even, ...), custom_call_target="tpu_custom_call" | custom-call | flops 1 | bytes 1 | tf_op jit(solution)/shard_map/pallas_call | solution.py:99
  27.1 3.6 %collective-permute-start.9 = (bf16[1,128,256]{2,1,0:T(8,128)(2,1)S(1)}, bf16[1,128,256]{2,1,0:T(8,128)(2,1)S(1)}, u32[]{:S(2)}, u32[]{:S(2)}) collective-permute-start(bf16[1,128,256]{2,1,0:T(8,128)(2,1)S(1)} %get-tuple-element.143), channel_id=1, source_target_pairs={{1,2},{2,1},{3,4},{4,3},{5,6},{6,5},{9,10},{10,9},{11,12},{12,11},... | collective-permute-start | bytes 196616 | tf_op jit(solution)/shard_map/ppermute | solution.py:137
  30.7 1.2 %shard_map.61 = (bf16[4,128,256]{2,1,0:T(8,128)(2,1)S(1)}, bf16[4,144,256]{2,1,0:T(8,128)(2,1)S(1)}, f32[2,128,256]{2,1,0:T(8,128)S(1)}) custom-call(bf16[4,128,256]{2,1,0:T(8,128)(2,1)S(1)} %shard_map.60.field, bf16[6912,256]{1,0:T(8,128)(2,1)S(1)} %bitcast.50), custom_call_target="tpu_custom_call" | custom-call | flops 1 | bytes 1 | tf_op jit(solution)/shard_map/pallas_call | solution.py:99
  32.8 1.2 %shard_map.62 = bf16[4,128,256]{2,1,0:T(8,128)(2,1)S(1)} custom-call(s32[1]{0:T(128)} %bitcast.flags, bf16[1,128,256]{2,1,0:T(8,128)(2,1)S(1)} %collective-permute-done.8.near, bf16[1,128,256]{2,1,0:T(8,128)(2,1)S(1)} %collective-permute-done.9.far, bf16[4,128,256]{2,1,0:T(8,128)(2,1)S(1)} %get-tuple-element.92.even, ...), custom_call_target="tpu_custom_call" | custom-call | flops 1 | bytes 1 | tf_op jit(solution)/shard_map/pallas_call | solution.py:99
  34.0 3.1 %collective-permute-start.13 = (bf16[4,128,256]{2,1,0:T(8,128)(2,1)S(1)}, bf16[4,128,256]{2,1,0:T(8,128)(2,1)S(1)}, u32[]{:S(2)}, u32[]{:S(2)}) collective-permute-start(bf16[4,128,256]{2,1,0:T(8,128)(2,1)S(1)} %shard_map.62), channel_id=1, source_target_pairs={{0,8},{8,16},{16,24},{1,9},{9,17},{17,25},{2,10},{10,18},{18,26},{... | collective-permute-start | bytes 786440 | tf_op jit(solution)/shard_map/ppermute | solution.py:171
  37.8 1.9 %collective-permute-start.10 = (bf16[4,128,256]{2,1,0:T(8,128)(2,1)S(1)}, bf16[4,128,256]{2,1,0:T(8,128)(2,1)S(1)}, u32[]{:S(2)}, u32[]{:S(2)}) collective-permute-start(bf16[4,128,256]{2,1,0:T(8,128)(2,1)S(1)} %shard_map.60.field), channel_id=1, source_target_pairs={{0,8},{8,16},{16,24},{1,9},{9,17},{17,25},{2,10},{10,18},{18,26},{... | collective-permute-start | bytes 786440 | tf_op jit(solution)/shard_map/ppermute | solution.py:171
  40.5 3.8 %collective-permute-done.13 = bf16[4,128,256]{2,1,0:T(8,128)(2,1)S(1)} collective-permute-done((bf16[4,128,256]{2,1,0:T(8,128)(2,1)S(1)}, bf16[4,128,256]{2,1,0:T(8,128)(2,1)S(1)}, u32[]{:S(2)}, u32[]{:S(2)}) %collective-permute-start.13) | collective-permute-done | bytes 262176 | tf_op jit(solution)/shard_map/ppermute | solution.py:171
  44.4 2.1 %collective-permute-start.15 = (bf16[1,128,256]{2,1,0:T(8,128)(2,1)S(1)}, bf16[1,128,256]{2,1,0:T(8,128)(2,1)S(1)}, u32[]{:S(2)}, u32[]{:S(2)}) collective-permute-start(bf16[1,128,256]{2,1,0:T(8,128)(2,1)S(1)} %get-tuple-element.142), channel_id=1, source_target_pairs={{0,1},{1,0},{2,3},{3,2},{4,5},{5,4},{6,7},{7,6},{8,9},{9,8},{10,11... | collective-permute-start | bytes 196616 | tf_op jit(solution)/shard_map/ppermute | solution.py:137
  46.6 3.3 %collective-permute-start.16 = (bf16[1,128,256]{2,1,0:T(8,128)(2,1)S(1)}, bf16[1,128,256]{2,1,0:T(8,128)(2,1)S(1)}, u32[]{:S(2)}, u32[]{:S(2)}) collective-permute-start(bf16[1,128,256]{2,1,0:T(8,128)(2,1)S(1)} %get-tuple-element.141), channel_id=1, source_target_pairs={{1,2},{2,1},{3,4},{4,3},{5,6},{6,5},{9,10},{10,9},{11,12},{12,11},... | collective-permute-start | bytes 196616 | tf_op jit(solution)/shard_map/ppermute | solution.py:137
  49.8 1.2 %shard_map.63 = (bf16[4,128,256]{2,1,0:T(8,128)(2,1)S(1)}, bf16[4,144,256]{2,1,0:T(8,128)(2,1)S(1)}, f32[2,128,256]{2,1,0:T(8,128)S(1)}) custom-call(bf16[4,128,256]{2,1,0:T(8,128)(2,1)S(1)} %fusion.16.field.rest_0_, bf16[6912,256]{1,0:T(8,128)(2,1)S(1)} %get-tuple-element.78.weights), custom_call_target="tpu_custom_call" | custom-call | flops 1 | bytes 1 | tf_op jit(solution)/shard_map/pallas_call | solution.py:99
  51.1 1.1 collective-permute-done.16.far
  52.1 1.2 shard_map.64
  53.6 3.6 %collective-permute-start.18 = (bf16[1,128,256]{2,1,0:T(8,128)(2,1)S(1)}, bf16[1,128,256]{2,1,0:T(8,128)(2,1)S(1)}, u32[]{:S(2)}, u32[]{:S(2)}) collective-permute-start(bf16[1,128,256]{2,1,0:T(8,128)(2,1)S(1)} %get-tuple-element.139), channel_id=1, source_target_pairs={{1,2},{2,1},{3,4},{4,3},{5,6},{6,5},{9,10},{10,9},{11,12},{12,11},... | collective-permute-start | bytes 196616 | tf_op jit(solution)/shard_map/ppermute | solution.py:137
  57.2 1.2 %shard_map.65 = (bf16[4,128,256]{2,1,0:T(8,128)(2,1)S(1)}, bf16[4,144,256]{2,1,0:T(8,128)(2,1)S(1)}, f32[2,128,256]{2,1,0:T(8,128)S(1)}) custom-call(bf16[4,128,256]{2,1,0:T(8,128)(2,1)S(1)} %add_convert_fusion.6.field, bf16[6912,256]{1,0:T(8,128)(2,1)S(1)} %bitcast.52), custom_call_target="tpu_custom_call" | custom-call | flops 1 | bytes 1 | tf_op jit(solution)/shard_map/pallas_call | solution.py:99
  59.3 1.2 %shard_map.66 = bf16[4,128,256]{2,1,0:T(8,128)(2,1)S(1)} custom-call(s32[1]{0:T(128)} %bitcast.flags, bf16[1,128,256]{2,1,0:T(8,128)(2,1)S(1)} %collective-permute-done.17.near, bf16[1,128,256]{2,1,0:T(8,128)(2,1)S(1)} %collective-permute-done.18.far, bf16[4,128,256]{2,1,0:T(8,128)(2,1)S(1)} %get-tuple-element.104.even, ...), custom_call_target="tpu_custom_call" | custom-call | flops 1 | bytes 1 | tf_op jit(solution)/shard_map/pallas_call | solution.py:99
  60.5 4.5 %collective-permute-start.21 = (bf16[4,128,256]{2,1,0:T(8,128)(2,1)S(1)}, bf16[4,128,256]{2,1,0:T(8,128)(2,1)S(1)}, u32[]{:S(2)}, u32[]{:S(2)}) collective-permute-start(bf16[4,128,256]{2,1,0:T(8,128)(2,1)S(1)} %shard_map.66), channel_id=1, source_target_pairs={{0,8},{8,16},{16,24},{1,9},{9,17},{17,25},{2,10},{10,18},{18,26},{... | collective-permute-start | bytes 786440 | tf_op jit(solution)/shard_map/ppermute | solution.py:171
  65.7 1.9 %collective-permute-start.19 = (bf16[4,128,256]{2,1,0:T(8,128)(2,1)S(1)}, bf16[4,128,256]{2,1,0:T(8,128)(2,1)S(1)}, u32[]{:S(2)}, u32[]{:S(2)}) collective-permute-start(bf16[4,128,256]{2,1,0:T(8,128)(2,1)S(1)} %add_convert_fusion.6.field), channel_id=1, source_target_pairs={{0,8},{8,16},{16,24},{1,9},{9,17},{17,25},{2,10},{10,18},{18,26},{... | collective-permute-start | bytes 786440 | tf_op jit(solution)/shard_map/ppermute | solution.py:171
  68.3 2.5 %collective-permute-done.21 = bf16[4,128,256]{2,1,0:T(8,128)(2,1)S(1)} collective-permute-done((bf16[4,128,256]{2,1,0:T(8,128)(2,1)S(1)}, bf16[4,128,256]{2,1,0:T(8,128)(2,1)S(1)}, u32[]{:S(2)}, u32[]{:S(2)}) %collective-permute-start.21) | collective-permute-done | bytes 262176 | tf_op jit(solution)/shard_map/ppermute | solution.py:171
  70.9 1.6 %collective-permute-start.23 = (bf16[1,128,256]{2,1,0:T(8,128)(2,1)S(1)}, bf16[1,128,256]{2,1,0:T(8,128)(2,1)S(1)}, u32[]{:S(2)}, u32[]{:S(2)}) collective-permute-start(bf16[1,128,256]{2,1,0:T(8,128)(2,1)S(1)} %get-tuple-element.138), channel_id=1, source_target_pairs={{0,1},{1,0},{2,3},{3,2},{4,5},{5,4},{6,7},{7,6},{8,9},{9,8},{10,11... | collective-permute-start | bytes 196616 | tf_op jit(solution)/shard_map/ppermute | solution.py:137
  72.6 3.6 %collective-permute-start.24 = (bf16[1,128,256]{2,1,0:T(8,128)(2,1)S(1)}, bf16[1,128,256]{2,1,0:T(8,128)(2,1)S(1)}, u32[]{:S(2)}, u32[]{:S(2)}) collective-permute-start(bf16[1,128,256]{2,1,0:T(8,128)(2,1)S(1)} %get-tuple-element.137), channel_id=1, source_target_pairs={{1,2},{2,1},{3,4},{4,3},{5,6},{6,5},{9,10},{10,9},{11,12},{12,11},... | collective-permute-start | bytes 196616 | tf_op jit(solution)/shard_map/ppermute | solution.py:137
  76.2 1.2 %shard_map.67 = (bf16[4,128,256]{2,1,0:T(8,128)(2,1)S(1)}, bf16[4,144,256]{2,1,0:T(8,128)(2,1)S(1)}, f32[2,128,256]{2,1,0:T(8,128)S(1)}) custom-call(bf16[4,128,256]{2,1,0:T(8,128)(2,1)S(1)} %fusion.14.field.rest_0_, bf16[6912,256]{1,0:T(8,128)(2,1)S(1)} %get-tuple-element.78.weights), custom_call_target="tpu_custom_call" | custom-call | flops 1 | bytes 1 | tf_op jit(solution)/shard_map/pallas_call | solution.py:99
  78.2 1.2 shard_map.68
  79.7 4.0 %collective-permute-start.26 = (bf16[1,128,256]{2,1,0:T(8,128)(2,1)S(1)}, bf16[1,128,256]{2,1,0:T(8,128)(2,1)S(1)}, u32[]{:S(2)}, u32[]{:S(2)}) collective-permute-start(bf16[1,128,256]{2,1,0:T(8,128)(2,1)S(1)} %get-tuple-element.135), channel_id=1, source_target_pairs={{1,2},{2,1},{3,4},{4,3},{5,6},{6,5},{9,10},{10,9},{11,12},{12,11},... | collective-permute-start | bytes 196616 | tf_op jit(solution)/shard_map/ppermute | solution.py:137
  83.7 1.2 %shard_map.69 = (bf16[4,128,256]{2,1,0:T(8,128)(2,1)S(1)}, bf16[4,144,256]{2,1,0:T(8,128)(2,1)S(1)}, f32[2,128,256]{2,1,0:T(8,128)S(1)}) custom-call(bf16[4,128,256]{2,1,0:T(8,128)(2,1)S(1)} %add_convert_fusion.3.field, bf16[6912,256]{1,0:T(8,128)(2,1)S(1)} %bitcast.54), custom_call_target="tpu_custom_call" | custom-call | flops 1 | bytes 1 | tf_op jit(solution)/shard_map/pallas_call | solution.py:99
  85.7 1.2 %shard_map.70 = bf16[4,128,256]{2,1,0:T(8,128)(2,1)S(1)} custom-call(s32[1]{0:T(128)} %bitcast.flags, bf16[1,128,256]{2,1,0:T(8,128)(2,1)S(1)} %collective-permute-done.25.near, bf16[1,128,256]{2,1,0:T(8,128)(2,1)S(1)} %collective-permute-done.26.far, bf16[4,128,256]{2,1,0:T(8,128)(2,1)S(1)} %get-tuple-element.114.even, ...), custom_call_target="tpu_custom_call" | custom-call | flops 1 | bytes 1 | tf_op jit(solution)/shard_map/pallas_call | solution.py:99
  87.5 5.7 %collective-permute-start.29 = (bf16[4,128,256]{2,1,0:T(8,128)(2,1)S(1)}, bf16[4,128,256]{2,1,0:T(8,128)(2,1)S(1)}, u32[]{:S(2)}, u32[]{:S(2)}) collective-permute-start(bf16[4,128,256]{2,1,0:T(8,128)(2,1)S(1)} %shard_map.70), channel_id=1, source_target_pairs={{8,16},{16,24},{9,17},{17,25},{10,18},{18,26},{11,19},{19,27},{12,... | collective-permute-start | bytes 786440 | tf_op jit(solution)/shard_map/ppermute | solution.py:171
  93.9 1.9 %collective-permute-start.27 = (bf16[4,128,256]{2,1,0:T(8,128)(2,1)S(1)}, bf16[4,128,256]{2,1,0:T(8,128)(2,1)S(1)}, u32[]{:S(2)}, u32[]{:S(2)}) collective-permute-start(bf16[4,128,256]{2,1,0:T(8,128)(2,1)S(1)} %add_convert_fusion.3.field), channel_id=1, source_target_pairs={{8,16},{16,24},{9,17},{17,25},{10,18},{18,26},{11,19},{19,27},{12,... | collective-permute-start | bytes 786440 | tf_op jit(solution)/shard_map/ppermute | solution.py:171
  95.8 4.6 %collective-permute-done.29 = bf16[4,128,256]{2,1,0:T(8,128)(2,1)S(1)} collective-permute-done((bf16[4,128,256]{2,1,0:T(8,128)(2,1)S(1)}, bf16[4,128,256]{2,1,0:T(8,128)(2,1)S(1)}, u32[]{:S(2)}, u32[]{:S(2)}) %collective-permute-start.29) | collective-permute-done | bytes 262176 | tf_op jit(solution)/shard_map/ppermute | solution.py:171
  100.6 2.1 %collective-permute-start.31 = (bf16[1,128,256]{2,1,0:T(8,128)(2,1)S(1)}, bf16[1,128,256]{2,1,0:T(8,128)(2,1)S(1)}, u32[]{:S(2)}, u32[]{:S(2)}) collective-permute-start(bf16[1,128,256]{2,1,0:T(8,128)(2,1)S(1)} %get-tuple-element.134), channel_id=1, source_target_pairs={{0,1},{1,0},{2,3},{3,2},{4,5},{5,4},{6,7},{7,6},{8,9},{9,8},{10,11... | collective-permute-start | bytes 196616 | tf_op jit(solution)/shard_map/ppermute | solution.py:137
  102.7 2.1 %collective-permute-start.32 = (bf16[1,128,256]{2,1,0:T(8,128)(2,1)S(1)}, bf16[1,128,256]{2,1,0:T(8,128)(2,1)S(1)}, u32[]{:S(2)}, u32[]{:S(2)}) collective-permute-start(bf16[1,128,256]{2,1,0:T(8,128)(2,1)S(1)} %get-tuple-element.133), channel_id=1, source_target_pairs={{1,2},{2,1},{3,4},{4,3},{5,6},{6,5},{9,10},{10,9},{11,12},{12,11},... | collective-permute-start | bytes 196616 | tf_op jit(solution)/shard_map/ppermute | solution.py:137
  104.8 1.2 %shard_map.71 = (bf16[4,128,256]{2,1,0:T(8,128)(2,1)S(1)}, bf16[4,144,256]{2,1,0:T(8,128)(2,1)S(1)}, f32[2,128,256]{2,1,0:T(8,128)S(1)}) custom-call(bf16[4,128,256]{2,1,0:T(8,128)(2,1)S(1)} %fusion.12.field.rest_1_, bf16[6912,256]{1,0:T(8,128)(2,1)S(1)} %get-tuple-element.78.weights), custom_call_target="tpu_custom_call" | custom-call | flops 1 | bytes 1 | tf_op jit(solution)/shard_map/pallas_call | solution.py:99
  106.0 2.2 %collective-permute-done.32.far = bf16[1,128,256]{2,1,0:T(8,128)(2,1)S(1)} collective-permute-done((bf16[1,128,256]{2,1,0:T(8,128)(2,1)S(1)}, bf16[1,128,256]{2,1,0:T(8,128)(2,1)S(1)}, u32[]{:S(2)}, u32[]{:S(2)}) %collective-permute-start.32) | collective-permute-done | bytes 65568 | tf_op jit(solution)/shard_map/ppermute | solution.py:137
  108.3 1.2 shard_map.72
  109.8 2.6 %collective-permute-start.34 = (bf16[1,128,256]{2,1,0:T(8,128)(2,1)S(1)}, bf16[1,128,256]{2,1,0:T(8,128)(2,1)S(1)}, u32[]{:S(2)}, u32[]{:S(2)}) collective-permute-start(bf16[1,128,256]{2,1,0:T(8,128)(2,1)S(1)} %get-tuple-element.131), channel_id=1, source_target_pairs={{1,2},{2,1},{3,4},{4,3},{5,6},{6,5},{9,10},{10,9},{11,12},{12,11},... | collective-permute-start | bytes 196616 | tf_op jit(solution)/shard_map/ppermute | solution.py:137
  112.4 1.2 %shard_map.73 = (bf16[4,128,256]{2,1,0:T(8,128)(2,1)S(1)}, bf16[4,144,256]{2,1,0:T(8,128)(2,1)S(1)}, f32[2,128,256]{2,1,0:T(8,128)S(1)}) custom-call(bf16[4,128,256]{2,1,0:T(8,128)(2,1)S(1)} %add_convert_fusion.field.rest_0_, bf16[6912,256]{1,0:T(8,128)(2,1)S(1)} %bitcast.56), custom_call_target="tpu_custom_call" | custom-call | flops 1 | bytes 1 | tf_op jit(solution)/shard_map/pallas_call | solution.py:99
  113.6 1.8 %collective-permute-done.34.far = bf16[1,128,256]{2,1,0:T(8,128)(2,1)S(1)} collective-permute-done((bf16[1,128,256]{2,1,0:T(8,128)(2,1)S(1)}, bf16[1,128,256]{2,1,0:T(8,128)(2,1)S(1)}, u32[]{:S(2)}, u32[]{:S(2)}) %collective-permute-start.34) | collective-permute-done | bytes 65568 | tf_op jit(solution)/shard_map/ppermute | solution.py:137
  115.4 2.0 %shard_map.74 = bf16[2,4,128,256]{3,2,1,0:T(8,128)(2,1)} custom-call(s32[1]{0:T(128)} %bitcast.flags, bf16[1,128,256]{2,1,0:T(8,128)(2,1)S(1)} %collective-permute-done.33.near, bf16[1,128,256]{2,1,0:T(8,128)(2,1)S(1)} %collective-permute-done.34.far, bf16[4,128,256]{2,1,0:T(8,128)(2,1)S(1)} %get-tuple-element.124.even, ...), custom_call_target="tpu_custom_call" | custom-call | flops 1 | bytes 1 | tf_op jit(solution)/shard_map/pallas_call | solution.py:99
  (66 shorter events, 12.3 us)
Async XLA Ops:
  0.0 15.8 %collective-permute-start.2 = (bf16[2,4,128,256]{3,2,1,0:T(8,128)(2,1)}, bf16[2,4,128,256]{3,2,1,0:T(8,128)(2,1)S(1)}, u32[]{:S(2)}, u32[]{:S(2)}) collective-permute-start(bf16[2,4,128,256]{3,2,1,0:T(8,128)(2,1)} %bitcast.66), channel_id=1, source_target_pairs={{0,24},{8,16},{1,25},{9,17},{2,26},{10,18},{3,27},{11,19},{4,28},{... | collective-permute-start | bytes 1572872 | tf_op jit(solution)/shard_map/ppermute | solution.py:171
  2.4 7.0 %collective-permute-start = (bf16[1,128,256]{2,1,0:T(8,128)(2,1)S(1)}, bf16[1,128,256]{2,1,0:T(8,128)(2,1)S(1)}, u32[]{:S(2)}, u32[]{:S(2)}) collective-permute-start(bf16[1,128,256]{2,1,0:T(8,128)(2,1)S(1)} %get-tuple-element.150), channel_id=1, source_target_pairs={{0,1},{1,0},{2,3},{3,2},{4,5},{5,4},{6,7},{7,6},{8,9},{9,8},{10,11... | collective-permute-start | bytes 196616 | tf_op jit(solution)/shard_map/ppermute | solution.py:137
  3.1 6.3 %collective-permute-start.1 = (bf16[1,128,256]{2,1,0:T(8,128)(2,1)S(1)}, bf16[1,128,256]{2,1,0:T(8,128)(2,1)S(1)}, u32[]{:S(2)}, u32[]{:S(2)}) collective-permute-start(bf16[1,128,256]{2,1,0:T(8,128)(2,1)S(1)} %get-tuple-element.149), channel_id=1, source_target_pairs={{1,2},{2,1},{3,4},{4,3},{5,6},{6,5},{9,10},{10,9},{11,12},{12,11},... | collective-permute-start | bytes 196616 | tf_op jit(solution)/shard_map/ppermute | solution.py:137
  6.2 9.5 %copy-start.2 = (bf16[1,2,4,16,8,256]{5,4,3,2,1,0:T(8,128)(2,1)S(1)}, bf16[1,2,4,16,8,256]{5,4,3,2,1,0:T(8,128)(2,1)}, u32[]{:S(2)}) copy-start(bf16[1,2,4,16,8,256]{5,4,3,2,1,0:T(8,128)(2,1)} %param.5) | copy-start | bytes 1572868
  9.5 6.3 %copy-start.1 = (bf16[3,2,4,16,8,256]{5,4,3,2,1,0:T(8,128)(2,1)S(1)}, bf16[3,2,4,16,8,256]{5,4,3,2,1,0:T(8,128)(2,1)}, u32[]{:S(2)}) copy-start(bf16[3,2,4,16,8,256]{5,4,3,2,1,0:T(8,128)(2,1)} %param.7) | copy-start | bytes 4718596
  9.5 11.3 %copy-start = (bf16[1,3,3,3,256,256]{5,4,3,2,1,0:T(8,128)(2,1)S(1)}, bf16[1,3,3,3,256,256]{5,4,3,2,1,0:T(8,128)(2,1)}, u32[]{:S(2)}) copy-start(bf16[1,3,3,3,256,256]{5,4,3,2,1,0:T(8,128)(2,1)} %param.9) | copy-start | bytes 10616836
  10.7 11.3 %collective-permute-start.5 = (bf16[1,128,256]{2,1,0:T(8,128)(2,1)S(1)}, bf16[1,128,256]{2,1,0:T(8,128)(2,1)S(1)}, u32[]{:S(2)}, u32[]{:S(2)}) collective-permute-start(bf16[1,128,256]{2,1,0:T(8,128)(2,1)S(1)} %get-tuple-element.146), channel_id=1, source_target_pairs={{0,1},{1,0},{2,3},{3,2},{4,5},{5,4},{6,7},{7,6},{8,9},{9,8},{10,11... | collective-permute-start | bytes 196616 | tf_op jit(solution)/shard_map/ppermute | solution.py:137
  10.8 11.2 %collective-permute-start.6 = (bf16[1,128,256]{2,1,0:T(8,128)(2,1)S(1)}, bf16[1,128,256]{2,1,0:T(8,128)(2,1)S(1)}, u32[]{:S(2)}, u32[]{:S(2)}) collective-permute-start(bf16[1,128,256]{2,1,0:T(8,128)(2,1)S(1)} %get-tuple-element.145), channel_id=1, source_target_pairs={{1,2},{2,1},{3,4},{4,3},{5,6},{6,5},{9,10},{10,9},{11,12},{12,11},... | collective-permute-start | bytes 196616 | tf_op jit(solution)/shard_map/ppermute | solution.py:137
  16.1 7.2 %collective-permute-start.3 = (bf16[1,128,256]{2,1,0:T(8,128)(2,1)S(1)}, bf16[1,128,256]{2,1,0:T(8,128)(2,1)S(1)}, u32[]{:S(2)}, u32[]{:S(2)}) collective-permute-start(bf16[1,128,256]{2,1,0:T(8,128)(2,1)S(1)} %get-tuple-element.148), channel_id=1, source_target_pairs={{0,1},{1,0},{2,3},{3,2},{4,5},{5,4},{6,7},{7,6},{8,9},{9,8},{10,11... | collective-permute-start | bytes 196616 | tf_op jit(solution)/shard_map/ppermute | solution.py:137
  17.7 5.6 %collective-permute-start.4 = (bf16[1,128,256]{2,1,0:T(8,128)(2,1)S(1)}, bf16[1,128,256]{2,1,0:T(8,128)(2,1)S(1)}, u32[]{:S(2)}, u32[]{:S(2)}) collective-permute-start(bf16[1,128,256]{2,1,0:T(8,128)(2,1)S(1)} %get-tuple-element.147), channel_id=1, source_target_pairs={{1,2},{2,1},{3,4},{4,3},{5,6},{6,5},{9,10},{10,9},{11,12},{12,11},... | collective-permute-start | bytes 196616 | tf_op jit(solution)/shard_map/ppermute | solution.py:137
  23.2 13.9 %collective-permute-start.7 = (bf16[4,128,256]{2,1,0:T(8,128)(2,1)S(1)}, bf16[4,128,256]{2,1,0:T(8,128)(2,1)S(1)}, u32[]{:S(2)}, u32[]{:S(2)}) collective-permute-start(bf16[4,128,256]{2,1,0:T(8,128)(2,1)S(1)} %shard_map.56.field), channel_id=1, source_target_pairs={{0,8},{1,9},{2,10},{3,11},{4,12},{5,13},{6,14},{7,15}} | collective-permute-start | bytes 786440 | tf_op jit(solution)/shard_map/ppermute | solution.py:171
  23.9 13.2 %collective-permute-start.11 = (bf16[4,128,256]{2,1,0:T(8,128)(2,1)S(1)}, bf16[4,128,256]{2,1,0:T(8,128)(2,1)S(1)}, u32[]{:S(2)}, u32[]{:S(2)}) collective-permute-start(bf16[4,128,256]{2,1,0:T(8,128)(2,1)S(1)} %shard_map.58), channel_id=1, source_target_pairs={{0,8},{1,9},{2,10},{3,11},{4,12},{5,13},{6,14},{7,15}} | collective-permute-start | bytes 786440 | tf_op jit(solution)/shard_map/ppermute | solution.py:171
  27.1 4.9 %collective-permute-start.8 = (bf16[1,128,256]{2,1,0:T(8,128)(2,1)S(1)}, bf16[1,128,256]{2,1,0:T(8,128)(2,1)S(1)}, u32[]{:S(2)}, u32[]{:S(2)}) collective-permute-start(bf16[1,128,256]{2,1,0:T(8,128)(2,1)S(1)} %get-tuple-element.144), channel_id=1, source_target_pairs={{0,1},{1,0},{2,3},{3,2},{4,5},{5,4},{6,7},{7,6},{8,9},{9,8},{10,11... | collective-permute-start | bytes 196616 | tf_op jit(solution)/shard_map/ppermute | solution.py:137
  27.1 5.7 %collective-permute-start.9 = (bf16[1,128,256]{2,1,0:T(8,128)(2,1)S(1)}, bf16[1,128,256]{2,1,0:T(8,128)(2,1)S(1)}, u32[]{:S(2)}, u32[]{:S(2)}) collective-permute-start(bf16[1,128,256]{2,1,0:T(8,128)(2,1)S(1)} %get-tuple-element.143), channel_id=1, source_target_pairs={{1,2},{2,1},{3,4},{4,3},{5,6},{6,5},{9,10},{10,9},{11,12},{12,11},... | collective-permute-start | bytes 196616 | tf_op jit(solution)/shard_map/ppermute | solution.py:137
  34.0 10.3 %collective-permute-start.13 = (bf16[4,128,256]{2,1,0:T(8,128)(2,1)S(1)}, bf16[4,128,256]{2,1,0:T(8,128)(2,1)S(1)}, u32[]{:S(2)}, u32[]{:S(2)}) collective-permute-start(bf16[4,128,256]{2,1,0:T(8,128)(2,1)S(1)} %shard_map.62), channel_id=1, source_target_pairs={{0,8},{8,16},{16,24},{1,9},{9,17},{17,25},{2,10},{10,18},{18,26},{... | collective-permute-start | bytes 786440 | tf_op jit(solution)/shard_map/ppermute | solution.py:171
  37.2 7.1 %collective-permute-start.14 = (bf16[4,128,256]{2,1,0:T(8,128)(2,1)S(1)}, bf16[4,128,256]{2,1,0:T(8,128)(2,1)S(1)}, u32[]{:S(2)}, u32[]{:S(2)}) collective-permute-start(bf16[4,128,256]{2,1,0:T(8,128)(2,1)S(1)} %collective-permute-done.11), channel_id=1, source_target_pairs={{8,24},{9,25},{10,26},{11,27},{12,28},{13,29},{14,30},{15,31}} | collective-permute-start | bytes 786440 | tf_op jit(solution)/shard_map/ppermute | solution.py:171
  37.8 15.5 %collective-permute-start.10 = (bf16[4,128,256]{2,1,0:T(8,128)(2,1)S(1)}, bf16[4,128,256]{2,1,0:T(8,128)(2,1)S(1)}, u32[]{:S(2)}, u32[]{:S(2)}) collective-permute-start(bf16[4,128,256]{2,1,0:T(8,128)(2,1)S(1)} %shard_map.60.field), channel_id=1, source_target_pairs={{0,8},{8,16},{16,24},{1,9},{9,17},{17,25},{2,10},{10,18},{18,26},{... | collective-permute-start | bytes 786440 | tf_op jit(solution)/shard_map/ppermute | solution.py:171
  39.8 13.5 %collective-permute-start.12 = (bf16[4,128,256]{2,1,0:T(8,128)(2,1)S(1)}, bf16[4,128,256]{2,1,0:T(8,128)(2,1)S(1)}, u32[]{:S(2)}, u32[]{:S(2)}) collective-permute-start(bf16[4,128,256]{2,1,0:T(8,128)(2,1)S(1)} %collective-permute-done.7), channel_id=1, source_target_pairs={{8,24},{9,25},{10,26},{11,27},{12,28},{13,29},{14,30},{15,31}} | collective-permute-start | bytes 786440 | tf_op jit(solution)/shard_map/ppermute | solution.py:171
  44.4 6.6 %collective-permute-start.15 = (bf16[1,128,256]{2,1,0:T(8,128)(2,1)S(1)}, bf16[1,128,256]{2,1,0:T(8,128)(2,1)S(1)}, u32[]{:S(2)}, u32[]{:S(2)}) collective-permute-start(bf16[1,128,256]{2,1,0:T(8,128)(2,1)S(1)} %get-tuple-element.142), channel_id=1, source_target_pairs={{0,1},{1,0},{2,3},{3,2},{4,5},{5,4},{6,7},{7,6},{8,9},{9,8},{10,11... | collective-permute-start | bytes 196616 | tf_op jit(solution)/shard_map/ppermute | solution.py:137
  46.6 5.6 %collective-permute-start.16 = (bf16[1,128,256]{2,1,0:T(8,128)(2,1)S(1)}, bf16[1,128,256]{2,1,0:T(8,128)(2,1)S(1)}, u32[]{:S(2)}, u32[]{:S(2)}) collective-permute-start(bf16[1,128,256]{2,1,0:T(8,128)(2,1)S(1)} %get-tuple-element.141), channel_id=1, source_target_pairs={{1,2},{2,1},{3,4},{4,3},{5,6},{6,5},{9,10},{10,9},{11,12},{12,11},... | collective-permute-start | bytes 196616 | tf_op jit(solution)/shard_map/ppermute | solution.py:137
  53.6 4.9 %collective-permute-start.17 = (bf16[1,128,256]{2,1,0:T(8,128)(2,1)S(1)}, bf16[1,128,256]{2,1,0:T(8,128)(2,1)S(1)}, u32[]{:S(2)}, u32[]{:S(2)}) collective-permute-start(bf16[1,128,256]{2,1,0:T(8,128)(2,1)S(1)} %get-tuple-element.140), channel_id=1, source_target_pairs={{0,1},{1,0},{2,3},{3,2},{4,5},{5,4},{6,7},{7,6},{8,9},{9,8},{10,11... | collective-permute-start | bytes 196616 | tf_op jit(solution)/shard_map/ppermute | solution.py:137
  53.6 5.7 %collective-permute-start.18 = (bf16[1,128,256]{2,1,0:T(8,128)(2,1)S(1)}, bf16[1,128,256]{2,1,0:T(8,128)(2,1)S(1)}, u32[]{:S(2)}, u32[]{:S(2)}) collective-permute-start(bf16[1,128,256]{2,1,0:T(8,128)(2,1)S(1)} %get-tuple-element.139), channel_id=1, source_target_pairs={{1,2},{2,1},{3,4},{4,3},{5,6},{6,5},{9,10},{10,9},{11,12},{12,11},... | collective-permute-start | bytes 196616 | tf_op jit(solution)/shard_map/ppermute | solution.py:137
  60.5 10.3 %collective-permute-start.21 = (bf16[4,128,256]{2,1,0:T(8,128)(2,1)S(1)}, bf16[4,128,256]{2,1,0:T(8,128)(2,1)S(1)}, u32[]{:S(2)}, u32[]{:S(2)}) collective-permute-start(bf16[4,128,256]{2,1,0:T(8,128)(2,1)S(1)} %shard_map.66), channel_id=1, source_target_pairs={{0,8},{8,16},{16,24},{1,9},{9,17},{17,25},{2,10},{10,18},{18,26},{... | collective-permute-start | bytes 786440 | tf_op jit(solution)/shard_map/ppermute | solution.py:171
  65.0 5.8 %collective-permute-start.22 = (bf16[4,128,256]{2,1,0:T(8,128)(2,1)S(1)}, bf16[4,128,256]{2,1,0:T(8,128)(2,1)S(1)}, u32[]{:S(2)}, u32[]{:S(2)}) collective-permute-start(bf16[4,128,256]{2,1,0:T(8,128)(2,1)S(1)} %collective-permute-done.13), channel_id=1, source_target_pairs={{8,24},{9,25},{10,26},{11,27},{12,28},{13,29},{14,30},{15,31}} | collective-permute-start | bytes 786440 | tf_op jit(solution)/shard_map/ppermute | solution.py:171
  65.7 13.6 %collective-permute-start.19 = (bf16[4,128,256]{2,1,0:T(8,128)(2,1)S(1)}, bf16[4,128,256]{2,1,0:T(8,128)(2,1)S(1)}, u32[]{:S(2)}, u32[]{:S(2)}) collective-permute-start(bf16[4,128,256]{2,1,0:T(8,128)(2,1)S(1)} %add_convert_fusion.6.field), channel_id=1, source_target_pairs={{0,8},{8,16},{16,24},{1,9},{9,17},{17,25},{2,10},{10,18},{18,26},{... | collective-permute-start | bytes 786440 | tf_op jit(solution)/shard_map/ppermute | solution.py:171
  67.6 11.7 %collective-permute-start.20 = (bf16[4,128,256]{2,1,0:T(8,128)(2,1)S(1)}, bf16[4,128,256]{2,1,0:T(8,128)(2,1)S(1)}, u32[]{:S(2)}, u32[]{:S(2)}) collective-permute-start(bf16[4,128,256]{2,1,0:T(8,128)(2,1)S(1)} %collective-permute-done.10), channel_id=1, source_target_pairs={{8,24},{9,25},{10,26},{11,27},{12,28},{13,29},{14,30},{15,31}} | collective-permute-start | bytes 786440 | tf_op jit(solution)/shard_map/ppermute | solution.py:171
  70.9 6.4 %collective-permute-start.23 = (bf16[1,128,256]{2,1,0:T(8,128)(2,1)S(1)}, bf16[1,128,256]{2,1,0:T(8,128)(2,1)S(1)}, u32[]{:S(2)}, u32[]{:S(2)}) collective-permute-start(bf16[1,128,256]{2,1,0:T(8,128)(2,1)S(1)} %get-tuple-element.138), channel_id=1, source_target_pairs={{0,1},{1,0},{2,3},{3,2},{4,5},{5,4},{6,7},{7,6},{8,9},{9,8},{10,11... | collective-permute-start | bytes 196616 | tf_op jit(solution)/shard_map/ppermute | solution.py:137
  72.6 5.6 %collective-permute-start.24 = (bf16[1,128,256]{2,1,0:T(8,128)(2,1)S(1)}, bf16[1,128,256]{2,1,0:T(8,128)(2,1)S(1)}, u32[]{:S(2)}, u32[]{:S(2)}) collective-permute-start(bf16[1,128,256]{2,1,0:T(8,128)(2,1)S(1)} %get-tuple-element.137), channel_id=1, source_target_pairs={{1,2},{2,1},{3,4},{4,3},{5,6},{6,5},{9,10},{10,9},{11,12},{12,11},... | collective-permute-start | bytes 196616 | tf_op jit(solution)/shard_map/ppermute | solution.py:137
  79.6 5.3 %collective-permute-start.25 = (bf16[1,128,256]{2,1,0:T(8,128)(2,1)S(1)}, bf16[1,128,256]{2,1,0:T(8,128)(2,1)S(1)}, u32[]{:S(2)}, u32[]{:S(2)}) collective-permute-start(bf16[1,128,256]{2,1,0:T(8,128)(2,1)S(1)} %get-tuple-element.136), channel_id=1, source_target_pairs={{0,1},{1,0},{2,3},{3,2},{4,5},{5,4},{6,7},{7,6},{8,9},{9,8},{10,11... | collective-permute-start | bytes 196616 | tf_op jit(solution)/shard_map/ppermute | solution.py:137
  79.7 6.0 %collective-permute-start.26 = (bf16[1,128,256]{2,1,0:T(8,128)(2,1)S(1)}, bf16[1,128,256]{2,1,0:T(8,128)(2,1)S(1)}, u32[]{:S(2)}, u32[]{:S(2)}) collective-permute-start(bf16[1,128,256]{2,1,0:T(8,128)(2,1)S(1)} %get-tuple-element.135), channel_id=1, source_target_pairs={{1,2},{2,1},{3,4},{4,3},{5,6},{6,5},{9,10},{10,9},{11,12},{12,11},... | collective-permute-start | bytes 196616 | tf_op jit(solution)/shard_map/ppermute | solution.py:137
  86.9 9.0 %collective-permute-start.30 = (bf16[4,128,256]{2,1,0:T(8,128)(2,1)S(1)}, bf16[4,128,256]{2,1,0:T(8,128)(2,1)S(1)}, u32[]{:S(2)}, u32[]{:S(2)}) collective-permute-start(bf16[4,128,256]{2,1,0:T(8,128)(2,1)S(1)} %collective-permute-done.21), channel_id=1, source_target_pairs={{8,24},{9,25},{10,26},{11,27},{12,28},{13,29},{14,30},{15,31}} | collective-permute-start | bytes 786440 | tf_op jit(solution)/shard_map/ppermute | solution.py:171
  87.5 12.9 %collective-permute-start.29 = (bf16[4,128,256]{2,1,0:T(8,128)(2,1)S(1)}, bf16[4,128,256]{2,1,0:T(8,128)(2,1)S(1)}, u32[]{:S(2)}, u32[]{:S(2)}) collective-permute-start(bf16[4,128,256]{2,1,0:T(8,128)(2,1)S(1)} %shard_map.70), channel_id=1, source_target_pairs={{8,16},{16,24},{9,17},{17,25},{10,18},{18,26},{11,19},{19,27},{12,... | collective-permute-start | bytes 786440 | tf_op jit(solution)/shard_map/ppermute | solution.py:171
  93.2 16.2 %collective-permute-start.28 = (bf16[4,128,256]{2,1,0:T(8,128)(2,1)S(1)}, bf16[4,128,256]{2,1,0:T(8,128)(2,1)S(1)}, u32[]{:S(2)}, u32[]{:S(2)}) collective-permute-start(bf16[4,128,256]{2,1,0:T(8,128)(2,1)S(1)} %collective-permute-done.19), channel_id=1, source_target_pairs={{8,24},{9,25},{10,26},{11,27},{12,28},{13,29},{14,30},{15,31}} | collective-permute-start | bytes 786440 | tf_op jit(solution)/shard_map/ppermute | solution.py:171
  93.9 15.5 %collective-permute-start.27 = (bf16[4,128,256]{2,1,0:T(8,128)(2,1)S(1)}, bf16[4,128,256]{2,1,0:T(8,128)(2,1)S(1)}, u32[]{:S(2)}, u32[]{:S(2)}) collective-permute-start(bf16[4,128,256]{2,1,0:T(8,128)(2,1)S(1)} %add_convert_fusion.3.field), channel_id=1, source_target_pairs={{8,16},{16,24},{9,17},{17,25},{10,18},{18,26},{11,19},{19,27},{12,... | collective-permute-start | bytes 786440 | tf_op jit(solution)/shard_map/ppermute | solution.py:171
  100.6 5.5 %collective-permute-start.31 = (bf16[1,128,256]{2,1,0:T(8,128)(2,1)S(1)}, bf16[1,128,256]{2,1,0:T(8,128)(2,1)S(1)}, u32[]{:S(2)}, u32[]{:S(2)}) collective-permute-start(bf16[1,128,256]{2,1,0:T(8,128)(2,1)S(1)} %get-tuple-element.134), channel_id=1, source_target_pairs={{0,1},{1,0},{2,3},{3,2},{4,5},{5,4},{6,7},{7,6},{8,9},{9,8},{10,11... | collective-permute-start | bytes 196616 | tf_op jit(solution)/shard_map/ppermute | solution.py:137
  102.7 5.6 %collective-permute-start.32 = (bf16[1,128,256]{2,1,0:T(8,128)(2,1)S(1)}, bf16[1,128,256]{2,1,0:T(8,128)(2,1)S(1)}, u32[]{:S(2)}, u32[]{:S(2)}) collective-permute-start(bf16[1,128,256]{2,1,0:T(8,128)(2,1)S(1)} %get-tuple-element.133), channel_id=1, source_target_pairs={{1,2},{2,1},{3,4},{4,3},{5,6},{6,5},{9,10},{10,9},{11,12},{12,11},... | collective-permute-start | bytes 196616 | tf_op jit(solution)/shard_map/ppermute | solution.py:137
  109.7 3.9 %collective-permute-start.33 = (bf16[1,128,256]{2,1,0:T(8,128)(2,1)S(1)}, bf16[1,128,256]{2,1,0:T(8,128)(2,1)S(1)}, u32[]{:S(2)}, u32[]{:S(2)}) collective-permute-start(bf16[1,128,256]{2,1,0:T(8,128)(2,1)S(1)} %get-tuple-element.132), channel_id=1, source_target_pairs={{0,1},{1,0},{2,3},{3,2},{4,5},{5,4},{6,7},{7,6},{8,9},{9,8},{10,11... | collective-permute-start | bytes 196616 | tf_op jit(solution)/shard_map/ppermute | solution.py:137
  109.8 5.7 %collective-permute-start.34 = (bf16[1,128,256]{2,1,0:T(8,128)(2,1)S(1)}, bf16[1,128,256]{2,1,0:T(8,128)(2,1)S(1)}, u32[]{:S(2)}, u32[]{:S(2)}) collective-permute-start(bf16[1,128,256]{2,1,0:T(8,128)(2,1)S(1)} %get-tuple-element.131), channel_id=1, source_target_pairs={{1,2},{2,1},{3,4},{4,3},{5,6},{6,5},{9,10},{10,9},{11,12},{12,11},... | collective-permute-start | bytes 196616 | tf_op jit(solution)/shard_map/ppermute | solution.py:137

commit v9 on v8

--- a/solution.py
+++ b/solution.py
@@ -169,6 +169,10 @@
 
     def send(block, pairs):
         return lax.ppermute(block, "section", pairs) if pairs else block
+
+    def relay(block):
+        groups = [[0, half]] + [[j, sections - j] for j in range(1, half)]
+        return lax.all_gather(block, "section", axis_index_groups=groups)[0]
 
     def join(held, skip):
         total = (held.astype(jnp.float32) + skip.astype(jnp.float32)).astype(jnp.bfloat16)
@@ -215,11 +219,11 @@
             onward = [(j, j + 1) for j in range(1, sections - 1)] if slot > 0 else []
             if slot < ticks - 1:
                 onward = [(0, 1)] + onward
+            received, relays = {}, {k: relay(newer[k]) for k in newer}
             first, second = lax.optimization_barrier((first, second))
-            received, relays = {1: send(second, onward), 0: send(first, onward)}, {}
+            received[1] = send(second, onward)
+            received[0] = send(first, onward)
             if slot > 0:
-                held, _ = lax.optimization_barrier((newer, second))
-                relays = {k: send(held[k], [(1, sections - 1)]) for k in (1, 0)}
                 if across:
                     direct = {0: send(first, across), 1: send(second, across)}
             older, newer, relayed = newer, received, relays

time: 118 us -> 164 us (1.39)
  blocking collectives: 0 us -> 74.6 us
  waiting for transfers between devices: 20.8 us -> 5.65 us
  starting transfers between devices: 67 us -> 53.6 us
    all_gather x0 -> x6, blocking collectives: none -> 74.6 us  [relay(): return lax.all_gather(block, 'section', axis_index_groups=groups)[0]]
    ppermute x15 -> x9, waiting for transfers between devices: 12.3 us -> 1.45 us  [send(): return lax.ppermute(block, 'section', pairs) if pairs else block]
    ppermute x15 -> x9, starting transfers between devices: 25.8 us -> 15.3 us  [send(): return lax.ppermute(block, 'section', pairs) if pairs else block]
    ppermute x20, waiting for transfers between devices: 8.41 us -> 4.2 us  [swap(): lax.ppermute(lax.dynamic_slice_in_dim(block, starts[turn], 1, axis=0), 'd...]
    ppermute x20, starting transfers between devices: 41.2 us -> 38.3 us  [swap(): lax.ppermute(lax.dynamic_slice_in_dim(block, starts[turn], 1, axis=0), 'd...]
  transfers between devices with their start and end apart: 35 -> 29, of which waited for: 11 -> 5; matrix products, arithmetic and copies ran while one was open for 1% -> 1% of each run, Pallas kernels for 19% -> 14%
where the time goes in v9:
time: 164 us
  blocking collectives  74.6 us (45%)
  starting transfers between devices  53.6 us (33%)
  Pallas kernels  26.6 us (16%)
  waiting for transfers between devices  5.65 us (3%)
    all_gather x6, blocking collectives, relay(): return lax.all_gather(block, 'section', axis_index_groups=groups)[0]  74.6 us
    ppermute x20, starting transfers between devices, swap(): lax.ppermute(lax.dynamic_slice_in_dim(block, starts[turn], 1, axis=0), 'd...  38.3 us
    pallas_call x20, Pallas kernels, call(): pl.pallas_call(functools.partial(kernel, width), out_shape=[jax.ShapeDtyp...  26.6 us
    ppermute x9, starting transfers between devices, send(): return lax.ppermute(block, 'section', pairs) if pairs else block  15.3 us
    ppermute x20, waiting for transfers between devices, swap(): lax.ppermute(lax.dynamic_slice_in_dim(block, starts[turn], 1, axis=0), 'd...  4.2 us
  transfers between devices with their start and end apart: 29, of which 5 were waited for; matrix products, arithmetic and copies ran while one was open for 1% of the time, Pallas kernels for 14%

profile of v9, /device:TPU:13, one launch (start us, length us, event | category | flops | bytes accessed | tf_op | source)
XLA Modules:
  0.0 163.6 jit_solution(237958840886791901)
XLA Ops:
  0.0 1.3 collective-permute-start.2
  1.3 1.1 slice_bitcast_fusion.6
  3.1 3.1 %collective-permute-start.1 = (bf16[1,128,256]{2,1,0:T(8,128)(2,1)S(1)}, bf16[1,128,256]{2,1,0:T(8,128)(2,1)S(1)}, u32[]{:S(2)}, u32[]{:S(2)}) collective-permute-start(bf16[1,128,256]{2,1,0:T(8,128)(2,1)S(1)} %get-tuple-element.137), channel_id=1, source_target_pairs={{1,2},{2,1},{3,4},{4,3},{5,6},{6,5},{9,10},{10,9},{11,12},{12,11},... | collective-permute-start | bytes 196616 | tf_op jit(solution)/shard_map/ppermute | solution.py:137
  6.2 3.2 %shard_map.55 = (bf16[4,128,256]{2,1,0:T(8,128)(2,1)S(1)}, bf16[4,144,256]{2,1,0:T(8,128)(2,1)S(1)}, f32[2,128,256]{2,1,0:T(8,128)S(1)}, bf16[6912,256]{1,0:T(8,128)(2,1)S(1)}) custom-call(bf16[4,128,256]{2,1,0:T(8,128)(2,1)S(1)} %get-tuple-element.118.field.rest_0_, bf16[6912,256]{1,0:T(8,128)(2,1)} %bitcast.58), custom_call_target="tpu_custom_call" | custom-call | flops 1 | bytes 1 | tf_op jit(solution)/shard_map/pallas_call | solution.py:99
  9.5 1.2 shard_map.56.field
  10.8 3.6 %collective-permute-start.6 = (bf16[1,128,256]{2,1,0:T(8,128)(2,1)S(1)}, bf16[1,128,256]{2,1,0:T(8,128)(2,1)S(1)}, u32[]{:S(2)}, u32[]{:S(2)}) collective-permute-start(bf16[1,128,256]{2,1,0:T(8,128)(2,1)S(1)} %get-tuple-element.133), channel_id=1, source_target_pairs={{1,2},{2,1},{3,4},{4,3},{5,6},{6,5},{9,10},{10,9},{11,12},{12,11},... | collective-permute-start | bytes 196616 | tf_op jit(solution)/shard_map/ppermute | solution.py:137
  14.4 1.4 collective-permute-done.2
  16.1 1.6 collective-permute-start.3
  17.7 3.1 %collective-permute-start.4 = (bf16[1,128,256]{2,1,0:T(8,128)(2,1)S(1)}, bf16[1,128,256]{2,1,0:T(8,128)(2,1)S(1)}, u32[]{:S(2)}, u32[]{:S(2)}) collective-permute-start(bf16[1,128,256]{2,1,0:T(8,128)(2,1)S(1)} %get-tuple-element.135), channel_id=1, source_target_pairs={{1,2},{2,1},{3,4},{4,3},{5,6},{6,5},{9,10},{10,9},{11,12},{12,11},... | collective-permute-start | bytes 196616 | tf_op jit(solution)/shard_map/ppermute | solution.py:137
  20.8 1.2 shard_map.57
  22.0 1.2 shard_map.58
  23.2 1.2 shard_map.59
  25.1 1.2 shard_map.60.field
  26.4 3.6 %collective-permute-start.9 = (bf16[1,128,256]{2,1,0:T(8,128)(2,1)S(1)}, bf16[1,128,256]{2,1,0:T(8,128)(2,1)S(1)}, u32[]{:S(2)}, u32[]{:S(2)}) collective-permute-start(bf16[1,128,256]{2,1,0:T(8,128)(2,1)S(1)} %get-tuple-element.131), channel_id=1, source_target_pairs={{1,2},{2,1},{3,4},{4,3},{5,6},{6,5},{9,10},{10,9},{11,12},{12,11},... | collective-permute-start | bytes 196616 | tf_op jit(solution)/shard_map/ppermute | solution.py:137
  30.0 1.2 shard_map.61
  32.1 1.2 shard_map.62
  33.3 3.1 %collective-permute-start.12 = (bf16[4,128,256]{2,1,0:T(8,128)(2,1)S(1)}, bf16[4,128,256]{2,1,0:T(8,128)(2,1)S(1)}, u32[]{:S(2)}, u32[]{:S(2)}) collective-permute-start(bf16[4,128,256]{2,1,0:T(8,128)(2,1)S(1)} %shard_map.62), channel_id=1, source_target_pairs={{0,8},{8,16},{16,24},{1,9},{9,17},{17,25},{2,10},{10,18},{18,26},{... | collective-permute-start | bytes 786440 | tf_op jit(solution)/shard_map/ppermute | solution.py:171
  37.1 1.9 %collective-permute-start.10 = (bf16[4,128,256]{2,1,0:T(8,128)(2,1)S(1)}, bf16[4,128,256]{2,1,0:T(8,128)(2,1)S(1)}, u32[]{:S(2)}, u32[]{:S(2)}) collective-permute-start(bf16[4,128,256]{2,1,0:T(8,128)(2,1)S(1)} %shard_map.60.field), channel_id=1, source_target_pairs={{0,8},{8,16},{16,24},{1,9},{9,17},{17,25},{2,10},{10,18},{18,26},{... | collective-permute-start | bytes 786440 | tf_op jit(solution)/shard_map/ppermute | solution.py:171
  39.1 16.5 %all-gather.1 = bf16[8,128,256]{2,1,0:T(8,128)(2,1)S(1)} all-gather(bf16[4,128,256]{2,1,0:T(8,128)(2,1)S(1)} %collective-permute-done.11), channel_id=3, replica_groups={{0,16},{8,24},{1,17},{9,25},{2,18},{10,26},{3,19},{11,27},{4,20},{12,28..., dimensions={0}, use_global_device_ids=true | all-gather | bytes 786432 | tf_op jit(solution)/shard_map/all_gather | solution.py:175
  56.3 3.1 %collective-permute-start.14 = (bf16[1,128,256]{2,1,0:T(8,128)(2,1)S(1)}, bf16[1,128,256]{2,1,0:T(8,128)(2,1)S(1)}, u32[]{:S(2)}, u32[]{:S(2)}) collective-permute-start(bf16[1,128,256]{2,1,0:T(8,128)(2,1)S(1)} %get-tuple-element.129), channel_id=1, source_target_pairs={{1,2},{2,1},{3,4},{4,3},{5,6},{6,5},{9,10},{10,9},{11,12},{12,11},... | collective-permute-start | bytes 196616 | tf_op jit(solution)/shard_map/ppermute | solution.py:137
  59.4 8.2 %all-gather = bf16[8,128,256]{2,1,0:T(8,128)(2,1)S(1)} all-gather(bf16[4,128,256]{2,1,0:T(8,128)(2,1)S(1)} %collective-permute-done.7), channel_id=2, replica_groups={{0,16},{8,24},{1,17},{9,25},{2,18},{10,26},{3,19},{11,27},{4,20},{12,28..., dimensions={0}, use_global_device_ids=true | all-gather | bytes 786432 | tf_op jit(solution)/shard_map/all_gather | solution.py:175
  67.6 1.2 shard_map.63
  68.8 1.2 shard_map.64
  70.3 3.3 %collective-permute-start.16 = (bf16[1,128,256]{2,1,0:T(8,128)(2,1)S(1)}, bf16[1,128,256]{2,1,0:T(8,128)(2,1)S(1)}, u32[]{:S(2)}, u32[]{:S(2)}) collective-permute-start(bf16[1,128,256]{2,1,0:T(8,128)(2,1)S(1)} %get-tuple-element.127), channel_id=1, source_target_pairs={{1,2},{2,1},{3,4},{4,3},{5,6},{6,5},{9,10},{10,9},{11,12},{12,11},... | collective-permute-start | bytes 196616 | tf_op jit(solution)/shard_map/ppermute | solution.py:137
  73.6 1.2 shard_map.65
  74.8 1.2 collective-permute-done.16.far
  76.0 1.2 shard_map.66
  77.2 1.9 %collective-permute-start.18 = (bf16[4,128,256]{2,1,0:T(8,128)(2,1)S(1)}, bf16[4,128,256]{2,1,0:T(8,128)(2,1)S(1)}, u32[]{:S(2)}, u32[]{:S(2)}) collective-permute-start(bf16[4,128,256]{2,1,0:T(8,128)(2,1)S(1)} %shard_map.66), channel_id=1, source_target_pairs={{0,8},{8,16},{16,24},{1,9},{9,17},{17,25},{2,10},{10,18},{18,26},{... | collective-permute-start | bytes 786440 | tf_op jit(solution)/shard_map/ppermute | solution.py:171
  79.1 14.3 %all-gather.3 = bf16[8,128,256]{2,1,0:T(8,128)(2,1)S(1)} all-gather(bf16[4,128,256]{2,1,0:T(8,128)(2,1)S(1)} %collective-permute-done.12), channel_id=5, replica_groups={{0,16},{8,24},{1,17},{9,25},{2,18},{10,26},{3,19},{11,27},{4,20},{12,28..., dimensions={0}, use_global_device_ids=true | all-gather | bytes 786432 | tf_op jit(solution)/shard_map/all_gather | solution.py:175
  93.4 1.9 %collective-permute-start.17 = (bf16[4,128,256]{2,1,0:T(8,128)(2,1)S(1)}, bf16[4,128,256]{2,1,0:T(8,128)(2,1)S(1)}, u32[]{:S(2)}, u32[]{:S(2)}) collective-permute-start(bf16[4,128,256]{2,1,0:T(8,128)(2,1)S(1)} %add_convert_fusion.6.field), channel_id=1, source_target_pairs={{0,8},{8,16},{16,24},{1,9},{9,17},{17,25},{2,10},{10,18},{18,26},{... | collective-permute-start | bytes 786440 | tf_op jit(solution)/shard_map/ppermute | solution.py:171
  96.3 3.2 %collective-permute-start.20 = (bf16[1,128,256]{2,1,0:T(8,128)(2,1)S(1)}, bf16[1,128,256]{2,1,0:T(8,128)(2,1)S(1)}, u32[]{:S(2)}, u32[]{:S(2)}) collective-permute-start(bf16[1,128,256]{2,1,0:T(8,128)(2,1)S(1)} %get-tuple-element.125), channel_id=1, source_target_pairs={{1,2},{2,1},{3,4},{4,3},{5,6},{6,5},{9,10},{10,9},{11,12},{12,11},... | collective-permute-start | bytes 196616 | tf_op jit(solution)/shard_map/ppermute | solution.py:137
  99.5 10.6 %all-gather.2 = bf16[8,128,256]{2,1,0:T(8,128)(2,1)S(1)} all-gather(bf16[4,128,256]{2,1,0:T(8,128)(2,1)S(1)} %collective-permute-done.10), channel_id=4, replica_groups={{0,16},{8,24},{1,17},{9,25},{2,18},{10,26},{3,19},{11,27},{4,20},{12,28..., dimensions={0}, use_global_device_ids=true | all-gather | bytes 786432 | tf_op jit(solution)/shard_map/all_gather | solution.py:175
  110.1 1.2 shard_map.67
  111.3 1.2 shard_map.68
  113.2 3.3 %collective-permute-start.22 = (bf16[1,128,256]{2,1,0:T(8,128)(2,1)S(1)}, bf16[1,128,256]{2,1,0:T(8,128)(2,1)S(1)}, u32[]{:S(2)}, u32[]{:S(2)}) collective-permute-start(bf16[1,128,256]{2,1,0:T(8,128)(2,1)S(1)} %get-tuple-element.123), channel_id=1, source_target_pairs={{1,2},{2,1},{3,4},{4,3},{5,6},{6,5},{9,10},{10,9},{11,12},{12,11},... | collective-permute-start | bytes 196616 | tf_op jit(solution)/shard_map/ppermute | solution.py:137
  116.5 1.2 shard_map.69
  117.7 1.1 collective-permute-done.22.far
  118.8 1.2 shard_map.70
  120.0 1.9 %collective-permute-start.24 = (bf16[4,128,256]{2,1,0:T(8,128)(2,1)S(1)}, bf16[4,128,256]{2,1,0:T(8,128)(2,1)S(1)}, u32[]{:S(2)}, u32[]{:S(2)}) collective-permute-start(bf16[4,128,256]{2,1,0:T(8,128)(2,1)S(1)} %shard_map.70), channel_id=1, source_target_pairs={{8,16},{16,24},{9,17},{17,25},{10,18},{18,26},{11,19},{19,27},{12,... | collective-permute-start | bytes 786440 | tf_op jit(solution)/shard_map/ppermute | solution.py:171
  121.9 14.4 %all-gather.5 = bf16[8,128,256]{2,1,0:T(8,128)(2,1)S(1)} all-gather(bf16[4,128,256]{2,1,0:T(8,128)(2,1)S(1)} %collective-permute-done.18), channel_id=7, replica_groups={{0,16},{8,24},{1,17},{9,25},{2,18},{10,26},{3,19},{11,27},{4,20},{12,28..., dimensions={0}, use_global_device_ids=true | all-gather | bytes 786432 | tf_op jit(solution)/shard_map/all_gather | solution.py:175
  136.3 1.9 %collective-permute-start.23 = (bf16[4,128,256]{2,1,0:T(8,128)(2,1)S(1)}, bf16[4,128,256]{2,1,0:T(8,128)(2,1)S(1)}, u32[]{:S(2)}, u32[]{:S(2)}) collective-permute-start(bf16[4,128,256]{2,1,0:T(8,128)(2,1)S(1)} %add_convert_fusion.3.field), channel_id=1, source_target_pairs={{8,16},{16,24},{9,17},{17,25},{10,18},{18,26},{11,19},{19,27},{12,... | collective-permute-start | bytes 786440 | tf_op jit(solution)/shard_map/ppermute | solution.py:171
  139.1 3.2 %collective-permute-start.26 = (bf16[1,128,256]{2,1,0:T(8,128)(2,1)S(1)}, bf16[1,128,256]{2,1,0:T(8,128)(2,1)S(1)}, u32[]{:S(2)}, u32[]{:S(2)}) collective-permute-start(bf16[1,128,256]{2,1,0:T(8,128)(2,1)S(1)} %get-tuple-element.121), channel_id=1, source_target_pairs={{1,2},{2,1},{3,4},{4,3},{5,6},{6,5},{9,10},{10,9},{11,12},{12,11},... | collective-permute-start | bytes 196616 | tf_op jit(solution)/shard_map/ppermute | solution.py:137
  142.3 10.6 %all-gather.4 = bf16[8,128,256]{2,1,0:T(8,128)(2,1)S(1)} all-gather(bf16[4,128,256]{2,1,0:T(8,128)(2,1)S(1)} %collective-permute-done.17), channel_id=6, replica_groups={{0,16},{8,24},{1,17},{9,25},{2,18},{10,26},{3,19},{11,27},{4,20},{12,28..., dimensions={0}, use_global_device_ids=true | all-gather | bytes 786432 | tf_op jit(solution)/shard_map/all_gather | solution.py:175
  152.9 1.2 shard_map.71
  154.1 1.2 shard_map.72
  156.0 3.3 %collective-permute-start.28 = (bf16[1,128,256]{2,1,0:T(8,128)(2,1)S(1)}, bf16[1,128,256]{2,1,0:T(8,128)(2,1)S(1)}, u32[]{:S(2)}, u32[]{:S(2)}) collective-permute-start(bf16[1,128,256]{2,1,0:T(8,128)(2,1)S(1)} %get-tuple-element.119), channel_id=1, source_target_pairs={{1,2},{2,1},{3,4},{4,3},{5,6},{6,5},{9,10},{10,9},{11,12},{12,11},... | collective-permute-start | bytes 196616 | tf_op jit(solution)/shard_map/ppermute | solution.py:137
  159.3 1.2 shard_map.73
  161.6 2.0 %shard_map.74 = bf16[2,4,128,256]{3,2,1,0:T(8,128)(2,1)} custom-call(s32[1]{0:T(128)} %bitcast.flags, bf16[1,128,256]{2,1,0:T(8,128)(2,1)S(1)} %collective-permute-done.27.near, bf16[1,128,256]{2,1,0:T(8,128)(2,1)S(1)} %collective-permute-done.28.far, bf16[4,128,256]{2,1,0:T(8,128)(2,1)S(1)} %get-tuple-element.112.even, ...), custom_call_target="tpu_custom_call" | custom-call | flops 1 | bytes 1 | tf_op jit(solution)/shard_map/pallas_call | solution.py:99
  (60 shorter events, 8.6 us)
Async XLA Ops:
  0.0 15.8 %collective-permute-start.2 = (bf16[2,4,128,256]{3,2,1,0:T(8,128)(2,1)}, bf16[2,4,128,256]{3,2,1,0:T(8,128)(2,1)S(1)}, u32[]{:S(2)}, u32[]{:S(2)}) collective-permute-start(bf16[2,4,128,256]{3,2,1,0:T(8,128)(2,1)} %bitcast.66), channel_id=1, source_target_pairs={{0,24},{8,16},{1,25},{9,17},{2,26},{10,18},{3,27},{11,19},{4,28},{... | collective-permute-start | bytes 1572872 | tf_op jit(solution)/shard_map/ppermute | solution.py:171
  2.4 7.0 %collective-permute-start = (bf16[1,128,256]{2,1,0:T(8,128)(2,1)S(1)}, bf16[1,128,256]{2,1,0:T(8,128)(2,1)S(1)}, u32[]{:S(2)}, u32[]{:S(2)}) collective-permute-start(bf16[1,128,256]{2,1,0:T(8,128)(2,1)S(1)} %get-tuple-element.138), channel_id=1, source_target_pairs={{0,1},{1,0},{2,3},{3,2},{4,5},{5,4},{6,7},{7,6},{8,9},{9,8},{10,11... | collective-permute-start | bytes 196616 | tf_op jit(solution)/shard_map/ppermute | solution.py:137
  3.1 6.3 %collective-permute-start.1 = (bf16[1,128,256]{2,1,0:T(8,128)(2,1)S(1)}, bf16[1,128,256]{2,1,0:T(8,128)(2,1)S(1)}, u32[]{:S(2)}, u32[]{:S(2)}) collective-permute-start(bf16[1,128,256]{2,1,0:T(8,128)(2,1)S(1)} %get-tuple-element.137), channel_id=1, source_target_pairs={{1,2},{2,1},{3,4},{4,3},{5,6},{6,5},{9,10},{10,9},{11,12},{12,11},... | collective-permute-start | bytes 196616 | tf_op jit(solution)/shard_map/ppermute | solution.py:137
  6.2 9.5 %copy-start.2 = (bf16[1,2,4,16,8,256]{5,4,3,2,1,0:T(8,128)(2,1)S(1)}, bf16[1,2,4,16,8,256]{5,4,3,2,1,0:T(8,128)(2,1)}, u32[]{:S(2)}) copy-start(bf16[1,2,4,16,8,256]{5,4,3,2,1,0:T(8,128)(2,1)} %param.5) | copy-start | bytes 1572868
  9.5 6.3 %copy-start.1 = (bf16[3,2,4,16,8,256]{5,4,3,2,1,0:T(8,128)(2,1)S(1)}, bf16[3,2,4,16,8,256]{5,4,3,2,1,0:T(8,128)(2,1)}, u32[]{:S(2)}) copy-start(bf16[3,2,4,16,8,256]{5,4,3,2,1,0:T(8,128)(2,1)} %param.7) | copy-start | bytes 4718596
  9.5 11.3 %copy-start = (bf16[1,3,3,3,256,256]{5,4,3,2,1,0:T(8,128)(2,1)S(1)}, bf16[1,3,3,3,256,256]{5,4,3,2,1,0:T(8,128)(2,1)}, u32[]{:S(2)}) copy-start(bf16[1,3,3,3,256,256]{5,4,3,2,1,0:T(8,128)(2,1)} %param.9) | copy-start | bytes 10616836
  10.7 11.3 %collective-permute-start.5 = (bf16[1,128,256]{2,1,0:T(8,128)(2,1)S(1)}, bf16[1,128,256]{2,1,0:T(8,128)(2,1)S(1)}, u32[]{:S(2)}, u32[]{:S(2)}) collective-permute-start(bf16[1,128,256]{2,1,0:T(8,128)(2,1)S(1)} %get-tuple-element.134), channel_id=1, source_target_pairs={{0,1},{1,0},{2,3},{3,2},{4,5},{5,4},{6,7},{7,6},{8,9},{9,8},{10,11... | collective-permute-start | bytes 196616 | tf_op jit(solution)/shard_map/ppermute | solution.py:137
  10.8 11.2 %collective-permute-start.6 = (bf16[1,128,256]{2,1,0:T(8,128)(2,1)S(1)}, bf16[1,128,256]{2,1,0:T(8,128)(2,1)S(1)}, u32[]{:S(2)}, u32[]{:S(2)}) collective-permute-start(bf16[1,128,256]{2,1,0:T(8,128)(2,1)S(1)} %get-tuple-element.133), channel_id=1, source_target_pairs={{1,2},{2,1},{3,4},{4,3},{5,6},{6,5},{9,10},{10,9},{11,12},{12,11},... | collective-permute-start | bytes 196616 | tf_op jit(solution)/shard_map/ppermute | solution.py:137
  16.1 8.4 %collective-permute-start.3 = (bf16[1,128,256]{2,1,0:T(8,128)(2,1)S(1)}, bf16[1,128,256]{2,1,0:T(8,128)(2,1)S(1)}, u32[]{:S(2)}, u32[]{:S(2)}) collective-permute-start(bf16[1,128,256]{2,1,0:T(8,128)(2,1)S(1)} %get-tuple-element.136), channel_id=1, source_target_pairs={{0,1},{1,0},{2,3},{3,2},{4,5},{5,4},{6,7},{7,6},{8,9},{9,8},{10,11... | collective-permute-start | bytes 196616 | tf_op jit(solution)/shard_map/ppermute | solution.py:137
  17.7 6.8 %collective-permute-start.4 = (bf16[1,128,256]{2,1,0:T(8,128)(2,1)S(1)}, bf16[1,128,256]{2,1,0:T(8,128)(2,1)S(1)}, u32[]{:S(2)}, u32[]{:S(2)}) collective-permute-start(bf16[1,128,256]{2,1,0:T(8,128)(2,1)S(1)} %get-tuple-element.135), channel_id=1, source_target_pairs={{1,2},{2,1},{3,4},{4,3},{5,6},{6,5},{9,10},{10,9},{11,12},{12,11},... | collective-permute-start | bytes 196616 | tf_op jit(solution)/shard_map/ppermute | solution.py:137
  24.5 14.6 %collective-permute-start.11 = (bf16[4,128,256]{2,1,0:T(8,128)(2,1)S(1)}, bf16[4,128,256]{2,1,0:T(8,128)(2,1)S(1)}, u32[]{:S(2)}, u32[]{:S(2)}) collective-permute-start(bf16[4,128,256]{2,1,0:T(8,128)(2,1)S(1)} %shard_map.58), channel_id=1, source_target_pairs={{0,8},{1,9},{2,10},{3,11},{4,12},{5,13},{6,14},{7,15}} | collective-permute-start | bytes 786440 | tf_op jit(solution)/shard_map/ppermute | solution.py:171
  26.4 4.9 %collective-permute-start.8 = (bf16[1,128,256]{2,1,0:T(8,128)(2,1)S(1)}, bf16[1,128,256]{2,1,0:T(8,128)(2,1)S(1)}, u32[]{:S(2)}, u32[]{:S(2)}) collective-permute-start(bf16[1,128,256]{2,1,0:T(8,128)(2,1)S(1)} %get-tuple-element.132), channel_id=1, source_target_pairs={{0,1},{1,0},{2,3},{3,2},{4,5},{5,4},{6,7},{7,6},{8,9},{9,8},{10,11... | collective-permute-start | bytes 196616 | tf_op jit(solution)/shard_map/ppermute | solution.py:137
  26.4 5.7 %collective-permute-start.9 = (bf16[1,128,256]{2,1,0:T(8,128)(2,1)S(1)}, bf16[1,128,256]{2,1,0:T(8,128)(2,1)S(1)}, u32[]{:S(2)}, u32[]{:S(2)}) collective-permute-start(bf16[1,128,256]{2,1,0:T(8,128)(2,1)S(1)} %get-tuple-element.131), channel_id=1, source_target_pairs={{1,2},{2,1},{3,4},{4,3},{5,6},{6,5},{9,10},{10,9},{11,12},{12,11},... | collective-permute-start | bytes 196616 | tf_op jit(solution)/shard_map/ppermute | solution.py:137
  33.3 22.3 %collective-permute-start.12 = (bf16[4,128,256]{2,1,0:T(8,128)(2,1)S(1)}, bf16[4,128,256]{2,1,0:T(8,128)(2,1)S(1)}, u32[]{:S(2)}, u32[]{:S(2)}) collective-permute-start(bf16[4,128,256]{2,1,0:T(8,128)(2,1)S(1)} %shard_map.62), channel_id=1, source_target_pairs={{0,8},{8,16},{16,24},{1,9},{9,17},{17,25},{2,10},{10,18},{18,26},{... | collective-permute-start | bytes 786440 | tf_op jit(solution)/shard_map/ppermute | solution.py:171
  36.5 22.9 %collective-permute-start.7 = (bf16[4,128,256]{2,1,0:T(8,128)(2,1)S(1)}, bf16[4,128,256]{2,1,0:T(8,128)(2,1)S(1)}, u32[]{:S(2)}, u32[]{:S(2)}) collective-permute-start(bf16[4,128,256]{2,1,0:T(8,128)(2,1)S(1)} %shard_map.56.field), channel_id=1, source_target_pairs={{0,8},{1,9},{2,10},{3,11},{4,12},{5,13},{6,14},{7,15}} | collective-permute-start | bytes 786440 | tf_op jit(solution)/shard_map/ppermute | solution.py:171
  37.1 32.9 %collective-permute-start.10 = (bf16[4,128,256]{2,1,0:T(8,128)(2,1)S(1)}, bf16[4,128,256]{2,1,0:T(8,128)(2,1)S(1)}, u32[]{:S(2)}, u32[]{:S(2)}) collective-permute-start(bf16[4,128,256]{2,1,0:T(8,128)(2,1)S(1)} %shard_map.60.field), channel_id=1, source_target_pairs={{0,8},{8,16},{16,24},{1,9},{9,17},{17,25},{2,10},{10,18},{18,26},{... | collective-permute-start | bytes 786440 | tf_op jit(solution)/shard_map/ppermute | solution.py:171
  55.7 13.1 %collective-permute-start.13 = (bf16[1,128,256]{2,1,0:T(8,128)(2,1)S(1)}, bf16[1,128,256]{2,1,0:T(8,128)(2,1)S(1)}, u32[]{:S(2)}, u32[]{:S(2)}) collective-permute-start(bf16[1,128,256]{2,1,0:T(8,128)(2,1)S(1)} %get-tuple-element.130), channel_id=1, source_target_pairs={{0,1},{1,0},{2,3},{3,2},{4,5},{5,4},{6,7},{7,6},{8,9},{9,8},{10,11... | collective-permute-start | bytes 196616 | tf_op jit(solution)/shard_map/ppermute | solution.py:137
  56.3 12.5 %collective-permute-start.14 = (bf16[1,128,256]{2,1,0:T(8,128)(2,1)S(1)}, bf16[1,128,256]{2,1,0:T(8,128)(2,1)S(1)}, u32[]{:S(2)}, u32[]{:S(2)}) collective-permute-start(bf16[1,128,256]{2,1,0:T(8,128)(2,1)S(1)} %get-tuple-element.129), channel_id=1, source_target_pairs={{1,2},{2,1},{3,4},{4,3},{5,6},{6,5},{9,10},{10,9},{11,12},{12,11},... | collective-permute-start | bytes 196616 | tf_op jit(solution)/shard_map/ppermute | solution.py:137
  70.2 4.6 %collective-permute-start.15 = (bf16[1,128,256]{2,1,0:T(8,128)(2,1)S(1)}, bf16[1,128,256]{2,1,0:T(8,128)(2,1)S(1)}, u32[]{:S(2)}, u32[]{:S(2)}) collective-permute-start(bf16[1,128,256]{2,1,0:T(8,128)(2,1)S(1)} %get-tuple-element.128), channel_id=1, source_target_pairs={{0,1},{1,0},{2,3},{3,2},{4,5},{5,4},{6,7},{7,6},{8,9},{9,8},{10,11... | collective-permute-start | bytes 196616 | tf_op jit(solution)/shard_map/ppermute | solution.py:137
  70.3 5.7 %collective-permute-start.16 = (bf16[1,128,256]{2,1,0:T(8,128)(2,1)S(1)}, bf16[1,128,256]{2,1,0:T(8,128)(2,1)S(1)}, u32[]{:S(2)}, u32[]{:S(2)}) collective-permute-start(bf16[1,128,256]{2,1,0:T(8,128)(2,1)S(1)} %get-tuple-element.127), channel_id=1, source_target_pairs={{1,2},{2,1},{3,4},{4,3},{5,6},{6,5},{9,10},{10,9},{11,12},{12,11},... | collective-permute-start | bytes 196616 | tf_op jit(solution)/shard_map/ppermute | solution.py:137
  77.2 18.2 %collective-permute-start.18 = (bf16[4,128,256]{2,1,0:T(8,128)(2,1)S(1)}, bf16[4,128,256]{2,1,0:T(8,128)(2,1)S(1)}, u32[]{:S(2)}, u32[]{:S(2)}) collective-permute-start(bf16[4,128,256]{2,1,0:T(8,128)(2,1)S(1)} %shard_map.66), channel_id=1, source_target_pairs={{0,8},{8,16},{16,24},{1,9},{9,17},{17,25},{2,10},{10,18},{18,26},{... | collective-permute-start | bytes 786440 | tf_op jit(solution)/shard_map/ppermute | solution.py:171
  93.4 19.1 %collective-permute-start.17 = (bf16[4,128,256]{2,1,0:T(8,128)(2,1)S(1)}, bf16[4,128,256]{2,1,0:T(8,128)(2,1)S(1)}, u32[]{:S(2)}, u32[]{:S(2)}) collective-permute-start(bf16[4,128,256]{2,1,0:T(8,128)(2,1)S(1)} %add_convert_fusion.6.field), channel_id=1, source_target_pairs={{0,8},{8,16},{16,24},{1,9},{9,17},{17,25},{2,10},{10,18},{18,26},{... | collective-permute-start | bytes 786440 | tf_op jit(solution)/shard_map/ppermute | solution.py:171
  95.5 15.8 %collective-permute-start.19 = (bf16[1,128,256]{2,1,0:T(8,128)(2,1)S(1)}, bf16[1,128,256]{2,1,0:T(8,128)(2,1)S(1)}, u32[]{:S(2)}, u32[]{:S(2)}) collective-permute-start(bf16[1,128,256]{2,1,0:T(8,128)(2,1)S(1)} %get-tuple-element.126), channel_id=1, source_target_pairs={{0,1},{1,0},{2,3},{3,2},{4,5},{5,4},{6,7},{7,6},{8,9},{9,8},{10,11... | collective-permute-start | bytes 196616 | tf_op jit(solution)/shard_map/ppermute | solution.py:137
  96.3 15.0 %collective-permute-start.20 = (bf16[1,128,256]{2,1,0:T(8,128)(2,1)S(1)}, bf16[1,128,256]{2,1,0:T(8,128)(2,1)S(1)}, u32[]{:S(2)}, u32[]{:S(2)}) collective-permute-start(bf16[1,128,256]{2,1,0:T(8,128)(2,1)S(1)} %get-tuple-element.125), channel_id=1, source_target_pairs={{1,2},{2,1},{3,4},{4,3},{5,6},{6,5},{9,10},{10,9},{11,12},{12,11},... | collective-permute-start | bytes 196616 | tf_op jit(solution)/shard_map/ppermute | solution.py:137
  112.7 4.9 %collective-permute-start.21 = (bf16[1,128,256]{2,1,0:T(8,128)(2,1)S(1)}, bf16[1,128,256]{2,1,0:T(8,128)(2,1)S(1)}, u32[]{:S(2)}, u32[]{:S(2)}) collective-permute-start(bf16[1,128,256]{2,1,0:T(8,128)(2,1)S(1)} %get-tuple-element.124), channel_id=1, source_target_pairs={{0,1},{1,0},{2,3},{3,2},{4,5},{5,4},{6,7},{7,6},{8,9},{9,8},{10,11... | collective-permute-start | bytes 196616 | tf_op jit(solution)/shard_map/ppermute | solution.py:137
  113.2 5.6 %collective-permute-start.22 = (bf16[1,128,256]{2,1,0:T(8,128)(2,1)S(1)}, bf16[1,128,256]{2,1,0:T(8,128)(2,1)S(1)}, u32[]{:S(2)}, u32[]{:S(2)}) collective-permute-start(bf16[1,128,256]{2,1,0:T(8,128)(2,1)S(1)} %get-tuple-element.123), channel_id=1, source_target_pairs={{1,2},{2,1},{3,4},{4,3},{5,6},{6,5},{9,10},{10,9},{11,12},{12,11},... | collective-permute-start | bytes 196616 | tf_op jit(solution)/shard_map/ppermute | solution.py:137
  120.0 18.2 %collective-permute-start.24 = (bf16[4,128,256]{2,1,0:T(8,128)(2,1)S(1)}, bf16[4,128,256]{2,1,0:T(8,128)(2,1)S(1)}, u32[]{:S(2)}, u32[]{:S(2)}) collective-permute-start(bf16[4,128,256]{2,1,0:T(8,128)(2,1)S(1)} %shard_map.70), channel_id=1, source_target_pairs={{8,16},{16,24},{9,17},{17,25},{10,18},{18,26},{11,19},{19,27},{12,... | collective-permute-start | bytes 786440 | tf_op jit(solution)/shard_map/ppermute | solution.py:171
  136.3 19.1 %collective-permute-start.23 = (bf16[4,128,256]{2,1,0:T(8,128)(2,1)S(1)}, bf16[4,128,256]{2,1,0:T(8,128)(2,1)S(1)}, u32[]{:S(2)}, u32[]{:S(2)}) collective-permute-start(bf16[4,128,256]{2,1,0:T(8,128)(2,1)S(1)} %add_convert_fusion.3.field), channel_id=1, source_target_pairs={{8,16},{16,24},{9,17},{17,25},{10,18},{18,26},{11,19},{19,27},{12,... | collective-permute-start | bytes 786440 | tf_op jit(solution)/shard_map/ppermute | solution.py:171
  138.3 15.8 %collective-permute-start.25 = (bf16[1,128,256]{2,1,0:T(8,128)(2,1)S(1)}, bf16[1,128,256]{2,1,0:T(8,128)(2,1)S(1)}, u32[]{:S(2)}, u32[]{:S(2)}) collective-permute-start(bf16[1,128,256]{2,1,0:T(8,128)(2,1)S(1)} %get-tuple-element.122), channel_id=1, source_target_pairs={{0,1},{1,0},{2,3},{3,2},{4,5},{5,4},{6,7},{7,6},{8,9},{9,8},{10,11... | collective-permute-start | bytes 196616 | tf_op jit(solution)/shard_map/ppermute | solution.py:137
  139.1 15.0 %collective-permute-start.26 = (bf16[1,128,256]{2,1,0:T(8,128)(2,1)S(1)}, bf16[1,128,256]{2,1,0:T(8,128)(2,1)S(1)}, u32[]{:S(2)}, u32[]{:S(2)}) collective-permute-start(bf16[1,128,256]{2,1,0:T(8,128)(2,1)S(1)} %get-tuple-element.121), channel_id=1, source_target_pairs={{1,2},{2,1},{3,4},{4,3},{5,6},{6,5},{9,10},{10,9},{11,12},{12,11},... | collective-permute-start | bytes 196616 | tf_op jit(solution)/shard_map/ppermute | solution.py:137
  155.6 5.0 %collective-permute-start.27 = (bf16[1,128,256]{2,1,0:T(8,128)(2,1)S(1)}, bf16[1,128,256]{2,1,0:T(8,128)(2,1)S(1)}, u32[]{:S(2)}, u32[]{:S(2)}) collective-permute-start(bf16[1,128,256]{2,1,0:T(8,128)(2,1)S(1)} %get-tuple-element.120), channel_id=1, source_target_pairs={{0,1},{1,0},{2,3},{3,2},{4,5},{5,4},{6,7},{7,6},{8,9},{9,8},{10,11... | collective-permute-start | bytes 196616 | tf_op jit(solution)/shard_map/ppermute | solution.py:137
  156.0 5.6 %collective-permute-start.28 = (bf16[1,128,256]{2,1,0:T(8,128)(2,1)S(1)}, bf16[1,128,256]{2,1,0:T(8,128)(2,1)S(1)}, u32[]{:S(2)}, u32[]{:S(2)}) collective-permute-start(bf16[1,128,256]{2,1,0:T(8,128)(2,1)S(1)} %get-tuple-element.119), channel_id=1, source_target_pairs={{1,2},{2,1},{3,4},{4,3},{5,6},{6,5},{9,10},{10,9},{11,12},{12,11},... | collective-permute-start | bytes 196616 | tf_op jit(solution)/shard_map/ppermute | solution.py:137

commit v10 on v8

--- a/solution.py
+++ b/solution.py
@@ -153,8 +153,9 @@
         "starts": (jnp.where(above, planes - 1, 0), jnp.where(above, 0, planes - 1)),
         "first": section == 0,
         "second": section == 1,
-        "last": section == sections - 1,
+        "before": section == sections - 2,
         "decoder": section >= half,
+        "joins": (section >= half) & (section < sections - 1),
         "direct": (section > half) & (section < sections - 1) if across else (),
     }
     places, resident, previous, incoming, first_weights, second_weights = lax.optimization_barrier(
@@ -170,21 +171,20 @@
     def send(block, pairs):
         return lax.ppermute(block, "section", pairs) if pairs else block
 
-    def join(held, skip):
-        total = (held.astype(jnp.float32) + skip.astype(jnp.float32)).astype(jnp.bfloat16)
-        return jnp.where(places["decoder"], total, held)
-
-    newer, older, relayed, direct = {}, {}, {}, {}
+    def added(block, other):
+        return (block.astype(jnp.float32) + other.astype(jnp.float32)).astype(jnp.bfloat16)
+
+    newer, older, direct = {}, {}, {}
 
     def arrived(slot, stream):
         fresh = incoming[min(slot, ticks - 1) - 1, stream]
         if slot == 1:
-            return jnp.where(places["first"], fresh, join(resident[stream], mirrored[stream]))
-        held = jnp.where(places["second"], older[stream], newer[stream])
-        skip = jnp.where(places["last"], relayed[stream], newer[stream])
-        if across:
-            skip = jnp.where(places["direct"], direct[stream], skip)
-        return jnp.where(places["first"], fresh, join(held, skip))
+            held = jnp.where(places["decoder"], added(resident[stream], mirrored[stream]), resident[stream])
+        else:
+            held = jnp.where(places["second"], older[stream], newer[stream])
+            skip = jnp.where(places["direct"], direct[stream], newer[stream]) if across else newer[stream]
+            held = jnp.where(places["joins"], added(held, skip), held)
+        return jnp.where(places["first"], fresh, held)
 
     def swaps(block):
         return swap(0, starts, block), swap(1, starts, block)
@@ -211,18 +211,25 @@
         if slot == 0:
             p, q, halos = following
             halos, second = lax.optimization_barrier((halos, second))
-        if slot < ticks:
-            onward = [(j, j + 1) for j in range(1, sections - 1)] if slot > 0 else []
+        if slot == 0:
+            whole = jnp.stack([first, second])
+            newer = {1: send(second, [(0, 1)]), 0: send(first, [(0, 1)])}
+        elif slot < ticks:
+            onward = [(j, j + 1) for j in range(1, sections - 1)]
             if slot < ticks - 1:
                 onward = [(0, 1)] + onward
-            first, second = lax.optimization_barrier((first, second))
-            received, relays = {1: send(second, onward), 0: send(first, onward)}, {}
-            if slot > 0:
-                held, _ = lax.optimization_barrier((newer, second))
-                relays = {k: send(held[k], [(1, sections - 1)]) for k in (1, 0)}
-                if across:
-                    direct = {0: send(first, across), 1: send(second, across)}
-            older, newer, relayed = newer, received, relays
+            if slot == 1:
+                newer[1], second = lax.optimization_barrier((newer[1], second))
+            early, second = lax.optimization_barrier((early, second))
+            sent_q = jnp.where(places["before"], added(second, early[1]), second)
+            early, first, sent_q = lax.optimization_barrier((early, first, sent_q))
+            sent_p = jnp.where(places["before"], added(first, early[0]), first)
+            older, newer = newer, {1: send(sent_q, onward), 0: send(sent_p, onward)}
+            whole = jnp.stack([sent_p, sent_q])
+            if across:
+                direct = {0: send(first, across), 1: send(second, across)}
+        if slot < ticks - 1:
+            early = send(whole, [(0, sections - 2)])
     result = second
     return result.reshape(1, 2, planes, rows, width, chans)
 

time: 118 us -> 123 us (1.042)
  waiting for transfers between devices: 20.8 us -> 29.3 us
  starting transfers between devices: 67 us -> 62.5 us
    ppermute x15 -> x12, waiting for transfers between devices: 12.3 us -> 21.9 us  [send(): return lax.ppermute(block, 'section', pairs) if pairs else block]
    ppermute x15 -> x12, starting transfers between devices: 25.8 us -> 18 us  [send(): return lax.ppermute(block, 'section', pairs) if pairs else block]
    ppermute x20, starting transfers between devices: 41.2 us -> 44.4 us  [swap(): lax.ppermute(lax.dynamic_slice_in_dim(block, starts[turn], 1, axis=0), 'd...]
  transfers between devices with their start and end apart: 35 -> 32, of which waited for: 11 -> 14; matrix products, arithmetic and copies ran while one was open for 1% -> 2% of each run, Pallas kernels for 19% -> 20%
where the time goes in v10:
time: 123 us; the launch traced here: 122 us
  starting transfers between devices  62.5 us (51%)
  waiting for transfers between devices  29.3 us (24%)
  Pallas kernels  26.7 us (22%)
  other arithmetic  1.79 us (1%)
  local copies, waits for them, and re-layouts  1.27 us (1%)
    ppermute x20, starting transfers between devices, swap(): lax.ppermute(lax.dynamic_slice_in_dim(block, starts[turn], 1, axis=0), 'd...  44.4 us
    pallas_call x20, Pallas kernels, call(): pl.pallas_call(functools.partial(kernel, width), out_shape=[jax.ShapeDtyp...  26.7 us
    ppermute x12, waiting for transfers between devices, send(): return lax.ppermute(block, 'section', pairs) if pairs else block  21.9 us
    ppermute x12, starting transfers between devices, send(): return lax.ppermute(block, 'section', pairs) if pairs else block  18 us
    ppermute x20, waiting for transfers between devices, swap(): lax.ppermute(lax.dynamic_slice_in_dim(block, starts[turn], 1, axis=0), 'd...  7.41 us
  transfers between devices with their start and end apart: 32, of which 14 were waited for; matrix products, arithmetic and copies ran while one was open for 2% of the time, Pallas kernels for 20%

profile of v10, /device:TPU:13, one launch (start us, length us, event | category | flops | bytes accessed | tf_op | source)
XLA Modules:
  0.0 122.1 jit_solution(13263454214111337296)
XLA Ops:
  0.0 1.3 %collective-permute-start.2 = (bf16[2,4,128,256]{3,2,1,0:T(8,128)(2,1)}, bf16[2,4,128,256]{3,2,1,0:T(8,128)(2,1)S(1)}, u32[]{:S(2)}, u32[]{:S(2)}) collective-permute-start(bf16[2,4,128,256]{3,2,1,0:T(8,128)(2,1)} %bitcast.96), channel_id=1, source_target_pairs={{0,24},{8,16},{1,25},{9,17},{2,26},{10,18},{3,27},{11,19},{4,28},{... | collective-permute-start | bytes 1572872 | tf_op jit(solution)/shard_map/ppermute | solution.py:172
  3.1 3.1 %collective-permute-start.1 = (bf16[1,128,256]{2,1,0:T(8,128)(2,1)S(1)}, bf16[1,128,256]{2,1,0:T(8,128)(2,1)S(1)}, u32[]{:S(2)}, u32[]{:S(2)}) collective-permute-start(bf16[1,128,256]{2,1,0:T(8,128)(2,1)S(1)} %get-tuple-element.157), channel_id=1, source_target_pairs={{1,2},{2,1},{3,4},{4,3},{5,6},{6,5},{9,10},{10,9},{11,12},{12,11},... | collective-permute-start | bytes 196616 | tf_op jit(solution)/shard_map/ppermute | solution.py:137
  6.2 3.2 %shard_map.55 = (bf16[4,128,256]{2,1,0:T(8,128)(2,1)S(1)}, bf16[4,144,256]{2,1,0:T(8,128)(2,1)S(1)}, f32[2,128,256]{2,1,0:T(8,128)S(1)}, bf16[6912,256]{1,0:T(8,128)(2,1)S(1)}) custom-call(bf16[4,128,256]{2,1,0:T(8,128)(2,1)S(1)} %get-tuple-element.138.field.rest_0_, bf16[6912,256]{1,0:T(8,128)(2,1)} %bitcast.84), custom_call_target="tpu_custom_call" | custom-call | flops 1 | bytes 1 | tf_op jit(solution)/shard_map/pallas_call | solution.py:99
  9.5 1.2 shard_map.56.field
  10.8 3.6 %collective-permute-start.6 = (bf16[1,128,256]{2,1,0:T(8,128)(2,1)S(1)}, bf16[1,128,256]{2,1,0:T(8,128)(2,1)S(1)}, u32[]{:S(2)}, u32[]{:S(2)}) collective-permute-start(bf16[1,128,256]{2,1,0:T(8,128)(2,1)S(1)} %get-tuple-element.153), channel_id=1, source_target_pairs={{1,2},{2,1},{3,4},{4,3},{5,6},{6,5},{9,10},{10,9},{11,12},{12,11},... | collective-permute-start | bytes 196616 | tf_op jit(solution)/shard_map/ppermute | solution.py:137
  14.4 1.4 %collective-permute-done.2 = bf16[2,4,128,256]{3,2,1,0:T(8,128)(2,1)S(1)} collective-permute-done((bf16[2,4,128,256]{3,2,1,0:T(8,128)(2,1)}, bf16[2,4,128,256]{3,2,1,0:T(8,128)(2,1)S(1)}, u32[]{:S(2)}, u32[]{:S(2)}) %collective-permute-start.2) | collective-permute-done | bytes 524320 | tf_op jit(solution)/shard_map/ppermute | solution.py:172
  16.1 1.6 %collective-permute-start.3 = (bf16[1,128,256]{2,1,0:T(8,128)(2,1)S(1)}, bf16[1,128,256]{2,1,0:T(8,128)(2,1)S(1)}, u32[]{:S(2)}, u32[]{:S(2)}) collective-permute-start(bf16[1,128,256]{2,1,0:T(8,128)(2,1)S(1)} %get-tuple-element.156), channel_id=1, source_target_pairs={{0,1},{1,0},{2,3},{3,2},{4,5},{5,4},{6,7},{7,6},{8,9},{9,8},{10,11... | collective-permute-start | bytes 196616 | tf_op jit(solution)/shard_map/ppermute | solution.py:137
  17.7 3.1 %collective-permute-start.4 = (bf16[1,128,256]{2,1,0:T(8,128)(2,1)S(1)}, bf16[1,128,256]{2,1,0:T(8,128)(2,1)S(1)}, u32[]{:S(2)}, u32[]{:S(2)}) collective-permute-start(bf16[1,128,256]{2,1,0:T(8,128)(2,1)S(1)} %get-tuple-element.155), channel_id=1, source_target_pairs={{1,2},{2,1},{3,4},{4,3},{5,6},{6,5},{9,10},{10,9},{11,12},{12,11},... | collective-permute-start | bytes 196616 | tf_op jit(solution)/shard_map/ppermute | solution.py:137
  20.8 1.2 shard_map.57
  22.0 1.2 shard_map.58
  23.3 1.3 %collective-permute-start.7 = (bf16[2,4,128,256]{3,2,1,0:T(8,128)(2,1)S(1)}, bf16[2,4,128,256]{3,2,1,0:T(8,128)(2,1)S(1)}, u32[]{:S(2)}, u32[]{:S(2)}) collective-permute-start(bf16[2,4,128,256]{3,2,1,0:T(8,128)(2,1)S(1)} %pad_maximum_fusion), channel_id=1, source_target_pairs={{0,16},{1,17},{2,18},{3,19},{4,20},{5,21},{6,22},{7,23}} | collective-permute-start | bytes 1572872 | tf_op jit(solution)/shard_map/ppermute | solution.py:172
  25.3 1.2 shard_map.59
  26.5 1.2 shard_map.60.field
  27.8 3.6 %collective-permute-start.10 = (bf16[1,128,256]{2,1,0:T(8,128)(2,1)S(1)}, bf16[1,128,256]{2,1,0:T(8,128)(2,1)S(1)}, u32[]{:S(2)}, u32[]{:S(2)}) collective-permute-start(bf16[1,128,256]{2,1,0:T(8,128)(2,1)S(1)} %get-tuple-element.151), channel_id=1, source_target_pairs={{1,2},{2,1},{3,4},{4,3},{5,6},{6,5},{9,10},{10,9},{11,12},{12,11},... | collective-permute-start | bytes 196616 | tf_op jit(solution)/shard_map/ppermute | solution.py:137
  32.1 1.2 shard_map.61
  33.7 1.2 shard_map.62
  34.9 3.8 %collective-permute-done.7 = bf16[2,4,128,256]{3,2,1,0:T(8,128)(2,1)S(1)} collective-permute-done((bf16[2,4,128,256]{3,2,1,0:T(8,128)(2,1)S(1)}, bf16[2,4,128,256]{3,2,1,0:T(8,128)(2,1)S(1)}, u32[]{:S(2)}, u32[]{:S(2)}) %collective-permute-start.7) | collective-permute-done | bytes 524320 | tf_op jit(solution)/shard_map/ppermute | solution.py:172
  38.8 1.9 %collective-permute-start.14 = (bf16[4,128,256]{2,1,0:T(8,128)(2,1)S(1)}, bf16[4,128,256]{2,1,0:T(8,128)(2,1)S(1)}, u32[]{:S(2)}, u32[]{:S(2)}) collective-permute-start(bf16[4,128,256]{2,1,0:T(8,128)(2,1)S(1)} %fusion.16), channel_id=1, source_target_pairs={{0,8},{8,16},{16,24},{1,9},{9,17},{17,25},{2,10},{10,18},{18,26},{... | collective-permute-start | bytes 786440 | tf_op jit(solution)/shard_map/ppermute | solution.py:172
  40.8 1.9 %collective-permute-start.13 = (bf16[4,128,256]{2,1,0:T(8,128)(2,1)S(1)}, bf16[4,128,256]{2,1,0:T(8,128)(2,1)S(1)}, u32[]{:S(2)}, u32[]{:S(2)}) collective-permute-start(bf16[4,128,256]{2,1,0:T(8,128)(2,1)S(1)} %fusion.17), channel_id=1, source_target_pairs={{0,8},{8,16},{16,24},{1,9},{9,17},{17,25},{2,10},{10,18},{18,26},{... | collective-permute-start | bytes 786440 | tf_op jit(solution)/shard_map/ppermute | solution.py:172
  42.8 1.3 %collective-permute-start.11 = (bf16[2,4,128,256]{3,2,1,0:T(8,128)(2,1)S(1)}, bf16[2,4,128,256]{3,2,1,0:T(8,128)(2,1)S(1)}, u32[]{:S(2)}, u32[]{:S(2)}) collective-permute-start(bf16[2,4,128,256]{3,2,1,0:T(8,128)(2,1)S(1)} %pad_maximum_fusion.1), channel_id=1, source_target_pairs={{0,16},{1,17},{2,18},{3,19},{4,20},{5,21},{6,22},{7,23}} | collective-permute-start | bytes 1572872 | tf_op jit(solution)/shard_map/ppermute | solution.py:172
  44.1 4.5 %collective-permute-done.14 = bf16[4,128,256]{2,1,0:T(8,128)(2,1)S(1)} collective-permute-done((bf16[4,128,256]{2,1,0:T(8,128)(2,1)S(1)}, bf16[4,128,256]{2,1,0:T(8,128)(2,1)S(1)}, u32[]{:S(2)}, u32[]{:S(2)}) %collective-permute-start.14) | collective-permute-done | bytes 262176 | tf_op jit(solution)/shard_map/ppermute | solution.py:172
  48.8 3.1 %collective-permute-start.15 = (bf16[1,128,256]{2,1,0:T(8,128)(2,1)S(1)}, bf16[1,128,256]{2,1,0:T(8,128)(2,1)S(1)}, u32[]{:S(2)}, u32[]{:S(2)}) collective-permute-start(bf16[1,128,256]{2,1,0:T(8,128)(2,1)S(1)} %get-tuple-element.150), channel_id=1, source_target_pairs={{0,1},{1,0},{2,3},{3,2},{4,5},{5,4},{6,7},{7,6},{8,9},{9,8},{10,11... | collective-permute-start | bytes 196616 | tf_op jit(solution)/shard_map/ppermute | solution.py:137
  52.0 3.3 %collective-permute-start.16 = (bf16[1,128,256]{2,1,0:T(8,128)(2,1)S(1)}, bf16[1,128,256]{2,1,0:T(8,128)(2,1)S(1)}, u32[]{:S(2)}, u32[]{:S(2)}) collective-permute-start(bf16[1,128,256]{2,1,0:T(8,128)(2,1)S(1)} %get-tuple-element.149), channel_id=1, source_target_pairs={{1,2},{2,1},{3,4},{4,3},{5,6},{6,5},{9,10},{10,9},{11,12},{12,11},... | collective-permute-start | bytes 196616 | tf_op jit(solution)/shard_map/ppermute | solution.py:137
  55.2 1.2 shard_map.63
  56.5 1.4 %collective-permute-done.16.far = bf16[1,128,256]{2,1,0:T(8,128)(2,1)S(1)} collective-permute-done((bf16[1,128,256]{2,1,0:T(8,128)(2,1)S(1)}, bf16[1,128,256]{2,1,0:T(8,128)(2,1)S(1)}, u32[]{:S(2)}, u32[]{:S(2)}) %collective-permute-start.16) | collective-permute-done | bytes 65568 | tf_op jit(solution)/shard_map/ppermute | solution.py:137
  59.3 3.6 %collective-permute-start.18 = (bf16[1,128,256]{2,1,0:T(8,128)(2,1)S(1)}, bf16[1,128,256]{2,1,0:T(8,128)(2,1)S(1)}, u32[]{:S(2)}, u32[]{:S(2)}) collective-permute-start(bf16[1,128,256]{2,1,0:T(8,128)(2,1)S(1)} %get-tuple-element.147), channel_id=1, source_target_pairs={{1,2},{2,1},{3,4},{4,3},{5,6},{6,5},{9,10},{10,9},{11,12},{12,11},... | collective-permute-start | bytes 196616 | tf_op jit(solution)/shard_map/ppermute | solution.py:137
  62.9 1.2 shard_map.65
  65.2 1.2 shard_map.66
  66.8 1.9 %collective-permute-start.21 = (bf16[4,128,256]{2,1,0:T(8,128)(2,1)S(1)}, bf16[4,128,256]{2,1,0:T(8,128)(2,1)S(1)}, u32[]{:S(2)}, u32[]{:S(2)}) collective-permute-start(bf16[4,128,256]{2,1,0:T(8,128)(2,1)S(1)} %fusion.18), channel_id=1, source_target_pairs={{0,8},{8,16},{16,24},{1,9},{9,17},{17,25},{2,10},{10,18},{18,26},{... | collective-permute-start | bytes 786440 | tf_op jit(solution)/shard_map/ppermute | solution.py:172
  68.8 1.9 %collective-permute-start.19 = (bf16[4,128,256]{2,1,0:T(8,128)(2,1)S(1)}, bf16[4,128,256]{2,1,0:T(8,128)(2,1)S(1)}, u32[]{:S(2)}, u32[]{:S(2)}) collective-permute-start(bf16[4,128,256]{2,1,0:T(8,128)(2,1)S(1)} %fusion.19), channel_id=1, source_target_pairs={{0,8},{8,16},{16,24},{1,9},{9,17},{17,25},{2,10},{10,18},{18,26},{... | collective-permute-start | bytes 786440 | tf_op jit(solution)/shard_map/ppermute | solution.py:172
  70.8 1.3 %collective-permute-start.20 = (bf16[2,4,128,256]{3,2,1,0:T(8,128)(2,1)S(1)}, bf16[2,4,128,256]{3,2,1,0:T(8,128)(2,1)S(1)}, u32[]{:S(2)}, u32[]{:S(2)}) collective-permute-start(bf16[2,4,128,256]{3,2,1,0:T(8,128)(2,1)S(1)} %pad_maximum_fusion.2), channel_id=1, source_target_pairs={{0,16},{1,17},{2,18},{3,19},{4,20},{5,21},{6,22},{7,23}} | collective-permute-start | bytes 1572872 | tf_op jit(solution)/shard_map/ppermute | solution.py:172
  72.1 4.9 %collective-permute-done.21 = bf16[4,128,256]{2,1,0:T(8,128)(2,1)S(1)} collective-permute-done((bf16[4,128,256]{2,1,0:T(8,128)(2,1)S(1)}, bf16[4,128,256]{2,1,0:T(8,128)(2,1)S(1)}, u32[]{:S(2)}, u32[]{:S(2)}) %collective-permute-start.21) | collective-permute-done | bytes 262176 | tf_op jit(solution)/shard_map/ppermute | solution.py:172
  77.1 2.4 %collective-permute-start.22 = (bf16[1,128,256]{2,1,0:T(8,128)(2,1)S(1)}, bf16[1,128,256]{2,1,0:T(8,128)(2,1)S(1)}, u32[]{:S(2)}, u32[]{:S(2)}) collective-permute-start(bf16[1,128,256]{2,1,0:T(8,128)(2,1)S(1)} %get-tuple-element.146), channel_id=1, source_target_pairs={{0,1},{1,0},{2,3},{3,2},{4,5},{5,4},{6,7},{7,6},{8,9},{9,8},{10,11... | collective-permute-start | bytes 196616 | tf_op jit(solution)/shard_map/ppermute | solution.py:137
  79.6 3.1 %collective-permute-start.23 = (bf16[1,128,256]{2,1,0:T(8,128)(2,1)S(1)}, bf16[1,128,256]{2,1,0:T(8,128)(2,1)S(1)}, u32[]{:S(2)}, u32[]{:S(2)}) collective-permute-start(bf16[1,128,256]{2,1,0:T(8,128)(2,1)S(1)} %get-tuple-element.145), channel_id=1, source_target_pairs={{1,2},{2,1},{3,4},{4,3},{5,6},{6,5},{9,10},{10,9},{11,12},{12,11},... | collective-permute-start | bytes 196616 | tf_op jit(solution)/shard_map/ppermute | solution.py:137
  82.7 1.2 shard_map.67
  83.9 1.5 %collective-permute-done.23.far = bf16[1,128,256]{2,1,0:T(8,128)(2,1)S(1)} collective-permute-done((bf16[1,128,256]{2,1,0:T(8,128)(2,1)S(1)}, bf16[1,128,256]{2,1,0:T(8,128)(2,1)S(1)}, u32[]{:S(2)}, u32[]{:S(2)}) %collective-permute-start.23) | collective-permute-done | bytes 65568 | tf_op jit(solution)/shard_map/ppermute | solution.py:137
  86.9 3.6 %collective-permute-start.25 = (bf16[1,128,256]{2,1,0:T(8,128)(2,1)S(1)}, bf16[1,128,256]{2,1,0:T(8,128)(2,1)S(1)}, u32[]{:S(2)}, u32[]{:S(2)}) collective-permute-start(bf16[1,128,256]{2,1,0:T(8,128)(2,1)S(1)} %get-tuple-element.143), channel_id=1, source_target_pairs={{1,2},{2,1},{3,4},{4,3},{5,6},{6,5},{9,10},{10,9},{11,12},{12,11},... | collective-permute-start | bytes 196616 | tf_op jit(solution)/shard_map/ppermute | solution.py:137
  90.5 1.2 shard_map.69
  92.8 1.2 shard_map.70
  94.7 1.9 %collective-permute-start.27 = (bf16[4,128,256]{2,1,0:T(8,128)(2,1)S(1)}, bf16[4,128,256]{2,1,0:T(8,128)(2,1)S(1)}, u32[]{:S(2)}, u32[]{:S(2)}) collective-permute-start(bf16[4,128,256]{2,1,0:T(8,128)(2,1)S(1)} %fusion.20), channel_id=1, source_target_pairs={{8,16},{16,24},{9,17},{17,25},{10,18},{18,26},{11,19},{19,27},{12,... | collective-permute-start | bytes 786440 | tf_op jit(solution)/shard_map/ppermute | solution.py:172
  96.8 1.9 %collective-permute-start.26 = (bf16[4,128,256]{2,1,0:T(8,128)(2,1)S(1)}, bf16[4,128,256]{2,1,0:T(8,128)(2,1)S(1)}, u32[]{:S(2)}, u32[]{:S(2)}) collective-permute-start(bf16[4,128,256]{2,1,0:T(8,128)(2,1)S(1)} %fusion.21), channel_id=1, source_target_pairs={{8,16},{16,24},{9,17},{17,25},{10,18},{18,26},{11,19},{19,27},{12,... | collective-permute-start | bytes 786440 | tf_op jit(solution)/shard_map/ppermute | solution.py:172
  98.7 6.2 %collective-permute-done.27 = bf16[4,128,256]{2,1,0:T(8,128)(2,1)S(1)} collective-permute-done((bf16[4,128,256]{2,1,0:T(8,128)(2,1)S(1)}, bf16[4,128,256]{2,1,0:T(8,128)(2,1)S(1)}, u32[]{:S(2)}, u32[]{:S(2)}) %collective-permute-start.27) | collective-permute-done | bytes 262176 | tf_op jit(solution)/shard_map/ppermute | solution.py:172
  105.1 2.3 %collective-permute-start.28 = (bf16[1,128,256]{2,1,0:T(8,128)(2,1)S(1)}, bf16[1,128,256]{2,1,0:T(8,128)(2,1)S(1)}, u32[]{:S(2)}, u32[]{:S(2)}) collective-permute-start(bf16[1,128,256]{2,1,0:T(8,128)(2,1)S(1)} %get-tuple-element.142), channel_id=1, source_target_pairs={{0,1},{1,0},{2,3},{3,2},{4,5},{5,4},{6,7},{7,6},{8,9},{9,8},{10,11... | collective-permute-start | bytes 196616 | tf_op jit(solution)/shard_map/ppermute | solution.py:137
  107.4 3.3 %collective-permute-start.29 = (bf16[1,128,256]{2,1,0:T(8,128)(2,1)S(1)}, bf16[1,128,256]{2,1,0:T(8,128)(2,1)S(1)}, u32[]{:S(2)}, u32[]{:S(2)}) collective-permute-start(bf16[1,128,256]{2,1,0:T(8,128)(2,1)S(1)} %get-tuple-element.141), channel_id=1, source_target_pairs={{1,2},{2,1},{3,4},{4,3},{5,6},{6,5},{9,10},{10,9},{11,12},{12,11},... | collective-permute-start | bytes 196616 | tf_op jit(solution)/shard_map/ppermute | solution.py:137
  110.8 1.2 shard_map.71
  114.5 3.6 %collective-permute-start.31 = (bf16[1,128,256]{2,1,0:T(8,128)(2,1)S(1)}, bf16[1,128,256]{2,1,0:T(8,128)(2,1)S(1)}, u32[]{:S(2)}, u32[]{:S(2)}) collective-permute-start(bf16[1,128,256]{2,1,0:T(8,128)(2,1)S(1)} %get-tuple-element.139), channel_id=1, source_target_pairs={{1,2},{2,1},{3,4},{4,3},{5,6},{6,5},{9,10},{10,9},{11,12},{12,11},... | collective-permute-start | bytes 196616 | tf_op jit(solution)/shard_map/ppermute | solution.py:137
  118.0 1.2 shard_map.73
  120.1 2.0 %shard_map.74 = bf16[2,4,128,256]{3,2,1,0:T(8,128)(2,1)} custom-call(s32[1]{0:T(128)} %bitcast.flags, bf16[1,128,256]{2,1,0:T(8,128)(2,1)S(1)} %collective-permute-done.30.near, bf16[1,128,256]{2,1,0:T(8,128)(2,1)S(1)} %collective-permute-done.31.far, bf16[4,128,256]{2,1,0:T(8,128)(2,1)S(1)} %get-tuple-element.132.even, ...), custom_call_target="tpu_custom_call" | custom-call | flops 1 | bytes 1 | tf_op jit(solution)/shard_map/pallas_call | solution.py:99
  (69 shorter events, 14.6 us)
Async XLA Ops:
  0.0 15.8 %collective-permute-start.2 = (bf16[2,4,128,256]{3,2,1,0:T(8,128)(2,1)}, bf16[2,4,128,256]{3,2,1,0:T(8,128)(2,1)S(1)}, u32[]{:S(2)}, u32[]{:S(2)}) collective-permute-start(bf16[2,4,128,256]{3,2,1,0:T(8,128)(2,1)} %bitcast.96), channel_id=1, source_target_pairs={{0,24},{8,16},{1,25},{9,17},{2,26},{10,18},{3,27},{11,19},{4,28},{... | collective-permute-start | bytes 1572872 | tf_op jit(solution)/shard_map/ppermute | solution.py:172
  2.4 7.0 %collective-permute-start = (bf16[1,128,256]{2,1,0:T(8,128)(2,1)S(1)}, bf16[1,128,256]{2,1,0:T(8,128)(2,1)S(1)}, u32[]{:S(2)}, u32[]{:S(2)}) collective-permute-start(bf16[1,128,256]{2,1,0:T(8,128)(2,1)S(1)} %get-tuple-element.158), channel_id=1, source_target_pairs={{0,1},{1,0},{2,3},{3,2},{4,5},{5,4},{6,7},{7,6},{8,9},{9,8},{10,11... | collective-permute-start | bytes 196616 | tf_op jit(solution)/shard_map/ppermute | solution.py:137
  3.1 6.3 %collective-permute-start.1 = (bf16[1,128,256]{2,1,0:T(8,128)(2,1)S(1)}, bf16[1,128,256]{2,1,0:T(8,128)(2,1)S(1)}, u32[]{:S(2)}, u32[]{:S(2)}) collective-permute-start(bf16[1,128,256]{2,1,0:T(8,128)(2,1)S(1)} %get-tuple-element.157), channel_id=1, source_target_pairs={{1,2},{2,1},{3,4},{4,3},{5,6},{6,5},{9,10},{10,9},{11,12},{12,11},... | collective-permute-start | bytes 196616 | tf_op jit(solution)/shard_map/ppermute | solution.py:137
  6.2 9.5 %copy-start.2 = (bf16[1,2,4,16,8,256]{5,4,3,2,1,0:T(8,128)(2,1)S(1)}, bf16[1,2,4,16,8,256]{5,4,3,2,1,0:T(8,128)(2,1)}, u32[]{:S(2)}) copy-start(bf16[1,2,4,16,8,256]{5,4,3,2,1,0:T(8,128)(2,1)} %param.5) | copy-start | bytes 1572868
  9.5 6.3 %copy-start.1 = (bf16[3,2,4,16,8,256]{5,4,3,2,1,0:T(8,128)(2,1)S(1)}, bf16[3,2,4,16,8,256]{5,4,3,2,1,0:T(8,128)(2,1)}, u32[]{:S(2)}) copy-start(bf16[3,2,4,16,8,256]{5,4,3,2,1,0:T(8,128)(2,1)} %param.7) | copy-start | bytes 4718596
  9.5 11.3 %copy-start = (bf16[1,3,3,3,256,256]{5,4,3,2,1,0:T(8,128)(2,1)S(1)}, bf16[1,3,3,3,256,256]{5,4,3,2,1,0:T(8,128)(2,1)}, u32[]{:S(2)}) copy-start(bf16[1,3,3,3,256,256]{5,4,3,2,1,0:T(8,128)(2,1)} %param.9) | copy-start | bytes 10616836
  10.7 11.3 %collective-permute-start.5 = (bf16[1,128,256]{2,1,0:T(8,128)(2,1)S(1)}, bf16[1,128,256]{2,1,0:T(8,128)(2,1)S(1)}, u32[]{:S(2)}, u32[]{:S(2)}) collective-permute-start(bf16[1,128,256]{2,1,0:T(8,128)(2,1)S(1)} %get-tuple-element.154), channel_id=1, source_target_pairs={{0,1},{1,0},{2,3},{3,2},{4,5},{5,4},{6,7},{7,6},{8,9},{9,8},{10,11... | collective-permute-start | bytes 196616 | tf_op jit(solution)/shard_map/ppermute | solution.py:137
  10.8 11.2 %collective-permute-start.6 = (bf16[1,128,256]{2,1,0:T(8,128)(2,1)S(1)}, bf16[1,128,256]{2,1,0:T(8,128)(2,1)S(1)}, u32[]{:S(2)}, u32[]{:S(2)}) collective-permute-start(bf16[1,128,256]{2,1,0:T(8,128)(2,1)S(1)} %get-tuple-element.153), channel_id=1, source_target_pairs={{1,2},{2,1},{3,4},{4,3},{5,6},{6,5},{9,10},{10,9},{11,12},{12,11},... | collective-permute-start | bytes 196616 | tf_op jit(solution)/shard_map/ppermute | solution.py:137
  16.1 7.2 %collective-permute-start.3 = (bf16[1,128,256]{2,1,0:T(8,128)(2,1)S(1)}, bf16[1,128,256]{2,1,0:T(8,128)(2,1)S(1)}, u32[]{:S(2)}, u32[]{:S(2)}) collective-permute-start(bf16[1,128,256]{2,1,0:T(8,128)(2,1)S(1)} %get-tuple-element.156), channel_id=1, source_target_pairs={{0,1},{1,0},{2,3},{3,2},{4,5},{5,4},{6,7},{7,6},{8,9},{9,8},{10,11... | collective-permute-start | bytes 196616 | tf_op jit(solution)/shard_map/ppermute | solution.py:137
  17.7 5.6 %collective-permute-start.4 = (bf16[1,128,256]{2,1,0:T(8,128)(2,1)S(1)}, bf16[1,128,256]{2,1,0:T(8,128)(2,1)S(1)}, u32[]{:S(2)}, u32[]{:S(2)}) collective-permute-start(bf16[1,128,256]{2,1,0:T(8,128)(2,1)S(1)} %get-tuple-element.155), channel_id=1, source_target_pairs={{1,2},{2,1},{3,4},{4,3},{5,6},{6,5},{9,10},{10,9},{11,12},{12,11},... | collective-permute-start | bytes 196616 | tf_op jit(solution)/shard_map/ppermute | solution.py:137
  23.3 15.4 %collective-permute-start.7 = (bf16[2,4,128,256]{3,2,1,0:T(8,128)(2,1)S(1)}, bf16[2,4,128,256]{3,2,1,0:T(8,128)(2,1)S(1)}, u32[]{:S(2)}, u32[]{:S(2)}) collective-permute-start(bf16[2,4,128,256]{3,2,1,0:T(8,128)(2,1)S(1)} %pad_maximum_fusion), channel_id=1, source_target_pairs={{0,16},{1,17},{2,18},{3,19},{4,20},{5,21},{6,22},{7,23}} | collective-permute-start | bytes 1572872 | tf_op jit(solution)/shard_map/ppermute | solution.py:172
  24.6 10.3 %collective-permute-start.8 = (bf16[4,128,256]{2,1,0:T(8,128)(2,1)S(1)}, bf16[4,128,256]{2,1,0:T(8,128)(2,1)S(1)}, u32[]{:S(2)}, u32[]{:S(2)}) collective-permute-start(bf16[4,128,256]{2,1,0:T(8,128)(2,1)S(1)} %shard_map.58), channel_id=1, source_target_pairs={{0,8},{1,9},{2,10},{3,11},{4,12},{5,13},{6,14},{7,15}} | collective-permute-start | bytes 786440 | tf_op jit(solution)/shard_map/ppermute | solution.py:172
  27.7 5.6 %collective-permute-start.9 = (bf16[1,128,256]{2,1,0:T(8,128)(2,1)S(1)}, bf16[1,128,256]{2,1,0:T(8,128)(2,1)S(1)}, u32[]{:S(2)}, u32[]{:S(2)}) collective-permute-start(bf16[1,128,256]{2,1,0:T(8,128)(2,1)S(1)} %get-tuple-element.152), channel_id=1, source_target_pairs={{0,1},{1,0},{2,3},{3,2},{4,5},{5,4},{6,7},{7,6},{8,9},{9,8},{10,11... | collective-permute-start | bytes 196616 | tf_op jit(solution)/shard_map/ppermute | solution.py:137
  27.8 5.9 %collective-permute-start.10 = (bf16[1,128,256]{2,1,0:T(8,128)(2,1)S(1)}, bf16[1,128,256]{2,1,0:T(8,128)(2,1)S(1)}, u32[]{:S(2)}, u32[]{:S(2)}) collective-permute-start(bf16[1,128,256]{2,1,0:T(8,128)(2,1)S(1)} %get-tuple-element.151), channel_id=1, source_target_pairs={{1,2},{2,1},{3,4},{4,3},{5,6},{6,5},{9,10},{10,9},{11,12},{12,11},... | collective-permute-start | bytes 196616 | tf_op jit(solution)/shard_map/ppermute | solution.py:137
  31.4 27.6 %collective-permute-start.12 = (bf16[4,128,256]{2,1,0:T(8,128)(2,1)S(1)}, bf16[4,128,256]{2,1,0:T(8,128)(2,1)S(1)}, u32[]{:S(2)}, u32[]{:S(2)}) collective-permute-start(bf16[4,128,256]{2,1,0:T(8,128)(2,1)S(1)} %shard_map.56.field), channel_id=1, source_target_pairs={{0,8},{1,9},{2,10},{3,11},{4,12},{5,13},{6,14},{7,15}} | collective-permute-start | bytes 786440 | tf_op jit(solution)/shard_map/ppermute | solution.py:172
  38.8 9.8 %collective-permute-start.14 = (bf16[4,128,256]{2,1,0:T(8,128)(2,1)S(1)}, bf16[4,128,256]{2,1,0:T(8,128)(2,1)S(1)}, u32[]{:S(2)}, u32[]{:S(2)}) collective-permute-start(bf16[4,128,256]{2,1,0:T(8,128)(2,1)S(1)} %fusion.16), channel_id=1, source_target_pairs={{0,8},{8,16},{16,24},{1,9},{9,17},{17,25},{2,10},{10,18},{18,26},{... | collective-permute-start | bytes 786440 | tf_op jit(solution)/shard_map/ppermute | solution.py:172
  40.8 18.2 %collective-permute-start.13 = (bf16[4,128,256]{2,1,0:T(8,128)(2,1)S(1)}, bf16[4,128,256]{2,1,0:T(8,128)(2,1)S(1)}, u32[]{:S(2)}, u32[]{:S(2)}) collective-permute-start(bf16[4,128,256]{2,1,0:T(8,128)(2,1)S(1)} %fusion.17), channel_id=1, source_target_pairs={{0,8},{8,16},{16,24},{1,9},{9,17},{17,25},{2,10},{10,18},{18,26},{... | collective-permute-start | bytes 786440 | tf_op jit(solution)/shard_map/ppermute | solution.py:172
  42.8 23.9 %collective-permute-start.11 = (bf16[2,4,128,256]{3,2,1,0:T(8,128)(2,1)S(1)}, bf16[2,4,128,256]{3,2,1,0:T(8,128)(2,1)S(1)}, u32[]{:S(2)}, u32[]{:S(2)}) collective-permute-start(bf16[2,4,128,256]{3,2,1,0:T(8,128)(2,1)S(1)} %pad_maximum_fusion.1), channel_id=1, source_target_pairs={{0,16},{1,17},{2,18},{3,19},{4,20},{5,21},{6,22},{7,23}} | collective-permute-start | bytes 1572872 | tf_op jit(solution)/shard_map/ppermute | solution.py:172
  48.8 7.6 %collective-permute-start.15 = (bf16[1,128,256]{2,1,0:T(8,128)(2,1)S(1)}, bf16[1,128,256]{2,1,0:T(8,128)(2,1)S(1)}, u32[]{:S(2)}, u32[]{:S(2)}) collective-permute-start(bf16[1,128,256]{2,1,0:T(8,128)(2,1)S(1)} %get-tuple-element.150), channel_id=1, source_target_pairs={{0,1},{1,0},{2,3},{3,2},{4,5},{5,4},{6,7},{7,6},{8,9},{9,8},{10,11... | collective-permute-start | bytes 196616 | tf_op jit(solution)/shard_map/ppermute | solution.py:137
  52.0 5.9 %collective-permute-start.16 = (bf16[1,128,256]{2,1,0:T(8,128)(2,1)S(1)}, bf16[1,128,256]{2,1,0:T(8,128)(2,1)S(1)}, u32[]{:S(2)}, u32[]{:S(2)}) collective-permute-start(bf16[1,128,256]{2,1,0:T(8,128)(2,1)S(1)} %get-tuple-element.149), channel_id=1, source_target_pairs={{1,2},{2,1},{3,4},{4,3},{5,6},{6,5},{9,10},{10,9},{11,12},{12,11},... | collective-permute-start | bytes 196616 | tf_op jit(solution)/shard_map/ppermute | solution.py:137
  59.2 4.9 %collective-permute-start.17 = (bf16[1,128,256]{2,1,0:T(8,128)(2,1)S(1)}, bf16[1,128,256]{2,1,0:T(8,128)(2,1)S(1)}, u32[]{:S(2)}, u32[]{:S(2)}) collective-permute-start(bf16[1,128,256]{2,1,0:T(8,128)(2,1)S(1)} %get-tuple-element.148), channel_id=1, source_target_pairs={{0,1},{1,0},{2,3},{3,2},{4,5},{5,4},{6,7},{7,6},{8,9},{9,8},{10,11... | collective-permute-start | bytes 196616 | tf_op jit(solution)/shard_map/ppermute | solution.py:137
  59.3 5.9 %collective-permute-start.18 = (bf16[1,128,256]{2,1,0:T(8,128)(2,1)S(1)}, bf16[1,128,256]{2,1,0:T(8,128)(2,1)S(1)}, u32[]{:S(2)}, u32[]{:S(2)}) collective-permute-start(bf16[1,128,256]{2,1,0:T(8,128)(2,1)S(1)} %get-tuple-element.147), channel_id=1, source_target_pairs={{1,2},{2,1},{3,4},{4,3},{5,6},{6,5},{9,10},{10,9},{11,12},{12,11},... | collective-permute-start | bytes 196616 | tf_op jit(solution)/shard_map/ppermute | solution.py:137
  66.8 10.2 %collective-permute-start.21 = (bf16[4,128,256]{2,1,0:T(8,128)(2,1)S(1)}, bf16[4,128,256]{2,1,0:T(8,128)(2,1)S(1)}, u32[]{:S(2)}, u32[]{:S(2)}) collective-permute-start(bf16[4,128,256]{2,1,0:T(8,128)(2,1)S(1)} %fusion.18), channel_id=1, source_target_pairs={{0,8},{8,16},{16,24},{1,9},{9,17},{17,25},{2,10},{10,18},{18,26},{... | collective-permute-start | bytes 786440 | tf_op jit(solution)/shard_map/ppermute | solution.py:172
  68.8 17.8 %collective-permute-start.19 = (bf16[4,128,256]{2,1,0:T(8,128)(2,1)S(1)}, bf16[4,128,256]{2,1,0:T(8,128)(2,1)S(1)}, u32[]{:S(2)}, u32[]{:S(2)}) collective-permute-start(bf16[4,128,256]{2,1,0:T(8,128)(2,1)S(1)} %fusion.19), channel_id=1, source_target_pairs={{0,8},{8,16},{16,24},{1,9},{9,17},{17,25},{2,10},{10,18},{18,26},{... | collective-permute-start | bytes 786440 | tf_op jit(solution)/shard_map/ppermute | solution.py:172
  70.8 23.9 %collective-permute-start.20 = (bf16[2,4,128,256]{3,2,1,0:T(8,128)(2,1)S(1)}, bf16[2,4,128,256]{3,2,1,0:T(8,128)(2,1)S(1)}, u32[]{:S(2)}, u32[]{:S(2)}) collective-permute-start(bf16[2,4,128,256]{3,2,1,0:T(8,128)(2,1)S(1)} %pad_maximum_fusion.2), channel_id=1, source_target_pairs={{0,16},{1,17},{2,18},{3,19},{4,20},{5,21},{6,22},{7,23}} | collective-permute-start | bytes 1572872 | tf_op jit(solution)/shard_map/ppermute | solution.py:172
  77.1 6.8 %collective-permute-start.22 = (bf16[1,128,256]{2,1,0:T(8,128)(2,1)S(1)}, bf16[1,128,256]{2,1,0:T(8,128)(2,1)S(1)}, u32[]{:S(2)}, u32[]{:S(2)}) collective-permute-start(bf16[1,128,256]{2,1,0:T(8,128)(2,1)S(1)} %get-tuple-element.146), channel_id=1, source_target_pairs={{0,1},{1,0},{2,3},{3,2},{4,5},{5,4},{6,7},{7,6},{8,9},{9,8},{10,11... | collective-permute-start | bytes 196616 | tf_op jit(solution)/shard_map/ppermute | solution.py:137
  79.6 5.9 %collective-permute-start.23 = (bf16[1,128,256]{2,1,0:T(8,128)(2,1)S(1)}, bf16[1,128,256]{2,1,0:T(8,128)(2,1)S(1)}, u32[]{:S(2)}, u32[]{:S(2)}) collective-permute-start(bf16[1,128,256]{2,1,0:T(8,128)(2,1)S(1)} %get-tuple-element.145), channel_id=1, source_target_pairs={{1,2},{2,1},{3,4},{4,3},{5,6},{6,5},{9,10},{10,9},{11,12},{12,11},... | collective-permute-start | bytes 196616 | tf_op jit(solution)/shard_map/ppermute | solution.py:137
  86.8 4.9 %collective-permute-start.24 = (bf16[1,128,256]{2,1,0:T(8,128)(2,1)S(1)}, bf16[1,128,256]{2,1,0:T(8,128)(2,1)S(1)}, u32[]{:S(2)}, u32[]{:S(2)}) collective-permute-start(bf16[1,128,256]{2,1,0:T(8,128)(2,1)S(1)} %get-tuple-element.144), channel_id=1, source_target_pairs={{0,1},{1,0},{2,3},{3,2},{4,5},{5,4},{6,7},{7,6},{8,9},{9,8},{10,11... | collective-permute-start | bytes 196616 | tf_op jit(solution)/shard_map/ppermute | solution.py:137
  86.9 5.9 %collective-permute-start.25 = (bf16[1,128,256]{2,1,0:T(8,128)(2,1)S(1)}, bf16[1,128,256]{2,1,0:T(8,128)(2,1)S(1)}, u32[]{:S(2)}, u32[]{:S(2)}) collective-permute-start(bf16[1,128,256]{2,1,0:T(8,128)(2,1)S(1)} %get-tuple-element.143), channel_id=1, source_target_pairs={{1,2},{2,1},{3,4},{4,3},{5,6},{6,5},{9,10},{10,9},{11,12},{12,11},... | collective-permute-start | bytes 196616 | tf_op jit(solution)/shard_map/ppermute | solution.py:137
  94.7 10.2 %collective-permute-start.27 = (bf16[4,128,256]{2,1,0:T(8,128)(2,1)S(1)}, bf16[4,128,256]{2,1,0:T(8,128)(2,1)S(1)}, u32[]{:S(2)}, u32[]{:S(2)}) collective-permute-start(bf16[4,128,256]{2,1,0:T(8,128)(2,1)S(1)} %fusion.20), channel_id=1, source_target_pairs={{8,16},{16,24},{9,17},{17,25},{10,18},{18,26},{11,19},{19,27},{12,... | collective-permute-start | bytes 786440 | tf_op jit(solution)/shard_map/ppermute | solution.py:172
  96.8 17.4 %collective-permute-start.26 = (bf16[4,128,256]{2,1,0:T(8,128)(2,1)S(1)}, bf16[4,128,256]{2,1,0:T(8,128)(2,1)S(1)}, u32[]{:S(2)}, u32[]{:S(2)}) collective-permute-start(bf16[4,128,256]{2,1,0:T(8,128)(2,1)S(1)} %fusion.21), channel_id=1, source_target_pairs={{8,16},{16,24},{9,17},{17,25},{10,18},{18,26},{11,19},{19,27},{12,... | collective-permute-start | bytes 786440 | tf_op jit(solution)/shard_map/ppermute | solution.py:172
  105.1 6.9 %collective-permute-start.28 = (bf16[1,128,256]{2,1,0:T(8,128)(2,1)S(1)}, bf16[1,128,256]{2,1,0:T(8,128)(2,1)S(1)}, u32[]{:S(2)}, u32[]{:S(2)}) collective-permute-start(bf16[1,128,256]{2,1,0:T(8,128)(2,1)S(1)} %get-tuple-element.142), channel_id=1, source_target_pairs={{0,1},{1,0},{2,3},{3,2},{4,5},{5,4},{6,7},{7,6},{8,9},{9,8},{10,11... | collective-permute-start | bytes 196616 | tf_op jit(solution)/shard_map/ppermute | solution.py:137
  107.4 5.6 %collective-permute-start.29 = (bf16[1,128,256]{2,1,0:T(8,128)(2,1)S(1)}, bf16[1,128,256]{2,1,0:T(8,128)(2,1)S(1)}, u32[]{:S(2)}, u32[]{:S(2)}) collective-permute-start(bf16[1,128,256]{2,1,0:T(8,128)(2,1)S(1)} %get-tuple-element.141), channel_id=1, source_target_pairs={{1,2},{2,1},{3,4},{4,3},{5,6},{6,5},{9,10},{10,9},{11,12},{12,11},... | collective-permute-start | bytes 196616 | tf_op jit(solution)/shard_map/ppermute | solution.py:137
  114.4 4.9 %collective-permute-start.30 = (bf16[1,128,256]{2,1,0:T(8,128)(2,1)S(1)}, bf16[1,128,256]{2,1,0:T(8,128)(2,1)S(1)}, u32[]{:S(2)}, u32[]{:S(2)}) collective-permute-start(bf16[1,128,256]{2,1,0:T(8,128)(2,1)S(1)} %get-tuple-element.140), channel_id=1, source_target_pairs={{0,1},{1,0},{2,3},{3,2},{4,5},{5,4},{6,7},{7,6},{8,9},{9,8},{10,11... | collective-permute-start | bytes 196616 | tf_op jit(solution)/shard_map/ppermute | solution.py:137
  114.5 5.7 %collective-permute-start.31 = (bf16[1,128,256]{2,1,0:T(8,128)(2,1)S(1)}, bf16[1,128,256]{2,1,0:T(8,128)(2,1)S(1)}, u32[]{:S(2)}, u32[]{:S(2)}) collective-permute-start(bf16[1,128,256]{2,1,0:T(8,128)(2,1)S(1)} %get-tuple-element.139), channel_id=1, source_target_pairs={{1,2},{2,1},{3,4},{4,3},{5,6},{6,5},{9,10},{10,9},{11,12},{12,11},... | collective-permute-start | bytes 196616 | tf_op jit(solution)/shard_map/ppermute | solution.py:137

commit v11 on v8

--- a/solution.py
+++ b/solution.py
@@ -194,6 +194,8 @@
     halos = swaps(q)
     for slot in range(ticks + 1):
         if slot > 1:
+            if slot > 2:
+                newer[1], relayed[0] = lax.optimization_barrier((newer[1], relayed[0]))
             q = arrived(slot, 1)
             halos = swaps(q)
         *kept, w_one = inner_planes(q, w_one, width, slot == 0)
@@ -215,11 +217,17 @@
             onward = [(j, j + 1) for j in range(1, sections - 1)] if slot > 0 else []
             if slot < ticks - 1:
                 onward = [(0, 1)] + onward
+            relays = {}
+            if slot > 0:
+                held = newer
+                if slot == 1:
+                    held, _ = lax.optimization_barrier((held, second))
+                relays = {k: send(held[k], [(1, sections - 1)]) for k in (1, 0)}
+                if slot > 1:
+                    relays[1], second = lax.optimization_barrier((relays[1], second))
             first, second = lax.optimization_barrier((first, second))
-            received, relays = {1: send(second, onward), 0: send(first, onward)}, {}
+            received = {1: send(second, onward), 0: send(first, onward)}
             if slot > 0:
-                held, _ = lax.optimization_barrier((newer, second))
-                relays = {k: send(held[k], [(1, sections - 1)]) for k in (1, 0)}
                 if across:
                     direct = {0: send(first, across), 1: send(second, across)}
             older, newer, relayed = newer, received, relays

time: 118 us -> 116 us (0.983)
  starting transfers between devices: 67 us -> 63.5 us
  waiting for transfers between devices: 20.8 us -> 22.3 us
    ppermute x15, waiting for transfers between devices: 12.3 us -> 17.7 us  [send(): return lax.ppermute(block, 'section', pairs) if pairs else block]
    ppermute x20, waiting for transfers between devices: 8.41 us -> 4.64 us  [swap(): lax.ppermute(lax.dynamic_slice_in_dim(block, starts[turn], 1, axis=0), 'd...]
    ppermute x15, starting transfers between devices: 25.8 us -> 22.6 us  [send(): return lax.ppermute(block, 'section', pairs) if pairs else block]
  transfers between devices with their start and end apart: 35 -> 35, of which waited for: 11 -> 11; matrix products, arithmetic and copies ran while one was open for 1% -> 2% of each run, Pallas kernels for 19% -> 21%
where the time goes in v11:
time: 116 us
  starting transfers between devices  63.5 us (55%)
  Pallas kernels  26.6 us (23%)
  waiting for transfers between devices  22.3 us (19%)
  local copies, waits for them, and re-layouts  1.27 us (1%)
    ppermute x20, starting transfers between devices, swap(): lax.ppermute(lax.dynamic_slice_in_dim(block, starts[turn], 1, axis=0), 'd...  40.9 us
    pallas_call x20, Pallas kernels, call(): pl.pallas_call(functools.partial(kernel, width), out_shape=[jax.ShapeDtyp...  26.6 us
    ppermute x15, starting transfers between devices, send(): return lax.ppermute(block, 'section', pairs) if pairs else block  22.6 us
    ppermute x15, waiting for transfers between devices, send(): return lax.ppermute(block, 'section', pairs) if pairs else block  17.7 us
    ppermute x20, waiting for transfers between devices, swap(): lax.ppermute(lax.dynamic_slice_in_dim(block, starts[turn], 1, axis=0), 'd...  4.64 us
  transfers between devices with their start and end apart: 35, of which 11 were waited for; matrix products, arithmetic and copies ran while one was open for 2% of the time, Pallas kernels for 21%

profile of v11, /device:TPU:13, one launch (start us, length us, event | category | flops | bytes accessed | tf_op | source)
XLA Modules:
  0.0 115.6 jit_solution(15545180035474885981)
XLA Ops:
  0.0 1.3 %collective-permute-start.2 = (bf16[2,4,128,256]{3,2,1,0:T(8,128)(2,1)}, bf16[2,4,128,256]{3,2,1,0:T(8,128)(2,1)S(1)}, u32[]{:S(2)}, u32[]{:S(2)}) collective-permute-start(bf16[2,4,128,256]{3,2,1,0:T(8,128)(2,1)} %bitcast.66), channel_id=1, source_target_pairs={{0,24},{8,16},{1,25},{9,17},{2,26},{10,18},{3,27},{11,19},{4,28},{... | collective-permute-start | bytes 1572872 | tf_op jit(solution)/shard_map/ppermute | solution.py:171
  1.3 1.1 slice_bitcast_fusion.6
  3.1 3.1 %collective-permute-start.1 = (bf16[1,128,256]{2,1,0:T(8,128)(2,1)S(1)}, bf16[1,128,256]{2,1,0:T(8,128)(2,1)S(1)}, u32[]{:S(2)}, u32[]{:S(2)}) collective-permute-start(bf16[1,128,256]{2,1,0:T(8,128)(2,1)S(1)} %get-tuple-element.157), channel_id=1, source_target_pairs={{1,2},{2,1},{3,4},{4,3},{5,6},{6,5},{9,10},{10,9},{11,12},{12,11},... | collective-permute-start | bytes 196616 | tf_op jit(solution)/shard_map/ppermute | solution.py:137
  6.2 3.2 %shard_map.55 = (bf16[4,128,256]{2,1,0:T(8,128)(2,1)S(1)}, bf16[4,144,256]{2,1,0:T(8,128)(2,1)S(1)}, f32[2,128,256]{2,1,0:T(8,128)S(1)}, bf16[6912,256]{1,0:T(8,128)(2,1)S(1)}) custom-call(bf16[4,128,256]{2,1,0:T(8,128)(2,1)S(1)} %get-tuple-element.138.field.rest_0_, bf16[6912,256]{1,0:T(8,128)(2,1)} %bitcast.58), custom_call_target="tpu_custom_call" | custom-call | flops 1 | bytes 1 | tf_op jit(solution)/shard_map/pallas_call | solution.py:99
  9.5 1.2 %shard_map.56.field = bf16[4,128,256]{2,1,0:T(8,128)(2,1)S(1)} custom-call(s32[1]{0:T(128)} %bitcast.flags, bf16[1,128,256]{2,1,0:T(8,128)(2,1)S(1)} %collective-permute-done.near, bf16[1,128,256]{2,1,0:T(8,128)(2,1)S(1)} %collective-permute-done.1.far, bf16[4,128,256]{2,1,0:T(8,128)(2,1)S(1)} %get-tuple-element.79.even, ...), custom_call_target="tpu_custom_call" | custom-call | flops 1 | bytes 1 | tf_op jit(solution)/shard_map/pallas_call | solution.py:99
  10.8 3.6 %collective-permute-start.6 = (bf16[1,128,256]{2,1,0:T(8,128)(2,1)S(1)}, bf16[1,128,256]{2,1,0:T(8,128)(2,1)S(1)}, u32[]{:S(2)}, u32[]{:S(2)}) collective-permute-start(bf16[1,128,256]{2,1,0:T(8,128)(2,1)S(1)} %get-tuple-element.153), channel_id=1, source_target_pairs={{1,2},{2,1},{3,4},{4,3},{5,6},{6,5},{9,10},{10,9},{11,12},{12,11},... | collective-permute-start | bytes 196616 | tf_op jit(solution)/shard_map/ppermute | solution.py:137
  14.4 1.4 %collective-permute-done.2 = bf16[2,4,128,256]{3,2,1,0:T(8,128)(2,1)S(1)} collective-permute-done((bf16[2,4,128,256]{3,2,1,0:T(8,128)(2,1)}, bf16[2,4,128,256]{3,2,1,0:T(8,128)(2,1)S(1)}, u32[]{:S(2)}, u32[]{:S(2)}) %collective-permute-start.2) | collective-permute-done | bytes 524320 | tf_op jit(solution)/shard_map/ppermute | solution.py:171
  16.1 1.6 %collective-permute-start.3 = (bf16[1,128,256]{2,1,0:T(8,128)(2,1)S(1)}, bf16[1,128,256]{2,1,0:T(8,128)(2,1)S(1)}, u32[]{:S(2)}, u32[]{:S(2)}) collective-permute-start(bf16[1,128,256]{2,1,0:T(8,128)(2,1)S(1)} %get-tuple-element.156), channel_id=1, source_target_pairs={{0,1},{1,0},{2,3},{3,2},{4,5},{5,4},{6,7},{7,6},{8,9},{9,8},{10,11... | collective-permute-start | bytes 196616 | tf_op jit(solution)/shard_map/ppermute | solution.py:137
  17.7 3.1 %collective-permute-start.4 = (bf16[1,128,256]{2,1,0:T(8,128)(2,1)S(1)}, bf16[1,128,256]{2,1,0:T(8,128)(2,1)S(1)}, u32[]{:S(2)}, u32[]{:S(2)}) collective-permute-start(bf16[1,128,256]{2,1,0:T(8,128)(2,1)S(1)} %get-tuple-element.155), channel_id=1, source_target_pairs={{1,2},{2,1},{3,4},{4,3},{5,6},{6,5},{9,10},{10,9},{11,12},{12,11},... | collective-permute-start | bytes 196616 | tf_op jit(solution)/shard_map/ppermute | solution.py:137
  20.8 1.2 %shard_map.57 = (bf16[4,128,256]{2,1,0:T(8,128)(2,1)S(1)}, bf16[4,144,256]{2,1,0:T(8,128)(2,1)S(1)}, f32[2,128,256]{2,1,0:T(8,128)S(1)}) custom-call(bf16[4,128,256]{2,1,0:T(8,128)(2,1)S(1)} %shard_map.56.field, bf16[6912,256]{1,0:T(8,128)(2,1)S(1)} %bitcast.48), custom_call_target="tpu_custom_call" | custom-call | flops 1 | bytes 1 | tf_op jit(solution)/shard_map/pallas_call | solution.py:99
  22.0 1.2 %shard_map.58 = bf16[4,128,256]{2,1,0:T(8,128)(2,1)S(1)} custom-call(s32[1]{0:T(128)} %bitcast.flags, bf16[1,128,256]{2,1,0:T(8,128)(2,1)S(1)} %collective-permute-done.5.near, bf16[1,128,256]{2,1,0:T(8,128)(2,1)S(1)} %collective-permute-done.6.far, bf16[4,128,256]{2,1,0:T(8,128)(2,1)S(1)} %get-tuple-element.86.even, ...), custom_call_target="tpu_custom_call" | custom-call | flops 1 | bytes 1 | tf_op jit(solution)/shard_map/pallas_call | solution.py:99
  24.6 1.2 %shard_map.59 = (bf16[4,128,256]{2,1,0:T(8,128)(2,1)S(1)}, bf16[4,144,256]{2,1,0:T(8,128)(2,1)S(1)}, f32[2,128,256]{2,1,0:T(8,128)S(1)}) custom-call(bf16[4,128,256]{2,1,0:T(8,128)(2,1)S(1)} %get-tuple-element.136.field.rest_0_, bf16[6912,256]{1,0:T(8,128)(2,1)S(1)} %get-tuple-element.82.weights), custom_call_target="tpu_custom_call" | custom-call | flops 1 | bytes 1 | tf_op jit(solution)/shard_map/pallas_call | solution.py:99
  25.8 1.2 %shard_map.60.field = bf16[4,128,256]{2,1,0:T(8,128)(2,1)S(1)} custom-call(s32[1]{0:T(128)} %bitcast.flags, bf16[1,128,256]{2,1,0:T(8,128)(2,1)S(1)} %collective-permute-done.3.near, bf16[1,128,256]{2,1,0:T(8,128)(2,1)S(1)} %collective-permute-done.4.far, bf16[4,128,256]{2,1,0:T(8,128)(2,1)S(1)} %get-tuple-element.93.even, ...), custom_call_target="tpu_custom_call" | custom-call | flops 1 | bytes 1 | tf_op jit(solution)/shard_map/pallas_call | solution.py:99
  27.1 3.6 %collective-permute-start.9 = (bf16[1,128,256]{2,1,0:T(8,128)(2,1)S(1)}, bf16[1,128,256]{2,1,0:T(8,128)(2,1)S(1)}, u32[]{:S(2)}, u32[]{:S(2)}) collective-permute-start(bf16[1,128,256]{2,1,0:T(8,128)(2,1)S(1)} %get-tuple-element.151), channel_id=1, source_target_pairs={{1,2},{2,1},{3,4},{4,3},{5,6},{6,5},{9,10},{10,9},{11,12},{12,11},... | collective-permute-start | bytes 196616 | tf_op jit(solution)/shard_map/ppermute | solution.py:137
  30.7 1.2 %shard_map.61 = (bf16[4,128,256]{2,1,0:T(8,128)(2,1)S(1)}, bf16[4,144,256]{2,1,0:T(8,128)(2,1)S(1)}, f32[2,128,256]{2,1,0:T(8,128)S(1)}) custom-call(bf16[4,128,256]{2,1,0:T(8,128)(2,1)S(1)} %shard_map.60.field, bf16[6912,256]{1,0:T(8,128)(2,1)S(1)} %bitcast.50), custom_call_target="tpu_custom_call" | custom-call | flops 1 | bytes 1 | tf_op jit(solution)/shard_map/pallas_call | solution.py:99
  31.9 0.9 collective-permute-done.9.far
  32.8 1.2 %shard_map.62 = bf16[4,128,256]{2,1,0:T(8,128)(2,1)S(1)} custom-call(s32[1]{0:T(128)} %bitcast.flags, bf16[1,128,256]{2,1,0:T(8,128)(2,1)S(1)} %collective-permute-done.8.near, bf16[1,128,256]{2,1,0:T(8,128)(2,1)S(1)} %collective-permute-done.9.far, bf16[4,128,256]{2,1,0:T(8,128)(2,1)S(1)} %get-tuple-element.96.even, ...), custom_call_target="tpu_custom_call" | custom-call | flops 1 | bytes 1 | tf_op jit(solution)/shard_map/pallas_call | solution.py:99
  34.0 3.1 %collective-permute-start.13 = (bf16[4,128,256]{2,1,0:T(8,128)(2,1)S(1)}, bf16[4,128,256]{2,1,0:T(8,128)(2,1)S(1)}, u32[]{:S(2)}, u32[]{:S(2)}) collective-permute-start(bf16[4,128,256]{2,1,0:T(8,128)(2,1)S(1)} %shard_map.62), channel_id=1, source_target_pairs={{0,8},{8,16},{16,24},{1,9},{9,17},{17,25},{2,10},{10,18},{18,26},{... | collective-permute-start | bytes 786440 | tf_op jit(solution)/shard_map/ppermute | solution.py:171
  37.8 1.9 %collective-permute-start.10 = (bf16[4,128,256]{2,1,0:T(8,128)(2,1)S(1)}, bf16[4,128,256]{2,1,0:T(8,128)(2,1)S(1)}, u32[]{:S(2)}, u32[]{:S(2)}) collective-permute-start(bf16[4,128,256]{2,1,0:T(8,128)(2,1)S(1)} %shard_map.60.field), channel_id=1, source_target_pairs={{0,8},{8,16},{16,24},{1,9},{9,17},{17,25},{2,10},{10,18},{18,26},{... | collective-permute-start | bytes 786440 | tf_op jit(solution)/shard_map/ppermute | solution.py:171
  40.5 3.8 %collective-permute-done.13 = bf16[4,128,256]{2,1,0:T(8,128)(2,1)S(1)} collective-permute-done((bf16[4,128,256]{2,1,0:T(8,128)(2,1)S(1)}, bf16[4,128,256]{2,1,0:T(8,128)(2,1)S(1)}, u32[]{:S(2)}, u32[]{:S(2)}) %collective-permute-start.13) | collective-permute-done | bytes 262176 | tf_op jit(solution)/shard_map/ppermute | solution.py:171
  44.4 2.1 %collective-permute-start.15 = (bf16[1,128,256]{2,1,0:T(8,128)(2,1)S(1)}, bf16[1,128,256]{2,1,0:T(8,128)(2,1)S(1)}, u32[]{:S(2)}, u32[]{:S(2)}) collective-permute-start(bf16[1,128,256]{2,1,0:T(8,128)(2,1)S(1)} %get-tuple-element.150), channel_id=1, source_target_pairs={{0,1},{1,0},{2,3},{3,2},{4,5},{5,4},{6,7},{7,6},{8,9},{9,8},{10,11... | collective-permute-start | bytes 196616 | tf_op jit(solution)/shard_map/ppermute | solution.py:137
  46.6 3.1 %collective-permute-start.16 = (bf16[1,128,256]{2,1,0:T(8,128)(2,1)S(1)}, bf16[1,128,256]{2,1,0:T(8,128)(2,1)S(1)}, u32[]{:S(2)}, u32[]{:S(2)}) collective-permute-start(bf16[1,128,256]{2,1,0:T(8,128)(2,1)S(1)} %get-tuple-element.149), channel_id=1, source_target_pairs={{1,2},{2,1},{3,4},{4,3},{5,6},{6,5},{9,10},{10,9},{11,12},{12,11},... | collective-permute-start | bytes 196616 | tf_op jit(solution)/shard_map/ppermute | solution.py:137
  50.5 1.2 %shard_map.63 = (bf16[4,128,256]{2,1,0:T(8,128)(2,1)S(1)}, bf16[4,144,256]{2,1,0:T(8,128)(2,1)S(1)}, f32[2,128,256]{2,1,0:T(8,128)S(1)}) custom-call(bf16[4,128,256]{2,1,0:T(8,128)(2,1)S(1)} %fusion.16.field.rest_0_, bf16[6912,256]{1,0:T(8,128)(2,1)S(1)} %get-tuple-element.82.weights), custom_call_target="tpu_custom_call" | custom-call | flops 1 | bytes 1 | tf_op jit(solution)/shard_map/pallas_call | solution.py:99
  52.1 1.2 %shard_map.64 = f32[4,128,256]{2,1,0:T(8,128)S(1)} custom-call(s32[1]{0:T(128)} %bitcast.flags, bf16[1,128,256]{2,1,0:T(8,128)(2,1)S(1)} %collective-permute-done.15.near, bf16[1,128,256]{2,1,0:T(8,128)(2,1)S(1)} %collective-permute-done.16.far, bf16[4,128,256]{2,1,0:T(8,128)(2,1)S(1)} %get-tuple-element.105.even, ...), custom_call_target="tpu_custom_call" | custom-call | flops 1 | bytes 1 | tf_op jit(solution)/shard_map/pallas_call | solution.py:99
  53.7 3.6 %collective-permute-start.19 = (bf16[1,128,256]{2,1,0:T(8,128)(2,1)S(1)}, bf16[1,128,256]{2,1,0:T(8,128)(2,1)S(1)}, u32[]{:S(2)}, u32[]{:S(2)}) collective-permute-start(bf16[1,128,256]{2,1,0:T(8,128)(2,1)S(1)} %get-tuple-element.147), channel_id=1, source_target_pairs={{1,2},{2,1},{3,4},{4,3},{5,6},{6,5},{9,10},{10,9},{11,12},{12,11},... | collective-permute-start | bytes 196616 | tf_op jit(solution)/shard_map/ppermute | solution.py:137
  57.9 1.2 %shard_map.65 = (bf16[4,128,256]{2,1,0:T(8,128)(2,1)S(1)}, bf16[4,144,256]{2,1,0:T(8,128)(2,1)S(1)}, f32[2,128,256]{2,1,0:T(8,128)S(1)}) custom-call(bf16[4,128,256]{2,1,0:T(8,128)(2,1)S(1)} %add_convert_fusion.6.field, bf16[6912,256]{1,0:T(8,128)(2,1)S(1)} %bitcast.52), custom_call_target="tpu_custom_call" | custom-call | flops 1 | bytes 1 | tf_op jit(solution)/shard_map/pallas_call | solution.py:99
  59.3 1.2 %shard_map.66 = bf16[4,128,256]{2,1,0:T(8,128)(2,1)S(1)} custom-call(s32[1]{0:T(128)} %bitcast.flags, bf16[1,128,256]{2,1,0:T(8,128)(2,1)S(1)} %collective-permute-done.18.near, bf16[1,128,256]{2,1,0:T(8,128)(2,1)S(1)} %collective-permute-done.19.far, bf16[4,128,256]{2,1,0:T(8,128)(2,1)S(1)} %get-tuple-element.108.even, ...), custom_call_target="tpu_custom_call" | custom-call | flops 1 | bytes 1 | tf_op jit(solution)/shard_map/pallas_call | solution.py:99
  60.5 4.5 %collective-permute-start.21 = (bf16[4,128,256]{2,1,0:T(8,128)(2,1)S(1)}, bf16[4,128,256]{2,1,0:T(8,128)(2,1)S(1)}, u32[]{:S(2)}, u32[]{:S(2)}) collective-permute-start(bf16[4,128,256]{2,1,0:T(8,128)(2,1)S(1)} %shard_map.66), channel_id=1, source_target_pairs={{0,8},{8,16},{16,24},{1,9},{9,17},{17,25},{2,10},{10,18},{18,26},{... | collective-permute-start | bytes 786440 | tf_op jit(solution)/shard_map/ppermute | solution.py:171
  65.0 1.9 %collective-permute-start.20 = (bf16[4,128,256]{2,1,0:T(8,128)(2,1)S(1)}, bf16[4,128,256]{2,1,0:T(8,128)(2,1)S(1)}, u32[]{:S(2)}, u32[]{:S(2)}) collective-permute-start(bf16[4,128,256]{2,1,0:T(8,128)(2,1)S(1)} %add_convert_fusion.6.field), channel_id=1, source_target_pairs={{0,8},{8,16},{16,24},{1,9},{9,17},{17,25},{2,10},{10,18},{18,26},{... | collective-permute-start | bytes 786440 | tf_op jit(solution)/shard_map/ppermute | solution.py:171
  67.0 6.4 %collective-permute-done.21 = bf16[4,128,256]{2,1,0:T(8,128)(2,1)S(1)} collective-permute-done((bf16[4,128,256]{2,1,0:T(8,128)(2,1)S(1)}, bf16[4,128,256]{2,1,0:T(8,128)(2,1)S(1)}, u32[]{:S(2)}, u32[]{:S(2)}) %collective-permute-start.21) | collective-permute-done | bytes 262176 | tf_op jit(solution)/shard_map/ppermute | solution.py:171
  74.3 3.0 %collective-permute-start.24 = (bf16[1,128,256]{2,1,0:T(8,128)(2,1)S(1)}, bf16[1,128,256]{2,1,0:T(8,128)(2,1)S(1)}, u32[]{:S(2)}, u32[]{:S(2)}) collective-permute-start(bf16[1,128,256]{2,1,0:T(8,128)(2,1)S(1)} %get-tuple-element.145), channel_id=1, source_target_pairs={{1,2},{2,1},{3,4},{4,3},{5,6},{6,5},{9,10},{10,9},{11,12},{12,11},... | collective-permute-start | bytes 196616 | tf_op jit(solution)/shard_map/ppermute | solution.py:137
  78.1 1.2 %shard_map.67 = (bf16[4,128,256]{2,1,0:T(8,128)(2,1)S(1)}, bf16[4,144,256]{2,1,0:T(8,128)(2,1)S(1)}, f32[2,128,256]{2,1,0:T(8,128)S(1)}) custom-call(bf16[4,128,256]{2,1,0:T(8,128)(2,1)S(1)} %fusion.14.field.rest_0_, bf16[6912,256]{1,0:T(8,128)(2,1)S(1)} %get-tuple-element.82.weights), custom_call_target="tpu_custom_call" | custom-call | flops 1 | bytes 1 | tf_op jit(solution)/shard_map/pallas_call | solution.py:99
  79.9 1.2 %shard_map.68 = f32[4,128,256]{2,1,0:T(8,128)S(1)} custom-call(s32[1]{0:T(128)} %bitcast.flags, bf16[1,128,256]{2,1,0:T(8,128)(2,1)S(1)} %collective-permute-done.23.near, bf16[1,128,256]{2,1,0:T(8,128)(2,1)S(1)} %collective-permute-done.24.far, bf16[4,128,256]{2,1,0:T(8,128)(2,1)S(1)} %get-tuple-element.117.even, ...), custom_call_target="tpu_custom_call" | custom-call | flops 1 | bytes 1 | tf_op jit(solution)/shard_map/pallas_call | solution.py:99
  81.4 3.5 %collective-permute-start.27 = (bf16[1,128,256]{2,1,0:T(8,128)(2,1)S(1)}, bf16[1,128,256]{2,1,0:T(8,128)(2,1)S(1)}, u32[]{:S(2)}, u32[]{:S(2)}) collective-permute-start(bf16[1,128,256]{2,1,0:T(8,128)(2,1)S(1)} %get-tuple-element.143), channel_id=1, source_target_pairs={{1,2},{2,1},{3,4},{4,3},{5,6},{6,5},{9,10},{10,9},{11,12},{12,11},... | collective-permute-start | bytes 196616 | tf_op jit(solution)/shard_map/ppermute | solution.py:137
  85.6 1.2 %shard_map.69 = (bf16[4,128,256]{2,1,0:T(8,128)(2,1)S(1)}, bf16[4,144,256]{2,1,0:T(8,128)(2,1)S(1)}, f32[2,128,256]{2,1,0:T(8,128)S(1)}) custom-call(bf16[4,128,256]{2,1,0:T(8,128)(2,1)S(1)} %add_convert_fusion.3.field, bf16[6912,256]{1,0:T(8,128)(2,1)S(1)} %bitcast.54), custom_call_target="tpu_custom_call" | custom-call | flops 1 | bytes 1 | tf_op jit(solution)/shard_map/pallas_call | solution.py:99
  87.1 1.2 %shard_map.70 = bf16[4,128,256]{2,1,0:T(8,128)(2,1)S(1)} custom-call(s32[1]{0:T(128)} %bitcast.flags, bf16[1,128,256]{2,1,0:T(8,128)(2,1)S(1)} %collective-permute-done.26.near, bf16[1,128,256]{2,1,0:T(8,128)(2,1)S(1)} %collective-permute-done.27.far, bf16[4,128,256]{2,1,0:T(8,128)(2,1)S(1)} %get-tuple-element.120.even, ...), custom_call_target="tpu_custom_call" | custom-call | flops 1 | bytes 1 | tf_op jit(solution)/shard_map/pallas_call | solution.py:99
  88.3 2.3 %collective-permute-start.29 = (bf16[4,128,256]{2,1,0:T(8,128)(2,1)S(1)}, bf16[4,128,256]{2,1,0:T(8,128)(2,1)S(1)}, u32[]{:S(2)}, u32[]{:S(2)}) collective-permute-start(bf16[4,128,256]{2,1,0:T(8,128)(2,1)S(1)} %shard_map.70), channel_id=1, source_target_pairs={{8,16},{16,24},{9,17},{17,25},{10,18},{18,26},{11,19},{19,27},{12,... | collective-permute-start | bytes 786440 | tf_op jit(solution)/shard_map/ppermute | solution.py:171
  90.6 1.9 %collective-permute-start.28 = (bf16[4,128,256]{2,1,0:T(8,128)(2,1)S(1)}, bf16[4,128,256]{2,1,0:T(8,128)(2,1)S(1)}, u32[]{:S(2)}, u32[]{:S(2)}) collective-permute-start(bf16[4,128,256]{2,1,0:T(8,128)(2,1)S(1)} %add_convert_fusion.3.field), channel_id=1, source_target_pairs={{8,16},{16,24},{9,17},{17,25},{10,18},{18,26},{11,19},{19,27},{12,... | collective-permute-start | bytes 786440 | tf_op jit(solution)/shard_map/ppermute | solution.py:171
  92.6 6.0 %collective-permute-done.29 = bf16[4,128,256]{2,1,0:T(8,128)(2,1)S(1)} collective-permute-done((bf16[4,128,256]{2,1,0:T(8,128)(2,1)S(1)}, bf16[4,128,256]{2,1,0:T(8,128)(2,1)S(1)}, u32[]{:S(2)}, u32[]{:S(2)}) %collective-permute-start.29) | collective-permute-done | bytes 262176 | tf_op jit(solution)/shard_map/ppermute | solution.py:171
  98.7 2.1 %collective-permute-start.31 = (bf16[1,128,256]{2,1,0:T(8,128)(2,1)S(1)}, bf16[1,128,256]{2,1,0:T(8,128)(2,1)S(1)}, u32[]{:S(2)}, u32[]{:S(2)}) collective-permute-start(bf16[1,128,256]{2,1,0:T(8,128)(2,1)S(1)} %get-tuple-element.142), channel_id=1, source_target_pairs={{0,1},{1,0},{2,3},{3,2},{4,5},{5,4},{6,7},{7,6},{8,9},{9,8},{10,11... | collective-permute-start | bytes 196616 | tf_op jit(solution)/shard_map/ppermute | solution.py:137
  100.8 3.0 %collective-permute-start.32 = (bf16[1,128,256]{2,1,0:T(8,128)(2,1)S(1)}, bf16[1,128,256]{2,1,0:T(8,128)(2,1)S(1)}, u32[]{:S(2)}, u32[]{:S(2)}) collective-permute-start(bf16[1,128,256]{2,1,0:T(8,128)(2,1)S(1)} %get-tuple-element.141), channel_id=1, source_target_pairs={{1,2},{2,1},{3,4},{4,3},{5,6},{6,5},{9,10},{10,9},{11,12},{12,11},... | collective-permute-start | bytes 196616 | tf_op jit(solution)/shard_map/ppermute | solution.py:137
  103.9 1.2 %shard_map.71 = (bf16[4,128,256]{2,1,0:T(8,128)(2,1)S(1)}, bf16[4,144,256]{2,1,0:T(8,128)(2,1)S(1)}, f32[2,128,256]{2,1,0:T(8,128)S(1)}) custom-call(bf16[4,128,256]{2,1,0:T(8,128)(2,1)S(1)} %fusion.12.field.rest_1_, bf16[6912,256]{1,0:T(8,128)(2,1)S(1)} %get-tuple-element.82.weights), custom_call_target="tpu_custom_call" | custom-call | flops 1 | bytes 1 | tf_op jit(solution)/shard_map/pallas_call | solution.py:99
  105.1 1.3 %collective-permute-done.32.far = bf16[1,128,256]{2,1,0:T(8,128)(2,1)S(1)} collective-permute-done((bf16[1,128,256]{2,1,0:T(8,128)(2,1)S(1)}, bf16[1,128,256]{2,1,0:T(8,128)(2,1)S(1)}, u32[]{:S(2)}, u32[]{:S(2)}) %collective-permute-start.32) | collective-permute-done | bytes 65568 | tf_op jit(solution)/shard_map/ppermute | solution.py:137
  106.4 1.2 %shard_map.72 = f32[4,128,256]{2,1,0:T(8,128)S(1)} custom-call(s32[1]{0:T(128)} %bitcast.flags, bf16[1,128,256]{2,1,0:T(8,128)(2,1)S(1)} %collective-permute-done.31.near, bf16[1,128,256]{2,1,0:T(8,128)(2,1)S(1)} %collective-permute-done.32.far, bf16[4,128,256]{2,1,0:T(8,128)(2,1)S(1)} %get-tuple-element.129.even, ...), custom_call_target="tpu_custom_call" | custom-call | flops 1 | bytes 1 | tf_op jit(solution)/shard_map/pallas_call | solution.py:99
  107.9 3.5 %collective-permute-start.34 = (bf16[1,128,256]{2,1,0:T(8,128)(2,1)S(1)}, bf16[1,128,256]{2,1,0:T(8,128)(2,1)S(1)}, u32[]{:S(2)}, u32[]{:S(2)}) collective-permute-start(bf16[1,128,256]{2,1,0:T(8,128)(2,1)S(1)} %get-tuple-element.139), channel_id=1, source_target_pairs={{1,2},{2,1},{3,4},{4,3},{5,6},{6,5},{9,10},{10,9},{11,12},{12,11},... | collective-permute-start | bytes 196616 | tf_op jit(solution)/shard_map/ppermute | solution.py:137
  111.4 1.2 %shard_map.73 = (bf16[4,128,256]{2,1,0:T(8,128)(2,1)S(1)}, bf16[4,144,256]{2,1,0:T(8,128)(2,1)S(1)}, f32[2,128,256]{2,1,0:T(8,128)S(1)}) custom-call(bf16[4,128,256]{2,1,0:T(8,128)(2,1)S(1)} %add_convert_fusion.field.rest_0_, bf16[6912,256]{1,0:T(8,128)(2,1)S(1)} %bitcast.56), custom_call_target="tpu_custom_call" | custom-call | flops 1 | bytes 1 | tf_op jit(solution)/shard_map/pallas_call | solution.py:99
  112.6 0.9 collective-permute-done.34.far
  113.6 2.0 %shard_map.74 = bf16[2,4,128,256]{3,2,1,0:T(8,128)(2,1)} custom-call(s32[1]{0:T(128)} %bitcast.flags, bf16[1,128,256]{2,1,0:T(8,128)(2,1)S(1)} %collective-permute-done.33.near, bf16[1,128,256]{2,1,0:T(8,128)(2,1)S(1)} %collective-permute-done.34.far, bf16[4,128,256]{2,1,0:T(8,128)(2,1)S(1)} %get-tuple-element.132.even, ...), custom_call_target="tpu_custom_call" | custom-call | flops 1 | bytes 1 | tf_op jit(solution)/shard_map/pallas_call | solution.py:99
  (66 shorter events, 10.5 us)
Async XLA Ops:
  0.0 15.8 %collective-permute-start.2 = (bf16[2,4,128,256]{3,2,1,0:T(8,128)(2,1)}, bf16[2,4,128,256]{3,2,1,0:T(8,128)(2,1)S(1)}, u32[]{:S(2)}, u32[]{:S(2)}) collective-permute-start(bf16[2,4,128,256]{3,2,1,0:T(8,128)(2,1)} %bitcast.66), channel_id=1, source_target_pairs={{0,24},{8,16},{1,25},{9,17},{2,26},{10,18},{3,27},{11,19},{4,28},{... | collective-permute-start | bytes 1572872 | tf_op jit(solution)/shard_map/ppermute | solution.py:171
  2.4 7.0 %collective-permute-start = (bf16[1,128,256]{2,1,0:T(8,128)(2,1)S(1)}, bf16[1,128,256]{2,1,0:T(8,128)(2,1)S(1)}, u32[]{:S(2)}, u32[]{:S(2)}) collective-permute-start(bf16[1,128,256]{2,1,0:T(8,128)(2,1)S(1)} %get-tuple-element.158), channel_id=1, source_target_pairs={{0,1},{1,0},{2,3},{3,2},{4,5},{5,4},{6,7},{7,6},{8,9},{9,8},{10,11... | collective-permute-start | bytes 196616 | tf_op jit(solution)/shard_map/ppermute | solution.py:137
  3.1 6.3 %collective-permute-start.1 = (bf16[1,128,256]{2,1,0:T(8,128)(2,1)S(1)}, bf16[1,128,256]{2,1,0:T(8,128)(2,1)S(1)}, u32[]{:S(2)}, u32[]{:S(2)}) collective-permute-start(bf16[1,128,256]{2,1,0:T(8,128)(2,1)S(1)} %get-tuple-element.157), channel_id=1, source_target_pairs={{1,2},{2,1},{3,4},{4,3},{5,6},{6,5},{9,10},{10,9},{11,12},{12,11},... | collective-permute-start | bytes 196616 | tf_op jit(solution)/shard_map/ppermute | solution.py:137
  6.2 9.5 %copy-start.2 = (bf16[1,2,4,16,8,256]{5,4,3,2,1,0:T(8,128)(2,1)S(1)}, bf16[1,2,4,16,8,256]{5,4,3,2,1,0:T(8,128)(2,1)}, u32[]{:S(2)}) copy-start(bf16[1,2,4,16,8,256]{5,4,3,2,1,0:T(8,128)(2,1)} %param.5) | copy-start | bytes 1572868
  9.5 6.3 %copy-start.1 = (bf16[3,2,4,16,8,256]{5,4,3,2,1,0:T(8,128)(2,1)S(1)}, bf16[3,2,4,16,8,256]{5,4,3,2,1,0:T(8,128)(2,1)}, u32[]{:S(2)}) copy-start(bf16[3,2,4,16,8,256]{5,4,3,2,1,0:T(8,128)(2,1)} %param.7) | copy-start | bytes 4718596
  9.5 11.3 %copy-start = (bf16[1,3,3,3,256,256]{5,4,3,2,1,0:T(8,128)(2,1)S(1)}, bf16[1,3,3,3,256,256]{5,4,3,2,1,0:T(8,128)(2,1)}, u32[]{:S(2)}) copy-start(bf16[1,3,3,3,256,256]{5,4,3,2,1,0:T(8,128)(2,1)} %param.9) | copy-start | bytes 10616836
  10.7 11.3 %collective-permute-start.5 = (bf16[1,128,256]{2,1,0:T(8,128)(2,1)S(1)}, bf16[1,128,256]{2,1,0:T(8,128)(2,1)S(1)}, u32[]{:S(2)}, u32[]{:S(2)}) collective-permute-start(bf16[1,128,256]{2,1,0:T(8,128)(2,1)S(1)} %get-tuple-element.154), channel_id=1, source_target_pairs={{0,1},{1,0},{2,3},{3,2},{4,5},{5,4},{6,7},{7,6},{8,9},{9,8},{10,11... | collective-permute-start | bytes 196616 | tf_op jit(solution)/shard_map/ppermute | solution.py:137
  10.8 11.2 %collective-permute-start.6 = (bf16[1,128,256]{2,1,0:T(8,128)(2,1)S(1)}, bf16[1,128,256]{2,1,0:T(8,128)(2,1)S(1)}, u32[]{:S(2)}, u32[]{:S(2)}) collective-permute-start(bf16[1,128,256]{2,1,0:T(8,128)(2,1)S(1)} %get-tuple-element.153), channel_id=1, source_target_pairs={{1,2},{2,1},{3,4},{4,3},{5,6},{6,5},{9,10},{10,9},{11,12},{12,11},... | collective-permute-start | bytes 196616 | tf_op jit(solution)/shard_map/ppermute | solution.py:137
  16.1 7.2 %collective-permute-start.3 = (bf16[1,128,256]{2,1,0:T(8,128)(2,1)S(1)}, bf16[1,128,256]{2,1,0:T(8,128)(2,1)S(1)}, u32[]{:S(2)}, u32[]{:S(2)}) collective-permute-start(bf16[1,128,256]{2,1,0:T(8,128)(2,1)S(1)} %get-tuple-element.156), channel_id=1, source_target_pairs={{0,1},{1,0},{2,3},{3,2},{4,5},{5,4},{6,7},{7,6},{8,9},{9,8},{10,11... | collective-permute-start | bytes 196616 | tf_op jit(solution)/shard_map/ppermute | solution.py:137
  17.7 5.6 %collective-permute-start.4 = (bf16[1,128,256]{2,1,0:T(8,128)(2,1)S(1)}, bf16[1,128,256]{2,1,0:T(8,128)(2,1)S(1)}, u32[]{:S(2)}, u32[]{:S(2)}) collective-permute-start(bf16[1,128,256]{2,1,0:T(8,128)(2,1)S(1)} %get-tuple-element.155), channel_id=1, source_target_pairs={{1,2},{2,1},{3,4},{4,3},{5,6},{6,5},{9,10},{10,9},{11,12},{12,11},... | collective-permute-start | bytes 196616 | tf_op jit(solution)/shard_map/ppermute | solution.py:137
  23.2 13.9 %collective-permute-start.7 = (bf16[4,128,256]{2,1,0:T(8,128)(2,1)S(1)}, bf16[4,128,256]{2,1,0:T(8,128)(2,1)S(1)}, u32[]{:S(2)}, u32[]{:S(2)}) collective-permute-start(bf16[4,128,256]{2,1,0:T(8,128)(2,1)S(1)} %shard_map.56.field), channel_id=1, source_target_pairs={{0,8},{1,9},{2,10},{3,11},{4,12},{5,13},{6,14},{7,15}} | collective-permute-start | bytes 786440 | tf_op jit(solution)/shard_map/ppermute | solution.py:171
  23.9 13.2 %collective-permute-start.11 = (bf16[4,128,256]{2,1,0:T(8,128)(2,1)S(1)}, bf16[4,128,256]{2,1,0:T(8,128)(2,1)S(1)}, u32[]{:S(2)}, u32[]{:S(2)}) collective-permute-start(bf16[4,128,256]{2,1,0:T(8,128)(2,1)S(1)} %shard_map.58), channel_id=1, source_target_pairs={{0,8},{1,9},{2,10},{3,11},{4,12},{5,13},{6,14},{7,15}} | collective-permute-start | bytes 786440 | tf_op jit(solution)/shard_map/ppermute | solution.py:171
  27.1 4.9 %collective-permute-start.8 = (bf16[1,128,256]{2,1,0:T(8,128)(2,1)S(1)}, bf16[1,128,256]{2,1,0:T(8,128)(2,1)S(1)}, u32[]{:S(2)}, u32[]{:S(2)}) collective-permute-start(bf16[1,128,256]{2,1,0:T(8,128)(2,1)S(1)} %get-tuple-element.152), channel_id=1, source_target_pairs={{0,1},{1,0},{2,3},{3,2},{4,5},{5,4},{6,7},{7,6},{8,9},{9,8},{10,11... | collective-permute-start | bytes 196616 | tf_op jit(solution)/shard_map/ppermute | solution.py:137
  27.1 5.7 %collective-permute-start.9 = (bf16[1,128,256]{2,1,0:T(8,128)(2,1)S(1)}, bf16[1,128,256]{2,1,0:T(8,128)(2,1)S(1)}, u32[]{:S(2)}, u32[]{:S(2)}) collective-permute-start(bf16[1,128,256]{2,1,0:T(8,128)(2,1)S(1)} %get-tuple-element.151), channel_id=1, source_target_pairs={{1,2},{2,1},{3,4},{4,3},{5,6},{6,5},{9,10},{10,9},{11,12},{12,11},... | collective-permute-start | bytes 196616 | tf_op jit(solution)/shard_map/ppermute | solution.py:137
  34.0 10.3 %collective-permute-start.13 = (bf16[4,128,256]{2,1,0:T(8,128)(2,1)S(1)}, bf16[4,128,256]{2,1,0:T(8,128)(2,1)S(1)}, u32[]{:S(2)}, u32[]{:S(2)}) collective-permute-start(bf16[4,128,256]{2,1,0:T(8,128)(2,1)S(1)} %shard_map.62), channel_id=1, source_target_pairs={{0,8},{8,16},{16,24},{1,9},{9,17},{17,25},{2,10},{10,18},{18,26},{... | collective-permute-start | bytes 786440 | tf_op jit(solution)/shard_map/ppermute | solution.py:171
  37.2 7.1 %collective-permute-start.14 = (bf16[4,128,256]{2,1,0:T(8,128)(2,1)S(1)}, bf16[4,128,256]{2,1,0:T(8,128)(2,1)S(1)}, u32[]{:S(2)}, u32[]{:S(2)}) collective-permute-start(bf16[4,128,256]{2,1,0:T(8,128)(2,1)S(1)} %collective-permute-done.11), channel_id=1, source_target_pairs={{8,24},{9,25},{10,26},{11,27},{12,28},{13,29},{14,30},{15,31}} | collective-permute-start | bytes 786440 | tf_op jit(solution)/shard_map/ppermute | solution.py:171
  37.8 15.5 %collective-permute-start.10 = (bf16[4,128,256]{2,1,0:T(8,128)(2,1)S(1)}, bf16[4,128,256]{2,1,0:T(8,128)(2,1)S(1)}, u32[]{:S(2)}, u32[]{:S(2)}) collective-permute-start(bf16[4,128,256]{2,1,0:T(8,128)(2,1)S(1)} %shard_map.60.field), channel_id=1, source_target_pairs={{0,8},{8,16},{16,24},{1,9},{9,17},{17,25},{2,10},{10,18},{18,26},{... | collective-permute-start | bytes 786440 | tf_op jit(solution)/shard_map/ppermute | solution.py:171
  39.8 13.6 %collective-permute-start.12 = (bf16[4,128,256]{2,1,0:T(8,128)(2,1)S(1)}, bf16[4,128,256]{2,1,0:T(8,128)(2,1)S(1)}, u32[]{:S(2)}, u32[]{:S(2)}) collective-permute-start(bf16[4,128,256]{2,1,0:T(8,128)(2,1)S(1)} %collective-permute-done.7), channel_id=1, source_target_pairs={{8,24},{9,25},{10,26},{11,27},{12,28},{13,29},{14,30},{15,31}} | collective-permute-start | bytes 786440 | tf_op jit(solution)/shard_map/ppermute | solution.py:171
  44.4 7.3 %collective-permute-start.15 = (bf16[1,128,256]{2,1,0:T(8,128)(2,1)S(1)}, bf16[1,128,256]{2,1,0:T(8,128)(2,1)S(1)}, u32[]{:S(2)}, u32[]{:S(2)}) collective-permute-start(bf16[1,128,256]{2,1,0:T(8,128)(2,1)S(1)} %get-tuple-element.150), channel_id=1, source_target_pairs={{0,1},{1,0},{2,3},{3,2},{4,5},{5,4},{6,7},{7,6},{8,9},{9,8},{10,11... | collective-permute-start | bytes 196616 | tf_op jit(solution)/shard_map/ppermute | solution.py:137
  46.6 5.6 %collective-permute-start.16 = (bf16[1,128,256]{2,1,0:T(8,128)(2,1)S(1)}, bf16[1,128,256]{2,1,0:T(8,128)(2,1)S(1)}, u32[]{:S(2)}, u32[]{:S(2)}) collective-permute-start(bf16[1,128,256]{2,1,0:T(8,128)(2,1)S(1)} %get-tuple-element.149), channel_id=1, source_target_pairs={{1,2},{2,1},{3,4},{4,3},{5,6},{6,5},{9,10},{10,9},{11,12},{12,11},... | collective-permute-start | bytes 196616 | tf_op jit(solution)/shard_map/ppermute | solution.py:137
  49.7 10.8 %collective-permute-start.17 = (bf16[4,128,256]{2,1,0:T(8,128)(2,1)S(1)}, bf16[4,128,256]{2,1,0:T(8,128)(2,1)S(1)}, u32[]{:S(2)}, u32[]{:S(2)}) collective-permute-start(bf16[4,128,256]{2,1,0:T(8,128)(2,1)S(1)} %collective-permute-done.13), channel_id=1, source_target_pairs={{8,24},{9,25},{10,26},{11,27},{12,28},{13,29},{14,30},{15,31}} | collective-permute-start | bytes 786440 | tf_op jit(solution)/shard_map/ppermute | solution.py:171
  53.6 5.6 %collective-permute-start.18 = (bf16[1,128,256]{2,1,0:T(8,128)(2,1)S(1)}, bf16[1,128,256]{2,1,0:T(8,128)(2,1)S(1)}, u32[]{:S(2)}, u32[]{:S(2)}) collective-permute-start(bf16[1,128,256]{2,1,0:T(8,128)(2,1)S(1)} %get-tuple-element.148), channel_id=1, source_target_pairs={{0,1},{1,0},{2,3},{3,2},{4,5},{5,4},{6,7},{7,6},{8,9},{9,8},{10,11... | collective-permute-start | bytes 196616 | tf_op jit(solution)/shard_map/ppermute | solution.py:137
  53.7 5.7 %collective-permute-start.19 = (bf16[1,128,256]{2,1,0:T(8,128)(2,1)S(1)}, bf16[1,128,256]{2,1,0:T(8,128)(2,1)S(1)}, u32[]{:S(2)}, u32[]{:S(2)}) collective-permute-start(bf16[1,128,256]{2,1,0:T(8,128)(2,1)S(1)} %get-tuple-element.147), channel_id=1, source_target_pairs={{1,2},{2,1},{3,4},{4,3},{5,6},{6,5},{9,10},{10,9},{11,12},{12,11},... | collective-permute-start | bytes 196616 | tf_op jit(solution)/shard_map/ppermute | solution.py:137
  57.2 9.8 %collective-permute-start.22 = (bf16[4,128,256]{2,1,0:T(8,128)(2,1)S(1)}, bf16[4,128,256]{2,1,0:T(8,128)(2,1)S(1)}, u32[]{:S(2)}, u32[]{:S(2)}) collective-permute-start(bf16[4,128,256]{2,1,0:T(8,128)(2,1)S(1)} %collective-permute-done.10), channel_id=1, source_target_pairs={{8,24},{9,25},{10,26},{11,27},{12,28},{13,29},{14,30},{15,31}} | collective-permute-start | bytes 786440 | tf_op jit(solution)/shard_map/ppermute | solution.py:171
  60.5 12.8 %collective-permute-start.21 = (bf16[4,128,256]{2,1,0:T(8,128)(2,1)S(1)}, bf16[4,128,256]{2,1,0:T(8,128)(2,1)S(1)}, u32[]{:S(2)}, u32[]{:S(2)}) collective-permute-start(bf16[4,128,256]{2,1,0:T(8,128)(2,1)S(1)} %shard_map.66), channel_id=1, source_target_pairs={{0,8},{8,16},{16,24},{1,9},{9,17},{17,25},{2,10},{10,18},{18,26},{... | collective-permute-start | bytes 786440 | tf_op jit(solution)/shard_map/ppermute | solution.py:171
  65.0 16.0 %collective-permute-start.20 = (bf16[4,128,256]{2,1,0:T(8,128)(2,1)S(1)}, bf16[4,128,256]{2,1,0:T(8,128)(2,1)S(1)}, u32[]{:S(2)}, u32[]{:S(2)}) collective-permute-start(bf16[4,128,256]{2,1,0:T(8,128)(2,1)S(1)} %add_convert_fusion.6.field), channel_id=1, source_target_pairs={{0,8},{8,16},{16,24},{1,9},{9,17},{17,25},{2,10},{10,18},{18,26},{... | collective-permute-start | bytes 786440 | tf_op jit(solution)/shard_map/ppermute | solution.py:171
  73.5 5.8 %collective-permute-start.23 = (bf16[1,128,256]{2,1,0:T(8,128)(2,1)S(1)}, bf16[1,128,256]{2,1,0:T(8,128)(2,1)S(1)}, u32[]{:S(2)}, u32[]{:S(2)}) collective-permute-start(bf16[1,128,256]{2,1,0:T(8,128)(2,1)S(1)} %get-tuple-element.146), channel_id=1, source_target_pairs={{0,1},{1,0},{2,3},{3,2},{4,5},{5,4},{6,7},{7,6},{8,9},{9,8},{10,11... | collective-permute-start | bytes 196616 | tf_op jit(solution)/shard_map/ppermute | solution.py:137
  74.3 5.6 %collective-permute-start.24 = (bf16[1,128,256]{2,1,0:T(8,128)(2,1)S(1)}, bf16[1,128,256]{2,1,0:T(8,128)(2,1)S(1)}, u32[]{:S(2)}, u32[]{:S(2)}) collective-permute-start(bf16[1,128,256]{2,1,0:T(8,128)(2,1)S(1)} %get-tuple-element.145), channel_id=1, source_target_pairs={{1,2},{2,1},{3,4},{4,3},{5,6},{6,5},{9,10},{10,9},{11,12},{12,11},... | collective-permute-start | bytes 196616 | tf_op jit(solution)/shard_map/ppermute | solution.py:137
  77.4 10.9 %collective-permute-start.25 = (bf16[4,128,256]{2,1,0:T(8,128)(2,1)S(1)}, bf16[4,128,256]{2,1,0:T(8,128)(2,1)S(1)}, u32[]{:S(2)}, u32[]{:S(2)}) collective-permute-start(bf16[4,128,256]{2,1,0:T(8,128)(2,1)S(1)} %collective-permute-done.21), channel_id=1, source_target_pairs={{8,24},{9,25},{10,26},{11,27},{12,28},{13,29},{14,30},{15,31}} | collective-permute-start | bytes 786440 | tf_op jit(solution)/shard_map/ppermute | solution.py:171
  81.3 5.5 %collective-permute-start.26 = (bf16[1,128,256]{2,1,0:T(8,128)(2,1)S(1)}, bf16[1,128,256]{2,1,0:T(8,128)(2,1)S(1)}, u32[]{:S(2)}, u32[]{:S(2)}) collective-permute-start(bf16[1,128,256]{2,1,0:T(8,128)(2,1)S(1)} %get-tuple-element.144), channel_id=1, source_target_pairs={{0,1},{1,0},{2,3},{3,2},{4,5},{5,4},{6,7},{7,6},{8,9},{9,8},{10,11... | collective-permute-start | bytes 196616 | tf_op jit(solution)/shard_map/ppermute | solution.py:137
  81.4 5.7 %collective-permute-start.27 = (bf16[1,128,256]{2,1,0:T(8,128)(2,1)S(1)}, bf16[1,128,256]{2,1,0:T(8,128)(2,1)S(1)}, u32[]{:S(2)}, u32[]{:S(2)}) collective-permute-start(bf16[1,128,256]{2,1,0:T(8,128)(2,1)S(1)} %get-tuple-element.143), channel_id=1, source_target_pairs={{1,2},{2,1},{3,4},{4,3},{5,6},{6,5},{9,10},{10,9},{11,12},{12,11},... | collective-permute-start | bytes 196616 | tf_op jit(solution)/shard_map/ppermute | solution.py:137
  84.9 7.7 %collective-permute-start.30 = (bf16[4,128,256]{2,1,0:T(8,128)(2,1)S(1)}, bf16[4,128,256]{2,1,0:T(8,128)(2,1)S(1)}, u32[]{:S(2)}, u32[]{:S(2)}) collective-permute-start(bf16[4,128,256]{2,1,0:T(8,128)(2,1)S(1)} %collective-permute-done.20), channel_id=1, source_target_pairs={{8,24},{9,25},{10,26},{11,27},{12,28},{13,29},{14,30},{15,31}} | collective-permute-start | bytes 786440 | tf_op jit(solution)/shard_map/ppermute | solution.py:171
  88.3 10.3 %collective-permute-start.29 = (bf16[4,128,256]{2,1,0:T(8,128)(2,1)S(1)}, bf16[4,128,256]{2,1,0:T(8,128)(2,1)S(1)}, u32[]{:S(2)}, u32[]{:S(2)}) collective-permute-start(bf16[4,128,256]{2,1,0:T(8,128)(2,1)S(1)} %shard_map.70), channel_id=1, source_target_pairs={{8,16},{16,24},{9,17},{17,25},{10,18},{18,26},{11,19},{19,27},{12,... | collective-permute-start | bytes 786440 | tf_op jit(solution)/shard_map/ppermute | solution.py:171
  90.6 17.0 %collective-permute-start.28 = (bf16[4,128,256]{2,1,0:T(8,128)(2,1)S(1)}, bf16[4,128,256]{2,1,0:T(8,128)(2,1)S(1)}, u32[]{:S(2)}, u32[]{:S(2)}) collective-permute-start(bf16[4,128,256]{2,1,0:T(8,128)(2,1)S(1)} %add_convert_fusion.3.field), channel_id=1, source_target_pairs={{8,16},{16,24},{9,17},{17,25},{10,18},{18,26},{11,19},{19,27},{12,... | collective-permute-start | bytes 786440 | tf_op jit(solution)/shard_map/ppermute | solution.py:171
  98.7 6.4 %collective-permute-start.31 = (bf16[1,128,256]{2,1,0:T(8,128)(2,1)S(1)}, bf16[1,128,256]{2,1,0:T(8,128)(2,1)S(1)}, u32[]{:S(2)}, u32[]{:S(2)}) collective-permute-start(bf16[1,128,256]{2,1,0:T(8,128)(2,1)S(1)} %get-tuple-element.142), channel_id=1, source_target_pairs={{0,1},{1,0},{2,3},{3,2},{4,5},{5,4},{6,7},{7,6},{8,9},{9,8},{10,11... | collective-permute-start | bytes 196616 | tf_op jit(solution)/shard_map/ppermute | solution.py:137
  100.8 5.6 %collective-permute-start.32 = (bf16[1,128,256]{2,1,0:T(8,128)(2,1)S(1)}, bf16[1,128,256]{2,1,0:T(8,128)(2,1)S(1)}, u32[]{:S(2)}, u32[]{:S(2)}) collective-permute-start(bf16[1,128,256]{2,1,0:T(8,128)(2,1)S(1)} %get-tuple-element.141), channel_id=1, source_target_pairs={{1,2},{2,1},{3,4},{4,3},{5,6},{6,5},{9,10},{10,9},{11,12},{12,11},... | collective-permute-start | bytes 196616 | tf_op jit(solution)/shard_map/ppermute | solution.py:137
  107.8 4.8 %collective-permute-start.33 = (bf16[1,128,256]{2,1,0:T(8,128)(2,1)S(1)}, bf16[1,128,256]{2,1,0:T(8,128)(2,1)S(1)}, u32[]{:S(2)}, u32[]{:S(2)}) collective-permute-start(bf16[1,128,256]{2,1,0:T(8,128)(2,1)S(1)} %get-tuple-element.140), channel_id=1, source_target_pairs={{0,1},{1,0},{2,3},{3,2},{4,5},{5,4},{6,7},{7,6},{8,9},{9,8},{10,11... | collective-permute-start | bytes 196616 | tf_op jit(solution)/shard_map/ppermute | solution.py:137
  107.9 5.7 %collective-permute-start.34 = (bf16[1,128,256]{2,1,0:T(8,128)(2,1)S(1)}, bf16[1,128,256]{2,1,0:T(8,128)(2,1)S(1)}, u32[]{:S(2)}, u32[]{:S(2)}) collective-permute-start(bf16[1,128,256]{2,1,0:T(8,128)(2,1)S(1)} %get-tuple-element.139), channel_id=1, source_target_pairs={{1,2},{2,1},{3,4},{4,3},{5,6},{6,5},{9,10},{10,9},{11,12},{12,11},... | collective-permute-start | bytes 196616 | tf_op jit(solution)/shard_map/ppermute | solution.py:137

commit v12 on v7

--- a/solution.py
+++ b/solution.py
@@ -25,20 +25,41 @@
     odd[pl.ds(at, planes)] = jnp.concatenate([edge, field, edge], axis=1).astype(jnp.bfloat16)
 
 
-def convolve(taps, weights, width):
+def shifted(part, k, width):
+    planes, voxels, chans = part.shape
+    part = part.reshape(-1, width, chans)
+    column = lax.broadcasted_iota(jnp.int32, part.shape, 1)
+    if k == 0:
+        part = jnp.where(column == 0, 0.0, pltpu.roll(part, 1, 1))
+    elif k == 2:
+        part = jnp.where(column == width - 1, 0.0, pltpu.roll(part, width - 1, 1))
+    return part.reshape(planes, voxels, chans)
+
+
+def product(taps, weights, offsets, k):
     planes, voxels, chans = taps[0].shape
     slab = jnp.concatenate([part.reshape(planes * voxels, chans) for part in taps], axis=-1)
+    columns = jnp.concatenate([weights[(3 * n + k) * chans : (3 * n + k + 1) * chans] for n in offsets], axis=0)
+    part = jnp.dot(slab, columns, preferred_element_type=jnp.float32)
+    return part.reshape(planes, voxels, chans)
+
+
+def convolve(taps, weights, width):
+    return sum(shifted(product(taps, weights, range(9), k), k, width) for k in (1, 0, 2))
+
+
+def edges(sources, targets, weights, width):
     total = None
     for k in (1, 0, 2):
-        columns = jnp.concatenate([weights[(3 * n + k) * chans : (3 * n + k + 1) * chans] for n in range(9)], axis=0)
-        part = jnp.dot(slab, columns, preferred_element_type=jnp.float32).reshape(-1, width, chans)
-        column = lax.broadcasted_iota(jnp.int32, part.shape, 1)
-        if k == 0:
-            part = jnp.where(column == 0, 0.0, pltpu.roll(part, 1, 1))
-        elif k == 2:
-            part = jnp.where(column == width - 1, 0.0, pltpu.roll(part, width - 1, 1))
+        sums = [None] * 4
+        for i in range(3):
+            part = product(sources[i], weights, range(3 * i, 3 * i + 3), k)
+            for plane, target in enumerate(targets[i]):
+                piece = part[plane : plane + 1]
+                sums[target] = piece if sums[target] is None else sums[target] + piece
+        part = shifted(jnp.concatenate(sums, axis=0), k, width)
         total = part if total is None else total + part
-    return total.reshape(planes, voxels, chans)
+    return total
 
 
 def planes_at(even, odd, start, count, width):
@@ -49,40 +70,37 @@
     ]
 
 
-def inner_kernel(width, p, q, weights, even, odd, inner):
+def own_planes(width, p, q, weights, inner, partial, even, odd, ready=None):
     planes = q.shape[0]
     fill(even, odd, 0, q[...], width)
+    if ready is not None:
+        ready.wait()
     taps = [part for i in range(3) for part in planes_at(even, odd, i, planes - 2, width)]
     inner[...] = (p[1:-1].astype(jnp.float32) + convolve(taps, weights, width)).astype(inner.dtype)
-
-
-def loading_kernel(width, p, q, weights_hbm, even, odd, inner, weights, sem):
+    own = lambda plane: planes_at(even, odd, plane, 1, width)
+    pair = lambda one, other: [jnp.concatenate(both, axis=0) for both in zip(own(one), own(other))]
+    sources = (pair(planes - 2, planes - 1), pair(0, planes - 1), pair(0, 1))
+    partial[...] = edges(sources, ((2, 3), (1, 2), (0, 1)), weights, width)
+
+
+def inner_kernel(width, p, q, weights, inner, partial, even, odd):
+    own_planes(width, p, q, weights, inner, partial, even, odd)
+
+
+def loading_kernel(width, p, q, weights_hbm, inner, partial, weights, even, odd, sem):
     copy = pltpu.make_async_copy(weights_hbm, weights, sem)
     copy.start()
-    planes = q.shape[0]
-    fill(even, odd, 0, q[...], width)
-    taps = [part for i in range(3) for part in planes_at(even, odd, i, planes - 2, width)]
-    copy.wait()
-    inner[...] = (p[1:-1].astype(jnp.float32) + convolve(taps, weights, width)).astype(inner.dtype)
-
-
-def edge_kernel(
-    width, flags, p, even, odd, inner, q_near, q_far, p_near, p_far, weights, low, mid, high, edge_even, edge_odd
-):
+    own_planes(width, p, q, weights, inner, partial, even, odd, copy)
+
+
+def edge_kernel(width, flags, p, inner, partial, q_near, q_far, p_near, p_far, weights, low, mid, high, even, odd):
     planes = p.shape[0]
     above = flags[2] > 0
     near, far = q_near[:2].astype(jnp.float32), q_far[:2].astype(jnp.float32)
-    fill(edge_even, edge_odd, 0, jnp.where(above, far, near), width)
-    fill(edge_even, edge_odd, 2, jnp.where(above, near, far), width)
-    halo = lambda start, count: planes_at(edge_even, edge_odd, start, count, width)
-    own = lambda start, count: planes_at(even, odd, start, count, width)
-    sources = (
-        (halo(0, 2), own(planes - 2, 2)),
-        (halo(1, 1), own(0, 1), own(planes - 1, 1), halo(2, 1)),
-        (own(0, 2), halo(2, 2)),
-    )
-    taps = [jnp.concatenate(parts, axis=0) for source in sources for parts in zip(*source)]
-    total = convolve(taps, weights, width)
+    fill(even, odd, 0, jnp.where(above, far, near), width)
+    fill(even, odd, 2, jnp.where(above, near, far), width)
+    sources = [planes_at(even, odd, start, 2, width) for start in range(3)]
+    total = partial[...] + edges(sources, ((0, 1), (0, 3), (2, 3)), weights, width)
     near, far = p_near[-1:].astype(jnp.float32), p_far[-1:].astype(jnp.float32)
     low[...] = jnp.where(flags[0] > 0, jnp.where(above, far, near) + total[:1], 0.0).astype(low.dtype)
     mid[pl.ds(0, 1)] = (p[:1].astype(jnp.float32) + total[1:2]).astype(mid.dtype)
@@ -105,18 +123,17 @@
         out[...] = second
 
 
-def call(kernel, out_shape, scratch, arguments, width):
+def call(kernel, outputs, scratch, arguments, width):
     specs = [pl.BlockSpec(memory_space=pltpu.VMEM) for _ in arguments]
     if kernel is edge_kernel:
         specs[0] = pl.BlockSpec(memory_space=pltpu.SMEM)
     if kernel is loading_kernel:
         specs[-1] = pl.BlockSpec(memory_space=pltpu.HBM)
-    shapes = [jax.ShapeDtypeStruct(shape, jnp.bfloat16) for shape in out_shape]
     return pl.pallas_call(
         functools.partial(kernel, width),
-        out_shape=shapes,
+        out_shape=[jax.ShapeDtypeStruct(shape, dtype) for shape, dtype in outputs],
         in_specs=specs,
-        out_specs=[pl.BlockSpec(memory_space=pltpu.VMEM) for _ in shapes],
+        out_specs=[pl.BlockSpec(memory_space=pltpu.VMEM) for _ in outputs],
         scratch_shapes=[pltpu.VMEM(shape, jnp.bfloat16) if shape else pltpu.SemaphoreType.DMA for shape in scratch],
         compiler_params=pltpu.CompilerParams(vmem_limit_bytes=VMEM_LIMIT),
         cost_estimate=pl.CostEstimate(flops=1, bytes_accessed=1, transcendentals=0),
@@ -129,18 +146,20 @@
 
 def inner_half(p, q, weights, width, load):
     planes, voxels, chans = q.shape
-    shapes = [*stored(planes, voxels, chans, width), (planes - 2, voxels, chans)]
+    outputs = [((planes - 2, voxels, chans), jnp.bfloat16), ((4, voxels, chans), jnp.float32)]
+    scratch = stored(planes, voxels, chans, width)
     if load:
         weights = pltpu.with_memory_space_constraint(weights, pltpu.HBM)
-        return call(loading_kernel, shapes + [weights.shape], [()], (p, q, weights), width)
-    return *call(inner_kernel, shapes, [], (p, q, weights), width), weights
+        outputs.append((weights.shape, jnp.bfloat16))
+        return call(loading_kernel, outputs, [*scratch, ()], (p, q, weights), width)
+    return *call(inner_kernel, outputs, scratch, (p, q, weights), width), weights
 
 
 def first_half(flags, p, kept, q_halos, p_halos, weights, width):
     planes, voxels, chans = p.shape
     return call(
         edge_kernel,
-        [(1, voxels, chans), (planes, voxels, chans), (1, voxels, chans)],
+        [((n, voxels, chans), jnp.bfloat16) for n in (1, planes, 1)],
         stored(4, voxels, chans, width),
         (flags, p, *kept, *q_halos, *p_halos, weights),
         width,
@@ -151,7 +170,7 @@
     planes, voxels, chans = q.shape
     (out,) = call(
         second_kernel,
-        [(2, *q.shape) if both else q.shape],
+        [((2, *q.shape) if both else q.shape, jnp.bfloat16)],
         stored(planes + 2, voxels, chans, width),
         (*first, q, weights),
         width,

time: 114 us -> 111 us (0.974)
  waiting for transfers between devices: 24.9 us -> 20.7 us
    ppermute x13, waiting for transfers between devices: 10.5 us -> 5.55 us  [swap(): return lax.ppermute(jnp.concatenate(parts, axis=0), 'depth', pairs)]
  transfers between devices with their start and end apart: 28 -> 28, of which waited for: 13 -> 14; matrix products, arithmetic and copies ran while one was open for 2% -> 2% of each run, Pallas kernels for 24% -> 26%
where the time goes in v12:
time: 111 us; the launch traced here: 110 us
  starting transfers between devices  53.2 us (48%)
  Pallas kernels  33 us (30%)
  waiting for transfers between devices  20.7 us (19%)
  local copies, waits for them, and re-layouts  1.34 us (1%)
    ppermute x13, starting transfers between devices, swap(): return lax.ppermute(jnp.concatenate(parts, axis=0), 'depth', pairs)  33 us
    pallas_call x15, Pallas kernels, call(): pl.pallas_call(functools.partial(kernel, width), out_shape=[jax.ShapeDtyp...  33 us
    ppermute x15, starting transfers between devices, send(): return lax.ppermute(block, 'section', pairs) if pairs else block  20.2 us
    ppermute x15, waiting for transfers between devices, send(): return lax.ppermute(block, 'section', pairs) if pairs else block  15.2 us
    ppermute x13, waiting for transfers between devices, swap(): return lax.ppermute(jnp.concatenate(parts, axis=0), 'depth', pairs)  5.55 us
  transfers between devices with their start and end apart: 28, of which 14 were waited for; matrix products, arithmetic and copies ran while one was open for 2% of the time, Pallas kernels for 26%

profile of v12, /device:TPU:13, one launch (start us, length us, event | category | flops | bytes accessed | tf_op | source)
XLA Modules:
  0.0 110.0 jit_solution(18100412950090735852)
XLA Ops:
  0.1 1.3 %collective-permute-start.3 = (bf16[2,4,128,256]{3,2,1,0:T(8,128)(2,1)}, bf16[2,4,128,256]{3,2,1,0:T(8,128)(2,1)S(1)}, u32[]{:S(2)}, u32[]{:S(2)}) collective-permute-start(bf16[2,4,128,256]{3,2,1,0:T(8,128)(2,1)} %bitcast.63), channel_id=1, source_target_pairs={{0,24},{8,16},{1,25},{9,17},{2,26},{10,18},{3,27},{11,19},{4,28},{... | collective-permute-start | bytes 1572872 | tf_op jit(solution)/shard_map/ppermute | solution.py:221
  1.4 1.1 slice_bitcast_fusion.6
  2.5 0.7 collective-permute-start
  3.3 3.1 %collective-permute-start.1 = (bf16[3,128,256]{2,1,0:T(8,128)(2,1)S(1)}, bf16[3,128,256]{2,1,0:T(8,128)(2,1)S(1)}, u32[]{:S(2)}, u32[]{:S(2)}) collective-permute-start(bf16[3,128,256]{2,1,0:T(8,128)(2,1)S(1)} %pad_maximum_fusion.1), channel_id=1, source_target_pairs={{1,2},{2,1},{3,4},{4,3},{5,6},{6,5},{9,10},{10,9},{11,12},{12,11},... | collective-permute-start | bytes 589832 | tf_op jit(solution)/shard_map/ppermute | solution.py:185
  6.4 4.1 %shard_map.55 = (bf16[2,128,256]{2,1,0:T(8,128)(2,1)S(1)}, f32[4,128,256]{2,1,0:T(8,128)S(1)}, bf16[6912,256]{1,0:T(8,128)(2,1)S(1)}) custom-call(bf16[4,128,256]{2,1,0:T(8,128)(2,1)S(1)} %get-tuple-element.114.p, bf16[4,128,256]{2,1,0:T(8,128)(2,1)S(1)} %get-tuple-element.113.q, bf16[6912,256]{1,0:T(8,128)(2,1)} %bitcast.55), custom_call_target="tpu_custom_call" | custom-call | flops 1 | bytes 1 | tf_op jit(solution)/shard_map/pallas_call | solution.py:132
  10.6 1.8 %shard_map.56 = (bf16[1,128,256]{2,1,0:T(8,128)(2,1)S(1)}, bf16[4,128,256]{2,1,0:T(8,128)(2,1)S(1)}, bf16[1,128,256]{2,1,0:T(8,128)(2,1)S(1)}) custom-call(s32[3]{0:T(128)S(1)} %add_convert_fusion.6.flags, bf16[4,128,256]{2,1,0:T(8,128)(2,1)S(1)} %get-tuple-element.114.p, bf16[2,128,256]{2,1,0:T(8,128)(2,1)S(1)} %get-tuple-element.65.inner, ...), custom_call_target="tpu_custom_call" | custom-call | flops 1 | bytes 1 | tf_op jit(solution)/shard_map/pallas_call | solution.py:132
  12.4 0.7 collective-permute-start.2
  13.1 2.1 %shard_map.57 = bf16[4,128,256]{2,1,0:T(8,128)(2,1)S(1)} custom-call(bf16[1,128,256]{2,1,0:T(8,128)(2,1)S(1)} %get-tuple-element.74.first_low, bf16[4,128,256]{2,1,0:T(8,128)(2,1)S(1)} %get-tuple-element.72.first_mid, bf16[1,128,256]{2,1,0:T(8,128)(2,1)S(1)} %get-tuple-element.75.first_high, bf16[4,128,256]{2,1,0:T(8,128)(2,1)S(1)} %get-tuple-element.113.q, ...), custom_call_target="tpu_custom_call" | custom-call | flops 1 | bytes 1 | tf_op jit(solution)/shard_map/pallas_call | solution.py:132
  16.2 4.6 %collective-permute-start.5 = (bf16[3,128,256]{2,1,0:T(8,128)(2,1)S(1)}, bf16[3,128,256]{2,1,0:T(8,128)(2,1)S(1)}, u32[]{:S(2)}, u32[]{:S(2)}) collective-permute-start(bf16[3,128,256]{2,1,0:T(8,128)(2,1)S(1)} %pad_maximum_fusion.3), channel_id=1, source_target_pairs={{1,2},{2,1},{3,4},{4,3},{5,6},{6,5},{9,10},{10,9},{11,12},{12,11},... | collective-permute-start | bytes 589832 | tf_op jit(solution)/shard_map/ppermute | solution.py:185
  20.9 0.7 collective-permute-start.10
  21.6 0.7 collective-permute-start.7
  22.3 2.1 %shard_map.58 = (bf16[2,128,256]{2,1,0:T(8,128)(2,1)S(1)}, f32[4,128,256]{2,1,0:T(8,128)S(1)}) custom-call(bf16[4,128,256]{2,1,0:T(8,128)(2,1)S(1)} %get-tuple-element.112.p, bf16[4,128,256]{2,1,0:T(8,128)(2,1)S(1)} %get-tuple-element.111.q, bf16[6912,256]{1,0:T(8,128)(2,1)S(1)} %get-tuple-element.71.weights), custom_call_target="tpu_custom_call" | custom-call | flops 1 | bytes 1 | tf_op jit(solution)/shard_map/pallas_call | solution.py:132
  24.5 1.8 %shard_map.59 = (bf16[1,128,256]{2,1,0:T(8,128)(2,1)S(1)}, bf16[4,128,256]{2,1,0:T(8,128)(2,1)S(1)}, bf16[1,128,256]{2,1,0:T(8,128)(2,1)S(1)}) custom-call(s32[3]{0:T(128)S(1)} %add_convert_fusion.6.flags, bf16[4,128,256]{2,1,0:T(8,128)(2,1)S(1)} %get-tuple-element.112.p, bf16[2,128,256]{2,1,0:T(8,128)(2,1)S(1)} %get-tuple-element.78.inner, ...), custom_call_target="tpu_custom_call" | custom-call | flops 1 | bytes 1 | tf_op jit(solution)/shard_map/pallas_call | solution.py:132
  26.3 3.7 %collective-permute-start.6 = (bf16[4,128,256]{2,1,0:T(8,128)(2,1)S(1)}, bf16[4,128,256]{2,1,0:T(8,128)(2,1)S(1)}, u32[]{:S(2)}, u32[]{:S(2)}) collective-permute-start(bf16[4,128,256]{2,1,0:T(8,128)(2,1)S(1)} %get-tuple-element.80.first_mid), channel_id=1, source_target_pairs={{0,8},{8,16},{16,24},{1,9},{9,17},{17,25},{2,10},{10,18},{18,26},{... | collective-permute-start | bytes 786440 | tf_op jit(solution)/shard_map/ppermute | solution.py:221
  30.0 2.1 %shard_map.60 = bf16[4,128,256]{2,1,0:T(8,128)(2,1)S(1)} custom-call(bf16[1,128,256]{2,1,0:T(8,128)(2,1)S(1)} %get-tuple-element.82.first_low, bf16[4,128,256]{2,1,0:T(8,128)(2,1)S(1)} %get-tuple-element.80.first_mid, bf16[1,128,256]{2,1,0:T(8,128)(2,1)S(1)} %get-tuple-element.83.first_high, bf16[4,128,256]{2,1,0:T(8,128)(2,1)S(1)} %get-tuple-element.111.q, ...), custom_call_target="tpu_custom_call" | custom-call | flops 1 | bytes 1 | tf_op jit(solution)/shard_map/pallas_call | solution.py:132
  32.2 1.9 %collective-permute-start.9 = (bf16[4,128,256]{2,1,0:T(8,128)(2,1)S(1)}, bf16[4,128,256]{2,1,0:T(8,128)(2,1)S(1)}, u32[]{:S(2)}, u32[]{:S(2)}) collective-permute-start(bf16[4,128,256]{2,1,0:T(8,128)(2,1)S(1)} %shard_map.60), channel_id=1, source_target_pairs={{0,8},{8,16},{16,24},{1,9},{9,17},{17,25},{2,10},{10,18},{18,26},{... | collective-permute-start | bytes 786440 | tf_op jit(solution)/shard_map/ppermute | solution.py:221
  34.1 0.7 collective-permute-start.11
  34.8 4.0 %collective-permute-done.6 = bf16[4,128,256]{2,1,0:T(8,128)(2,1)S(1)} collective-permute-done((bf16[4,128,256]{2,1,0:T(8,128)(2,1)S(1)}, bf16[4,128,256]{2,1,0:T(8,128)(2,1)S(1)}, u32[]{:S(2)}, u32[]{:S(2)}) %collective-permute-start.6) | collective-permute-done | bytes 262176 | tf_op jit(solution)/shard_map/ppermute | solution.py:221
  38.9 5.1 %collective-permute-start.8 = (bf16[1,128,256]{2,1,0:T(8,128)(2,1)S(1)}, bf16[1,128,256]{2,1,0:T(8,128)(2,1)S(1)}, u32[]{:S(2)}, u32[]{:S(2)}) collective-permute-start(bf16[1,128,256]{2,1,0:T(8,128)(2,1)S(1)} %constant_dynamic-slice_fusion.11), channel_id=1, source_target_pairs={{1,2},{2,1},{3,4},{4,3},{5,6},{6,5},{9,10},{10,9},{11,12},{12,11},... | collective-permute-start | bytes 196616 | tf_op jit(solution)/shard_map/ppermute | solution.py:185
  44.4 1.7 %collective-permute-done.8.p_far = bf16[1,128,256]{2,1,0:T(8,128)(2,1)S(1)} collective-permute-done((bf16[1,128,256]{2,1,0:T(8,128)(2,1)S(1)}, bf16[1,128,256]{2,1,0:T(8,128)(2,1)S(1)}, u32[]{:S(2)}, u32[]{:S(2)}) %collective-permute-start.8) | collective-permute-done | bytes 65568 | tf_op jit(solution)/shard_map/ppermute | solution.py:185
  46.8 3.1 %collective-permute-start.13 = (bf16[2,128,256]{2,1,0:T(8,128)(2,1)S(1)}, bf16[2,128,256]{2,1,0:T(8,128)(2,1)S(1)}, u32[]{:S(2)}, u32[]{:S(2)}) collective-permute-start(bf16[2,128,256]{2,1,0:T(8,128)(2,1)S(1)} %get-tuple-element.119), channel_id=1, source_target_pairs={{1,2},{2,1},{3,4},{4,3},{5,6},{6,5},{9,10},{10,9},{11,12},{12,11},... | collective-permute-start | bytes 393224 | tf_op jit(solution)/shard_map/ppermute | solution.py:185
  49.9 0.9 collective-permute-start.15
  50.7 2.1 %shard_map.61 = (bf16[2,128,256]{2,1,0:T(8,128)(2,1)S(1)}, f32[4,128,256]{2,1,0:T(8,128)S(1)}) custom-call(bf16[4,128,256]{2,1,0:T(8,128)(2,1)S(1)} %fusion.17.p, bf16[4,128,256]{2,1,0:T(8,128)(2,1)S(1)} %fusion.16.q, bf16[6912,256]{1,0:T(8,128)(2,1)S(1)} %get-tuple-element.71.weights), custom_call_target="tpu_custom_call" | custom-call | flops 1 | bytes 1 | tf_op jit(solution)/shard_map/pallas_call | solution.py:132
  53.0 1.8 %shard_map.62 = (bf16[1,128,256]{2,1,0:T(8,128)(2,1)S(1)}, bf16[4,128,256]{2,1,0:T(8,128)(2,1)S(1)}, bf16[1,128,256]{2,1,0:T(8,128)(2,1)S(1)}) custom-call(s32[3]{0:T(128)S(1)} %add_convert_fusion.6.flags, bf16[4,128,256]{2,1,0:T(8,128)(2,1)S(1)} %fusion.17.p, bf16[2,128,256]{2,1,0:T(8,128)(2,1)S(1)} %get-tuple-element.87.inner, ...), custom_call_target="tpu_custom_call" | custom-call | flops 1 | bytes 1 | tf_op jit(solution)/shard_map/pallas_call | solution.py:132
  54.8 1.9 %collective-permute-start.14 = (bf16[4,128,256]{2,1,0:T(8,128)(2,1)S(1)}, bf16[4,128,256]{2,1,0:T(8,128)(2,1)S(1)}, u32[]{:S(2)}, u32[]{:S(2)}) collective-permute-start(bf16[4,128,256]{2,1,0:T(8,128)(2,1)S(1)} %get-tuple-element.90.first_mid), channel_id=1, source_target_pairs={{0,8},{8,16},{16,24},{1,9},{9,17},{17,25},{2,10},{10,18},{18,26},{... | collective-permute-start | bytes 786440 | tf_op jit(solution)/shard_map/ppermute | solution.py:221
  56.8 2.1 %shard_map.63 = bf16[4,128,256]{2,1,0:T(8,128)(2,1)S(1)} custom-call(bf16[1,128,256]{2,1,0:T(8,128)(2,1)S(1)} %get-tuple-element.91.first_low, bf16[4,128,256]{2,1,0:T(8,128)(2,1)S(1)} %get-tuple-element.90.first_mid, bf16[1,128,256]{2,1,0:T(8,128)(2,1)S(1)} %get-tuple-element.92.first_high, bf16[4,128,256]{2,1,0:T(8,128)(2,1)S(1)} %fusion.16.q, ...), custom_call_target="tpu_custom_call" | custom-call | flops 1 | bytes 1 | tf_op jit(solution)/shard_map/pallas_call | solution.py:132
  58.9 1.9 %collective-permute-start.17 = (bf16[4,128,256]{2,1,0:T(8,128)(2,1)S(1)}, bf16[4,128,256]{2,1,0:T(8,128)(2,1)S(1)}, u32[]{:S(2)}, u32[]{:S(2)}) collective-permute-start(bf16[4,128,256]{2,1,0:T(8,128)(2,1)S(1)} %shard_map.63), channel_id=1, source_target_pairs={{0,8},{8,16},{16,24},{1,9},{9,17},{17,25},{2,10},{10,18},{18,26},{... | collective-permute-start | bytes 786440 | tf_op jit(solution)/shard_map/ppermute | solution.py:221
  60.8 0.7 collective-permute-start.18
  61.5 4.0 %collective-permute-done.14 = bf16[4,128,256]{2,1,0:T(8,128)(2,1)S(1)} collective-permute-done((bf16[4,128,256]{2,1,0:T(8,128)(2,1)S(1)}, bf16[4,128,256]{2,1,0:T(8,128)(2,1)S(1)}, u32[]{:S(2)}, u32[]{:S(2)}) %collective-permute-start.14) | collective-permute-done | bytes 262176 | tf_op jit(solution)/shard_map/ppermute | solution.py:221
  65.6 4.3 %collective-permute-start.16 = (bf16[1,128,256]{2,1,0:T(8,128)(2,1)S(1)}, bf16[1,128,256]{2,1,0:T(8,128)(2,1)S(1)}, u32[]{:S(2)}, u32[]{:S(2)}) collective-permute-start(bf16[1,128,256]{2,1,0:T(8,128)(2,1)S(1)} %constant_dynamic-slice_fusion.7), channel_id=1, source_target_pairs={{1,2},{2,1},{3,4},{4,3},{5,6},{6,5},{9,10},{10,9},{11,12},{12,11},... | collective-permute-start | bytes 196616 | tf_op jit(solution)/shard_map/ppermute | solution.py:185
  70.0 1.1 %collective-permute-done.17 = bf16[4,128,256]{2,1,0:T(8,128)(2,1)S(1)} collective-permute-done((bf16[4,128,256]{2,1,0:T(8,128)(2,1)S(1)}, bf16[4,128,256]{2,1,0:T(8,128)(2,1)S(1)}, u32[]{:S(2)}, u32[]{:S(2)}) %collective-permute-start.17) | collective-permute-done | bytes 262176 | tf_op jit(solution)/shard_map/ppermute | solution.py:221
  71.1 1.0 collective-permute-done.16.p_far
  72.8 3.0 %collective-permute-start.20 = (bf16[2,128,256]{2,1,0:T(8,128)(2,1)S(1)}, bf16[2,128,256]{2,1,0:T(8,128)(2,1)S(1)}, u32[]{:S(2)}, u32[]{:S(2)}) collective-permute-start(bf16[2,128,256]{2,1,0:T(8,128)(2,1)S(1)} %get-tuple-element.117), channel_id=1, source_target_pairs={{1,2},{2,1},{3,4},{4,3},{5,6},{6,5},{9,10},{10,9},{11,12},{12,11},... | collective-permute-start | bytes 393224 | tf_op jit(solution)/shard_map/ppermute | solution.py:185
  76.5 2.1 %shard_map.64 = (bf16[2,128,256]{2,1,0:T(8,128)(2,1)S(1)}, f32[4,128,256]{2,1,0:T(8,128)S(1)}) custom-call(bf16[4,128,256]{2,1,0:T(8,128)(2,1)S(1)} %fusion.15.p, bf16[4,128,256]{2,1,0:T(8,128)(2,1)S(1)} %fusion.14.q, bf16[6912,256]{1,0:T(8,128)(2,1)S(1)} %get-tuple-element.71.weights), custom_call_target="tpu_custom_call" | custom-call | flops 1 | bytes 1 | tf_op jit(solution)/shard_map/pallas_call | solution.py:132
  79.1 1.8 %shard_map.65 = (bf16[1,128,256]{2,1,0:T(8,128)(2,1)S(1)}, bf16[4,128,256]{2,1,0:T(8,128)(2,1)S(1)}, bf16[1,128,256]{2,1,0:T(8,128)(2,1)S(1)}) custom-call(s32[3]{0:T(128)S(1)} %add_convert_fusion.6.flags, bf16[4,128,256]{2,1,0:T(8,128)(2,1)S(1)} %fusion.15.p, bf16[2,128,256]{2,1,0:T(8,128)(2,1)S(1)} %get-tuple-element.96.inner, ...), custom_call_target="tpu_custom_call" | custom-call | flops 1 | bytes 1 | tf_op jit(solution)/shard_map/pallas_call | solution.py:132
  80.9 1.9 %collective-permute-start.21 = (bf16[4,128,256]{2,1,0:T(8,128)(2,1)S(1)}, bf16[4,128,256]{2,1,0:T(8,128)(2,1)S(1)}, u32[]{:S(2)}, u32[]{:S(2)}) collective-permute-start(bf16[4,128,256]{2,1,0:T(8,128)(2,1)S(1)} %get-tuple-element.99.first_mid), channel_id=1, source_target_pairs={{8,16},{16,24},{9,17},{17,25},{10,18},{18,26},{11,19},{19,27},{12,... | collective-permute-start | bytes 786440 | tf_op jit(solution)/shard_map/ppermute | solution.py:221
  82.8 2.1 %shard_map.66 = bf16[4,128,256]{2,1,0:T(8,128)(2,1)S(1)} custom-call(bf16[1,128,256]{2,1,0:T(8,128)(2,1)S(1)} %get-tuple-element.100.first_low, bf16[4,128,256]{2,1,0:T(8,128)(2,1)S(1)} %get-tuple-element.99.first_mid, bf16[1,128,256]{2,1,0:T(8,128)(2,1)S(1)} %get-tuple-element.101.first_high, bf16[4,128,256]{2,1,0:T(8,128)(2,1)S(1)} %fusion.14.q, ...), custom_call_target="tpu_custom_call" | custom-call | flops 1 | bytes 1 | tf_op jit(solution)/shard_map/pallas_call | solution.py:132
  85.0 1.9 %collective-permute-start.24 = (bf16[4,128,256]{2,1,0:T(8,128)(2,1)S(1)}, bf16[4,128,256]{2,1,0:T(8,128)(2,1)S(1)}, u32[]{:S(2)}, u32[]{:S(2)}) collective-permute-start(bf16[4,128,256]{2,1,0:T(8,128)(2,1)S(1)} %shard_map.66), channel_id=1, source_target_pairs={{8,16},{16,24},{9,17},{17,25},{10,18},{18,26},{11,19},{19,27},{12,... | collective-permute-start | bytes 786440 | tf_op jit(solution)/shard_map/ppermute | solution.py:221
  86.9 0.7 collective-permute-start.25
  87.6 3.9 %collective-permute-done.21 = bf16[4,128,256]{2,1,0:T(8,128)(2,1)S(1)} collective-permute-done((bf16[4,128,256]{2,1,0:T(8,128)(2,1)S(1)}, bf16[4,128,256]{2,1,0:T(8,128)(2,1)S(1)}, u32[]{:S(2)}, u32[]{:S(2)}) %collective-permute-start.21) | collective-permute-done | bytes 262176 | tf_op jit(solution)/shard_map/ppermute | solution.py:221
  91.6 4.4 %collective-permute-start.23 = (bf16[1,128,256]{2,1,0:T(8,128)(2,1)S(1)}, bf16[1,128,256]{2,1,0:T(8,128)(2,1)S(1)}, u32[]{:S(2)}, u32[]{:S(2)}) collective-permute-start(bf16[1,128,256]{2,1,0:T(8,128)(2,1)S(1)} %constant_dynamic-slice_fusion.3), channel_id=1, source_target_pairs={{1,2},{2,1},{3,4},{4,3},{5,6},{6,5},{9,10},{10,9},{11,12},{12,11},... | collective-permute-start | bytes 196616 | tf_op jit(solution)/shard_map/ppermute | solution.py:185
  96.0 1.1 %collective-permute-done.24 = bf16[4,128,256]{2,1,0:T(8,128)(2,1)S(1)} collective-permute-done((bf16[4,128,256]{2,1,0:T(8,128)(2,1)S(1)}, bf16[4,128,256]{2,1,0:T(8,128)(2,1)S(1)}, u32[]{:S(2)}, u32[]{:S(2)}) %collective-permute-start.24) | collective-permute-done | bytes 262176 | tf_op jit(solution)/shard_map/ppermute | solution.py:221
  97.1 1.1 collective-permute-done.23.p_far
  99.0 3.1 %collective-permute-start.27 = (bf16[2,128,256]{2,1,0:T(8,128)(2,1)S(1)}, bf16[2,128,256]{2,1,0:T(8,128)(2,1)S(1)}, u32[]{:S(2)}, u32[]{:S(2)}) collective-permute-start(bf16[2,128,256]{2,1,0:T(8,128)(2,1)S(1)} %get-tuple-element.115), channel_id=1, source_target_pairs={{1,2},{2,1},{3,4},{4,3},{5,6},{6,5},{9,10},{10,9},{11,12},{12,11},... | collective-permute-start | bytes 393224 | tf_op jit(solution)/shard_map/ppermute | solution.py:185
  102.1 2.1 %shard_map.67 = (bf16[2,128,256]{2,1,0:T(8,128)(2,1)S(1)}, f32[4,128,256]{2,1,0:T(8,128)S(1)}) custom-call(bf16[4,128,256]{2,1,0:T(8,128)(2,1)S(1)} %fusion.13.p, bf16[4,128,256]{2,1,0:T(8,128)(2,1)S(1)} %fusion.12.q, bf16[6912,256]{1,0:T(8,128)(2,1)S(1)} %get-tuple-element.71.weights), custom_call_target="tpu_custom_call" | custom-call | flops 1 | bytes 1 | tf_op jit(solution)/shard_map/pallas_call | solution.py:132
  104.2 1.0 collective-permute-done.27.q_far
  105.2 1.8 %shard_map.68 = (bf16[1,128,256]{2,1,0:T(8,128)(2,1)S(1)}, bf16[4,128,256]{2,1,0:T(8,128)(2,1)S(1)}, bf16[1,128,256]{2,1,0:T(8,128)(2,1)S(1)}) custom-call(s32[3]{0:T(128)S(1)} %add_convert_fusion.6.flags, bf16[4,128,256]{2,1,0:T(8,128)(2,1)S(1)} %fusion.13.p, bf16[2,128,256]{2,1,0:T(8,128)(2,1)S(1)} %get-tuple-element.105.inner, ...), custom_call_target="tpu_custom_call" | custom-call | flops 1 | bytes 1 | tf_op jit(solution)/shard_map/pallas_call | solution.py:132
  107.0 2.9 %shard_map.69 = bf16[2,4,128,256]{3,2,1,0:T(8,128)(2,1)} custom-call(bf16[1,128,256]{2,1,0:T(8,128)(2,1)S(1)} %get-tuple-element.108.first_low, bf16[4,128,256]{2,1,0:T(8,128)(2,1)S(1)} %get-tuple-element.109.first_mid, bf16[1,128,256]{2,1,0:T(8,128)(2,1)S(1)} %get-tuple-element.110.first_high, bf16[4,128,256]{2,1,0:T(8,128)(2,1)S(1)} %fusion.12.q, ...), custom_call_target="tpu_custom_call" | custom-call | flops 1 | bytes 1 | tf_op jit(solution)/shard_map/pallas_call | solution.py:132
  (58 shorter events, 5.3 us)
Async XLA Ops:
  0.1 15.8 %collective-permute-start.3 = (bf16[2,4,128,256]{3,2,1,0:T(8,128)(2,1)}, bf16[2,4,128,256]{3,2,1,0:T(8,128)(2,1)S(1)}, u32[]{:S(2)}, u32[]{:S(2)}) collective-permute-start(bf16[2,4,128,256]{3,2,1,0:T(8,128)(2,1)} %bitcast.63), channel_id=1, source_target_pairs={{0,24},{8,16},{1,25},{9,17},{2,26},{10,18},{3,27},{11,19},{4,28},{... | collective-permute-start | bytes 1572872 | tf_op jit(solution)/shard_map/ppermute | solution.py:221
  2.5 7.9 %collective-permute-start = (bf16[3,128,256]{2,1,0:T(8,128)(2,1)S(1)}, bf16[3,128,256]{2,1,0:T(8,128)(2,1)S(1)}, u32[]{:S(2)}, u32[]{:S(2)}) collective-permute-start(bf16[3,128,256]{2,1,0:T(8,128)(2,1)S(1)} %pad_maximum_fusion), channel_id=1, source_target_pairs={{0,1},{1,0},{2,3},{3,2},{4,5},{5,4},{6,7},{7,6},{8,9},{9,8},{10,11... | collective-permute-start | bytes 589832 | tf_op jit(solution)/shard_map/ppermute | solution.py:185
  3.3 7.3 %collective-permute-start.1 = (bf16[3,128,256]{2,1,0:T(8,128)(2,1)S(1)}, bf16[3,128,256]{2,1,0:T(8,128)(2,1)S(1)}, u32[]{:S(2)}, u32[]{:S(2)}) collective-permute-start(bf16[3,128,256]{2,1,0:T(8,128)(2,1)S(1)} %pad_maximum_fusion.1), channel_id=1, source_target_pairs={{1,2},{2,1},{3,4},{4,3},{5,6},{6,5},{9,10},{10,9},{11,12},{12,11},... | collective-permute-start | bytes 589832 | tf_op jit(solution)/shard_map/ppermute | solution.py:185
  10.6 2.5 %copy-start = (bf16[1,3,3,3,256,256]{5,4,3,2,1,0:T(8,128)(2,1)S(1)}, bf16[1,3,3,3,256,256]{5,4,3,2,1,0:T(8,128)(2,1)}, u32[]{:S(2)}) copy-start(bf16[1,3,3,3,256,256]{5,4,3,2,1,0:T(8,128)(2,1)} %param.9) | copy-start | bytes 10616836
  12.4 9.3 %collective-permute-start.2 = (bf16[4,128,256]{2,1,0:T(8,128)(2,1)S(1)}, bf16[4,128,256]{2,1,0:T(8,128)(2,1)S(1)}, u32[]{:S(2)}, u32[]{:S(2)}) collective-permute-start(bf16[4,128,256]{2,1,0:T(8,128)(2,1)S(1)} %get-tuple-element.72.first_mid), channel_id=1, source_target_pairs={{0,8},{1,9},{2,10},{3,11},{4,12},{5,13},{6,14},{7,15}} | collective-permute-start | bytes 786440 | tf_op jit(solution)/shard_map/ppermute | solution.py:221
  13.1 2.8 %copy-start.1 = (bf16[3,2,4,16,8,256]{5,4,3,2,1,0:T(8,128)(2,1)S(1)}, bf16[3,2,4,16,8,256]{5,4,3,2,1,0:T(8,128)(2,1)}, u32[]{:S(2)}) copy-start(bf16[3,2,4,16,8,256]{5,4,3,2,1,0:T(8,128)(2,1)} %param.7) | copy-start | bytes 4718596
  13.1 2.8 %copy-start.2 = (bf16[1,2,4,16,8,256]{5,4,3,2,1,0:T(8,128)(2,1)S(1)}, bf16[1,2,4,16,8,256]{5,4,3,2,1,0:T(8,128)(2,1)}, u32[]{:S(2)}) copy-start(bf16[1,2,4,16,8,256]{5,4,3,2,1,0:T(8,128)(2,1)} %param.5) | copy-start | bytes 1572868
  16.2 8.3 %collective-permute-start.5 = (bf16[3,128,256]{2,1,0:T(8,128)(2,1)S(1)}, bf16[3,128,256]{2,1,0:T(8,128)(2,1)S(1)}, u32[]{:S(2)}, u32[]{:S(2)}) collective-permute-start(bf16[3,128,256]{2,1,0:T(8,128)(2,1)S(1)} %pad_maximum_fusion.3), channel_id=1, source_target_pairs={{1,2},{2,1},{3,4},{4,3},{5,6},{6,5},{9,10},{10,9},{11,12},{12,11},... | collective-permute-start | bytes 589832 | tf_op jit(solution)/shard_map/ppermute | solution.py:185
  20.9 3.6 %collective-permute-start.4 = (bf16[3,128,256]{2,1,0:T(8,128)(2,1)S(1)}, bf16[3,128,256]{2,1,0:T(8,128)(2,1)S(1)}, u32[]{:S(2)}, u32[]{:S(2)}) collective-permute-start(bf16[3,128,256]{2,1,0:T(8,128)(2,1)S(1)} %pad_maximum_fusion.2), channel_id=1, source_target_pairs={{0,1},{1,0},{2,3},{3,2},{4,5},{5,4},{6,7},{7,6},{8,9},{9,8},{10,11... | collective-permute-start | bytes 589832 | tf_op jit(solution)/shard_map/ppermute | solution.py:185
  20.9 13.1 %collective-permute-start.10 = (bf16[4,128,256]{2,1,0:T(8,128)(2,1)S(1)}, bf16[4,128,256]{2,1,0:T(8,128)(2,1)S(1)}, u32[]{:S(2)}, u32[]{:S(2)}) collective-permute-start(bf16[4,128,256]{2,1,0:T(8,128)(2,1)S(1)} %shard_map.57), channel_id=1, source_target_pairs={{0,8},{1,9},{2,10},{3,11},{4,12},{5,13},{6,14},{7,15}} | collective-permute-start | bytes 786440 | tf_op jit(solution)/shard_map/ppermute | solution.py:221
  21.6 13.1 %collective-permute-start.7 = (bf16[4,128,256]{2,1,0:T(8,128)(2,1)S(1)}, bf16[4,128,256]{2,1,0:T(8,128)(2,1)S(1)}, u32[]{:S(2)}, u32[]{:S(2)}) collective-permute-start(bf16[4,128,256]{2,1,0:T(8,128)(2,1)S(1)} %collective-permute-done.2), channel_id=1, source_target_pairs={{8,24},{9,25},{10,26},{11,27},{12,28},{13,29},{14,30},{15,31}} | collective-permute-start | bytes 786440 | tf_op jit(solution)/shard_map/ppermute | solution.py:221
  26.3 12.5 %collective-permute-start.6 = (bf16[4,128,256]{2,1,0:T(8,128)(2,1)S(1)}, bf16[4,128,256]{2,1,0:T(8,128)(2,1)S(1)}, u32[]{:S(2)}, u32[]{:S(2)}) collective-permute-start(bf16[4,128,256]{2,1,0:T(8,128)(2,1)S(1)} %get-tuple-element.80.first_mid), channel_id=1, source_target_pairs={{0,8},{8,16},{16,24},{1,9},{9,17},{17,25},{2,10},{10,18},{18,26},{... | collective-permute-start | bytes 786440 | tf_op jit(solution)/shard_map/ppermute | solution.py:221
  32.2 12.2 %collective-permute-start.9 = (bf16[4,128,256]{2,1,0:T(8,128)(2,1)S(1)}, bf16[4,128,256]{2,1,0:T(8,128)(2,1)S(1)}, u32[]{:S(2)}, u32[]{:S(2)}) collective-permute-start(bf16[4,128,256]{2,1,0:T(8,128)(2,1)S(1)} %shard_map.60), channel_id=1, source_target_pairs={{0,8},{8,16},{16,24},{1,9},{9,17},{17,25},{2,10},{10,18},{18,26},{... | collective-permute-start | bytes 786440 | tf_op jit(solution)/shard_map/ppermute | solution.py:221
  34.1 12.0 %collective-permute-start.11 = (bf16[4,128,256]{2,1,0:T(8,128)(2,1)S(1)}, bf16[4,128,256]{2,1,0:T(8,128)(2,1)S(1)}, u32[]{:S(2)}, u32[]{:S(2)}) collective-permute-start(bf16[4,128,256]{2,1,0:T(8,128)(2,1)S(1)} %collective-permute-done.10), channel_id=1, source_target_pairs={{8,24},{9,25},{10,26},{11,27},{12,28},{13,29},{14,30},{15,31}} | collective-permute-start | bytes 786440 | tf_op jit(solution)/shard_map/ppermute | solution.py:221
  38.9 7.2 %collective-permute-start.8 = (bf16[1,128,256]{2,1,0:T(8,128)(2,1)S(1)}, bf16[1,128,256]{2,1,0:T(8,128)(2,1)S(1)}, u32[]{:S(2)}, u32[]{:S(2)}) collective-permute-start(bf16[1,128,256]{2,1,0:T(8,128)(2,1)S(1)} %constant_dynamic-slice_fusion.11), channel_id=1, source_target_pairs={{1,2},{2,1},{3,4},{4,3},{5,6},{6,5},{9,10},{10,9},{11,12},{12,11},... | collective-permute-start | bytes 196616 | tf_op jit(solution)/shard_map/ppermute | solution.py:185
  46.3 6.7 %collective-permute-start.12 = (bf16[3,128,256]{2,1,0:T(8,128)(2,1)S(1)}, bf16[3,128,256]{2,1,0:T(8,128)(2,1)S(1)}, u32[]{:S(2)}, u32[]{:S(2)}) collective-permute-start(bf16[3,128,256]{2,1,0:T(8,128)(2,1)S(1)} %pad_maximum_fusion.4), channel_id=1, source_target_pairs={{0,1},{1,0},{2,3},{3,2},{4,5},{5,4},{6,7},{7,6},{8,9},{9,8},{10,11... | collective-permute-start | bytes 589832 | tf_op jit(solution)/shard_map/ppermute | solution.py:185
  46.8 6.3 %collective-permute-start.13 = (bf16[2,128,256]{2,1,0:T(8,128)(2,1)S(1)}, bf16[2,128,256]{2,1,0:T(8,128)(2,1)S(1)}, u32[]{:S(2)}, u32[]{:S(2)}) collective-permute-start(bf16[2,128,256]{2,1,0:T(8,128)(2,1)S(1)} %get-tuple-element.119), channel_id=1, source_target_pairs={{1,2},{2,1},{3,4},{4,3},{5,6},{6,5},{9,10},{10,9},{11,12},{12,11},... | collective-permute-start | bytes 393224 | tf_op jit(solution)/shard_map/ppermute | solution.py:185
  49.9 11.6 %collective-permute-start.15 = (bf16[4,128,256]{2,1,0:T(8,128)(2,1)S(1)}, bf16[4,128,256]{2,1,0:T(8,128)(2,1)S(1)}, u32[]{:S(2)}, u32[]{:S(2)}) collective-permute-start(bf16[4,128,256]{2,1,0:T(8,128)(2,1)S(1)} %collective-permute-done.6), channel_id=1, source_target_pairs={{8,24},{9,25},{10,26},{11,27},{12,28},{13,29},{14,30},{15,31}} | collective-permute-start | bytes 786440 | tf_op jit(solution)/shard_map/ppermute | solution.py:221
  54.8 10.7 %collective-permute-start.14 = (bf16[4,128,256]{2,1,0:T(8,128)(2,1)S(1)}, bf16[4,128,256]{2,1,0:T(8,128)(2,1)S(1)}, u32[]{:S(2)}, u32[]{:S(2)}) collective-permute-start(bf16[4,128,256]{2,1,0:T(8,128)(2,1)S(1)} %get-tuple-element.90.first_mid), channel_id=1, source_target_pairs={{0,8},{8,16},{16,24},{1,9},{9,17},{17,25},{2,10},{10,18},{18,26},{... | collective-permute-start | bytes 786440 | tf_op jit(solution)/shard_map/ppermute | solution.py:221
  58.9 12.2 %collective-permute-start.17 = (bf16[4,128,256]{2,1,0:T(8,128)(2,1)S(1)}, bf16[4,128,256]{2,1,0:T(8,128)(2,1)S(1)}, u32[]{:S(2)}, u32[]{:S(2)}) collective-permute-start(bf16[4,128,256]{2,1,0:T(8,128)(2,1)S(1)} %shard_map.63), channel_id=1, source_target_pairs={{0,8},{8,16},{16,24},{1,9},{9,17},{17,25},{2,10},{10,18},{18,26},{... | collective-permute-start | bytes 786440 | tf_op jit(solution)/shard_map/ppermute | solution.py:221
  60.8 11.4 %collective-permute-start.18 = (bf16[4,128,256]{2,1,0:T(8,128)(2,1)S(1)}, bf16[4,128,256]{2,1,0:T(8,128)(2,1)S(1)}, u32[]{:S(2)}, u32[]{:S(2)}) collective-permute-start(bf16[4,128,256]{2,1,0:T(8,128)(2,1)S(1)} %collective-permute-done.9), channel_id=1, source_target_pairs={{8,24},{9,25},{10,26},{11,27},{12,28},{13,29},{14,30},{15,31}} | collective-permute-start | bytes 786440 | tf_op jit(solution)/shard_map/ppermute | solution.py:221
  65.6 6.5 %collective-permute-start.16 = (bf16[1,128,256]{2,1,0:T(8,128)(2,1)S(1)}, bf16[1,128,256]{2,1,0:T(8,128)(2,1)S(1)}, u32[]{:S(2)}, u32[]{:S(2)}) collective-permute-start(bf16[1,128,256]{2,1,0:T(8,128)(2,1)S(1)} %constant_dynamic-slice_fusion.7), channel_id=1, source_target_pairs={{1,2},{2,1},{3,4},{4,3},{5,6},{6,5},{9,10},{10,9},{11,12},{12,11},... | collective-permute-start | bytes 196616 | tf_op jit(solution)/shard_map/ppermute | solution.py:185
  72.4 6.7 %collective-permute-start.19 = (bf16[3,128,256]{2,1,0:T(8,128)(2,1)S(1)}, bf16[3,128,256]{2,1,0:T(8,128)(2,1)S(1)}, u32[]{:S(2)}, u32[]{:S(2)}) collective-permute-start(bf16[3,128,256]{2,1,0:T(8,128)(2,1)S(1)} %pad_maximum_fusion.5), channel_id=1, source_target_pairs={{0,1},{1,0},{2,3},{3,2},{4,5},{5,4},{6,7},{7,6},{8,9},{9,8},{10,11... | collective-permute-start | bytes 589832 | tf_op jit(solution)/shard_map/ppermute | solution.py:185
  72.8 6.3 %collective-permute-start.20 = (bf16[2,128,256]{2,1,0:T(8,128)(2,1)S(1)}, bf16[2,128,256]{2,1,0:T(8,128)(2,1)S(1)}, u32[]{:S(2)}, u32[]{:S(2)}) collective-permute-start(bf16[2,128,256]{2,1,0:T(8,128)(2,1)S(1)} %get-tuple-element.117), channel_id=1, source_target_pairs={{1,2},{2,1},{3,4},{4,3},{5,6},{6,5},{9,10},{10,9},{11,12},{12,11},... | collective-permute-start | bytes 393224 | tf_op jit(solution)/shard_map/ppermute | solution.py:185
  75.9 11.7 %collective-permute-start.22 = (bf16[4,128,256]{2,1,0:T(8,128)(2,1)S(1)}, bf16[4,128,256]{2,1,0:T(8,128)(2,1)S(1)}, u32[]{:S(2)}, u32[]{:S(2)}) collective-permute-start(bf16[4,128,256]{2,1,0:T(8,128)(2,1)S(1)} %collective-permute-done.14), channel_id=1, source_target_pairs={{8,24},{9,25},{10,26},{11,27},{12,28},{13,29},{14,30},{15,31}} | collective-permute-start | bytes 786440 | tf_op jit(solution)/shard_map/ppermute | solution.py:221
  80.9 10.6 %collective-permute-start.21 = (bf16[4,128,256]{2,1,0:T(8,128)(2,1)S(1)}, bf16[4,128,256]{2,1,0:T(8,128)(2,1)S(1)}, u32[]{:S(2)}, u32[]{:S(2)}) collective-permute-start(bf16[4,128,256]{2,1,0:T(8,128)(2,1)S(1)} %get-tuple-element.99.first_mid), channel_id=1, source_target_pairs={{8,16},{16,24},{9,17},{17,25},{10,18},{18,26},{11,19},{19,27},{12,... | collective-permute-start | bytes 786440 | tf_op jit(solution)/shard_map/ppermute | solution.py:221
  85.0 12.1 %collective-permute-start.24 = (bf16[4,128,256]{2,1,0:T(8,128)(2,1)S(1)}, bf16[4,128,256]{2,1,0:T(8,128)(2,1)S(1)}, u32[]{:S(2)}, u32[]{:S(2)}) collective-permute-start(bf16[4,128,256]{2,1,0:T(8,128)(2,1)S(1)} %shard_map.66), channel_id=1, source_target_pairs={{8,16},{16,24},{9,17},{17,25},{10,18},{18,26},{11,19},{19,27},{12,... | collective-permute-start | bytes 786440 | tf_op jit(solution)/shard_map/ppermute | solution.py:221
  86.9 11.3 %collective-permute-start.25 = (bf16[4,128,256]{2,1,0:T(8,128)(2,1)S(1)}, bf16[4,128,256]{2,1,0:T(8,128)(2,1)S(1)}, u32[]{:S(2)}, u32[]{:S(2)}) collective-permute-start(bf16[4,128,256]{2,1,0:T(8,128)(2,1)S(1)} %collective-permute-done.17), channel_id=1, source_target_pairs={{8,24},{9,25},{10,26},{11,27},{12,28},{13,29},{14,30},{15,31}} | collective-permute-start | bytes 786440 | tf_op jit(solution)/shard_map/ppermute | solution.py:221
  91.6 6.6 %collective-permute-start.23 = (bf16[1,128,256]{2,1,0:T(8,128)(2,1)S(1)}, bf16[1,128,256]{2,1,0:T(8,128)(2,1)S(1)}, u32[]{:S(2)}, u32[]{:S(2)}) collective-permute-start(bf16[1,128,256]{2,1,0:T(8,128)(2,1)S(1)} %constant_dynamic-slice_fusion.3), channel_id=1, source_target_pairs={{1,2},{2,1},{3,4},{4,3},{5,6},{6,5},{9,10},{10,9},{11,12},{12,11},... | collective-permute-start | bytes 196616 | tf_op jit(solution)/shard_map/ppermute | solution.py:185
  98.4 6.8 %collective-permute-start.26 = (bf16[3,128,256]{2,1,0:T(8,128)(2,1)S(1)}, bf16[3,128,256]{2,1,0:T(8,128)(2,1)S(1)}, u32[]{:S(2)}, u32[]{:S(2)}) collective-permute-start(bf16[3,128,256]{2,1,0:T(8,128)(2,1)S(1)} %pad_maximum_fusion.6), channel_id=1, source_target_pairs={{0,1},{1,0},{2,3},{3,2},{4,5},{5,4},{6,7},{7,6},{8,9},{9,8},{10,11... | collective-permute-start | bytes 589832 | tf_op jit(solution)/shard_map/ppermute | solution.py:185
  99.0 6.3 %collective-permute-start.27 = (bf16[2,128,256]{2,1,0:T(8,128)(2,1)S(1)}, bf16[2,128,256]{2,1,0:T(8,128)(2,1)S(1)}, u32[]{:S(2)}, u32[]{:S(2)}) collective-permute-start(bf16[2,128,256]{2,1,0:T(8,128)(2,1)S(1)} %get-tuple-element.115), channel_id=1, source_target_pairs={{1,2},{2,1},{3,4},{4,3},{5,6},{6,5},{9,10},{10,9},{11,12},{12,11},... | collective-permute-start | bytes 393224 | tf_op jit(solution)/shard_map/ppermute | solution.py:185

commit v13 on v8

--- a/solution.py
+++ b/solution.py
@@ -25,20 +25,41 @@
     odd[pl.ds(at, planes)] = jnp.concatenate([edge, field, edge], axis=1).astype(jnp.bfloat16)
 
 
-def convolve(taps, weights, width):
+def shifted(part, k, width):
+    planes, voxels, chans = part.shape
+    part = part.reshape(-1, width, chans)
+    column = lax.broadcasted_iota(jnp.int32, part.shape, 1)
+    if k == 0:
+        part = jnp.where(column == 0, 0.0, pltpu.roll(part, 1, 1))
+    elif k == 2:
+        part = jnp.where(column == width - 1, 0.0, pltpu.roll(part, width - 1, 1))
+    return part.reshape(planes, voxels, chans)
+
+
+def product(taps, weights, offsets, k):
     planes, voxels, chans = taps[0].shape
     slab = jnp.concatenate([part.reshape(planes * voxels, chans) for part in taps], axis=-1)
+    columns = jnp.concatenate([weights[(3 * n + k) * chans : (3 * n + k + 1) * chans] for n in offsets], axis=0)
+    part = jnp.dot(slab, columns, preferred_element_type=jnp.float32)
+    return part.reshape(planes, voxels, chans)
+
+
+def convolve(taps, weights, width):
+    return sum(shifted(product(taps, weights, range(9), k), k, width) for k in (1, 0, 2))
+
+
+def ends(sources, weights, width):
     total = None
     for k in (1, 0, 2):
-        columns = jnp.concatenate([weights[(3 * n + k) * chans : (3 * n + k + 1) * chans] for n in range(9)], axis=0)
-        part = jnp.dot(slab, columns, preferred_element_type=jnp.float32).reshape(-1, width, chans)
-        column = lax.broadcasted_iota(jnp.int32, part.shape, 1)
-        if k == 0:
-            part = jnp.where(column == 0, 0.0, pltpu.roll(part, 1, 1))
-        elif k == 2:
-            part = jnp.where(column == width - 1, 0.0, pltpu.roll(part, width - 1, 1))
+        sums = [None, None]
+        for i, (taps, targets) in sources.items():
+            part = product(taps, weights, range(3 * i, 3 * i + 3), k)
+            for plane, target in enumerate(targets):
+                piece = part[plane : plane + 1]
+                sums[target] = piece if sums[target] is None else sums[target] + piece
+        part = shifted(jnp.concatenate(sums, axis=0), k, width)
         total = part if total is None else total + part
-    return total.reshape(planes, voxels, chans)
+    return total
 
 
 def planes_at(even, odd, start, count, width):
@@ -49,36 +70,46 @@
     ]
 
 
-def inner_kernel(width, field, weights, even, odd, total):
+def own_planes(width, field, weights, total, even, odd, ready=None):
     planes = field.shape[0]
     fill(even, odd, 0, field[...], width)
+    if ready is not None:
+        ready.wait()
     taps = [part for i in range(3) for part in planes_at(even, odd, i, planes - 2, width)]
-    total[...] = convolve(taps, weights, width)
-
-
-def loading_kernel(width, field, weights_hbm, even, odd, total, weights, sem):
+    total[pl.ds(1, planes - 2)] = convolve(taps, weights, width)
+    own = lambda plane: planes_at(even, odd, plane, 1, width)
+    both = [jnp.concatenate(pair, axis=0) for pair in zip(own(0), own(planes - 1))]
+    sources = {0: (own(planes - 2), (1,)), 1: (both, (0, 1)), 2: (own(1), (0,))}
+    partial = ends(sources, weights, width)
+    total[pl.ds(0, 1)] = partial[:1]
+    total[pl.ds(planes - 1, 1)] = partial[1:]
+
+
+def inner_kernel(width, field, weights, total, even, odd):
+    own_planes(width, field, weights, total, even, odd)
+
+
+def loading_kernel(width, field, weights_hbm, total, weights, even, odd, sem):
     copy = pltpu.make_async_copy(weights_hbm, weights, sem)
     copy.start()
-    planes = field.shape[0]
-    fill(even, odd, 0, field[...], width)
-    taps = [part for i in range(3) for part in planes_at(even, odd, i, planes - 2, width)]
-    copy.wait()
-    total[...] = convolve(taps, weights, width)
-
-
-def edge_kernel(width, flags, near, far, even, odd, inner, weights, *rest):
-    *added, out, edge_even, edge_odd = rest
-    planes = even.shape[0]
+    own_planes(width, field, weights, total, even, odd, copy)
+
+
+def edge_kernel(width, flags, near, far, own, weights, *rest):
+    *added, out, even, odd = rest
+    planes = own.shape[0]
     above = flags[0] > 0
     near, far = near[...].astype(jnp.float32), far[...].astype(jnp.float32)
-    fill(edge_even, edge_odd, 0, jnp.where(above, far, near), width)
-    fill(edge_even, edge_odd, 1, jnp.where(above, near, far), width)
-    halo = lambda plane: planes_at(edge_even, edge_odd, plane, 1, width)
-    own = lambda plane: planes_at(even, odd, plane, 1, width)
-    sources = ((halo(0), own(planes - 2)), (own(0), own(planes - 1)), (own(1), halo(1)))
-    taps = [jnp.concatenate(pair, axis=0) for source in sources for pair in zip(*source)]
-    total = convolve(taps, weights, width)
-    pieces = ((0, 1, total[:1]), (1, planes - 2, inner[...]), (planes - 1, 1, total[1:]))
+    fill(even, odd, 0, jnp.where(above, far, near), width)
+    fill(even, odd, 1, jnp.where(above, near, far), width)
+    halo = lambda plane: planes_at(even, odd, plane, 1, width)
+    total = ends({0: (halo(0), (0,)), 2: (halo(1), (1,))}, weights, width)
+    last = planes - 1
+    pieces = (
+        (0, 1, own[pl.ds(0, 1)] + total[:1]),
+        (1, planes - 2, own[pl.ds(1, planes - 2)]),
+        (last, 1, own[pl.ds(last, 1)] + total[1:]),
+    )
     for start, count, piece in pieces:
         where = pl.ds(start, count)
         if added:
@@ -113,20 +144,19 @@
 
 def inner_planes(field, weights, width, load=False):
     planes, voxels, chans = field.shape
-    outputs = [(shape, jnp.bfloat16) for shape in stored(planes, voxels, chans, width)]
-    outputs.append(((planes - 2, voxels, chans), jnp.float32))
+    outputs = [(field.shape, jnp.float32)]
+    scratch = stored(planes, voxels, chans, width)
     if load:
         weights = pltpu.with_memory_space_constraint(weights, pltpu.HBM)
         outputs.append((weights.shape, jnp.bfloat16))
-        return call(loading_kernel, outputs, [()], (field, weights), width)
-    return *call(inner_kernel, outputs, [], (field, weights), width), weights
-
-
-def all_planes(flags, near, far, kept, weights, added, width):
-    shape = kept[0].shape
-    _, voxels, chans = shape
-    output = ((2, *shape) if len(added) == 2 else shape, jnp.bfloat16 if added else jnp.float32)
-    arguments = (flags, near, far, *kept, weights, *added)
+        return call(loading_kernel, outputs, [*scratch, ()], (field, weights), width)
+    return *call(inner_kernel, outputs, scratch, (field, weights), width), weights
+
+
+def all_planes(flags, near, far, own, weights, added, width):
+    _, voxels, chans = own.shape
+    output = ((2, *own.shape) if len(added) == 2 else own.shape, jnp.bfloat16 if added else jnp.float32)
+    arguments = (flags, near, far, own, weights, *added)
     (out,) = call(edge_kernel, [output], stored(2, voxels, chans, width), arguments, width)
     return out
 
@@ -196,25 +226,23 @@
         if slot > 1:
             q = arrived(slot, 1)
             halos = swaps(q)
-        *kept, w_one = inner_planes(q, w_one, width, slot == 0)
-        first = all_planes(flags, *halos, kept, w_one, (p,) if slot < 2 else (), width)
+        own, w_one = inner_planes(q, w_one, width, slot == 0)
+        first = all_planes(flags, *halos, own, w_one, (p,) if slot < 2 else (), width)
         if slot > 1:
             p = arrived(slot, 0)
             first = (p.astype(jnp.float32) + first).astype(jnp.bfloat16)
         halos = swaps(first)
-        *kept, _ = inner_planes(first, w_two, width)
+        own, _ = inner_planes(first, w_two, width)
         if slot == 0:
             mirrored, _ = lax.optimization_barrier((mirrored, first))
             following = arrived(1, 0), arrived(1, 1)
             following += (swaps(following[1]),)
-        second = all_planes(flags, *halos, kept, w_two, (first, q) if slot == ticks else (q,), width)
+        second = all_planes(flags, *halos, own, w_two, (first, q) if slot == ticks else (q,), width)
         if slot == 0:
             p, q, halos = following
             halos, second = lax.optimization_barrier((halos, second))
         if slot < ticks:
-            onward = [(j, j + 1) for j in range(1, sections - 1)] if slot > 0 else []
-            if slot < ticks - 1:
-                onward = [(0, 1)] + onward
+            onward = [(j, j + 1) for j in range(sections - 1)] if slot > 0 else [(0, 1)]
             first, second = lax.optimization_barrier((first, second))
             received, relays = {1: send(second, onward), 0: send(first, onward)}, {}
             if slot > 0:

time: 118 us -> 116 us (0.983)
  waiting for transfers between devices: 20.8 us -> 17.5 us
    ppermute x20, waiting for transfers between devices: 8.41 us -> 5.11 us  [swap(): lax.ppermute(lax.dynamic_slice_in_dim(block, starts[turn], 1, axis=0), 'd...]
  transfers between devices with their start and end apart: 35 -> 35, of which waited for: 11 -> 11; matrix products, arithmetic and copies ran while one was open for 1% -> 2% of each run, Pallas kernels for 19% -> 21%
where the time goes in v13:
time: 116 us; the launch traced here: 115 us
  starting transfers between devices  67.1 us (58%)
  Pallas kernels  26.9 us (23%)
  waiting for transfers between devices  17.5 us (15%)
  local copies, waits for them, and re-layouts  1.27 us (1%)
    ppermute x20, starting transfers between devices, swap(): lax.ppermute(lax.dynamic_slice_in_dim(block, starts[turn], 1, axis=0), 'd...  40.4 us
    pallas_call x20, Pallas kernels, call(): pl.pallas_call(functools.partial(kernel, width), out_shape=[jax.ShapeDtyp...  26.9 us
    ppermute x15, starting transfers between devices, send(): return lax.ppermute(block, 'section', pairs) if pairs else block  26.8 us
    ppermute x15, waiting for transfers between devices, send(): return lax.ppermute(block, 'section', pairs) if pairs else block  12.4 us
    ppermute x20, waiting for transfers between devices, swap(): lax.ppermute(lax.dynamic_slice_in_dim(block, starts[turn], 1, axis=0), 'd...  5.11 us
  transfers between devices with their start and end apart: 35, of which 11 were waited for; matrix products, arithmetic and copies ran while one was open for 2% of the time, Pallas kernels for 21%

profile of v13, /device:TPU:13, one launch (start us, length us, event | category | flops | bytes accessed | tf_op | source)
XLA Modules:
  0.0 114.6 jit_solution(1354351221426266362)
XLA Ops:
  0.0 1.3 %collective-permute-start.2 = (bf16[2,4,128,256]{3,2,1,0:T(8,128)(2,1)}, bf16[2,4,128,256]{3,2,1,0:T(8,128)(2,1)S(1)}, u32[]{:S(2)}, u32[]{:S(2)}) collective-permute-start(bf16[2,4,128,256]{3,2,1,0:T(8,128)(2,1)} %bitcast.66), channel_id=1, source_target_pairs={{0,24},{8,16},{1,25},{9,17},{2,26},{10,18},{3,27},{11,19},{4,28},{... | collective-permute-start | bytes 1572872 | tf_op jit(solution)/shard_map/ppermute | solution.py:201
  1.3 1.1 slice_bitcast_fusion.6
  2.4 0.7 collective-permute-start
  3.1 3.1 %collective-permute-start.1 = (bf16[1,128,256]{2,1,0:T(8,128)(2,1)S(1)}, bf16[1,128,256]{2,1,0:T(8,128)(2,1)S(1)}, u32[]{:S(2)}, u32[]{:S(2)}) collective-permute-start(bf16[1,128,256]{2,1,0:T(8,128)(2,1)S(1)} %get-tuple-element.91), channel_id=1, source_target_pairs={{1,2},{2,1},{3,4},{4,3},{5,6},{6,5},{9,10},{10,9},{11,12},{12,11},... | collective-permute-start | bytes 196616 | tf_op jit(solution)/shard_map/ppermute | solution.py:167
  6.2 3.9 %shard_map.55 = (f32[4,128,256]{2,1,0:T(8,128)S(1)}, bf16[6912,256]{1,0:T(8,128)(2,1)S(1)}) custom-call(bf16[4,128,256]{2,1,0:T(8,128)(2,1)S(1)} %get-tuple-element.72.field.rest_0_, bf16[6912,256]{1,0:T(8,128)(2,1)} %bitcast.58), custom_call_target="tpu_custom_call" | custom-call | flops 1 | bytes 1 | tf_op jit(solution)/shard_map/pallas_call | solution.py:130
  10.9 3.6 %collective-permute-start.6 = (bf16[1,128,256]{2,1,0:T(8,128)(2,1)S(1)}, bf16[1,128,256]{2,1,0:T(8,128)(2,1)S(1)}, u32[]{:S(2)}, u32[]{:S(2)}) collective-permute-start(bf16[1,128,256]{2,1,0:T(8,128)(2,1)S(1)} %get-tuple-element.87), channel_id=1, source_target_pairs={{1,2},{2,1},{3,4},{4,3},{5,6},{6,5},{9,10},{10,9},{11,12},{12,11},... | collective-permute-start | bytes 196616 | tf_op jit(solution)/shard_map/ppermute | solution.py:167
  14.5 1.3 %collective-permute-done.2 = bf16[2,4,128,256]{3,2,1,0:T(8,128)(2,1)S(1)} collective-permute-done((bf16[2,4,128,256]{3,2,1,0:T(8,128)(2,1)}, bf16[2,4,128,256]{3,2,1,0:T(8,128)(2,1)S(1)}, u32[]{:S(2)}, u32[]{:S(2)}) %collective-permute-start.2) | collective-permute-done | bytes 524320 | tf_op jit(solution)/shard_map/ppermute | solution.py:201
  16.1 1.6 %collective-permute-start.3 = (bf16[1,128,256]{2,1,0:T(8,128)(2,1)S(1)}, bf16[1,128,256]{2,1,0:T(8,128)(2,1)S(1)}, u32[]{:S(2)}, u32[]{:S(2)}) collective-permute-start(bf16[1,128,256]{2,1,0:T(8,128)(2,1)S(1)} %get-tuple-element.90), channel_id=1, source_target_pairs={{0,1},{1,0},{2,3},{3,2},{4,5},{5,4},{6,7},{7,6},{8,9},{9,8},{10,11... | collective-permute-start | bytes 196616 | tf_op jit(solution)/shard_map/ppermute | solution.py:167
  17.7 3.1 %collective-permute-start.4 = (bf16[1,128,256]{2,1,0:T(8,128)(2,1)S(1)}, bf16[1,128,256]{2,1,0:T(8,128)(2,1)S(1)}, u32[]{:S(2)}, u32[]{:S(2)}) collective-permute-start(bf16[1,128,256]{2,1,0:T(8,128)(2,1)S(1)} %get-tuple-element.89), channel_id=1, source_target_pairs={{1,2},{2,1},{3,4},{4,3},{5,6},{6,5},{9,10},{10,9},{11,12},{12,11},... | collective-permute-start | bytes 196616 | tf_op jit(solution)/shard_map/ppermute | solution.py:167
  20.8 1.8 %shard_map.57.own = f32[4,128,256]{2,1,0:T(8,128)S(1)} custom-call(bf16[4,128,256]{2,1,0:T(8,128)(2,1)S(1)} %shard_map.56.field, bf16[6912,256]{1,0:T(8,128)(2,1)S(1)} %bitcast.48), custom_call_target="tpu_custom_call" | custom-call | flops 1 | bytes 1 | tf_op jit(solution)/shard_map/pallas_call | solution.py:130
  23.3 0.7 collective-permute-start.7
  24.0 0.7 collective-permute-start.11
  24.6 1.8 %shard_map.59.own = f32[4,128,256]{2,1,0:T(8,128)S(1)} custom-call(bf16[4,128,256]{2,1,0:T(8,128)(2,1)S(1)} %get-tuple-element.70.field.rest_0_, bf16[6912,256]{1,0:T(8,128)(2,1)S(1)} %get-tuple-element.47.weights), custom_call_target="tpu_custom_call" | custom-call | flops 1 | bytes 1 | tf_op jit(solution)/shard_map/pallas_call | solution.py:130
  27.2 3.6 %collective-permute-start.9 = (bf16[1,128,256]{2,1,0:T(8,128)(2,1)S(1)}, bf16[1,128,256]{2,1,0:T(8,128)(2,1)S(1)}, u32[]{:S(2)}, u32[]{:S(2)}) collective-permute-start(bf16[1,128,256]{2,1,0:T(8,128)(2,1)S(1)} %get-tuple-element.85), channel_id=1, source_target_pairs={{1,2},{2,1},{3,4},{4,3},{5,6},{6,5},{9,10},{10,9},{11,12},{12,11},... | collective-permute-start | bytes 196616 | tf_op jit(solution)/shard_map/ppermute | solution.py:167
  30.8 1.8 %shard_map.61.own = f32[4,128,256]{2,1,0:T(8,128)S(1)} custom-call(bf16[4,128,256]{2,1,0:T(8,128)(2,1)S(1)} %shard_map.60.field, bf16[6912,256]{1,0:T(8,128)(2,1)S(1)} %bitcast.50), custom_call_target="tpu_custom_call" | custom-call | flops 1 | bytes 1 | tf_op jit(solution)/shard_map/pallas_call | solution.py:130
  33.5 3.1 %collective-permute-start.13 = (bf16[4,128,256]{2,1,0:T(8,128)(2,1)S(1)}, bf16[4,128,256]{2,1,0:T(8,128)(2,1)S(1)}, u32[]{:S(2)}, u32[]{:S(2)}) collective-permute-start(bf16[4,128,256]{2,1,0:T(8,128)(2,1)S(1)} %shard_map.62), channel_id=1, source_target_pairs={{0,8},{8,16},{16,24},{1,9},{9,17},{17,25},{2,10},{10,18},{18,26},{... | collective-permute-start | bytes 786440 | tf_op jit(solution)/shard_map/ppermute | solution.py:201
  36.6 0.7 collective-permute-start.14
  37.3 1.9 %collective-permute-start.10 = (bf16[4,128,256]{2,1,0:T(8,128)(2,1)S(1)}, bf16[4,128,256]{2,1,0:T(8,128)(2,1)S(1)}, u32[]{:S(2)}, u32[]{:S(2)}) collective-permute-start(bf16[4,128,256]{2,1,0:T(8,128)(2,1)S(1)} %shard_map.60.field), channel_id=1, source_target_pairs={{0,8},{8,16},{16,24},{1,9},{9,17},{17,25},{2,10},{10,18},{18,26},{... | collective-permute-start | bytes 786440 | tf_op jit(solution)/shard_map/ppermute | solution.py:201
  39.2 0.7 collective-permute-start.12
  39.9 3.8 %collective-permute-done.13 = bf16[4,128,256]{2,1,0:T(8,128)(2,1)S(1)} collective-permute-done((bf16[4,128,256]{2,1,0:T(8,128)(2,1)S(1)}, bf16[4,128,256]{2,1,0:T(8,128)(2,1)S(1)}, u32[]{:S(2)}, u32[]{:S(2)}) %collective-permute-start.13) | collective-permute-done | bytes 262176 | tf_op jit(solution)/shard_map/ppermute | solution.py:201
  43.9 2.1 %collective-permute-start.15 = (bf16[1,128,256]{2,1,0:T(8,128)(2,1)S(1)}, bf16[1,128,256]{2,1,0:T(8,128)(2,1)S(1)}, u32[]{:S(2)}, u32[]{:S(2)}) collective-permute-start(bf16[1,128,256]{2,1,0:T(8,128)(2,1)S(1)} %get-tuple-element.84), channel_id=1, source_target_pairs={{0,1},{1,0},{2,3},{3,2},{4,5},{5,4},{6,7},{7,6},{8,9},{9,8},{10,11... | collective-permute-start | bytes 196616 | tf_op jit(solution)/shard_map/ppermute | solution.py:167
  46.0 3.3 %collective-permute-start.16 = (bf16[1,128,256]{2,1,0:T(8,128)(2,1)S(1)}, bf16[1,128,256]{2,1,0:T(8,128)(2,1)S(1)}, u32[]{:S(2)}, u32[]{:S(2)}) collective-permute-start(bf16[1,128,256]{2,1,0:T(8,128)(2,1)S(1)} %get-tuple-element.83), channel_id=1, source_target_pairs={{1,2},{2,1},{3,4},{4,3},{5,6},{6,5},{9,10},{10,9},{11,12},{12,11},... | collective-permute-start | bytes 196616 | tf_op jit(solution)/shard_map/ppermute | solution.py:167
  49.3 1.8 %shard_map.63.own = f32[4,128,256]{2,1,0:T(8,128)S(1)} custom-call(bf16[4,128,256]{2,1,0:T(8,128)(2,1)S(1)} %fusion.16.field.rest_0_, bf16[6912,256]{1,0:T(8,128)(2,1)S(1)} %get-tuple-element.47.weights), custom_call_target="tpu_custom_call" | custom-call | flops 1 | bytes 1 | tf_op jit(solution)/shard_map/pallas_call | solution.py:130
  52.5 3.6 %collective-permute-start.18 = (bf16[1,128,256]{2,1,0:T(8,128)(2,1)S(1)}, bf16[1,128,256]{2,1,0:T(8,128)(2,1)S(1)}, u32[]{:S(2)}, u32[]{:S(2)}) collective-permute-start(bf16[1,128,256]{2,1,0:T(8,128)(2,1)S(1)} %get-tuple-element.81), channel_id=1, source_target_pairs={{1,2},{2,1},{3,4},{4,3},{5,6},{6,5},{9,10},{10,9},{11,12},{12,11},... | collective-permute-start | bytes 196616 | tf_op jit(solution)/shard_map/ppermute | solution.py:167
  56.1 1.8 %shard_map.65.own = f32[4,128,256]{2,1,0:T(8,128)S(1)} custom-call(bf16[4,128,256]{2,1,0:T(8,128)(2,1)S(1)} %add_convert_fusion.6.field, bf16[6912,256]{1,0:T(8,128)(2,1)S(1)} %bitcast.52), custom_call_target="tpu_custom_call" | custom-call | flops 1 | bytes 1 | tf_op jit(solution)/shard_map/pallas_call | solution.py:130
  58.8 5.2 %collective-permute-start.21 = (bf16[4,128,256]{2,1,0:T(8,128)(2,1)S(1)}, bf16[4,128,256]{2,1,0:T(8,128)(2,1)S(1)}, u32[]{:S(2)}, u32[]{:S(2)}) collective-permute-start(bf16[4,128,256]{2,1,0:T(8,128)(2,1)S(1)} %shard_map.66), channel_id=1, source_target_pairs={{0,8},{8,16},{16,24},{1,9},{9,17},{17,25},{2,10},{10,18},{18,26},{... | collective-permute-start | bytes 786440 | tf_op jit(solution)/shard_map/ppermute | solution.py:201
  63.9 0.7 collective-permute-start.22
  64.6 1.9 %collective-permute-start.19 = (bf16[4,128,256]{2,1,0:T(8,128)(2,1)S(1)}, bf16[4,128,256]{2,1,0:T(8,128)(2,1)S(1)}, u32[]{:S(2)}, u32[]{:S(2)}) collective-permute-start(bf16[4,128,256]{2,1,0:T(8,128)(2,1)S(1)} %add_convert_fusion.6.field), channel_id=1, source_target_pairs={{0,8},{8,16},{16,24},{1,9},{9,17},{17,25},{2,10},{10,18},{18,26},{... | collective-permute-start | bytes 786440 | tf_op jit(solution)/shard_map/ppermute | solution.py:201
  66.6 0.7 collective-permute-start.20
  67.2 2.0 %collective-permute-done.21 = bf16[4,128,256]{2,1,0:T(8,128)(2,1)S(1)} collective-permute-done((bf16[4,128,256]{2,1,0:T(8,128)(2,1)S(1)}, bf16[4,128,256]{2,1,0:T(8,128)(2,1)S(1)}, u32[]{:S(2)}, u32[]{:S(2)}) %collective-permute-start.21) | collective-permute-done | bytes 262176 | tf_op jit(solution)/shard_map/ppermute | solution.py:201
  69.3 2.1 %collective-permute-start.23 = (bf16[1,128,256]{2,1,0:T(8,128)(2,1)S(1)}, bf16[1,128,256]{2,1,0:T(8,128)(2,1)S(1)}, u32[]{:S(2)}, u32[]{:S(2)}) collective-permute-start(bf16[1,128,256]{2,1,0:T(8,128)(2,1)S(1)} %get-tuple-element.80), channel_id=1, source_target_pairs={{0,1},{1,0},{2,3},{3,2},{4,5},{5,4},{6,7},{7,6},{8,9},{9,8},{10,11... | collective-permute-start | bytes 196616 | tf_op jit(solution)/shard_map/ppermute | solution.py:167
  71.5 2.8 %collective-permute-start.24 = (bf16[1,128,256]{2,1,0:T(8,128)(2,1)S(1)}, bf16[1,128,256]{2,1,0:T(8,128)(2,1)S(1)}, u32[]{:S(2)}, u32[]{:S(2)}) collective-permute-start(bf16[1,128,256]{2,1,0:T(8,128)(2,1)S(1)} %get-tuple-element.79), channel_id=1, source_target_pairs={{1,2},{2,1},{3,4},{4,3},{5,6},{6,5},{9,10},{10,9},{11,12},{12,11},... | collective-permute-start | bytes 196616 | tf_op jit(solution)/shard_map/ppermute | solution.py:167
  74.3 1.8 %shard_map.67.own = f32[4,128,256]{2,1,0:T(8,128)S(1)} custom-call(bf16[4,128,256]{2,1,0:T(8,128)(2,1)S(1)} %fusion.14.field.rest_0_, bf16[6912,256]{1,0:T(8,128)(2,1)S(1)} %get-tuple-element.47.weights), custom_call_target="tpu_custom_call" | custom-call | flops 1 | bytes 1 | tf_op jit(solution)/shard_map/pallas_call | solution.py:130
  76.1 0.9 collective-permute-done.24.far
  78.0 3.3 %collective-permute-start.26 = (bf16[1,128,256]{2,1,0:T(8,128)(2,1)S(1)}, bf16[1,128,256]{2,1,0:T(8,128)(2,1)S(1)}, u32[]{:S(2)}, u32[]{:S(2)}) collective-permute-start(bf16[1,128,256]{2,1,0:T(8,128)(2,1)S(1)} %get-tuple-element.77), channel_id=1, source_target_pairs={{1,2},{2,1},{3,4},{4,3},{5,6},{6,5},{9,10},{10,9},{11,12},{12,11},... | collective-permute-start | bytes 196616 | tf_op jit(solution)/shard_map/ppermute | solution.py:167
  81.3 1.8 %shard_map.69.own = f32[4,128,256]{2,1,0:T(8,128)S(1)} custom-call(bf16[4,128,256]{2,1,0:T(8,128)(2,1)S(1)} %add_convert_fusion.3.field, bf16[6912,256]{1,0:T(8,128)(2,1)S(1)} %bitcast.54), custom_call_target="tpu_custom_call" | custom-call | flops 1 | bytes 1 | tf_op jit(solution)/shard_map/pallas_call | solution.py:130
  84.2 0.7 collective-permute-start.30
  84.9 6.0 %collective-permute-start.29 = (bf16[4,128,256]{2,1,0:T(8,128)(2,1)S(1)}, bf16[4,128,256]{2,1,0:T(8,128)(2,1)S(1)}, u32[]{:S(2)}, u32[]{:S(2)}) collective-permute-start(bf16[4,128,256]{2,1,0:T(8,128)(2,1)S(1)} %shard_map.70), channel_id=1, source_target_pairs={{0,8},{8,16},{16,24},{1,9},{9,17},{17,25},{2,10},{10,18},{18,26},{... | collective-permute-start | bytes 786440 | tf_op jit(solution)/shard_map/ppermute | solution.py:201
  91.6 1.9 %collective-permute-start.27 = (bf16[4,128,256]{2,1,0:T(8,128)(2,1)S(1)}, bf16[4,128,256]{2,1,0:T(8,128)(2,1)S(1)}, u32[]{:S(2)}, u32[]{:S(2)}) collective-permute-start(bf16[4,128,256]{2,1,0:T(8,128)(2,1)S(1)} %add_convert_fusion.3.field), channel_id=1, source_target_pairs={{0,8},{8,16},{16,24},{1,9},{9,17},{17,25},{2,10},{10,18},{18,26},{... | collective-permute-start | bytes 786440 | tf_op jit(solution)/shard_map/ppermute | solution.py:201
  93.6 5.2 %collective-permute-done.29 = bf16[4,128,256]{2,1,0:T(8,128)(2,1)S(1)} collective-permute-done((bf16[4,128,256]{2,1,0:T(8,128)(2,1)S(1)}, bf16[4,128,256]{2,1,0:T(8,128)(2,1)S(1)}, u32[]{:S(2)}, u32[]{:S(2)}) %collective-permute-start.29) | collective-permute-done | bytes 262176 | tf_op jit(solution)/shard_map/ppermute | solution.py:201
  98.9 2.1 %collective-permute-start.31 = (bf16[1,128,256]{2,1,0:T(8,128)(2,1)S(1)}, bf16[1,128,256]{2,1,0:T(8,128)(2,1)S(1)}, u32[]{:S(2)}, u32[]{:S(2)}) collective-permute-start(bf16[1,128,256]{2,1,0:T(8,128)(2,1)S(1)} %get-tuple-element.76), channel_id=1, source_target_pairs={{0,1},{1,0},{2,3},{3,2},{4,5},{5,4},{6,7},{7,6},{8,9},{9,8},{10,11... | collective-permute-start | bytes 196616 | tf_op jit(solution)/shard_map/ppermute | solution.py:167
  101.0 2.3 %collective-permute-start.32 = (bf16[1,128,256]{2,1,0:T(8,128)(2,1)S(1)}, bf16[1,128,256]{2,1,0:T(8,128)(2,1)S(1)}, u32[]{:S(2)}, u32[]{:S(2)}) collective-permute-start(bf16[1,128,256]{2,1,0:T(8,128)(2,1)S(1)} %get-tuple-element.75), channel_id=1, source_target_pairs={{1,2},{2,1},{3,4},{4,3},{5,6},{6,5},{9,10},{10,9},{11,12},{12,11},... | collective-permute-start | bytes 196616 | tf_op jit(solution)/shard_map/ppermute | solution.py:167
  103.4 1.8 %shard_map.71.own = f32[4,128,256]{2,1,0:T(8,128)S(1)} custom-call(bf16[4,128,256]{2,1,0:T(8,128)(2,1)S(1)} %fusion.12.field.rest_1_, bf16[6912,256]{1,0:T(8,128)(2,1)S(1)} %get-tuple-element.47.weights), custom_call_target="tpu_custom_call" | custom-call | flops 1 | bytes 1 | tf_op jit(solution)/shard_map/pallas_call | solution.py:130
  105.2 1.4 %collective-permute-done.32.far = bf16[1,128,256]{2,1,0:T(8,128)(2,1)S(1)} collective-permute-done((bf16[1,128,256]{2,1,0:T(8,128)(2,1)S(1)}, bf16[1,128,256]{2,1,0:T(8,128)(2,1)S(1)}, u32[]{:S(2)}, u32[]{:S(2)}) %collective-permute-start.32) | collective-permute-done | bytes 65568 | tf_op jit(solution)/shard_map/ppermute | solution.py:167
  107.5 2.6 %collective-permute-start.34 = (bf16[1,128,256]{2,1,0:T(8,128)(2,1)S(1)}, bf16[1,128,256]{2,1,0:T(8,128)(2,1)S(1)}, u32[]{:S(2)}, u32[]{:S(2)}) collective-permute-start(bf16[1,128,256]{2,1,0:T(8,128)(2,1)S(1)} %get-tuple-element.73), channel_id=1, source_target_pairs={{1,2},{2,1},{3,4},{4,3},{5,6},{6,5},{9,10},{10,9},{11,12},{12,11},... | collective-permute-start | bytes 196616 | tf_op jit(solution)/shard_map/ppermute | solution.py:167
  110.1 1.8 %shard_map.73.own = f32[4,128,256]{2,1,0:T(8,128)S(1)} custom-call(bf16[4,128,256]{2,1,0:T(8,128)(2,1)S(1)} %add_convert_fusion.field.rest_0_, bf16[6912,256]{1,0:T(8,128)(2,1)S(1)} %bitcast.56), custom_call_target="tpu_custom_call" | custom-call | flops 1 | bytes 1 | tf_op jit(solution)/shard_map/pallas_call | solution.py:130
  111.9 1.3 %collective-permute-done.34.far = bf16[1,128,256]{2,1,0:T(8,128)(2,1)S(1)} collective-permute-done((bf16[1,128,256]{2,1,0:T(8,128)(2,1)S(1)}, bf16[1,128,256]{2,1,0:T(8,128)(2,1)S(1)}, u32[]{:S(2)}, u32[]{:S(2)}) %collective-permute-start.34) | collective-permute-done | bytes 65568 | tf_op jit(solution)/shard_map/ppermute | solution.py:167
  113.2 1.4 %shard_map.74 = bf16[2,4,128,256]{3,2,1,0:T(8,128)(2,1)} custom-call(s32[1]{0:T(128)} %bitcast.flags, bf16[1,128,256]{2,1,0:T(8,128)(2,1)S(1)} %collective-permute-done.33.near, bf16[1,128,256]{2,1,0:T(8,128)(2,1)S(1)} %collective-permute-done.34.far, f32[4,128,256]{2,1,0:T(8,128)S(1)} %shard_map.73.own, bf16[6912,256]{1,0:T(8,128)(2,1)S(1)} %bitcast.57, ...), custom_call_target="tpu_custom_call" | custom-call | flops 1 | bytes 1 | tf_op jit(solution)/shard_map/pallas_call | solution.py:130
  (66 shorter events, 9.4 us)
Async XLA Ops:
  0.0 15.8 %collective-permute-start.2 = (bf16[2,4,128,256]{3,2,1,0:T(8,128)(2,1)}, bf16[2,4,128,256]{3,2,1,0:T(8,128)(2,1)S(1)}, u32[]{:S(2)}, u32[]{:S(2)}) collective-permute-start(bf16[2,4,128,256]{3,2,1,0:T(8,128)(2,1)} %bitcast.66), channel_id=1, source_target_pairs={{0,24},{8,16},{1,25},{9,17},{2,26},{10,18},{3,27},{11,19},{4,28},{... | collective-permute-start | bytes 1572872 | tf_op jit(solution)/shard_map/ppermute | solution.py:201
  2.4 7.7 %collective-permute-start = (bf16[1,128,256]{2,1,0:T(8,128)(2,1)S(1)}, bf16[1,128,256]{2,1,0:T(8,128)(2,1)S(1)}, u32[]{:S(2)}, u32[]{:S(2)}) collective-permute-start(bf16[1,128,256]{2,1,0:T(8,128)(2,1)S(1)} %get-tuple-element.92), channel_id=1, source_target_pairs={{0,1},{1,0},{2,3},{3,2},{4,5},{5,4},{6,7},{7,6},{8,9},{9,8},{10,11... | collective-permute-start | bytes 196616 | tf_op jit(solution)/shard_map/ppermute | solution.py:167
  3.1 7.0 %collective-permute-start.1 = (bf16[1,128,256]{2,1,0:T(8,128)(2,1)S(1)}, bf16[1,128,256]{2,1,0:T(8,128)(2,1)S(1)}, u32[]{:S(2)}, u32[]{:S(2)}) collective-permute-start(bf16[1,128,256]{2,1,0:T(8,128)(2,1)S(1)} %get-tuple-element.91), channel_id=1, source_target_pairs={{1,2},{2,1},{3,4},{4,3},{5,6},{6,5},{9,10},{10,9},{11,12},{12,11},... | collective-permute-start | bytes 196616 | tf_op jit(solution)/shard_map/ppermute | solution.py:167
  6.2 9.5 %copy-start.1 = (bf16[3,2,4,16,8,256]{5,4,3,2,1,0:T(8,128)(2,1)S(1)}, bf16[3,2,4,16,8,256]{5,4,3,2,1,0:T(8,128)(2,1)}, u32[]{:S(2)}) copy-start(bf16[3,2,4,16,8,256]{5,4,3,2,1,0:T(8,128)(2,1)} %param.7) | copy-start | bytes 4718596
  10.1 5.7 %copy-start.2 = (bf16[1,2,4,16,8,256]{5,4,3,2,1,0:T(8,128)(2,1)S(1)}, bf16[1,2,4,16,8,256]{5,4,3,2,1,0:T(8,128)(2,1)}, u32[]{:S(2)}) copy-start(bf16[1,2,4,16,8,256]{5,4,3,2,1,0:T(8,128)(2,1)} %param.5) | copy-start | bytes 1572868
  10.2 10.6 %copy-start = (bf16[1,3,3,3,256,256]{5,4,3,2,1,0:T(8,128)(2,1)S(1)}, bf16[1,3,3,3,256,256]{5,4,3,2,1,0:T(8,128)(2,1)}, u32[]{:S(2)}) copy-start(bf16[1,3,3,3,256,256]{5,4,3,2,1,0:T(8,128)(2,1)} %param.9) | copy-start | bytes 10616836
  10.8 11.8 %collective-permute-start.5 = (bf16[1,128,256]{2,1,0:T(8,128)(2,1)S(1)}, bf16[1,128,256]{2,1,0:T(8,128)(2,1)S(1)}, u32[]{:S(2)}, u32[]{:S(2)}) collective-permute-start(bf16[1,128,256]{2,1,0:T(8,128)(2,1)S(1)} %get-tuple-element.88), channel_id=1, source_target_pairs={{0,1},{1,0},{2,3},{3,2},{4,5},{5,4},{6,7},{7,6},{8,9},{9,8},{10,11... | collective-permute-start | bytes 196616 | tf_op jit(solution)/shard_map/ppermute | solution.py:167
  10.9 11.7 %collective-permute-start.6 = (bf16[1,128,256]{2,1,0:T(8,128)(2,1)S(1)}, bf16[1,128,256]{2,1,0:T(8,128)(2,1)S(1)}, u32[]{:S(2)}, u32[]{:S(2)}) collective-permute-start(bf16[1,128,256]{2,1,0:T(8,128)(2,1)S(1)} %get-tuple-element.87), channel_id=1, source_target_pairs={{1,2},{2,1},{3,4},{4,3},{5,6},{6,5},{9,10},{10,9},{11,12},{12,11},... | collective-permute-start | bytes 196616 | tf_op jit(solution)/shard_map/ppermute | solution.py:167
  16.1 7.2 %collective-permute-start.3 = (bf16[1,128,256]{2,1,0:T(8,128)(2,1)S(1)}, bf16[1,128,256]{2,1,0:T(8,128)(2,1)S(1)}, u32[]{:S(2)}, u32[]{:S(2)}) collective-permute-start(bf16[1,128,256]{2,1,0:T(8,128)(2,1)S(1)} %get-tuple-element.90), channel_id=1, source_target_pairs={{0,1},{1,0},{2,3},{3,2},{4,5},{5,4},{6,7},{7,6},{8,9},{9,8},{10,11... | collective-permute-start | bytes 196616 | tf_op jit(solution)/shard_map/ppermute | solution.py:167
  17.7 5.6 %collective-permute-start.4 = (bf16[1,128,256]{2,1,0:T(8,128)(2,1)S(1)}, bf16[1,128,256]{2,1,0:T(8,128)(2,1)S(1)}, u32[]{:S(2)}, u32[]{:S(2)}) collective-permute-start(bf16[1,128,256]{2,1,0:T(8,128)(2,1)S(1)} %get-tuple-element.89), channel_id=1, source_target_pairs={{1,2},{2,1},{3,4},{4,3},{5,6},{6,5},{9,10},{10,9},{11,12},{12,11},... | collective-permute-start | bytes 196616 | tf_op jit(solution)/shard_map/ppermute | solution.py:167
  23.3 13.3 %collective-permute-start.7 = (bf16[4,128,256]{2,1,0:T(8,128)(2,1)S(1)}, bf16[4,128,256]{2,1,0:T(8,128)(2,1)S(1)}, u32[]{:S(2)}, u32[]{:S(2)}) collective-permute-start(bf16[4,128,256]{2,1,0:T(8,128)(2,1)S(1)} %shard_map.56.field), channel_id=1, source_target_pairs={{0,8},{1,9},{2,10},{3,11},{4,12},{5,13},{6,14},{7,15}} | collective-permute-start | bytes 786440 | tf_op jit(solution)/shard_map/ppermute | solution.py:201
  24.0 12.7 %collective-permute-start.11 = (bf16[4,128,256]{2,1,0:T(8,128)(2,1)S(1)}, bf16[4,128,256]{2,1,0:T(8,128)(2,1)S(1)}, u32[]{:S(2)}, u32[]{:S(2)}) collective-permute-start(bf16[4,128,256]{2,1,0:T(8,128)(2,1)S(1)} %shard_map.58), channel_id=1, source_target_pairs={{0,8},{1,9},{2,10},{3,11},{4,12},{5,13},{6,14},{7,15}} | collective-permute-start | bytes 786440 | tf_op jit(solution)/shard_map/ppermute | solution.py:201
  27.1 5.5 %collective-permute-start.8 = (bf16[1,128,256]{2,1,0:T(8,128)(2,1)S(1)}, bf16[1,128,256]{2,1,0:T(8,128)(2,1)S(1)}, u32[]{:S(2)}, u32[]{:S(2)}) collective-permute-start(bf16[1,128,256]{2,1,0:T(8,128)(2,1)S(1)} %get-tuple-element.86), channel_id=1, source_target_pairs={{0,1},{1,0},{2,3},{3,2},{4,5},{5,4},{6,7},{7,6},{8,9},{9,8},{10,11... | collective-permute-start | bytes 196616 | tf_op jit(solution)/shard_map/ppermute | solution.py:167
  27.2 5.7 %collective-permute-start.9 = (bf16[1,128,256]{2,1,0:T(8,128)(2,1)S(1)}, bf16[1,128,256]{2,1,0:T(8,128)(2,1)S(1)}, u32[]{:S(2)}, u32[]{:S(2)}) collective-permute-start(bf16[1,128,256]{2,1,0:T(8,128)(2,1)S(1)} %get-tuple-element.85), channel_id=1, source_target_pairs={{1,2},{2,1},{3,4},{4,3},{5,6},{6,5},{9,10},{10,9},{11,12},{12,11},... | collective-permute-start | bytes 196616 | tf_op jit(solution)/shard_map/ppermute | solution.py:167
  33.5 10.3 %collective-permute-start.13 = (bf16[4,128,256]{2,1,0:T(8,128)(2,1)S(1)}, bf16[4,128,256]{2,1,0:T(8,128)(2,1)S(1)}, u32[]{:S(2)}, u32[]{:S(2)}) collective-permute-start(bf16[4,128,256]{2,1,0:T(8,128)(2,1)S(1)} %shard_map.62), channel_id=1, source_target_pairs={{0,8},{8,16},{16,24},{1,9},{9,17},{17,25},{2,10},{10,18},{18,26},{... | collective-permute-start | bytes 786440 | tf_op jit(solution)/shard_map/ppermute | solution.py:201
  36.6 7.1 %collective-permute-start.14 = (bf16[4,128,256]{2,1,0:T(8,128)(2,1)S(1)}, bf16[4,128,256]{2,1,0:T(8,128)(2,1)S(1)}, u32[]{:S(2)}, u32[]{:S(2)}) collective-permute-start(bf16[4,128,256]{2,1,0:T(8,128)(2,1)S(1)} %collective-permute-done.11), channel_id=1, source_target_pairs={{8,24},{9,25},{10,26},{11,27},{12,28},{13,29},{14,30},{15,31}} | collective-permute-start | bytes 786440 | tf_op jit(solution)/shard_map/ppermute | solution.py:201
  37.3 14.9 %collective-permute-start.10 = (bf16[4,128,256]{2,1,0:T(8,128)(2,1)S(1)}, bf16[4,128,256]{2,1,0:T(8,128)(2,1)S(1)}, u32[]{:S(2)}, u32[]{:S(2)}) collective-permute-start(bf16[4,128,256]{2,1,0:T(8,128)(2,1)S(1)} %shard_map.60.field), channel_id=1, source_target_pairs={{0,8},{8,16},{16,24},{1,9},{9,17},{17,25},{2,10},{10,18},{18,26},{... | collective-permute-start | bytes 786440 | tf_op jit(solution)/shard_map/ppermute | solution.py:201
  39.2 12.9 %collective-permute-start.12 = (bf16[4,128,256]{2,1,0:T(8,128)(2,1)S(1)}, bf16[4,128,256]{2,1,0:T(8,128)(2,1)S(1)}, u32[]{:S(2)}, u32[]{:S(2)}) collective-permute-start(bf16[4,128,256]{2,1,0:T(8,128)(2,1)S(1)} %collective-permute-done.7), channel_id=1, source_target_pairs={{8,24},{9,25},{10,26},{11,27},{12,28},{13,29},{14,30},{15,31}} | collective-permute-start | bytes 786440 | tf_op jit(solution)/shard_map/ppermute | solution.py:201
  43.9 7.2 %collective-permute-start.15 = (bf16[1,128,256]{2,1,0:T(8,128)(2,1)S(1)}, bf16[1,128,256]{2,1,0:T(8,128)(2,1)S(1)}, u32[]{:S(2)}, u32[]{:S(2)}) collective-permute-start(bf16[1,128,256]{2,1,0:T(8,128)(2,1)S(1)} %get-tuple-element.84), channel_id=1, source_target_pairs={{0,1},{1,0},{2,3},{3,2},{4,5},{5,4},{6,7},{7,6},{8,9},{9,8},{10,11... | collective-permute-start | bytes 196616 | tf_op jit(solution)/shard_map/ppermute | solution.py:167
  46.0 5.6 %collective-permute-start.16 = (bf16[1,128,256]{2,1,0:T(8,128)(2,1)S(1)}, bf16[1,128,256]{2,1,0:T(8,128)(2,1)S(1)}, u32[]{:S(2)}, u32[]{:S(2)}) collective-permute-start(bf16[1,128,256]{2,1,0:T(8,128)(2,1)S(1)} %get-tuple-element.83), channel_id=1, source_target_pairs={{1,2},{2,1},{3,4},{4,3},{5,6},{6,5},{9,10},{10,9},{11,12},{12,11},... | collective-permute-start | bytes 196616 | tf_op jit(solution)/shard_map/ppermute | solution.py:167
  52.4 5.5 %collective-permute-start.17 = (bf16[1,128,256]{2,1,0:T(8,128)(2,1)S(1)}, bf16[1,128,256]{2,1,0:T(8,128)(2,1)S(1)}, u32[]{:S(2)}, u32[]{:S(2)}) collective-permute-start(bf16[1,128,256]{2,1,0:T(8,128)(2,1)S(1)} %get-tuple-element.82), channel_id=1, source_target_pairs={{0,1},{1,0},{2,3},{3,2},{4,5},{5,4},{6,7},{7,6},{8,9},{9,8},{10,11... | collective-permute-start | bytes 196616 | tf_op jit(solution)/shard_map/ppermute | solution.py:167
  52.5 5.7 %collective-permute-start.18 = (bf16[1,128,256]{2,1,0:T(8,128)(2,1)S(1)}, bf16[1,128,256]{2,1,0:T(8,128)(2,1)S(1)}, u32[]{:S(2)}, u32[]{:S(2)}) collective-permute-start(bf16[1,128,256]{2,1,0:T(8,128)(2,1)S(1)} %get-tuple-element.81), channel_id=1, source_target_pairs={{1,2},{2,1},{3,4},{4,3},{5,6},{6,5},{9,10},{10,9},{11,12},{12,11},... | collective-permute-start | bytes 196616 | tf_op jit(solution)/shard_map/ppermute | solution.py:167
  58.8 10.4 %collective-permute-start.21 = (bf16[4,128,256]{2,1,0:T(8,128)(2,1)S(1)}, bf16[4,128,256]{2,1,0:T(8,128)(2,1)S(1)}, u32[]{:S(2)}, u32[]{:S(2)}) collective-permute-start(bf16[4,128,256]{2,1,0:T(8,128)(2,1)S(1)} %shard_map.66), channel_id=1, source_target_pairs={{0,8},{8,16},{16,24},{1,9},{9,17},{17,25},{2,10},{10,18},{18,26},{... | collective-permute-start | bytes 786440 | tf_op jit(solution)/shard_map/ppermute | solution.py:201
  63.9 5.3 %collective-permute-start.22 = (bf16[4,128,256]{2,1,0:T(8,128)(2,1)S(1)}, bf16[4,128,256]{2,1,0:T(8,128)(2,1)S(1)}, u32[]{:S(2)}, u32[]{:S(2)}) collective-permute-start(bf16[4,128,256]{2,1,0:T(8,128)(2,1)S(1)} %collective-permute-done.13), channel_id=1, source_target_pairs={{8,24},{9,25},{10,26},{11,27},{12,28},{13,29},{14,30},{15,31}} | collective-permute-start | bytes 786440 | tf_op jit(solution)/shard_map/ppermute | solution.py:201
  64.6 13.0 %collective-permute-start.19 = (bf16[4,128,256]{2,1,0:T(8,128)(2,1)S(1)}, bf16[4,128,256]{2,1,0:T(8,128)(2,1)S(1)}, u32[]{:S(2)}, u32[]{:S(2)}) collective-permute-start(bf16[4,128,256]{2,1,0:T(8,128)(2,1)S(1)} %add_convert_fusion.6.field), channel_id=1, source_target_pairs={{0,8},{8,16},{16,24},{1,9},{9,17},{17,25},{2,10},{10,18},{18,26},{... | collective-permute-start | bytes 786440 | tf_op jit(solution)/shard_map/ppermute | solution.py:201
  66.6 11.1 %collective-permute-start.20 = (bf16[4,128,256]{2,1,0:T(8,128)(2,1)S(1)}, bf16[4,128,256]{2,1,0:T(8,128)(2,1)S(1)}, u32[]{:S(2)}, u32[]{:S(2)}) collective-permute-start(bf16[4,128,256]{2,1,0:T(8,128)(2,1)S(1)} %collective-permute-done.10), channel_id=1, source_target_pairs={{8,24},{9,25},{10,26},{11,27},{12,28},{13,29},{14,30},{15,31}} | collective-permute-start | bytes 786440 | tf_op jit(solution)/shard_map/ppermute | solution.py:201
  69.3 6.8 %collective-permute-start.23 = (bf16[1,128,256]{2,1,0:T(8,128)(2,1)S(1)}, bf16[1,128,256]{2,1,0:T(8,128)(2,1)S(1)}, u32[]{:S(2)}, u32[]{:S(2)}) collective-permute-start(bf16[1,128,256]{2,1,0:T(8,128)(2,1)S(1)} %get-tuple-element.80), channel_id=1, source_target_pairs={{0,1},{1,0},{2,3},{3,2},{4,5},{5,4},{6,7},{7,6},{8,9},{9,8},{10,11... | collective-permute-start | bytes 196616 | tf_op jit(solution)/shard_map/ppermute | solution.py:167
  71.5 5.6 %collective-permute-start.24 = (bf16[1,128,256]{2,1,0:T(8,128)(2,1)S(1)}, bf16[1,128,256]{2,1,0:T(8,128)(2,1)S(1)}, u32[]{:S(2)}, u32[]{:S(2)}) collective-permute-start(bf16[1,128,256]{2,1,0:T(8,128)(2,1)S(1)} %get-tuple-element.79), channel_id=1, source_target_pairs={{1,2},{2,1},{3,4},{4,3},{5,6},{6,5},{9,10},{10,9},{11,12},{12,11},... | collective-permute-start | bytes 196616 | tf_op jit(solution)/shard_map/ppermute | solution.py:167
  77.9 5.2 %collective-permute-start.25 = (bf16[1,128,256]{2,1,0:T(8,128)(2,1)S(1)}, bf16[1,128,256]{2,1,0:T(8,128)(2,1)S(1)}, u32[]{:S(2)}, u32[]{:S(2)}) collective-permute-start(bf16[1,128,256]{2,1,0:T(8,128)(2,1)S(1)} %get-tuple-element.78), channel_id=1, source_target_pairs={{0,1},{1,0},{2,3},{3,2},{4,5},{5,4},{6,7},{7,6},{8,9},{9,8},{10,11... | collective-permute-start | bytes 196616 | tf_op jit(solution)/shard_map/ppermute | solution.py:167
  78.0 5.7 %collective-permute-start.26 = (bf16[1,128,256]{2,1,0:T(8,128)(2,1)S(1)}, bf16[1,128,256]{2,1,0:T(8,128)(2,1)S(1)}, u32[]{:S(2)}, u32[]{:S(2)}) collective-permute-start(bf16[1,128,256]{2,1,0:T(8,128)(2,1)S(1)} %get-tuple-element.77), channel_id=1, source_target_pairs={{1,2},{2,1},{3,4},{4,3},{5,6},{6,5},{9,10},{10,9},{11,12},{12,11},... | collective-permute-start | bytes 196616 | tf_op jit(solution)/shard_map/ppermute | solution.py:167
  84.2 9.3 %collective-permute-start.30 = (bf16[4,128,256]{2,1,0:T(8,128)(2,1)S(1)}, bf16[4,128,256]{2,1,0:T(8,128)(2,1)S(1)}, u32[]{:S(2)}, u32[]{:S(2)}) collective-permute-start(bf16[4,128,256]{2,1,0:T(8,128)(2,1)S(1)} %collective-permute-done.21), channel_id=1, source_target_pairs={{8,24},{9,25},{10,26},{11,27},{12,28},{13,29},{14,30},{15,31}} | collective-permute-start | bytes 786440 | tf_op jit(solution)/shard_map/ppermute | solution.py:201
  84.9 13.9 %collective-permute-start.29 = (bf16[4,128,256]{2,1,0:T(8,128)(2,1)S(1)}, bf16[4,128,256]{2,1,0:T(8,128)(2,1)S(1)}, u32[]{:S(2)}, u32[]{:S(2)}) collective-permute-start(bf16[4,128,256]{2,1,0:T(8,128)(2,1)S(1)} %shard_map.70), channel_id=1, source_target_pairs={{0,8},{8,16},{16,24},{1,9},{9,17},{17,25},{2,10},{10,18},{18,26},{... | collective-permute-start | bytes 786440 | tf_op jit(solution)/shard_map/ppermute | solution.py:201
  91.0 16.2 %collective-permute-start.28 = (bf16[4,128,256]{2,1,0:T(8,128)(2,1)S(1)}, bf16[4,128,256]{2,1,0:T(8,128)(2,1)S(1)}, u32[]{:S(2)}, u32[]{:S(2)}) collective-permute-start(bf16[4,128,256]{2,1,0:T(8,128)(2,1)S(1)} %collective-permute-done.19), channel_id=1, source_target_pairs={{8,24},{9,25},{10,26},{11,27},{12,28},{13,29},{14,30},{15,31}} | collective-permute-start | bytes 786440 | tf_op jit(solution)/shard_map/ppermute | solution.py:201
  91.6 15.6 %collective-permute-start.27 = (bf16[4,128,256]{2,1,0:T(8,128)(2,1)S(1)}, bf16[4,128,256]{2,1,0:T(8,128)(2,1)S(1)}, u32[]{:S(2)}, u32[]{:S(2)}) collective-permute-start(bf16[4,128,256]{2,1,0:T(8,128)(2,1)S(1)} %add_convert_fusion.3.field), channel_id=1, source_target_pairs={{0,8},{8,16},{16,24},{1,9},{9,17},{17,25},{2,10},{10,18},{18,26},{... | collective-permute-start | bytes 786440 | tf_op jit(solution)/shard_map/ppermute | solution.py:201
  98.9 6.3 %collective-permute-start.31 = (bf16[1,128,256]{2,1,0:T(8,128)(2,1)S(1)}, bf16[1,128,256]{2,1,0:T(8,128)(2,1)S(1)}, u32[]{:S(2)}, u32[]{:S(2)}) collective-permute-start(bf16[1,128,256]{2,1,0:T(8,128)(2,1)S(1)} %get-tuple-element.76), channel_id=1, source_target_pairs={{0,1},{1,0},{2,3},{3,2},{4,5},{5,4},{6,7},{7,6},{8,9},{9,8},{10,11... | collective-permute-start | bytes 196616 | tf_op jit(solution)/shard_map/ppermute | solution.py:167
  101.0 5.6 %collective-permute-start.32 = (bf16[1,128,256]{2,1,0:T(8,128)(2,1)S(1)}, bf16[1,128,256]{2,1,0:T(8,128)(2,1)S(1)}, u32[]{:S(2)}, u32[]{:S(2)}) collective-permute-start(bf16[1,128,256]{2,1,0:T(8,128)(2,1)S(1)} %get-tuple-element.75), channel_id=1, source_target_pairs={{1,2},{2,1},{3,4},{4,3},{5,6},{6,5},{9,10},{10,9},{11,12},{12,11},... | collective-permute-start | bytes 196616 | tf_op jit(solution)/shard_map/ppermute | solution.py:167
  107.4 4.5 %collective-permute-start.33 = (bf16[1,128,256]{2,1,0:T(8,128)(2,1)S(1)}, bf16[1,128,256]{2,1,0:T(8,128)(2,1)S(1)}, u32[]{:S(2)}, u32[]{:S(2)}) collective-permute-start(bf16[1,128,256]{2,1,0:T(8,128)(2,1)S(1)} %get-tuple-element.74), channel_id=1, source_target_pairs={{0,1},{1,0},{2,3},{3,2},{4,5},{5,4},{6,7},{7,6},{8,9},{9,8},{10,11... | collective-permute-start | bytes 196616 | tf_op jit(solution)/shard_map/ppermute | solution.py:167
  107.5 5.7 %collective-permute-start.34 = (bf16[1,128,256]{2,1,0:T(8,128)(2,1)S(1)}, bf16[1,128,256]{2,1,0:T(8,128)(2,1)S(1)}, u32[]{:S(2)}, u32[]{:S(2)}) collective-permute-start(bf16[1,128,256]{2,1,0:T(8,128)(2,1)S(1)} %get-tuple-element.73), channel_id=1, source_target_pairs={{1,2},{2,1},{3,4},{4,3},{5,6},{6,5},{9,10},{10,9},{11,12},{12,11},... | collective-permute-start | bytes 196616 | tf_op jit(solution)/shard_map/ppermute | solution.py:167

commit v14 on v13

--- a/solution.py
+++ b/solution.py
@@ -225,6 +225,8 @@
     for slot in range(ticks + 1):
         if slot > 1:
             q = arrived(slot, 1)
+            if slot > 2:
+                q, relayed[0] = lax.optimization_barrier((q, relayed[0]))
             halos = swaps(q)
         own, w_one = inner_planes(q, w_one, width, slot == 0)
         first = all_planes(flags, *halos, own, w_one, (p,) if slot < 2 else (), width)
@@ -243,13 +245,22 @@
             halos, second = lax.optimization_barrier((halos, second))
         if slot < ticks:
             onward = [(j, j + 1) for j in range(sections - 1)] if slot > 0 else [(0, 1)]
-            first, second = lax.optimization_barrier((first, second))
-            received, relays = {1: send(second, onward), 0: send(first, onward)}, {}
+            relays = {}
             if slot > 0:
-                held, _ = lax.optimization_barrier((newer, second))
+                held = newer
+                if slot == 1:
+                    held, _ = lax.optimization_barrier((held, second))
                 relays = {k: send(held[k], [(1, sections - 1)]) for k in (1, 0)}
+                if slot > 1:
+                    relays[1], second = lax.optimization_barrier((relays[1], second))
                 if across:
                     direct = {0: send(first, across), 1: send(second, across)}
+            received = {1: send(second, onward)}
+            if slot > 0:
+                first, received[1] = lax.optimization_barrier((first, received[1]))
+            else:
+                first, _ = lax.optimization_barrier((first, second))
+            received[0] = send(first, onward)
             older, newer, relayed = newer, received, relays
     result = second
     return result.reshape(1, 2, planes, rows, width, chans)

time: 116 us -> 121 us (1.043)
  waiting for transfers between devices: 17.5 us -> 25.9 us
  starting transfers between devices: 67.1 us -> 64 us
    ppermute x15, waiting for transfers between devices: 12.4 us -> 23.7 us  [send(): return lax.ppermute(block, 'section', pairs) if pairs else block]
    ppermute x15, starting transfers between devices: 26.8 us -> 20.3 us  [send(): return lax.ppermute(block, 'section', pairs) if pairs else block]
    ppermute x20, starting transfers between devices: 40.4 us -> 43.6 us  [swap(): lax.ppermute(lax.dynamic_slice_in_dim(block, starts[turn], 1, axis=0), 'd...]
    ppermute x20, waiting for transfers between devices: 5.11 us -> 2.24 us  [swap(): lax.ppermute(lax.dynamic_slice_in_dim(block, starts[turn], 1, axis=0), 'd...]
  transfers between devices with their start and end apart: 35 -> 35, of which waited for: 11 -> 13; matrix products, arithmetic and copies ran while one was open for 2% -> 2% of each run, Pallas kernels for 21% -> 21%
where the time goes in v14:
time: 121 us; the launch traced here: 120 us
  starting transfers between devices  64 us (53%)
  Pallas kernels  26.9 us (22%)
  waiting for transfers between devices  25.9 us (21%)
  local copies, waits for them, and re-layouts  1.27 us (1%)
    ppermute x20, starting transfers between devices, swap(): lax.ppermute(lax.dynamic_slice_in_dim(block, starts[turn], 1, axis=0), 'd...  43.6 us
    pallas_call x20, Pallas kernels, call(): pl.pallas_call(functools.partial(kernel, width), out_shape=[jax.ShapeDtyp...  26.9 us
    ppermute x15, waiting for transfers between devices, send(): return lax.ppermute(block, 'section', pairs) if pairs else block  23.7 us
    ppermute x15, starting transfers between devices, send(): return lax.ppermute(block, 'section', pairs) if pairs else block  20.3 us
  transfers between devices with their start and end apart: 35, of which 13 were waited for; matrix products, arithmetic and copies ran while one was open for 2% of the time, Pallas kernels for 21%

profile of v14, /device:TPU:13, one launch (start us, length us, event | category | flops | bytes accessed | tf_op | source)
XLA Modules:
  0.0 119.9 jit_solution(11685920861836458853)
XLA Ops:
  0.0 1.3 %collective-permute-start.2 = (bf16[2,4,128,256]{3,2,1,0:T(8,128)(2,1)}, bf16[2,4,128,256]{3,2,1,0:T(8,128)(2,1)S(1)}, u32[]{:S(2)}, u32[]{:S(2)}) collective-permute-start(bf16[2,4,128,256]{3,2,1,0:T(8,128)(2,1)} %bitcast.66), channel_id=1, source_target_pairs={{0,24},{8,16},{1,25},{9,17},{2,26},{10,18},{3,27},{11,19},{4,28},{... | collective-permute-start | bytes 1572872 | tf_op jit(solution)/shard_map/ppermute | solution.py:201
  1.3 1.1 slice_bitcast_fusion.6
  2.4 0.7 collective-permute-start
  3.1 3.1 %collective-permute-start.1 = (bf16[1,128,256]{2,1,0:T(8,128)(2,1)S(1)}, bf16[1,128,256]{2,1,0:T(8,128)(2,1)S(1)}, u32[]{:S(2)}, u32[]{:S(2)}) collective-permute-start(bf16[1,128,256]{2,1,0:T(8,128)(2,1)S(1)} %get-tuple-element.97), channel_id=1, source_target_pairs={{1,2},{2,1},{3,4},{4,3},{5,6},{6,5},{9,10},{10,9},{11,12},{12,11},... | collective-permute-start | bytes 196616 | tf_op jit(solution)/shard_map/ppermute | solution.py:167
  6.2 3.9 %shard_map.55 = (f32[4,128,256]{2,1,0:T(8,128)S(1)}, bf16[6912,256]{1,0:T(8,128)(2,1)S(1)}) custom-call(bf16[4,128,256]{2,1,0:T(8,128)(2,1)S(1)} %get-tuple-element.78.field.rest_0_, bf16[6912,256]{1,0:T(8,128)(2,1)} %bitcast.58), custom_call_target="tpu_custom_call" | custom-call | flops 1 | bytes 1 | tf_op jit(solution)/shard_map/pallas_call | solution.py:130
  10.9 3.6 %collective-permute-start.6 = (bf16[1,128,256]{2,1,0:T(8,128)(2,1)S(1)}, bf16[1,128,256]{2,1,0:T(8,128)(2,1)S(1)}, u32[]{:S(2)}, u32[]{:S(2)}) collective-permute-start(bf16[1,128,256]{2,1,0:T(8,128)(2,1)S(1)} %get-tuple-element.93), channel_id=1, source_target_pairs={{1,2},{2,1},{3,4},{4,3},{5,6},{6,5},{9,10},{10,9},{11,12},{12,11},... | collective-permute-start | bytes 196616 | tf_op jit(solution)/shard_map/ppermute | solution.py:167
  14.5 1.3 %collective-permute-done.2 = bf16[2,4,128,256]{3,2,1,0:T(8,128)(2,1)S(1)} collective-permute-done((bf16[2,4,128,256]{3,2,1,0:T(8,128)(2,1)}, bf16[2,4,128,256]{3,2,1,0:T(8,128)(2,1)S(1)}, u32[]{:S(2)}, u32[]{:S(2)}) %collective-permute-start.2) | collective-permute-done | bytes 524320 | tf_op jit(solution)/shard_map/ppermute | solution.py:201
  16.1 1.6 %collective-permute-start.3 = (bf16[1,128,256]{2,1,0:T(8,128)(2,1)S(1)}, bf16[1,128,256]{2,1,0:T(8,128)(2,1)S(1)}, u32[]{:S(2)}, u32[]{:S(2)}) collective-permute-start(bf16[1,128,256]{2,1,0:T(8,128)(2,1)S(1)} %get-tuple-element.96), channel_id=1, source_target_pairs={{0,1},{1,0},{2,3},{3,2},{4,5},{5,4},{6,7},{7,6},{8,9},{9,8},{10,11... | collective-permute-start | bytes 196616 | tf_op jit(solution)/shard_map/ppermute | solution.py:167
  17.7 3.1 %collective-permute-start.4 = (bf16[1,128,256]{2,1,0:T(8,128)(2,1)S(1)}, bf16[1,128,256]{2,1,0:T(8,128)(2,1)S(1)}, u32[]{:S(2)}, u32[]{:S(2)}) collective-permute-start(bf16[1,128,256]{2,1,0:T(8,128)(2,1)S(1)} %get-tuple-element.95), channel_id=1, source_target_pairs={{1,2},{2,1},{3,4},{4,3},{5,6},{6,5},{9,10},{10,9},{11,12},{12,11},... | collective-permute-start | bytes 196616 | tf_op jit(solution)/shard_map/ppermute | solution.py:167
  20.8 1.8 %shard_map.57.own = f32[4,128,256]{2,1,0:T(8,128)S(1)} custom-call(bf16[4,128,256]{2,1,0:T(8,128)(2,1)S(1)} %shard_map.56.field, bf16[6912,256]{1,0:T(8,128)(2,1)S(1)} %bitcast.48), custom_call_target="tpu_custom_call" | custom-call | flops 1 | bytes 1 | tf_op jit(solution)/shard_map/pallas_call | solution.py:130
  23.3 0.7 collective-permute-start.7
  24.0 0.7 collective-permute-start.12
  24.6 1.8 %shard_map.59.own = f32[4,128,256]{2,1,0:T(8,128)S(1)} custom-call(bf16[4,128,256]{2,1,0:T(8,128)(2,1)S(1)} %get-tuple-element.76.field.rest_0_, bf16[6912,256]{1,0:T(8,128)(2,1)S(1)} %get-tuple-element.50.weights), custom_call_target="tpu_custom_call" | custom-call | flops 1 | bytes 1 | tf_op jit(solution)/shard_map/pallas_call | solution.py:130
  27.2 3.6 %collective-permute-start.9 = (bf16[1,128,256]{2,1,0:T(8,128)(2,1)S(1)}, bf16[1,128,256]{2,1,0:T(8,128)(2,1)S(1)}, u32[]{:S(2)}, u32[]{:S(2)}) collective-permute-start(bf16[1,128,256]{2,1,0:T(8,128)(2,1)S(1)} %get-tuple-element.91), channel_id=1, source_target_pairs={{1,2},{2,1},{3,4},{4,3},{5,6},{6,5},{9,10},{10,9},{11,12},{12,11},... | collective-permute-start | bytes 196616 | tf_op jit(solution)/shard_map/ppermute | solution.py:167
  30.8 1.8 %shard_map.61.own = f32[4,128,256]{2,1,0:T(8,128)S(1)} custom-call(bf16[4,128,256]{2,1,0:T(8,128)(2,1)S(1)} %shard_map.60.field, bf16[6912,256]{1,0:T(8,128)(2,1)S(1)} %bitcast.50), custom_call_target="tpu_custom_call" | custom-call | flops 1 | bytes 1 | tf_op jit(solution)/shard_map/pallas_call | solution.py:130
  33.5 3.1 %collective-permute-start.10 = (bf16[4,128,256]{2,1,0:T(8,128)(2,1)S(1)}, bf16[4,128,256]{2,1,0:T(8,128)(2,1)S(1)}, u32[]{:S(2)}, u32[]{:S(2)}) collective-permute-start(bf16[4,128,256]{2,1,0:T(8,128)(2,1)S(1)} %shard_map.62), channel_id=1, source_target_pairs={{0,8},{8,16},{16,24},{1,9},{9,17},{17,25},{2,10},{10,18},{18,26},{... | collective-permute-start | bytes 786440 | tf_op jit(solution)/shard_map/ppermute | solution.py:201
  36.6 0.7 collective-permute-start.14
  37.3 0.7 collective-permute-start.13
  38.0 5.8 %collective-permute-done.10 = bf16[4,128,256]{2,1,0:T(8,128)(2,1)S(1)} collective-permute-done((bf16[4,128,256]{2,1,0:T(8,128)(2,1)S(1)}, bf16[4,128,256]{2,1,0:T(8,128)(2,1)S(1)}, u32[]{:S(2)}, u32[]{:S(2)}) %collective-permute-start.10) | collective-permute-done | bytes 262176 | tf_op jit(solution)/shard_map/ppermute | solution.py:201
  43.8 2.2 %collective-permute-start.11 = (bf16[4,128,256]{2,1,0:T(8,128)(2,1)S(1)}, bf16[4,128,256]{2,1,0:T(8,128)(2,1)S(1)}, u32[]{:S(2)}, u32[]{:S(2)}) collective-permute-start(bf16[4,128,256]{2,1,0:T(8,128)(2,1)S(1)} %shard_map.60.field), channel_id=1, source_target_pairs={{0,8},{8,16},{16,24},{1,9},{9,17},{17,25},{2,10},{10,18},{18,26},{... | collective-permute-start | bytes 786440 | tf_op jit(solution)/shard_map/ppermute | solution.py:201
  46.1 1.6 %collective-permute-start.15 = (bf16[1,128,256]{2,1,0:T(8,128)(2,1)S(1)}, bf16[1,128,256]{2,1,0:T(8,128)(2,1)S(1)}, u32[]{:S(2)}, u32[]{:S(2)}) collective-permute-start(bf16[1,128,256]{2,1,0:T(8,128)(2,1)S(1)} %get-tuple-element.90), channel_id=1, source_target_pairs={{0,1},{1,0},{2,3},{3,2},{4,5},{5,4},{6,7},{7,6},{8,9},{9,8},{10,11... | collective-permute-start | bytes 196616 | tf_op jit(solution)/shard_map/ppermute | solution.py:167
  47.7 3.1 %collective-permute-start.16 = (bf16[1,128,256]{2,1,0:T(8,128)(2,1)S(1)}, bf16[1,128,256]{2,1,0:T(8,128)(2,1)S(1)}, u32[]{:S(2)}, u32[]{:S(2)}) collective-permute-start(bf16[1,128,256]{2,1,0:T(8,128)(2,1)S(1)} %get-tuple-element.89), channel_id=1, source_target_pairs={{1,2},{2,1},{3,4},{4,3},{5,6},{6,5},{9,10},{10,9},{11,12},{12,11},... | collective-permute-start | bytes 196616 | tf_op jit(solution)/shard_map/ppermute | solution.py:167
  50.8 0.9 collective-permute-start.17
  51.7 1.8 %shard_map.63.own = f32[4,128,256]{2,1,0:T(8,128)S(1)} custom-call(bf16[4,128,256]{2,1,0:T(8,128)(2,1)S(1)} %fusion.16.field.rest_0_, bf16[6912,256]{1,0:T(8,128)(2,1)S(1)} %get-tuple-element.50.weights), custom_call_target="tpu_custom_call" | custom-call | flops 1 | bytes 1 | tf_op jit(solution)/shard_map/pallas_call | solution.py:130
  54.4 1.2 collective-permute-start.18
  55.5 3.1 %collective-permute-start.19 = (bf16[1,128,256]{2,1,0:T(8,128)(2,1)S(1)}, bf16[1,128,256]{2,1,0:T(8,128)(2,1)S(1)}, u32[]{:S(2)}, u32[]{:S(2)}) collective-permute-start(bf16[1,128,256]{2,1,0:T(8,128)(2,1)S(1)} %get-tuple-element.87), channel_id=1, source_target_pairs={{1,2},{2,1},{3,4},{4,3},{5,6},{6,5},{9,10},{10,9},{11,12},{12,11},... | collective-permute-start | bytes 196616 | tf_op jit(solution)/shard_map/ppermute | solution.py:167
  58.7 1.8 %shard_map.65.own = f32[4,128,256]{2,1,0:T(8,128)S(1)} custom-call(bf16[4,128,256]{2,1,0:T(8,128)(2,1)S(1)} %add_convert_fusion.6.field, bf16[6912,256]{1,0:T(8,128)(2,1)S(1)} %bitcast.52), custom_call_target="tpu_custom_call" | custom-call | flops 1 | bytes 1 | tf_op jit(solution)/shard_map/pallas_call | solution.py:130
  61.7 2.4 %collective-permute-start.20 = (bf16[4,128,256]{2,1,0:T(8,128)(2,1)S(1)}, bf16[4,128,256]{2,1,0:T(8,128)(2,1)S(1)}, u32[]{:S(2)}, u32[]{:S(2)}) collective-permute-start(bf16[4,128,256]{2,1,0:T(8,128)(2,1)S(1)} %shard_map.66), channel_id=1, source_target_pairs={{0,8},{8,16},{16,24},{1,9},{9,17},{17,25},{2,10},{10,18},{18,26},{... | collective-permute-start | bytes 786440 | tf_op jit(solution)/shard_map/ppermute | solution.py:201
  64.1 0.7 collective-permute-start.22
  64.8 7.6 %collective-permute-done.20 = bf16[4,128,256]{2,1,0:T(8,128)(2,1)S(1)} collective-permute-done((bf16[4,128,256]{2,1,0:T(8,128)(2,1)S(1)}, bf16[4,128,256]{2,1,0:T(8,128)(2,1)S(1)}, u32[]{:S(2)}, u32[]{:S(2)}) %collective-permute-start.20) | collective-permute-done | bytes 262176 | tf_op jit(solution)/shard_map/ppermute | solution.py:201
  72.5 1.9 %collective-permute-start.21 = (bf16[4,128,256]{2,1,0:T(8,128)(2,1)S(1)}, bf16[4,128,256]{2,1,0:T(8,128)(2,1)S(1)}, u32[]{:S(2)}, u32[]{:S(2)}) collective-permute-start(bf16[4,128,256]{2,1,0:T(8,128)(2,1)S(1)} %add_convert_fusion.6.field), channel_id=1, source_target_pairs={{0,8},{8,16},{16,24},{1,9},{9,17},{17,25},{2,10},{10,18},{18,26},{... | collective-permute-start | bytes 786440 | tf_op jit(solution)/shard_map/ppermute | solution.py:201
  74.5 0.9 collective-permute-start.23
  75.4 3.2 %collective-permute-start.24 = (bf16[1,128,256]{2,1,0:T(8,128)(2,1)S(1)}, bf16[1,128,256]{2,1,0:T(8,128)(2,1)S(1)}, u32[]{:S(2)}, u32[]{:S(2)}) collective-permute-start(bf16[1,128,256]{2,1,0:T(8,128)(2,1)S(1)} %get-tuple-element.85), channel_id=1, source_target_pairs={{1,2},{2,1},{3,4},{4,3},{5,6},{6,5},{9,10},{10,9},{11,12},{12,11},... | collective-permute-start | bytes 196616 | tf_op jit(solution)/shard_map/ppermute | solution.py:167
  78.6 1.8 %shard_map.67.own = f32[4,128,256]{2,1,0:T(8,128)S(1)} custom-call(bf16[4,128,256]{2,1,0:T(8,128)(2,1)S(1)} %fusion.15.field.rest_0_, bf16[6912,256]{1,0:T(8,128)(2,1)S(1)} %get-tuple-element.50.weights), custom_call_target="tpu_custom_call" | custom-call | flops 1 | bytes 1 | tf_op jit(solution)/shard_map/pallas_call | solution.py:130
  80.5 0.7 collective-permute-start.25
  82.5 1.8 %collective-permute-start.26 = (bf16[1,128,256]{2,1,0:T(8,128)(2,1)S(1)}, bf16[1,128,256]{2,1,0:T(8,128)(2,1)S(1)}, u32[]{:S(2)}, u32[]{:S(2)}) collective-permute-start(bf16[1,128,256]{2,1,0:T(8,128)(2,1)S(1)} %get-tuple-element.84), channel_id=1, source_target_pairs={{0,1},{1,0},{2,3},{3,2},{4,5},{5,4},{6,7},{7,6},{8,9},{9,8},{10,11... | collective-permute-start | bytes 196616 | tf_op jit(solution)/shard_map/ppermute | solution.py:167
  84.2 3.4 %collective-permute-start.27 = (bf16[1,128,256]{2,1,0:T(8,128)(2,1)S(1)}, bf16[1,128,256]{2,1,0:T(8,128)(2,1)S(1)}, u32[]{:S(2)}, u32[]{:S(2)}) collective-permute-start(bf16[1,128,256]{2,1,0:T(8,128)(2,1)S(1)} %get-tuple-element.83), channel_id=1, source_target_pairs={{1,2},{2,1},{3,4},{4,3},{5,6},{6,5},{9,10},{10,9},{11,12},{12,11},... | collective-permute-start | bytes 196616 | tf_op jit(solution)/shard_map/ppermute | solution.py:167
  87.6 1.8 %shard_map.69.own = f32[4,128,256]{2,1,0:T(8,128)S(1)} custom-call(bf16[4,128,256]{2,1,0:T(8,128)(2,1)S(1)} %add_convert_fusion.3.field, bf16[6912,256]{1,0:T(8,128)(2,1)S(1)} %bitcast.54), custom_call_target="tpu_custom_call" | custom-call | flops 1 | bytes 1 | tf_op jit(solution)/shard_map/pallas_call | solution.py:130
  90.4 1.9 %collective-permute-start.28 = (bf16[4,128,256]{2,1,0:T(8,128)(2,1)S(1)}, bf16[4,128,256]{2,1,0:T(8,128)(2,1)S(1)}, u32[]{:S(2)}, u32[]{:S(2)}) collective-permute-start(bf16[4,128,256]{2,1,0:T(8,128)(2,1)S(1)} %shard_map.70), channel_id=1, source_target_pairs={{0,8},{8,16},{16,24},{1,9},{9,17},{17,25},{2,10},{10,18},{18,26},{... | collective-permute-start | bytes 786440 | tf_op jit(solution)/shard_map/ppermute | solution.py:201
  93.1 8.1 %collective-permute-done.28 = bf16[4,128,256]{2,1,0:T(8,128)(2,1)S(1)} collective-permute-done((bf16[4,128,256]{2,1,0:T(8,128)(2,1)S(1)}, bf16[4,128,256]{2,1,0:T(8,128)(2,1)S(1)}, u32[]{:S(2)}, u32[]{:S(2)}) %collective-permute-start.28) | collective-permute-done | bytes 262176 | tf_op jit(solution)/shard_map/ppermute | solution.py:201
  101.1 1.9 %collective-permute-start.29 = (bf16[4,128,256]{2,1,0:T(8,128)(2,1)S(1)}, bf16[4,128,256]{2,1,0:T(8,128)(2,1)S(1)}, u32[]{:S(2)}, u32[]{:S(2)}) collective-permute-start(bf16[4,128,256]{2,1,0:T(8,128)(2,1)S(1)} %add_convert_fusion.3.field), channel_id=1, source_target_pairs={{0,8},{8,16},{16,24},{1,9},{9,17},{17,25},{2,10},{10,18},{18,26},{... | collective-permute-start | bytes 786440 | tf_op jit(solution)/shard_map/ppermute | solution.py:201
  103.2 0.9 collective-permute-start.31
  104.1 3.6 %collective-permute-start.32 = (bf16[1,128,256]{2,1,0:T(8,128)(2,1)S(1)}, bf16[1,128,256]{2,1,0:T(8,128)(2,1)S(1)}, u32[]{:S(2)}, u32[]{:S(2)}) collective-permute-start(bf16[1,128,256]{2,1,0:T(8,128)(2,1)S(1)} %get-tuple-element.81), channel_id=1, source_target_pairs={{1,2},{2,1},{3,4},{4,3},{5,6},{6,5},{9,10},{10,9},{11,12},{12,11},... | collective-permute-start | bytes 196616 | tf_op jit(solution)/shard_map/ppermute | solution.py:167
  107.7 1.8 %shard_map.71.own = f32[4,128,256]{2,1,0:T(8,128)S(1)} custom-call(bf16[4,128,256]{2,1,0:T(8,128)(2,1)S(1)} %fusion.13.field.rest_1_, bf16[6912,256]{1,0:T(8,128)(2,1)S(1)} %get-tuple-element.50.weights), custom_call_target="tpu_custom_call" | custom-call | flops 1 | bytes 1 | tf_op jit(solution)/shard_map/pallas_call | solution.py:130
  111.2 1.8 %collective-permute-start.33 = (bf16[1,128,256]{2,1,0:T(8,128)(2,1)S(1)}, bf16[1,128,256]{2,1,0:T(8,128)(2,1)S(1)}, u32[]{:S(2)}, u32[]{:S(2)}) collective-permute-start(bf16[1,128,256]{2,1,0:T(8,128)(2,1)S(1)} %get-tuple-element.80), channel_id=1, source_target_pairs={{0,1},{1,0},{2,3},{3,2},{4,5},{5,4},{6,7},{7,6},{8,9},{9,8},{10,11... | collective-permute-start | bytes 196616 | tf_op jit(solution)/shard_map/ppermute | solution.py:167
  112.9 3.4 %collective-permute-start.34 = (bf16[1,128,256]{2,1,0:T(8,128)(2,1)S(1)}, bf16[1,128,256]{2,1,0:T(8,128)(2,1)S(1)}, u32[]{:S(2)}, u32[]{:S(2)}) collective-permute-start(bf16[1,128,256]{2,1,0:T(8,128)(2,1)S(1)} %get-tuple-element.79), channel_id=1, source_target_pairs={{1,2},{2,1},{3,4},{4,3},{5,6},{6,5},{9,10},{10,9},{11,12},{12,11},... | collective-permute-start | bytes 196616 | tf_op jit(solution)/shard_map/ppermute | solution.py:167
  116.3 1.8 %shard_map.73.own = f32[4,128,256]{2,1,0:T(8,128)S(1)} custom-call(bf16[4,128,256]{2,1,0:T(8,128)(2,1)S(1)} %add_convert_fusion.field.rest_0_, bf16[6912,256]{1,0:T(8,128)(2,1)S(1)} %bitcast.56), custom_call_target="tpu_custom_call" | custom-call | flops 1 | bytes 1 | tf_op jit(solution)/shard_map/pallas_call | solution.py:130
  118.5 1.4 %shard_map.74 = bf16[2,4,128,256]{3,2,1,0:T(8,128)(2,1)} custom-call(s32[1]{0:T(128)} %bitcast.flags, bf16[1,128,256]{2,1,0:T(8,128)(2,1)S(1)} %collective-permute-done.33.near, bf16[1,128,256]{2,1,0:T(8,128)(2,1)S(1)} %collective-permute-done.34.far, f32[4,128,256]{2,1,0:T(8,128)S(1)} %shard_map.73.own, bf16[6912,256]{1,0:T(8,128)(2,1)S(1)} %bitcast.57, ...), custom_call_target="tpu_custom_call" | custom-call | flops 1 | bytes 1 | tf_op jit(solution)/shard_map/pallas_call | solution.py:130
  (66 shorter events, 10.6 us)
Async XLA Ops:
  0.0 15.8 %collective-permute-start.2 = (bf16[2,4,128,256]{3,2,1,0:T(8,128)(2,1)}, bf16[2,4,128,256]{3,2,1,0:T(8,128)(2,1)S(1)}, u32[]{:S(2)}, u32[]{:S(2)}) collective-permute-start(bf16[2,4,128,256]{3,2,1,0:T(8,128)(2,1)} %bitcast.66), channel_id=1, source_target_pairs={{0,24},{8,16},{1,25},{9,17},{2,26},{10,18},{3,27},{11,19},{4,28},{... | collective-permute-start | bytes 1572872 | tf_op jit(solution)/shard_map/ppermute | solution.py:201
  2.4 7.7 %collective-permute-start = (bf16[1,128,256]{2,1,0:T(8,128)(2,1)S(1)}, bf16[1,128,256]{2,1,0:T(8,128)(2,1)S(1)}, u32[]{:S(2)}, u32[]{:S(2)}) collective-permute-start(bf16[1,128,256]{2,1,0:T(8,128)(2,1)S(1)} %get-tuple-element.98), channel_id=1, source_target_pairs={{0,1},{1,0},{2,3},{3,2},{4,5},{5,4},{6,7},{7,6},{8,9},{9,8},{10,11... | collective-permute-start | bytes 196616 | tf_op jit(solution)/shard_map/ppermute | solution.py:167
  3.1 7.0 %collective-permute-start.1 = (bf16[1,128,256]{2,1,0:T(8,128)(2,1)S(1)}, bf16[1,128,256]{2,1,0:T(8,128)(2,1)S(1)}, u32[]{:S(2)}, u32[]{:S(2)}) collective-permute-start(bf16[1,128,256]{2,1,0:T(8,128)(2,1)S(1)} %get-tuple-element.97), channel_id=1, source_target_pairs={{1,2},{2,1},{3,4},{4,3},{5,6},{6,5},{9,10},{10,9},{11,12},{12,11},... | collective-permute-start | bytes 196616 | tf_op jit(solution)/shard_map/ppermute | solution.py:167
  6.2 9.5 %copy-start.1 = (bf16[3,2,4,16,8,256]{5,4,3,2,1,0:T(8,128)(2,1)S(1)}, bf16[3,2,4,16,8,256]{5,4,3,2,1,0:T(8,128)(2,1)}, u32[]{:S(2)}) copy-start(bf16[3,2,4,16,8,256]{5,4,3,2,1,0:T(8,128)(2,1)} %param.7) | copy-start | bytes 4718596
  10.1 5.7 %copy-start.2 = (bf16[1,2,4,16,8,256]{5,4,3,2,1,0:T(8,128)(2,1)S(1)}, bf16[1,2,4,16,8,256]{5,4,3,2,1,0:T(8,128)(2,1)}, u32[]{:S(2)}) copy-start(bf16[1,2,4,16,8,256]{5,4,3,2,1,0:T(8,128)(2,1)} %param.5) | copy-start | bytes 1572868
  10.2 10.6 %copy-start = (bf16[1,3,3,3,256,256]{5,4,3,2,1,0:T(8,128)(2,1)S(1)}, bf16[1,3,3,3,256,256]{5,4,3,2,1,0:T(8,128)(2,1)}, u32[]{:S(2)}) copy-start(bf16[1,3,3,3,256,256]{5,4,3,2,1,0:T(8,128)(2,1)} %param.9) | copy-start | bytes 10616836
  10.8 11.8 %collective-permute-start.5 = (bf16[1,128,256]{2,1,0:T(8,128)(2,1)S(1)}, bf16[1,128,256]{2,1,0:T(8,128)(2,1)S(1)}, u32[]{:S(2)}, u32[]{:S(2)}) collective-permute-start(bf16[1,128,256]{2,1,0:T(8,128)(2,1)S(1)} %get-tuple-element.94), channel_id=1, source_target_pairs={{0,1},{1,0},{2,3},{3,2},{4,5},{5,4},{6,7},{7,6},{8,9},{9,8},{10,11... | collective-permute-start | bytes 196616 | tf_op jit(solution)/shard_map/ppermute | solution.py:167
  10.9 11.7 %collective-permute-start.6 = (bf16[1,128,256]{2,1,0:T(8,128)(2,1)S(1)}, bf16[1,128,256]{2,1,0:T(8,128)(2,1)S(1)}, u32[]{:S(2)}, u32[]{:S(2)}) collective-permute-start(bf16[1,128,256]{2,1,0:T(8,128)(2,1)S(1)} %get-tuple-element.93), channel_id=1, source_target_pairs={{1,2},{2,1},{3,4},{4,3},{5,6},{6,5},{9,10},{10,9},{11,12},{12,11},... | collective-permute-start | bytes 196616 | tf_op jit(solution)/shard_map/ppermute | solution.py:167
  16.1 7.2 %collective-permute-start.3 = (bf16[1,128,256]{2,1,0:T(8,128)(2,1)S(1)}, bf16[1,128,256]{2,1,0:T(8,128)(2,1)S(1)}, u32[]{:S(2)}, u32[]{:S(2)}) collective-permute-start(bf16[1,128,256]{2,1,0:T(8,128)(2,1)S(1)} %get-tuple-element.96), channel_id=1, source_target_pairs={{0,1},{1,0},{2,3},{3,2},{4,5},{5,4},{6,7},{7,6},{8,9},{9,8},{10,11... | collective-permute-start | bytes 196616 | tf_op jit(solution)/shard_map/ppermute | solution.py:167
  17.7 5.6 %collective-permute-start.4 = (bf16[1,128,256]{2,1,0:T(8,128)(2,1)S(1)}, bf16[1,128,256]{2,1,0:T(8,128)(2,1)S(1)}, u32[]{:S(2)}, u32[]{:S(2)}) collective-permute-start(bf16[1,128,256]{2,1,0:T(8,128)(2,1)S(1)} %get-tuple-element.95), channel_id=1, source_target_pairs={{1,2},{2,1},{3,4},{4,3},{5,6},{6,5},{9,10},{10,9},{11,12},{12,11},... | collective-permute-start | bytes 196616 | tf_op jit(solution)/shard_map/ppermute | solution.py:167
  23.3 13.3 %collective-permute-start.7 = (bf16[4,128,256]{2,1,0:T(8,128)(2,1)S(1)}, bf16[4,128,256]{2,1,0:T(8,128)(2,1)S(1)}, u32[]{:S(2)}, u32[]{:S(2)}) collective-permute-start(bf16[4,128,256]{2,1,0:T(8,128)(2,1)S(1)} %shard_map.56.field), channel_id=1, source_target_pairs={{0,8},{1,9},{2,10},{3,11},{4,12},{5,13},{6,14},{7,15}} | collective-permute-start | bytes 786440 | tf_op jit(solution)/shard_map/ppermute | solution.py:201
  24.0 12.7 %collective-permute-start.12 = (bf16[4,128,256]{2,1,0:T(8,128)(2,1)S(1)}, bf16[4,128,256]{2,1,0:T(8,128)(2,1)S(1)}, u32[]{:S(2)}, u32[]{:S(2)}) collective-permute-start(bf16[4,128,256]{2,1,0:T(8,128)(2,1)S(1)} %shard_map.58), channel_id=1, source_target_pairs={{0,8},{1,9},{2,10},{3,11},{4,12},{5,13},{6,14},{7,15}} | collective-permute-start | bytes 786440 | tf_op jit(solution)/shard_map/ppermute | solution.py:201
  27.1 5.5 %collective-permute-start.8 = (bf16[1,128,256]{2,1,0:T(8,128)(2,1)S(1)}, bf16[1,128,256]{2,1,0:T(8,128)(2,1)S(1)}, u32[]{:S(2)}, u32[]{:S(2)}) collective-permute-start(bf16[1,128,256]{2,1,0:T(8,128)(2,1)S(1)} %get-tuple-element.92), channel_id=1, source_target_pairs={{0,1},{1,0},{2,3},{3,2},{4,5},{5,4},{6,7},{7,6},{8,9},{9,8},{10,11... | collective-permute-start | bytes 196616 | tf_op jit(solution)/shard_map/ppermute | solution.py:167
  27.2 5.7 %collective-permute-start.9 = (bf16[1,128,256]{2,1,0:T(8,128)(2,1)S(1)}, bf16[1,128,256]{2,1,0:T(8,128)(2,1)S(1)}, u32[]{:S(2)}, u32[]{:S(2)}) collective-permute-start(bf16[1,128,256]{2,1,0:T(8,128)(2,1)S(1)} %get-tuple-element.91), channel_id=1, source_target_pairs={{1,2},{2,1},{3,4},{4,3},{5,6},{6,5},{9,10},{10,9},{11,12},{12,11},... | collective-permute-start | bytes 196616 | tf_op jit(solution)/shard_map/ppermute | solution.py:167
  33.5 10.3 %collective-permute-start.10 = (bf16[4,128,256]{2,1,0:T(8,128)(2,1)S(1)}, bf16[4,128,256]{2,1,0:T(8,128)(2,1)S(1)}, u32[]{:S(2)}, u32[]{:S(2)}) collective-permute-start(bf16[4,128,256]{2,1,0:T(8,128)(2,1)S(1)} %shard_map.62), channel_id=1, source_target_pairs={{0,8},{8,16},{16,24},{1,9},{9,17},{17,25},{2,10},{10,18},{18,26},{... | collective-permute-start | bytes 786440 | tf_op jit(solution)/shard_map/ppermute | solution.py:201
  36.6 9.4 %collective-permute-start.14 = (bf16[4,128,256]{2,1,0:T(8,128)(2,1)S(1)}, bf16[4,128,256]{2,1,0:T(8,128)(2,1)S(1)}, u32[]{:S(2)}, u32[]{:S(2)}) collective-permute-start(bf16[4,128,256]{2,1,0:T(8,128)(2,1)S(1)} %collective-permute-done.12), channel_id=1, source_target_pairs={{8,24},{9,25},{10,26},{11,27},{12,28},{13,29},{14,30},{15,31}} | collective-permute-start | bytes 786440 | tf_op jit(solution)/shard_map/ppermute | solution.py:201
  37.3 16.8 %collective-permute-start.13 = (bf16[4,128,256]{2,1,0:T(8,128)(2,1)S(1)}, bf16[4,128,256]{2,1,0:T(8,128)(2,1)S(1)}, u32[]{:S(2)}, u32[]{:S(2)}) collective-permute-start(bf16[4,128,256]{2,1,0:T(8,128)(2,1)S(1)} %collective-permute-done.7), channel_id=1, source_target_pairs={{8,24},{9,25},{10,26},{11,27},{12,28},{13,29},{14,30},{15,31}} | collective-permute-start | bytes 786440 | tf_op jit(solution)/shard_map/ppermute | solution.py:201
  43.8 10.4 %collective-permute-start.11 = (bf16[4,128,256]{2,1,0:T(8,128)(2,1)S(1)}, bf16[4,128,256]{2,1,0:T(8,128)(2,1)S(1)}, u32[]{:S(2)}, u32[]{:S(2)}) collective-permute-start(bf16[4,128,256]{2,1,0:T(8,128)(2,1)S(1)} %shard_map.60.field), channel_id=1, source_target_pairs={{0,8},{8,16},{16,24},{1,9},{9,17},{17,25},{2,10},{10,18},{18,26},{... | collective-permute-start | bytes 786440 | tf_op jit(solution)/shard_map/ppermute | solution.py:201
  46.1 7.4 %collective-permute-start.15 = (bf16[1,128,256]{2,1,0:T(8,128)(2,1)S(1)}, bf16[1,128,256]{2,1,0:T(8,128)(2,1)S(1)}, u32[]{:S(2)}, u32[]{:S(2)}) collective-permute-start(bf16[1,128,256]{2,1,0:T(8,128)(2,1)S(1)} %get-tuple-element.90), channel_id=1, source_target_pairs={{0,1},{1,0},{2,3},{3,2},{4,5},{5,4},{6,7},{7,6},{8,9},{9,8},{10,11... | collective-permute-start | bytes 196616 | tf_op jit(solution)/shard_map/ppermute | solution.py:167
  47.7 5.9 %collective-permute-start.16 = (bf16[1,128,256]{2,1,0:T(8,128)(2,1)S(1)}, bf16[1,128,256]{2,1,0:T(8,128)(2,1)S(1)}, u32[]{:S(2)}, u32[]{:S(2)}) collective-permute-start(bf16[1,128,256]{2,1,0:T(8,128)(2,1)S(1)} %get-tuple-element.89), channel_id=1, source_target_pairs={{1,2},{2,1},{3,4},{4,3},{5,6},{6,5},{9,10},{10,9},{11,12},{12,11},... | collective-permute-start | bytes 196616 | tf_op jit(solution)/shard_map/ppermute | solution.py:167
  50.8 10.9 %collective-permute-start.17 = (bf16[4,128,256]{2,1,0:T(8,128)(2,1)S(1)}, bf16[4,128,256]{2,1,0:T(8,128)(2,1)S(1)}, u32[]{:S(2)}, u32[]{:S(2)}) collective-permute-start(bf16[4,128,256]{2,1,0:T(8,128)(2,1)S(1)} %collective-permute-done.10), channel_id=1, source_target_pairs={{8,24},{9,25},{10,26},{11,27},{12,28},{13,29},{14,30},{15,31}} | collective-permute-start | bytes 786440 | tf_op jit(solution)/shard_map/ppermute | solution.py:201
  54.4 6.1 %collective-permute-start.18 = (bf16[1,128,256]{2,1,0:T(8,128)(2,1)S(1)}, bf16[1,128,256]{2,1,0:T(8,128)(2,1)S(1)}, u32[]{:S(2)}, u32[]{:S(2)}) collective-permute-start(bf16[1,128,256]{2,1,0:T(8,128)(2,1)S(1)} %get-tuple-element.88), channel_id=1, source_target_pairs={{0,1},{1,0},{2,3},{3,2},{4,5},{5,4},{6,7},{7,6},{8,9},{9,8},{10,11... | collective-permute-start | bytes 196616 | tf_op jit(solution)/shard_map/ppermute | solution.py:167
  55.5 5.6 %collective-permute-start.19 = (bf16[1,128,256]{2,1,0:T(8,128)(2,1)S(1)}, bf16[1,128,256]{2,1,0:T(8,128)(2,1)S(1)}, u32[]{:S(2)}, u32[]{:S(2)}) collective-permute-start(bf16[1,128,256]{2,1,0:T(8,128)(2,1)S(1)} %get-tuple-element.87), channel_id=1, source_target_pairs={{1,2},{2,1},{3,4},{4,3},{5,6},{6,5},{9,10},{10,9},{11,12},{12,11},... | collective-permute-start | bytes 196616 | tf_op jit(solution)/shard_map/ppermute | solution.py:167
  61.7 10.7 %collective-permute-start.20 = (bf16[4,128,256]{2,1,0:T(8,128)(2,1)S(1)}, bf16[4,128,256]{2,1,0:T(8,128)(2,1)S(1)}, u32[]{:S(2)}, u32[]{:S(2)}) collective-permute-start(bf16[4,128,256]{2,1,0:T(8,128)(2,1)S(1)} %shard_map.66), channel_id=1, source_target_pairs={{0,8},{8,16},{16,24},{1,9},{9,17},{17,25},{2,10},{10,18},{18,26},{... | collective-permute-start | bytes 786440 | tf_op jit(solution)/shard_map/ppermute | solution.py:201
  64.1 10.3 %collective-permute-start.22 = (bf16[4,128,256]{2,1,0:T(8,128)(2,1)S(1)}, bf16[4,128,256]{2,1,0:T(8,128)(2,1)S(1)}, u32[]{:S(2)}, u32[]{:S(2)}) collective-permute-start(bf16[4,128,256]{2,1,0:T(8,128)(2,1)S(1)} %collective-permute-done.11), channel_id=1, source_target_pairs={{8,24},{9,25},{10,26},{11,27},{12,28},{13,29},{14,30},{15,31}} | collective-permute-start | bytes 786440 | tf_op jit(solution)/shard_map/ppermute | solution.py:201
  72.5 9.8 %collective-permute-start.21 = (bf16[4,128,256]{2,1,0:T(8,128)(2,1)S(1)}, bf16[4,128,256]{2,1,0:T(8,128)(2,1)S(1)}, u32[]{:S(2)}, u32[]{:S(2)}) collective-permute-start(bf16[4,128,256]{2,1,0:T(8,128)(2,1)S(1)} %add_convert_fusion.6.field), channel_id=1, source_target_pairs={{0,8},{8,16},{16,24},{1,9},{9,17},{17,25},{2,10},{10,18},{18,26},{... | collective-permute-start | bytes 786440 | tf_op jit(solution)/shard_map/ppermute | solution.py:201
  74.5 6.6 %collective-permute-start.23 = (bf16[1,128,256]{2,1,0:T(8,128)(2,1)S(1)}, bf16[1,128,256]{2,1,0:T(8,128)(2,1)S(1)}, u32[]{:S(2)}, u32[]{:S(2)}) collective-permute-start(bf16[1,128,256]{2,1,0:T(8,128)(2,1)S(1)} %get-tuple-element.86), channel_id=1, source_target_pairs={{0,1},{1,0},{2,3},{3,2},{4,5},{5,4},{6,7},{7,6},{8,9},{9,8},{10,11... | collective-permute-start | bytes 196616 | tf_op jit(solution)/shard_map/ppermute | solution.py:167
  75.4 5.9 %collective-permute-start.24 = (bf16[1,128,256]{2,1,0:T(8,128)(2,1)S(1)}, bf16[1,128,256]{2,1,0:T(8,128)(2,1)S(1)}, u32[]{:S(2)}, u32[]{:S(2)}) collective-permute-start(bf16[1,128,256]{2,1,0:T(8,128)(2,1)S(1)} %get-tuple-element.85), channel_id=1, source_target_pairs={{1,2},{2,1},{3,4},{4,3},{5,6},{6,5},{9,10},{10,9},{11,12},{12,11},... | collective-permute-start | bytes 196616 | tf_op jit(solution)/shard_map/ppermute | solution.py:167
  80.5 10.0 %collective-permute-start.25 = (bf16[4,128,256]{2,1,0:T(8,128)(2,1)S(1)}, bf16[4,128,256]{2,1,0:T(8,128)(2,1)S(1)}, u32[]{:S(2)}, u32[]{:S(2)}) collective-permute-start(bf16[4,128,256]{2,1,0:T(8,128)(2,1)S(1)} %collective-permute-done.20), channel_id=1, source_target_pairs={{8,24},{9,25},{10,26},{11,27},{12,28},{13,29},{14,30},{15,31}} | collective-permute-start | bytes 786440 | tf_op jit(solution)/shard_map/ppermute | solution.py:201
  82.5 7.0 %collective-permute-start.26 = (bf16[1,128,256]{2,1,0:T(8,128)(2,1)S(1)}, bf16[1,128,256]{2,1,0:T(8,128)(2,1)S(1)}, u32[]{:S(2)}, u32[]{:S(2)}) collective-permute-start(bf16[1,128,256]{2,1,0:T(8,128)(2,1)S(1)} %get-tuple-element.84), channel_id=1, source_target_pairs={{0,1},{1,0},{2,3},{3,2},{4,5},{5,4},{6,7},{7,6},{8,9},{9,8},{10,11... | collective-permute-start | bytes 196616 | tf_op jit(solution)/shard_map/ppermute | solution.py:167
  84.2 5.6 %collective-permute-start.27 = (bf16[1,128,256]{2,1,0:T(8,128)(2,1)S(1)}, bf16[1,128,256]{2,1,0:T(8,128)(2,1)S(1)}, u32[]{:S(2)}, u32[]{:S(2)}) collective-permute-start(bf16[1,128,256]{2,1,0:T(8,128)(2,1)S(1)} %get-tuple-element.83), channel_id=1, source_target_pairs={{1,2},{2,1},{3,4},{4,3},{5,6},{6,5},{9,10},{10,9},{11,12},{12,11},... | collective-permute-start | bytes 196616 | tf_op jit(solution)/shard_map/ppermute | solution.py:167
  90.4 10.7 %collective-permute-start.28 = (bf16[4,128,256]{2,1,0:T(8,128)(2,1)S(1)}, bf16[4,128,256]{2,1,0:T(8,128)(2,1)S(1)}, u32[]{:S(2)}, u32[]{:S(2)}) collective-permute-start(bf16[4,128,256]{2,1,0:T(8,128)(2,1)S(1)} %shard_map.70), channel_id=1, source_target_pairs={{0,8},{8,16},{16,24},{1,9},{9,17},{17,25},{2,10},{10,18},{18,26},{... | collective-permute-start | bytes 786440 | tf_op jit(solution)/shard_map/ppermute | solution.py:201
  92.4 10.8 %collective-permute-start.30 = (bf16[4,128,256]{2,1,0:T(8,128)(2,1)S(1)}, bf16[4,128,256]{2,1,0:T(8,128)(2,1)S(1)}, u32[]{:S(2)}, u32[]{:S(2)}) collective-permute-start(bf16[4,128,256]{2,1,0:T(8,128)(2,1)S(1)} %collective-permute-done.21), channel_id=1, source_target_pairs={{8,24},{9,25},{10,26},{11,27},{12,28},{13,29},{14,30},{15,31}} | collective-permute-start | bytes 786440 | tf_op jit(solution)/shard_map/ppermute | solution.py:201
  101.1 9.8 %collective-permute-start.29 = (bf16[4,128,256]{2,1,0:T(8,128)(2,1)S(1)}, bf16[4,128,256]{2,1,0:T(8,128)(2,1)S(1)}, u32[]{:S(2)}, u32[]{:S(2)}) collective-permute-start(bf16[4,128,256]{2,1,0:T(8,128)(2,1)S(1)} %add_convert_fusion.3.field), channel_id=1, source_target_pairs={{0,8},{8,16},{16,24},{1,9},{9,17},{17,25},{2,10},{10,18},{18,26},{... | collective-permute-start | bytes 786440 | tf_op jit(solution)/shard_map/ppermute | solution.py:201
  103.2 6.3 %collective-permute-start.31 = (bf16[1,128,256]{2,1,0:T(8,128)(2,1)S(1)}, bf16[1,128,256]{2,1,0:T(8,128)(2,1)S(1)}, u32[]{:S(2)}, u32[]{:S(2)}) collective-permute-start(bf16[1,128,256]{2,1,0:T(8,128)(2,1)S(1)} %get-tuple-element.82), channel_id=1, source_target_pairs={{0,1},{1,0},{2,3},{3,2},{4,5},{5,4},{6,7},{7,6},{8,9},{9,8},{10,11... | collective-permute-start | bytes 196616 | tf_op jit(solution)/shard_map/ppermute | solution.py:167
  104.1 5.9 %collective-permute-start.32 = (bf16[1,128,256]{2,1,0:T(8,128)(2,1)S(1)}, bf16[1,128,256]{2,1,0:T(8,128)(2,1)S(1)}, u32[]{:S(2)}, u32[]{:S(2)}) collective-permute-start(bf16[1,128,256]{2,1,0:T(8,128)(2,1)S(1)} %get-tuple-element.81), channel_id=1, source_target_pairs={{1,2},{2,1},{3,4},{4,3},{5,6},{6,5},{9,10},{10,9},{11,12},{12,11},... | collective-permute-start | bytes 196616 | tf_op jit(solution)/shard_map/ppermute | solution.py:167
  111.2 7.0 %collective-permute-start.33 = (bf16[1,128,256]{2,1,0:T(8,128)(2,1)S(1)}, bf16[1,128,256]{2,1,0:T(8,128)(2,1)S(1)}, u32[]{:S(2)}, u32[]{:S(2)}) collective-permute-start(bf16[1,128,256]{2,1,0:T(8,128)(2,1)S(1)} %get-tuple-element.80), channel_id=1, source_target_pairs={{0,1},{1,0},{2,3},{3,2},{4,5},{5,4},{6,7},{7,6},{8,9},{9,8},{10,11... | collective-permute-start | bytes 196616 | tf_op jit(solution)/shard_map/ppermute | solution.py:167
  112.9 5.6 %collective-permute-start.34 = (bf16[1,128,256]{2,1,0:T(8,128)(2,1)S(1)}, bf16[1,128,256]{2,1,0:T(8,128)(2,1)S(1)}, u32[]{:S(2)}, u32[]{:S(2)}) collective-permute-start(bf16[1,128,256]{2,1,0:T(8,128)(2,1)S(1)} %get-tuple-element.79), channel_id=1, source_target_pairs={{1,2},{2,1},{3,4},{4,3},{5,6},{6,5},{9,10},{10,9},{11,12},{12,11},... | collective-permute-start | bytes 196616 | tf_op jit(solution)/shard_map/ppermute | solution.py:167

commit v15 on v12

v15 whole, which is shorter than its diff:
```python
import functools

import jax
import jax.numpy as jnp
from jax import lax
from jax.experimental import pallas as pl
from jax.experimental.pallas import tpu as pltpu
from jax.sharding import PartitionSpec as P

EPS = 1e-05
VMEM_LIMIT = 12 * 1024 * 1024


def act(values):
    values = values.astype(jnp.float32)
    scaled = values * lax.rsqrt(jnp.mean(values * values, axis=-1, keepdims=True) + EPS)
    return scaled * (0.5 + 0.5 * jnp.tanh(0.5 * scaled))


def fill(even, odd, at, values, width):
    planes, _, chans = values.shape
    field = act(values)
    edge = jnp.zeros((planes, width, chans), jnp.float32)
    even[pl.ds(at, planes)] = field.astype(jnp.bfloat16)
    odd[pl.ds(at, planes)] = jnp.concatenate([edge, field, edge], axis=1).astype(jnp.bfloat16)


def shifted(part, k, width):
    planes, voxels, chans = part.shape
    part = part.reshape(-1, width, chans)
    column = lax.broadcasted_iota(jnp.int32, part.shape, 1)
    if k == 0:
        part = jnp.where(column == 0, 0.0, pltpu.roll(part, 1, 1))
    elif k == 2:
        part = jnp.where(column == width - 1, 0.0, pltpu.roll(part, width - 1, 1))
    return part.reshape(planes, voxels, chans)


def product(taps, weights, offsets, k):
    planes, voxels, chans = taps[0].shape
    slab = jnp.concatenate([part.reshape(planes * voxels, chans) for part in taps], axis=-1)
    columns = jnp.concatenate([weights[(3 * n + k) * chans : (3 * n + k + 1) * chans] for n in offsets], axis=0)
    part = jnp.dot(slab, columns, preferred_element_type=jnp.float32)
    return part.reshape(planes, voxels, chans)


def convolve(taps, weights, width):
    return sum(shifted(product(taps, weights, range(9), k), k, width) for k in (1, 0, 2))


def edges(sources, targets, weights, width):
    total = None
    for k in (1, 0, 2):
        sums = [None] * 4
        for i in range(3):
            part = product(sources[i], weights, range(3 * i, 3 * i + 3), k)
            for plane, target in enumerate(targets[i]):
                piece = part[plane : plane + 1]
                sums[target] = piece if sums[target] is None else sums[target] + piece
        part = shifted(jnp.concatenate(sums, axis=0), k, width)
        total = part if total is None else total + part
    return total


def planes_at(even, odd, start, count, width):
    voxels = even.shape[1]
    return [
        even[start : start + count] if j == 1 else odd[start : start + count, j * width : j * width + voxels]
        for j in range(3)
    ]


def own_planes(width, inner_p, outer, weights, inner, partial, even, odd, ready=None):
    planes = outer.shape[0] - 2
    fill(even, odd, 0, outer[pl.ds(1, planes)], width)
    if ready is not None:
        ready.wait()
    taps = [part for i in range(3) for part in planes_at(even, odd, i, planes - 2, width)]
    inner[...] = (inner_p[...].astype(jnp.float32) + convolve(taps, weights, width)).astype(inner.dtype)
    own = lambda plane: planes_at(even, odd, plane, 1, width)
    pair = lambda one, other: [jnp.concatenate(both, axis=0) for both in zip(own(one), own(other))]
    sources = (pair(planes - 2, planes - 1), pair(0, planes - 1), pair(0, 1))
    partial[...] = edges(sources, ((2, 3), (1, 2), (0, 1)), weights, width)


def inner_kernel(width, inner_p, outer, weights, inner, partial, even, odd):
    own_planes(width, inner_p, outer, weights, inner, partial, even, odd)


def loading_kernel(width, inner_p, outer, weights_hbm, inner, partial, weights, even, odd, sem):
    copy = pltpu.make_async_copy(weights_hbm, weights, sem)
    copy.start()
    own_planes(width, inner_p, outer, weights, inner, partial, even, odd, copy)


def edge_kernel(width, flags, outer, inner, partial, near, far, weights, low, mid, high, even, odd):
    planes = mid.shape[0]
    above = flags[2] > 0
    near, far = near[...].astype(jnp.float32), far[...].astype(jnp.float32)
    below, beyond = jnp.where(above, far, near), jnp.where(above, near, far)
    fill(even, odd, 0, below[:2], width)
    fill(even, odd, 2, beyond[1:], width)
    sources = [planes_at(even, odd, start, 2, width) for start in range(3)]
    total = partial[...] + edges(sources, ((0, 1), (0, 3), (2, 3)), weights, width)
    low[...] = jnp.where(flags[0] > 0, below[2:] + total[:1], 0.0).astype(low.dtype)
    mid[pl.ds(0, 1)] = (outer[pl.ds(0, 1)].astype(jnp.float32) + total[1:2]).astype(mid.dtype)
    mid[pl.ds(1, planes - 2)] = inner[...]
    mid[pl.ds(planes - 1, 1)] = (outer[pl.ds(planes + 1, 1)].astype(jnp.float32) + total[2:3]).astype(mid.dtype)
    high[...] = jnp.where(flags[1] > 0, beyond[:1] + total[3:], 0.0).astype(high.dtype)


def second_kernel(width, first_low, first_mid, first_high, outer, weights, out, even, odd):
    planes = first_mid.shape[0]
    fill(even, odd, 0, first_low[...], width)
    fill(even, odd, 1, first_mid[...], width)
    fill(even, odd, 1 + planes, first_high[...], width)
    taps = [part for i in range(3) for part in planes_at(even, odd, i, planes, width)]
    second = (outer[pl.ds(1, planes)].astype(jnp.float32) + convolve(taps, weights, width)).astype(out.dtype)
    if len(out.shape) == 4:
        out[0] = first_mid[...]
        out[1] = second
    else:
        out[pl.ds(0, 1)] = first_mid[pl.ds(0, 1)]
        out[pl.ds(1, planes)] = second
        out[pl.ds(planes + 1, 1)] = first_mid[pl.ds(planes - 1, 1)]


def call(kernel, outputs, scratch, arguments, width):
    specs = [pl.BlockSpec(memory_space=pltpu.VMEM) for _ in arguments]
    if kernel is edge_kernel:
        specs[0] = pl.BlockSpec(memory_space=pltpu.SMEM)
    if kernel is loading_kernel:
        specs[-1] = pl.BlockSpec(memory_space=pltpu.HBM)
    return pl.pallas_call(
        functools.partial(kernel, width),
        out_shape=[jax.ShapeDtypeStruct(shape, dtype) for shape, dtype in outputs],
        in_specs=specs,
        out_specs=[pl.BlockSpec(memory_space=pltpu.VMEM) for _ in outputs],
        scratch_shapes=[pltpu.VMEM(shape, jnp.bfloat16) if shape else pltpu.SemaphoreType.DMA for shape in scratch],
        compiler_params=pltpu.CompilerParams(vmem_limit_bytes=VMEM_LIMIT),
        cost_estimate=pl.CostEstimate(flops=1, bytes_accessed=1, transcendentals=0),
    )(*arguments)


def stored(planes, voxels, chans, width):
    return (planes, voxels, chans), (planes, voxels + 2 * width, chans)


def inner_half(inner_p, outer, weights, width, load):
    inner, voxels, chans = inner_p.shape
    outputs = [(inner_p.shape, jnp.bfloat16), ((4, voxels, chans), jnp.float32)]
    scratch = stored(inner + 2, voxels, chans, width)
    if load:
        weights = pltpu.with_memory_space_constraint(weights, pltpu.HBM)
        outputs.append((weights.shape, jnp.bfloat16))
        return call(loading_kernel, outputs, [*scratch, ()], (inner_p, outer, weights), width)
    return *call(inner_kernel, outputs, scratch, (inner_p, outer, weights), width), weights


def first_half(flags, outer, inner, partial, halos, weights, width):
    rows, voxels, chans = outer.shape
    return call(
        edge_kernel,
        [((n, voxels, chans), jnp.bfloat16) for n in (1, rows - 2, 1)],
        stored(4, voxels, chans, width),
        (flags, outer, inner, partial, *halos, weights),
        width,
    )


def second_half(first, outer, weights, width, both):
    rows, voxels, chans = outer.shape
    (out,) = call(
        second_kernel,
        [((2, rows - 2, voxels, chans) if both else outer.shape, jnp.bfloat16)],
        stored(rows, voxels, chans, width),
        (*first, outer, weights),
        width,
    )
    return out


def swap(turn, starts, block):
    count = lax.axis_size("depth")
    pairs = [pair for i in range(turn, count - 1, 2) for pair in ((i, i + 1), (i + 1, i))]
    return lax.ppermute(lax.dynamic_slice_in_dim(block, starts[turn], 3, axis=0), "depth", pairs)


def local(resident, previous, incoming, first_weights, second_weights):
    section = lax.axis_index("section")
    sections = lax.axis_size("section")
    half = sections // 2
    depth = lax.axis_index("depth")
    ticks = incoming.shape[0] + 1
    _, _, planes, rows, width, chans = resident.shape
    voxels = rows * width
    across = [(j, sections - 1 - j) for j in range(1, half - 1)]

    above = depth % 2 == 0
    places = {
        "flags": jnp.stack([depth > 0, depth < lax.axis_size("depth") - 1, above]).astype(jnp.int32),
        "starts": (jnp.where(above, planes - 1, 0), jnp.where(above, 0, planes - 1)),
        "first": section == 0,
        "second": section == 1,
        "last": section == sections - 1,
        "decoder": section >= half,
        "direct": (section > half) & (section < sections - 1) if across else (),
    }
    places, resident, previous, incoming, first_weights, second_weights = lax.optimization_barrier(
        (places, resident, previous, incoming, first_weights, second_weights)
    )
    flags, starts = places["flags"], places["starts"]

    flat = lambda a: a.reshape(a.shape[0], 2, planes, voxels, chans)
    resident, previous, incoming = flat(resident)[0], flat(previous)[0], flat(incoming)
    w_one = first_weights.reshape(27 * chans, chans)
    w_two = second_weights.reshape(27 * chans, chans)

    def send(block, pairs):
        return lax.ppermute(block, "section", pairs) if pairs else block

    def join(held, skip):
        total = (held.astype(jnp.float32) + skip.astype(jnp.float32)).astype(jnp.bfloat16)
        return jnp.where(places["decoder"], total, held)

    def parted(streams):
        p, q = streams
        return p[1:-1], jnp.concatenate([p[:1], q, p[-1:]], axis=0)

    newer, older, direct = {}, {}, {}
    relayed = None

    def arrived(slot, part):
        fresh = parted(incoming[min(slot, ticks - 1) - 1])[part]
        held = jnp.where(places["second"], older[part], newer[part])
        passed = relayed[: planes - 2] if part == 0 else relayed[planes - 2 :]
        skip = jnp.where(places["last"], passed, newer[part])
        if across:
            skip = jnp.where(places["direct"], direct[part], skip)
        return jnp.where(places["first"], fresh, join(held, skip))

    def swaps(block):
        return swap(0, starts, block), swap(1, starts, block)

    mirrored = send(previous, [(j, sections - 1 - j) for j in range(half)])
    inner_p, outer = parted(resident)
    halos = swaps(outer)
    for slot in range(ticks + 1):
        if slot == 1:
            inner_p, outer, halos = following
        elif slot > 1:
            outer = arrived(slot, 1)
            halos = swaps(outer)
            inner_p = arrived(slot, 0)
        inner, partial, w_one = inner_half(inner_p, outer, w_one, width, slot == 0)
        onward = [(j, j + 1) for j in range(1, sections - 1)] if slot > 0 else []
        if slot < ticks - 1:
            onward = [(0, 1)] + onward
        received = {}
        if slot < ticks:
            received[0] = send(inner, onward)
            if across and slot > 0:
                direct[0] = send(inner, across)
        first = first_half(flags, outer, inner, partial, halos, w_one, width)
        sent = second_half(first, outer, w_two, width, slot == ticks)
        if slot == 0:
            mirrored, _ = lax.optimization_barrier((mirrored, sent))
            fresh = incoming[0]
            following = parted([jnp.where(places["first"], fresh[n], join(resident[n], mirrored[n])) for n in range(2)])
            following += (swaps(following[1]),)
        if slot < ticks:
            if slot > 0:
                received[0], sent = lax.optimization_barrier((received[0], sent))
            received[1] = send(sent, onward)
            if across and slot > 0:
                direct[1] = send(sent, across)
        if 0 < slot < ticks:
            held = jnp.concatenate([newer[0], newer[1]], axis=0)
            held, _ = lax.optimization_barrier((held, first[1] if slot == 1 else inner_p))
            relayed = send(held, [(1, sections - 1)])
        older, newer = newer, received
    result = sent
    return result.reshape(1, 2, planes, rows, width, chans)


def solution(mesh):
    in_specs = (
        P("section", None, "depth", None, None, None),
        P("section", None, "depth", None, None, None),
        P(None, None, "depth", None, None, None),
        P("section", None, None, None, None, None),
        P("section", None, None, None, None, None),
    )
    out_specs = P("section", None, "depth", None, None, None)
    return jax.shard_map(local, mesh=mesh, in_specs=in_specs, out_specs=out_specs, check_vma=False)
```

time: 111 us -> 122 us (1.099)
  waiting for transfers between devices: 20.7 us -> 46.8 us
  starting transfers between devices: 53.2 us -> 37.5 us
    ppermute x15 -> x12, waiting for transfers between devices: 15.2 us -> 41.1 us  [send(): return lax.ppermute(block, 'section', pairs) if pairs else block]
    ppermute x13 -> x10, starting transfers between devices: 33 us -> 18.3 us  [swap(): lax.ppermute(lax.dynamic_slice_in_dim(block, starts[turn], 3, axis=0), 'd...]
    ppermute x15 -> x12, starting transfers between devices: 20.2 us -> 19.2 us  [send(): return lax.ppermute(block, 'section', pairs) if pairs else block]
    ppermute x13 -> x10, waiting for transfers between devices: 5.55 us -> 5.76 us  [swap(): lax.ppermute(lax.dynamic_slice_in_dim(block, starts[turn], 3, axis=0), 'd...]
  transfers between devices with their start and end apart: 28 -> 22, of which waited for: 14 -> 7; matrix products, arithmetic and copies ran while one was open for 2% -> 2% of each run, Pallas kernels for 26% -> 22%
where the time goes in v15:
time: 122 us; the launch traced here: 121 us
  waiting for transfers between devices  46.8 us (38%)
  starting transfers between devices  37.5 us (31%)
  Pallas kernels  33 us (27%)
  local copies, waits for them, and re-layouts  2.33 us (2%)
  other arithmetic  1.28 us (1%)
    ppermute x12, waiting for transfers between devices, send(): return lax.ppermute(block, 'section', pairs) if pairs else block  41.1 us
    pallas_call x15, Pallas kernels, call(): pl.pallas_call(functools.partial(kernel, width), out_shape=[jax.ShapeDtyp...  33 us
    ppermute x12, starting transfers between devices, send(): return lax.ppermute(block, 'section', pairs) if pairs else block  19.2 us
    ppermute x10, starting transfers between devices, swap(): lax.ppermute(lax.dynamic_slice_in_dim(block, starts[turn], 3, axis=0), 'd...  18.3 us
    ppermute x10, waiting for transfers between devices, swap(): lax.ppermute(lax.dynamic_slice_in_dim(block, starts[turn], 3, axis=0), 'd...  5.76 us
  transfers between devices with their start and end apart: 22, of which 7 were waited for; matrix products, arithmetic and copies ran while one was open for 2% of the time, Pallas kernels for 22%

profile of v15, /device:TPU:13, one launch (start us, length us, event | category | flops | bytes accessed | tf_op | source)
XLA Modules:
  0.0 121.4 jit_solution(9396320665378154714)
XLA Ops:
  0.1 1.4 %collective-permute-start.1 = (bf16[2,4,128,256]{3,2,1,0:T(8,128)(2,1)}, bf16[2,4,128,256]{3,2,1,0:T(8,128)(2,1)S(1)}, u32[]{:S(2)}, u32[]{:S(2)}) collective-permute-start(bf16[2,4,128,256]{3,2,1,0:T(8,128)(2,1)} %bitcast.52), channel_id=1, source_target_pairs={{0,24},{8,16},{1,25},{9,17},{2,26},{10,18},{3,27},{11,19},{4,28},{... | collective-permute-start | bytes 1572872 | tf_op jit(solution)/shard_map/ppermute | solution.py:220
  1.5 1.0 slice_bitcast_fusion.1
  2.5 0.9 slice_bitcast_fusion.7
  3.5 0.7 collective-permute-start.2
  4.2 3.1 %collective-permute-start.3 = (bf16[3,128,256]{2,1,0:T(8,128)(2,1)S(1)}, bf16[3,128,256]{2,1,0:T(8,128)(2,1)S(1)}, u32[]{:S(2)}, u32[]{:S(2)}) collective-permute-start(bf16[3,128,256]{2,1,0:T(8,128)(2,1)S(1)} %get-tuple-element.119), channel_id=1, source_target_pairs={{1,2},{2,1},{3,4},{4,3},{5,6},{6,5},{9,10},{10,9},{11,12},{12,11},... | collective-permute-start | bytes 589832 | tf_op jit(solution)/shard_map/ppermute | solution.py:186
  7.3 4.1 %shard_map.55 = (bf16[2,128,256]{2,1,0:T(8,128)(2,1)S(1)}, f32[4,128,256]{2,1,0:T(8,128)S(1)}, bf16[6912,256]{1,0:T(8,128)(2,1)S(1)}) custom-call(bf16[2,128,256]{2,1,0:T(8,128)(2,1)S(1)} %slice_bitcast_fusion.3.inner_p, bf16[6,128,256]{2,1,0:T(8,128)(2,1)S(1)} %pad_maximum_fusion.4.outer, bf16[6912,256]{1,0:T(8,128)(2,1)} %bitcast.51), custom_call_target="tpu_custom_call" | custom-call | flops 1 | bytes 1 | tf_op jit(solution)/shard_map/pallas_call | solution.py:134
  11.4 0.7 collective-permute-start
  12.1 1.8 %shard_map.56 = (bf16[1,128,256]{2,1,0:T(8,128)(2,1)S(1)}, bf16[4,128,256]{2,1,0:T(8,128)(2,1)S(1)}, bf16[1,128,256]{2,1,0:T(8,128)(2,1)S(1)}) custom-call(s32[3]{0:T(128)S(1)} %add_convert_fusion.6.flags, bf16[6,128,256]{2,1,0:T(8,128)(2,1)S(1)} %pad_maximum_fusion.4.outer, bf16[2,128,256]{2,1,0:T(8,128)(2,1)S(1)} %get-tuple-element.60.inner, ...), custom_call_target="tpu_custom_call" | custom-call | flops 1 | bytes 1 | tf_op jit(solution)/shard_map/pallas_call | solution.py:134
  13.9 0.2 copy-done
  14.1 2.1 %shard_map.57 = bf16[6,128,256]{2,1,0:T(8,128)(2,1)S(1)} custom-call(bf16[1,128,256]{2,1,0:T(8,128)(2,1)S(1)} %get-tuple-element.66.first_low, bf16[4,128,256]{2,1,0:T(8,128)(2,1)S(1)} %get-tuple-element.67.first_mid, bf16[1,128,256]{2,1,0:T(8,128)(2,1)S(1)} %get-tuple-element.68.first_high, bf16[6,128,256]{2,1,0:T(8,128)(2,1)S(1)} %pad_maximum_fusion.4.outer, ...), custom_call_target="tpu_custom_call" | custom-call | flops 1 | bytes 1 | tf_op jit(solution)/shard_map/pallas_call | solution.py:134
  16.2 0.7 collective-permute-start.7
  17.0 0.2 fusion.10
  17.3 0.7 collective-permute-start.5
  18.0 3.1 %collective-permute-start.6 = (bf16[3,128,256]{2,1,0:T(8,128)(2,1)S(1)}, bf16[3,128,256]{2,1,0:T(8,128)(2,1)S(1)}, u32[]{:S(2)}, u32[]{:S(2)}) collective-permute-start(bf16[3,128,256]{2,1,0:T(8,128)(2,1)S(1)} %get-tuple-element.117), channel_id=1, source_target_pairs={{1,2},{2,1},{3,4},{4,3},{5,6},{6,5},{9,10},{10,9},{11,12},{12,11},... | collective-permute-start | bytes 589832 | tf_op jit(solution)/shard_map/ppermute | solution.py:186
  21.1 2.1 %shard_map.58 = (bf16[2,128,256]{2,1,0:T(8,128)(2,1)S(1)}, f32[4,128,256]{2,1,0:T(8,128)S(1)}) custom-call(bf16[2,128,256]{2,1,0:T(8,128)(2,1)S(1)} %slice.162.inner_p, bf16[6,128,256]{2,1,0:T(8,128)(2,1)S(1)} %pad_maximum_fusion.5.outer, bf16[6912,256]{1,0:T(8,128)(2,1)S(1)} %get-tuple-element.65.weights), custom_call_target="tpu_custom_call" | custom-call | flops 1 | bytes 1 | tf_op jit(solution)/shard_map/pallas_call | solution.py:134
  23.2 3.1 %collective-permute-start.4 = (bf16[2,128,256]{2,1,0:T(8,128)(2,1)S(1)}, bf16[2,128,256]{2,1,0:T(8,128)(2,1)S(1)}, u32[]{:S(2)}, u32[]{:S(2)}) collective-permute-start(bf16[2,128,256]{2,1,0:T(8,128)(2,1)S(1)} %get-tuple-element.71.inner), channel_id=1, source_target_pairs={{0,8},{8,16},{16,24},{1,9},{9,17},{17,25},{2,10},{10,18},{18,26},{... | collective-permute-start | bytes 393224 | tf_op jit(solution)/shard_map/ppermute | solution.py:220
  26.5 1.8 %shard_map.59 = (bf16[1,128,256]{2,1,0:T(8,128)(2,1)S(1)}, bf16[4,128,256]{2,1,0:T(8,128)(2,1)S(1)}, bf16[1,128,256]{2,1,0:T(8,128)(2,1)S(1)}) custom-call(s32[3]{0:T(128)S(1)} %add_convert_fusion.6.flags, bf16[6,128,256]{2,1,0:T(8,128)(2,1)S(1)} %pad_maximum_fusion.5.outer, bf16[2,128,256]{2,1,0:T(8,128)(2,1)S(1)} %get-tuple-element.71.inner, ...), custom_call_target="tpu_custom_call" | custom-call | flops 1 | bytes 1 | tf_op jit(solution)/shard_map/pallas_call | solution.py:134
  28.3 2.1 %shard_map.60 = bf16[6,128,256]{2,1,0:T(8,128)(2,1)S(1)} custom-call(bf16[1,128,256]{2,1,0:T(8,128)(2,1)S(1)} %get-tuple-element.73.first_low, bf16[4,128,256]{2,1,0:T(8,128)(2,1)S(1)} %get-tuple-element.74.first_mid, bf16[1,128,256]{2,1,0:T(8,128)(2,1)S(1)} %get-tuple-element.75.first_high, bf16[6,128,256]{2,1,0:T(8,128)(2,1)S(1)} %pad_maximum_fusion.5.outer, ...), custom_call_target="tpu_custom_call" | custom-call | flops 1 | bytes 1 | tf_op jit(solution)/shard_map/pallas_call | solution.py:134
  30.4 2.0 %collective-permute-done.4 = bf16[2,128,256]{2,1,0:T(8,128)(2,1)S(1)} collective-permute-done((bf16[2,128,256]{2,1,0:T(8,128)(2,1)S(1)}, bf16[2,128,256]{2,1,0:T(8,128)(2,1)S(1)}, u32[]{:S(2)}, u32[]{:S(2)}) %collective-permute-start.4) | collective-permute-done | bytes 131104 | tf_op jit(solution)/shard_map/ppermute | solution.py:220
  32.4 0.7 collective-permute-start.8
  33.1 1.9 %collective-permute-start.9 = (bf16[6,128,256]{2,1,0:T(8,128)(2,1)S(1)}, bf16[6,128,256]{2,1,0:T(8,128)(2,1)S(1)}, u32[]{:S(2)}, u32[]{:S(2)}) collective-permute-start(bf16[6,128,256]{2,1,0:T(8,128)(2,1)S(1)} %shard_map.60), channel_id=1, source_target_pairs={{0,8},{8,16},{16,24},{1,9},{9,17},{17,25},{2,10},{10,18},{18,26},{... | collective-permute-start | bytes 1179656 | tf_op jit(solution)/shard_map/ppermute | solution.py:220
  35.1 14.8 %collective-permute-done.9 = bf16[6,128,256]{2,1,0:T(8,128)(2,1)S(1)} collective-permute-done((bf16[6,128,256]{2,1,0:T(8,128)(2,1)S(1)}, bf16[6,128,256]{2,1,0:T(8,128)(2,1)S(1)}, u32[]{:S(2)}, u32[]{:S(2)}) %collective-permute-start.9) | collective-permute-done | bytes 393248 | tf_op jit(solution)/shard_map/ppermute | solution.py:220
  50.0 0.7 collective-permute-start.14
  50.9 0.7 collective-permute-start.11
  51.6 3.3 %collective-permute-start.12 = (bf16[3,128,256]{2,1,0:T(8,128)(2,1)S(1)}, bf16[3,128,256]{2,1,0:T(8,128)(2,1)S(1)}, u32[]{:S(2)}, u32[]{:S(2)}) collective-permute-start(bf16[3,128,256]{2,1,0:T(8,128)(2,1)S(1)} %get-tuple-element.115), channel_id=1, source_target_pairs={{1,2},{2,1},{3,4},{4,3},{5,6},{6,5},{9,10},{10,9},{11,12},{12,11},... | collective-permute-start | bytes 589832 | tf_op jit(solution)/shard_map/ppermute | solution.py:186
  54.9 2.1 %shard_map.61 = (bf16[2,128,256]{2,1,0:T(8,128)(2,1)S(1)}, f32[4,128,256]{2,1,0:T(8,128)S(1)}) custom-call(bf16[2,128,256]{2,1,0:T(8,128)(2,1)S(1)} %fusion.17.inner_p, bf16[6,128,256]{2,1,0:T(8,128)(2,1)S(1)} %fusion.9.outer, bf16[6912,256]{1,0:T(8,128)(2,1)S(1)} %get-tuple-element.65.weights), custom_call_target="tpu_custom_call" | custom-call | flops 1 | bytes 1 | tf_op jit(solution)/shard_map/pallas_call | solution.py:134
  57.1 3.6 %collective-permute-start.10 = (bf16[2,128,256]{2,1,0:T(8,128)(2,1)S(1)}, bf16[2,128,256]{2,1,0:T(8,128)(2,1)S(1)}, u32[]{:S(2)}, u32[]{:S(2)}) collective-permute-start(bf16[2,128,256]{2,1,0:T(8,128)(2,1)S(1)} %get-tuple-element.80.inner), channel_id=1, source_target_pairs={{0,8},{8,16},{16,24},{1,9},{9,17},{17,25},{2,10},{10,18},{18,26},{... | collective-permute-start | bytes 393224 | tf_op jit(solution)/shard_map/ppermute | solution.py:220
  60.7 1.8 %shard_map.62 = (bf16[1,128,256]{2,1,0:T(8,128)(2,1)S(1)}, bf16[4,128,256]{2,1,0:T(8,128)(2,1)S(1)}, bf16[1,128,256]{2,1,0:T(8,128)(2,1)S(1)}) custom-call(s32[3]{0:T(128)S(1)} %add_convert_fusion.6.flags, bf16[6,128,256]{2,1,0:T(8,128)(2,1)S(1)} %fusion.9.outer, bf16[2,128,256]{2,1,0:T(8,128)(2,1)S(1)} %get-tuple-element.80.inner, ...), custom_call_target="tpu_custom_call" | custom-call | flops 1 | bytes 1 | tf_op jit(solution)/shard_map/pallas_call | solution.py:134
  62.4 2.1 %shard_map.63 = bf16[6,128,256]{2,1,0:T(8,128)(2,1)S(1)} custom-call(bf16[1,128,256]{2,1,0:T(8,128)(2,1)S(1)} %get-tuple-element.82.first_low, bf16[4,128,256]{2,1,0:T(8,128)(2,1)S(1)} %get-tuple-element.83.first_mid, bf16[1,128,256]{2,1,0:T(8,128)(2,1)S(1)} %get-tuple-element.84.first_high, bf16[6,128,256]{2,1,0:T(8,128)(2,1)S(1)} %fusion.9.outer, ...), custom_call_target="tpu_custom_call" | custom-call | flops 1 | bytes 1 | tf_op jit(solution)/shard_map/pallas_call | solution.py:134
  64.6 0.9 collective-permute-done.10
  65.5 1.9 %collective-permute-start.13 = (bf16[6,128,256]{2,1,0:T(8,128)(2,1)S(1)}, bf16[6,128,256]{2,1,0:T(8,128)(2,1)S(1)}, u32[]{:S(2)}, u32[]{:S(2)}) collective-permute-start(bf16[6,128,256]{2,1,0:T(8,128)(2,1)S(1)} %shard_map.63), channel_id=1, source_target_pairs={{0,8},{8,16},{16,24},{1,9},{9,17},{17,25},{2,10},{10,18},{18,26},{... | collective-permute-start | bytes 1179656 | tf_op jit(solution)/shard_map/ppermute | solution.py:220
  67.5 11.8 %collective-permute-done.13 = bf16[6,128,256]{2,1,0:T(8,128)(2,1)S(1)} collective-permute-done((bf16[6,128,256]{2,1,0:T(8,128)(2,1)S(1)}, bf16[6,128,256]{2,1,0:T(8,128)(2,1)S(1)}, u32[]{:S(2)}, u32[]{:S(2)}) %collective-permute-start.13) | collective-permute-done | bytes 393248 | tf_op jit(solution)/shard_map/ppermute | solution.py:220
  79.5 2.1 %shard_map.64 = (bf16[2,128,256]{2,1,0:T(8,128)(2,1)S(1)}, f32[4,128,256]{2,1,0:T(8,128)S(1)}) custom-call(bf16[2,128,256]{2,1,0:T(8,128)(2,1)S(1)} %fusion.16.inner_p, bf16[6,128,256]{2,1,0:T(8,128)(2,1)S(1)} %fusion.8.outer, bf16[6912,256]{1,0:T(8,128)(2,1)S(1)} %get-tuple-element.65.weights), custom_call_target="tpu_custom_call" | custom-call | flops 1 | bytes 1 | tf_op jit(solution)/shard_map/pallas_call | solution.py:134
  81.6 1.9 %collective-permute-start.15 = (bf16[2,128,256]{2,1,0:T(8,128)(2,1)S(1)}, bf16[2,128,256]{2,1,0:T(8,128)(2,1)S(1)}, u32[]{:S(2)}, u32[]{:S(2)}) collective-permute-start(bf16[2,128,256]{2,1,0:T(8,128)(2,1)S(1)} %get-tuple-element.88.inner), channel_id=1, source_target_pairs={{8,16},{16,24},{9,17},{17,25},{10,18},{18,26},{11,19},{19,27},{12,... | collective-permute-start | bytes 393224 | tf_op jit(solution)/shard_map/ppermute | solution.py:220
  83.5 0.6 collective-permute-start.16
  84.2 2.5 %collective-permute-start.17 = (bf16[3,128,256]{2,1,0:T(8,128)(2,1)S(1)}, bf16[3,128,256]{2,1,0:T(8,128)(2,1)S(1)}, u32[]{:S(2)}, u32[]{:S(2)}) collective-permute-start(bf16[3,128,256]{2,1,0:T(8,128)(2,1)S(1)} %get-tuple-element.113), channel_id=1, source_target_pairs={{1,2},{2,1},{3,4},{4,3},{5,6},{6,5},{9,10},{10,9},{11,12},{12,11},... | collective-permute-start | bytes 589832 | tf_op jit(solution)/shard_map/ppermute | solution.py:186
  86.7 0.7 collective-permute-start.19
  87.4 3.7 %collective-permute-done.17.far = bf16[3,128,256]{2,1,0:T(8,128)(2,1)S(1)} collective-permute-done((bf16[3,128,256]{2,1,0:T(8,128)(2,1)S(1)}, bf16[3,128,256]{2,1,0:T(8,128)(2,1)S(1)}, u32[]{:S(2)}, u32[]{:S(2)}) %collective-permute-start.17) | collective-permute-done | bytes 196640 | tf_op jit(solution)/shard_map/ppermute | solution.py:186
  91.1 1.8 %shard_map.65 = (bf16[1,128,256]{2,1,0:T(8,128)(2,1)S(1)}, bf16[4,128,256]{2,1,0:T(8,128)(2,1)S(1)}, bf16[1,128,256]{2,1,0:T(8,128)(2,1)S(1)}) custom-call(s32[3]{0:T(128)S(1)} %add_convert_fusion.6.flags, bf16[6,128,256]{2,1,0:T(8,128)(2,1)S(1)} %fusion.8.outer, bf16[2,128,256]{2,1,0:T(8,128)(2,1)S(1)} %get-tuple-element.88.inner, ...), custom_call_target="tpu_custom_call" | custom-call | flops 1 | bytes 1 | tf_op jit(solution)/shard_map/pallas_call | solution.py:134
  92.9 2.1 %shard_map.66 = bf16[6,128,256]{2,1,0:T(8,128)(2,1)S(1)} custom-call(bf16[1,128,256]{2,1,0:T(8,128)(2,1)S(1)} %get-tuple-element.90.first_low, bf16[4,128,256]{2,1,0:T(8,128)(2,1)S(1)} %get-tuple-element.91.first_mid, bf16[1,128,256]{2,1,0:T(8,128)(2,1)S(1)} %get-tuple-element.92.first_high, bf16[6,128,256]{2,1,0:T(8,128)(2,1)S(1)} %fusion.8.outer, ...), custom_call_target="tpu_custom_call" | custom-call | flops 1 | bytes 1 | tf_op jit(solution)/shard_map/pallas_call | solution.py:134
  95.1 1.9 %collective-permute-start.18 = (bf16[6,128,256]{2,1,0:T(8,128)(2,1)S(1)}, bf16[6,128,256]{2,1,0:T(8,128)(2,1)S(1)}, u32[]{:S(2)}, u32[]{:S(2)}) collective-permute-start(bf16[6,128,256]{2,1,0:T(8,128)(2,1)S(1)} %shard_map.66), channel_id=1, source_target_pairs={{8,16},{16,24},{9,17},{17,25},{10,18},{18,26},{11,19},{19,27},{12,... | collective-permute-start | bytes 1179656 | tf_op jit(solution)/shard_map/ppermute | solution.py:220
  97.0 11.6 %collective-permute-done.18 = bf16[6,128,256]{2,1,0:T(8,128)(2,1)S(1)} collective-permute-done((bf16[6,128,256]{2,1,0:T(8,128)(2,1)S(1)}, bf16[6,128,256]{2,1,0:T(8,128)(2,1)S(1)}, u32[]{:S(2)}, u32[]{:S(2)}) %collective-permute-start.18) | collective-permute-done | bytes 393248 | tf_op jit(solution)/shard_map/ppermute | solution.py:220
  108.8 0.9 collective-permute-start.20
  109.7 2.7 %collective-permute-start.21 = (bf16[3,128,256]{2,1,0:T(8,128)(2,1)S(1)}, bf16[3,128,256]{2,1,0:T(8,128)(2,1)S(1)}, u32[]{:S(2)}, u32[]{:S(2)}) collective-permute-start(bf16[3,128,256]{2,1,0:T(8,128)(2,1)S(1)} %get-tuple-element.111), channel_id=1, source_target_pairs={{1,2},{2,1},{3,4},{4,3},{5,6},{6,5},{9,10},{10,9},{11,12},{12,11},... | collective-permute-start | bytes 589832 | tf_op jit(solution)/shard_map/ppermute | solution.py:186
  112.5 2.1 %shard_map.67 = (bf16[2,128,256]{2,1,0:T(8,128)(2,1)S(1)}, f32[4,128,256]{2,1,0:T(8,128)S(1)}) custom-call(bf16[2,128,256]{2,1,0:T(8,128)(2,1)S(1)} %fusion.15.inner_p, bf16[6,128,256]{2,1,0:T(8,128)(2,1)S(1)} %fusion.7.outer, bf16[6912,256]{1,0:T(8,128)(2,1)S(1)} %get-tuple-element.65.weights), custom_call_target="tpu_custom_call" | custom-call | flops 1 | bytes 1 | tf_op jit(solution)/shard_map/pallas_call | solution.py:134
  114.6 2.0 %collective-permute-done.21.far = bf16[3,128,256]{2,1,0:T(8,128)(2,1)S(1)} collective-permute-done((bf16[3,128,256]{2,1,0:T(8,128)(2,1)S(1)}, bf16[3,128,256]{2,1,0:T(8,128)(2,1)S(1)}, u32[]{:S(2)}, u32[]{:S(2)}) %collective-permute-start.21) | collective-permute-done | bytes 196640 | tf_op jit(solution)/shard_map/ppermute | solution.py:186
  116.7 1.8 %shard_map.68 = (bf16[1,128,256]{2,1,0:T(8,128)(2,1)S(1)}, bf16[4,128,256]{2,1,0:T(8,128)(2,1)S(1)}, bf16[1,128,256]{2,1,0:T(8,128)(2,1)S(1)}) custom-call(s32[3]{0:T(128)S(1)} %add_convert_fusion.6.flags, bf16[6,128,256]{2,1,0:T(8,128)(2,1)S(1)} %fusion.7.outer, bf16[2,128,256]{2,1,0:T(8,128)(2,1)S(1)} %get-tuple-element.96.inner, ...), custom_call_target="tpu_custom_call" | custom-call | flops 1 | bytes 1 | tf_op jit(solution)/shard_map/pallas_call | solution.py:134
  118.5 2.9 %shard_map.69 = bf16[2,4,128,256]{3,2,1,0:T(8,128)(2,1)} custom-call(bf16[1,128,256]{2,1,0:T(8,128)(2,1)S(1)} %get-tuple-element.98.first_low, bf16[4,128,256]{2,1,0:T(8,128)(2,1)S(1)} %get-tuple-element.99.first_mid, bf16[1,128,256]{2,1,0:T(8,128)(2,1)S(1)} %get-tuple-element.100.first_high, bf16[6,128,256]{2,1,0:T(8,128)(2,1)S(1)} %fusion.7.outer, ...), custom_call_target="tpu_custom_call" | custom-call | flops 1 | bytes 1 | tf_op jit(solution)/shard_map/pallas_call | solution.py:134
  (42 shorter events, 1.4 us)
Async XLA Ops:
  0.0 7.3 %copy-start.1 = (bf16[1,2,4,16,8,256]{5,4,3,2,1,0:T(8,128)(2,1)S(1)}, bf16[1,2,4,16,8,256]{5,4,3,2,1,0:T(8,128)(2,1)}, u32[]{:S(2)}) copy-start(bf16[1,2,4,16,8,256]{5,4,3,2,1,0:T(8,128)(2,1)} %param.5) | copy-start | bytes 1572868
  0.1 16.9 %collective-permute-start.1 = (bf16[2,4,128,256]{3,2,1,0:T(8,128)(2,1)}, bf16[2,4,128,256]{3,2,1,0:T(8,128)(2,1)S(1)}, u32[]{:S(2)}, u32[]{:S(2)}) collective-permute-start(bf16[2,4,128,256]{3,2,1,0:T(8,128)(2,1)} %bitcast.52), channel_id=1, source_target_pairs={{0,24},{8,16},{1,25},{9,17},{2,26},{10,18},{3,27},{11,19},{4,28},{... | collective-permute-start | bytes 1572872 | tf_op jit(solution)/shard_map/ppermute | solution.py:220
  3.5 8.6 %collective-permute-start.2 = (bf16[3,128,256]{2,1,0:T(8,128)(2,1)S(1)}, bf16[3,128,256]{2,1,0:T(8,128)(2,1)S(1)}, u32[]{:S(2)}, u32[]{:S(2)}) collective-permute-start(bf16[3,128,256]{2,1,0:T(8,128)(2,1)S(1)} %get-tuple-element.120), channel_id=1, source_target_pairs={{0,1},{1,0},{2,3},{3,2},{4,5},{5,4},{6,7},{7,6},{8,9},{9,8},{10,11... | collective-permute-start | bytes 589832 | tf_op jit(solution)/shard_map/ppermute | solution.py:186
  4.2 7.9 %collective-permute-start.3 = (bf16[3,128,256]{2,1,0:T(8,128)(2,1)S(1)}, bf16[3,128,256]{2,1,0:T(8,128)(2,1)S(1)}, u32[]{:S(2)}, u32[]{:S(2)}) collective-permute-start(bf16[3,128,256]{2,1,0:T(8,128)(2,1)S(1)} %get-tuple-element.119), channel_id=1, source_target_pairs={{1,2},{2,1},{3,4},{4,3},{5,6},{6,5},{9,10},{10,9},{11,12},{12,11},... | collective-permute-start | bytes 589832 | tf_op jit(solution)/shard_map/ppermute | solution.py:186
  11.4 15.0 %collective-permute-start = (bf16[2,128,256]{2,1,0:T(8,128)(2,1)S(1)}, bf16[2,128,256]{2,1,0:T(8,128)(2,1)S(1)}, u32[]{:S(2)}, u32[]{:S(2)}) collective-permute-start(bf16[2,128,256]{2,1,0:T(8,128)(2,1)S(1)} %get-tuple-element.60.inner), channel_id=1, source_target_pairs={{0,8},{1,9},{2,10},{3,11},{4,12},{5,13},{6,14},{7,15}} | collective-permute-start | bytes 393224 | tf_op jit(solution)/shard_map/ppermute | solution.py:220
  12.1 2.0 %copy-start = (bf16[1,3,3,3,256,256]{5,4,3,2,1,0:T(8,128)(2,1)S(1)}, bf16[1,3,3,3,256,256]{5,4,3,2,1,0:T(8,128)(2,1)}, u32[]{:S(2)}) copy-start(bf16[1,3,3,3,256,256]{5,4,3,2,1,0:T(8,128)(2,1)} %param.9) | copy-start | bytes 10616836
  14.1 2.8 %copy-start.2 = (bf16[3,2,4,16,8,256]{5,4,3,2,1,0:T(8,128)(2,1)S(1)}, bf16[3,2,4,16,8,256]{5,4,3,2,1,0:T(8,128)(2,1)}, u32[]{:S(2)}) copy-start(bf16[3,2,4,16,8,256]{5,4,3,2,1,0:T(8,128)(2,1)} %param.7) | copy-start | bytes 4718596
  16.2 10.2 %collective-permute-start.7 = (bf16[6,128,256]{2,1,0:T(8,128)(2,1)S(1)}, bf16[6,128,256]{2,1,0:T(8,128)(2,1)S(1)}, u32[]{:S(2)}, u32[]{:S(2)}) collective-permute-start(bf16[6,128,256]{2,1,0:T(8,128)(2,1)S(1)} %shard_map.57), channel_id=1, source_target_pairs={{0,8},{1,9},{2,10},{3,11},{4,12},{5,13},{6,14},{7,15}} | collective-permute-start | bytes 1179656 | tf_op jit(solution)/shard_map/ppermute | solution.py:220
  17.3 9.1 %collective-permute-start.5 = (bf16[3,128,256]{2,1,0:T(8,128)(2,1)S(1)}, bf16[3,128,256]{2,1,0:T(8,128)(2,1)S(1)}, u32[]{:S(2)}, u32[]{:S(2)}) collective-permute-start(bf16[3,128,256]{2,1,0:T(8,128)(2,1)S(1)} %get-tuple-element.118), channel_id=1, source_target_pairs={{0,1},{1,0},{2,3},{3,2},{4,5},{5,4},{6,7},{7,6},{8,9},{9,8},{10,11... | collective-permute-start | bytes 589832 | tf_op jit(solution)/shard_map/ppermute | solution.py:186
  18.0 8.5 %collective-permute-start.6 = (bf16[3,128,256]{2,1,0:T(8,128)(2,1)S(1)}, bf16[3,128,256]{2,1,0:T(8,128)(2,1)S(1)}, u32[]{:S(2)}, u32[]{:S(2)}) collective-permute-start(bf16[3,128,256]{2,1,0:T(8,128)(2,1)S(1)} %get-tuple-element.117), channel_id=1, source_target_pairs={{1,2},{2,1},{3,4},{4,3},{5,6},{6,5},{9,10},{10,9},{11,12},{12,11},... | collective-permute-start | bytes 589832 | tf_op jit(solution)/shard_map/ppermute | solution.py:186
  23.2 9.2 %collective-permute-start.4 = (bf16[2,128,256]{2,1,0:T(8,128)(2,1)S(1)}, bf16[2,128,256]{2,1,0:T(8,128)(2,1)S(1)}, u32[]{:S(2)}, u32[]{:S(2)}) collective-permute-start(bf16[2,128,256]{2,1,0:T(8,128)(2,1)S(1)} %get-tuple-element.71.inner), channel_id=1, source_target_pairs={{0,8},{8,16},{16,24},{1,9},{9,17},{17,25},{2,10},{10,18},{18,26},{... | collective-permute-start | bytes 393224 | tf_op jit(solution)/shard_map/ppermute | solution.py:220
  32.4 17.5 %collective-permute-start.8 = (bf16[8,128,256]{2,1,0:T(8,128)(2,1)S(1)}, bf16[8,128,256]{2,1,0:T(8,128)(2,1)S(1)}, u32[]{:S(2)}, u32[]{:S(2)}) collective-permute-start(bf16[8,128,256]{2,1,0:T(8,128)(2,1)S(1)} %pad_maximum_fusion), channel_id=1, source_target_pairs={{8,24},{9,25},{10,26},{11,27},{12,28},{13,29},{14,30},{15,31}} | collective-permute-start | bytes 1572872 | tf_op jit(solution)/shard_map/ppermute | solution.py:220
  33.1 16.8 %collective-permute-start.9 = (bf16[6,128,256]{2,1,0:T(8,128)(2,1)S(1)}, bf16[6,128,256]{2,1,0:T(8,128)(2,1)S(1)}, u32[]{:S(2)}, u32[]{:S(2)}) collective-permute-start(bf16[6,128,256]{2,1,0:T(8,128)(2,1)S(1)} %shard_map.60), channel_id=1, source_target_pairs={{0,8},{8,16},{16,24},{1,9},{9,17},{17,25},{2,10},{10,18},{18,26},{... | collective-permute-start | bytes 1179656 | tf_op jit(solution)/shard_map/ppermute | solution.py:220
  50.0 17.4 %collective-permute-start.14 = (bf16[8,128,256]{2,1,0:T(8,128)(2,1)S(1)}, bf16[8,128,256]{2,1,0:T(8,128)(2,1)S(1)}, u32[]{:S(2)}, u32[]{:S(2)}) collective-permute-start(bf16[8,128,256]{2,1,0:T(8,128)(2,1)S(1)} %pad_maximum_fusion.1), channel_id=1, source_target_pairs={{8,24},{9,25},{10,26},{11,27},{12,28},{13,29},{14,30},{15,31}} | collective-permute-start | bytes 1572872 | tf_op jit(solution)/shard_map/ppermute | solution.py:220
  50.9 9.7 %collective-permute-start.11 = (bf16[3,128,256]{2,1,0:T(8,128)(2,1)S(1)}, bf16[3,128,256]{2,1,0:T(8,128)(2,1)S(1)}, u32[]{:S(2)}, u32[]{:S(2)}) collective-permute-start(bf16[3,128,256]{2,1,0:T(8,128)(2,1)S(1)} %get-tuple-element.116), channel_id=1, source_target_pairs={{0,1},{1,0},{2,3},{3,2},{4,5},{5,4},{6,7},{7,6},{8,9},{9,8},{10,11... | collective-permute-start | bytes 589832 | tf_op jit(solution)/shard_map/ppermute | solution.py:186
  51.6 9.0 %collective-permute-start.12 = (bf16[3,128,256]{2,1,0:T(8,128)(2,1)S(1)}, bf16[3,128,256]{2,1,0:T(8,128)(2,1)S(1)}, u32[]{:S(2)}, u32[]{:S(2)}) collective-permute-start(bf16[3,128,256]{2,1,0:T(8,128)(2,1)S(1)} %get-tuple-element.115), channel_id=1, source_target_pairs={{1,2},{2,1},{3,4},{4,3},{5,6},{6,5},{9,10},{10,9},{11,12},{12,11},... | collective-permute-start | bytes 589832 | tf_op jit(solution)/shard_map/ppermute | solution.py:186
  57.1 8.4 %collective-permute-start.10 = (bf16[2,128,256]{2,1,0:T(8,128)(2,1)S(1)}, bf16[2,128,256]{2,1,0:T(8,128)(2,1)S(1)}, u32[]{:S(2)}, u32[]{:S(2)}) collective-permute-start(bf16[2,128,256]{2,1,0:T(8,128)(2,1)S(1)} %get-tuple-element.80.inner), channel_id=1, source_target_pairs={{0,8},{8,16},{16,24},{1,9},{9,17},{17,25},{2,10},{10,18},{18,26},{... | collective-permute-start | bytes 393224 | tf_op jit(solution)/shard_map/ppermute | solution.py:220
  65.5 13.8 %collective-permute-start.13 = (bf16[6,128,256]{2,1,0:T(8,128)(2,1)S(1)}, bf16[6,128,256]{2,1,0:T(8,128)(2,1)S(1)}, u32[]{:S(2)}, u32[]{:S(2)}) collective-permute-start(bf16[6,128,256]{2,1,0:T(8,128)(2,1)S(1)} %shard_map.63), channel_id=1, source_target_pairs={{0,8},{8,16},{16,24},{1,9},{9,17},{17,25},{2,10},{10,18},{18,26},{... | collective-permute-start | bytes 1179656 | tf_op jit(solution)/shard_map/ppermute | solution.py:220
  81.6 13.5 %collective-permute-start.15 = (bf16[2,128,256]{2,1,0:T(8,128)(2,1)S(1)}, bf16[2,128,256]{2,1,0:T(8,128)(2,1)S(1)}, u32[]{:S(2)}, u32[]{:S(2)}) collective-permute-start(bf16[2,128,256]{2,1,0:T(8,128)(2,1)S(1)} %get-tuple-element.88.inner), channel_id=1, source_target_pairs={{8,16},{16,24},{9,17},{17,25},{10,18},{18,26},{11,19},{19,27},{12,... | collective-permute-start | bytes 393224 | tf_op jit(solution)/shard_map/ppermute | solution.py:220
  83.5 3.9 %collective-permute-start.16 = (bf16[3,128,256]{2,1,0:T(8,128)(2,1)S(1)}, bf16[3,128,256]{2,1,0:T(8,128)(2,1)S(1)}, u32[]{:S(2)}, u32[]{:S(2)}) collective-permute-start(bf16[3,128,256]{2,1,0:T(8,128)(2,1)S(1)} %get-tuple-element.114), channel_id=1, source_target_pairs={{0,1},{1,0},{2,3},{3,2},{4,5},{5,4},{6,7},{7,6},{8,9},{9,8},{10,11... | collective-permute-start | bytes 589832 | tf_op jit(solution)/shard_map/ppermute | solution.py:186
  84.2 7.0 %collective-permute-start.17 = (bf16[3,128,256]{2,1,0:T(8,128)(2,1)S(1)}, bf16[3,128,256]{2,1,0:T(8,128)(2,1)S(1)}, u32[]{:S(2)}, u32[]{:S(2)}) collective-permute-start(bf16[3,128,256]{2,1,0:T(8,128)(2,1)S(1)} %get-tuple-element.113), channel_id=1, source_target_pairs={{1,2},{2,1},{3,4},{4,3},{5,6},{6,5},{9,10},{10,9},{11,12},{12,11},... | collective-permute-start | bytes 589832 | tf_op jit(solution)/shard_map/ppermute | solution.py:186
  86.7 10.3 %collective-permute-start.19 = (bf16[8,128,256]{2,1,0:T(8,128)(2,1)S(1)}, bf16[8,128,256]{2,1,0:T(8,128)(2,1)S(1)}, u32[]{:S(2)}, u32[]{:S(2)}) collective-permute-start(bf16[8,128,256]{2,1,0:T(8,128)(2,1)S(1)} %pad_maximum_fusion.2), channel_id=1, source_target_pairs={{8,24},{9,25},{10,26},{11,27},{12,28},{13,29},{14,30},{15,31}} | collective-permute-start | bytes 1572872 | tf_op jit(solution)/shard_map/ppermute | solution.py:220
  95.1 13.5 %collective-permute-start.18 = (bf16[6,128,256]{2,1,0:T(8,128)(2,1)S(1)}, bf16[6,128,256]{2,1,0:T(8,128)(2,1)S(1)}, u32[]{:S(2)}, u32[]{:S(2)}) collective-permute-start(bf16[6,128,256]{2,1,0:T(8,128)(2,1)S(1)} %shard_map.66), channel_id=1, source_target_pairs={{8,16},{16,24},{9,17},{17,25},{10,18},{18,26},{11,19},{19,27},{12,... | collective-permute-start | bytes 1179656 | tf_op jit(solution)/shard_map/ppermute | solution.py:220
  108.8 5.8 %collective-permute-start.20 = (bf16[3,128,256]{2,1,0:T(8,128)(2,1)S(1)}, bf16[3,128,256]{2,1,0:T(8,128)(2,1)S(1)}, u32[]{:S(2)}, u32[]{:S(2)}) collective-permute-start(bf16[3,128,256]{2,1,0:T(8,128)(2,1)S(1)} %get-tuple-element.112), channel_id=1, source_target_pairs={{0,1},{1,0},{2,3},{3,2},{4,5},{5,4},{6,7},{7,6},{8,9},{9,8},{10,11... | collective-permute-start | bytes 589832 | tf_op jit(solution)/shard_map/ppermute | solution.py:186
  109.7 7.0 %collective-permute-start.21 = (bf16[3,128,256]{2,1,0:T(8,128)(2,1)S(1)}, bf16[3,128,256]{2,1,0:T(8,128)(2,1)S(1)}, u32[]{:S(2)}, u32[]{:S(2)}) collective-permute-start(bf16[3,128,256]{2,1,0:T(8,128)(2,1)S(1)} %get-tuple-element.111), channel_id=1, source_target_pairs={{1,2},{2,1},{3,4},{4,3},{5,6},{6,5},{9,10},{10,9},{11,12},{12,11},... | collective-permute-start | bytes 589832 | tf_op jit(solution)/shard_map/ppermute | solution.py:186

commit v16 on v12

--- a/solution.py
+++ b/solution.py
@@ -70,7 +70,12 @@
     ]
 
 
+def stream(ref, number):
+    return ref.at[number] if len(ref.shape) == 4 else ref
+
+
 def own_planes(width, p, q, weights, inner, partial, even, odd, ready=None):
+    p, q = stream(p, 0), stream(q, 1)
     planes = q.shape[0]
     fill(even, odd, 0, q[...], width)
     if ready is not None:
@@ -93,34 +98,45 @@
     own_planes(width, p, q, weights, inner, partial, even, odd, copy)
 
 
-def edge_kernel(width, flags, p, inner, partial, q_near, q_far, p_near, p_far, weights, low, mid, high, even, odd):
+def edge_kernel(width, flags, p, inner, partial, near, far, weights, low, mid, high, even, odd):
+    p = stream(p, 0)
     planes = p.shape[0]
     above = flags[2] > 0
-    near, far = q_near[:2].astype(jnp.float32), q_far[:2].astype(jnp.float32)
-    fill(even, odd, 0, jnp.where(above, far, near), width)
-    fill(even, odd, 2, jnp.where(above, near, far), width)
+    near, far = near[...].astype(jnp.float32), far[...].astype(jnp.float32)
+    below, beyond = jnp.where(above, far, near), jnp.where(above, near, far)
+    fill(even, odd, 0, below[:2], width)
+    fill(even, odd, 2, beyond[:2], width)
     sources = [planes_at(even, odd, start, 2, width) for start in range(3)]
     total = partial[...] + edges(sources, ((0, 1), (0, 3), (2, 3)), weights, width)
-    near, far = p_near[-1:].astype(jnp.float32), p_far[-1:].astype(jnp.float32)
-    low[...] = jnp.where(flags[0] > 0, jnp.where(above, far, near) + total[:1], 0.0).astype(low.dtype)
+    low[...] = jnp.where(flags[0] > 0, below[2:] + total[:1], 0.0).astype(low.dtype)
     mid[pl.ds(0, 1)] = (p[:1].astype(jnp.float32) + total[1:2]).astype(mid.dtype)
     mid[pl.ds(1, planes - 2)] = inner[...]
     mid[pl.ds(planes - 1, 1)] = (p[-1:].astype(jnp.float32) + total[2:3]).astype(mid.dtype)
-    high[...] = jnp.where(flags[1] > 0, jnp.where(above, near, far) + total[3:], 0.0).astype(high.dtype)
-
-
-def second_kernel(width, first_low, first_mid, first_high, q, weights, out, even, odd):
+    high[...] = jnp.where(flags[1] > 0, beyond[2:] + total[3:], 0.0).astype(high.dtype)
+
+
+def second_sum(width, first_low, first_mid, first_high, q, weights, even, odd):
+    q = stream(q, 1)
     planes = q.shape[0]
     fill(even, odd, 0, first_low[...], width)
     fill(even, odd, 1, first_mid[...], width)
     fill(even, odd, 1 + planes, first_high[...], width)
     taps = [part for i in range(3) for part in planes_at(even, odd, i, planes, width)]
-    second = (q[...].astype(jnp.float32) + convolve(taps, weights, width)).astype(out.dtype)
-    if len(out.shape) == 4:
-        out[0] = first_mid[...]
-        out[1] = second
-    else:
-        out[...] = second
+    return q[...].astype(jnp.float32) + convolve(taps, weights, width)
+
+
+def second_kernel(width, first_low, first_mid, first_high, q, weights, out, even, odd):
+    out[...] = second_sum(width, first_low, first_mid, first_high, q, weights, even, odd).astype(out.dtype)
+
+
+def last_kernel(width, first_low, first_mid, first_high, q, weights, out, even, odd, second, first_sem, second_sem):
+    first_copy = pltpu.make_async_copy(first_mid, out.at[0], first_sem)
+    first_copy.start()
+    second[...] = second_sum(width, first_low, first_mid, first_high, q, weights, even, odd).astype(second.dtype)
+    second_copy = pltpu.make_async_copy(second, out.at[1], second_sem)
+    second_copy.start()
+    first_copy.wait()
+    second_copy.wait()
 
 
 def call(kernel, outputs, scratch, arguments, width):
@@ -133,7 +149,7 @@
         functools.partial(kernel, width),
         out_shape=[jax.ShapeDtypeStruct(shape, dtype) for shape, dtype in outputs],
         in_specs=specs,
-        out_specs=[pl.BlockSpec(memory_space=pltpu.VMEM) for _ in outputs],
+        out_specs=[pl.BlockSpec(memory_space=pltpu.HBM if kernel is last_kernel else pltpu.VMEM) for _ in outputs],
         scratch_shapes=[pltpu.VMEM(shape, jnp.bfloat16) if shape else pltpu.SemaphoreType.DMA for shape in scratch],
         compiler_params=pltpu.CompilerParams(vmem_limit_bytes=VMEM_LIMIT),
         cost_estimate=pl.CostEstimate(flops=1, bytes_accessed=1, transcendentals=0),
@@ -145,7 +161,7 @@
 
 
 def inner_half(p, q, weights, width, load):
-    planes, voxels, chans = q.shape
+    planes, voxels, chans = q.shape[-3:]
     outputs = [((planes - 2, voxels, chans), jnp.bfloat16), ((4, voxels, chans), jnp.float32)]
     scratch = stored(planes, voxels, chans, width)
     if load:
@@ -155,32 +171,33 @@
     return *call(inner_kernel, outputs, scratch, (p, q, weights), width), weights
 
 
-def first_half(flags, p, kept, q_halos, p_halos, weights, width):
-    planes, voxels, chans = p.shape
+def first_half(flags, p, kept, halos, weights, width):
+    planes, voxels, chans = p.shape[-3:]
     return call(
         edge_kernel,
         [((n, voxels, chans), jnp.bfloat16) for n in (1, planes, 1)],
         stored(4, voxels, chans, width),
-        (flags, p, *kept, *q_halos, *p_halos, weights),
+        (flags, p, *kept, *halos, weights),
         width,
     )
 
 
-def second_half(first, q, weights, width, both):
-    planes, voxels, chans = q.shape
-    (out,) = call(
-        second_kernel,
-        [((2, *q.shape) if both else q.shape, jnp.bfloat16)],
-        stored(planes + 2, voxels, chans, width),
-        (*first, q, weights),
-        width,
-    )
+def second_half(first, q, weights, width, last):
+    shape = q.shape[-3:]
+    scratch = stored(shape[0] + 2, *shape[1:], width)
+    output = shape
+    if last:
+        scratch, output = [*scratch, shape, (), ()], (2, *shape)
+    (out,) = call(last_kernel if last else second_kernel, [(output, jnp.bfloat16)], scratch, (*first, q, weights), width)
     return out
 
 
 def swap(turn, starts, *blocks):
     count = lax.axis_size("depth")
-    parts = [lax.dynamic_slice_in_dim(block, starts[n][turn], n, axis=0) for block, n in blocks]
+    parts = []
+    for block, n, *number in blocks:
+        part = lax.dynamic_slice(block, (*number, starts[n][turn], 0, 0), (*[1] * len(number), n, *block.shape[-2:]))
+        parts.append(part.reshape(part.shape[-3:]))
     pairs = [pair for i in range(turn, count - 1, 2) for pair in ((i, i + 1), (i + 1, i))]
     return lax.ppermute(jnp.concatenate(parts, axis=0), "depth", pairs)
 
@@ -236,23 +253,19 @@
             skip = jnp.where(places["direct"], direct[stream], skip)
         return jnp.where(places["first"], fresh, join(held, skip))
 
-    p, q = resident
+    p = q = resident
     mirrored = send(previous, [(j, sections - 1 - j) for j in range(half)])
-    near, q_far = (swap(turn, starts, (q, 2), (p, 1)) for turn in range(2))
-    p_far = q_far
+    near, far = (swap(turn, starts, (resident, 2, 1), (resident, 1, 0)) for turn in range(2))
     for slot in range(ticks + 1):
         if slot == 1:
-            p, q, near, q_far = following
-            p_far = q_far
+            p, q, near, far = following
         elif slot > 1:
             p = arrived(slot, 0)
-            p_far = swap(1, starts, (p, 1))
-            p, p_far, newer[1] = lax.optimization_barrier((p, p_far, newer[1]))
+            p, newer[1] = lax.optimization_barrier((p, newer[1]))
             q = arrived(slot, 1)
-            near = swap(0, starts, (q, 2), (p, 1))
-            q_far = swap(1, starts, (q, 2))
+            near, far = (swap(turn, starts, (q, 2), (p, 1)) for turn in range(2))
         *kept, w_one = inner_half(p, q, w_one, width, slot == 0)
-        first = first_half(flags, p, kept, (near, q_far), (near, p_far), w_one, width)
+        first = first_half(flags, p, kept, (near, far), w_one, width)
         onward = [(j, j + 1) for j in range(1, sections - 1)] if slot > 0 else []
         if slot < ticks - 1:
             onward = [(0, 1)] + onward

time: 111 us -> 110 us (level)
  starting transfers between devices: 53.2 us -> 41.2 us
  waiting for transfers between devices: 20.7 us -> 30.2 us
    ppermute x15, waiting for transfers between devices: 15.2 us -> 27.8 us  [send(): return lax.ppermute(block, 'section', pairs) if pairs else block]
    ppermute x13 -> x10, starting transfers between devices: 33 us -> 20.7 us  [swap(): return lax.ppermute(jnp.concatenate(parts, axis=0), 'depth', pairs)]
    ppermute x13 -> x10, waiting for transfers between devices: 5.55 us -> 2.43 us  [swap(): return lax.ppermute(jnp.concatenate(parts, axis=0), 'depth', pairs)]
    reshape x0 -> x2, local copies, waits for them, and re-layouts: none -> 1.88 us  [swap(): parts.append(part.reshape(part.shape[-3:]))]
  transfers between devices with their start and end apart: 28 -> 25, of which waited for: 14 -> 10; matrix products, arithmetic and copies ran while one was open for 2% -> 2% of each run, Pallas kernels for 26% -> 26%
where the time goes in v16:
time: 110 us; the launch traced here: 108 us
  starting transfers between devices  41.2 us (37%)
  Pallas kernels  32.9 us (30%)
  waiting for transfers between devices  30.2 us (27%)
  local copies, waits for them, and re-layouts  2.08 us (2%)
  other arithmetic  1.15 us (1%)
    pallas_call x15, Pallas kernels, call(): pl.pallas_call(functools.partial(kernel, width), out_shape=[jax.ShapeDtyp...  32.9 us
    ppermute x15, waiting for transfers between devices, send(): return lax.ppermute(block, 'section', pairs) if pairs else block  27.8 us
    ppermute x10, starting transfers between devices, swap(): return lax.ppermute(jnp.concatenate(parts, axis=0), 'depth', pairs)  20.7 us
    ppermute x15, starting transfers between devices, send(): return lax.ppermute(block, 'section', pairs) if pairs else block  20.5 us
    ppermute x10, waiting for transfers between devices, swap(): return lax.ppermute(jnp.concatenate(parts, axis=0), 'depth', pairs)  2.43 us
  transfers between devices with their start and end apart: 25, of which 10 were waited for; matrix products, arithmetic and copies ran while one was open for 2% of the time, Pallas kernels for 26%

profile of v16, /device:TPU:13, one launch (start us, length us, event | category | flops | bytes accessed | tf_op | source)
XLA Modules:
  0.0 108.3 jit_solution(8935754390876545994)
XLA Ops:
  0.1 1.4 %collective-permute-start.3 = (bf16[2,4,128,256]{3,2,1,0:T(8,128)(2,1)}, bf16[2,4,128,256]{3,2,1,0:T(8,128)(2,1)S(1)}, u32[]{:S(2)}, u32[]{:S(2)}) collective-permute-start(bf16[2,4,128,256]{3,2,1,0:T(8,128)(2,1)} %bitcast.74), channel_id=1, source_target_pairs={{0,24},{8,16},{1,25},{9,17},{2,26},{10,18},{3,27},{11,19},{4,28},{... | collective-permute-start | bytes 1572872 | tf_op jit(solution)/shard_map/ppermute | solution.py:238
  1.5 1.0 dynamic-slice_bitcast_fusion
  2.5 0.9 dynamic-slice_bitcast_fusion.2
  3.4 0.7 collective-permute-start
  4.2 3.1 %collective-permute-start.1 = (bf16[3,128,256]{2,1,0:T(8,128)(2,1)S(1)}, bf16[3,128,256]{2,1,0:T(8,128)(2,1)S(1)}, u32[]{:S(2)}, u32[]{:S(2)}) collective-permute-start(bf16[3,128,256]{2,1,0:T(8,128)(2,1)S(1)} %pad_maximum_fusion.1), channel_id=1, source_target_pairs={{1,2},{2,1},{3,4},{4,3},{5,6},{6,5},{9,10},{10,9},{11,12},{12,11},... | collective-permute-start | bytes 589832 | tf_op jit(solution)/shard_map/ppermute | solution.py:202
  7.3 4.1 %shard_map.55 = (bf16[2,128,256]{2,1,0:T(8,128)(2,1)S(1)}, f32[4,128,256]{2,1,0:T(8,128)S(1)}, bf16[6912,256]{1,0:T(8,128)(2,1)S(1)}) custom-call(bf16[2,4,128,256]{3,2,1,0:T(8,128)(2,1)S(1)} %bitcast.62, bf16[2,4,128,256]{3,2,1,0:T(8,128)(2,1)S(1)} %bitcast.63, bf16[6912,256]{1,0:T(8,128)(2,1)} %bitcast.66), custom_call_target="tpu_custom_call" | custom-call | flops 1 | bytes 1 | tf_op jit(solution)/shard_map/pallas_call | solution.py:148
  11.5 1.8 %shard_map.56 = (bf16[1,128,256]{2,1,0:T(8,128)(2,1)S(1)}, bf16[4,128,256]{2,1,0:T(8,128)(2,1)S(1)}, bf16[1,128,256]{2,1,0:T(8,128)(2,1)S(1)}) custom-call(s32[3]{0:T(128)S(1)} %add_convert_fusion.6.flags, bf16[2,4,128,256]{3,2,1,0:T(8,128)(2,1)S(1)} %bitcast.64, bf16[2,128,256]{2,1,0:T(8,128)(2,1)S(1)} %get-tuple-element.62.inner, ...), custom_call_target="tpu_custom_call" | custom-call | flops 1 | bytes 1 | tf_op jit(solution)/shard_map/pallas_call | solution.py:148
  13.3 0.7 collective-permute-start.2
  14.0 2.1 %shard_map.57 = bf16[4,128,256]{2,1,0:T(8,128)(2,1)S(1)} custom-call(bf16[1,128,256]{2,1,0:T(8,128)(2,1)S(1)} %get-tuple-element.71.first_low, bf16[4,128,256]{2,1,0:T(8,128)(2,1)S(1)} %get-tuple-element.69.first_mid, bf16[1,128,256]{2,1,0:T(8,128)(2,1)S(1)} %get-tuple-element.72.first_high, bf16[2,4,128,256]{3,2,1,0:T(8,128)(2,1)S(1)} %bitcast.65, ...), custom_call_target="tpu_custom_call" | custom-call | flops 1 | bytes 1 | tf_op jit(solution)/shard_map/pallas_call | solution.py:148
  16.1 0.2 fusion.10
  16.4 4.5 %collective-permute-start.5 = (bf16[3,128,256]{2,1,0:T(8,128)(2,1)S(1)}, bf16[3,128,256]{2,1,0:T(8,128)(2,1)S(1)}, u32[]{:S(2)}, u32[]{:S(2)}) collective-permute-start(bf16[3,128,256]{2,1,0:T(8,128)(2,1)S(1)} %pad_maximum_fusion.3), channel_id=1, source_target_pairs={{1,2},{2,1},{3,4},{4,3},{5,6},{6,5},{9,10},{10,9},{11,12},{12,11},... | collective-permute-start | bytes 589832 | tf_op jit(solution)/shard_map/ppermute | solution.py:202
  21.1 0.7 collective-permute-start.9
  21.8 0.7 collective-permute-start.7
  22.5 2.1 %shard_map.58 = (bf16[2,128,256]{2,1,0:T(8,128)(2,1)S(1)}, f32[4,128,256]{2,1,0:T(8,128)S(1)}) custom-call(bf16[4,128,256]{2,1,0:T(8,128)(2,1)S(1)} %get-tuple-element.106.p, bf16[4,128,256]{2,1,0:T(8,128)(2,1)S(1)} %get-tuple-element.105.q, bf16[6912,256]{1,0:T(8,128)(2,1)S(1)} %get-tuple-element.68.weights), custom_call_target="tpu_custom_call" | custom-call | flops 1 | bytes 1 | tf_op jit(solution)/shard_map/pallas_call | solution.py:148
  24.6 1.8 %shard_map.59 = (bf16[1,128,256]{2,1,0:T(8,128)(2,1)S(1)}, bf16[4,128,256]{2,1,0:T(8,128)(2,1)S(1)}, bf16[1,128,256]{2,1,0:T(8,128)(2,1)S(1)}) custom-call(s32[3]{0:T(128)S(1)} %add_convert_fusion.6.flags, bf16[4,128,256]{2,1,0:T(8,128)(2,1)S(1)} %get-tuple-element.106.p, bf16[2,128,256]{2,1,0:T(8,128)(2,1)S(1)} %get-tuple-element.75.inner, ...), custom_call_target="tpu_custom_call" | custom-call | flops 1 | bytes 1 | tf_op jit(solution)/shard_map/pallas_call | solution.py:148
  26.4 3.7 %collective-permute-start.6 = (bf16[4,128,256]{2,1,0:T(8,128)(2,1)S(1)}, bf16[4,128,256]{2,1,0:T(8,128)(2,1)S(1)}, u32[]{:S(2)}, u32[]{:S(2)}) collective-permute-start(bf16[4,128,256]{2,1,0:T(8,128)(2,1)S(1)} %get-tuple-element.77.first_mid), channel_id=1, source_target_pairs={{0,8},{8,16},{16,24},{1,9},{9,17},{17,25},{2,10},{10,18},{18,26},{... | collective-permute-start | bytes 786440 | tf_op jit(solution)/shard_map/ppermute | solution.py:238
  30.2 2.1 %shard_map.60 = bf16[4,128,256]{2,1,0:T(8,128)(2,1)S(1)} custom-call(bf16[1,128,256]{2,1,0:T(8,128)(2,1)S(1)} %get-tuple-element.79.first_low, bf16[4,128,256]{2,1,0:T(8,128)(2,1)S(1)} %get-tuple-element.77.first_mid, bf16[1,128,256]{2,1,0:T(8,128)(2,1)S(1)} %get-tuple-element.80.first_high, bf16[4,128,256]{2,1,0:T(8,128)(2,1)S(1)} %get-tuple-element.105.q, ...), custom_call_target="tpu_custom_call" | custom-call | flops 1 | bytes 1 | tf_op jit(solution)/shard_map/pallas_call | solution.py:148
  32.3 1.9 %collective-permute-start.8 = (bf16[4,128,256]{2,1,0:T(8,128)(2,1)S(1)}, bf16[4,128,256]{2,1,0:T(8,128)(2,1)S(1)}, u32[]{:S(2)}, u32[]{:S(2)}) collective-permute-start(bf16[4,128,256]{2,1,0:T(8,128)(2,1)S(1)} %shard_map.60), channel_id=1, source_target_pairs={{0,8},{8,16},{16,24},{1,9},{9,17},{17,25},{2,10},{10,18},{18,26},{... | collective-permute-start | bytes 786440 | tf_op jit(solution)/shard_map/ppermute | solution.py:238
  34.2 0.7 collective-permute-start.10
  34.9 4.8 %collective-permute-done.6 = bf16[4,128,256]{2,1,0:T(8,128)(2,1)S(1)} collective-permute-done((bf16[4,128,256]{2,1,0:T(8,128)(2,1)S(1)}, bf16[4,128,256]{2,1,0:T(8,128)(2,1)S(1)}, u32[]{:S(2)}, u32[]{:S(2)}) %collective-permute-start.6) | collective-permute-done | bytes 262176 | tf_op jit(solution)/shard_map/ppermute | solution.py:238
  39.8 5.5 %collective-permute-done.8 = bf16[4,128,256]{2,1,0:T(8,128)(2,1)S(1)} collective-permute-done((bf16[4,128,256]{2,1,0:T(8,128)(2,1)S(1)}, bf16[4,128,256]{2,1,0:T(8,128)(2,1)S(1)}, u32[]{:S(2)}, u32[]{:S(2)}) %collective-permute-start.8) | collective-permute-done | bytes 262176 | tf_op jit(solution)/shard_map/ppermute | solution.py:238
  45.5 4.5 %collective-permute-start.12 = (bf16[3,128,256]{2,1,0:T(8,128)(2,1)S(1)}, bf16[3,128,256]{2,1,0:T(8,128)(2,1)S(1)}, u32[]{:S(2)}, u32[]{:S(2)}) collective-permute-start(bf16[3,128,256]{2,1,0:T(8,128)(2,1)S(1)} %pad_maximum_fusion.5), channel_id=1, source_target_pairs={{1,2},{2,1},{3,4},{4,3},{5,6},{6,5},{9,10},{10,9},{11,12},{12,11},... | collective-permute-start | bytes 589832 | tf_op jit(solution)/shard_map/ppermute | solution.py:202
  50.1 2.1 %shard_map.61 = (bf16[2,128,256]{2,1,0:T(8,128)(2,1)S(1)}, f32[4,128,256]{2,1,0:T(8,128)S(1)}) custom-call(bf16[4,128,256]{2,1,0:T(8,128)(2,1)S(1)} %fusion.17.p, bf16[4,128,256]{2,1,0:T(8,128)(2,1)S(1)} %fusion.16.q, bf16[6912,256]{1,0:T(8,128)(2,1)S(1)} %get-tuple-element.68.weights), custom_call_target="tpu_custom_call" | custom-call | flops 1 | bytes 1 | tf_op jit(solution)/shard_map/pallas_call | solution.py:148
  52.2 0.7 collective-permute-start.14
  52.9 0.4 collective-permute-done.12.far
  53.3 1.8 %shard_map.62 = (bf16[1,128,256]{2,1,0:T(8,128)(2,1)S(1)}, bf16[4,128,256]{2,1,0:T(8,128)(2,1)S(1)}, bf16[1,128,256]{2,1,0:T(8,128)(2,1)S(1)}) custom-call(s32[3]{0:T(128)S(1)} %add_convert_fusion.6.flags, bf16[4,128,256]{2,1,0:T(8,128)(2,1)S(1)} %fusion.17.p, bf16[2,128,256]{2,1,0:T(8,128)(2,1)S(1)} %get-tuple-element.84.inner, ...), custom_call_target="tpu_custom_call" | custom-call | flops 1 | bytes 1 | tf_op jit(solution)/shard_map/pallas_call | solution.py:148
  55.1 2.2 %collective-permute-start.13 = (bf16[4,128,256]{2,1,0:T(8,128)(2,1)S(1)}, bf16[4,128,256]{2,1,0:T(8,128)(2,1)S(1)}, u32[]{:S(2)}, u32[]{:S(2)}) collective-permute-start(bf16[4,128,256]{2,1,0:T(8,128)(2,1)S(1)} %get-tuple-element.86.first_mid), channel_id=1, source_target_pairs={{0,8},{8,16},{16,24},{1,9},{9,17},{17,25},{2,10},{10,18},{18,26},{... | collective-permute-start | bytes 786440 | tf_op jit(solution)/shard_map/ppermute | solution.py:238
  57.3 2.1 %shard_map.63 = bf16[4,128,256]{2,1,0:T(8,128)(2,1)S(1)} custom-call(bf16[1,128,256]{2,1,0:T(8,128)(2,1)S(1)} %get-tuple-element.87.first_low, bf16[4,128,256]{2,1,0:T(8,128)(2,1)S(1)} %get-tuple-element.86.first_mid, bf16[1,128,256]{2,1,0:T(8,128)(2,1)S(1)} %get-tuple-element.88.first_high, bf16[4,128,256]{2,1,0:T(8,128)(2,1)S(1)} %fusion.16.q, ...), custom_call_target="tpu_custom_call" | custom-call | flops 1 | bytes 1 | tf_op jit(solution)/shard_map/pallas_call | solution.py:148
  59.4 1.9 %collective-permute-start.15 = (bf16[4,128,256]{2,1,0:T(8,128)(2,1)S(1)}, bf16[4,128,256]{2,1,0:T(8,128)(2,1)S(1)}, u32[]{:S(2)}, u32[]{:S(2)}) collective-permute-start(bf16[4,128,256]{2,1,0:T(8,128)(2,1)S(1)} %shard_map.63), channel_id=1, source_target_pairs={{0,8},{8,16},{16,24},{1,9},{9,17},{17,25},{2,10},{10,18},{18,26},{... | collective-permute-start | bytes 786440 | tf_op jit(solution)/shard_map/ppermute | solution.py:238
  61.4 0.7 collective-permute-start.16
  62.1 3.3 %collective-permute-done.13 = bf16[4,128,256]{2,1,0:T(8,128)(2,1)S(1)} collective-permute-done((bf16[4,128,256]{2,1,0:T(8,128)(2,1)S(1)}, bf16[4,128,256]{2,1,0:T(8,128)(2,1)S(1)}, u32[]{:S(2)}, u32[]{:S(2)}) %collective-permute-start.13) | collective-permute-done | bytes 262176 | tf_op jit(solution)/shard_map/ppermute | solution.py:238
  65.5 5.5 %collective-permute-done.15 = bf16[4,128,256]{2,1,0:T(8,128)(2,1)S(1)} collective-permute-done((bf16[4,128,256]{2,1,0:T(8,128)(2,1)S(1)}, bf16[4,128,256]{2,1,0:T(8,128)(2,1)S(1)}, u32[]{:S(2)}, u32[]{:S(2)}) %collective-permute-start.15) | collective-permute-done | bytes 262176 | tf_op jit(solution)/shard_map/ppermute | solution.py:238
  71.2 3.8 %collective-permute-start.18 = (bf16[3,128,256]{2,1,0:T(8,128)(2,1)S(1)}, bf16[3,128,256]{2,1,0:T(8,128)(2,1)S(1)}, u32[]{:S(2)}, u32[]{:S(2)}) collective-permute-start(bf16[3,128,256]{2,1,0:T(8,128)(2,1)S(1)} %pad_maximum_fusion.7), channel_id=1, source_target_pairs={{1,2},{2,1},{3,4},{4,3},{5,6},{6,5},{9,10},{10,9},{11,12},{12,11},... | collective-permute-start | bytes 589832 | tf_op jit(solution)/shard_map/ppermute | solution.py:202
  75.1 2.1 %shard_map.64 = (bf16[2,128,256]{2,1,0:T(8,128)(2,1)S(1)}, f32[4,128,256]{2,1,0:T(8,128)S(1)}) custom-call(bf16[4,128,256]{2,1,0:T(8,128)(2,1)S(1)} %fusion.15.p, bf16[4,128,256]{2,1,0:T(8,128)(2,1)S(1)} %fusion.14.q, bf16[6912,256]{1,0:T(8,128)(2,1)S(1)} %get-tuple-element.68.weights), custom_call_target="tpu_custom_call" | custom-call | flops 1 | bytes 1 | tf_op jit(solution)/shard_map/pallas_call | solution.py:148
  77.3 0.7 collective-permute-start.20
  78.0 0.7 collective-permute-done.18.far
  78.7 1.8 %shard_map.65 = (bf16[1,128,256]{2,1,0:T(8,128)(2,1)S(1)}, bf16[4,128,256]{2,1,0:T(8,128)(2,1)S(1)}, bf16[1,128,256]{2,1,0:T(8,128)(2,1)S(1)}) custom-call(s32[3]{0:T(128)S(1)} %add_convert_fusion.6.flags, bf16[4,128,256]{2,1,0:T(8,128)(2,1)S(1)} %fusion.15.p, bf16[2,128,256]{2,1,0:T(8,128)(2,1)S(1)} %get-tuple-element.92.inner, ...), custom_call_target="tpu_custom_call" | custom-call | flops 1 | bytes 1 | tf_op jit(solution)/shard_map/pallas_call | solution.py:148
  80.5 2.0 %collective-permute-start.19 = (bf16[4,128,256]{2,1,0:T(8,128)(2,1)S(1)}, bf16[4,128,256]{2,1,0:T(8,128)(2,1)S(1)}, u32[]{:S(2)}, u32[]{:S(2)}) collective-permute-start(bf16[4,128,256]{2,1,0:T(8,128)(2,1)S(1)} %get-tuple-element.94.first_mid), channel_id=1, source_target_pairs={{8,16},{16,24},{9,17},{17,25},{10,18},{18,26},{11,19},{19,27},{12,... | collective-permute-start | bytes 786440 | tf_op jit(solution)/shard_map/ppermute | solution.py:238
  82.4 2.1 %shard_map.66 = bf16[4,128,256]{2,1,0:T(8,128)(2,1)S(1)} custom-call(bf16[1,128,256]{2,1,0:T(8,128)(2,1)S(1)} %get-tuple-element.95.first_low, bf16[4,128,256]{2,1,0:T(8,128)(2,1)S(1)} %get-tuple-element.94.first_mid, bf16[1,128,256]{2,1,0:T(8,128)(2,1)S(1)} %get-tuple-element.96.first_high, bf16[4,128,256]{2,1,0:T(8,128)(2,1)S(1)} %fusion.14.q, ...), custom_call_target="tpu_custom_call" | custom-call | flops 1 | bytes 1 | tf_op jit(solution)/shard_map/pallas_call | solution.py:148
  84.6 1.9 %collective-permute-start.21 = (bf16[4,128,256]{2,1,0:T(8,128)(2,1)S(1)}, bf16[4,128,256]{2,1,0:T(8,128)(2,1)S(1)}, u32[]{:S(2)}, u32[]{:S(2)}) collective-permute-start(bf16[4,128,256]{2,1,0:T(8,128)(2,1)S(1)} %shard_map.66), channel_id=1, source_target_pairs={{8,16},{16,24},{9,17},{17,25},{10,18},{18,26},{11,19},{19,27},{12,... | collective-permute-start | bytes 786440 | tf_op jit(solution)/shard_map/ppermute | solution.py:238
  86.5 0.7 collective-permute-start.22
  87.2 3.2 %collective-permute-done.19 = bf16[4,128,256]{2,1,0:T(8,128)(2,1)S(1)} collective-permute-done((bf16[4,128,256]{2,1,0:T(8,128)(2,1)S(1)}, bf16[4,128,256]{2,1,0:T(8,128)(2,1)S(1)}, u32[]{:S(2)}, u32[]{:S(2)}) %collective-permute-start.19) | collective-permute-done | bytes 262176 | tf_op jit(solution)/shard_map/ppermute | solution.py:238
  90.4 5.5 %collective-permute-done.21 = bf16[4,128,256]{2,1,0:T(8,128)(2,1)S(1)} collective-permute-done((bf16[4,128,256]{2,1,0:T(8,128)(2,1)S(1)}, bf16[4,128,256]{2,1,0:T(8,128)(2,1)S(1)}, u32[]{:S(2)}, u32[]{:S(2)}) %collective-permute-start.21) | collective-permute-done | bytes 262176 | tf_op jit(solution)/shard_map/ppermute | solution.py:238
  96.2 3.7 %collective-permute-start.24 = (bf16[3,128,256]{2,1,0:T(8,128)(2,1)S(1)}, bf16[3,128,256]{2,1,0:T(8,128)(2,1)S(1)}, u32[]{:S(2)}, u32[]{:S(2)}) collective-permute-start(bf16[3,128,256]{2,1,0:T(8,128)(2,1)S(1)} %pad_maximum_fusion.9), channel_id=1, source_target_pairs={{1,2},{2,1},{3,4},{4,3},{5,6},{6,5},{9,10},{10,9},{11,12},{12,11},... | collective-permute-start | bytes 589832 | tf_op jit(solution)/shard_map/ppermute | solution.py:202
  100.1 2.1 %shard_map.67 = (bf16[2,128,256]{2,1,0:T(8,128)(2,1)S(1)}, f32[4,128,256]{2,1,0:T(8,128)S(1)}) custom-call(bf16[4,128,256]{2,1,0:T(8,128)(2,1)S(1)} %fusion.13.p, bf16[4,128,256]{2,1,0:T(8,128)(2,1)S(1)} %fusion.12.q, bf16[6912,256]{1,0:T(8,128)(2,1)S(1)} %get-tuple-element.68.weights), custom_call_target="tpu_custom_call" | custom-call | flops 1 | bytes 1 | tf_op jit(solution)/shard_map/pallas_call | solution.py:148
  102.2 1.3 %collective-permute-done.24.far = bf16[3,128,256]{2,1,0:T(8,128)(2,1)S(1)} collective-permute-done((bf16[3,128,256]{2,1,0:T(8,128)(2,1)S(1)}, bf16[3,128,256]{2,1,0:T(8,128)(2,1)S(1)}, u32[]{:S(2)}, u32[]{:S(2)}) %collective-permute-start.24) | collective-permute-done | bytes 196640 | tf_op jit(solution)/shard_map/ppermute | solution.py:202
  103.5 1.8 %shard_map.68 = (bf16[1,128,256]{2,1,0:T(8,128)(2,1)S(1)}, bf16[4,128,256]{2,1,0:T(8,128)(2,1)S(1)}, bf16[1,128,256]{2,1,0:T(8,128)(2,1)S(1)}) custom-call(s32[3]{0:T(128)S(1)} %add_convert_fusion.6.flags, bf16[4,128,256]{2,1,0:T(8,128)(2,1)S(1)} %fusion.13.p, bf16[2,128,256]{2,1,0:T(8,128)(2,1)S(1)} %get-tuple-element.100.inner, ...), custom_call_target="tpu_custom_call" | custom-call | flops 1 | bytes 1 | tf_op jit(solution)/shard_map/pallas_call | solution.py:148
  105.3 2.8 %shard_map.69 = bf16[2,4,128,256]{3,2,1,0:T(8,128)(2,1)} custom-call(bf16[1,128,256]{2,1,0:T(8,128)(2,1)S(1)} %get-tuple-element.102.first_low, bf16[4,128,256]{2,1,0:T(8,128)(2,1)S(1)} %get-tuple-element.103.first_mid, bf16[1,128,256]{2,1,0:T(8,128)(2,1)S(1)} %get-tuple-element.104.first_high, bf16[4,128,256]{2,1,0:T(8,128)(2,1)S(1)} %fusion.12.q, ...), custom_call_target="tpu_custom_call" | custom-call | flops 1 | bytes 1 | tf_op jit(solution)/shard_map/pallas_call | solution.py:148
  (51 shorter events, 1.6 us)
Async XLA Ops:
  0.0 7.3 %copy-start.1 = (bf16[1,2,4,16,8,256]{5,4,3,2,1,0:T(8,128)(2,1)S(1)}, bf16[1,2,4,16,8,256]{5,4,3,2,1,0:T(8,128)(2,1)}, u32[]{:S(2)}) copy-start(bf16[1,2,4,16,8,256]{5,4,3,2,1,0:T(8,128)(2,1)} %param.5) | copy-start | bytes 1572868
  0.1 16.0 %collective-permute-start.3 = (bf16[2,4,128,256]{3,2,1,0:T(8,128)(2,1)}, bf16[2,4,128,256]{3,2,1,0:T(8,128)(2,1)S(1)}, u32[]{:S(2)}, u32[]{:S(2)}) collective-permute-start(bf16[2,4,128,256]{3,2,1,0:T(8,128)(2,1)} %bitcast.74), channel_id=1, source_target_pairs={{0,24},{8,16},{1,25},{9,17},{2,26},{10,18},{3,27},{11,19},{4,28},{... | collective-permute-start | bytes 1572872 | tf_op jit(solution)/shard_map/ppermute | solution.py:238
  3.4 8.0 %collective-permute-start = (bf16[3,128,256]{2,1,0:T(8,128)(2,1)S(1)}, bf16[3,128,256]{2,1,0:T(8,128)(2,1)S(1)}, u32[]{:S(2)}, u32[]{:S(2)}) collective-permute-start(bf16[3,128,256]{2,1,0:T(8,128)(2,1)S(1)} %pad_maximum_fusion), channel_id=1, source_target_pairs={{0,1},{1,0},{2,3},{3,2},{4,5},{5,4},{6,7},{7,6},{8,9},{9,8},{10,11... | collective-permute-start | bytes 589832 | tf_op jit(solution)/shard_map/ppermute | solution.py:202
  4.2 7.3 %collective-permute-start.1 = (bf16[3,128,256]{2,1,0:T(8,128)(2,1)S(1)}, bf16[3,128,256]{2,1,0:T(8,128)(2,1)S(1)}, u32[]{:S(2)}, u32[]{:S(2)}) collective-permute-start(bf16[3,128,256]{2,1,0:T(8,128)(2,1)S(1)} %pad_maximum_fusion.1), channel_id=1, source_target_pairs={{1,2},{2,1},{3,4},{4,3},{5,6},{6,5},{9,10},{10,9},{11,12},{12,11},... | collective-permute-start | bytes 589832 | tf_op jit(solution)/shard_map/ppermute | solution.py:202
  11.5 2.5 %copy-start = (bf16[1,3,3,3,256,256]{5,4,3,2,1,0:T(8,128)(2,1)S(1)}, bf16[1,3,3,3,256,256]{5,4,3,2,1,0:T(8,128)(2,1)}, u32[]{:S(2)}) copy-start(bf16[1,3,3,3,256,256]{5,4,3,2,1,0:T(8,128)(2,1)} %param.9) | copy-start | bytes 10616836
  13.3 8.5 %collective-permute-start.2 = (bf16[4,128,256]{2,1,0:T(8,128)(2,1)S(1)}, bf16[4,128,256]{2,1,0:T(8,128)(2,1)S(1)}, u32[]{:S(2)}, u32[]{:S(2)}) collective-permute-start(bf16[4,128,256]{2,1,0:T(8,128)(2,1)S(1)} %get-tuple-element.69.first_mid), channel_id=1, source_target_pairs={{0,8},{1,9},{2,10},{3,11},{4,12},{5,13},{6,14},{7,15}} | collective-permute-start | bytes 786440 | tf_op jit(solution)/shard_map/ppermute | solution.py:238
  14.0 2.2 %copy-start.2 = (bf16[3,2,4,16,8,256]{5,4,3,2,1,0:T(8,128)(2,1)S(1)}, bf16[3,2,4,16,8,256]{5,4,3,2,1,0:T(8,128)(2,1)}, u32[]{:S(2)}) copy-start(bf16[3,2,4,16,8,256]{5,4,3,2,1,0:T(8,128)(2,1)} %param.7) | copy-start | bytes 4718596
  16.4 8.2 %collective-permute-start.5 = (bf16[3,128,256]{2,1,0:T(8,128)(2,1)S(1)}, bf16[3,128,256]{2,1,0:T(8,128)(2,1)S(1)}, u32[]{:S(2)}, u32[]{:S(2)}) collective-permute-start(bf16[3,128,256]{2,1,0:T(8,128)(2,1)S(1)} %pad_maximum_fusion.3), channel_id=1, source_target_pairs={{1,2},{2,1},{3,4},{4,3},{5,6},{6,5},{9,10},{10,9},{11,12},{12,11},... | collective-permute-start | bytes 589832 | tf_op jit(solution)/shard_map/ppermute | solution.py:202
  21.0 3.6 %collective-permute-start.4 = (bf16[3,128,256]{2,1,0:T(8,128)(2,1)S(1)}, bf16[3,128,256]{2,1,0:T(8,128)(2,1)S(1)}, u32[]{:S(2)}, u32[]{:S(2)}) collective-permute-start(bf16[3,128,256]{2,1,0:T(8,128)(2,1)S(1)} %pad_maximum_fusion.2), channel_id=1, source_target_pairs={{0,1},{1,0},{2,3},{3,2},{4,5},{5,4},{6,7},{7,6},{8,9},{9,8},{10,11... | collective-permute-start | bytes 589832 | tf_op jit(solution)/shard_map/ppermute | solution.py:202
  21.1 13.1 %collective-permute-start.9 = (bf16[4,128,256]{2,1,0:T(8,128)(2,1)S(1)}, bf16[4,128,256]{2,1,0:T(8,128)(2,1)S(1)}, u32[]{:S(2)}, u32[]{:S(2)}) collective-permute-start(bf16[4,128,256]{2,1,0:T(8,128)(2,1)S(1)} %shard_map.57), channel_id=1, source_target_pairs={{0,8},{1,9},{2,10},{3,11},{4,12},{5,13},{6,14},{7,15}} | collective-permute-start | bytes 786440 | tf_op jit(solution)/shard_map/ppermute | solution.py:238
  21.8 13.1 %collective-permute-start.7 = (bf16[4,128,256]{2,1,0:T(8,128)(2,1)S(1)}, bf16[4,128,256]{2,1,0:T(8,128)(2,1)S(1)}, u32[]{:S(2)}, u32[]{:S(2)}) collective-permute-start(bf16[4,128,256]{2,1,0:T(8,128)(2,1)S(1)} %collective-permute-done.2), channel_id=1, source_target_pairs={{8,24},{9,25},{10,26},{11,27},{12,28},{13,29},{14,30},{15,31}} | collective-permute-start | bytes 786440 | tf_op jit(solution)/shard_map/ppermute | solution.py:238
  26.4 13.3 %collective-permute-start.6 = (bf16[4,128,256]{2,1,0:T(8,128)(2,1)S(1)}, bf16[4,128,256]{2,1,0:T(8,128)(2,1)S(1)}, u32[]{:S(2)}, u32[]{:S(2)}) collective-permute-start(bf16[4,128,256]{2,1,0:T(8,128)(2,1)S(1)} %get-tuple-element.77.first_mid), channel_id=1, source_target_pairs={{0,8},{8,16},{16,24},{1,9},{9,17},{17,25},{2,10},{10,18},{18,26},{... | collective-permute-start | bytes 786440 | tf_op jit(solution)/shard_map/ppermute | solution.py:238
  32.3 13.0 %collective-permute-start.8 = (bf16[4,128,256]{2,1,0:T(8,128)(2,1)S(1)}, bf16[4,128,256]{2,1,0:T(8,128)(2,1)S(1)}, u32[]{:S(2)}, u32[]{:S(2)}) collective-permute-start(bf16[4,128,256]{2,1,0:T(8,128)(2,1)S(1)} %shard_map.60), channel_id=1, source_target_pairs={{0,8},{8,16},{16,24},{1,9},{9,17},{17,25},{2,10},{10,18},{18,26},{... | collective-permute-start | bytes 786440 | tf_op jit(solution)/shard_map/ppermute | solution.py:238
  34.2 11.1 %collective-permute-start.10 = (bf16[4,128,256]{2,1,0:T(8,128)(2,1)S(1)}, bf16[4,128,256]{2,1,0:T(8,128)(2,1)S(1)}, u32[]{:S(2)}, u32[]{:S(2)}) collective-permute-start(bf16[4,128,256]{2,1,0:T(8,128)(2,1)S(1)} %collective-permute-done.9), channel_id=1, source_target_pairs={{8,24},{9,25},{10,26},{11,27},{12,28},{13,29},{14,30},{15,31}} | collective-permute-start | bytes 786440 | tf_op jit(solution)/shard_map/ppermute | solution.py:238
  45.5 7.8 %collective-permute-start.12 = (bf16[3,128,256]{2,1,0:T(8,128)(2,1)S(1)}, bf16[3,128,256]{2,1,0:T(8,128)(2,1)S(1)}, u32[]{:S(2)}, u32[]{:S(2)}) collective-permute-start(bf16[3,128,256]{2,1,0:T(8,128)(2,1)S(1)} %pad_maximum_fusion.5), channel_id=1, source_target_pairs={{1,2},{2,1},{3,4},{4,3},{5,6},{6,5},{9,10},{10,9},{11,12},{12,11},... | collective-permute-start | bytes 589832 | tf_op jit(solution)/shard_map/ppermute | solution.py:202
  50.0 3.3 %collective-permute-start.11 = (bf16[3,128,256]{2,1,0:T(8,128)(2,1)S(1)}, bf16[3,128,256]{2,1,0:T(8,128)(2,1)S(1)}, u32[]{:S(2)}, u32[]{:S(2)}) collective-permute-start(bf16[3,128,256]{2,1,0:T(8,128)(2,1)S(1)} %pad_maximum_fusion.4), channel_id=1, source_target_pairs={{0,1},{1,0},{2,3},{3,2},{4,5},{5,4},{6,7},{7,6},{8,9},{9,8},{10,11... | collective-permute-start | bytes 589832 | tf_op jit(solution)/shard_map/ppermute | solution.py:202
  52.2 9.8 %collective-permute-start.14 = (bf16[4,128,256]{2,1,0:T(8,128)(2,1)S(1)}, bf16[4,128,256]{2,1,0:T(8,128)(2,1)S(1)}, u32[]{:S(2)}, u32[]{:S(2)}) collective-permute-start(bf16[4,128,256]{2,1,0:T(8,128)(2,1)S(1)} %collective-permute-done.6), channel_id=1, source_target_pairs={{8,24},{9,25},{10,26},{11,27},{12,28},{13,29},{14,30},{15,31}} | collective-permute-start | bytes 786440 | tf_op jit(solution)/shard_map/ppermute | solution.py:238
  55.1 10.3 %collective-permute-start.13 = (bf16[4,128,256]{2,1,0:T(8,128)(2,1)S(1)}, bf16[4,128,256]{2,1,0:T(8,128)(2,1)S(1)}, u32[]{:S(2)}, u32[]{:S(2)}) collective-permute-start(bf16[4,128,256]{2,1,0:T(8,128)(2,1)S(1)} %get-tuple-element.86.first_mid), channel_id=1, source_target_pairs={{0,8},{8,16},{16,24},{1,9},{9,17},{17,25},{2,10},{10,18},{18,26},{... | collective-permute-start | bytes 786440 | tf_op jit(solution)/shard_map/ppermute | solution.py:238
  59.4 11.6 %collective-permute-start.15 = (bf16[4,128,256]{2,1,0:T(8,128)(2,1)S(1)}, bf16[4,128,256]{2,1,0:T(8,128)(2,1)S(1)}, u32[]{:S(2)}, u32[]{:S(2)}) collective-permute-start(bf16[4,128,256]{2,1,0:T(8,128)(2,1)S(1)} %shard_map.63), channel_id=1, source_target_pairs={{0,8},{8,16},{16,24},{1,9},{9,17},{17,25},{2,10},{10,18},{18,26},{... | collective-permute-start | bytes 786440 | tf_op jit(solution)/shard_map/ppermute | solution.py:238
  61.4 9.6 %collective-permute-start.16 = (bf16[4,128,256]{2,1,0:T(8,128)(2,1)S(1)}, bf16[4,128,256]{2,1,0:T(8,128)(2,1)S(1)}, u32[]{:S(2)}, u32[]{:S(2)}) collective-permute-start(bf16[4,128,256]{2,1,0:T(8,128)(2,1)S(1)} %collective-permute-done.8), channel_id=1, source_target_pairs={{8,24},{9,25},{10,26},{11,27},{12,28},{13,29},{14,30},{15,31}} | collective-permute-start | bytes 786440 | tf_op jit(solution)/shard_map/ppermute | solution.py:238
  71.2 7.5 %collective-permute-start.18 = (bf16[3,128,256]{2,1,0:T(8,128)(2,1)S(1)}, bf16[3,128,256]{2,1,0:T(8,128)(2,1)S(1)}, u32[]{:S(2)}, u32[]{:S(2)}) collective-permute-start(bf16[3,128,256]{2,1,0:T(8,128)(2,1)S(1)} %pad_maximum_fusion.7), channel_id=1, source_target_pairs={{1,2},{2,1},{3,4},{4,3},{5,6},{6,5},{9,10},{10,9},{11,12},{12,11},... | collective-permute-start | bytes 589832 | tf_op jit(solution)/shard_map/ppermute | solution.py:202
  75.1 3.6 %collective-permute-start.17 = (bf16[3,128,256]{2,1,0:T(8,128)(2,1)S(1)}, bf16[3,128,256]{2,1,0:T(8,128)(2,1)S(1)}, u32[]{:S(2)}, u32[]{:S(2)}) collective-permute-start(bf16[3,128,256]{2,1,0:T(8,128)(2,1)S(1)} %pad_maximum_fusion.6), channel_id=1, source_target_pairs={{0,1},{1,0},{2,3},{3,2},{4,5},{5,4},{6,7},{7,6},{8,9},{9,8},{10,11... | collective-permute-start | bytes 589832 | tf_op jit(solution)/shard_map/ppermute | solution.py:202
  77.3 9.9 %collective-permute-start.20 = (bf16[4,128,256]{2,1,0:T(8,128)(2,1)S(1)}, bf16[4,128,256]{2,1,0:T(8,128)(2,1)S(1)}, u32[]{:S(2)}, u32[]{:S(2)}) collective-permute-start(bf16[4,128,256]{2,1,0:T(8,128)(2,1)S(1)} %collective-permute-done.13), channel_id=1, source_target_pairs={{8,24},{9,25},{10,26},{11,27},{12,28},{13,29},{14,30},{15,31}} | collective-permute-start | bytes 786440 | tf_op jit(solution)/shard_map/ppermute | solution.py:238
  80.5 9.9 %collective-permute-start.19 = (bf16[4,128,256]{2,1,0:T(8,128)(2,1)S(1)}, bf16[4,128,256]{2,1,0:T(8,128)(2,1)S(1)}, u32[]{:S(2)}, u32[]{:S(2)}) collective-permute-start(bf16[4,128,256]{2,1,0:T(8,128)(2,1)S(1)} %get-tuple-element.94.first_mid), channel_id=1, source_target_pairs={{8,16},{16,24},{9,17},{17,25},{10,18},{18,26},{11,19},{19,27},{12,... | collective-permute-start | bytes 786440 | tf_op jit(solution)/shard_map/ppermute | solution.py:238
  84.6 11.4 %collective-permute-start.21 = (bf16[4,128,256]{2,1,0:T(8,128)(2,1)S(1)}, bf16[4,128,256]{2,1,0:T(8,128)(2,1)S(1)}, u32[]{:S(2)}, u32[]{:S(2)}) collective-permute-start(bf16[4,128,256]{2,1,0:T(8,128)(2,1)S(1)} %shard_map.66), channel_id=1, source_target_pairs={{8,16},{16,24},{9,17},{17,25},{10,18},{18,26},{11,19},{19,27},{12,... | collective-permute-start | bytes 786440 | tf_op jit(solution)/shard_map/ppermute | solution.py:238
  86.5 9.5 %collective-permute-start.22 = (bf16[4,128,256]{2,1,0:T(8,128)(2,1)S(1)}, bf16[4,128,256]{2,1,0:T(8,128)(2,1)S(1)}, u32[]{:S(2)}, u32[]{:S(2)}) collective-permute-start(bf16[4,128,256]{2,1,0:T(8,128)(2,1)S(1)} %collective-permute-done.15), channel_id=1, source_target_pairs={{8,24},{9,25},{10,26},{11,27},{12,28},{13,29},{14,30},{15,31}} | collective-permute-start | bytes 786440 | tf_op jit(solution)/shard_map/ppermute | solution.py:238
  96.2 7.3 %collective-permute-start.24 = (bf16[3,128,256]{2,1,0:T(8,128)(2,1)S(1)}, bf16[3,128,256]{2,1,0:T(8,128)(2,1)S(1)}, u32[]{:S(2)}, u32[]{:S(2)}) collective-permute-start(bf16[3,128,256]{2,1,0:T(8,128)(2,1)S(1)} %pad_maximum_fusion.9), channel_id=1, source_target_pairs={{1,2},{2,1},{3,4},{4,3},{5,6},{6,5},{9,10},{10,9},{11,12},{12,11},... | collective-permute-start | bytes 589832 | tf_op jit(solution)/shard_map/ppermute | solution.py:202
  99.9 3.5 %collective-permute-start.23 = (bf16[3,128,256]{2,1,0:T(8,128)(2,1)S(1)}, bf16[3,128,256]{2,1,0:T(8,128)(2,1)S(1)}, u32[]{:S(2)}, u32[]{:S(2)}) collective-permute-start(bf16[3,128,256]{2,1,0:T(8,128)(2,1)S(1)} %pad_maximum_fusion.8), channel_id=1, source_target_pairs={{0,1},{1,0},{2,3},{3,2},{4,5},{5,4},{6,7},{7,6},{8,9},{9,8},{10,11... | collective-permute-start | bytes 589832 | tf_op jit(solution)/shard_map/ppermute | solution.py:202

commit v17 on v16

--- a/solution.py
+++ b/solution.py
@@ -70,12 +70,7 @@
     ]
 
 
-def stream(ref, number):
-    return ref.at[number] if len(ref.shape) == 4 else ref
-
-
 def own_planes(width, p, q, weights, inner, partial, even, odd, ready=None):
-    p, q = stream(p, 0), stream(q, 1)
     planes = q.shape[0]
     fill(even, odd, 0, q[...], width)
     if ready is not None:
@@ -99,7 +94,6 @@
 
 
 def edge_kernel(width, flags, p, inner, partial, near, far, weights, low, mid, high, even, odd):
-    p = stream(p, 0)
     planes = p.shape[0]
     above = flags[2] > 0
     near, far = near[...].astype(jnp.float32), far[...].astype(jnp.float32)
@@ -116,7 +110,6 @@
 
 
 def second_sum(width, first_low, first_mid, first_high, q, weights, even, odd):
-    q = stream(q, 1)
     planes = q.shape[0]
     fill(even, odd, 0, first_low[...], width)
     fill(even, odd, 1, first_mid[...], width)
@@ -161,7 +154,7 @@
 
 
 def inner_half(p, q, weights, width, load):
-    planes, voxels, chans = q.shape[-3:]
+    planes, voxels, chans = q.shape
     outputs = [((planes - 2, voxels, chans), jnp.bfloat16), ((4, voxels, chans), jnp.float32)]
     scratch = stored(planes, voxels, chans, width)
     if load:
@@ -172,7 +165,7 @@
 
 
 def first_half(flags, p, kept, halos, weights, width):
-    planes, voxels, chans = p.shape[-3:]
+    planes, voxels, chans = p.shape
     return call(
         edge_kernel,
         [((n, voxels, chans), jnp.bfloat16) for n in (1, planes, 1)],
@@ -183,7 +176,7 @@
 
 
 def second_half(first, q, weights, width, last):
-    shape = q.shape[-3:]
+    shape = q.shape
     scratch = stored(shape[0] + 2, *shape[1:], width)
     output = shape
     if last:
@@ -194,10 +187,7 @@
 
 def swap(turn, starts, *blocks):
     count = lax.axis_size("depth")
-    parts = []
-    for block, n, *number in blocks:
-        part = lax.dynamic_slice(block, (*number, starts[n][turn], 0, 0), (*[1] * len(number), n, *block.shape[-2:]))
-        parts.append(part.reshape(part.shape[-3:]))
+    parts = [lax.dynamic_slice_in_dim(block, starts[n][turn], n, axis=0) for block, n in blocks]
     pairs = [pair for i in range(turn, count - 1, 2) for pair in ((i, i + 1), (i + 1, i))]
     return lax.ppermute(jnp.concatenate(parts, axis=0), "depth", pairs)
 
@@ -253,9 +243,9 @@
             skip = jnp.where(places["direct"], direct[stream], skip)
         return jnp.where(places["first"], fresh, join(held, skip))
 
-    p = q = resident
+    p, q = resident
     mirrored = send(previous, [(j, sections - 1 - j) for j in range(half)])
-    near, far = (swap(turn, starts, (resident, 2, 1), (resident, 1, 0)) for turn in range(2))
+    near, far = (swap(turn, starts, (q, 2), (p, 1)) for turn in range(2))
     for slot in range(ticks + 1):
         if slot == 1:
             p, q, near, far = following
@@ -265,14 +255,24 @@
             q = arrived(slot, 1)
             near, far = (swap(turn, starts, (q, 2), (p, 1)) for turn in range(2))
         *kept, w_one = inner_half(p, q, w_one, width, slot == 0)
-        first = first_half(flags, p, kept, (near, far), w_one, width)
         onward = [(j, j + 1) for j in range(1, sections - 1)] if slot > 0 else []
         if slot < ticks - 1:
             onward = [(0, 1)] + onward
         received, relays = {}, {}
-        if slot < ticks:
+        if 0 < slot < ticks:
+            early = send(kept[0], onward)
+        first = first_half(flags, p, kept, (near, far), w_one, width)
+        if slot == 0:
             received[0] = send(first[1], onward)
+        elif slot < ticks:
+            late = send(jnp.concatenate([first[1][:1], first[1][-1:]], axis=0), onward)
         second = second_half(first, q, w_two, width, slot == ticks)
+        if 0 < slot < ticks:
+            relays[0] = send(newer[0], [(1, sections - 1)])
+            if slot == 1:
+                relays[0], second = lax.optimization_barrier((relays[0], second))
+            early, second = lax.optimization_barrier((early, second))
+            received[0] = jnp.concatenate([late[:1], early, late[1:]], axis=0)
         if slot < ticks:
             received[1] = send(second, onward)
         if slot == 0:
@@ -281,7 +281,7 @@
             following += tuple(swap(turn, starts, (following[1], 2), (following[0], 1)) for turn in range(2))
         elif slot < ticks:
             relay_q, second = lax.optimization_barrier((newer[1], second))
-            relays = {0: send(newer[0], [(1, sections - 1)]), 1: send(relay_q, [(1, sections - 1)])}
+            relays[1] = send(relay_q, [(1, sections - 1)])
             if across:
                 direct = {0: send(first[1], across), 1: send(second, across)}
         older, newer, relayed = newer, received, relays

time: 110 us -> 114 us (1.036)
  starting transfers between devices: 41.2 us -> 50.1 us
  waiting for transfers between devices: 30.2 us -> 26.1 us
    ppermute x15 -> x18, starting transfers between devices: 20.5 us -> 29.3 us  [send(): return lax.ppermute(block, 'section', pairs) if pairs else block]
    ppermute x15 -> x18, waiting for transfers between devices: 27.8 us -> 24 us  [send(): return lax.ppermute(block, 'section', pairs) if pairs else block]
    reshape x2 -> x0, local copies, waits for them, and re-layouts: 1.88 us -> none  [swap(): parts.append(part.reshape(part.shape[-3:]))]
  transfers between devices with their start and end apart: 25 -> 28, of which waited for: 10 -> 9; matrix products, arithmetic and copies ran while one was open for 2% -> 2% of each run, Pallas kernels for 26% -> 25%
where the time goes in v17:
time: 114 us; the launch traced here: 113 us
  starting transfers between devices  50.1 us (44%)
  Pallas kernels  32.9 us (29%)
  waiting for transfers between devices  26.1 us (23%)
  local copies, waits for them, and re-layouts  1.35 us (1%)
  other arithmetic  1.28 us (1%)
    pallas_call x15, Pallas kernels, call(): pl.pallas_call(functools.partial(kernel, width), out_shape=[jax.ShapeDtyp...  32.9 us
    ppermute x18, starting transfers between devices, send(): return lax.ppermute(block, 'section', pairs) if pairs else block  29.3 us
    ppermute x18, waiting for transfers between devices, send(): return lax.ppermute(block, 'section', pairs) if pairs else block  24 us
    ppermute x10, starting transfers between devices, swap(): return lax.ppermute(jnp.concatenate(parts, axis=0), 'depth', pairs)  20.9 us
  transfers between devices with their start and end apart: 28, of which 9 were waited for; matrix products, arithmetic and copies ran while one was open for 2% of the time, Pallas kernels for 25%

profile of v17, /device:TPU:13, one launch (start us, length us, event | category | flops | bytes accessed | tf_op | source)
XLA Modules:
  0.0 112.6 jit_solution(10587433221520242574)
XLA Ops:
  0.1 1.3 %collective-permute-start.3 = (bf16[2,4,128,256]{3,2,1,0:T(8,128)(2,1)}, bf16[2,4,128,256]{3,2,1,0:T(8,128)(2,1)S(1)}, u32[]{:S(2)}, u32[]{:S(2)}) collective-permute-start(bf16[2,4,128,256]{3,2,1,0:T(8,128)(2,1)} %bitcast.63), channel_id=1, source_target_pairs={{0,24},{8,16},{1,25},{9,17},{2,26},{10,18},{3,27},{11,19},{4,28},{... | collective-permute-start | bytes 1572872 | tf_op jit(solution)/shard_map/ppermute | solution.py:228
  1.4 1.1 slice_bitcast_fusion.6
  2.5 0.7 collective-permute-start
  3.3 3.1 %collective-permute-start.1 = (bf16[3,128,256]{2,1,0:T(8,128)(2,1)S(1)}, bf16[3,128,256]{2,1,0:T(8,128)(2,1)S(1)}, u32[]{:S(2)}, u32[]{:S(2)}) collective-permute-start(bf16[3,128,256]{2,1,0:T(8,128)(2,1)S(1)} %pad_maximum_fusion.4), channel_id=1, source_target_pairs={{1,2},{2,1},{3,4},{4,3},{5,6},{6,5},{9,10},{10,9},{11,12},{12,11},... | collective-permute-start | bytes 589832 | tf_op jit(solution)/shard_map/ppermute | solution.py:192
  6.4 4.1 %shard_map.55 = (bf16[2,128,256]{2,1,0:T(8,128)(2,1)S(1)}, f32[4,128,256]{2,1,0:T(8,128)S(1)}, bf16[6912,256]{1,0:T(8,128)(2,1)S(1)}) custom-call(bf16[4,128,256]{2,1,0:T(8,128)(2,1)S(1)} %get-tuple-element.124.p, bf16[4,128,256]{2,1,0:T(8,128)(2,1)S(1)} %get-tuple-element.123.q, bf16[6912,256]{1,0:T(8,128)(2,1)} %bitcast.55), custom_call_target="tpu_custom_call" | custom-call | flops 1 | bytes 1 | tf_op jit(solution)/shard_map/pallas_call | solution.py:141
  10.6 1.8 %shard_map.56 = (bf16[1,128,256]{2,1,0:T(8,128)(2,1)S(1)}, bf16[4,128,256]{2,1,0:T(8,128)(2,1)S(1)}, bf16[1,128,256]{2,1,0:T(8,128)(2,1)S(1)}) custom-call(s32[3]{0:T(128)S(1)} %add_convert_fusion.6.flags, bf16[4,128,256]{2,1,0:T(8,128)(2,1)S(1)} %get-tuple-element.124.p, bf16[2,128,256]{2,1,0:T(8,128)(2,1)S(1)} %get-tuple-element.70.inner, ...), custom_call_target="tpu_custom_call" | custom-call | flops 1 | bytes 1 | tf_op jit(solution)/shard_map/pallas_call | solution.py:141
  12.4 0.7 collective-permute-start.2
  13.1 2.1 %shard_map.57 = bf16[4,128,256]{2,1,0:T(8,128)(2,1)S(1)} custom-call(bf16[1,128,256]{2,1,0:T(8,128)(2,1)S(1)} %get-tuple-element.79.first_low, bf16[4,128,256]{2,1,0:T(8,128)(2,1)S(1)} %get-tuple-element.77.first_mid, bf16[1,128,256]{2,1,0:T(8,128)(2,1)S(1)} %get-tuple-element.80.first_high, bf16[4,128,256]{2,1,0:T(8,128)(2,1)S(1)} %get-tuple-element.123.q, ...), custom_call_target="tpu_custom_call" | custom-call | flops 1 | bytes 1 | tf_op jit(solution)/shard_map/pallas_call | solution.py:141
  16.2 1.6 %collective-permute-start.4 = (bf16[3,128,256]{2,1,0:T(8,128)(2,1)S(1)}, bf16[3,128,256]{2,1,0:T(8,128)(2,1)S(1)}, u32[]{:S(2)}, u32[]{:S(2)}) collective-permute-start(bf16[3,128,256]{2,1,0:T(8,128)(2,1)S(1)} %pad_maximum_fusion.5), channel_id=1, source_target_pairs={{0,1},{1,0},{2,3},{3,2},{4,5},{5,4},{6,7},{7,6},{8,9},{9,8},{10,11... | collective-permute-start | bytes 589832 | tf_op jit(solution)/shard_map/ppermute | solution.py:192
  17.8 3.1 %collective-permute-start.5 = (bf16[3,128,256]{2,1,0:T(8,128)(2,1)S(1)}, bf16[3,128,256]{2,1,0:T(8,128)(2,1)S(1)}, u32[]{:S(2)}, u32[]{:S(2)}) collective-permute-start(bf16[3,128,256]{2,1,0:T(8,128)(2,1)S(1)} %pad_maximum_fusion.6), channel_id=1, source_target_pairs={{1,2},{2,1},{3,4},{4,3},{5,6},{6,5},{9,10},{10,9},{11,12},{12,11},... | collective-permute-start | bytes 589832 | tf_op jit(solution)/shard_map/ppermute | solution.py:192
  20.9 0.7 collective-permute-start.10
  21.6 0.7 collective-permute-start.8
  22.3 2.1 %shard_map.58 = (bf16[2,128,256]{2,1,0:T(8,128)(2,1)S(1)}, f32[4,128,256]{2,1,0:T(8,128)S(1)}) custom-call(bf16[4,128,256]{2,1,0:T(8,128)(2,1)S(1)} %get-tuple-element.122.p, bf16[4,128,256]{2,1,0:T(8,128)(2,1)S(1)} %get-tuple-element.121.q, bf16[6912,256]{1,0:T(8,128)(2,1)S(1)} %get-tuple-element.76.weights), custom_call_target="tpu_custom_call" | custom-call | flops 1 | bytes 1 | tf_op jit(solution)/shard_map/pallas_call | solution.py:141
  24.5 3.7 %collective-permute-start.7 = (bf16[2,128,256]{2,1,0:T(8,128)(2,1)S(1)}, bf16[2,128,256]{2,1,0:T(8,128)(2,1)S(1)}, u32[]{:S(2)}, u32[]{:S(2)}) collective-permute-start(bf16[2,128,256]{2,1,0:T(8,128)(2,1)S(1)} %get-tuple-element.83.inner), channel_id=1, source_target_pairs={{0,8},{8,16},{16,24},{1,9},{9,17},{17,25},{2,10},{10,18},{18,26},{... | collective-permute-start | bytes 393224 | tf_op jit(solution)/shard_map/ppermute | solution.py:228
  28.2 1.8 %shard_map.59 = (bf16[1,128,256]{2,1,0:T(8,128)(2,1)S(1)}, bf16[4,128,256]{2,1,0:T(8,128)(2,1)S(1)}, bf16[1,128,256]{2,1,0:T(8,128)(2,1)S(1)}) custom-call(s32[3]{0:T(128)S(1)} %add_convert_fusion.6.flags, bf16[4,128,256]{2,1,0:T(8,128)(2,1)S(1)} %get-tuple-element.122.p, bf16[2,128,256]{2,1,0:T(8,128)(2,1)S(1)} %get-tuple-element.83.inner, ...), custom_call_target="tpu_custom_call" | custom-call | flops 1 | bytes 1 | tf_op jit(solution)/shard_map/pallas_call | solution.py:141
  30.1 1.9 %collective-permute-start.6 = (bf16[2,128,256]{2,1,0:T(8,128)(2,1)S(1)}, bf16[2,128,256]{2,1,0:T(8,128)(2,1)S(1)}, u32[]{:S(2)}, u32[]{:S(2)}) collective-permute-start(bf16[2,128,256]{2,1,0:T(8,128)(2,1)S(1)} %pad_maximum_fusion.13), channel_id=1, source_target_pairs={{0,8},{8,16},{16,24},{1,9},{9,17},{17,25},{2,10},{10,18},{18,26},{... | collective-permute-start | bytes 393224 | tf_op jit(solution)/shard_map/ppermute | solution.py:228
  32.0 2.1 %shard_map.60 = bf16[4,128,256]{2,1,0:T(8,128)(2,1)S(1)} custom-call(bf16[1,128,256]{2,1,0:T(8,128)(2,1)S(1)} %get-tuple-element.86.first_low, bf16[4,128,256]{2,1,0:T(8,128)(2,1)S(1)} %get-tuple-element.85.first_mid, bf16[1,128,256]{2,1,0:T(8,128)(2,1)S(1)} %get-tuple-element.87.first_high, bf16[4,128,256]{2,1,0:T(8,128)(2,1)S(1)} %get-tuple-element.121.q, ...), custom_call_target="tpu_custom_call" | custom-call | flops 1 | bytes 1 | tf_op jit(solution)/shard_map/pallas_call | solution.py:141
  34.2 1.9 %collective-permute-start.9 = (bf16[4,128,256]{2,1,0:T(8,128)(2,1)S(1)}, bf16[4,128,256]{2,1,0:T(8,128)(2,1)S(1)}, u32[]{:S(2)}, u32[]{:S(2)}) collective-permute-start(bf16[4,128,256]{2,1,0:T(8,128)(2,1)S(1)} %shard_map.60), channel_id=1, source_target_pairs={{0,8},{8,16},{16,24},{1,9},{9,17},{17,25},{2,10},{10,18},{18,26},{... | collective-permute-start | bytes 786440 | tf_op jit(solution)/shard_map/ppermute | solution.py:228
  36.1 0.7 collective-permute-start.11
  36.8 1.2 %collective-permute-done.6 = bf16[2,128,256]{2,1,0:T(8,128)(2,1)S(1)} collective-permute-done((bf16[2,128,256]{2,1,0:T(8,128)(2,1)S(1)}, bf16[2,128,256]{2,1,0:T(8,128)(2,1)S(1)}, u32[]{:S(2)}, u32[]{:S(2)}) %collective-permute-start.6) | collective-permute-done | bytes 131104 | tf_op jit(solution)/shard_map/ppermute | solution.py:228
  38.1 6.2 %collective-permute-done.9 = bf16[4,128,256]{2,1,0:T(8,128)(2,1)S(1)} collective-permute-done((bf16[4,128,256]{2,1,0:T(8,128)(2,1)S(1)}, bf16[4,128,256]{2,1,0:T(8,128)(2,1)S(1)}, u32[]{:S(2)}, u32[]{:S(2)}) %collective-permute-start.9) | collective-permute-done | bytes 262176 | tf_op jit(solution)/shard_map/ppermute | solution.py:228
  44.5 1.8 %collective-permute-start.12 = (bf16[3,128,256]{2,1,0:T(8,128)(2,1)S(1)}, bf16[3,128,256]{2,1,0:T(8,128)(2,1)S(1)}, u32[]{:S(2)}, u32[]{:S(2)}) collective-permute-start(bf16[3,128,256]{2,1,0:T(8,128)(2,1)S(1)} %pad_maximum_fusion.7), channel_id=1, source_target_pairs={{0,1},{1,0},{2,3},{3,2},{4,5},{5,4},{6,7},{7,6},{8,9},{9,8},{10,11... | collective-permute-start | bytes 589832 | tf_op jit(solution)/shard_map/ppermute | solution.py:192
  46.3 3.3 %collective-permute-start.13 = (bf16[3,128,256]{2,1,0:T(8,128)(2,1)S(1)}, bf16[3,128,256]{2,1,0:T(8,128)(2,1)S(1)}, u32[]{:S(2)}, u32[]{:S(2)}) collective-permute-start(bf16[3,128,256]{2,1,0:T(8,128)(2,1)S(1)} %pad_maximum_fusion.8), channel_id=1, source_target_pairs={{1,2},{2,1},{3,4},{4,3},{5,6},{6,5},{9,10},{10,9},{11,12},{12,11},... | collective-permute-start | bytes 589832 | tf_op jit(solution)/shard_map/ppermute | solution.py:192
  49.7 2.1 %shard_map.61 = (bf16[2,128,256]{2,1,0:T(8,128)(2,1)S(1)}, f32[4,128,256]{2,1,0:T(8,128)S(1)}) custom-call(bf16[4,128,256]{2,1,0:T(8,128)(2,1)S(1)} %get-tuple-element.93.p, bf16[4,128,256]{2,1,0:T(8,128)(2,1)S(1)} %fusion.16.q, bf16[6912,256]{1,0:T(8,128)(2,1)S(1)} %get-tuple-element.76.weights), custom_call_target="tpu_custom_call" | custom-call | flops 1 | bytes 1 | tf_op jit(solution)/shard_map/pallas_call | solution.py:141
  51.8 3.5 %collective-permute-start.15 = (bf16[2,128,256]{2,1,0:T(8,128)(2,1)S(1)}, bf16[2,128,256]{2,1,0:T(8,128)(2,1)S(1)}, u32[]{:S(2)}, u32[]{:S(2)}) collective-permute-start(bf16[2,128,256]{2,1,0:T(8,128)(2,1)S(1)} %get-tuple-element.96.inner), channel_id=1, source_target_pairs={{0,8},{8,16},{16,24},{1,9},{9,17},{17,25},{2,10},{10,18},{18,26},{... | collective-permute-start | bytes 393224 | tf_op jit(solution)/shard_map/ppermute | solution.py:228
  55.3 1.8 %shard_map.62 = (bf16[1,128,256]{2,1,0:T(8,128)(2,1)S(1)}, bf16[4,128,256]{2,1,0:T(8,128)(2,1)S(1)}, bf16[1,128,256]{2,1,0:T(8,128)(2,1)S(1)}) custom-call(s32[3]{0:T(128)S(1)} %add_convert_fusion.6.flags, bf16[4,128,256]{2,1,0:T(8,128)(2,1)S(1)} %get-tuple-element.93.p, bf16[2,128,256]{2,1,0:T(8,128)(2,1)S(1)} %get-tuple-element.96.inner, ...), custom_call_target="tpu_custom_call" | custom-call | flops 1 | bytes 1 | tf_op jit(solution)/shard_map/pallas_call | solution.py:141
  57.1 1.9 %collective-permute-start.14 = (bf16[2,128,256]{2,1,0:T(8,128)(2,1)S(1)}, bf16[2,128,256]{2,1,0:T(8,128)(2,1)S(1)}, u32[]{:S(2)}, u32[]{:S(2)}) collective-permute-start(bf16[2,128,256]{2,1,0:T(8,128)(2,1)S(1)} %pad_maximum_fusion.14), channel_id=1, source_target_pairs={{0,8},{8,16},{16,24},{1,9},{9,17},{17,25},{2,10},{10,18},{18,26},{... | collective-permute-start | bytes 393224 | tf_op jit(solution)/shard_map/ppermute | solution.py:228
  59.1 0.7 collective-permute-start.16
  59.8 2.1 %shard_map.63 = bf16[4,128,256]{2,1,0:T(8,128)(2,1)S(1)} custom-call(bf16[1,128,256]{2,1,0:T(8,128)(2,1)S(1)} %get-tuple-element.99.first_low, bf16[4,128,256]{2,1,0:T(8,128)(2,1)S(1)} %get-tuple-element.98.first_mid, bf16[1,128,256]{2,1,0:T(8,128)(2,1)S(1)} %get-tuple-element.100.first_high, bf16[4,128,256]{2,1,0:T(8,128)(2,1)S(1)} %fusion.16.q, ...), custom_call_target="tpu_custom_call" | custom-call | flops 1 | bytes 1 | tf_op jit(solution)/shard_map/pallas_call | solution.py:141
  61.9 1.9 %collective-permute-start.17 = (bf16[4,128,256]{2,1,0:T(8,128)(2,1)S(1)}, bf16[4,128,256]{2,1,0:T(8,128)(2,1)S(1)}, u32[]{:S(2)}, u32[]{:S(2)}) collective-permute-start(bf16[4,128,256]{2,1,0:T(8,128)(2,1)S(1)} %shard_map.63), channel_id=1, source_target_pairs={{0,8},{8,16},{16,24},{1,9},{9,17},{17,25},{2,10},{10,18},{18,26},{... | collective-permute-start | bytes 786440 | tf_op jit(solution)/shard_map/ppermute | solution.py:228
  63.8 0.7 collective-permute-start.18
  64.9 8.2 %collective-permute-done.17 = bf16[4,128,256]{2,1,0:T(8,128)(2,1)S(1)} collective-permute-done((bf16[4,128,256]{2,1,0:T(8,128)(2,1)S(1)}, bf16[4,128,256]{2,1,0:T(8,128)(2,1)S(1)}, u32[]{:S(2)}, u32[]{:S(2)}) %collective-permute-start.17) | collective-permute-done | bytes 262176 | tf_op jit(solution)/shard_map/ppermute | solution.py:228
  73.7 2.7 %collective-permute-start.20 = (bf16[3,128,256]{2,1,0:T(8,128)(2,1)S(1)}, bf16[3,128,256]{2,1,0:T(8,128)(2,1)S(1)}, u32[]{:S(2)}, u32[]{:S(2)}) collective-permute-start(bf16[3,128,256]{2,1,0:T(8,128)(2,1)S(1)} %pad_maximum_fusion.10), channel_id=1, source_target_pairs={{1,2},{2,1},{3,4},{4,3},{5,6},{6,5},{9,10},{10,9},{11,12},{12,11},... | collective-permute-start | bytes 589832 | tf_op jit(solution)/shard_map/ppermute | solution.py:192
  76.4 2.1 %shard_map.64 = (bf16[2,128,256]{2,1,0:T(8,128)(2,1)S(1)}, f32[4,128,256]{2,1,0:T(8,128)S(1)}) custom-call(bf16[4,128,256]{2,1,0:T(8,128)(2,1)S(1)} %get-tuple-element.103.p, bf16[4,128,256]{2,1,0:T(8,128)(2,1)S(1)} %fusion.14.q, bf16[6912,256]{1,0:T(8,128)(2,1)S(1)} %get-tuple-element.76.weights), custom_call_target="tpu_custom_call" | custom-call | flops 1 | bytes 1 | tf_op jit(solution)/shard_map/pallas_call | solution.py:141
  78.6 3.5 %collective-permute-start.22 = (bf16[2,128,256]{2,1,0:T(8,128)(2,1)S(1)}, bf16[2,128,256]{2,1,0:T(8,128)(2,1)S(1)}, u32[]{:S(2)}, u32[]{:S(2)}) collective-permute-start(bf16[2,128,256]{2,1,0:T(8,128)(2,1)S(1)} %get-tuple-element.106.inner), channel_id=1, source_target_pairs={{8,16},{16,24},{9,17},{17,25},{10,18},{18,26},{11,19},{19,27},{12,... | collective-permute-start | bytes 393224 | tf_op jit(solution)/shard_map/ppermute | solution.py:228
  82.1 1.8 %shard_map.65 = (bf16[1,128,256]{2,1,0:T(8,128)(2,1)S(1)}, bf16[4,128,256]{2,1,0:T(8,128)(2,1)S(1)}, bf16[1,128,256]{2,1,0:T(8,128)(2,1)S(1)}) custom-call(s32[3]{0:T(128)S(1)} %add_convert_fusion.6.flags, bf16[4,128,256]{2,1,0:T(8,128)(2,1)S(1)} %get-tuple-element.103.p, bf16[2,128,256]{2,1,0:T(8,128)(2,1)S(1)} %get-tuple-element.106.inner, ...), custom_call_target="tpu_custom_call" | custom-call | flops 1 | bytes 1 | tf_op jit(solution)/shard_map/pallas_call | solution.py:141
  84.0 2.2 %collective-permute-start.21 = (bf16[2,128,256]{2,1,0:T(8,128)(2,1)S(1)}, bf16[2,128,256]{2,1,0:T(8,128)(2,1)S(1)}, u32[]{:S(2)}, u32[]{:S(2)}) collective-permute-start(bf16[2,128,256]{2,1,0:T(8,128)(2,1)S(1)} %pad_maximum_fusion.15), channel_id=1, source_target_pairs={{8,16},{16,24},{9,17},{17,25},{10,18},{18,26},{11,19},{19,27},{12,... | collective-permute-start | bytes 393224 | tf_op jit(solution)/shard_map/ppermute | solution.py:228
  86.2 0.7 collective-permute-start.23
  86.9 2.1 %shard_map.66 = bf16[4,128,256]{2,1,0:T(8,128)(2,1)S(1)} custom-call(bf16[1,128,256]{2,1,0:T(8,128)(2,1)S(1)} %get-tuple-element.109.first_low, bf16[4,128,256]{2,1,0:T(8,128)(2,1)S(1)} %get-tuple-element.108.first_mid, bf16[1,128,256]{2,1,0:T(8,128)(2,1)S(1)} %get-tuple-element.110.first_high, bf16[4,128,256]{2,1,0:T(8,128)(2,1)S(1)} %fusion.14.q, ...), custom_call_target="tpu_custom_call" | custom-call | flops 1 | bytes 1 | tf_op jit(solution)/shard_map/pallas_call | solution.py:141
  89.0 1.9 %collective-permute-start.24 = (bf16[4,128,256]{2,1,0:T(8,128)(2,1)S(1)}, bf16[4,128,256]{2,1,0:T(8,128)(2,1)S(1)}, u32[]{:S(2)}, u32[]{:S(2)}) collective-permute-start(bf16[4,128,256]{2,1,0:T(8,128)(2,1)S(1)} %shard_map.66), channel_id=1, source_target_pairs={{8,16},{16,24},{9,17},{17,25},{10,18},{18,26},{11,19},{19,27},{12,... | collective-permute-start | bytes 786440 | tf_op jit(solution)/shard_map/ppermute | solution.py:228
  91.0 0.7 collective-permute-start.25
  92.3 7.1 %collective-permute-done.24 = bf16[4,128,256]{2,1,0:T(8,128)(2,1)S(1)} collective-permute-done((bf16[4,128,256]{2,1,0:T(8,128)(2,1)S(1)}, bf16[4,128,256]{2,1,0:T(8,128)(2,1)S(1)}, u32[]{:S(2)}, u32[]{:S(2)}) %collective-permute-start.24) | collective-permute-done | bytes 262176 | tf_op jit(solution)/shard_map/ppermute | solution.py:228
  99.6 1.3 %collective-permute-start.26 = (bf16[3,128,256]{2,1,0:T(8,128)(2,1)S(1)}, bf16[3,128,256]{2,1,0:T(8,128)(2,1)S(1)}, u32[]{:S(2)}, u32[]{:S(2)}) collective-permute-start(bf16[3,128,256]{2,1,0:T(8,128)(2,1)S(1)} %pad_maximum_fusion.11), channel_id=1, source_target_pairs={{0,1},{1,0},{2,3},{3,2},{4,5},{5,4},{6,7},{7,6},{8,9},{9,8},{10,11... | collective-permute-start | bytes 589832 | tf_op jit(solution)/shard_map/ppermute | solution.py:192
  100.8 2.8 %collective-permute-start.27 = (bf16[3,128,256]{2,1,0:T(8,128)(2,1)S(1)}, bf16[3,128,256]{2,1,0:T(8,128)(2,1)S(1)}, u32[]{:S(2)}, u32[]{:S(2)}) collective-permute-start(bf16[3,128,256]{2,1,0:T(8,128)(2,1)S(1)} %pad_maximum_fusion.12), channel_id=1, source_target_pairs={{1,2},{2,1},{3,4},{4,3},{5,6},{6,5},{9,10},{10,9},{11,12},{12,11},... | collective-permute-start | bytes 589832 | tf_op jit(solution)/shard_map/ppermute | solution.py:192
  103.6 2.1 %shard_map.67 = (bf16[2,128,256]{2,1,0:T(8,128)(2,1)S(1)}, f32[4,128,256]{2,1,0:T(8,128)S(1)}) custom-call(bf16[4,128,256]{2,1,0:T(8,128)(2,1)S(1)} %fusion.13.p, bf16[4,128,256]{2,1,0:T(8,128)(2,1)S(1)} %fusion.12.q, bf16[6912,256]{1,0:T(8,128)(2,1)S(1)} %get-tuple-element.76.weights), custom_call_target="tpu_custom_call" | custom-call | flops 1 | bytes 1 | tf_op jit(solution)/shard_map/pallas_call | solution.py:141
  105.8 2.0 %collective-permute-done.27.far = bf16[3,128,256]{2,1,0:T(8,128)(2,1)S(1)} collective-permute-done((bf16[3,128,256]{2,1,0:T(8,128)(2,1)S(1)}, bf16[3,128,256]{2,1,0:T(8,128)(2,1)S(1)}, u32[]{:S(2)}, u32[]{:S(2)}) %collective-permute-start.27) | collective-permute-done | bytes 196640 | tf_op jit(solution)/shard_map/ppermute | solution.py:192
  107.8 1.8 %shard_map.68 = (bf16[1,128,256]{2,1,0:T(8,128)(2,1)S(1)}, bf16[4,128,256]{2,1,0:T(8,128)(2,1)S(1)}, bf16[1,128,256]{2,1,0:T(8,128)(2,1)S(1)}) custom-call(s32[3]{0:T(128)S(1)} %add_convert_fusion.6.flags, bf16[4,128,256]{2,1,0:T(8,128)(2,1)S(1)} %fusion.13.p, bf16[2,128,256]{2,1,0:T(8,128)(2,1)S(1)} %get-tuple-element.116.inner, ...), custom_call_target="tpu_custom_call" | custom-call | flops 1 | bytes 1 | tf_op jit(solution)/shard_map/pallas_call | solution.py:141
  109.6 2.8 %shard_map.69 = bf16[2,4,128,256]{3,2,1,0:T(8,128)(2,1)} custom-call(bf16[1,128,256]{2,1,0:T(8,128)(2,1)S(1)} %get-tuple-element.118.first_low, bf16[4,128,256]{2,1,0:T(8,128)(2,1)S(1)} %get-tuple-element.119.first_mid, bf16[1,128,256]{2,1,0:T(8,128)(2,1)S(1)} %get-tuple-element.120.first_high, bf16[4,128,256]{2,1,0:T(8,128)(2,1)S(1)} %fusion.12.q, ...), custom_call_target="tpu_custom_call" | custom-call | flops 1 | bytes 1 | tf_op jit(solution)/shard_map/pallas_call | solution.py:141
  (67 shorter events, 3.5 us)
Async XLA Ops:
  0.1 15.8 %collective-permute-start.3 = (bf16[2,4,128,256]{3,2,1,0:T(8,128)(2,1)}, bf16[2,4,128,256]{3,2,1,0:T(8,128)(2,1)S(1)}, u32[]{:S(2)}, u32[]{:S(2)}) collective-permute-start(bf16[2,4,128,256]{3,2,1,0:T(8,128)(2,1)} %bitcast.63), channel_id=1, source_target_pairs={{0,24},{8,16},{1,25},{9,17},{2,26},{10,18},{3,27},{11,19},{4,28},{... | collective-permute-start | bytes 1572872 | tf_op jit(solution)/shard_map/ppermute | solution.py:228
  2.5 7.9 %collective-permute-start = (bf16[3,128,256]{2,1,0:T(8,128)(2,1)S(1)}, bf16[3,128,256]{2,1,0:T(8,128)(2,1)S(1)}, u32[]{:S(2)}, u32[]{:S(2)}) collective-permute-start(bf16[3,128,256]{2,1,0:T(8,128)(2,1)S(1)} %pad_maximum_fusion.3), channel_id=1, source_target_pairs={{0,1},{1,0},{2,3},{3,2},{4,5},{5,4},{6,7},{7,6},{8,9},{9,8},{10,11... | collective-permute-start | bytes 589832 | tf_op jit(solution)/shard_map/ppermute | solution.py:192
  3.3 7.3 %collective-permute-start.1 = (bf16[3,128,256]{2,1,0:T(8,128)(2,1)S(1)}, bf16[3,128,256]{2,1,0:T(8,128)(2,1)S(1)}, u32[]{:S(2)}, u32[]{:S(2)}) collective-permute-start(bf16[3,128,256]{2,1,0:T(8,128)(2,1)S(1)} %pad_maximum_fusion.4), channel_id=1, source_target_pairs={{1,2},{2,1},{3,4},{4,3},{5,6},{6,5},{9,10},{10,9},{11,12},{12,11},... | collective-permute-start | bytes 589832 | tf_op jit(solution)/shard_map/ppermute | solution.py:192
  10.6 2.5 %copy-start = (bf16[1,3,3,3,256,256]{5,4,3,2,1,0:T(8,128)(2,1)S(1)}, bf16[1,3,3,3,256,256]{5,4,3,2,1,0:T(8,128)(2,1)}, u32[]{:S(2)}) copy-start(bf16[1,3,3,3,256,256]{5,4,3,2,1,0:T(8,128)(2,1)} %param.9) | copy-start | bytes 10616836
  12.4 9.3 %collective-permute-start.2 = (bf16[4,128,256]{2,1,0:T(8,128)(2,1)S(1)}, bf16[4,128,256]{2,1,0:T(8,128)(2,1)S(1)}, u32[]{:S(2)}, u32[]{:S(2)}) collective-permute-start(bf16[4,128,256]{2,1,0:T(8,128)(2,1)S(1)} %get-tuple-element.77.first_mid), channel_id=1, source_target_pairs={{0,8},{1,9},{2,10},{3,11},{4,12},{5,13},{6,14},{7,15}} | collective-permute-start | bytes 786440 | tf_op jit(solution)/shard_map/ppermute | solution.py:228
  13.1 2.8 %copy-start.1 = (bf16[3,2,4,16,8,256]{5,4,3,2,1,0:T(8,128)(2,1)S(1)}, bf16[3,2,4,16,8,256]{5,4,3,2,1,0:T(8,128)(2,1)}, u32[]{:S(2)}) copy-start(bf16[3,2,4,16,8,256]{5,4,3,2,1,0:T(8,128)(2,1)} %param.7) | copy-start | bytes 4718596
  13.1 2.8 %copy-start.2 = (bf16[1,2,4,16,8,256]{5,4,3,2,1,0:T(8,128)(2,1)S(1)}, bf16[1,2,4,16,8,256]{5,4,3,2,1,0:T(8,128)(2,1)}, u32[]{:S(2)}) copy-start(bf16[1,2,4,16,8,256]{5,4,3,2,1,0:T(8,128)(2,1)} %param.5) | copy-start | bytes 1572868
  16.2 12.0 %collective-permute-start.4 = (bf16[3,128,256]{2,1,0:T(8,128)(2,1)S(1)}, bf16[3,128,256]{2,1,0:T(8,128)(2,1)S(1)}, u32[]{:S(2)}, u32[]{:S(2)}) collective-permute-start(bf16[3,128,256]{2,1,0:T(8,128)(2,1)S(1)} %pad_maximum_fusion.5), channel_id=1, source_target_pairs={{0,1},{1,0},{2,3},{3,2},{4,5},{5,4},{6,7},{7,6},{8,9},{9,8},{10,11... | collective-permute-start | bytes 589832 | tf_op jit(solution)/shard_map/ppermute | solution.py:192
  17.8 10.4 %collective-permute-start.5 = (bf16[3,128,256]{2,1,0:T(8,128)(2,1)S(1)}, bf16[3,128,256]{2,1,0:T(8,128)(2,1)S(1)}, u32[]{:S(2)}, u32[]{:S(2)}) collective-permute-start(bf16[3,128,256]{2,1,0:T(8,128)(2,1)S(1)} %pad_maximum_fusion.6), channel_id=1, source_target_pairs={{1,2},{2,1},{3,4},{4,3},{5,6},{6,5},{9,10},{10,9},{11,12},{12,11},... | collective-permute-start | bytes 589832 | tf_op jit(solution)/shard_map/ppermute | solution.py:192
  20.9 15.1 %collective-permute-start.10 = (bf16[4,128,256]{2,1,0:T(8,128)(2,1)S(1)}, bf16[4,128,256]{2,1,0:T(8,128)(2,1)S(1)}, u32[]{:S(2)}, u32[]{:S(2)}) collective-permute-start(bf16[4,128,256]{2,1,0:T(8,128)(2,1)S(1)} %shard_map.57), channel_id=1, source_target_pairs={{0,8},{1,9},{2,10},{3,11},{4,12},{5,13},{6,14},{7,15}} | collective-permute-start | bytes 786440 | tf_op jit(solution)/shard_map/ppermute | solution.py:228
  21.6 12.5 %collective-permute-start.8 = (bf16[4,128,256]{2,1,0:T(8,128)(2,1)S(1)}, bf16[4,128,256]{2,1,0:T(8,128)(2,1)S(1)}, u32[]{:S(2)}, u32[]{:S(2)}) collective-permute-start(bf16[4,128,256]{2,1,0:T(8,128)(2,1)S(1)} %collective-permute-done.2), channel_id=1, source_target_pairs={{8,24},{9,25},{10,26},{11,27},{12,28},{13,29},{14,30},{15,31}} | collective-permute-start | bytes 786440 | tf_op jit(solution)/shard_map/ppermute | solution.py:228
  24.5 9.7 %collective-permute-start.7 = (bf16[2,128,256]{2,1,0:T(8,128)(2,1)S(1)}, bf16[2,128,256]{2,1,0:T(8,128)(2,1)S(1)}, u32[]{:S(2)}, u32[]{:S(2)}) collective-permute-start(bf16[2,128,256]{2,1,0:T(8,128)(2,1)S(1)} %get-tuple-element.83.inner), channel_id=1, source_target_pairs={{0,8},{8,16},{16,24},{1,9},{9,17},{17,25},{2,10},{10,18},{18,26},{... | collective-permute-start | bytes 393224 | tf_op jit(solution)/shard_map/ppermute | solution.py:228
  30.1 7.9 %collective-permute-start.6 = (bf16[2,128,256]{2,1,0:T(8,128)(2,1)S(1)}, bf16[2,128,256]{2,1,0:T(8,128)(2,1)S(1)}, u32[]{:S(2)}, u32[]{:S(2)}) collective-permute-start(bf16[2,128,256]{2,1,0:T(8,128)(2,1)S(1)} %pad_maximum_fusion.13), channel_id=1, source_target_pairs={{0,8},{8,16},{16,24},{1,9},{9,17},{17,25},{2,10},{10,18},{18,26},{... | collective-permute-start | bytes 393224 | tf_op jit(solution)/shard_map/ppermute | solution.py:228
  34.2 10.1 %collective-permute-start.9 = (bf16[4,128,256]{2,1,0:T(8,128)(2,1)S(1)}, bf16[4,128,256]{2,1,0:T(8,128)(2,1)S(1)}, u32[]{:S(2)}, u32[]{:S(2)}) collective-permute-start(bf16[4,128,256]{2,1,0:T(8,128)(2,1)S(1)} %shard_map.60), channel_id=1, source_target_pairs={{0,8},{8,16},{16,24},{1,9},{9,17},{17,25},{2,10},{10,18},{18,26},{... | collective-permute-start | bytes 786440 | tf_op jit(solution)/shard_map/ppermute | solution.py:228
  36.1 8.2 %collective-permute-start.11 = (bf16[4,128,256]{2,1,0:T(8,128)(2,1)S(1)}, bf16[4,128,256]{2,1,0:T(8,128)(2,1)S(1)}, u32[]{:S(2)}, u32[]{:S(2)}) collective-permute-start(bf16[4,128,256]{2,1,0:T(8,128)(2,1)S(1)} %collective-permute-done.10), channel_id=1, source_target_pairs={{8,24},{9,25},{10,26},{11,27},{12,28},{13,29},{14,30},{15,31}} | collective-permute-start | bytes 786440 | tf_op jit(solution)/shard_map/ppermute | solution.py:228
  44.5 10.8 %collective-permute-start.12 = (bf16[3,128,256]{2,1,0:T(8,128)(2,1)S(1)}, bf16[3,128,256]{2,1,0:T(8,128)(2,1)S(1)}, u32[]{:S(2)}, u32[]{:S(2)}) collective-permute-start(bf16[3,128,256]{2,1,0:T(8,128)(2,1)S(1)} %pad_maximum_fusion.7), channel_id=1, source_target_pairs={{0,1},{1,0},{2,3},{3,2},{4,5},{5,4},{6,7},{7,6},{8,9},{9,8},{10,11... | collective-permute-start | bytes 589832 | tf_op jit(solution)/shard_map/ppermute | solution.py:192
  46.3 9.0 %collective-permute-start.13 = (bf16[3,128,256]{2,1,0:T(8,128)(2,1)S(1)}, bf16[3,128,256]{2,1,0:T(8,128)(2,1)S(1)}, u32[]{:S(2)}, u32[]{:S(2)}) collective-permute-start(bf16[3,128,256]{2,1,0:T(8,128)(2,1)S(1)} %pad_maximum_fusion.8), channel_id=1, source_target_pairs={{1,2},{2,1},{3,4},{4,3},{5,6},{6,5},{9,10},{10,9},{11,12},{12,11},... | collective-permute-start | bytes 589832 | tf_op jit(solution)/shard_map/ppermute | solution.py:192
  51.8 10.1 %collective-permute-start.15 = (bf16[2,128,256]{2,1,0:T(8,128)(2,1)S(1)}, bf16[2,128,256]{2,1,0:T(8,128)(2,1)S(1)}, u32[]{:S(2)}, u32[]{:S(2)}) collective-permute-start(bf16[2,128,256]{2,1,0:T(8,128)(2,1)S(1)} %get-tuple-element.96.inner), channel_id=1, source_target_pairs={{0,8},{8,16},{16,24},{1,9},{9,17},{17,25},{2,10},{10,18},{18,26},{... | collective-permute-start | bytes 393224 | tf_op jit(solution)/shard_map/ppermute | solution.py:228
  57.1 7.5 %collective-permute-start.14 = (bf16[2,128,256]{2,1,0:T(8,128)(2,1)S(1)}, bf16[2,128,256]{2,1,0:T(8,128)(2,1)S(1)}, u32[]{:S(2)}, u32[]{:S(2)}) collective-permute-start(bf16[2,128,256]{2,1,0:T(8,128)(2,1)S(1)} %pad_maximum_fusion.14), channel_id=1, source_target_pairs={{0,8},{8,16},{16,24},{1,9},{9,17},{17,25},{2,10},{10,18},{18,26},{... | collective-permute-start | bytes 393224 | tf_op jit(solution)/shard_map/ppermute | solution.py:228
  59.1 5.6 %collective-permute-start.16 = (bf16[4,128,256]{2,1,0:T(8,128)(2,1)S(1)}, bf16[4,128,256]{2,1,0:T(8,128)(2,1)S(1)}, u32[]{:S(2)}, u32[]{:S(2)}) collective-permute-start(bf16[4,128,256]{2,1,0:T(8,128)(2,1)S(1)} %get-tuple-element.137), channel_id=1, source_target_pairs={{8,24},{9,25},{10,26},{11,27},{12,28},{13,29},{14,30},{15,31}} | collective-permute-start | bytes 786440 | tf_op jit(solution)/shard_map/ppermute | solution.py:228
  61.9 11.1 %collective-permute-start.17 = (bf16[4,128,256]{2,1,0:T(8,128)(2,1)S(1)}, bf16[4,128,256]{2,1,0:T(8,128)(2,1)S(1)}, u32[]{:S(2)}, u32[]{:S(2)}) collective-permute-start(bf16[4,128,256]{2,1,0:T(8,128)(2,1)S(1)} %shard_map.63), channel_id=1, source_target_pairs={{0,8},{8,16},{16,24},{1,9},{9,17},{17,25},{2,10},{10,18},{18,26},{... | collective-permute-start | bytes 786440 | tf_op jit(solution)/shard_map/ppermute | solution.py:228
  63.8 9.2 %collective-permute-start.18 = (bf16[4,128,256]{2,1,0:T(8,128)(2,1)S(1)}, bf16[4,128,256]{2,1,0:T(8,128)(2,1)S(1)}, u32[]{:S(2)}, u32[]{:S(2)}) collective-permute-start(bf16[4,128,256]{2,1,0:T(8,128)(2,1)S(1)} %collective-permute-done.9), channel_id=1, source_target_pairs={{8,24},{9,25},{10,26},{11,27},{12,28},{13,29},{14,30},{15,31}} | collective-permute-start | bytes 786440 | tf_op jit(solution)/shard_map/ppermute | solution.py:228
  73.2 8.9 %collective-permute-start.19 = (bf16[3,128,256]{2,1,0:T(8,128)(2,1)S(1)}, bf16[3,128,256]{2,1,0:T(8,128)(2,1)S(1)}, u32[]{:S(2)}, u32[]{:S(2)}) collective-permute-start(bf16[3,128,256]{2,1,0:T(8,128)(2,1)S(1)} %pad_maximum_fusion.9), channel_id=1, source_target_pairs={{0,1},{1,0},{2,3},{3,2},{4,5},{5,4},{6,7},{7,6},{8,9},{9,8},{10,11... | collective-permute-start | bytes 589832 | tf_op jit(solution)/shard_map/ppermute | solution.py:192
  73.7 8.4 %collective-permute-start.20 = (bf16[3,128,256]{2,1,0:T(8,128)(2,1)S(1)}, bf16[3,128,256]{2,1,0:T(8,128)(2,1)S(1)}, u32[]{:S(2)}, u32[]{:S(2)}) collective-permute-start(bf16[3,128,256]{2,1,0:T(8,128)(2,1)S(1)} %pad_maximum_fusion.10), channel_id=1, source_target_pairs={{1,2},{2,1},{3,4},{4,3},{5,6},{6,5},{9,10},{10,9},{11,12},{12,11},... | collective-permute-start | bytes 589832 | tf_op jit(solution)/shard_map/ppermute | solution.py:192
  78.6 10.5 %collective-permute-start.22 = (bf16[2,128,256]{2,1,0:T(8,128)(2,1)S(1)}, bf16[2,128,256]{2,1,0:T(8,128)(2,1)S(1)}, u32[]{:S(2)}, u32[]{:S(2)}) collective-permute-start(bf16[2,128,256]{2,1,0:T(8,128)(2,1)S(1)} %get-tuple-element.106.inner), channel_id=1, source_target_pairs={{8,16},{16,24},{9,17},{17,25},{10,18},{18,26},{11,19},{19,27},{12,... | collective-permute-start | bytes 393224 | tf_op jit(solution)/shard_map/ppermute | solution.py:228
  84.0 8.1 %collective-permute-start.21 = (bf16[2,128,256]{2,1,0:T(8,128)(2,1)S(1)}, bf16[2,128,256]{2,1,0:T(8,128)(2,1)S(1)}, u32[]{:S(2)}, u32[]{:S(2)}) collective-permute-start(bf16[2,128,256]{2,1,0:T(8,128)(2,1)S(1)} %pad_maximum_fusion.15), channel_id=1, source_target_pairs={{8,16},{16,24},{9,17},{17,25},{10,18},{18,26},{11,19},{19,27},{12,... | collective-permute-start | bytes 393224 | tf_op jit(solution)/shard_map/ppermute | solution.py:228
  86.2 5.9 %collective-permute-start.23 = (bf16[4,128,256]{2,1,0:T(8,128)(2,1)S(1)}, bf16[4,128,256]{2,1,0:T(8,128)(2,1)S(1)}, u32[]{:S(2)}, u32[]{:S(2)}) collective-permute-start(bf16[4,128,256]{2,1,0:T(8,128)(2,1)S(1)} %get-tuple-element.136), channel_id=1, source_target_pairs={{8,24},{9,25},{10,26},{11,27},{12,28},{13,29},{14,30},{15,31}} | collective-permute-start | bytes 786440 | tf_op jit(solution)/shard_map/ppermute | solution.py:228
  89.0 10.3 %collective-permute-start.24 = (bf16[4,128,256]{2,1,0:T(8,128)(2,1)S(1)}, bf16[4,128,256]{2,1,0:T(8,128)(2,1)S(1)}, u32[]{:S(2)}, u32[]{:S(2)}) collective-permute-start(bf16[4,128,256]{2,1,0:T(8,128)(2,1)S(1)} %shard_map.66), channel_id=1, source_target_pairs={{8,16},{16,24},{9,17},{17,25},{10,18},{18,26},{11,19},{19,27},{12,... | collective-permute-start | bytes 786440 | tf_op jit(solution)/shard_map/ppermute | solution.py:228
  91.0 8.4 %collective-permute-start.25 = (bf16[4,128,256]{2,1,0:T(8,128)(2,1)S(1)}, bf16[4,128,256]{2,1,0:T(8,128)(2,1)S(1)}, u32[]{:S(2)}, u32[]{:S(2)}) collective-permute-start(bf16[4,128,256]{2,1,0:T(8,128)(2,1)S(1)} %collective-permute-done.17), channel_id=1, source_target_pairs={{8,24},{9,25},{10,26},{11,27},{12,28},{13,29},{14,30},{15,31}} | collective-permute-start | bytes 786440 | tf_op jit(solution)/shard_map/ppermute | solution.py:228
  99.6 6.2 %collective-permute-start.26 = (bf16[3,128,256]{2,1,0:T(8,128)(2,1)S(1)}, bf16[3,128,256]{2,1,0:T(8,128)(2,1)S(1)}, u32[]{:S(2)}, u32[]{:S(2)}) collective-permute-start(bf16[3,128,256]{2,1,0:T(8,128)(2,1)S(1)} %pad_maximum_fusion.11), channel_id=1, source_target_pairs={{0,1},{1,0},{2,3},{3,2},{4,5},{5,4},{6,7},{7,6},{8,9},{9,8},{10,11... | collective-permute-start | bytes 589832 | tf_op jit(solution)/shard_map/ppermute | solution.py:192
  100.8 7.0 %collective-permute-start.27 = (bf16[3,128,256]{2,1,0:T(8,128)(2,1)S(1)}, bf16[3,128,256]{2,1,0:T(8,128)(2,1)S(1)}, u32[]{:S(2)}, u32[]{:S(2)}) collective-permute-start(bf16[3,128,256]{2,1,0:T(8,128)(2,1)S(1)} %pad_maximum_fusion.12), channel_id=1, source_target_pairs={{1,2},{2,1},{3,4},{4,3},{5,6},{6,5},{9,10},{10,9},{11,12},{12,11},... | collective-permute-start | bytes 589832 | tf_op jit(solution)/shard_map/ppermute | solution.py:192

commit v18 on v17

--- a/solution.py
+++ b/solution.py
@@ -255,24 +255,14 @@
             q = arrived(slot, 1)
             near, far = (swap(turn, starts, (q, 2), (p, 1)) for turn in range(2))
         *kept, w_one = inner_half(p, q, w_one, width, slot == 0)
+        first = first_half(flags, p, kept, (near, far), w_one, width)
         onward = [(j, j + 1) for j in range(1, sections - 1)] if slot > 0 else []
         if slot < ticks - 1:
             onward = [(0, 1)] + onward
         received, relays = {}, {}
-        if 0 < slot < ticks:
-            early = send(kept[0], onward)
-        first = first_half(flags, p, kept, (near, far), w_one, width)
-        if slot == 0:
+        if slot < ticks:
             received[0] = send(first[1], onward)
-        elif slot < ticks:
-            late = send(jnp.concatenate([first[1][:1], first[1][-1:]], axis=0), onward)
         second = second_half(first, q, w_two, width, slot == ticks)
-        if 0 < slot < ticks:
-            relays[0] = send(newer[0], [(1, sections - 1)])
-            if slot == 1:
-                relays[0], second = lax.optimization_barrier((relays[0], second))
-            early, second = lax.optimization_barrier((early, second))
-            received[0] = jnp.concatenate([late[:1], early, late[1:]], axis=0)
         if slot < ticks:
             received[1] = send(second, onward)
         if slot == 0:
@@ -281,7 +271,7 @@
             following += tuple(swap(turn, starts, (following[1], 2), (following[0], 1)) for turn in range(2))
         elif slot < ticks:
             relay_q, second = lax.optimization_barrier((newer[1], second))
-            relays[1] = send(relay_q, [(1, sections - 1)])
+            relays = {0: send(newer[0], [(1, sections - 1)]), 1: send(relay_q, [(1, sections - 1)])}
             if across:
                 direct = {0: send(first[1], across), 1: send(second, across)}
         older, newer, relayed = newer, received, relays

time: 114 us -> 109 us (0.956)
  starting transfers between devices: 50.1 us -> 41.2 us
  waiting for transfers between devices: 26.1 us -> 30.1 us
    ppermute x18 -> x15, starting transfers between devices: 29.3 us -> 20.4 us  [send(): return lax.ppermute(block, 'section', pairs) if pairs else block]
    ppermute x18 -> x15, waiting for transfers between devices: 24 us -> 27.7 us  [send(): return lax.ppermute(block, 'section', pairs) if pairs else block]
  transfers between devices with their start and end apart: 28 -> 25, of which waited for: 9 -> 11; matrix products, arithmetic and copies ran while one was open for 2% -> 2% of each run, Pallas kernels for 25% -> 26%
where the time goes in v18:
time: 109 us; the launch traced here: 107 us
  starting transfers between devices  41.2 us (38%)
  Pallas kernels  32.9 us (30%)
  waiting for transfers between devices  30.1 us (28%)
  local copies, waits for them, and re-layouts  1.31 us (1%)
  other arithmetic  1.15 us (1%)
    pallas_call x15, Pallas kernels, call(): pl.pallas_call(functools.partial(kernel, width), out_shape=[jax.ShapeDtyp...  32.9 us
    ppermute x15, waiting for transfers between devices, send(): return lax.ppermute(block, 'section', pairs) if pairs else block  27.7 us
    ppermute x10, starting transfers between devices, swap(): return lax.ppermute(jnp.concatenate(parts, axis=0), 'depth', pairs)  20.9 us
    ppermute x15, starting transfers between devices, send(): return lax.ppermute(block, 'section', pairs) if pairs else block  20.4 us
    ppermute x10, waiting for transfers between devices, swap(): return lax.ppermute(jnp.concatenate(parts, axis=0), 'depth', pairs)  2.44 us
  transfers between devices with their start and end apart: 25, of which 11 were waited for; matrix products, arithmetic and copies ran while one was open for 2% of the time, Pallas kernels for 26%

profile of v18, /device:TPU:13, one launch (start us, length us, event | category | flops | bytes accessed | tf_op | source)
XLA Modules:
  0.0 107.4 jit_solution(3946754320099818841)
XLA Ops:
  0.1 1.3 %collective-permute-start.3 = (bf16[2,4,128,256]{3,2,1,0:T(8,128)(2,1)}, bf16[2,4,128,256]{3,2,1,0:T(8,128)(2,1)S(1)}, u32[]{:S(2)}, u32[]{:S(2)}) collective-permute-start(bf16[2,4,128,256]{3,2,1,0:T(8,128)(2,1)} %bitcast.63), channel_id=1, source_target_pairs={{0,24},{8,16},{1,25},{9,17},{2,26},{10,18},{3,27},{11,19},{4,28},{... | collective-permute-start | bytes 1572872 | tf_op jit(solution)/shard_map/ppermute | solution.py:228
  1.4 1.1 slice_bitcast_fusion.6
  2.5 0.7 collective-permute-start
  3.3 3.1 %collective-permute-start.1 = (bf16[3,128,256]{2,1,0:T(8,128)(2,1)S(1)}, bf16[3,128,256]{2,1,0:T(8,128)(2,1)S(1)}, u32[]{:S(2)}, u32[]{:S(2)}) collective-permute-start(bf16[3,128,256]{2,1,0:T(8,128)(2,1)S(1)} %pad_maximum_fusion.1), channel_id=1, source_target_pairs={{1,2},{2,1},{3,4},{4,3},{5,6},{6,5},{9,10},{10,9},{11,12},{12,11},... | collective-permute-start | bytes 589832 | tf_op jit(solution)/shard_map/ppermute | solution.py:192
  6.4 4.1 %shard_map.55 = (bf16[2,128,256]{2,1,0:T(8,128)(2,1)S(1)}, f32[4,128,256]{2,1,0:T(8,128)S(1)}, bf16[6912,256]{1,0:T(8,128)(2,1)S(1)}) custom-call(bf16[4,128,256]{2,1,0:T(8,128)(2,1)S(1)} %get-tuple-element.108.p, bf16[4,128,256]{2,1,0:T(8,128)(2,1)S(1)} %get-tuple-element.107.q, bf16[6912,256]{1,0:T(8,128)(2,1)} %bitcast.55), custom_call_target="tpu_custom_call" | custom-call | flops 1 | bytes 1 | tf_op jit(solution)/shard_map/pallas_call | solution.py:141
  10.6 1.8 %shard_map.56 = (bf16[1,128,256]{2,1,0:T(8,128)(2,1)S(1)}, bf16[4,128,256]{2,1,0:T(8,128)(2,1)S(1)}, bf16[1,128,256]{2,1,0:T(8,128)(2,1)S(1)}) custom-call(s32[3]{0:T(128)S(1)} %add_convert_fusion.6.flags, bf16[4,128,256]{2,1,0:T(8,128)(2,1)S(1)} %get-tuple-element.108.p, bf16[2,128,256]{2,1,0:T(8,128)(2,1)S(1)} %get-tuple-element.62.inner, ...), custom_call_target="tpu_custom_call" | custom-call | flops 1 | bytes 1 | tf_op jit(solution)/shard_map/pallas_call | solution.py:141
  12.4 0.7 collective-permute-start.2
  13.1 2.1 %shard_map.57 = bf16[4,128,256]{2,1,0:T(8,128)(2,1)S(1)} custom-call(bf16[1,128,256]{2,1,0:T(8,128)(2,1)S(1)} %get-tuple-element.71.first_low, bf16[4,128,256]{2,1,0:T(8,128)(2,1)S(1)} %get-tuple-element.69.first_mid, bf16[1,128,256]{2,1,0:T(8,128)(2,1)S(1)} %get-tuple-element.72.first_high, bf16[4,128,256]{2,1,0:T(8,128)(2,1)S(1)} %get-tuple-element.107.q, ...), custom_call_target="tpu_custom_call" | custom-call | flops 1 | bytes 1 | tf_op jit(solution)/shard_map/pallas_call | solution.py:141
  15.2 0.6 collective-permute-done.3
  15.9 0.2 fusion.10
  16.2 4.6 %collective-permute-start.5 = (bf16[3,128,256]{2,1,0:T(8,128)(2,1)S(1)}, bf16[3,128,256]{2,1,0:T(8,128)(2,1)S(1)}, u32[]{:S(2)}, u32[]{:S(2)}) collective-permute-start(bf16[3,128,256]{2,1,0:T(8,128)(2,1)S(1)} %pad_maximum_fusion.3), channel_id=1, source_target_pairs={{1,2},{2,1},{3,4},{4,3},{5,6},{6,5},{9,10},{10,9},{11,12},{12,11},... | collective-permute-start | bytes 589832 | tf_op jit(solution)/shard_map/ppermute | solution.py:192
  21.0 0.7 collective-permute-start.9
  21.6 0.7 collective-permute-start.7
  22.3 2.1 %shard_map.58 = (bf16[2,128,256]{2,1,0:T(8,128)(2,1)S(1)}, f32[4,128,256]{2,1,0:T(8,128)S(1)}) custom-call(bf16[4,128,256]{2,1,0:T(8,128)(2,1)S(1)} %get-tuple-element.106.p, bf16[4,128,256]{2,1,0:T(8,128)(2,1)S(1)} %get-tuple-element.105.q, bf16[6912,256]{1,0:T(8,128)(2,1)S(1)} %get-tuple-element.68.weights), custom_call_target="tpu_custom_call" | custom-call | flops 1 | bytes 1 | tf_op jit(solution)/shard_map/pallas_call | solution.py:141
  24.5 1.8 %shard_map.59 = (bf16[1,128,256]{2,1,0:T(8,128)(2,1)S(1)}, bf16[4,128,256]{2,1,0:T(8,128)(2,1)S(1)}, bf16[1,128,256]{2,1,0:T(8,128)(2,1)S(1)}) custom-call(s32[3]{0:T(128)S(1)} %add_convert_fusion.6.flags, bf16[4,128,256]{2,1,0:T(8,128)(2,1)S(1)} %get-tuple-element.106.p, bf16[2,128,256]{2,1,0:T(8,128)(2,1)S(1)} %get-tuple-element.75.inner, ...), custom_call_target="tpu_custom_call" | custom-call | flops 1 | bytes 1 | tf_op jit(solution)/shard_map/pallas_call | solution.py:141
  26.3 3.7 %collective-permute-start.6 = (bf16[4,128,256]{2,1,0:T(8,128)(2,1)S(1)}, bf16[4,128,256]{2,1,0:T(8,128)(2,1)S(1)}, u32[]{:S(2)}, u32[]{:S(2)}) collective-permute-start(bf16[4,128,256]{2,1,0:T(8,128)(2,1)S(1)} %get-tuple-element.77.first_mid), channel_id=1, source_target_pairs={{0,8},{8,16},{16,24},{1,9},{9,17},{17,25},{2,10},{10,18},{18,26},{... | collective-permute-start | bytes 786440 | tf_op jit(solution)/shard_map/ppermute | solution.py:228
  30.0 2.1 %shard_map.60 = bf16[4,128,256]{2,1,0:T(8,128)(2,1)S(1)} custom-call(bf16[1,128,256]{2,1,0:T(8,128)(2,1)S(1)} %get-tuple-element.79.first_low, bf16[4,128,256]{2,1,0:T(8,128)(2,1)S(1)} %get-tuple-element.77.first_mid, bf16[1,128,256]{2,1,0:T(8,128)(2,1)S(1)} %get-tuple-element.80.first_high, bf16[4,128,256]{2,1,0:T(8,128)(2,1)S(1)} %get-tuple-element.105.q, ...), custom_call_target="tpu_custom_call" | custom-call | flops 1 | bytes 1 | tf_op jit(solution)/shard_map/pallas_call | solution.py:141
  32.2 1.9 %collective-permute-start.8 = (bf16[4,128,256]{2,1,0:T(8,128)(2,1)S(1)}, bf16[4,128,256]{2,1,0:T(8,128)(2,1)S(1)}, u32[]{:S(2)}, u32[]{:S(2)}) collective-permute-start(bf16[4,128,256]{2,1,0:T(8,128)(2,1)S(1)} %shard_map.60), channel_id=1, source_target_pairs={{0,8},{8,16},{16,24},{1,9},{9,17},{17,25},{2,10},{10,18},{18,26},{... | collective-permute-start | bytes 786440 | tf_op jit(solution)/shard_map/ppermute | solution.py:228
  34.1 0.7 collective-permute-start.10
  34.8 4.0 %collective-permute-done.6 = bf16[4,128,256]{2,1,0:T(8,128)(2,1)S(1)} collective-permute-done((bf16[4,128,256]{2,1,0:T(8,128)(2,1)S(1)}, bf16[4,128,256]{2,1,0:T(8,128)(2,1)S(1)}, u32[]{:S(2)}, u32[]{:S(2)}) %collective-permute-start.6) | collective-permute-done | bytes 262176 | tf_op jit(solution)/shard_map/ppermute | solution.py:228
  38.9 5.5 %collective-permute-done.8 = bf16[4,128,256]{2,1,0:T(8,128)(2,1)S(1)} collective-permute-done((bf16[4,128,256]{2,1,0:T(8,128)(2,1)S(1)}, bf16[4,128,256]{2,1,0:T(8,128)(2,1)S(1)}, u32[]{:S(2)}, u32[]{:S(2)}) %collective-permute-start.8) | collective-permute-done | bytes 262176 | tf_op jit(solution)/shard_map/ppermute | solution.py:228
  44.6 4.5 %collective-permute-start.12 = (bf16[3,128,256]{2,1,0:T(8,128)(2,1)S(1)}, bf16[3,128,256]{2,1,0:T(8,128)(2,1)S(1)}, u32[]{:S(2)}, u32[]{:S(2)}) collective-permute-start(bf16[3,128,256]{2,1,0:T(8,128)(2,1)S(1)} %pad_maximum_fusion.5), channel_id=1, source_target_pairs={{1,2},{2,1},{3,4},{4,3},{5,6},{6,5},{9,10},{10,9},{11,12},{12,11},... | collective-permute-start | bytes 589832 | tf_op jit(solution)/shard_map/ppermute | solution.py:192
  49.2 2.1 %shard_map.61 = (bf16[2,128,256]{2,1,0:T(8,128)(2,1)S(1)}, f32[4,128,256]{2,1,0:T(8,128)S(1)}) custom-call(bf16[4,128,256]{2,1,0:T(8,128)(2,1)S(1)} %fusion.17.p, bf16[4,128,256]{2,1,0:T(8,128)(2,1)S(1)} %fusion.16.q, bf16[6912,256]{1,0:T(8,128)(2,1)S(1)} %get-tuple-element.68.weights), custom_call_target="tpu_custom_call" | custom-call | flops 1 | bytes 1 | tf_op jit(solution)/shard_map/pallas_call | solution.py:141
  51.3 0.7 collective-permute-start.14
  52.0 0.4 collective-permute-done.12.far
  52.4 1.8 %shard_map.62 = (bf16[1,128,256]{2,1,0:T(8,128)(2,1)S(1)}, bf16[4,128,256]{2,1,0:T(8,128)(2,1)S(1)}, bf16[1,128,256]{2,1,0:T(8,128)(2,1)S(1)}) custom-call(s32[3]{0:T(128)S(1)} %add_convert_fusion.6.flags, bf16[4,128,256]{2,1,0:T(8,128)(2,1)S(1)} %fusion.17.p, bf16[2,128,256]{2,1,0:T(8,128)(2,1)S(1)} %get-tuple-element.84.inner, ...), custom_call_target="tpu_custom_call" | custom-call | flops 1 | bytes 1 | tf_op jit(solution)/shard_map/pallas_call | solution.py:141
  54.2 2.2 %collective-permute-start.13 = (bf16[4,128,256]{2,1,0:T(8,128)(2,1)S(1)}, bf16[4,128,256]{2,1,0:T(8,128)(2,1)S(1)}, u32[]{:S(2)}, u32[]{:S(2)}) collective-permute-start(bf16[4,128,256]{2,1,0:T(8,128)(2,1)S(1)} %get-tuple-element.86.first_mid), channel_id=1, source_target_pairs={{0,8},{8,16},{16,24},{1,9},{9,17},{17,25},{2,10},{10,18},{18,26},{... | collective-permute-start | bytes 786440 | tf_op jit(solution)/shard_map/ppermute | solution.py:228
  56.4 2.1 %shard_map.63 = bf16[4,128,256]{2,1,0:T(8,128)(2,1)S(1)} custom-call(bf16[1,128,256]{2,1,0:T(8,128)(2,1)S(1)} %get-tuple-element.87.first_low, bf16[4,128,256]{2,1,0:T(8,128)(2,1)S(1)} %get-tuple-element.86.first_mid, bf16[1,128,256]{2,1,0:T(8,128)(2,1)S(1)} %get-tuple-element.88.first_high, bf16[4,128,256]{2,1,0:T(8,128)(2,1)S(1)} %fusion.16.q, ...), custom_call_target="tpu_custom_call" | custom-call | flops 1 | bytes 1 | tf_op jit(solution)/shard_map/pallas_call | solution.py:141
  58.6 1.9 %collective-permute-start.15 = (bf16[4,128,256]{2,1,0:T(8,128)(2,1)S(1)}, bf16[4,128,256]{2,1,0:T(8,128)(2,1)S(1)}, u32[]{:S(2)}, u32[]{:S(2)}) collective-permute-start(bf16[4,128,256]{2,1,0:T(8,128)(2,1)S(1)} %shard_map.63), channel_id=1, source_target_pairs={{0,8},{8,16},{16,24},{1,9},{9,17},{17,25},{2,10},{10,18},{18,26},{... | collective-permute-start | bytes 786440 | tf_op jit(solution)/shard_map/ppermute | solution.py:228
  60.5 0.7 collective-permute-start.16
  61.2 3.3 %collective-permute-done.13 = bf16[4,128,256]{2,1,0:T(8,128)(2,1)S(1)} collective-permute-done((bf16[4,128,256]{2,1,0:T(8,128)(2,1)S(1)}, bf16[4,128,256]{2,1,0:T(8,128)(2,1)S(1)}, u32[]{:S(2)}, u32[]{:S(2)}) %collective-permute-start.13) | collective-permute-done | bytes 262176 | tf_op jit(solution)/shard_map/ppermute | solution.py:228
  64.6 5.5 %collective-permute-done.15 = bf16[4,128,256]{2,1,0:T(8,128)(2,1)S(1)} collective-permute-done((bf16[4,128,256]{2,1,0:T(8,128)(2,1)S(1)}, bf16[4,128,256]{2,1,0:T(8,128)(2,1)S(1)}, u32[]{:S(2)}, u32[]{:S(2)}) %collective-permute-start.15) | collective-permute-done | bytes 262176 | tf_op jit(solution)/shard_map/ppermute | solution.py:228
  70.3 3.8 %collective-permute-start.18 = (bf16[3,128,256]{2,1,0:T(8,128)(2,1)S(1)}, bf16[3,128,256]{2,1,0:T(8,128)(2,1)S(1)}, u32[]{:S(2)}, u32[]{:S(2)}) collective-permute-start(bf16[3,128,256]{2,1,0:T(8,128)(2,1)S(1)} %pad_maximum_fusion.7), channel_id=1, source_target_pairs={{1,2},{2,1},{3,4},{4,3},{5,6},{6,5},{9,10},{10,9},{11,12},{12,11},... | collective-permute-start | bytes 589832 | tf_op jit(solution)/shard_map/ppermute | solution.py:192
  74.3 2.1 %shard_map.64 = (bf16[2,128,256]{2,1,0:T(8,128)(2,1)S(1)}, f32[4,128,256]{2,1,0:T(8,128)S(1)}) custom-call(bf16[4,128,256]{2,1,0:T(8,128)(2,1)S(1)} %fusion.15.p, bf16[4,128,256]{2,1,0:T(8,128)(2,1)S(1)} %fusion.14.q, bf16[6912,256]{1,0:T(8,128)(2,1)S(1)} %get-tuple-element.68.weights), custom_call_target="tpu_custom_call" | custom-call | flops 1 | bytes 1 | tf_op jit(solution)/shard_map/pallas_call | solution.py:141
  76.4 0.7 collective-permute-start.20
  77.1 0.7 collective-permute-done.18.far
  77.8 1.8 %shard_map.65 = (bf16[1,128,256]{2,1,0:T(8,128)(2,1)S(1)}, bf16[4,128,256]{2,1,0:T(8,128)(2,1)S(1)}, bf16[1,128,256]{2,1,0:T(8,128)(2,1)S(1)}) custom-call(s32[3]{0:T(128)S(1)} %add_convert_fusion.6.flags, bf16[4,128,256]{2,1,0:T(8,128)(2,1)S(1)} %fusion.15.p, bf16[2,128,256]{2,1,0:T(8,128)(2,1)S(1)} %get-tuple-element.92.inner, ...), custom_call_target="tpu_custom_call" | custom-call | flops 1 | bytes 1 | tf_op jit(solution)/shard_map/pallas_call | solution.py:141
  79.6 1.9 %collective-permute-start.19 = (bf16[4,128,256]{2,1,0:T(8,128)(2,1)S(1)}, bf16[4,128,256]{2,1,0:T(8,128)(2,1)S(1)}, u32[]{:S(2)}, u32[]{:S(2)}) collective-permute-start(bf16[4,128,256]{2,1,0:T(8,128)(2,1)S(1)} %get-tuple-element.94.first_mid), channel_id=1, source_target_pairs={{8,16},{16,24},{9,17},{17,25},{10,18},{18,26},{11,19},{19,27},{12,... | collective-permute-start | bytes 786440 | tf_op jit(solution)/shard_map/ppermute | solution.py:228
  81.5 2.1 %shard_map.66 = bf16[4,128,256]{2,1,0:T(8,128)(2,1)S(1)} custom-call(bf16[1,128,256]{2,1,0:T(8,128)(2,1)S(1)} %get-tuple-element.95.first_low, bf16[4,128,256]{2,1,0:T(8,128)(2,1)S(1)} %get-tuple-element.94.first_mid, bf16[1,128,256]{2,1,0:T(8,128)(2,1)S(1)} %get-tuple-element.96.first_high, bf16[4,128,256]{2,1,0:T(8,128)(2,1)S(1)} %fusion.14.q, ...), custom_call_target="tpu_custom_call" | custom-call | flops 1 | bytes 1 | tf_op jit(solution)/shard_map/pallas_call | solution.py:141
  83.6 1.9 %collective-permute-start.21 = (bf16[4,128,256]{2,1,0:T(8,128)(2,1)S(1)}, bf16[4,128,256]{2,1,0:T(8,128)(2,1)S(1)}, u32[]{:S(2)}, u32[]{:S(2)}) collective-permute-start(bf16[4,128,256]{2,1,0:T(8,128)(2,1)S(1)} %shard_map.66), channel_id=1, source_target_pairs={{8,16},{16,24},{9,17},{17,25},{10,18},{18,26},{11,19},{19,27},{12,... | collective-permute-start | bytes 786440 | tf_op jit(solution)/shard_map/ppermute | solution.py:228
  85.6 0.7 collective-permute-start.22
  86.3 3.2 %collective-permute-done.19 = bf16[4,128,256]{2,1,0:T(8,128)(2,1)S(1)} collective-permute-done((bf16[4,128,256]{2,1,0:T(8,128)(2,1)S(1)}, bf16[4,128,256]{2,1,0:T(8,128)(2,1)S(1)}, u32[]{:S(2)}, u32[]{:S(2)}) %collective-permute-start.19) | collective-permute-done | bytes 262176 | tf_op jit(solution)/shard_map/ppermute | solution.py:228
  89.6 5.5 %collective-permute-done.21 = bf16[4,128,256]{2,1,0:T(8,128)(2,1)S(1)} collective-permute-done((bf16[4,128,256]{2,1,0:T(8,128)(2,1)S(1)}, bf16[4,128,256]{2,1,0:T(8,128)(2,1)S(1)}, u32[]{:S(2)}, u32[]{:S(2)}) %collective-permute-start.21) | collective-permute-done | bytes 262176 | tf_op jit(solution)/shard_map/ppermute | solution.py:228
  95.3 3.7 %collective-permute-start.24 = (bf16[3,128,256]{2,1,0:T(8,128)(2,1)S(1)}, bf16[3,128,256]{2,1,0:T(8,128)(2,1)S(1)}, u32[]{:S(2)}, u32[]{:S(2)}) collective-permute-start(bf16[3,128,256]{2,1,0:T(8,128)(2,1)S(1)} %pad_maximum_fusion.9), channel_id=1, source_target_pairs={{1,2},{2,1},{3,4},{4,3},{5,6},{6,5},{9,10},{10,9},{11,12},{12,11},... | collective-permute-start | bytes 589832 | tf_op jit(solution)/shard_map/ppermute | solution.py:192
  99.2 2.1 %shard_map.67 = (bf16[2,128,256]{2,1,0:T(8,128)(2,1)S(1)}, f32[4,128,256]{2,1,0:T(8,128)S(1)}) custom-call(bf16[4,128,256]{2,1,0:T(8,128)(2,1)S(1)} %fusion.13.p, bf16[4,128,256]{2,1,0:T(8,128)(2,1)S(1)} %fusion.12.q, bf16[6912,256]{1,0:T(8,128)(2,1)S(1)} %get-tuple-element.68.weights), custom_call_target="tpu_custom_call" | custom-call | flops 1 | bytes 1 | tf_op jit(solution)/shard_map/pallas_call | solution.py:141
  101.3 1.3 %collective-permute-done.24.far = bf16[3,128,256]{2,1,0:T(8,128)(2,1)S(1)} collective-permute-done((bf16[3,128,256]{2,1,0:T(8,128)(2,1)S(1)}, bf16[3,128,256]{2,1,0:T(8,128)(2,1)S(1)}, u32[]{:S(2)}, u32[]{:S(2)}) %collective-permute-start.24) | collective-permute-done | bytes 196640 | tf_op jit(solution)/shard_map/ppermute | solution.py:192
  102.6 1.8 %shard_map.68 = (bf16[1,128,256]{2,1,0:T(8,128)(2,1)S(1)}, bf16[4,128,256]{2,1,0:T(8,128)(2,1)S(1)}, bf16[1,128,256]{2,1,0:T(8,128)(2,1)S(1)}) custom-call(s32[3]{0:T(128)S(1)} %add_convert_fusion.6.flags, bf16[4,128,256]{2,1,0:T(8,128)(2,1)S(1)} %fusion.13.p, bf16[2,128,256]{2,1,0:T(8,128)(2,1)S(1)} %get-tuple-element.100.inner, ...), custom_call_target="tpu_custom_call" | custom-call | flops 1 | bytes 1 | tf_op jit(solution)/shard_map/pallas_call | solution.py:141
  104.4 2.8 %shard_map.69 = bf16[2,4,128,256]{3,2,1,0:T(8,128)(2,1)} custom-call(bf16[1,128,256]{2,1,0:T(8,128)(2,1)S(1)} %get-tuple-element.102.first_low, bf16[4,128,256]{2,1,0:T(8,128)(2,1)S(1)} %get-tuple-element.103.first_mid, bf16[1,128,256]{2,1,0:T(8,128)(2,1)S(1)} %get-tuple-element.104.first_high, bf16[4,128,256]{2,1,0:T(8,128)(2,1)S(1)} %fusion.12.q, ...), custom_call_target="tpu_custom_call" | custom-call | flops 1 | bytes 1 | tf_op jit(solution)/shard_map/pallas_call | solution.py:141
  (52 shorter events, 1.6 us)
Async XLA Ops:
  0.1 15.8 %collective-permute-start.3 = (bf16[2,4,128,256]{3,2,1,0:T(8,128)(2,1)}, bf16[2,4,128,256]{3,2,1,0:T(8,128)(2,1)S(1)}, u32[]{:S(2)}, u32[]{:S(2)}) collective-permute-start(bf16[2,4,128,256]{3,2,1,0:T(8,128)(2,1)} %bitcast.63), channel_id=1, source_target_pairs={{0,24},{8,16},{1,25},{9,17},{2,26},{10,18},{3,27},{11,19},{4,28},{... | collective-permute-start | bytes 1572872 | tf_op jit(solution)/shard_map/ppermute | solution.py:228
  2.5 7.9 %collective-permute-start = (bf16[3,128,256]{2,1,0:T(8,128)(2,1)S(1)}, bf16[3,128,256]{2,1,0:T(8,128)(2,1)S(1)}, u32[]{:S(2)}, u32[]{:S(2)}) collective-permute-start(bf16[3,128,256]{2,1,0:T(8,128)(2,1)S(1)} %pad_maximum_fusion), channel_id=1, source_target_pairs={{0,1},{1,0},{2,3},{3,2},{4,5},{5,4},{6,7},{7,6},{8,9},{9,8},{10,11... | collective-permute-start | bytes 589832 | tf_op jit(solution)/shard_map/ppermute | solution.py:192
  3.3 7.3 %collective-permute-start.1 = (bf16[3,128,256]{2,1,0:T(8,128)(2,1)S(1)}, bf16[3,128,256]{2,1,0:T(8,128)(2,1)S(1)}, u32[]{:S(2)}, u32[]{:S(2)}) collective-permute-start(bf16[3,128,256]{2,1,0:T(8,128)(2,1)S(1)} %pad_maximum_fusion.1), channel_id=1, source_target_pairs={{1,2},{2,1},{3,4},{4,3},{5,6},{6,5},{9,10},{10,9},{11,12},{12,11},... | collective-permute-start | bytes 589832 | tf_op jit(solution)/shard_map/ppermute | solution.py:192
  10.6 2.5 %copy-start = (bf16[1,3,3,3,256,256]{5,4,3,2,1,0:T(8,128)(2,1)S(1)}, bf16[1,3,3,3,256,256]{5,4,3,2,1,0:T(8,128)(2,1)}, u32[]{:S(2)}) copy-start(bf16[1,3,3,3,256,256]{5,4,3,2,1,0:T(8,128)(2,1)} %param.9) | copy-start | bytes 10616836
  12.4 9.3 %collective-permute-start.2 = (bf16[4,128,256]{2,1,0:T(8,128)(2,1)S(1)}, bf16[4,128,256]{2,1,0:T(8,128)(2,1)S(1)}, u32[]{:S(2)}, u32[]{:S(2)}) collective-permute-start(bf16[4,128,256]{2,1,0:T(8,128)(2,1)S(1)} %get-tuple-element.69.first_mid), channel_id=1, source_target_pairs={{0,8},{1,9},{2,10},{3,11},{4,12},{5,13},{6,14},{7,15}} | collective-permute-start | bytes 786440 | tf_op jit(solution)/shard_map/ppermute | solution.py:228
  13.1 2.8 %copy-start.1 = (bf16[3,2,4,16,8,256]{5,4,3,2,1,0:T(8,128)(2,1)S(1)}, bf16[3,2,4,16,8,256]{5,4,3,2,1,0:T(8,128)(2,1)}, u32[]{:S(2)}) copy-start(bf16[3,2,4,16,8,256]{5,4,3,2,1,0:T(8,128)(2,1)} %param.7) | copy-start | bytes 4718596
  13.1 2.8 %copy-start.2 = (bf16[1,2,4,16,8,256]{5,4,3,2,1,0:T(8,128)(2,1)S(1)}, bf16[1,2,4,16,8,256]{5,4,3,2,1,0:T(8,128)(2,1)}, u32[]{:S(2)}) copy-start(bf16[1,2,4,16,8,256]{5,4,3,2,1,0:T(8,128)(2,1)} %param.5) | copy-start | bytes 1572868
  16.2 8.3 %collective-permute-start.5 = (bf16[3,128,256]{2,1,0:T(8,128)(2,1)S(1)}, bf16[3,128,256]{2,1,0:T(8,128)(2,1)S(1)}, u32[]{:S(2)}, u32[]{:S(2)}) collective-permute-start(bf16[3,128,256]{2,1,0:T(8,128)(2,1)S(1)} %pad_maximum_fusion.3), channel_id=1, source_target_pairs={{1,2},{2,1},{3,4},{4,3},{5,6},{6,5},{9,10},{10,9},{11,12},{12,11},... | collective-permute-start | bytes 589832 | tf_op jit(solution)/shard_map/ppermute | solution.py:192
  20.9 3.6 %collective-permute-start.4 = (bf16[3,128,256]{2,1,0:T(8,128)(2,1)S(1)}, bf16[3,128,256]{2,1,0:T(8,128)(2,1)S(1)}, u32[]{:S(2)}, u32[]{:S(2)}) collective-permute-start(bf16[3,128,256]{2,1,0:T(8,128)(2,1)S(1)} %pad_maximum_fusion.2), channel_id=1, source_target_pairs={{0,1},{1,0},{2,3},{3,2},{4,5},{5,4},{6,7},{7,6},{8,9},{9,8},{10,11... | collective-permute-start | bytes 589832 | tf_op jit(solution)/shard_map/ppermute | solution.py:192
  21.0 13.1 %collective-permute-start.9 = (bf16[4,128,256]{2,1,0:T(8,128)(2,1)S(1)}, bf16[4,128,256]{2,1,0:T(8,128)(2,1)S(1)}, u32[]{:S(2)}, u32[]{:S(2)}) collective-permute-start(bf16[4,128,256]{2,1,0:T(8,128)(2,1)S(1)} %shard_map.57), channel_id=1, source_target_pairs={{0,8},{1,9},{2,10},{3,11},{4,12},{5,13},{6,14},{7,15}} | collective-permute-start | bytes 786440 | tf_op jit(solution)/shard_map/ppermute | solution.py:228
  21.6 13.1 %collective-permute-start.7 = (bf16[4,128,256]{2,1,0:T(8,128)(2,1)S(1)}, bf16[4,128,256]{2,1,0:T(8,128)(2,1)S(1)}, u32[]{:S(2)}, u32[]{:S(2)}) collective-permute-start(bf16[4,128,256]{2,1,0:T(8,128)(2,1)S(1)} %collective-permute-done.2), channel_id=1, source_target_pairs={{8,24},{9,25},{10,26},{11,27},{12,28},{13,29},{14,30},{15,31}} | collective-permute-start | bytes 786440 | tf_op jit(solution)/shard_map/ppermute | solution.py:228
  26.3 12.5 %collective-permute-start.6 = (bf16[4,128,256]{2,1,0:T(8,128)(2,1)S(1)}, bf16[4,128,256]{2,1,0:T(8,128)(2,1)S(1)}, u32[]{:S(2)}, u32[]{:S(2)}) collective-permute-start(bf16[4,128,256]{2,1,0:T(8,128)(2,1)S(1)} %get-tuple-element.77.first_mid), channel_id=1, source_target_pairs={{0,8},{8,16},{16,24},{1,9},{9,17},{17,25},{2,10},{10,18},{18,26},{... | collective-permute-start | bytes 786440 | tf_op jit(solution)/shard_map/ppermute | solution.py:228
  32.2 12.2 %collective-permute-start.8 = (bf16[4,128,256]{2,1,0:T(8,128)(2,1)S(1)}, bf16[4,128,256]{2,1,0:T(8,128)(2,1)S(1)}, u32[]{:S(2)}, u32[]{:S(2)}) collective-permute-start(bf16[4,128,256]{2,1,0:T(8,128)(2,1)S(1)} %shard_map.60), channel_id=1, source_target_pairs={{0,8},{8,16},{16,24},{1,9},{9,17},{17,25},{2,10},{10,18},{18,26},{... | collective-permute-start | bytes 786440 | tf_op jit(solution)/shard_map/ppermute | solution.py:228
  34.1 10.3 %collective-permute-start.10 = (bf16[4,128,256]{2,1,0:T(8,128)(2,1)S(1)}, bf16[4,128,256]{2,1,0:T(8,128)(2,1)S(1)}, u32[]{:S(2)}, u32[]{:S(2)}) collective-permute-start(bf16[4,128,256]{2,1,0:T(8,128)(2,1)S(1)} %collective-permute-done.9), channel_id=1, source_target_pairs={{8,24},{9,25},{10,26},{11,27},{12,28},{13,29},{14,30},{15,31}} | collective-permute-start | bytes 786440 | tf_op jit(solution)/shard_map/ppermute | solution.py:228
  44.6 7.8 %collective-permute-start.12 = (bf16[3,128,256]{2,1,0:T(8,128)(2,1)S(1)}, bf16[3,128,256]{2,1,0:T(8,128)(2,1)S(1)}, u32[]{:S(2)}, u32[]{:S(2)}) collective-permute-start(bf16[3,128,256]{2,1,0:T(8,128)(2,1)S(1)} %pad_maximum_fusion.5), channel_id=1, source_target_pairs={{1,2},{2,1},{3,4},{4,3},{5,6},{6,5},{9,10},{10,9},{11,12},{12,11},... | collective-permute-start | bytes 589832 | tf_op jit(solution)/shard_map/ppermute | solution.py:192
  49.1 3.3 %collective-permute-start.11 = (bf16[3,128,256]{2,1,0:T(8,128)(2,1)S(1)}, bf16[3,128,256]{2,1,0:T(8,128)(2,1)S(1)}, u32[]{:S(2)}, u32[]{:S(2)}) collective-permute-start(bf16[3,128,256]{2,1,0:T(8,128)(2,1)S(1)} %pad_maximum_fusion.4), channel_id=1, source_target_pairs={{0,1},{1,0},{2,3},{3,2},{4,5},{5,4},{6,7},{7,6},{8,9},{9,8},{10,11... | collective-permute-start | bytes 589832 | tf_op jit(solution)/shard_map/ppermute | solution.py:192
  51.3 9.8 %collective-permute-start.14 = (bf16[4,128,256]{2,1,0:T(8,128)(2,1)S(1)}, bf16[4,128,256]{2,1,0:T(8,128)(2,1)S(1)}, u32[]{:S(2)}, u32[]{:S(2)}) collective-permute-start(bf16[4,128,256]{2,1,0:T(8,128)(2,1)S(1)} %collective-permute-done.6), channel_id=1, source_target_pairs={{8,24},{9,25},{10,26},{11,27},{12,28},{13,29},{14,30},{15,31}} | collective-permute-start | bytes 786440 | tf_op jit(solution)/shard_map/ppermute | solution.py:228
  54.2 10.3 %collective-permute-start.13 = (bf16[4,128,256]{2,1,0:T(8,128)(2,1)S(1)}, bf16[4,128,256]{2,1,0:T(8,128)(2,1)S(1)}, u32[]{:S(2)}, u32[]{:S(2)}) collective-permute-start(bf16[4,128,256]{2,1,0:T(8,128)(2,1)S(1)} %get-tuple-element.86.first_mid), channel_id=1, source_target_pairs={{0,8},{8,16},{16,24},{1,9},{9,17},{17,25},{2,10},{10,18},{18,26},{... | collective-permute-start | bytes 786440 | tf_op jit(solution)/shard_map/ppermute | solution.py:228
  58.6 11.5 %collective-permute-start.15 = (bf16[4,128,256]{2,1,0:T(8,128)(2,1)S(1)}, bf16[4,128,256]{2,1,0:T(8,128)(2,1)S(1)}, u32[]{:S(2)}, u32[]{:S(2)}) collective-permute-start(bf16[4,128,256]{2,1,0:T(8,128)(2,1)S(1)} %shard_map.63), channel_id=1, source_target_pairs={{0,8},{8,16},{16,24},{1,9},{9,17},{17,25},{2,10},{10,18},{18,26},{... | collective-permute-start | bytes 786440 | tf_op jit(solution)/shard_map/ppermute | solution.py:228
  60.5 9.6 %collective-permute-start.16 = (bf16[4,128,256]{2,1,0:T(8,128)(2,1)S(1)}, bf16[4,128,256]{2,1,0:T(8,128)(2,1)S(1)}, u32[]{:S(2)}, u32[]{:S(2)}) collective-permute-start(bf16[4,128,256]{2,1,0:T(8,128)(2,1)S(1)} %collective-permute-done.8), channel_id=1, source_target_pairs={{8,24},{9,25},{10,26},{11,27},{12,28},{13,29},{14,30},{15,31}} | collective-permute-start | bytes 786440 | tf_op jit(solution)/shard_map/ppermute | solution.py:228
  70.3 7.5 %collective-permute-start.18 = (bf16[3,128,256]{2,1,0:T(8,128)(2,1)S(1)}, bf16[3,128,256]{2,1,0:T(8,128)(2,1)S(1)}, u32[]{:S(2)}, u32[]{:S(2)}) collective-permute-start(bf16[3,128,256]{2,1,0:T(8,128)(2,1)S(1)} %pad_maximum_fusion.7), channel_id=1, source_target_pairs={{1,2},{2,1},{3,4},{4,3},{5,6},{6,5},{9,10},{10,9},{11,12},{12,11},... | collective-permute-start | bytes 589832 | tf_op jit(solution)/shard_map/ppermute | solution.py:192
  74.2 3.6 %collective-permute-start.17 = (bf16[3,128,256]{2,1,0:T(8,128)(2,1)S(1)}, bf16[3,128,256]{2,1,0:T(8,128)(2,1)S(1)}, u32[]{:S(2)}, u32[]{:S(2)}) collective-permute-start(bf16[3,128,256]{2,1,0:T(8,128)(2,1)S(1)} %pad_maximum_fusion.6), channel_id=1, source_target_pairs={{0,1},{1,0},{2,3},{3,2},{4,5},{5,4},{6,7},{7,6},{8,9},{9,8},{10,11... | collective-permute-start | bytes 589832 | tf_op jit(solution)/shard_map/ppermute | solution.py:192
  76.4 9.9 %collective-permute-start.20 = (bf16[4,128,256]{2,1,0:T(8,128)(2,1)S(1)}, bf16[4,128,256]{2,1,0:T(8,128)(2,1)S(1)}, u32[]{:S(2)}, u32[]{:S(2)}) collective-permute-start(bf16[4,128,256]{2,1,0:T(8,128)(2,1)S(1)} %collective-permute-done.13), channel_id=1, source_target_pairs={{8,24},{9,25},{10,26},{11,27},{12,28},{13,29},{14,30},{15,31}} | collective-permute-start | bytes 786440 | tf_op jit(solution)/shard_map/ppermute | solution.py:228
  79.6 9.9 %collective-permute-start.19 = (bf16[4,128,256]{2,1,0:T(8,128)(2,1)S(1)}, bf16[4,128,256]{2,1,0:T(8,128)(2,1)S(1)}, u32[]{:S(2)}, u32[]{:S(2)}) collective-permute-start(bf16[4,128,256]{2,1,0:T(8,128)(2,1)S(1)} %get-tuple-element.94.first_mid), channel_id=1, source_target_pairs={{8,16},{16,24},{9,17},{17,25},{10,18},{18,26},{11,19},{19,27},{12,... | collective-permute-start | bytes 786440 | tf_op jit(solution)/shard_map/ppermute | solution.py:228
  83.6 11.4 %collective-permute-start.21 = (bf16[4,128,256]{2,1,0:T(8,128)(2,1)S(1)}, bf16[4,128,256]{2,1,0:T(8,128)(2,1)S(1)}, u32[]{:S(2)}, u32[]{:S(2)}) collective-permute-start(bf16[4,128,256]{2,1,0:T(8,128)(2,1)S(1)} %shard_map.66), channel_id=1, source_target_pairs={{8,16},{16,24},{9,17},{17,25},{10,18},{18,26},{11,19},{19,27},{12,... | collective-permute-start | bytes 786440 | tf_op jit(solution)/shard_map/ppermute | solution.py:228
  85.6 9.5 %collective-permute-start.22 = (bf16[4,128,256]{2,1,0:T(8,128)(2,1)S(1)}, bf16[4,128,256]{2,1,0:T(8,128)(2,1)S(1)}, u32[]{:S(2)}, u32[]{:S(2)}) collective-permute-start(bf16[4,128,256]{2,1,0:T(8,128)(2,1)S(1)} %collective-permute-done.15), channel_id=1, source_target_pairs={{8,24},{9,25},{10,26},{11,27},{12,28},{13,29},{14,30},{15,31}} | collective-permute-start | bytes 786440 | tf_op jit(solution)/shard_map/ppermute | solution.py:228
  95.3 7.3 %collective-permute-start.24 = (bf16[3,128,256]{2,1,0:T(8,128)(2,1)S(1)}, bf16[3,128,256]{2,1,0:T(8,128)(2,1)S(1)}, u32[]{:S(2)}, u32[]{:S(2)}) collective-permute-start(bf16[3,128,256]{2,1,0:T(8,128)(2,1)S(1)} %pad_maximum_fusion.9), channel_id=1, source_target_pairs={{1,2},{2,1},{3,4},{4,3},{5,6},{6,5},{9,10},{10,9},{11,12},{12,11},... | collective-permute-start | bytes 589832 | tf_op jit(solution)/shard_map/ppermute | solution.py:192
  99.0 3.6 %collective-permute-start.23 = (bf16[3,128,256]{2,1,0:T(8,128)(2,1)S(1)}, bf16[3,128,256]{2,1,0:T(8,128)(2,1)S(1)}, u32[]{:S(2)}, u32[]{:S(2)}) collective-permute-start(bf16[3,128,256]{2,1,0:T(8,128)(2,1)S(1)} %pad_maximum_fusion.8), channel_id=1, source_target_pairs={{0,1},{1,0},{2,3},{3,2},{4,5},{5,4},{6,7},{7,6},{8,9},{9,8},{10,11... | collective-permute-start | bytes 589832 | tf_op jit(solution)/shard_map/ppermute | solution.py:192

commit v19 on v18

--- a/solution.py
+++ b/solution.py
@@ -270,8 +270,11 @@
             following = arrived(1, 0), arrived(1, 1)
             following += tuple(swap(turn, starts, (following[1], 2), (following[0], 1)) for turn in range(2))
         elif slot < ticks:
+            relay_p = newer[0]
+            if slot == 1:
+                relay_p, _ = lax.optimization_barrier((relay_p, first[1]))
             relay_q, second = lax.optimization_barrier((newer[1], second))
-            relays = {0: send(newer[0], [(1, sections - 1)]), 1: send(relay_q, [(1, sections - 1)])}
+            relays = {0: send(relay_p, [(1, sections - 1)]), 1: send(relay_q, [(1, sections - 1)])}
             if across:
                 direct = {0: send(first[1], across), 1: send(second, across)}
         older, newer, relayed = newer, received, relays

time: 109 us -> 109 us (level)
  starting transfers between devices: 41.2 us -> 42.6 us
  waiting for transfers between devices: 30.1 us -> 28.8 us
    ppermute x15, waiting for transfers between devices: 27.7 us -> 26.1 us  [send(): return lax.ppermute(block, 'section', pairs) if pairs else block]
  transfers between devices with their start and end apart: 25 -> 25, of which waited for: 11 -> 12; matrix products, arithmetic and copies ran while one was open for 2% -> 2% of each run, Pallas kernels for 26% -> 26%
where the time goes in v19:
time: 109 us; the launch traced here: 108 us
  starting transfers between devices  42.6 us (39%)
  Pallas kernels  32.9 us (30%)
  waiting for transfers between devices  28.8 us (26%)
  local copies, waits for them, and re-layouts  1.31 us (1%)
  other arithmetic  1.15 us (1%)
    pallas_call x15, Pallas kernels, call(): pl.pallas_call(functools.partial(kernel, width), out_shape=[jax.ShapeDtyp...  32.9 us
    ppermute x15, waiting for transfers between devices, send(): return lax.ppermute(block, 'section', pairs) if pairs else block  26.1 us
    ppermute x10, starting transfers between devices, swap(): return lax.ppermute(jnp.concatenate(parts, axis=0), 'depth', pairs)  21.4 us
    ppermute x15, starting transfers between devices, send(): return lax.ppermute(block, 'section', pairs) if pairs else block  21.2 us
    ppermute x10, waiting for transfers between devices, swap(): return lax.ppermute(jnp.concatenate(parts, axis=0), 'depth', pairs)  2.74 us
  transfers between devices with their start and end apart: 25, of which 12 were waited for; matrix products, arithmetic and copies ran while one was open for 2% of the time, Pallas kernels for 26%

profile of v19, /device:TPU:13, one launch (start us, length us, event | category | flops | bytes accessed | tf_op | source)
XLA Modules:
  0.0 107.6 jit_solution(5601156712673345494)
XLA Ops:
  0.1 1.3 %collective-permute-start.3 = (bf16[2,4,128,256]{3,2,1,0:T(8,128)(2,1)}, bf16[2,4,128,256]{3,2,1,0:T(8,128)(2,1)S(1)}, u32[]{:S(2)}, u32[]{:S(2)}) collective-permute-start(bf16[2,4,128,256]{3,2,1,0:T(8,128)(2,1)} %bitcast.63), channel_id=1, source_target_pairs={{0,24},{8,16},{1,25},{9,17},{2,26},{10,18},{3,27},{11,19},{4,28},{... | collective-permute-start | bytes 1572872 | tf_op jit(solution)/shard_map/ppermute | solution.py:228
  1.4 1.1 slice_bitcast_fusion.6
  2.5 0.7 collective-permute-start
  3.3 3.1 %collective-permute-start.1 = (bf16[3,128,256]{2,1,0:T(8,128)(2,1)S(1)}, bf16[3,128,256]{2,1,0:T(8,128)(2,1)S(1)}, u32[]{:S(2)}, u32[]{:S(2)}) collective-permute-start(bf16[3,128,256]{2,1,0:T(8,128)(2,1)S(1)} %pad_maximum_fusion.1), channel_id=1, source_target_pairs={{1,2},{2,1},{3,4},{4,3},{5,6},{6,5},{9,10},{10,9},{11,12},{12,11},... | collective-permute-start | bytes 589832 | tf_op jit(solution)/shard_map/ppermute | solution.py:192
  6.4 4.1 %shard_map.55 = (bf16[2,128,256]{2,1,0:T(8,128)(2,1)S(1)}, f32[4,128,256]{2,1,0:T(8,128)S(1)}, bf16[6912,256]{1,0:T(8,128)(2,1)S(1)}) custom-call(bf16[4,128,256]{2,1,0:T(8,128)(2,1)S(1)} %get-tuple-element.110.p, bf16[4,128,256]{2,1,0:T(8,128)(2,1)S(1)} %get-tuple-element.109.q, bf16[6912,256]{1,0:T(8,128)(2,1)} %bitcast.55), custom_call_target="tpu_custom_call" | custom-call | flops 1 | bytes 1 | tf_op jit(solution)/shard_map/pallas_call | solution.py:141
  10.6 1.8 %shard_map.56 = (bf16[1,128,256]{2,1,0:T(8,128)(2,1)S(1)}, bf16[4,128,256]{2,1,0:T(8,128)(2,1)S(1)}, bf16[1,128,256]{2,1,0:T(8,128)(2,1)S(1)}) custom-call(s32[3]{0:T(128)S(1)} %add_convert_fusion.6.flags, bf16[4,128,256]{2,1,0:T(8,128)(2,1)S(1)} %get-tuple-element.110.p, bf16[2,128,256]{2,1,0:T(8,128)(2,1)S(1)} %get-tuple-element.63.inner, ...), custom_call_target="tpu_custom_call" | custom-call | flops 1 | bytes 1 | tf_op jit(solution)/shard_map/pallas_call | solution.py:141
  12.4 0.7 collective-permute-start.2
  13.1 2.1 %shard_map.57 = bf16[4,128,256]{2,1,0:T(8,128)(2,1)S(1)} custom-call(bf16[1,128,256]{2,1,0:T(8,128)(2,1)S(1)} %get-tuple-element.72.first_low, bf16[4,128,256]{2,1,0:T(8,128)(2,1)S(1)} %get-tuple-element.70.first_mid, bf16[1,128,256]{2,1,0:T(8,128)(2,1)S(1)} %get-tuple-element.73.first_high, bf16[4,128,256]{2,1,0:T(8,128)(2,1)S(1)} %get-tuple-element.109.q, ...), custom_call_target="tpu_custom_call" | custom-call | flops 1 | bytes 1 | tf_op jit(solution)/shard_map/pallas_call | solution.py:141
  15.2 0.6 collective-permute-done.3
  15.9 0.2 fusion.10
  16.2 4.6 %collective-permute-start.5 = (bf16[3,128,256]{2,1,0:T(8,128)(2,1)S(1)}, bf16[3,128,256]{2,1,0:T(8,128)(2,1)S(1)}, u32[]{:S(2)}, u32[]{:S(2)}) collective-permute-start(bf16[3,128,256]{2,1,0:T(8,128)(2,1)S(1)} %pad_maximum_fusion.3), channel_id=1, source_target_pairs={{1,2},{2,1},{3,4},{4,3},{5,6},{6,5},{9,10},{10,9},{11,12},{12,11},... | collective-permute-start | bytes 589832 | tf_op jit(solution)/shard_map/ppermute | solution.py:192
  20.9 0.7 collective-permute-start.9
  21.6 2.1 %shard_map.58 = (bf16[2,128,256]{2,1,0:T(8,128)(2,1)S(1)}, f32[4,128,256]{2,1,0:T(8,128)S(1)}) custom-call(bf16[4,128,256]{2,1,0:T(8,128)(2,1)S(1)} %get-tuple-element.108.p, bf16[4,128,256]{2,1,0:T(8,128)(2,1)S(1)} %get-tuple-element.107.q, bf16[6912,256]{1,0:T(8,128)(2,1)S(1)} %get-tuple-element.69.weights), custom_call_target="tpu_custom_call" | custom-call | flops 1 | bytes 1 | tf_op jit(solution)/shard_map/pallas_call | solution.py:141
  23.8 0.6 collective-permute-done.5.far
  24.3 1.8 %shard_map.59 = (bf16[1,128,256]{2,1,0:T(8,128)(2,1)S(1)}, bf16[4,128,256]{2,1,0:T(8,128)(2,1)S(1)}, bf16[1,128,256]{2,1,0:T(8,128)(2,1)S(1)}) custom-call(s32[3]{0:T(128)S(1)} %add_convert_fusion.6.flags, bf16[4,128,256]{2,1,0:T(8,128)(2,1)S(1)} %get-tuple-element.108.p, bf16[2,128,256]{2,1,0:T(8,128)(2,1)S(1)} %get-tuple-element.76.inner, ...), custom_call_target="tpu_custom_call" | custom-call | flops 1 | bytes 1 | tf_op jit(solution)/shard_map/pallas_call | solution.py:141
  26.1 0.7 collective-permute-start.7
  26.8 3.7 %collective-permute-start.6 = (bf16[4,128,256]{2,1,0:T(8,128)(2,1)S(1)}, bf16[4,128,256]{2,1,0:T(8,128)(2,1)S(1)}, u32[]{:S(2)}, u32[]{:S(2)}) collective-permute-start(bf16[4,128,256]{2,1,0:T(8,128)(2,1)S(1)} %get-tuple-element.78.first_mid), channel_id=1, source_target_pairs={{0,8},{8,16},{16,24},{1,9},{9,17},{17,25},{2,10},{10,18},{18,26},{... | collective-permute-start | bytes 786440 | tf_op jit(solution)/shard_map/ppermute | solution.py:228
  30.6 2.1 %shard_map.60 = bf16[4,128,256]{2,1,0:T(8,128)(2,1)S(1)} custom-call(bf16[1,128,256]{2,1,0:T(8,128)(2,1)S(1)} %get-tuple-element.81.first_low, bf16[4,128,256]{2,1,0:T(8,128)(2,1)S(1)} %get-tuple-element.78.first_mid, bf16[1,128,256]{2,1,0:T(8,128)(2,1)S(1)} %get-tuple-element.82.first_high, bf16[4,128,256]{2,1,0:T(8,128)(2,1)S(1)} %get-tuple-element.107.q, ...), custom_call_target="tpu_custom_call" | custom-call | flops 1 | bytes 1 | tf_op jit(solution)/shard_map/pallas_call | solution.py:141
  32.7 1.9 %collective-permute-start.8 = (bf16[4,128,256]{2,1,0:T(8,128)(2,1)S(1)}, bf16[4,128,256]{2,1,0:T(8,128)(2,1)S(1)}, u32[]{:S(2)}, u32[]{:S(2)}) collective-permute-start(bf16[4,128,256]{2,1,0:T(8,128)(2,1)S(1)} %shard_map.60), channel_id=1, source_target_pairs={{0,8},{8,16},{16,24},{1,9},{9,17},{17,25},{2,10},{10,18},{18,26},{... | collective-permute-start | bytes 786440 | tf_op jit(solution)/shard_map/ppermute | solution.py:228
  34.6 0.7 collective-permute-start.10
  35.3 3.1 %collective-permute-done.6 = bf16[4,128,256]{2,1,0:T(8,128)(2,1)S(1)} collective-permute-done((bf16[4,128,256]{2,1,0:T(8,128)(2,1)S(1)}, bf16[4,128,256]{2,1,0:T(8,128)(2,1)S(1)}, u32[]{:S(2)}, u32[]{:S(2)}) %collective-permute-start.6) | collective-permute-done | bytes 262176 | tf_op jit(solution)/shard_map/ppermute | solution.py:228
  38.5 5.5 %collective-permute-done.8 = bf16[4,128,256]{2,1,0:T(8,128)(2,1)S(1)} collective-permute-done((bf16[4,128,256]{2,1,0:T(8,128)(2,1)S(1)}, bf16[4,128,256]{2,1,0:T(8,128)(2,1)S(1)}, u32[]{:S(2)}, u32[]{:S(2)}) %collective-permute-start.8) | collective-permute-done | bytes 262176 | tf_op jit(solution)/shard_map/ppermute | solution.py:228
  44.2 4.7 %collective-permute-start.12 = (bf16[3,128,256]{2,1,0:T(8,128)(2,1)S(1)}, bf16[3,128,256]{2,1,0:T(8,128)(2,1)S(1)}, u32[]{:S(2)}, u32[]{:S(2)}) collective-permute-start(bf16[3,128,256]{2,1,0:T(8,128)(2,1)S(1)} %pad_maximum_fusion.5), channel_id=1, source_target_pairs={{1,2},{2,1},{3,4},{4,3},{5,6},{6,5},{9,10},{10,9},{11,12},{12,11},... | collective-permute-start | bytes 589832 | tf_op jit(solution)/shard_map/ppermute | solution.py:192
  49.1 2.1 %shard_map.61 = (bf16[2,128,256]{2,1,0:T(8,128)(2,1)S(1)}, f32[4,128,256]{2,1,0:T(8,128)S(1)}) custom-call(bf16[4,128,256]{2,1,0:T(8,128)(2,1)S(1)} %fusion.17.p, bf16[4,128,256]{2,1,0:T(8,128)(2,1)S(1)} %fusion.16.q, bf16[6912,256]{1,0:T(8,128)(2,1)S(1)} %get-tuple-element.69.weights), custom_call_target="tpu_custom_call" | custom-call | flops 1 | bytes 1 | tf_op jit(solution)/shard_map/pallas_call | solution.py:141
  51.2 0.7 collective-permute-start.14
  52.1 1.8 %shard_map.62 = (bf16[1,128,256]{2,1,0:T(8,128)(2,1)S(1)}, bf16[4,128,256]{2,1,0:T(8,128)(2,1)S(1)}, bf16[1,128,256]{2,1,0:T(8,128)(2,1)S(1)}) custom-call(s32[3]{0:T(128)S(1)} %add_convert_fusion.6.flags, bf16[4,128,256]{2,1,0:T(8,128)(2,1)S(1)} %fusion.17.p, bf16[2,128,256]{2,1,0:T(8,128)(2,1)S(1)} %get-tuple-element.86.inner, ...), custom_call_target="tpu_custom_call" | custom-call | flops 1 | bytes 1 | tf_op jit(solution)/shard_map/pallas_call | solution.py:141
  53.9 2.9 %collective-permute-start.13 = (bf16[4,128,256]{2,1,0:T(8,128)(2,1)S(1)}, bf16[4,128,256]{2,1,0:T(8,128)(2,1)S(1)}, u32[]{:S(2)}, u32[]{:S(2)}) collective-permute-start(bf16[4,128,256]{2,1,0:T(8,128)(2,1)S(1)} %get-tuple-element.88.first_mid), channel_id=1, source_target_pairs={{0,8},{8,16},{16,24},{1,9},{9,17},{17,25},{2,10},{10,18},{18,26},{... | collective-permute-start | bytes 786440 | tf_op jit(solution)/shard_map/ppermute | solution.py:228
  56.8 2.1 %shard_map.63 = bf16[4,128,256]{2,1,0:T(8,128)(2,1)S(1)} custom-call(bf16[1,128,256]{2,1,0:T(8,128)(2,1)S(1)} %get-tuple-element.89.first_low, bf16[4,128,256]{2,1,0:T(8,128)(2,1)S(1)} %get-tuple-element.88.first_mid, bf16[1,128,256]{2,1,0:T(8,128)(2,1)S(1)} %get-tuple-element.90.first_high, bf16[4,128,256]{2,1,0:T(8,128)(2,1)S(1)} %fusion.16.q, ...), custom_call_target="tpu_custom_call" | custom-call | flops 1 | bytes 1 | tf_op jit(solution)/shard_map/pallas_call | solution.py:141
  58.9 1.9 %collective-permute-start.15 = (bf16[4,128,256]{2,1,0:T(8,128)(2,1)S(1)}, bf16[4,128,256]{2,1,0:T(8,128)(2,1)S(1)}, u32[]{:S(2)}, u32[]{:S(2)}) collective-permute-start(bf16[4,128,256]{2,1,0:T(8,128)(2,1)S(1)} %shard_map.63), channel_id=1, source_target_pairs={{0,8},{8,16},{16,24},{1,9},{9,17},{17,25},{2,10},{10,18},{18,26},{... | collective-permute-start | bytes 786440 | tf_op jit(solution)/shard_map/ppermute | solution.py:228
  60.9 0.7 collective-permute-start.16
  61.6 3.0 %collective-permute-done.13 = bf16[4,128,256]{2,1,0:T(8,128)(2,1)S(1)} collective-permute-done((bf16[4,128,256]{2,1,0:T(8,128)(2,1)S(1)}, bf16[4,128,256]{2,1,0:T(8,128)(2,1)S(1)}, u32[]{:S(2)}, u32[]{:S(2)}) %collective-permute-start.13) | collective-permute-done | bytes 262176 | tf_op jit(solution)/shard_map/ppermute | solution.py:228
  64.6 5.5 %collective-permute-done.15 = bf16[4,128,256]{2,1,0:T(8,128)(2,1)S(1)} collective-permute-done((bf16[4,128,256]{2,1,0:T(8,128)(2,1)S(1)}, bf16[4,128,256]{2,1,0:T(8,128)(2,1)S(1)}, u32[]{:S(2)}, u32[]{:S(2)}) %collective-permute-start.15) | collective-permute-done | bytes 262176 | tf_op jit(solution)/shard_map/ppermute | solution.py:228
  70.4 3.9 %collective-permute-start.18 = (bf16[3,128,256]{2,1,0:T(8,128)(2,1)S(1)}, bf16[3,128,256]{2,1,0:T(8,128)(2,1)S(1)}, u32[]{:S(2)}, u32[]{:S(2)}) collective-permute-start(bf16[3,128,256]{2,1,0:T(8,128)(2,1)S(1)} %pad_maximum_fusion.7), channel_id=1, source_target_pairs={{1,2},{2,1},{3,4},{4,3},{5,6},{6,5},{9,10},{10,9},{11,12},{12,11},... | collective-permute-start | bytes 589832 | tf_op jit(solution)/shard_map/ppermute | solution.py:192
  74.3 2.1 %shard_map.64 = (bf16[2,128,256]{2,1,0:T(8,128)(2,1)S(1)}, f32[4,128,256]{2,1,0:T(8,128)S(1)}) custom-call(bf16[4,128,256]{2,1,0:T(8,128)(2,1)S(1)} %fusion.15.p, bf16[4,128,256]{2,1,0:T(8,128)(2,1)S(1)} %fusion.14.q, bf16[6912,256]{1,0:T(8,128)(2,1)S(1)} %get-tuple-element.69.weights), custom_call_target="tpu_custom_call" | custom-call | flops 1 | bytes 1 | tf_op jit(solution)/shard_map/pallas_call | solution.py:141
  76.5 0.7 collective-permute-start.20
  77.2 0.7 collective-permute-done.18.far
  77.9 1.8 %shard_map.65 = (bf16[1,128,256]{2,1,0:T(8,128)(2,1)S(1)}, bf16[4,128,256]{2,1,0:T(8,128)(2,1)S(1)}, bf16[1,128,256]{2,1,0:T(8,128)(2,1)S(1)}) custom-call(s32[3]{0:T(128)S(1)} %add_convert_fusion.6.flags, bf16[4,128,256]{2,1,0:T(8,128)(2,1)S(1)} %fusion.15.p, bf16[2,128,256]{2,1,0:T(8,128)(2,1)S(1)} %get-tuple-element.94.inner, ...), custom_call_target="tpu_custom_call" | custom-call | flops 1 | bytes 1 | tf_op jit(solution)/shard_map/pallas_call | solution.py:141
  79.7 2.2 %collective-permute-start.19 = (bf16[4,128,256]{2,1,0:T(8,128)(2,1)S(1)}, bf16[4,128,256]{2,1,0:T(8,128)(2,1)S(1)}, u32[]{:S(2)}, u32[]{:S(2)}) collective-permute-start(bf16[4,128,256]{2,1,0:T(8,128)(2,1)S(1)} %get-tuple-element.96.first_mid), channel_id=1, source_target_pairs={{8,16},{16,24},{9,17},{17,25},{10,18},{18,26},{11,19},{19,27},{12,... | collective-permute-start | bytes 786440 | tf_op jit(solution)/shard_map/ppermute | solution.py:228
  81.8 2.1 %shard_map.66 = bf16[4,128,256]{2,1,0:T(8,128)(2,1)S(1)} custom-call(bf16[1,128,256]{2,1,0:T(8,128)(2,1)S(1)} %get-tuple-element.97.first_low, bf16[4,128,256]{2,1,0:T(8,128)(2,1)S(1)} %get-tuple-element.96.first_mid, bf16[1,128,256]{2,1,0:T(8,128)(2,1)S(1)} %get-tuple-element.98.first_high, bf16[4,128,256]{2,1,0:T(8,128)(2,1)S(1)} %fusion.14.q, ...), custom_call_target="tpu_custom_call" | custom-call | flops 1 | bytes 1 | tf_op jit(solution)/shard_map/pallas_call | solution.py:141
  84.0 1.9 %collective-permute-start.21 = (bf16[4,128,256]{2,1,0:T(8,128)(2,1)S(1)}, bf16[4,128,256]{2,1,0:T(8,128)(2,1)S(1)}, u32[]{:S(2)}, u32[]{:S(2)}) collective-permute-start(bf16[4,128,256]{2,1,0:T(8,128)(2,1)S(1)} %shard_map.66), channel_id=1, source_target_pairs={{8,16},{16,24},{9,17},{17,25},{10,18},{18,26},{11,19},{19,27},{12,... | collective-permute-start | bytes 786440 | tf_op jit(solution)/shard_map/ppermute | solution.py:228
  85.9 0.7 collective-permute-start.22
  86.6 2.9 %collective-permute-done.19 = bf16[4,128,256]{2,1,0:T(8,128)(2,1)S(1)} collective-permute-done((bf16[4,128,256]{2,1,0:T(8,128)(2,1)S(1)}, bf16[4,128,256]{2,1,0:T(8,128)(2,1)S(1)}, u32[]{:S(2)}, u32[]{:S(2)}) %collective-permute-start.19) | collective-permute-done | bytes 262176 | tf_op jit(solution)/shard_map/ppermute | solution.py:228
  89.6 5.5 %collective-permute-done.21 = bf16[4,128,256]{2,1,0:T(8,128)(2,1)S(1)} collective-permute-done((bf16[4,128,256]{2,1,0:T(8,128)(2,1)S(1)}, bf16[4,128,256]{2,1,0:T(8,128)(2,1)S(1)}, u32[]{:S(2)}, u32[]{:S(2)}) %collective-permute-start.21) | collective-permute-done | bytes 262176 | tf_op jit(solution)/shard_map/ppermute | solution.py:228
  95.3 4.0 %collective-permute-start.24 = (bf16[3,128,256]{2,1,0:T(8,128)(2,1)S(1)}, bf16[3,128,256]{2,1,0:T(8,128)(2,1)S(1)}, u32[]{:S(2)}, u32[]{:S(2)}) collective-permute-start(bf16[3,128,256]{2,1,0:T(8,128)(2,1)S(1)} %pad_maximum_fusion.9), channel_id=1, source_target_pairs={{1,2},{2,1},{3,4},{4,3},{5,6},{6,5},{9,10},{10,9},{11,12},{12,11},... | collective-permute-start | bytes 589832 | tf_op jit(solution)/shard_map/ppermute | solution.py:192
  99.4 2.1 %shard_map.67 = (bf16[2,128,256]{2,1,0:T(8,128)(2,1)S(1)}, f32[4,128,256]{2,1,0:T(8,128)S(1)}) custom-call(bf16[4,128,256]{2,1,0:T(8,128)(2,1)S(1)} %fusion.13.p, bf16[4,128,256]{2,1,0:T(8,128)(2,1)S(1)} %fusion.12.q, bf16[6912,256]{1,0:T(8,128)(2,1)S(1)} %get-tuple-element.69.weights), custom_call_target="tpu_custom_call" | custom-call | flops 1 | bytes 1 | tf_op jit(solution)/shard_map/pallas_call | solution.py:141
  101.6 1.2 %collective-permute-done.24.far = bf16[3,128,256]{2,1,0:T(8,128)(2,1)S(1)} collective-permute-done((bf16[3,128,256]{2,1,0:T(8,128)(2,1)S(1)}, bf16[3,128,256]{2,1,0:T(8,128)(2,1)S(1)}, u32[]{:S(2)}, u32[]{:S(2)}) %collective-permute-start.24) | collective-permute-done | bytes 196640 | tf_op jit(solution)/shard_map/ppermute | solution.py:192
  102.7 1.8 %shard_map.68 = (bf16[1,128,256]{2,1,0:T(8,128)(2,1)S(1)}, bf16[4,128,256]{2,1,0:T(8,128)(2,1)S(1)}, bf16[1,128,256]{2,1,0:T(8,128)(2,1)S(1)}) custom-call(s32[3]{0:T(128)S(1)} %add_convert_fusion.6.flags, bf16[4,128,256]{2,1,0:T(8,128)(2,1)S(1)} %fusion.13.p, bf16[2,128,256]{2,1,0:T(8,128)(2,1)S(1)} %get-tuple-element.102.inner, ...), custom_call_target="tpu_custom_call" | custom-call | flops 1 | bytes 1 | tf_op jit(solution)/shard_map/pallas_call | solution.py:141
  104.5 2.8 %shard_map.69 = bf16[2,4,128,256]{3,2,1,0:T(8,128)(2,1)} custom-call(bf16[1,128,256]{2,1,0:T(8,128)(2,1)S(1)} %get-tuple-element.104.first_low, bf16[4,128,256]{2,1,0:T(8,128)(2,1)S(1)} %get-tuple-element.105.first_mid, bf16[1,128,256]{2,1,0:T(8,128)(2,1)S(1)} %get-tuple-element.106.first_high, bf16[4,128,256]{2,1,0:T(8,128)(2,1)S(1)} %fusion.12.q, ...), custom_call_target="tpu_custom_call" | custom-call | flops 1 | bytes 1 | tf_op jit(solution)/shard_map/pallas_call | solution.py:141
  (52 shorter events, 1.8 us)
Async XLA Ops:
  0.1 15.8 %collective-permute-start.3 = (bf16[2,4,128,256]{3,2,1,0:T(8,128)(2,1)}, bf16[2,4,128,256]{3,2,1,0:T(8,128)(2,1)S(1)}, u32[]{:S(2)}, u32[]{:S(2)}) collective-permute-start(bf16[2,4,128,256]{3,2,1,0:T(8,128)(2,1)} %bitcast.63), channel_id=1, source_target_pairs={{0,24},{8,16},{1,25},{9,17},{2,26},{10,18},{3,27},{11,19},{4,28},{... | collective-permute-start | bytes 1572872 | tf_op jit(solution)/shard_map/ppermute | solution.py:228
  2.5 7.9 %collective-permute-start = (bf16[3,128,256]{2,1,0:T(8,128)(2,1)S(1)}, bf16[3,128,256]{2,1,0:T(8,128)(2,1)S(1)}, u32[]{:S(2)}, u32[]{:S(2)}) collective-permute-start(bf16[3,128,256]{2,1,0:T(8,128)(2,1)S(1)} %pad_maximum_fusion), channel_id=1, source_target_pairs={{0,1},{1,0},{2,3},{3,2},{4,5},{5,4},{6,7},{7,6},{8,9},{9,8},{10,11... | collective-permute-start | bytes 589832 | tf_op jit(solution)/shard_map/ppermute | solution.py:192
  3.3 7.3 %collective-permute-start.1 = (bf16[3,128,256]{2,1,0:T(8,128)(2,1)S(1)}, bf16[3,128,256]{2,1,0:T(8,128)(2,1)S(1)}, u32[]{:S(2)}, u32[]{:S(2)}) collective-permute-start(bf16[3,128,256]{2,1,0:T(8,128)(2,1)S(1)} %pad_maximum_fusion.1), channel_id=1, source_target_pairs={{1,2},{2,1},{3,4},{4,3},{5,6},{6,5},{9,10},{10,9},{11,12},{12,11},... | collective-permute-start | bytes 589832 | tf_op jit(solution)/shard_map/ppermute | solution.py:192
  10.6 2.5 %copy-start = (bf16[1,3,3,3,256,256]{5,4,3,2,1,0:T(8,128)(2,1)S(1)}, bf16[1,3,3,3,256,256]{5,4,3,2,1,0:T(8,128)(2,1)}, u32[]{:S(2)}) copy-start(bf16[1,3,3,3,256,256]{5,4,3,2,1,0:T(8,128)(2,1)} %param.9) | copy-start | bytes 10616836
  12.4 13.8 %collective-permute-start.2 = (bf16[4,128,256]{2,1,0:T(8,128)(2,1)S(1)}, bf16[4,128,256]{2,1,0:T(8,128)(2,1)S(1)}, u32[]{:S(2)}, u32[]{:S(2)}) collective-permute-start(bf16[4,128,256]{2,1,0:T(8,128)(2,1)S(1)} %get-tuple-element.70.first_mid), channel_id=1, source_target_pairs={{0,8},{1,9},{2,10},{3,11},{4,12},{5,13},{6,14},{7,15}} | collective-permute-start | bytes 786440 | tf_op jit(solution)/shard_map/ppermute | solution.py:228
  13.1 2.8 %copy-start.1 = (bf16[3,2,4,16,8,256]{5,4,3,2,1,0:T(8,128)(2,1)S(1)}, bf16[3,2,4,16,8,256]{5,4,3,2,1,0:T(8,128)(2,1)}, u32[]{:S(2)}) copy-start(bf16[3,2,4,16,8,256]{5,4,3,2,1,0:T(8,128)(2,1)} %param.7) | copy-start | bytes 4718596
  13.1 2.8 %copy-start.2 = (bf16[1,2,4,16,8,256]{5,4,3,2,1,0:T(8,128)(2,1)S(1)}, bf16[1,2,4,16,8,256]{5,4,3,2,1,0:T(8,128)(2,1)}, u32[]{:S(2)}) copy-start(bf16[1,2,4,16,8,256]{5,4,3,2,1,0:T(8,128)(2,1)} %param.5) | copy-start | bytes 1572868
  16.2 8.1 %collective-permute-start.5 = (bf16[3,128,256]{2,1,0:T(8,128)(2,1)S(1)}, bf16[3,128,256]{2,1,0:T(8,128)(2,1)S(1)}, u32[]{:S(2)}, u32[]{:S(2)}) collective-permute-start(bf16[3,128,256]{2,1,0:T(8,128)(2,1)S(1)} %pad_maximum_fusion.3), channel_id=1, source_target_pairs={{1,2},{2,1},{3,4},{4,3},{5,6},{6,5},{9,10},{10,9},{11,12},{12,11},... | collective-permute-start | bytes 589832 | tf_op jit(solution)/shard_map/ppermute | solution.py:192
  20.9 3.5 %collective-permute-start.4 = (bf16[3,128,256]{2,1,0:T(8,128)(2,1)S(1)}, bf16[3,128,256]{2,1,0:T(8,128)(2,1)S(1)}, u32[]{:S(2)}, u32[]{:S(2)}) collective-permute-start(bf16[3,128,256]{2,1,0:T(8,128)(2,1)S(1)} %pad_maximum_fusion.2), channel_id=1, source_target_pairs={{0,1},{1,0},{2,3},{3,2},{4,5},{5,4},{6,7},{7,6},{8,9},{9,8},{10,11... | collective-permute-start | bytes 589832 | tf_op jit(solution)/shard_map/ppermute | solution.py:192
  20.9 13.7 %collective-permute-start.9 = (bf16[4,128,256]{2,1,0:T(8,128)(2,1)S(1)}, bf16[4,128,256]{2,1,0:T(8,128)(2,1)S(1)}, u32[]{:S(2)}, u32[]{:S(2)}) collective-permute-start(bf16[4,128,256]{2,1,0:T(8,128)(2,1)S(1)} %shard_map.57), channel_id=1, source_target_pairs={{0,8},{1,9},{2,10},{3,11},{4,12},{5,13},{6,14},{7,15}} | collective-permute-start | bytes 786440 | tf_op jit(solution)/shard_map/ppermute | solution.py:228
  26.1 9.2 %collective-permute-start.7 = (bf16[4,128,256]{2,1,0:T(8,128)(2,1)S(1)}, bf16[4,128,256]{2,1,0:T(8,128)(2,1)S(1)}, u32[]{:S(2)}, u32[]{:S(2)}) collective-permute-start(bf16[4,128,256]{2,1,0:T(8,128)(2,1)S(1)} %collective-permute-done.2), channel_id=1, source_target_pairs={{8,24},{9,25},{10,26},{11,27},{12,28},{13,29},{14,30},{15,31}} | collective-permute-start | bytes 786440 | tf_op jit(solution)/shard_map/ppermute | solution.py:228
  26.8 11.6 %collective-permute-start.6 = (bf16[4,128,256]{2,1,0:T(8,128)(2,1)S(1)}, bf16[4,128,256]{2,1,0:T(8,128)(2,1)S(1)}, u32[]{:S(2)}, u32[]{:S(2)}) collective-permute-start(bf16[4,128,256]{2,1,0:T(8,128)(2,1)S(1)} %get-tuple-element.78.first_mid), channel_id=1, source_target_pairs={{0,8},{8,16},{16,24},{1,9},{9,17},{17,25},{2,10},{10,18},{18,26},{... | collective-permute-start | bytes 786440 | tf_op jit(solution)/shard_map/ppermute | solution.py:228
  32.7 11.3 %collective-permute-start.8 = (bf16[4,128,256]{2,1,0:T(8,128)(2,1)S(1)}, bf16[4,128,256]{2,1,0:T(8,128)(2,1)S(1)}, u32[]{:S(2)}, u32[]{:S(2)}) collective-permute-start(bf16[4,128,256]{2,1,0:T(8,128)(2,1)S(1)} %shard_map.60), channel_id=1, source_target_pairs={{0,8},{8,16},{16,24},{1,9},{9,17},{17,25},{2,10},{10,18},{18,26},{... | collective-permute-start | bytes 786440 | tf_op jit(solution)/shard_map/ppermute | solution.py:228
  34.6 9.4 %collective-permute-start.10 = (bf16[4,128,256]{2,1,0:T(8,128)(2,1)S(1)}, bf16[4,128,256]{2,1,0:T(8,128)(2,1)S(1)}, u32[]{:S(2)}, u32[]{:S(2)}) collective-permute-start(bf16[4,128,256]{2,1,0:T(8,128)(2,1)S(1)} %collective-permute-done.9), channel_id=1, source_target_pairs={{8,24},{9,25},{10,26},{11,27},{12,28},{13,29},{14,30},{15,31}} | collective-permute-start | bytes 786440 | tf_op jit(solution)/shard_map/ppermute | solution.py:228
  44.2 7.9 %collective-permute-start.12 = (bf16[3,128,256]{2,1,0:T(8,128)(2,1)S(1)}, bf16[3,128,256]{2,1,0:T(8,128)(2,1)S(1)}, u32[]{:S(2)}, u32[]{:S(2)}) collective-permute-start(bf16[3,128,256]{2,1,0:T(8,128)(2,1)S(1)} %pad_maximum_fusion.5), channel_id=1, source_target_pairs={{1,2},{2,1},{3,4},{4,3},{5,6},{6,5},{9,10},{10,9},{11,12},{12,11},... | collective-permute-start | bytes 589832 | tf_op jit(solution)/shard_map/ppermute | solution.py:192
  49.0 3.1 %collective-permute-start.11 = (bf16[3,128,256]{2,1,0:T(8,128)(2,1)S(1)}, bf16[3,128,256]{2,1,0:T(8,128)(2,1)S(1)}, u32[]{:S(2)}, u32[]{:S(2)}) collective-permute-start(bf16[3,128,256]{2,1,0:T(8,128)(2,1)S(1)} %pad_maximum_fusion.4), channel_id=1, source_target_pairs={{0,1},{1,0},{2,3},{3,2},{4,5},{5,4},{6,7},{7,6},{8,9},{9,8},{10,11... | collective-permute-start | bytes 589832 | tf_op jit(solution)/shard_map/ppermute | solution.py:192
  51.2 10.3 %collective-permute-start.14 = (bf16[4,128,256]{2,1,0:T(8,128)(2,1)S(1)}, bf16[4,128,256]{2,1,0:T(8,128)(2,1)S(1)}, u32[]{:S(2)}, u32[]{:S(2)}) collective-permute-start(bf16[4,128,256]{2,1,0:T(8,128)(2,1)S(1)} %collective-permute-done.6), channel_id=1, source_target_pairs={{8,24},{9,25},{10,26},{11,27},{12,28},{13,29},{14,30},{15,31}} | collective-permute-start | bytes 786440 | tf_op jit(solution)/shard_map/ppermute | solution.py:228
  53.9 10.6 %collective-permute-start.13 = (bf16[4,128,256]{2,1,0:T(8,128)(2,1)S(1)}, bf16[4,128,256]{2,1,0:T(8,128)(2,1)S(1)}, u32[]{:S(2)}, u32[]{:S(2)}) collective-permute-start(bf16[4,128,256]{2,1,0:T(8,128)(2,1)S(1)} %get-tuple-element.88.first_mid), channel_id=1, source_target_pairs={{0,8},{8,16},{16,24},{1,9},{9,17},{17,25},{2,10},{10,18},{18,26},{... | collective-permute-start | bytes 786440 | tf_op jit(solution)/shard_map/ppermute | solution.py:228
  58.9 11.2 %collective-permute-start.15 = (bf16[4,128,256]{2,1,0:T(8,128)(2,1)S(1)}, bf16[4,128,256]{2,1,0:T(8,128)(2,1)S(1)}, u32[]{:S(2)}, u32[]{:S(2)}) collective-permute-start(bf16[4,128,256]{2,1,0:T(8,128)(2,1)S(1)} %shard_map.63), channel_id=1, source_target_pairs={{0,8},{8,16},{16,24},{1,9},{9,17},{17,25},{2,10},{10,18},{18,26},{... | collective-permute-start | bytes 786440 | tf_op jit(solution)/shard_map/ppermute | solution.py:228
  60.9 9.3 %collective-permute-start.16 = (bf16[4,128,256]{2,1,0:T(8,128)(2,1)S(1)}, bf16[4,128,256]{2,1,0:T(8,128)(2,1)S(1)}, u32[]{:S(2)}, u32[]{:S(2)}) collective-permute-start(bf16[4,128,256]{2,1,0:T(8,128)(2,1)S(1)} %collective-permute-done.8), channel_id=1, source_target_pairs={{8,24},{9,25},{10,26},{11,27},{12,28},{13,29},{14,30},{15,31}} | collective-permute-start | bytes 786440 | tf_op jit(solution)/shard_map/ppermute | solution.py:228
  70.4 7.5 %collective-permute-start.18 = (bf16[3,128,256]{2,1,0:T(8,128)(2,1)S(1)}, bf16[3,128,256]{2,1,0:T(8,128)(2,1)S(1)}, u32[]{:S(2)}, u32[]{:S(2)}) collective-permute-start(bf16[3,128,256]{2,1,0:T(8,128)(2,1)S(1)} %pad_maximum_fusion.7), channel_id=1, source_target_pairs={{1,2},{2,1},{3,4},{4,3},{5,6},{6,5},{9,10},{10,9},{11,12},{12,11},... | collective-permute-start | bytes 589832 | tf_op jit(solution)/shard_map/ppermute | solution.py:192
  74.3 3.6 %collective-permute-start.17 = (bf16[3,128,256]{2,1,0:T(8,128)(2,1)S(1)}, bf16[3,128,256]{2,1,0:T(8,128)(2,1)S(1)}, u32[]{:S(2)}, u32[]{:S(2)}) collective-permute-start(bf16[3,128,256]{2,1,0:T(8,128)(2,1)S(1)} %pad_maximum_fusion.6), channel_id=1, source_target_pairs={{0,1},{1,0},{2,3},{3,2},{4,5},{5,4},{6,7},{7,6},{8,9},{9,8},{10,11... | collective-permute-start | bytes 589832 | tf_op jit(solution)/shard_map/ppermute | solution.py:192
  76.5 10.1 %collective-permute-start.20 = (bf16[4,128,256]{2,1,0:T(8,128)(2,1)S(1)}, bf16[4,128,256]{2,1,0:T(8,128)(2,1)S(1)}, u32[]{:S(2)}, u32[]{:S(2)}) collective-permute-start(bf16[4,128,256]{2,1,0:T(8,128)(2,1)S(1)} %collective-permute-done.13), channel_id=1, source_target_pairs={{8,24},{9,25},{10,26},{11,27},{12,28},{13,29},{14,30},{15,31}} | collective-permute-start | bytes 786440 | tf_op jit(solution)/shard_map/ppermute | solution.py:228
  79.7 9.8 %collective-permute-start.19 = (bf16[4,128,256]{2,1,0:T(8,128)(2,1)S(1)}, bf16[4,128,256]{2,1,0:T(8,128)(2,1)S(1)}, u32[]{:S(2)}, u32[]{:S(2)}) collective-permute-start(bf16[4,128,256]{2,1,0:T(8,128)(2,1)S(1)} %get-tuple-element.96.first_mid), channel_id=1, source_target_pairs={{8,16},{16,24},{9,17},{17,25},{10,18},{18,26},{11,19},{19,27},{12,... | collective-permute-start | bytes 786440 | tf_op jit(solution)/shard_map/ppermute | solution.py:228
  84.0 11.1 %collective-permute-start.21 = (bf16[4,128,256]{2,1,0:T(8,128)(2,1)S(1)}, bf16[4,128,256]{2,1,0:T(8,128)(2,1)S(1)}, u32[]{:S(2)}, u32[]{:S(2)}) collective-permute-start(bf16[4,128,256]{2,1,0:T(8,128)(2,1)S(1)} %shard_map.66), channel_id=1, source_target_pairs={{8,16},{16,24},{9,17},{17,25},{10,18},{18,26},{11,19},{19,27},{12,... | collective-permute-start | bytes 786440 | tf_op jit(solution)/shard_map/ppermute | solution.py:228
  85.9 9.2 %collective-permute-start.22 = (bf16[4,128,256]{2,1,0:T(8,128)(2,1)S(1)}, bf16[4,128,256]{2,1,0:T(8,128)(2,1)S(1)}, u32[]{:S(2)}, u32[]{:S(2)}) collective-permute-start(bf16[4,128,256]{2,1,0:T(8,128)(2,1)S(1)} %collective-permute-done.15), channel_id=1, source_target_pairs={{8,24},{9,25},{10,26},{11,27},{12,28},{13,29},{14,30},{15,31}} | collective-permute-start | bytes 786440 | tf_op jit(solution)/shard_map/ppermute | solution.py:228
  95.3 7.4 %collective-permute-start.24 = (bf16[3,128,256]{2,1,0:T(8,128)(2,1)S(1)}, bf16[3,128,256]{2,1,0:T(8,128)(2,1)S(1)}, u32[]{:S(2)}, u32[]{:S(2)}) collective-permute-start(bf16[3,128,256]{2,1,0:T(8,128)(2,1)S(1)} %pad_maximum_fusion.9), channel_id=1, source_target_pairs={{1,2},{2,1},{3,4},{4,3},{5,6},{6,5},{9,10},{10,9},{11,12},{12,11},... | collective-permute-start | bytes 589832 | tf_op jit(solution)/shard_map/ppermute | solution.py:192
  99.4 3.4 %collective-permute-start.23 = (bf16[3,128,256]{2,1,0:T(8,128)(2,1)S(1)}, bf16[3,128,256]{2,1,0:T(8,128)(2,1)S(1)}, u32[]{:S(2)}, u32[]{:S(2)}) collective-permute-start(bf16[3,128,256]{2,1,0:T(8,128)(2,1)S(1)} %pad_maximum_fusion.8), channel_id=1, source_target_pairs={{0,1},{1,0},{2,3},{3,2},{4,5},{5,4},{6,7},{7,6},{8,9},{9,8},{10,11... | collective-permute-start | bytes 589832 | tf_op jit(solution)/shard_map/ppermute | solution.py:192

commit v20 on v18

--- a/solution.py
+++ b/solution.py
@@ -263,6 +263,10 @@
         if slot < ticks:
             received[0] = send(first[1], onward)
         second = second_half(first, q, w_two, width, slot == ticks)
+        if 0 < slot < ticks:
+            relay_p = send(newer[0], [(1, sections - 1)])
+            if slot > 1:
+                relay_p, second = lax.optimization_barrier((relay_p, second))
         if slot < ticks:
             received[1] = send(second, onward)
         if slot == 0:
@@ -271,7 +275,7 @@
             following += tuple(swap(turn, starts, (following[1], 2), (following[0], 1)) for turn in range(2))
         elif slot < ticks:
             relay_q, second = lax.optimization_barrier((newer[1], second))
-            relays = {0: send(newer[0], [(1, sections - 1)]), 1: send(relay_q, [(1, sections - 1)])}
+            relays = {0: relay_p, 1: send(relay_q, [(1, sections - 1)])}
             if across:
                 direct = {0: send(first[1], across), 1: send(second, across)}
         older, newer, relayed = newer, received, relays

time: 109 us -> 109 us (level)
  no operation moved by 1% of the time
where the time goes in v20:
time: 109 us; the launch traced here: 107 us
  starting transfers between devices  41.2 us (38%)
  Pallas kernels  32.9 us (30%)
  waiting for transfers between devices  30.1 us (28%)
  local copies, waits for them, and re-layouts  1.31 us (1%)
  other arithmetic  1.15 us (1%)
    pallas_call x15, Pallas kernels, call(): pl.pallas_call(functools.partial(kernel, width), out_shape=[jax.ShapeDtyp...  32.9 us
    ppermute x15, waiting for transfers between devices, send(): return lax.ppermute(block, 'section', pairs) if pairs else block  27.6 us
    ppermute x10, starting transfers between devices, swap(): return lax.ppermute(jnp.concatenate(parts, axis=0), 'depth', pairs)  20.7 us
    ppermute x15, starting transfers between devices, send(): return lax.ppermute(block, 'section', pairs) if pairs else block  20.5 us
    ppermute x10, waiting for transfers between devices, swap(): return lax.ppermute(jnp.concatenate(parts, axis=0), 'depth', pairs)  2.44 us
  transfers between devices with their start and end apart: 25, of which 11 were waited for; matrix products, arithmetic and copies ran while one was open for 2% of the time, Pallas kernels for 26%

profile of v20, /device:TPU:13, one launch (start us, length us, event | category | flops | bytes accessed | tf_op | source)
XLA Modules:
  0.0 107.4 jit_solution(11902693501243910634)
XLA Ops:
  0.1 1.3 %collective-permute-start.3 = (bf16[2,4,128,256]{3,2,1,0:T(8,128)(2,1)}, bf16[2,4,128,256]{3,2,1,0:T(8,128)(2,1)S(1)}, u32[]{:S(2)}, u32[]{:S(2)}) collective-permute-start(bf16[2,4,128,256]{3,2,1,0:T(8,128)(2,1)} %bitcast.63), channel_id=1, source_target_pairs={{0,24},{8,16},{1,25},{9,17},{2,26},{10,18},{3,27},{11,19},{4,28},{... | collective-permute-start | bytes 1572872 | tf_op jit(solution)/shard_map/ppermute | solution.py:228
  1.4 1.1 slice_bitcast_fusion.6
  2.5 0.7 collective-permute-start
  3.3 3.1 %collective-permute-start.1 = (bf16[3,128,256]{2,1,0:T(8,128)(2,1)S(1)}, bf16[3,128,256]{2,1,0:T(8,128)(2,1)S(1)}, u32[]{:S(2)}, u32[]{:S(2)}) collective-permute-start(bf16[3,128,256]{2,1,0:T(8,128)(2,1)S(1)} %pad_maximum_fusion.1), channel_id=1, source_target_pairs={{1,2},{2,1},{3,4},{4,3},{5,6},{6,5},{9,10},{10,9},{11,12},{12,11},... | collective-permute-start | bytes 589832 | tf_op jit(solution)/shard_map/ppermute | solution.py:192
  6.4 4.1 %shard_map.55 = (bf16[2,128,256]{2,1,0:T(8,128)(2,1)S(1)}, f32[4,128,256]{2,1,0:T(8,128)S(1)}, bf16[6912,256]{1,0:T(8,128)(2,1)S(1)}) custom-call(bf16[4,128,256]{2,1,0:T(8,128)(2,1)S(1)} %get-tuple-element.116.p, bf16[4,128,256]{2,1,0:T(8,128)(2,1)S(1)} %get-tuple-element.115.q, bf16[6912,256]{1,0:T(8,128)(2,1)} %bitcast.55), custom_call_target="tpu_custom_call" | custom-call | flops 1 | bytes 1 | tf_op jit(solution)/shard_map/pallas_call | solution.py:141
  10.6 1.8 %shard_map.56 = (bf16[1,128,256]{2,1,0:T(8,128)(2,1)S(1)}, bf16[4,128,256]{2,1,0:T(8,128)(2,1)S(1)}, bf16[1,128,256]{2,1,0:T(8,128)(2,1)S(1)}) custom-call(s32[3]{0:T(128)S(1)} %add_convert_fusion.6.flags, bf16[4,128,256]{2,1,0:T(8,128)(2,1)S(1)} %get-tuple-element.116.p, bf16[2,128,256]{2,1,0:T(8,128)(2,1)S(1)} %get-tuple-element.66.inner, ...), custom_call_target="tpu_custom_call" | custom-call | flops 1 | bytes 1 | tf_op jit(solution)/shard_map/pallas_call | solution.py:141
  12.4 0.7 collective-permute-start.2
  13.1 2.1 %shard_map.57 = bf16[4,128,256]{2,1,0:T(8,128)(2,1)S(1)} custom-call(bf16[1,128,256]{2,1,0:T(8,128)(2,1)S(1)} %get-tuple-element.75.first_low, bf16[4,128,256]{2,1,0:T(8,128)(2,1)S(1)} %get-tuple-element.73.first_mid, bf16[1,128,256]{2,1,0:T(8,128)(2,1)S(1)} %get-tuple-element.76.first_high, bf16[4,128,256]{2,1,0:T(8,128)(2,1)S(1)} %get-tuple-element.115.q, ...), custom_call_target="tpu_custom_call" | custom-call | flops 1 | bytes 1 | tf_op jit(solution)/shard_map/pallas_call | solution.py:141
  15.2 0.6 collective-permute-done.3
  15.9 0.2 fusion.10
  16.2 4.6 %collective-permute-start.5 = (bf16[3,128,256]{2,1,0:T(8,128)(2,1)S(1)}, bf16[3,128,256]{2,1,0:T(8,128)(2,1)S(1)}, u32[]{:S(2)}, u32[]{:S(2)}) collective-permute-start(bf16[3,128,256]{2,1,0:T(8,128)(2,1)S(1)} %pad_maximum_fusion.3), channel_id=1, source_target_pairs={{1,2},{2,1},{3,4},{4,3},{5,6},{6,5},{9,10},{10,9},{11,12},{12,11},... | collective-permute-start | bytes 589832 | tf_op jit(solution)/shard_map/ppermute | solution.py:192
  21.0 0.7 collective-permute-start.9
  21.6 0.7 collective-permute-start.7
  22.3 2.1 %shard_map.58 = (bf16[2,128,256]{2,1,0:T(8,128)(2,1)S(1)}, f32[4,128,256]{2,1,0:T(8,128)S(1)}) custom-call(bf16[4,128,256]{2,1,0:T(8,128)(2,1)S(1)} %get-tuple-element.114.p, bf16[4,128,256]{2,1,0:T(8,128)(2,1)S(1)} %get-tuple-element.113.q, bf16[6912,256]{1,0:T(8,128)(2,1)S(1)} %get-tuple-element.72.weights), custom_call_target="tpu_custom_call" | custom-call | flops 1 | bytes 1 | tf_op jit(solution)/shard_map/pallas_call | solution.py:141
  24.5 1.8 %shard_map.59 = (bf16[1,128,256]{2,1,0:T(8,128)(2,1)S(1)}, bf16[4,128,256]{2,1,0:T(8,128)(2,1)S(1)}, bf16[1,128,256]{2,1,0:T(8,128)(2,1)S(1)}) custom-call(s32[3]{0:T(128)S(1)} %add_convert_fusion.6.flags, bf16[4,128,256]{2,1,0:T(8,128)(2,1)S(1)} %get-tuple-element.114.p, bf16[2,128,256]{2,1,0:T(8,128)(2,1)S(1)} %get-tuple-element.79.inner, ...), custom_call_target="tpu_custom_call" | custom-call | flops 1 | bytes 1 | tf_op jit(solution)/shard_map/pallas_call | solution.py:141
  26.3 3.7 %collective-permute-start.6 = (bf16[4,128,256]{2,1,0:T(8,128)(2,1)S(1)}, bf16[4,128,256]{2,1,0:T(8,128)(2,1)S(1)}, u32[]{:S(2)}, u32[]{:S(2)}) collective-permute-start(bf16[4,128,256]{2,1,0:T(8,128)(2,1)S(1)} %get-tuple-element.81.first_mid), channel_id=1, source_target_pairs={{0,8},{8,16},{16,24},{1,9},{9,17},{17,25},{2,10},{10,18},{18,26},{... | collective-permute-start | bytes 786440 | tf_op jit(solution)/shard_map/ppermute | solution.py:228
  30.0 2.1 %shard_map.60 = bf16[4,128,256]{2,1,0:T(8,128)(2,1)S(1)} custom-call(bf16[1,128,256]{2,1,0:T(8,128)(2,1)S(1)} %get-tuple-element.83.first_low, bf16[4,128,256]{2,1,0:T(8,128)(2,1)S(1)} %get-tuple-element.81.first_mid, bf16[1,128,256]{2,1,0:T(8,128)(2,1)S(1)} %get-tuple-element.84.first_high, bf16[4,128,256]{2,1,0:T(8,128)(2,1)S(1)} %get-tuple-element.113.q, ...), custom_call_target="tpu_custom_call" | custom-call | flops 1 | bytes 1 | tf_op jit(solution)/shard_map/pallas_call | solution.py:141
  32.2 1.9 %collective-permute-start.8 = (bf16[4,128,256]{2,1,0:T(8,128)(2,1)S(1)}, bf16[4,128,256]{2,1,0:T(8,128)(2,1)S(1)}, u32[]{:S(2)}, u32[]{:S(2)}) collective-permute-start(bf16[4,128,256]{2,1,0:T(8,128)(2,1)S(1)} %shard_map.60), channel_id=1, source_target_pairs={{0,8},{8,16},{16,24},{1,9},{9,17},{17,25},{2,10},{10,18},{18,26},{... | collective-permute-start | bytes 786440 | tf_op jit(solution)/shard_map/ppermute | solution.py:228
  34.1 0.7 collective-permute-start.10
  34.8 4.0 %collective-permute-done.6 = bf16[4,128,256]{2,1,0:T(8,128)(2,1)S(1)} collective-permute-done((bf16[4,128,256]{2,1,0:T(8,128)(2,1)S(1)}, bf16[4,128,256]{2,1,0:T(8,128)(2,1)S(1)}, u32[]{:S(2)}, u32[]{:S(2)}) %collective-permute-start.6) | collective-permute-done | bytes 262176 | tf_op jit(solution)/shard_map/ppermute | solution.py:228
  38.9 5.5 %collective-permute-done.8 = bf16[4,128,256]{2,1,0:T(8,128)(2,1)S(1)} collective-permute-done((bf16[4,128,256]{2,1,0:T(8,128)(2,1)S(1)}, bf16[4,128,256]{2,1,0:T(8,128)(2,1)S(1)}, u32[]{:S(2)}, u32[]{:S(2)}) %collective-permute-start.8) | collective-permute-done | bytes 262176 | tf_op jit(solution)/shard_map/ppermute | solution.py:228
  44.6 4.3 %collective-permute-start.12 = (bf16[3,128,256]{2,1,0:T(8,128)(2,1)S(1)}, bf16[3,128,256]{2,1,0:T(8,128)(2,1)S(1)}, u32[]{:S(2)}, u32[]{:S(2)}) collective-permute-start(bf16[3,128,256]{2,1,0:T(8,128)(2,1)S(1)} %pad_maximum_fusion.5), channel_id=1, source_target_pairs={{1,2},{2,1},{3,4},{4,3},{5,6},{6,5},{9,10},{10,9},{11,12},{12,11},... | collective-permute-start | bytes 589832 | tf_op jit(solution)/shard_map/ppermute | solution.py:192
  49.0 0.9 collective-permute-start.14
  49.9 2.1 %shard_map.61 = (bf16[2,128,256]{2,1,0:T(8,128)(2,1)S(1)}, f32[4,128,256]{2,1,0:T(8,128)S(1)}) custom-call(bf16[4,128,256]{2,1,0:T(8,128)(2,1)S(1)} %fusion.17.p, bf16[4,128,256]{2,1,0:T(8,128)(2,1)S(1)} %fusion.16.q, bf16[6912,256]{1,0:T(8,128)(2,1)S(1)} %get-tuple-element.72.weights), custom_call_target="tpu_custom_call" | custom-call | flops 1 | bytes 1 | tf_op jit(solution)/shard_map/pallas_call | solution.py:141
  52.0 0.4 collective-permute-done.12.far
  52.4 1.8 %shard_map.62 = (bf16[1,128,256]{2,1,0:T(8,128)(2,1)S(1)}, bf16[4,128,256]{2,1,0:T(8,128)(2,1)S(1)}, bf16[1,128,256]{2,1,0:T(8,128)(2,1)S(1)}) custom-call(s32[3]{0:T(128)S(1)} %add_convert_fusion.6.flags, bf16[4,128,256]{2,1,0:T(8,128)(2,1)S(1)} %fusion.17.p, bf16[2,128,256]{2,1,0:T(8,128)(2,1)S(1)} %get-tuple-element.88.inner, ...), custom_call_target="tpu_custom_call" | custom-call | flops 1 | bytes 1 | tf_op jit(solution)/shard_map/pallas_call | solution.py:141
  54.2 2.2 %collective-permute-start.13 = (bf16[4,128,256]{2,1,0:T(8,128)(2,1)S(1)}, bf16[4,128,256]{2,1,0:T(8,128)(2,1)S(1)}, u32[]{:S(2)}, u32[]{:S(2)}) collective-permute-start(bf16[4,128,256]{2,1,0:T(8,128)(2,1)S(1)} %get-tuple-element.90.first_mid), channel_id=1, source_target_pairs={{0,8},{8,16},{16,24},{1,9},{9,17},{17,25},{2,10},{10,18},{18,26},{... | collective-permute-start | bytes 786440 | tf_op jit(solution)/shard_map/ppermute | solution.py:228
  56.4 2.1 %shard_map.63 = bf16[4,128,256]{2,1,0:T(8,128)(2,1)S(1)} custom-call(bf16[1,128,256]{2,1,0:T(8,128)(2,1)S(1)} %get-tuple-element.91.first_low, bf16[4,128,256]{2,1,0:T(8,128)(2,1)S(1)} %get-tuple-element.90.first_mid, bf16[1,128,256]{2,1,0:T(8,128)(2,1)S(1)} %get-tuple-element.92.first_high, bf16[4,128,256]{2,1,0:T(8,128)(2,1)S(1)} %fusion.16.q, ...), custom_call_target="tpu_custom_call" | custom-call | flops 1 | bytes 1 | tf_op jit(solution)/shard_map/pallas_call | solution.py:141
  58.6 1.9 %collective-permute-start.15 = (bf16[4,128,256]{2,1,0:T(8,128)(2,1)S(1)}, bf16[4,128,256]{2,1,0:T(8,128)(2,1)S(1)}, u32[]{:S(2)}, u32[]{:S(2)}) collective-permute-start(bf16[4,128,256]{2,1,0:T(8,128)(2,1)S(1)} %shard_map.63), channel_id=1, source_target_pairs={{0,8},{8,16},{16,24},{1,9},{9,17},{17,25},{2,10},{10,18},{18,26},{... | collective-permute-start | bytes 786440 | tf_op jit(solution)/shard_map/ppermute | solution.py:228
  60.5 0.7 collective-permute-start.16
  61.2 3.3 %collective-permute-done.13 = bf16[4,128,256]{2,1,0:T(8,128)(2,1)S(1)} collective-permute-done((bf16[4,128,256]{2,1,0:T(8,128)(2,1)S(1)}, bf16[4,128,256]{2,1,0:T(8,128)(2,1)S(1)}, u32[]{:S(2)}, u32[]{:S(2)}) %collective-permute-start.13) | collective-permute-done | bytes 262176 | tf_op jit(solution)/shard_map/ppermute | solution.py:228
  64.6 5.5 %collective-permute-done.15 = bf16[4,128,256]{2,1,0:T(8,128)(2,1)S(1)} collective-permute-done((bf16[4,128,256]{2,1,0:T(8,128)(2,1)S(1)}, bf16[4,128,256]{2,1,0:T(8,128)(2,1)S(1)}, u32[]{:S(2)}, u32[]{:S(2)}) %collective-permute-start.15) | collective-permute-done | bytes 262176 | tf_op jit(solution)/shard_map/ppermute | solution.py:228
  70.3 3.8 %collective-permute-start.18 = (bf16[3,128,256]{2,1,0:T(8,128)(2,1)S(1)}, bf16[3,128,256]{2,1,0:T(8,128)(2,1)S(1)}, u32[]{:S(2)}, u32[]{:S(2)}) collective-permute-start(bf16[3,128,256]{2,1,0:T(8,128)(2,1)S(1)} %pad_maximum_fusion.7), channel_id=1, source_target_pairs={{1,2},{2,1},{3,4},{4,3},{5,6},{6,5},{9,10},{10,9},{11,12},{12,11},... | collective-permute-start | bytes 589832 | tf_op jit(solution)/shard_map/ppermute | solution.py:192
  74.3 0.7 collective-permute-start.20
  74.9 2.1 %shard_map.64 = (bf16[2,128,256]{2,1,0:T(8,128)(2,1)S(1)}, f32[4,128,256]{2,1,0:T(8,128)S(1)}) custom-call(bf16[4,128,256]{2,1,0:T(8,128)(2,1)S(1)} %fusion.15.p, bf16[4,128,256]{2,1,0:T(8,128)(2,1)S(1)} %fusion.14.q, bf16[6912,256]{1,0:T(8,128)(2,1)S(1)} %get-tuple-element.72.weights), custom_call_target="tpu_custom_call" | custom-call | flops 1 | bytes 1 | tf_op jit(solution)/shard_map/pallas_call | solution.py:141
  77.1 0.7 collective-permute-done.18.far
  77.8 1.8 %shard_map.65 = (bf16[1,128,256]{2,1,0:T(8,128)(2,1)S(1)}, bf16[4,128,256]{2,1,0:T(8,128)(2,1)S(1)}, bf16[1,128,256]{2,1,0:T(8,128)(2,1)S(1)}) custom-call(s32[3]{0:T(128)S(1)} %add_convert_fusion.6.flags, bf16[4,128,256]{2,1,0:T(8,128)(2,1)S(1)} %fusion.15.p, bf16[2,128,256]{2,1,0:T(8,128)(2,1)S(1)} %get-tuple-element.98.inner, ...), custom_call_target="tpu_custom_call" | custom-call | flops 1 | bytes 1 | tf_op jit(solution)/shard_map/pallas_call | solution.py:141
  79.6 1.9 %collective-permute-start.19 = (bf16[4,128,256]{2,1,0:T(8,128)(2,1)S(1)}, bf16[4,128,256]{2,1,0:T(8,128)(2,1)S(1)}, u32[]{:S(2)}, u32[]{:S(2)}) collective-permute-start(bf16[4,128,256]{2,1,0:T(8,128)(2,1)S(1)} %get-tuple-element.100.first_mid), channel_id=1, source_target_pairs={{8,16},{16,24},{9,17},{17,25},{10,18},{18,26},{11,19},{19,27},{12,... | collective-permute-start | bytes 786440 | tf_op jit(solution)/shard_map/ppermute | solution.py:228
  81.5 2.1 %shard_map.66 = bf16[4,128,256]{2,1,0:T(8,128)(2,1)S(1)} custom-call(bf16[1,128,256]{2,1,0:T(8,128)(2,1)S(1)} %get-tuple-element.101.first_low, bf16[4,128,256]{2,1,0:T(8,128)(2,1)S(1)} %get-tuple-element.100.first_mid, bf16[1,128,256]{2,1,0:T(8,128)(2,1)S(1)} %get-tuple-element.102.first_high, bf16[4,128,256]{2,1,0:T(8,128)(2,1)S(1)} %fusion.14.q, ...), custom_call_target="tpu_custom_call" | custom-call | flops 1 | bytes 1 | tf_op jit(solution)/shard_map/pallas_call | solution.py:141
  83.7 1.9 %collective-permute-start.21 = (bf16[4,128,256]{2,1,0:T(8,128)(2,1)S(1)}, bf16[4,128,256]{2,1,0:T(8,128)(2,1)S(1)}, u32[]{:S(2)}, u32[]{:S(2)}) collective-permute-start(bf16[4,128,256]{2,1,0:T(8,128)(2,1)S(1)} %shard_map.66), channel_id=1, source_target_pairs={{8,16},{16,24},{9,17},{17,25},{10,18},{18,26},{11,19},{19,27},{12,... | collective-permute-start | bytes 786440 | tf_op jit(solution)/shard_map/ppermute | solution.py:228
  85.6 0.7 collective-permute-start.22
  86.3 3.2 %collective-permute-done.19 = bf16[4,128,256]{2,1,0:T(8,128)(2,1)S(1)} collective-permute-done((bf16[4,128,256]{2,1,0:T(8,128)(2,1)S(1)}, bf16[4,128,256]{2,1,0:T(8,128)(2,1)S(1)}, u32[]{:S(2)}, u32[]{:S(2)}) %collective-permute-start.19) | collective-permute-done | bytes 262176 | tf_op jit(solution)/shard_map/ppermute | solution.py:228
  89.6 5.5 %collective-permute-done.21 = bf16[4,128,256]{2,1,0:T(8,128)(2,1)S(1)} collective-permute-done((bf16[4,128,256]{2,1,0:T(8,128)(2,1)S(1)}, bf16[4,128,256]{2,1,0:T(8,128)(2,1)S(1)}, u32[]{:S(2)}, u32[]{:S(2)}) %collective-permute-start.21) | collective-permute-done | bytes 262176 | tf_op jit(solution)/shard_map/ppermute | solution.py:228
  95.3 3.7 %collective-permute-start.24 = (bf16[3,128,256]{2,1,0:T(8,128)(2,1)S(1)}, bf16[3,128,256]{2,1,0:T(8,128)(2,1)S(1)}, u32[]{:S(2)}, u32[]{:S(2)}) collective-permute-start(bf16[3,128,256]{2,1,0:T(8,128)(2,1)S(1)} %pad_maximum_fusion.9), channel_id=1, source_target_pairs={{1,2},{2,1},{3,4},{4,3},{5,6},{6,5},{9,10},{10,9},{11,12},{12,11},... | collective-permute-start | bytes 589832 | tf_op jit(solution)/shard_map/ppermute | solution.py:192
  99.2 2.1 %shard_map.67 = (bf16[2,128,256]{2,1,0:T(8,128)(2,1)S(1)}, f32[4,128,256]{2,1,0:T(8,128)S(1)}) custom-call(bf16[4,128,256]{2,1,0:T(8,128)(2,1)S(1)} %fusion.13.p, bf16[4,128,256]{2,1,0:T(8,128)(2,1)S(1)} %fusion.12.q, bf16[6912,256]{1,0:T(8,128)(2,1)S(1)} %get-tuple-element.72.weights), custom_call_target="tpu_custom_call" | custom-call | flops 1 | bytes 1 | tf_op jit(solution)/shard_map/pallas_call | solution.py:141
  101.3 1.3 %collective-permute-done.24.far = bf16[3,128,256]{2,1,0:T(8,128)(2,1)S(1)} collective-permute-done((bf16[3,128,256]{2,1,0:T(8,128)(2,1)S(1)}, bf16[3,128,256]{2,1,0:T(8,128)(2,1)S(1)}, u32[]{:S(2)}, u32[]{:S(2)}) %collective-permute-start.24) | collective-permute-done | bytes 196640 | tf_op jit(solution)/shard_map/ppermute | solution.py:192
  102.6 1.8 %shard_map.68 = (bf16[1,128,256]{2,1,0:T(8,128)(2,1)S(1)}, bf16[4,128,256]{2,1,0:T(8,128)(2,1)S(1)}, bf16[1,128,256]{2,1,0:T(8,128)(2,1)S(1)}) custom-call(s32[3]{0:T(128)S(1)} %add_convert_fusion.6.flags, bf16[4,128,256]{2,1,0:T(8,128)(2,1)S(1)} %fusion.13.p, bf16[2,128,256]{2,1,0:T(8,128)(2,1)S(1)} %get-tuple-element.108.inner, ...), custom_call_target="tpu_custom_call" | custom-call | flops 1 | bytes 1 | tf_op jit(solution)/shard_map/pallas_call | solution.py:141
  104.4 2.8 %shard_map.69 = bf16[2,4,128,256]{3,2,1,0:T(8,128)(2,1)} custom-call(bf16[1,128,256]{2,1,0:T(8,128)(2,1)S(1)} %get-tuple-element.110.first_low, bf16[4,128,256]{2,1,0:T(8,128)(2,1)S(1)} %get-tuple-element.111.first_mid, bf16[1,128,256]{2,1,0:T(8,128)(2,1)S(1)} %get-tuple-element.112.first_high, bf16[4,128,256]{2,1,0:T(8,128)(2,1)S(1)} %fusion.12.q, ...), custom_call_target="tpu_custom_call" | custom-call | flops 1 | bytes 1 | tf_op jit(solution)/shard_map/pallas_call | solution.py:141
  (52 shorter events, 1.6 us)
Async XLA Ops:
  0.1 15.8 %collective-permute-start.3 = (bf16[2,4,128,256]{3,2,1,0:T(8,128)(2,1)}, bf16[2,4,128,256]{3,2,1,0:T(8,128)(2,1)S(1)}, u32[]{:S(2)}, u32[]{:S(2)}) collective-permute-start(bf16[2,4,128,256]{3,2,1,0:T(8,128)(2,1)} %bitcast.63), channel_id=1, source_target_pairs={{0,24},{8,16},{1,25},{9,17},{2,26},{10,18},{3,27},{11,19},{4,28},{... | collective-permute-start | bytes 1572872 | tf_op jit(solution)/shard_map/ppermute | solution.py:228
  2.5 7.9 %collective-permute-start = (bf16[3,128,256]{2,1,0:T(8,128)(2,1)S(1)}, bf16[3,128,256]{2,1,0:T(8,128)(2,1)S(1)}, u32[]{:S(2)}, u32[]{:S(2)}) collective-permute-start(bf16[3,128,256]{2,1,0:T(8,128)(2,1)S(1)} %pad_maximum_fusion), channel_id=1, source_target_pairs={{0,1},{1,0},{2,3},{3,2},{4,5},{5,4},{6,7},{7,6},{8,9},{9,8},{10,11... | collective-permute-start | bytes 589832 | tf_op jit(solution)/shard_map/ppermute | solution.py:192
  3.3 7.3 %collective-permute-start.1 = (bf16[3,128,256]{2,1,0:T(8,128)(2,1)S(1)}, bf16[3,128,256]{2,1,0:T(8,128)(2,1)S(1)}, u32[]{:S(2)}, u32[]{:S(2)}) collective-permute-start(bf16[3,128,256]{2,1,0:T(8,128)(2,1)S(1)} %pad_maximum_fusion.1), channel_id=1, source_target_pairs={{1,2},{2,1},{3,4},{4,3},{5,6},{6,5},{9,10},{10,9},{11,12},{12,11},... | collective-permute-start | bytes 589832 | tf_op jit(solution)/shard_map/ppermute | solution.py:192
  10.6 2.5 %copy-start = (bf16[1,3,3,3,256,256]{5,4,3,2,1,0:T(8,128)(2,1)S(1)}, bf16[1,3,3,3,256,256]{5,4,3,2,1,0:T(8,128)(2,1)}, u32[]{:S(2)}) copy-start(bf16[1,3,3,3,256,256]{5,4,3,2,1,0:T(8,128)(2,1)} %param.9) | copy-start | bytes 10616836
  12.4 9.3 %collective-permute-start.2 = (bf16[4,128,256]{2,1,0:T(8,128)(2,1)S(1)}, bf16[4,128,256]{2,1,0:T(8,128)(2,1)S(1)}, u32[]{:S(2)}, u32[]{:S(2)}) collective-permute-start(bf16[4,128,256]{2,1,0:T(8,128)(2,1)S(1)} %get-tuple-element.73.first_mid), channel_id=1, source_target_pairs={{0,8},{1,9},{2,10},{3,11},{4,12},{5,13},{6,14},{7,15}} | collective-permute-start | bytes 786440 | tf_op jit(solution)/shard_map/ppermute | solution.py:228
  13.1 2.8 %copy-start.1 = (bf16[3,2,4,16,8,256]{5,4,3,2,1,0:T(8,128)(2,1)S(1)}, bf16[3,2,4,16,8,256]{5,4,3,2,1,0:T(8,128)(2,1)}, u32[]{:S(2)}) copy-start(bf16[3,2,4,16,8,256]{5,4,3,2,1,0:T(8,128)(2,1)} %param.7) | copy-start | bytes 4718596
  13.1 2.8 %copy-start.2 = (bf16[1,2,4,16,8,256]{5,4,3,2,1,0:T(8,128)(2,1)S(1)}, bf16[1,2,4,16,8,256]{5,4,3,2,1,0:T(8,128)(2,1)}, u32[]{:S(2)}) copy-start(bf16[1,2,4,16,8,256]{5,4,3,2,1,0:T(8,128)(2,1)} %param.5) | copy-start | bytes 1572868
  16.2 8.3 %collective-permute-start.5 = (bf16[3,128,256]{2,1,0:T(8,128)(2,1)S(1)}, bf16[3,128,256]{2,1,0:T(8,128)(2,1)S(1)}, u32[]{:S(2)}, u32[]{:S(2)}) collective-permute-start(bf16[3,128,256]{2,1,0:T(8,128)(2,1)S(1)} %pad_maximum_fusion.3), channel_id=1, source_target_pairs={{1,2},{2,1},{3,4},{4,3},{5,6},{6,5},{9,10},{10,9},{11,12},{12,11},... | collective-permute-start | bytes 589832 | tf_op jit(solution)/shard_map/ppermute | solution.py:192
  20.9 3.6 %collective-permute-start.4 = (bf16[3,128,256]{2,1,0:T(8,128)(2,1)S(1)}, bf16[3,128,256]{2,1,0:T(8,128)(2,1)S(1)}, u32[]{:S(2)}, u32[]{:S(2)}) collective-permute-start(bf16[3,128,256]{2,1,0:T(8,128)(2,1)S(1)} %pad_maximum_fusion.2), channel_id=1, source_target_pairs={{0,1},{1,0},{2,3},{3,2},{4,5},{5,4},{6,7},{7,6},{8,9},{9,8},{10,11... | collective-permute-start | bytes 589832 | tf_op jit(solution)/shard_map/ppermute | solution.py:192
  21.0 13.1 %collective-permute-start.9 = (bf16[4,128,256]{2,1,0:T(8,128)(2,1)S(1)}, bf16[4,128,256]{2,1,0:T(8,128)(2,1)S(1)}, u32[]{:S(2)}, u32[]{:S(2)}) collective-permute-start(bf16[4,128,256]{2,1,0:T(8,128)(2,1)S(1)} %shard_map.57), channel_id=1, source_target_pairs={{0,8},{1,9},{2,10},{3,11},{4,12},{5,13},{6,14},{7,15}} | collective-permute-start | bytes 786440 | tf_op jit(solution)/shard_map/ppermute | solution.py:228
  21.6 13.1 %collective-permute-start.7 = (bf16[4,128,256]{2,1,0:T(8,128)(2,1)S(1)}, bf16[4,128,256]{2,1,0:T(8,128)(2,1)S(1)}, u32[]{:S(2)}, u32[]{:S(2)}) collective-permute-start(bf16[4,128,256]{2,1,0:T(8,128)(2,1)S(1)} %collective-permute-done.2), channel_id=1, source_target_pairs={{8,24},{9,25},{10,26},{11,27},{12,28},{13,29},{14,30},{15,31}} | collective-permute-start | bytes 786440 | tf_op jit(solution)/shard_map/ppermute | solution.py:228
  26.3 12.5 %collective-permute-start.6 = (bf16[4,128,256]{2,1,0:T(8,128)(2,1)S(1)}, bf16[4,128,256]{2,1,0:T(8,128)(2,1)S(1)}, u32[]{:S(2)}, u32[]{:S(2)}) collective-permute-start(bf16[4,128,256]{2,1,0:T(8,128)(2,1)S(1)} %get-tuple-element.81.first_mid), channel_id=1, source_target_pairs={{0,8},{8,16},{16,24},{1,9},{9,17},{17,25},{2,10},{10,18},{18,26},{... | collective-permute-start | bytes 786440 | tf_op jit(solution)/shard_map/ppermute | solution.py:228
  32.2 12.2 %collective-permute-start.8 = (bf16[4,128,256]{2,1,0:T(8,128)(2,1)S(1)}, bf16[4,128,256]{2,1,0:T(8,128)(2,1)S(1)}, u32[]{:S(2)}, u32[]{:S(2)}) collective-permute-start(bf16[4,128,256]{2,1,0:T(8,128)(2,1)S(1)} %shard_map.60), channel_id=1, source_target_pairs={{0,8},{8,16},{16,24},{1,9},{9,17},{17,25},{2,10},{10,18},{18,26},{... | collective-permute-start | bytes 786440 | tf_op jit(solution)/shard_map/ppermute | solution.py:228
  34.1 10.3 %collective-permute-start.10 = (bf16[4,128,256]{2,1,0:T(8,128)(2,1)S(1)}, bf16[4,128,256]{2,1,0:T(8,128)(2,1)S(1)}, u32[]{:S(2)}, u32[]{:S(2)}) collective-permute-start(bf16[4,128,256]{2,1,0:T(8,128)(2,1)S(1)} %collective-permute-done.9), channel_id=1, source_target_pairs={{8,24},{9,25},{10,26},{11,27},{12,28},{13,29},{14,30},{15,31}} | collective-permute-start | bytes 786440 | tf_op jit(solution)/shard_map/ppermute | solution.py:228
  44.6 7.8 %collective-permute-start.12 = (bf16[3,128,256]{2,1,0:T(8,128)(2,1)S(1)}, bf16[3,128,256]{2,1,0:T(8,128)(2,1)S(1)}, u32[]{:S(2)}, u32[]{:S(2)}) collective-permute-start(bf16[3,128,256]{2,1,0:T(8,128)(2,1)S(1)} %pad_maximum_fusion.5), channel_id=1, source_target_pairs={{1,2},{2,1},{3,4},{4,3},{5,6},{6,5},{9,10},{10,9},{11,12},{12,11},... | collective-permute-start | bytes 589832 | tf_op jit(solution)/shard_map/ppermute | solution.py:192
  48.9 3.5 %collective-permute-start.11 = (bf16[3,128,256]{2,1,0:T(8,128)(2,1)S(1)}, bf16[3,128,256]{2,1,0:T(8,128)(2,1)S(1)}, u32[]{:S(2)}, u32[]{:S(2)}) collective-permute-start(bf16[3,128,256]{2,1,0:T(8,128)(2,1)S(1)} %pad_maximum_fusion.4), channel_id=1, source_target_pairs={{0,1},{1,0},{2,3},{3,2},{4,5},{5,4},{6,7},{7,6},{8,9},{9,8},{10,11... | collective-permute-start | bytes 589832 | tf_op jit(solution)/shard_map/ppermute | solution.py:192
  49.0 9.6 %collective-permute-start.14 = (bf16[4,128,256]{2,1,0:T(8,128)(2,1)S(1)}, bf16[4,128,256]{2,1,0:T(8,128)(2,1)S(1)}, u32[]{:S(2)}, u32[]{:S(2)}) collective-permute-start(bf16[4,128,256]{2,1,0:T(8,128)(2,1)S(1)} %collective-permute-done.6), channel_id=1, source_target_pairs={{8,24},{9,25},{10,26},{11,27},{12,28},{13,29},{14,30},{15,31}} | collective-permute-start | bytes 786440 | tf_op jit(solution)/shard_map/ppermute | solution.py:228
  54.2 10.3 %collective-permute-start.13 = (bf16[4,128,256]{2,1,0:T(8,128)(2,1)S(1)}, bf16[4,128,256]{2,1,0:T(8,128)(2,1)S(1)}, u32[]{:S(2)}, u32[]{:S(2)}) collective-permute-start(bf16[4,128,256]{2,1,0:T(8,128)(2,1)S(1)} %get-tuple-element.90.first_mid), channel_id=1, source_target_pairs={{0,8},{8,16},{16,24},{1,9},{9,17},{17,25},{2,10},{10,18},{18,26},{... | collective-permute-start | bytes 786440 | tf_op jit(solution)/shard_map/ppermute | solution.py:228
  58.6 11.5 %collective-permute-start.15 = (bf16[4,128,256]{2,1,0:T(8,128)(2,1)S(1)}, bf16[4,128,256]{2,1,0:T(8,128)(2,1)S(1)}, u32[]{:S(2)}, u32[]{:S(2)}) collective-permute-start(bf16[4,128,256]{2,1,0:T(8,128)(2,1)S(1)} %shard_map.63), channel_id=1, source_target_pairs={{0,8},{8,16},{16,24},{1,9},{9,17},{17,25},{2,10},{10,18},{18,26},{... | collective-permute-start | bytes 786440 | tf_op jit(solution)/shard_map/ppermute | solution.py:228
  60.5 9.6 %collective-permute-start.16 = (bf16[4,128,256]{2,1,0:T(8,128)(2,1)S(1)}, bf16[4,128,256]{2,1,0:T(8,128)(2,1)S(1)}, u32[]{:S(2)}, u32[]{:S(2)}) collective-permute-start(bf16[4,128,256]{2,1,0:T(8,128)(2,1)S(1)} %collective-permute-done.8), channel_id=1, source_target_pairs={{8,24},{9,25},{10,26},{11,27},{12,28},{13,29},{14,30},{15,31}} | collective-permute-start | bytes 786440 | tf_op jit(solution)/shard_map/ppermute | solution.py:228
  70.3 7.5 %collective-permute-start.18 = (bf16[3,128,256]{2,1,0:T(8,128)(2,1)S(1)}, bf16[3,128,256]{2,1,0:T(8,128)(2,1)S(1)}, u32[]{:S(2)}, u32[]{:S(2)}) collective-permute-start(bf16[3,128,256]{2,1,0:T(8,128)(2,1)S(1)} %pad_maximum_fusion.7), channel_id=1, source_target_pairs={{1,2},{2,1},{3,4},{4,3},{5,6},{6,5},{9,10},{10,9},{11,12},{12,11},... | collective-permute-start | bytes 589832 | tf_op jit(solution)/shard_map/ppermute | solution.py:192
  74.2 3.6 %collective-permute-start.17 = (bf16[3,128,256]{2,1,0:T(8,128)(2,1)S(1)}, bf16[3,128,256]{2,1,0:T(8,128)(2,1)S(1)}, u32[]{:S(2)}, u32[]{:S(2)}) collective-permute-start(bf16[3,128,256]{2,1,0:T(8,128)(2,1)S(1)} %pad_maximum_fusion.6), channel_id=1, source_target_pairs={{0,1},{1,0},{2,3},{3,2},{4,5},{5,4},{6,7},{7,6},{8,9},{9,8},{10,11... | collective-permute-start | bytes 589832 | tf_op jit(solution)/shard_map/ppermute | solution.py:192
  74.3 9.4 %collective-permute-start.20 = (bf16[4,128,256]{2,1,0:T(8,128)(2,1)S(1)}, bf16[4,128,256]{2,1,0:T(8,128)(2,1)S(1)}, u32[]{:S(2)}, u32[]{:S(2)}) collective-permute-start(bf16[4,128,256]{2,1,0:T(8,128)(2,1)S(1)} %collective-permute-done.13), channel_id=1, source_target_pairs={{8,24},{9,25},{10,26},{11,27},{12,28},{13,29},{14,30},{15,31}} | collective-permute-start | bytes 786440 | tf_op jit(solution)/shard_map/ppermute | solution.py:228
  79.6 9.9 %collective-permute-start.19 = (bf16[4,128,256]{2,1,0:T(8,128)(2,1)S(1)}, bf16[4,128,256]{2,1,0:T(8,128)(2,1)S(1)}, u32[]{:S(2)}, u32[]{:S(2)}) collective-permute-start(bf16[4,128,256]{2,1,0:T(8,128)(2,1)S(1)} %get-tuple-element.100.first_mid), channel_id=1, source_target_pairs={{8,16},{16,24},{9,17},{17,25},{10,18},{18,26},{11,19},{19,27},{12,... | collective-permute-start | bytes 786440 | tf_op jit(solution)/shard_map/ppermute | solution.py:228
  83.7 11.4 %collective-permute-start.21 = (bf16[4,128,256]{2,1,0:T(8,128)(2,1)S(1)}, bf16[4,128,256]{2,1,0:T(8,128)(2,1)S(1)}, u32[]{:S(2)}, u32[]{:S(2)}) collective-permute-start(bf16[4,128,256]{2,1,0:T(8,128)(2,1)S(1)} %shard_map.66), channel_id=1, source_target_pairs={{8,16},{16,24},{9,17},{17,25},{10,18},{18,26},{11,19},{19,27},{12,... | collective-permute-start | bytes 786440 | tf_op jit(solution)/shard_map/ppermute | solution.py:228
  85.6 9.5 %collective-permute-start.22 = (bf16[4,128,256]{2,1,0:T(8,128)(2,1)S(1)}, bf16[4,128,256]{2,1,0:T(8,128)(2,1)S(1)}, u32[]{:S(2)}, u32[]{:S(2)}) collective-permute-start(bf16[4,128,256]{2,1,0:T(8,128)(2,1)S(1)} %collective-permute-done.15), channel_id=1, source_target_pairs={{8,24},{9,25},{10,26},{11,27},{12,28},{13,29},{14,30},{15,31}} | collective-permute-start | bytes 786440 | tf_op jit(solution)/shard_map/ppermute | solution.py:228
  95.3 7.3 %collective-permute-start.24 = (bf16[3,128,256]{2,1,0:T(8,128)(2,1)S(1)}, bf16[3,128,256]{2,1,0:T(8,128)(2,1)S(1)}, u32[]{:S(2)}, u32[]{:S(2)}) collective-permute-start(bf16[3,128,256]{2,1,0:T(8,128)(2,1)S(1)} %pad_maximum_fusion.9), channel_id=1, source_target_pairs={{1,2},{2,1},{3,4},{4,3},{5,6},{6,5},{9,10},{10,9},{11,12},{12,11},... | collective-permute-start | bytes 589832 | tf_op jit(solution)/shard_map/ppermute | solution.py:192
  99.0 3.6 %collective-permute-start.23 = (bf16[3,128,256]{2,1,0:T(8,128)(2,1)S(1)}, bf16[3,128,256]{2,1,0:T(8,128)(2,1)S(1)}, u32[]{:S(2)}, u32[]{:S(2)}) collective-permute-start(bf16[3,128,256]{2,1,0:T(8,128)(2,1)S(1)} %pad_maximum_fusion.8), channel_id=1, source_target_pairs={{0,1},{1,0},{2,3},{3,2},{4,5},{5,4},{6,7},{7,6},{8,9},{9,8},{10,11... | collective-permute-start | bytes 589832 | tf_op jit(solution)/shard_map/ppermute | solution.py:192

commit v21 on v18

--- a/solution.py
+++ b/solution.py
@@ -122,14 +122,24 @@
     out[...] = second_sum(width, first_low, first_mid, first_high, q, weights, even, odd).astype(out.dtype)
 
 
-def last_kernel(width, first_low, first_mid, first_high, q, weights, out, even, odd, second, first_sem, second_sem):
+def last_kernel(width, first_low, first_mid, first_high, q, weights, out, even, odd, second, first_sem, low_sem, high_sem):
     first_copy = pltpu.make_async_copy(first_mid, out.at[0], first_sem)
     first_copy.start()
-    second[...] = second_sum(width, first_low, first_mid, first_high, q, weights, even, odd).astype(second.dtype)
-    second_copy = pltpu.make_async_copy(second, out.at[1], second_sem)
-    second_copy.start()
-    first_copy.wait()
-    second_copy.wait()
+    planes = q.shape[0]
+    fill(even, odd, 0, first_low[...], width)
+    fill(even, odd, 1, first_mid[...], width)
+    fill(even, odd, 1 + planes, first_high[...], width)
+    half = planes // 2
+    copies = [first_copy]
+    for start, count, sem in ((0, half, low_sem), (half, planes - half, high_sem)):
+        taps = [part for i in range(3) for part in planes_at(even, odd, start + i, count, width)]
+        part = pl.ds(start, count)
+        second[part] = (q[part].astype(jnp.float32) + convolve(taps, weights, width)).astype(second.dtype)
+        copy = pltpu.make_async_copy(second.at[part], out.at[1, part], sem)
+        copy.start()
+        copies.append(copy)
+    for copy in copies:
+        copy.wait()
 
 
 def call(kernel, outputs, scratch, arguments, width):
@@ -180,7 +190,7 @@
     scratch = stored(shape[0] + 2, *shape[1:], width)
     output = shape
     if last:
-        scratch, output = [*scratch, shape, (), ()], (2, *shape)
+        scratch, output = [*scratch, shape, (), (), ()], (2, *shape)
     (out,) = call(last_kernel if last else second_kernel, [(output, jnp.bfloat16)], scratch, (*first, q, weights), width)
     return out
 

time: 109 us -> 109 us (level)
  no operation moved by 1% of the time
where the time goes in v21:
time: 109 us; the launch traced here: 107 us
  starting transfers between devices  41.2 us (38%)
  Pallas kernels  32.9 us (30%)
  waiting for transfers between devices  30.1 us (28%)
  local copies, waits for them, and re-layouts  1.31 us (1%)
  other arithmetic  1.15 us (1%)
    pallas_call x15, Pallas kernels, call(): pl.pallas_call(functools.partial(kernel, width), out_shape=[jax.ShapeDtyp...  32.9 us
    ppermute x15, waiting for transfers between devices, send(): return lax.ppermute(block, 'section', pairs) if pairs else block  27.7 us
    ppermute x10, starting transfers between devices, swap(): return lax.ppermute(jnp.concatenate(parts, axis=0), 'depth', pairs)  20.9 us
    ppermute x15, starting transfers between devices, send(): return lax.ppermute(block, 'section', pairs) if pairs else block  20.4 us
    ppermute x10, waiting for transfers between devices, swap(): return lax.ppermute(jnp.concatenate(parts, axis=0), 'depth', pairs)  2.44 us
  transfers between devices with their start and end apart: 25, of which 11 were waited for; matrix products, arithmetic and copies ran while one was open for 2% of the time, Pallas kernels for 26%

profile of v21, /device:TPU:13, one launch (start us, length us, event | category | flops | bytes accessed | tf_op | source)
XLA Modules:
  0.0 107.4 jit_solution(14056002321349761059)
XLA Ops:
  0.1 1.3 %collective-permute-start.3 = (bf16[2,4,128,256]{3,2,1,0:T(8,128)(2,1)}, bf16[2,4,128,256]{3,2,1,0:T(8,128)(2,1)S(1)}, u32[]{:S(2)}, u32[]{:S(2)}) collective-permute-start(bf16[2,4,128,256]{3,2,1,0:T(8,128)(2,1)} %bitcast.63), channel_id=1, source_target_pairs={{0,24},{8,16},{1,25},{9,17},{2,26},{10,18},{3,27},{11,19},{4,28},{... | collective-permute-start | bytes 1572872 | tf_op jit(solution)/shard_map/ppermute | solution.py:238
  1.4 1.1 slice_bitcast_fusion.6
  2.5 0.7 collective-permute-start
  3.3 3.1 %collective-permute-start.1 = (bf16[3,128,256]{2,1,0:T(8,128)(2,1)S(1)}, bf16[3,128,256]{2,1,0:T(8,128)(2,1)S(1)}, u32[]{:S(2)}, u32[]{:S(2)}) collective-permute-start(bf16[3,128,256]{2,1,0:T(8,128)(2,1)S(1)} %pad_maximum_fusion.1), channel_id=1, source_target_pairs={{1,2},{2,1},{3,4},{4,3},{5,6},{6,5},{9,10},{10,9},{11,12},{12,11},... | collective-permute-start | bytes 589832 | tf_op jit(solution)/shard_map/ppermute | solution.py:202
  6.4 4.1 %shard_map.55 = (bf16[2,128,256]{2,1,0:T(8,128)(2,1)S(1)}, f32[4,128,256]{2,1,0:T(8,128)S(1)}, bf16[6912,256]{1,0:T(8,128)(2,1)S(1)}) custom-call(bf16[4,128,256]{2,1,0:T(8,128)(2,1)S(1)} %get-tuple-element.108.p, bf16[4,128,256]{2,1,0:T(8,128)(2,1)S(1)} %get-tuple-element.107.q, bf16[6912,256]{1,0:T(8,128)(2,1)} %bitcast.55), custom_call_target="tpu_custom_call" | custom-call | flops 1 | bytes 1 | tf_op jit(solution)/shard_map/pallas_call | solution.py:151
  10.6 1.8 %shard_map.56 = (bf16[1,128,256]{2,1,0:T(8,128)(2,1)S(1)}, bf16[4,128,256]{2,1,0:T(8,128)(2,1)S(1)}, bf16[1,128,256]{2,1,0:T(8,128)(2,1)S(1)}) custom-call(s32[3]{0:T(128)S(1)} %add_convert_fusion.6.flags, bf16[4,128,256]{2,1,0:T(8,128)(2,1)S(1)} %get-tuple-element.108.p, bf16[2,128,256]{2,1,0:T(8,128)(2,1)S(1)} %get-tuple-element.62.inner, ...), custom_call_target="tpu_custom_call" | custom-call | flops 1 | bytes 1 | tf_op jit(solution)/shard_map/pallas_call | solution.py:151
  12.4 0.7 collective-permute-start.2
  13.1 2.1 %shard_map.57 = bf16[4,128,256]{2,1,0:T(8,128)(2,1)S(1)} custom-call(bf16[1,128,256]{2,1,0:T(8,128)(2,1)S(1)} %get-tuple-element.71.first_low, bf16[4,128,256]{2,1,0:T(8,128)(2,1)S(1)} %get-tuple-element.69.first_mid, bf16[1,128,256]{2,1,0:T(8,128)(2,1)S(1)} %get-tuple-element.72.first_high, bf16[4,128,256]{2,1,0:T(8,128)(2,1)S(1)} %get-tuple-element.107.q, ...), custom_call_target="tpu_custom_call" | custom-call | flops 1 | bytes 1 | tf_op jit(solution)/shard_map/pallas_call | solution.py:151
  15.2 0.6 collective-permute-done.3
  15.9 0.2 fusion.10
  16.2 4.6 %collective-permute-start.5 = (bf16[3,128,256]{2,1,0:T(8,128)(2,1)S(1)}, bf16[3,128,256]{2,1,0:T(8,128)(2,1)S(1)}, u32[]{:S(2)}, u32[]{:S(2)}) collective-permute-start(bf16[3,128,256]{2,1,0:T(8,128)(2,1)S(1)} %pad_maximum_fusion.3), channel_id=1, source_target_pairs={{1,2},{2,1},{3,4},{4,3},{5,6},{6,5},{9,10},{10,9},{11,12},{12,11},... | collective-permute-start | bytes 589832 | tf_op jit(solution)/shard_map/ppermute | solution.py:202
  21.0 0.7 collective-permute-start.9
  21.6 0.7 collective-permute-start.7
  22.3 2.1 %shard_map.58 = (bf16[2,128,256]{2,1,0:T(8,128)(2,1)S(1)}, f32[4,128,256]{2,1,0:T(8,128)S(1)}) custom-call(bf16[4,128,256]{2,1,0:T(8,128)(2,1)S(1)} %get-tuple-element.106.p, bf16[4,128,256]{2,1,0:T(8,128)(2,1)S(1)} %get-tuple-element.105.q, bf16[6912,256]{1,0:T(8,128)(2,1)S(1)} %get-tuple-element.68.weights), custom_call_target="tpu_custom_call" | custom-call | flops 1 | bytes 1 | tf_op jit(solution)/shard_map/pallas_call | solution.py:151
  24.5 1.8 %shard_map.59 = (bf16[1,128,256]{2,1,0:T(8,128)(2,1)S(1)}, bf16[4,128,256]{2,1,0:T(8,128)(2,1)S(1)}, bf16[1,128,256]{2,1,0:T(8,128)(2,1)S(1)}) custom-call(s32[3]{0:T(128)S(1)} %add_convert_fusion.6.flags, bf16[4,128,256]{2,1,0:T(8,128)(2,1)S(1)} %get-tuple-element.106.p, bf16[2,128,256]{2,1,0:T(8,128)(2,1)S(1)} %get-tuple-element.75.inner, ...), custom_call_target="tpu_custom_call" | custom-call | flops 1 | bytes 1 | tf_op jit(solution)/shard_map/pallas_call | solution.py:151
  26.3 3.7 %collective-permute-start.6 = (bf16[4,128,256]{2,1,0:T(8,128)(2,1)S(1)}, bf16[4,128,256]{2,1,0:T(8,128)(2,1)S(1)}, u32[]{:S(2)}, u32[]{:S(2)}) collective-permute-start(bf16[4,128,256]{2,1,0:T(8,128)(2,1)S(1)} %get-tuple-element.77.first_mid), channel_id=1, source_target_pairs={{0,8},{8,16},{16,24},{1,9},{9,17},{17,25},{2,10},{10,18},{18,26},{... | collective-permute-start | bytes 786440 | tf_op jit(solution)/shard_map/ppermute | solution.py:238
  30.0 2.1 %shard_map.60 = bf16[4,128,256]{2,1,0:T(8,128)(2,1)S(1)} custom-call(bf16[1,128,256]{2,1,0:T(8,128)(2,1)S(1)} %get-tuple-element.79.first_low, bf16[4,128,256]{2,1,0:T(8,128)(2,1)S(1)} %get-tuple-element.77.first_mid, bf16[1,128,256]{2,1,0:T(8,128)(2,1)S(1)} %get-tuple-element.80.first_high, bf16[4,128,256]{2,1,0:T(8,128)(2,1)S(1)} %get-tuple-element.105.q, ...), custom_call_target="tpu_custom_call" | custom-call | flops 1 | bytes 1 | tf_op jit(solution)/shard_map/pallas_call | solution.py:151
  32.2 1.9 %collective-permute-start.8 = (bf16[4,128,256]{2,1,0:T(8,128)(2,1)S(1)}, bf16[4,128,256]{2,1,0:T(8,128)(2,1)S(1)}, u32[]{:S(2)}, u32[]{:S(2)}) collective-permute-start(bf16[4,128,256]{2,1,0:T(8,128)(2,1)S(1)} %shard_map.60), channel_id=1, source_target_pairs={{0,8},{8,16},{16,24},{1,9},{9,17},{17,25},{2,10},{10,18},{18,26},{... | collective-permute-start | bytes 786440 | tf_op jit(solution)/shard_map/ppermute | solution.py:238
  34.1 0.7 collective-permute-start.10
  34.8 4.0 %collective-permute-done.6 = bf16[4,128,256]{2,1,0:T(8,128)(2,1)S(1)} collective-permute-done((bf16[4,128,256]{2,1,0:T(8,128)(2,1)S(1)}, bf16[4,128,256]{2,1,0:T(8,128)(2,1)S(1)}, u32[]{:S(2)}, u32[]{:S(2)}) %collective-permute-start.6) | collective-permute-done | bytes 262176 | tf_op jit(solution)/shard_map/ppermute | solution.py:238
  38.9 5.5 %collective-permute-done.8 = bf16[4,128,256]{2,1,0:T(8,128)(2,1)S(1)} collective-permute-done((bf16[4,128,256]{2,1,0:T(8,128)(2,1)S(1)}, bf16[4,128,256]{2,1,0:T(8,128)(2,1)S(1)}, u32[]{:S(2)}, u32[]{:S(2)}) %collective-permute-start.8) | collective-permute-done | bytes 262176 | tf_op jit(solution)/shard_map/ppermute | solution.py:238
  44.6 4.5 %collective-permute-start.12 = (bf16[3,128,256]{2,1,0:T(8,128)(2,1)S(1)}, bf16[3,128,256]{2,1,0:T(8,128)(2,1)S(1)}, u32[]{:S(2)}, u32[]{:S(2)}) collective-permute-start(bf16[3,128,256]{2,1,0:T(8,128)(2,1)S(1)} %pad_maximum_fusion.5), channel_id=1, source_target_pairs={{1,2},{2,1},{3,4},{4,3},{5,6},{6,5},{9,10},{10,9},{11,12},{12,11},... | collective-permute-start | bytes 589832 | tf_op jit(solution)/shard_map/ppermute | solution.py:202
  49.2 2.1 %shard_map.61 = (bf16[2,128,256]{2,1,0:T(8,128)(2,1)S(1)}, f32[4,128,256]{2,1,0:T(8,128)S(1)}) custom-call(bf16[4,128,256]{2,1,0:T(8,128)(2,1)S(1)} %fusion.17.p, bf16[4,128,256]{2,1,0:T(8,128)(2,1)S(1)} %fusion.16.q, bf16[6912,256]{1,0:T(8,128)(2,1)S(1)} %get-tuple-element.68.weights), custom_call_target="tpu_custom_call" | custom-call | flops 1 | bytes 1 | tf_op jit(solution)/shard_map/pallas_call | solution.py:151
  51.3 0.7 collective-permute-start.14
  52.0 0.4 collective-permute-done.12.far
  52.4 1.8 %shard_map.62 = (bf16[1,128,256]{2,1,0:T(8,128)(2,1)S(1)}, bf16[4,128,256]{2,1,0:T(8,128)(2,1)S(1)}, bf16[1,128,256]{2,1,0:T(8,128)(2,1)S(1)}) custom-call(s32[3]{0:T(128)S(1)} %add_convert_fusion.6.flags, bf16[4,128,256]{2,1,0:T(8,128)(2,1)S(1)} %fusion.17.p, bf16[2,128,256]{2,1,0:T(8,128)(2,1)S(1)} %get-tuple-element.84.inner, ...), custom_call_target="tpu_custom_call" | custom-call | flops 1 | bytes 1 | tf_op jit(solution)/shard_map/pallas_call | solution.py:151
  54.2 2.2 %collective-permute-start.13 = (bf16[4,128,256]{2,1,0:T(8,128)(2,1)S(1)}, bf16[4,128,256]{2,1,0:T(8,128)(2,1)S(1)}, u32[]{:S(2)}, u32[]{:S(2)}) collective-permute-start(bf16[4,128,256]{2,1,0:T(8,128)(2,1)S(1)} %get-tuple-element.86.first_mid), channel_id=1, source_target_pairs={{0,8},{8,16},{16,24},{1,9},{9,17},{17,25},{2,10},{10,18},{18,26},{... | collective-permute-start | bytes 786440 | tf_op jit(solution)/shard_map/ppermute | solution.py:238
  56.4 2.1 %shard_map.63 = bf16[4,128,256]{2,1,0:T(8,128)(2,1)S(1)} custom-call(bf16[1,128,256]{2,1,0:T(8,128)(2,1)S(1)} %get-tuple-element.87.first_low, bf16[4,128,256]{2,1,0:T(8,128)(2,1)S(1)} %get-tuple-element.86.first_mid, bf16[1,128,256]{2,1,0:T(8,128)(2,1)S(1)} %get-tuple-element.88.first_high, bf16[4,128,256]{2,1,0:T(8,128)(2,1)S(1)} %fusion.16.q, ...), custom_call_target="tpu_custom_call" | custom-call | flops 1 | bytes 1 | tf_op jit(solution)/shard_map/pallas_call | solution.py:151
  58.6 1.9 %collective-permute-start.15 = (bf16[4,128,256]{2,1,0:T(8,128)(2,1)S(1)}, bf16[4,128,256]{2,1,0:T(8,128)(2,1)S(1)}, u32[]{:S(2)}, u32[]{:S(2)}) collective-permute-start(bf16[4,128,256]{2,1,0:T(8,128)(2,1)S(1)} %shard_map.63), channel_id=1, source_target_pairs={{0,8},{8,16},{16,24},{1,9},{9,17},{17,25},{2,10},{10,18},{18,26},{... | collective-permute-start | bytes 786440 | tf_op jit(solution)/shard_map/ppermute | solution.py:238
  60.5 0.7 collective-permute-start.16
  61.2 3.3 %collective-permute-done.13 = bf16[4,128,256]{2,1,0:T(8,128)(2,1)S(1)} collective-permute-done((bf16[4,128,256]{2,1,0:T(8,128)(2,1)S(1)}, bf16[4,128,256]{2,1,0:T(8,128)(2,1)S(1)}, u32[]{:S(2)}, u32[]{:S(2)}) %collective-permute-start.13) | collective-permute-done | bytes 262176 | tf_op jit(solution)/shard_map/ppermute | solution.py:238
  64.6 5.5 %collective-permute-done.15 = bf16[4,128,256]{2,1,0:T(8,128)(2,1)S(1)} collective-permute-done((bf16[4,128,256]{2,1,0:T(8,128)(2,1)S(1)}, bf16[4,128,256]{2,1,0:T(8,128)(2,1)S(1)}, u32[]{:S(2)}, u32[]{:S(2)}) %collective-permute-start.15) | collective-permute-done | bytes 262176 | tf_op jit(solution)/shard_map/ppermute | solution.py:238
  70.3 3.8 %collective-permute-start.18 = (bf16[3,128,256]{2,1,0:T(8,128)(2,1)S(1)}, bf16[3,128,256]{2,1,0:T(8,128)(2,1)S(1)}, u32[]{:S(2)}, u32[]{:S(2)}) collective-permute-start(bf16[3,128,256]{2,1,0:T(8,128)(2,1)S(1)} %pad_maximum_fusion.7), channel_id=1, source_target_pairs={{1,2},{2,1},{3,4},{4,3},{5,6},{6,5},{9,10},{10,9},{11,12},{12,11},... | collective-permute-start | bytes 589832 | tf_op jit(solution)/shard_map/ppermute | solution.py:202
  74.3 2.1 %shard_map.64 = (bf16[2,128,256]{2,1,0:T(8,128)(2,1)S(1)}, f32[4,128,256]{2,1,0:T(8,128)S(1)}) custom-call(bf16[4,128,256]{2,1,0:T(8,128)(2,1)S(1)} %fusion.15.p, bf16[4,128,256]{2,1,0:T(8,128)(2,1)S(1)} %fusion.14.q, bf16[6912,256]{1,0:T(8,128)(2,1)S(1)} %get-tuple-element.68.weights), custom_call_target="tpu_custom_call" | custom-call | flops 1 | bytes 1 | tf_op jit(solution)/shard_map/pallas_call | solution.py:151
  76.4 0.7 collective-permute-start.20
  77.1 0.7 collective-permute-done.18.far
  77.8 1.8 %shard_map.65 = (bf16[1,128,256]{2,1,0:T(8,128)(2,1)S(1)}, bf16[4,128,256]{2,1,0:T(8,128)(2,1)S(1)}, bf16[1,128,256]{2,1,0:T(8,128)(2,1)S(1)}) custom-call(s32[3]{0:T(128)S(1)} %add_convert_fusion.6.flags, bf16[4,128,256]{2,1,0:T(8,128)(2,1)S(1)} %fusion.15.p, bf16[2,128,256]{2,1,0:T(8,128)(2,1)S(1)} %get-tuple-element.92.inner, ...), custom_call_target="tpu_custom_call" | custom-call | flops 1 | bytes 1 | tf_op jit(solution)/shard_map/pallas_call | solution.py:151
  79.6 1.9 %collective-permute-start.19 = (bf16[4,128,256]{2,1,0:T(8,128)(2,1)S(1)}, bf16[4,128,256]{2,1,0:T(8,128)(2,1)S(1)}, u32[]{:S(2)}, u32[]{:S(2)}) collective-permute-start(bf16[4,128,256]{2,1,0:T(8,128)(2,1)S(1)} %get-tuple-element.94.first_mid), channel_id=1, source_target_pairs={{8,16},{16,24},{9,17},{17,25},{10,18},{18,26},{11,19},{19,27},{12,... | collective-permute-start | bytes 786440 | tf_op jit(solution)/shard_map/ppermute | solution.py:238
  81.5 2.1 %shard_map.66 = bf16[4,128,256]{2,1,0:T(8,128)(2,1)S(1)} custom-call(bf16[1,128,256]{2,1,0:T(8,128)(2,1)S(1)} %get-tuple-element.95.first_low, bf16[4,128,256]{2,1,0:T(8,128)(2,1)S(1)} %get-tuple-element.94.first_mid, bf16[1,128,256]{2,1,0:T(8,128)(2,1)S(1)} %get-tuple-element.96.first_high, bf16[4,128,256]{2,1,0:T(8,128)(2,1)S(1)} %fusion.14.q, ...), custom_call_target="tpu_custom_call" | custom-call | flops 1 | bytes 1 | tf_op jit(solution)/shard_map/pallas_call | solution.py:151
  83.6 1.9 %collective-permute-start.21 = (bf16[4,128,256]{2,1,0:T(8,128)(2,1)S(1)}, bf16[4,128,256]{2,1,0:T(8,128)(2,1)S(1)}, u32[]{:S(2)}, u32[]{:S(2)}) collective-permute-start(bf16[4,128,256]{2,1,0:T(8,128)(2,1)S(1)} %shard_map.66), channel_id=1, source_target_pairs={{8,16},{16,24},{9,17},{17,25},{10,18},{18,26},{11,19},{19,27},{12,... | collective-permute-start | bytes 786440 | tf_op jit(solution)/shard_map/ppermute | solution.py:238
  85.6 0.7 collective-permute-start.22
  86.3 3.2 %collective-permute-done.19 = bf16[4,128,256]{2,1,0:T(8,128)(2,1)S(1)} collective-permute-done((bf16[4,128,256]{2,1,0:T(8,128)(2,1)S(1)}, bf16[4,128,256]{2,1,0:T(8,128)(2,1)S(1)}, u32[]{:S(2)}, u32[]{:S(2)}) %collective-permute-start.19) | collective-permute-done | bytes 262176 | tf_op jit(solution)/shard_map/ppermute | solution.py:238
  89.6 5.5 %collective-permute-done.21 = bf16[4,128,256]{2,1,0:T(8,128)(2,1)S(1)} collective-permute-done((bf16[4,128,256]{2,1,0:T(8,128)(2,1)S(1)}, bf16[4,128,256]{2,1,0:T(8,128)(2,1)S(1)}, u32[]{:S(2)}, u32[]{:S(2)}) %collective-permute-start.21) | collective-permute-done | bytes 262176 | tf_op jit(solution)/shard_map/ppermute | solution.py:238
  95.3 3.7 %collective-permute-start.24 = (bf16[3,128,256]{2,1,0:T(8,128)(2,1)S(1)}, bf16[3,128,256]{2,1,0:T(8,128)(2,1)S(1)}, u32[]{:S(2)}, u32[]{:S(2)}) collective-permute-start(bf16[3,128,256]{2,1,0:T(8,128)(2,1)S(1)} %pad_maximum_fusion.9), channel_id=1, source_target_pairs={{1,2},{2,1},{3,4},{4,3},{5,6},{6,5},{9,10},{10,9},{11,12},{12,11},... | collective-permute-start | bytes 589832 | tf_op jit(solution)/shard_map/ppermute | solution.py:202
  99.2 2.1 %shard_map.67 = (bf16[2,128,256]{2,1,0:T(8,128)(2,1)S(1)}, f32[4,128,256]{2,1,0:T(8,128)S(1)}) custom-call(bf16[4,128,256]{2,1,0:T(8,128)(2,1)S(1)} %fusion.13.p, bf16[4,128,256]{2,1,0:T(8,128)(2,1)S(1)} %fusion.12.q, bf16[6912,256]{1,0:T(8,128)(2,1)S(1)} %get-tuple-element.68.weights), custom_call_target="tpu_custom_call" | custom-call | flops 1 | bytes 1 | tf_op jit(solution)/shard_map/pallas_call | solution.py:151
  101.3 1.3 %collective-permute-done.24.far = bf16[3,128,256]{2,1,0:T(8,128)(2,1)S(1)} collective-permute-done((bf16[3,128,256]{2,1,0:T(8,128)(2,1)S(1)}, bf16[3,128,256]{2,1,0:T(8,128)(2,1)S(1)}, u32[]{:S(2)}, u32[]{:S(2)}) %collective-permute-start.24) | collective-permute-done | bytes 196640 | tf_op jit(solution)/shard_map/ppermute | solution.py:202
  102.6 1.8 %shard_map.68 = (bf16[1,128,256]{2,1,0:T(8,128)(2,1)S(1)}, bf16[4,128,256]{2,1,0:T(8,128)(2,1)S(1)}, bf16[1,128,256]{2,1,0:T(8,128)(2,1)S(1)}) custom-call(s32[3]{0:T(128)S(1)} %add_convert_fusion.6.flags, bf16[4,128,256]{2,1,0:T(8,128)(2,1)S(1)} %fusion.13.p, bf16[2,128,256]{2,1,0:T(8,128)(2,1)S(1)} %get-tuple-element.100.inner, ...), custom_call_target="tpu_custom_call" | custom-call | flops 1 | bytes 1 | tf_op jit(solution)/shard_map/pallas_call | solution.py:151
  104.4 2.8 %shard_map.69 = bf16[2,4,128,256]{3,2,1,0:T(8,128)(2,1)} custom-call(bf16[1,128,256]{2,1,0:T(8,128)(2,1)S(1)} %get-tuple-element.102.first_low, bf16[4,128,256]{2,1,0:T(8,128)(2,1)S(1)} %get-tuple-element.103.first_mid, bf16[1,128,256]{2,1,0:T(8,128)(2,1)S(1)} %get-tuple-element.104.first_high, bf16[4,128,256]{2,1,0:T(8,128)(2,1)S(1)} %fusion.12.q, ...), custom_call_target="tpu_custom_call" | custom-call | flops 1 | bytes 1 | tf_op jit(solution)/shard_map/pallas_call | solution.py:151
  (52 shorter events, 1.6 us)
Async XLA Ops:
  0.1 15.8 %collective-permute-start.3 = (bf16[2,4,128,256]{3,2,1,0:T(8,128)(2,1)}, bf16[2,4,128,256]{3,2,1,0:T(8,128)(2,1)S(1)}, u32[]{:S(2)}, u32[]{:S(2)}) collective-permute-start(bf16[2,4,128,256]{3,2,1,0:T(8,128)(2,1)} %bitcast.63), channel_id=1, source_target_pairs={{0,24},{8,16},{1,25},{9,17},{2,26},{10,18},{3,27},{11,19},{4,28},{... | collective-permute-start | bytes 1572872 | tf_op jit(solution)/shard_map/ppermute | solution.py:238
  2.5 7.9 %collective-permute-start = (bf16[3,128,256]{2,1,0:T(8,128)(2,1)S(1)}, bf16[3,128,256]{2,1,0:T(8,128)(2,1)S(1)}, u32[]{:S(2)}, u32[]{:S(2)}) collective-permute-start(bf16[3,128,256]{2,1,0:T(8,128)(2,1)S(1)} %pad_maximum_fusion), channel_id=1, source_target_pairs={{0,1},{1,0},{2,3},{3,2},{4,5},{5,4},{6,7},{7,6},{8,9},{9,8},{10,11... | collective-permute-start | bytes 589832 | tf_op jit(solution)/shard_map/ppermute | solution.py:202
  3.3 7.3 %collective-permute-start.1 = (bf16[3,128,256]{2,1,0:T(8,128)(2,1)S(1)}, bf16[3,128,256]{2,1,0:T(8,128)(2,1)S(1)}, u32[]{:S(2)}, u32[]{:S(2)}) collective-permute-start(bf16[3,128,256]{2,1,0:T(8,128)(2,1)S(1)} %pad_maximum_fusion.1), channel_id=1, source_target_pairs={{1,2},{2,1},{3,4},{4,3},{5,6},{6,5},{9,10},{10,9},{11,12},{12,11},... | collective-permute-start | bytes 589832 | tf_op jit(solution)/shard_map/ppermute | solution.py:202
  10.6 2.5 %copy-start = (bf16[1,3,3,3,256,256]{5,4,3,2,1,0:T(8,128)(2,1)S(1)}, bf16[1,3,3,3,256,256]{5,4,3,2,1,0:T(8,128)(2,1)}, u32[]{:S(2)}) copy-start(bf16[1,3,3,3,256,256]{5,4,3,2,1,0:T(8,128)(2,1)} %param.9) | copy-start | bytes 10616836
  12.4 9.3 %collective-permute-start.2 = (bf16[4,128,256]{2,1,0:T(8,128)(2,1)S(1)}, bf16[4,128,256]{2,1,0:T(8,128)(2,1)S(1)}, u32[]{:S(2)}, u32[]{:S(2)}) collective-permute-start(bf16[4,128,256]{2,1,0:T(8,128)(2,1)S(1)} %get-tuple-element.69.first_mid), channel_id=1, source_target_pairs={{0,8},{1,9},{2,10},{3,11},{4,12},{5,13},{6,14},{7,15}} | collective-permute-start | bytes 786440 | tf_op jit(solution)/shard_map/ppermute | solution.py:238
  13.1 2.8 %copy-start.1 = (bf16[3,2,4,16,8,256]{5,4,3,2,1,0:T(8,128)(2,1)S(1)}, bf16[3,2,4,16,8,256]{5,4,3,2,1,0:T(8,128)(2,1)}, u32[]{:S(2)}) copy-start(bf16[3,2,4,16,8,256]{5,4,3,2,1,0:T(8,128)(2,1)} %param.7) | copy-start | bytes 4718596
  13.1 2.8 %copy-start.2 = (bf16[1,2,4,16,8,256]{5,4,3,2,1,0:T(8,128)(2,1)S(1)}, bf16[1,2,4,16,8,256]{5,4,3,2,1,0:T(8,128)(2,1)}, u32[]{:S(2)}) copy-start(bf16[1,2,4,16,8,256]{5,4,3,2,1,0:T(8,128)(2,1)} %param.5) | copy-start | bytes 1572868
  16.2 8.3 %collective-permute-start.5 = (bf16[3,128,256]{2,1,0:T(8,128)(2,1)S(1)}, bf16[3,128,256]{2,1,0:T(8,128)(2,1)S(1)}, u32[]{:S(2)}, u32[]{:S(2)}) collective-permute-start(bf16[3,128,256]{2,1,0:T(8,128)(2,1)S(1)} %pad_maximum_fusion.3), channel_id=1, source_target_pairs={{1,2},{2,1},{3,4},{4,3},{5,6},{6,5},{9,10},{10,9},{11,12},{12,11},... | collective-permute-start | bytes 589832 | tf_op jit(solution)/shard_map/ppermute | solution.py:202
  20.9 3.6 %collective-permute-start.4 = (bf16[3,128,256]{2,1,0:T(8,128)(2,1)S(1)}, bf16[3,128,256]{2,1,0:T(8,128)(2,1)S(1)}, u32[]{:S(2)}, u32[]{:S(2)}) collective-permute-start(bf16[3,128,256]{2,1,0:T(8,128)(2,1)S(1)} %pad_maximum_fusion.2), channel_id=1, source_target_pairs={{0,1},{1,0},{2,3},{3,2},{4,5},{5,4},{6,7},{7,6},{8,9},{9,8},{10,11... | collective-permute-start | bytes 589832 | tf_op jit(solution)/shard_map/ppermute | solution.py:202
  21.0 13.1 %collective-permute-start.9 = (bf16[4,128,256]{2,1,0:T(8,128)(2,1)S(1)}, bf16[4,128,256]{2,1,0:T(8,128)(2,1)S(1)}, u32[]{:S(2)}, u32[]{:S(2)}) collective-permute-start(bf16[4,128,256]{2,1,0:T(8,128)(2,1)S(1)} %shard_map.57), channel_id=1, source_target_pairs={{0,8},{1,9},{2,10},{3,11},{4,12},{5,13},{6,14},{7,15}} | collective-permute-start | bytes 786440 | tf_op jit(solution)/shard_map/ppermute | solution.py:238
  21.6 13.1 %collective-permute-start.7 = (bf16[4,128,256]{2,1,0:T(8,128)(2,1)S(1)}, bf16[4,128,256]{2,1,0:T(8,128)(2,1)S(1)}, u32[]{:S(2)}, u32[]{:S(2)}) collective-permute-start(bf16[4,128,256]{2,1,0:T(8,128)(2,1)S(1)} %collective-permute-done.2), channel_id=1, source_target_pairs={{8,24},{9,25},{10,26},{11,27},{12,28},{13,29},{14,30},{15,31}} | collective-permute-start | bytes 786440 | tf_op jit(solution)/shard_map/ppermute | solution.py:238
  26.3 12.5 %collective-permute-start.6 = (bf16[4,128,256]{2,1,0:T(8,128)(2,1)S(1)}, bf16[4,128,256]{2,1,0:T(8,128)(2,1)S(1)}, u32[]{:S(2)}, u32[]{:S(2)}) collective-permute-start(bf16[4,128,256]{2,1,0:T(8,128)(2,1)S(1)} %get-tuple-element.77.first_mid), channel_id=1, source_target_pairs={{0,8},{8,16},{16,24},{1,9},{9,17},{17,25},{2,10},{10,18},{18,26},{... | collective-permute-start | bytes 786440 | tf_op jit(solution)/shard_map/ppermute | solution.py:238
  32.2 12.2 %collective-permute-start.8 = (bf16[4,128,256]{2,1,0:T(8,128)(2,1)S(1)}, bf16[4,128,256]{2,1,0:T(8,128)(2,1)S(1)}, u32[]{:S(2)}, u32[]{:S(2)}) collective-permute-start(bf16[4,128,256]{2,1,0:T(8,128)(2,1)S(1)} %shard_map.60), channel_id=1, source_target_pairs={{0,8},{8,16},{16,24},{1,9},{9,17},{17,25},{2,10},{10,18},{18,26},{... | collective-permute-start | bytes 786440 | tf_op jit(solution)/shard_map/ppermute | solution.py:238
  34.1 10.3 %collective-permute-start.10 = (bf16[4,128,256]{2,1,0:T(8,128)(2,1)S(1)}, bf16[4,128,256]{2,1,0:T(8,128)(2,1)S(1)}, u32[]{:S(2)}, u32[]{:S(2)}) collective-permute-start(bf16[4,128,256]{2,1,0:T(8,128)(2,1)S(1)} %collective-permute-done.9), channel_id=1, source_target_pairs={{8,24},{9,25},{10,26},{11,27},{12,28},{13,29},{14,30},{15,31}} | collective-permute-start | bytes 786440 | tf_op jit(solution)/shard_map/ppermute | solution.py:238
  44.6 7.8 %collective-permute-start.12 = (bf16[3,128,256]{2,1,0:T(8,128)(2,1)S(1)}, bf16[3,128,256]{2,1,0:T(8,128)(2,1)S(1)}, u32[]{:S(2)}, u32[]{:S(2)}) collective-permute-start(bf16[3,128,256]{2,1,0:T(8,128)(2,1)S(1)} %pad_maximum_fusion.5), channel_id=1, source_target_pairs={{1,2},{2,1},{3,4},{4,3},{5,6},{6,5},{9,10},{10,9},{11,12},{12,11},... | collective-permute-start | bytes 589832 | tf_op jit(solution)/shard_map/ppermute | solution.py:202
  49.1 3.3 %collective-permute-start.11 = (bf16[3,128,256]{2,1,0:T(8,128)(2,1)S(1)}, bf16[3,128,256]{2,1,0:T(8,128)(2,1)S(1)}, u32[]{:S(2)}, u32[]{:S(2)}) collective-permute-start(bf16[3,128,256]{2,1,0:T(8,128)(2,1)S(1)} %pad_maximum_fusion.4), channel_id=1, source_target_pairs={{0,1},{1,0},{2,3},{3,2},{4,5},{5,4},{6,7},{7,6},{8,9},{9,8},{10,11... | collective-permute-start | bytes 589832 | tf_op jit(solution)/shard_map/ppermute | solution.py:202
  51.3 9.8 %collective-permute-start.14 = (bf16[4,128,256]{2,1,0:T(8,128)(2,1)S(1)}, bf16[4,128,256]{2,1,0:T(8,128)(2,1)S(1)}, u32[]{:S(2)}, u32[]{:S(2)}) collective-permute-start(bf16[4,128,256]{2,1,0:T(8,128)(2,1)S(1)} %collective-permute-done.6), channel_id=1, source_target_pairs={{8,24},{9,25},{10,26},{11,27},{12,28},{13,29},{14,30},{15,31}} | collective-permute-start | bytes 786440 | tf_op jit(solution)/shard_map/ppermute | solution.py:238
  54.2 10.3 %collective-permute-start.13 = (bf16[4,128,256]{2,1,0:T(8,128)(2,1)S(1)}, bf16[4,128,256]{2,1,0:T(8,128)(2,1)S(1)}, u32[]{:S(2)}, u32[]{:S(2)}) collective-permute-start(bf16[4,128,256]{2,1,0:T(8,128)(2,1)S(1)} %get-tuple-element.86.first_mid), channel_id=1, source_target_pairs={{0,8},{8,16},{16,24},{1,9},{9,17},{17,25},{2,10},{10,18},{18,26},{... | collective-permute-start | bytes 786440 | tf_op jit(solution)/shard_map/ppermute | solution.py:238
  58.6 11.5 %collective-permute-start.15 = (bf16[4,128,256]{2,1,0:T(8,128)(2,1)S(1)}, bf16[4,128,256]{2,1,0:T(8,128)(2,1)S(1)}, u32[]{:S(2)}, u32[]{:S(2)}) collective-permute-start(bf16[4,128,256]{2,1,0:T(8,128)(2,1)S(1)} %shard_map.63), channel_id=1, source_target_pairs={{0,8},{8,16},{16,24},{1,9},{9,17},{17,25},{2,10},{10,18},{18,26},{... | collective-permute-start | bytes 786440 | tf_op jit(solution)/shard_map/ppermute | solution.py:238
  60.5 9.6 %collective-permute-start.16 = (bf16[4,128,256]{2,1,0:T(8,128)(2,1)S(1)}, bf16[4,128,256]{2,1,0:T(8,128)(2,1)S(1)}, u32[]{:S(2)}, u32[]{:S(2)}) collective-permute-start(bf16[4,128,256]{2,1,0:T(8,128)(2,1)S(1)} %collective-permute-done.8), channel_id=1, source_target_pairs={{8,24},{9,25},{10,26},{11,27},{12,28},{13,29},{14,30},{15,31}} | collective-permute-start | bytes 786440 | tf_op jit(solution)/shard_map/ppermute | solution.py:238
  70.3 7.5 %collective-permute-start.18 = (bf16[3,128,256]{2,1,0:T(8,128)(2,1)S(1)}, bf16[3,128,256]{2,1,0:T(8,128)(2,1)S(1)}, u32[]{:S(2)}, u32[]{:S(2)}) collective-permute-start(bf16[3,128,256]{2,1,0:T(8,128)(2,1)S(1)} %pad_maximum_fusion.7), channel_id=1, source_target_pairs={{1,2},{2,1},{3,4},{4,3},{5,6},{6,5},{9,10},{10,9},{11,12},{12,11},... | collective-permute-start | bytes 589832 | tf_op jit(solution)/shard_map/ppermute | solution.py:202
  74.2 3.6 %collective-permute-start.17 = (bf16[3,128,256]{2,1,0:T(8,128)(2,1)S(1)}, bf16[3,128,256]{2,1,0:T(8,128)(2,1)S(1)}, u32[]{:S(2)}, u32[]{:S(2)}) collective-permute-start(bf16[3,128,256]{2,1,0:T(8,128)(2,1)S(1)} %pad_maximum_fusion.6), channel_id=1, source_target_pairs={{0,1},{1,0},{2,3},{3,2},{4,5},{5,4},{6,7},{7,6},{8,9},{9,8},{10,11... | collective-permute-start | bytes 589832 | tf_op jit(solution)/shard_map/ppermute | solution.py:202
  76.4 9.9 %collective-permute-start.20 = (bf16[4,128,256]{2,1,0:T(8,128)(2,1)S(1)}, bf16[4,128,256]{2,1,0:T(8,128)(2,1)S(1)}, u32[]{:S(2)}, u32[]{:S(2)}) collective-permute-start(bf16[4,128,256]{2,1,0:T(8,128)(2,1)S(1)} %collective-permute-done.13), channel_id=1, source_target_pairs={{8,24},{9,25},{10,26},{11,27},{12,28},{13,29},{14,30},{15,31}} | collective-permute-start | bytes 786440 | tf_op jit(solution)/shard_map/ppermute | solution.py:238
  79.6 9.9 %collective-permute-start.19 = (bf16[4,128,256]{2,1,0:T(8,128)(2,1)S(1)}, bf16[4,128,256]{2,1,0:T(8,128)(2,1)S(1)}, u32[]{:S(2)}, u32[]{:S(2)}) collective-permute-start(bf16[4,128,256]{2,1,0:T(8,128)(2,1)S(1)} %get-tuple-element.94.first_mid), channel_id=1, source_target_pairs={{8,16},{16,24},{9,17},{17,25},{10,18},{18,26},{11,19},{19,27},{12,... | collective-permute-start | bytes 786440 | tf_op jit(solution)/shard_map/ppermute | solution.py:238
  83.6 11.4 %collective-permute-start.21 = (bf16[4,128,256]{2,1,0:T(8,128)(2,1)S(1)}, bf16[4,128,256]{2,1,0:T(8,128)(2,1)S(1)}, u32[]{:S(2)}, u32[]{:S(2)}) collective-permute-start(bf16[4,128,256]{2,1,0:T(8,128)(2,1)S(1)} %shard_map.66), channel_id=1, source_target_pairs={{8,16},{16,24},{9,17},{17,25},{10,18},{18,26},{11,19},{19,27},{12,... | collective-permute-start | bytes 786440 | tf_op jit(solution)/shard_map/ppermute | solution.py:238
  85.6 9.5 %collective-permute-start.22 = (bf16[4,128,256]{2,1,0:T(8,128)(2,1)S(1)}, bf16[4,128,256]{2,1,0:T(8,128)(2,1)S(1)}, u32[]{:S(2)}, u32[]{:S(2)}) collective-permute-start(bf16[4,128,256]{2,1,0:T(8,128)(2,1)S(1)} %collective-permute-done.15), channel_id=1, source_target_pairs={{8,24},{9,25},{10,26},{11,27},{12,28},{13,29},{14,30},{15,31}} | collective-permute-start | bytes 786440 | tf_op jit(solution)/shard_map/ppermute | solution.py:238
  95.3 7.3 %collective-permute-start.24 = (bf16[3,128,256]{2,1,0:T(8,128)(2,1)S(1)}, bf16[3,128,256]{2,1,0:T(8,128)(2,1)S(1)}, u32[]{:S(2)}, u32[]{:S(2)}) collective-permute-start(bf16[3,128,256]{2,1,0:T(8,128)(2,1)S(1)} %pad_maximum_fusion.9), channel_id=1, source_target_pairs={{1,2},{2,1},{3,4},{4,3},{5,6},{6,5},{9,10},{10,9},{11,12},{12,11},... | collective-permute-start | bytes 589832 | tf_op jit(solution)/shard_map/ppermute | solution.py:202
  99.0 3.6 %collective-permute-start.23 = (bf16[3,128,256]{2,1,0:T(8,128)(2,1)S(1)}, bf16[3,128,256]{2,1,0:T(8,128)(2,1)S(1)}, u32[]{:S(2)}, u32[]{:S(2)}) collective-permute-start(bf16[3,128,256]{2,1,0:T(8,128)(2,1)S(1)} %pad_maximum_fusion.8), channel_id=1, source_target_pairs={{0,1},{1,0},{2,3},{3,2},{4,5},{5,4},{6,7},{7,6},{8,9},{9,8},{10,11... | collective-permute-start | bytes 589832 | tf_op jit(solution)/shard_map/ppermute | solution.py:202

commit v22 on v21

--- a/solution.py
+++ b/solution.py
@@ -254,8 +254,9 @@
         return jnp.where(places["first"], fresh, join(held, skip))
 
     p, q = resident
+    near, far = (swap(turn, starts, (q, 2), (p, 1)) for turn in range(2))
+    near, previous = lax.optimization_barrier((near, previous))
     mirrored = send(previous, [(j, sections - 1 - j) for j in range(half)])
-    near, far = (swap(turn, starts, (q, 2), (p, 1)) for turn in range(2))
     for slot in range(ticks + 1):
         if slot == 1:
             p, q, near, far = following

time: 109 us -> 112 us (1.028)
  starting transfers between devices: 41.2 us -> 42.9 us
  transfers between devices with their start and end apart: 25 -> 25, of which waited for: 11 -> 11; matrix products, arithmetic and copies ran while one was open for 2% -> 1% of each run, Pallas kernels for 26% -> 26%
where the time goes in v22:
time: 112 us; the launch traced here: 110 us
  starting transfers between devices  42.9 us (38%)
  Pallas kernels  32.9 us (29%)
  waiting for transfers between devices  31 us (28%)
  local copies, waits for them, and re-layouts  1.36 us (1%)
  other arithmetic  1.16 us (1%)
    pallas_call x15, Pallas kernels, call(): pl.pallas_call(functools.partial(kernel, width), out_shape=[jax.ShapeDtyp...  32.9 us
    ppermute x15, waiting for transfers between devices, send(): return lax.ppermute(block, 'section', pairs) if pairs else block  27.8 us
    ppermute x10, starting transfers between devices, swap(): return lax.ppermute(jnp.concatenate(parts, axis=0), 'depth', pairs)  21.7 us
    ppermute x15, starting transfers between devices, send(): return lax.ppermute(block, 'section', pairs) if pairs else block  21.2 us
    ppermute x10, waiting for transfers between devices, swap(): return lax.ppermute(jnp.concatenate(parts, axis=0), 'depth', pairs)  3.15 us
  transfers between devices with their start and end apart: 25, of which 11 were waited for; matrix products, arithmetic and copies ran while one was open for 1% of the time, Pallas kernels for 26%

profile of v22, /device:TPU:13, one launch (start us, length us, event | category | flops | bytes accessed | tf_op | source)
XLA Modules:
  0.0 110.0 jit_solution(1682651893725748324)
XLA Ops:
  0.1 1.1 %slice_bitcast_fusion.6 = (bf16[4,128,256]{2,1,0:T(8,128)(2,1)S(1)}, bf16[4,128,256]{2,1,0:T(8,128)(2,1)S(1)}) fusion(bf16[1,2,4,16,8,256]{5,4,3,2,1,0:T(8,128)(2,1)} %param.5), kind=kLoop, calls=%fused_computation.32 | loop fusion | bytes 1048576 | tf_op jit(solution)/shard_map/unstack | solution.py:256
  1.3 0.7 collective-permute-start
  2.0 1.1 collective-permute-done.near
  3.1 1.3 %collective-permute-start.3 = (bf16[2,4,128,256]{3,2,1,0:T(8,128)(2,1)S(1)}, bf16[2,4,128,256]{3,2,1,0:T(8,128)(2,1)S(1)}, u32[]{:S(2)}, u32[]{:S(2)}) collective-permute-start(bf16[2,4,128,256]{3,2,1,0:T(8,128)(2,1)S(1)} %bitcast.63), channel_id=1, source_target_pairs={{0,24},{8,16},{1,25},{9,17},{2,26},{10,18},{3,27},{11,19},{4,28},{... | collective-permute-start | bytes 1572872 | tf_op jit(solution)/shard_map/ppermute | solution.py:238
  4.4 3.5 %collective-permute-start.1 = (bf16[3,128,256]{2,1,0:T(8,128)(2,1)S(1)}, bf16[3,128,256]{2,1,0:T(8,128)(2,1)S(1)}, u32[]{:S(2)}, u32[]{:S(2)}) collective-permute-start(bf16[3,128,256]{2,1,0:T(8,128)(2,1)S(1)} %pad_maximum_fusion.1), channel_id=1, source_target_pairs={{1,2},{2,1},{3,4},{4,3},{5,6},{6,5},{9,10},{10,9},{11,12},{12,11},... | collective-permute-start | bytes 589832 | tf_op jit(solution)/shard_map/ppermute | solution.py:202
  7.9 4.1 %shard_map.55 = (bf16[2,128,256]{2,1,0:T(8,128)(2,1)S(1)}, f32[4,128,256]{2,1,0:T(8,128)S(1)}, bf16[6912,256]{1,0:T(8,128)(2,1)S(1)}) custom-call(bf16[4,128,256]{2,1,0:T(8,128)(2,1)S(1)} %get-tuple-element.112.p, bf16[4,128,256]{2,1,0:T(8,128)(2,1)S(1)} %get-tuple-element.111.q, bf16[6912,256]{1,0:T(8,128)(2,1)} %bitcast.55), custom_call_target="tpu_custom_call" | custom-call | flops 1 | bytes 1 | tf_op jit(solution)/shard_map/pallas_call | solution.py:151
  12.0 1.8 %shard_map.56 = (bf16[1,128,256]{2,1,0:T(8,128)(2,1)S(1)}, bf16[4,128,256]{2,1,0:T(8,128)(2,1)S(1)}, bf16[1,128,256]{2,1,0:T(8,128)(2,1)S(1)}) custom-call(s32[3]{0:T(128)S(1)} %add_convert_fusion.6.flags, bf16[4,128,256]{2,1,0:T(8,128)(2,1)S(1)} %get-tuple-element.112.p, bf16[2,128,256]{2,1,0:T(8,128)(2,1)S(1)} %get-tuple-element.64.inner, ...), custom_call_target="tpu_custom_call" | custom-call | flops 1 | bytes 1 | tf_op jit(solution)/shard_map/pallas_call | solution.py:151
  13.8 0.7 collective-permute-start.2
  14.5 2.1 %shard_map.57 = bf16[4,128,256]{2,1,0:T(8,128)(2,1)S(1)} custom-call(bf16[1,128,256]{2,1,0:T(8,128)(2,1)S(1)} %get-tuple-element.75.first_low, bf16[4,128,256]{2,1,0:T(8,128)(2,1)S(1)} %get-tuple-element.73.first_mid, bf16[1,128,256]{2,1,0:T(8,128)(2,1)S(1)} %get-tuple-element.76.first_high, bf16[4,128,256]{2,1,0:T(8,128)(2,1)S(1)} %get-tuple-element.111.q, ...), custom_call_target="tpu_custom_call" | custom-call | flops 1 | bytes 1 | tf_op jit(solution)/shard_map/pallas_call | solution.py:151
  16.6 2.4 %collective-permute-done.3 = bf16[2,4,128,256]{3,2,1,0:T(8,128)(2,1)S(1)} collective-permute-done((bf16[2,4,128,256]{3,2,1,0:T(8,128)(2,1)S(1)}, bf16[2,4,128,256]{3,2,1,0:T(8,128)(2,1)S(1)}, u32[]{:S(2)}, u32[]{:S(2)}) %collective-permute-start.3) | collective-permute-done | bytes 524320 | tf_op jit(solution)/shard_map/ppermute | solution.py:238
  19.4 4.3 %collective-permute-start.5 = (bf16[3,128,256]{2,1,0:T(8,128)(2,1)S(1)}, bf16[3,128,256]{2,1,0:T(8,128)(2,1)S(1)}, u32[]{:S(2)}, u32[]{:S(2)}) collective-permute-start(bf16[3,128,256]{2,1,0:T(8,128)(2,1)S(1)} %pad_maximum_fusion.3), channel_id=1, source_target_pairs={{1,2},{2,1},{3,4},{4,3},{5,6},{6,5},{9,10},{10,9},{11,12},{12,11},... | collective-permute-start | bytes 589832 | tf_op jit(solution)/shard_map/ppermute | solution.py:202
  23.8 0.7 collective-permute-start.9
  24.5 0.7 collective-permute-start.7
  25.1 2.1 %shard_map.58 = (bf16[2,128,256]{2,1,0:T(8,128)(2,1)S(1)}, f32[4,128,256]{2,1,0:T(8,128)S(1)}) custom-call(bf16[4,128,256]{2,1,0:T(8,128)(2,1)S(1)} %get-tuple-element.110.p, bf16[4,128,256]{2,1,0:T(8,128)(2,1)S(1)} %get-tuple-element.109.q, bf16[6912,256]{1,0:T(8,128)(2,1)S(1)} %get-tuple-element.72.weights), custom_call_target="tpu_custom_call" | custom-call | flops 1 | bytes 1 | tf_op jit(solution)/shard_map/pallas_call | solution.py:151
  27.3 1.8 %shard_map.59 = (bf16[1,128,256]{2,1,0:T(8,128)(2,1)S(1)}, bf16[4,128,256]{2,1,0:T(8,128)(2,1)S(1)}, bf16[1,128,256]{2,1,0:T(8,128)(2,1)S(1)}) custom-call(s32[3]{0:T(128)S(1)} %add_convert_fusion.6.flags, bf16[4,128,256]{2,1,0:T(8,128)(2,1)S(1)} %get-tuple-element.110.p, bf16[2,128,256]{2,1,0:T(8,128)(2,1)S(1)} %get-tuple-element.79.inner, ...), custom_call_target="tpu_custom_call" | custom-call | flops 1 | bytes 1 | tf_op jit(solution)/shard_map/pallas_call | solution.py:151
  29.1 3.7 %collective-permute-start.6 = (bf16[4,128,256]{2,1,0:T(8,128)(2,1)S(1)}, bf16[4,128,256]{2,1,0:T(8,128)(2,1)S(1)}, u32[]{:S(2)}, u32[]{:S(2)}) collective-permute-start(bf16[4,128,256]{2,1,0:T(8,128)(2,1)S(1)} %get-tuple-element.81.first_mid), channel_id=1, source_target_pairs={{0,8},{8,16},{16,24},{1,9},{9,17},{17,25},{2,10},{10,18},{18,26},{... | collective-permute-start | bytes 786440 | tf_op jit(solution)/shard_map/ppermute | solution.py:238
  32.9 2.1 %shard_map.60 = bf16[4,128,256]{2,1,0:T(8,128)(2,1)S(1)} custom-call(bf16[1,128,256]{2,1,0:T(8,128)(2,1)S(1)} %get-tuple-element.83.first_low, bf16[4,128,256]{2,1,0:T(8,128)(2,1)S(1)} %get-tuple-element.81.first_mid, bf16[1,128,256]{2,1,0:T(8,128)(2,1)S(1)} %get-tuple-element.84.first_high, bf16[4,128,256]{2,1,0:T(8,128)(2,1)S(1)} %get-tuple-element.109.q, ...), custom_call_target="tpu_custom_call" | custom-call | flops 1 | bytes 1 | tf_op jit(solution)/shard_map/pallas_call | solution.py:151
  35.0 1.9 %collective-permute-start.8 = (bf16[4,128,256]{2,1,0:T(8,128)(2,1)S(1)}, bf16[4,128,256]{2,1,0:T(8,128)(2,1)S(1)}, u32[]{:S(2)}, u32[]{:S(2)}) collective-permute-start(bf16[4,128,256]{2,1,0:T(8,128)(2,1)S(1)} %shard_map.60), channel_id=1, source_target_pairs={{0,8},{8,16},{16,24},{1,9},{9,17},{17,25},{2,10},{10,18},{18,26},{... | collective-permute-start | bytes 786440 | tf_op jit(solution)/shard_map/ppermute | solution.py:238
  36.9 0.7 collective-permute-start.10
  37.6 3.0 %collective-permute-done.6 = bf16[4,128,256]{2,1,0:T(8,128)(2,1)S(1)} collective-permute-done((bf16[4,128,256]{2,1,0:T(8,128)(2,1)S(1)}, bf16[4,128,256]{2,1,0:T(8,128)(2,1)S(1)}, u32[]{:S(2)}, u32[]{:S(2)}) %collective-permute-start.6) | collective-permute-done | bytes 262176 | tf_op jit(solution)/shard_map/ppermute | solution.py:238
  40.7 5.5 %collective-permute-done.8 = bf16[4,128,256]{2,1,0:T(8,128)(2,1)S(1)} collective-permute-done((bf16[4,128,256]{2,1,0:T(8,128)(2,1)S(1)}, bf16[4,128,256]{2,1,0:T(8,128)(2,1)S(1)}, u32[]{:S(2)}, u32[]{:S(2)}) %collective-permute-start.8) | collective-permute-done | bytes 262176 | tf_op jit(solution)/shard_map/ppermute | solution.py:238
  46.4 5.4 %collective-permute-start.12 = (bf16[3,128,256]{2,1,0:T(8,128)(2,1)S(1)}, bf16[3,128,256]{2,1,0:T(8,128)(2,1)S(1)}, u32[]{:S(2)}, u32[]{:S(2)}) collective-permute-start(bf16[3,128,256]{2,1,0:T(8,128)(2,1)S(1)} %pad_maximum_fusion.5), channel_id=1, source_target_pairs={{1,2},{2,1},{3,4},{4,3},{5,6},{6,5},{9,10},{10,9},{11,12},{12,11},... | collective-permute-start | bytes 589832 | tf_op jit(solution)/shard_map/ppermute | solution.py:202
  51.9 2.1 %shard_map.61 = (bf16[2,128,256]{2,1,0:T(8,128)(2,1)S(1)}, f32[4,128,256]{2,1,0:T(8,128)S(1)}) custom-call(bf16[4,128,256]{2,1,0:T(8,128)(2,1)S(1)} %fusion.17.p, bf16[4,128,256]{2,1,0:T(8,128)(2,1)S(1)} %fusion.16.q, bf16[6912,256]{1,0:T(8,128)(2,1)S(1)} %get-tuple-element.72.weights), custom_call_target="tpu_custom_call" | custom-call | flops 1 | bytes 1 | tf_op jit(solution)/shard_map/pallas_call | solution.py:151
  54.1 0.7 collective-permute-start.14
  55.0 1.8 %shard_map.62 = (bf16[1,128,256]{2,1,0:T(8,128)(2,1)S(1)}, bf16[4,128,256]{2,1,0:T(8,128)(2,1)S(1)}, bf16[1,128,256]{2,1,0:T(8,128)(2,1)S(1)}) custom-call(s32[3]{0:T(128)S(1)} %add_convert_fusion.6.flags, bf16[4,128,256]{2,1,0:T(8,128)(2,1)S(1)} %fusion.17.p, bf16[2,128,256]{2,1,0:T(8,128)(2,1)S(1)} %get-tuple-element.88.inner, ...), custom_call_target="tpu_custom_call" | custom-call | flops 1 | bytes 1 | tf_op jit(solution)/shard_map/pallas_call | solution.py:151
  56.8 2.9 %collective-permute-start.13 = (bf16[4,128,256]{2,1,0:T(8,128)(2,1)S(1)}, bf16[4,128,256]{2,1,0:T(8,128)(2,1)S(1)}, u32[]{:S(2)}, u32[]{:S(2)}) collective-permute-start(bf16[4,128,256]{2,1,0:T(8,128)(2,1)S(1)} %get-tuple-element.90.first_mid), channel_id=1, source_target_pairs={{0,8},{8,16},{16,24},{1,9},{9,17},{17,25},{2,10},{10,18},{18,26},{... | collective-permute-start | bytes 786440 | tf_op jit(solution)/shard_map/ppermute | solution.py:238
  59.7 2.1 %shard_map.63 = bf16[4,128,256]{2,1,0:T(8,128)(2,1)S(1)} custom-call(bf16[1,128,256]{2,1,0:T(8,128)(2,1)S(1)} %get-tuple-element.91.first_low, bf16[4,128,256]{2,1,0:T(8,128)(2,1)S(1)} %get-tuple-element.90.first_mid, bf16[1,128,256]{2,1,0:T(8,128)(2,1)S(1)} %get-tuple-element.92.first_high, bf16[4,128,256]{2,1,0:T(8,128)(2,1)S(1)} %fusion.16.q, ...), custom_call_target="tpu_custom_call" | custom-call | flops 1 | bytes 1 | tf_op jit(solution)/shard_map/pallas_call | solution.py:151
  61.8 1.9 %collective-permute-start.15 = (bf16[4,128,256]{2,1,0:T(8,128)(2,1)S(1)}, bf16[4,128,256]{2,1,0:T(8,128)(2,1)S(1)}, u32[]{:S(2)}, u32[]{:S(2)}) collective-permute-start(bf16[4,128,256]{2,1,0:T(8,128)(2,1)S(1)} %shard_map.63), channel_id=1, source_target_pairs={{0,8},{8,16},{16,24},{1,9},{9,17},{17,25},{2,10},{10,18},{18,26},{... | collective-permute-start | bytes 786440 | tf_op jit(solution)/shard_map/ppermute | solution.py:238
  63.7 0.7 collective-permute-start.16
  64.4 3.0 %collective-permute-done.13 = bf16[4,128,256]{2,1,0:T(8,128)(2,1)S(1)} collective-permute-done((bf16[4,128,256]{2,1,0:T(8,128)(2,1)S(1)}, bf16[4,128,256]{2,1,0:T(8,128)(2,1)S(1)}, u32[]{:S(2)}, u32[]{:S(2)}) %collective-permute-start.13) | collective-permute-done | bytes 262176 | tf_op jit(solution)/shard_map/ppermute | solution.py:238
  67.5 5.5 %collective-permute-done.15 = bf16[4,128,256]{2,1,0:T(8,128)(2,1)S(1)} collective-permute-done((bf16[4,128,256]{2,1,0:T(8,128)(2,1)S(1)}, bf16[4,128,256]{2,1,0:T(8,128)(2,1)S(1)}, u32[]{:S(2)}, u32[]{:S(2)}) %collective-permute-start.15) | collective-permute-done | bytes 262176 | tf_op jit(solution)/shard_map/ppermute | solution.py:238
  73.2 3.5 %collective-permute-start.18 = (bf16[3,128,256]{2,1,0:T(8,128)(2,1)S(1)}, bf16[3,128,256]{2,1,0:T(8,128)(2,1)S(1)}, u32[]{:S(2)}, u32[]{:S(2)}) collective-permute-start(bf16[3,128,256]{2,1,0:T(8,128)(2,1)S(1)} %pad_maximum_fusion.7), channel_id=1, source_target_pairs={{1,2},{2,1},{3,4},{4,3},{5,6},{6,5},{9,10},{10,9},{11,12},{12,11},... | collective-permute-start | bytes 589832 | tf_op jit(solution)/shard_map/ppermute | solution.py:202
  76.8 2.1 %shard_map.64 = (bf16[2,128,256]{2,1,0:T(8,128)(2,1)S(1)}, f32[4,128,256]{2,1,0:T(8,128)S(1)}) custom-call(bf16[4,128,256]{2,1,0:T(8,128)(2,1)S(1)} %fusion.15.p, bf16[4,128,256]{2,1,0:T(8,128)(2,1)S(1)} %fusion.14.q, bf16[6912,256]{1,0:T(8,128)(2,1)S(1)} %get-tuple-element.72.weights), custom_call_target="tpu_custom_call" | custom-call | flops 1 | bytes 1 | tf_op jit(solution)/shard_map/pallas_call | solution.py:151
  79.0 0.7 collective-permute-start.20
  79.6 0.8 collective-permute-done.18.far
  80.5 1.8 %shard_map.65 = (bf16[1,128,256]{2,1,0:T(8,128)(2,1)S(1)}, bf16[4,128,256]{2,1,0:T(8,128)(2,1)S(1)}, bf16[1,128,256]{2,1,0:T(8,128)(2,1)S(1)}) custom-call(s32[3]{0:T(128)S(1)} %add_convert_fusion.6.flags, bf16[4,128,256]{2,1,0:T(8,128)(2,1)S(1)} %fusion.15.p, bf16[2,128,256]{2,1,0:T(8,128)(2,1)S(1)} %get-tuple-element.96.inner, ...), custom_call_target="tpu_custom_call" | custom-call | flops 1 | bytes 1 | tf_op jit(solution)/shard_map/pallas_call | solution.py:151
  82.3 2.1 %collective-permute-start.19 = (bf16[4,128,256]{2,1,0:T(8,128)(2,1)S(1)}, bf16[4,128,256]{2,1,0:T(8,128)(2,1)S(1)}, u32[]{:S(2)}, u32[]{:S(2)}) collective-permute-start(bf16[4,128,256]{2,1,0:T(8,128)(2,1)S(1)} %get-tuple-element.98.first_mid), channel_id=1, source_target_pairs={{8,16},{16,24},{9,17},{17,25},{10,18},{18,26},{11,19},{19,27},{12,... | collective-permute-start | bytes 786440 | tf_op jit(solution)/shard_map/ppermute | solution.py:238
  84.4 2.1 %shard_map.66 = bf16[4,128,256]{2,1,0:T(8,128)(2,1)S(1)} custom-call(bf16[1,128,256]{2,1,0:T(8,128)(2,1)S(1)} %get-tuple-element.99.first_low, bf16[4,128,256]{2,1,0:T(8,128)(2,1)S(1)} %get-tuple-element.98.first_mid, bf16[1,128,256]{2,1,0:T(8,128)(2,1)S(1)} %get-tuple-element.100.first_high, bf16[4,128,256]{2,1,0:T(8,128)(2,1)S(1)} %fusion.14.q, ...), custom_call_target="tpu_custom_call" | custom-call | flops 1 | bytes 1 | tf_op jit(solution)/shard_map/pallas_call | solution.py:151
  86.5 1.9 %collective-permute-start.21 = (bf16[4,128,256]{2,1,0:T(8,128)(2,1)S(1)}, bf16[4,128,256]{2,1,0:T(8,128)(2,1)S(1)}, u32[]{:S(2)}, u32[]{:S(2)}) collective-permute-start(bf16[4,128,256]{2,1,0:T(8,128)(2,1)S(1)} %shard_map.66), channel_id=1, source_target_pairs={{8,16},{16,24},{9,17},{17,25},{10,18},{18,26},{11,19},{19,27},{12,... | collective-permute-start | bytes 786440 | tf_op jit(solution)/shard_map/ppermute | solution.py:238
  88.5 0.7 collective-permute-start.22
  89.2 2.6 %collective-permute-done.19 = bf16[4,128,256]{2,1,0:T(8,128)(2,1)S(1)} collective-permute-done((bf16[4,128,256]{2,1,0:T(8,128)(2,1)S(1)}, bf16[4,128,256]{2,1,0:T(8,128)(2,1)S(1)}, u32[]{:S(2)}, u32[]{:S(2)}) %collective-permute-start.19) | collective-permute-done | bytes 262176 | tf_op jit(solution)/shard_map/ppermute | solution.py:238
  91.9 5.8 %collective-permute-done.21 = bf16[4,128,256]{2,1,0:T(8,128)(2,1)S(1)} collective-permute-done((bf16[4,128,256]{2,1,0:T(8,128)(2,1)S(1)}, bf16[4,128,256]{2,1,0:T(8,128)(2,1)S(1)}, u32[]{:S(2)}, u32[]{:S(2)}) %collective-permute-start.21) | collective-permute-done | bytes 262176 | tf_op jit(solution)/shard_map/ppermute | solution.py:238
  97.9 3.8 %collective-permute-start.24 = (bf16[3,128,256]{2,1,0:T(8,128)(2,1)S(1)}, bf16[3,128,256]{2,1,0:T(8,128)(2,1)S(1)}, u32[]{:S(2)}, u32[]{:S(2)}) collective-permute-start(bf16[3,128,256]{2,1,0:T(8,128)(2,1)S(1)} %pad_maximum_fusion.9), channel_id=1, source_target_pairs={{1,2},{2,1},{3,4},{4,3},{5,6},{6,5},{9,10},{10,9},{11,12},{12,11},... | collective-permute-start | bytes 589832 | tf_op jit(solution)/shard_map/ppermute | solution.py:202
  101.8 0.3 collective-permute-start.23
  102.1 2.1 %shard_map.67 = (bf16[2,128,256]{2,1,0:T(8,128)(2,1)S(1)}, f32[4,128,256]{2,1,0:T(8,128)S(1)}) custom-call(bf16[4,128,256]{2,1,0:T(8,128)(2,1)S(1)} %fusion.13.p, bf16[4,128,256]{2,1,0:T(8,128)(2,1)S(1)} %fusion.12.q, bf16[6912,256]{1,0:T(8,128)(2,1)S(1)} %get-tuple-element.72.weights), custom_call_target="tpu_custom_call" | custom-call | flops 1 | bytes 1 | tf_op jit(solution)/shard_map/pallas_call | solution.py:151
  104.2 1.0 collective-permute-done.24.far
  105.2 1.8 %shard_map.68 = (bf16[1,128,256]{2,1,0:T(8,128)(2,1)S(1)}, bf16[4,128,256]{2,1,0:T(8,128)(2,1)S(1)}, bf16[1,128,256]{2,1,0:T(8,128)(2,1)S(1)}) custom-call(s32[3]{0:T(128)S(1)} %add_convert_fusion.6.flags, bf16[4,128,256]{2,1,0:T(8,128)(2,1)S(1)} %fusion.13.p, bf16[2,128,256]{2,1,0:T(8,128)(2,1)S(1)} %get-tuple-element.104.inner, ...), custom_call_target="tpu_custom_call" | custom-call | flops 1 | bytes 1 | tf_op jit(solution)/shard_map/pallas_call | solution.py:151
  107.0 2.8 %shard_map.69 = bf16[2,4,128,256]{3,2,1,0:T(8,128)(2,1)} custom-call(bf16[1,128,256]{2,1,0:T(8,128)(2,1)S(1)} %get-tuple-element.106.first_low, bf16[4,128,256]{2,1,0:T(8,128)(2,1)S(1)} %get-tuple-element.107.first_mid, bf16[1,128,256]{2,1,0:T(8,128)(2,1)S(1)} %get-tuple-element.108.first_high, bf16[4,128,256]{2,1,0:T(8,128)(2,1)S(1)} %fusion.12.q, ...), custom_call_target="tpu_custom_call" | custom-call | flops 1 | bytes 1 | tf_op jit(solution)/shard_map/pallas_call | solution.py:151
  (54 shorter events, 1.9 us)
Async XLA Ops:
  0.0 3.1 %copy-start.3 = (bf16[1,2,4,16,8,256]{5,4,3,2,1,0:T(8,128)(2,1)S(1)}, bf16[1,2,4,16,8,256]{5,4,3,2,1,0:T(8,128)(2,1)}, u32[]{:S(2)}) copy-start(bf16[1,2,4,16,8,256]{5,4,3,2,1,0:T(8,128)(2,1)} %param.6) | copy-start | bytes 1572868
  1.3 1.8 %collective-permute-start = (bf16[3,128,256]{2,1,0:T(8,128)(2,1)S(1)}, bf16[3,128,256]{2,1,0:T(8,128)(2,1)S(1)}, u32[]{:S(2)}, u32[]{:S(2)}) collective-permute-start(bf16[3,128,256]{2,1,0:T(8,128)(2,1)S(1)} %pad_maximum_fusion), channel_id=1, source_target_pairs={{0,1},{1,0},{2,3},{3,2},{4,5},{5,4},{6,7},{7,6},{8,9},{9,8},{10,11... | collective-permute-start | bytes 589832 | tf_op jit(solution)/shard_map/ppermute | solution.py:202
  3.1 15.9 %collective-permute-start.3 = (bf16[2,4,128,256]{3,2,1,0:T(8,128)(2,1)S(1)}, bf16[2,4,128,256]{3,2,1,0:T(8,128)(2,1)S(1)}, u32[]{:S(2)}, u32[]{:S(2)}) collective-permute-start(bf16[2,4,128,256]{3,2,1,0:T(8,128)(2,1)S(1)} %bitcast.63), channel_id=1, source_target_pairs={{0,24},{8,16},{1,25},{9,17},{2,26},{10,18},{3,27},{11,19},{4,28},{... | collective-permute-start | bytes 1572872 | tf_op jit(solution)/shard_map/ppermute | solution.py:238
  4.4 7.5 %collective-permute-start.1 = (bf16[3,128,256]{2,1,0:T(8,128)(2,1)S(1)}, bf16[3,128,256]{2,1,0:T(8,128)(2,1)S(1)}, u32[]{:S(2)}, u32[]{:S(2)}) collective-permute-start(bf16[3,128,256]{2,1,0:T(8,128)(2,1)S(1)} %pad_maximum_fusion.1), channel_id=1, source_target_pairs={{1,2},{2,1},{3,4},{4,3},{5,6},{6,5},{9,10},{10,9},{11,12},{12,11},... | collective-permute-start | bytes 589832 | tf_op jit(solution)/shard_map/ppermute | solution.py:202
  12.0 2.5 %copy-start = (bf16[1,3,3,3,256,256]{5,4,3,2,1,0:T(8,128)(2,1)S(1)}, bf16[1,3,3,3,256,256]{5,4,3,2,1,0:T(8,128)(2,1)}, u32[]{:S(2)}) copy-start(bf16[1,3,3,3,256,256]{5,4,3,2,1,0:T(8,128)(2,1)} %param.9) | copy-start | bytes 10616836
  13.8 10.7 %collective-permute-start.2 = (bf16[4,128,256]{2,1,0:T(8,128)(2,1)S(1)}, bf16[4,128,256]{2,1,0:T(8,128)(2,1)S(1)}, u32[]{:S(2)}, u32[]{:S(2)}) collective-permute-start(bf16[4,128,256]{2,1,0:T(8,128)(2,1)S(1)} %get-tuple-element.73.first_mid), channel_id=1, source_target_pairs={{0,8},{1,9},{2,10},{3,11},{4,12},{5,13},{6,14},{7,15}} | collective-permute-start | bytes 786440 | tf_op jit(solution)/shard_map/ppermute | solution.py:238
  14.5 4.6 %copy-start.1 = (bf16[3,2,4,16,8,256]{5,4,3,2,1,0:T(8,128)(2,1)S(1)}, bf16[3,2,4,16,8,256]{5,4,3,2,1,0:T(8,128)(2,1)}, u32[]{:S(2)}) copy-start(bf16[3,2,4,16,8,256]{5,4,3,2,1,0:T(8,128)(2,1)} %param.7) | copy-start | bytes 4718596
  14.5 4.5 %copy-start.2 = (bf16[1,2,4,16,8,256]{5,4,3,2,1,0:T(8,128)(2,1)S(1)}, bf16[1,2,4,16,8,256]{5,4,3,2,1,0:T(8,128)(2,1)}, u32[]{:S(2)}) copy-start(bf16[1,2,4,16,8,256]{5,4,3,2,1,0:T(8,128)(2,1)} %param.5) | copy-start | bytes 1572868
  19.4 7.9 %collective-permute-start.5 = (bf16[3,128,256]{2,1,0:T(8,128)(2,1)S(1)}, bf16[3,128,256]{2,1,0:T(8,128)(2,1)S(1)}, u32[]{:S(2)}, u32[]{:S(2)}) collective-permute-start(bf16[3,128,256]{2,1,0:T(8,128)(2,1)S(1)} %pad_maximum_fusion.3), channel_id=1, source_target_pairs={{1,2},{2,1},{3,4},{4,3},{5,6},{6,5},{9,10},{10,9},{11,12},{12,11},... | collective-permute-start | bytes 589832 | tf_op jit(solution)/shard_map/ppermute | solution.py:202
  23.7 3.6 %collective-permute-start.4 = (bf16[3,128,256]{2,1,0:T(8,128)(2,1)S(1)}, bf16[3,128,256]{2,1,0:T(8,128)(2,1)S(1)}, u32[]{:S(2)}, u32[]{:S(2)}) collective-permute-start(bf16[3,128,256]{2,1,0:T(8,128)(2,1)S(1)} %pad_maximum_fusion.2), channel_id=1, source_target_pairs={{0,1},{1,0},{2,3},{3,2},{4,5},{5,4},{6,7},{7,6},{8,9},{9,8},{10,11... | collective-permute-start | bytes 589832 | tf_op jit(solution)/shard_map/ppermute | solution.py:202
  23.8 13.1 %collective-permute-start.9 = (bf16[4,128,256]{2,1,0:T(8,128)(2,1)S(1)}, bf16[4,128,256]{2,1,0:T(8,128)(2,1)S(1)}, u32[]{:S(2)}, u32[]{:S(2)}) collective-permute-start(bf16[4,128,256]{2,1,0:T(8,128)(2,1)S(1)} %shard_map.57), channel_id=1, source_target_pairs={{0,8},{1,9},{2,10},{3,11},{4,12},{5,13},{6,14},{7,15}} | collective-permute-start | bytes 786440 | tf_op jit(solution)/shard_map/ppermute | solution.py:238
  24.5 13.1 %collective-permute-start.7 = (bf16[4,128,256]{2,1,0:T(8,128)(2,1)S(1)}, bf16[4,128,256]{2,1,0:T(8,128)(2,1)S(1)}, u32[]{:S(2)}, u32[]{:S(2)}) collective-permute-start(bf16[4,128,256]{2,1,0:T(8,128)(2,1)S(1)} %collective-permute-done.2), channel_id=1, source_target_pairs={{8,24},{9,25},{10,26},{11,27},{12,28},{13,29},{14,30},{15,31}} | collective-permute-start | bytes 786440 | tf_op jit(solution)/shard_map/ppermute | solution.py:238
  29.1 11.5 %collective-permute-start.6 = (bf16[4,128,256]{2,1,0:T(8,128)(2,1)S(1)}, bf16[4,128,256]{2,1,0:T(8,128)(2,1)S(1)}, u32[]{:S(2)}, u32[]{:S(2)}) collective-permute-start(bf16[4,128,256]{2,1,0:T(8,128)(2,1)S(1)} %get-tuple-element.81.first_mid), channel_id=1, source_target_pairs={{0,8},{8,16},{16,24},{1,9},{9,17},{17,25},{2,10},{10,18},{18,26},{... | collective-permute-start | bytes 786440 | tf_op jit(solution)/shard_map/ppermute | solution.py:238
  35.0 11.2 %collective-permute-start.8 = (bf16[4,128,256]{2,1,0:T(8,128)(2,1)S(1)}, bf16[4,128,256]{2,1,0:T(8,128)(2,1)S(1)}, u32[]{:S(2)}, u32[]{:S(2)}) collective-permute-start(bf16[4,128,256]{2,1,0:T(8,128)(2,1)S(1)} %shard_map.60), channel_id=1, source_target_pairs={{0,8},{8,16},{16,24},{1,9},{9,17},{17,25},{2,10},{10,18},{18,26},{... | collective-permute-start | bytes 786440 | tf_op jit(solution)/shard_map/ppermute | solution.py:238
  36.9 9.3 %collective-permute-start.10 = (bf16[4,128,256]{2,1,0:T(8,128)(2,1)S(1)}, bf16[4,128,256]{2,1,0:T(8,128)(2,1)S(1)}, u32[]{:S(2)}, u32[]{:S(2)}) collective-permute-start(bf16[4,128,256]{2,1,0:T(8,128)(2,1)S(1)} %collective-permute-done.9), channel_id=1, source_target_pairs={{8,24},{9,25},{10,26},{11,27},{12,28},{13,29},{14,30},{15,31}} | collective-permute-start | bytes 786440 | tf_op jit(solution)/shard_map/ppermute | solution.py:238
  46.4 8.6 %collective-permute-start.12 = (bf16[3,128,256]{2,1,0:T(8,128)(2,1)S(1)}, bf16[3,128,256]{2,1,0:T(8,128)(2,1)S(1)}, u32[]{:S(2)}, u32[]{:S(2)}) collective-permute-start(bf16[3,128,256]{2,1,0:T(8,128)(2,1)S(1)} %pad_maximum_fusion.5), channel_id=1, source_target_pairs={{1,2},{2,1},{3,4},{4,3},{5,6},{6,5},{9,10},{10,9},{11,12},{12,11},... | collective-permute-start | bytes 589832 | tf_op jit(solution)/shard_map/ppermute | solution.py:202
  51.8 3.1 %collective-permute-start.11 = (bf16[3,128,256]{2,1,0:T(8,128)(2,1)S(1)}, bf16[3,128,256]{2,1,0:T(8,128)(2,1)S(1)}, u32[]{:S(2)}, u32[]{:S(2)}) collective-permute-start(bf16[3,128,256]{2,1,0:T(8,128)(2,1)S(1)} %pad_maximum_fusion.4), channel_id=1, source_target_pairs={{0,1},{1,0},{2,3},{3,2},{4,5},{5,4},{6,7},{7,6},{8,9},{9,8},{10,11... | collective-permute-start | bytes 589832 | tf_op jit(solution)/shard_map/ppermute | solution.py:202
  54.1 10.3 %collective-permute-start.14 = (bf16[4,128,256]{2,1,0:T(8,128)(2,1)S(1)}, bf16[4,128,256]{2,1,0:T(8,128)(2,1)S(1)}, u32[]{:S(2)}, u32[]{:S(2)}) collective-permute-start(bf16[4,128,256]{2,1,0:T(8,128)(2,1)S(1)} %collective-permute-done.6), channel_id=1, source_target_pairs={{8,24},{9,25},{10,26},{11,27},{12,28},{13,29},{14,30},{15,31}} | collective-permute-start | bytes 786440 | tf_op jit(solution)/shard_map/ppermute | solution.py:238
  56.8 10.6 %collective-permute-start.13 = (bf16[4,128,256]{2,1,0:T(8,128)(2,1)S(1)}, bf16[4,128,256]{2,1,0:T(8,128)(2,1)S(1)}, u32[]{:S(2)}, u32[]{:S(2)}) collective-permute-start(bf16[4,128,256]{2,1,0:T(8,128)(2,1)S(1)} %get-tuple-element.90.first_mid), channel_id=1, source_target_pairs={{0,8},{8,16},{16,24},{1,9},{9,17},{17,25},{2,10},{10,18},{18,26},{... | collective-permute-start | bytes 786440 | tf_op jit(solution)/shard_map/ppermute | solution.py:238
  61.8 11.2 %collective-permute-start.15 = (bf16[4,128,256]{2,1,0:T(8,128)(2,1)S(1)}, bf16[4,128,256]{2,1,0:T(8,128)(2,1)S(1)}, u32[]{:S(2)}, u32[]{:S(2)}) collective-permute-start(bf16[4,128,256]{2,1,0:T(8,128)(2,1)S(1)} %shard_map.63), channel_id=1, source_target_pairs={{0,8},{8,16},{16,24},{1,9},{9,17},{17,25},{2,10},{10,18},{18,26},{... | collective-permute-start | bytes 786440 | tf_op jit(solution)/shard_map/ppermute | solution.py:238
  63.7 9.3 %collective-permute-start.16 = (bf16[4,128,256]{2,1,0:T(8,128)(2,1)S(1)}, bf16[4,128,256]{2,1,0:T(8,128)(2,1)S(1)}, u32[]{:S(2)}, u32[]{:S(2)}) collective-permute-start(bf16[4,128,256]{2,1,0:T(8,128)(2,1)S(1)} %collective-permute-done.8), channel_id=1, source_target_pairs={{8,24},{9,25},{10,26},{11,27},{12,28},{13,29},{14,30},{15,31}} | collective-permute-start | bytes 786440 | tf_op jit(solution)/shard_map/ppermute | solution.py:238
  73.2 7.3 %collective-permute-start.18 = (bf16[3,128,256]{2,1,0:T(8,128)(2,1)S(1)}, bf16[3,128,256]{2,1,0:T(8,128)(2,1)S(1)}, u32[]{:S(2)}, u32[]{:S(2)}) collective-permute-start(bf16[3,128,256]{2,1,0:T(8,128)(2,1)S(1)} %pad_maximum_fusion.7), channel_id=1, source_target_pairs={{1,2},{2,1},{3,4},{4,3},{5,6},{6,5},{9,10},{10,9},{11,12},{12,11},... | collective-permute-start | bytes 589832 | tf_op jit(solution)/shard_map/ppermute | solution.py:202
  76.7 3.7 %collective-permute-start.17 = (bf16[3,128,256]{2,1,0:T(8,128)(2,1)S(1)}, bf16[3,128,256]{2,1,0:T(8,128)(2,1)S(1)}, u32[]{:S(2)}, u32[]{:S(2)}) collective-permute-start(bf16[3,128,256]{2,1,0:T(8,128)(2,1)S(1)} %pad_maximum_fusion.6), channel_id=1, source_target_pairs={{0,1},{1,0},{2,3},{3,2},{4,5},{5,4},{6,7},{7,6},{8,9},{9,8},{10,11... | collective-permute-start | bytes 589832 | tf_op jit(solution)/shard_map/ppermute | solution.py:202
  79.0 10.2 %collective-permute-start.20 = (bf16[4,128,256]{2,1,0:T(8,128)(2,1)S(1)}, bf16[4,128,256]{2,1,0:T(8,128)(2,1)S(1)}, u32[]{:S(2)}, u32[]{:S(2)}) collective-permute-start(bf16[4,128,256]{2,1,0:T(8,128)(2,1)S(1)} %collective-permute-done.13), channel_id=1, source_target_pairs={{8,24},{9,25},{10,26},{11,27},{12,28},{13,29},{14,30},{15,31}} | collective-permute-start | bytes 786440 | tf_op jit(solution)/shard_map/ppermute | solution.py:238
  82.3 9.5 %collective-permute-start.19 = (bf16[4,128,256]{2,1,0:T(8,128)(2,1)S(1)}, bf16[4,128,256]{2,1,0:T(8,128)(2,1)S(1)}, u32[]{:S(2)}, u32[]{:S(2)}) collective-permute-start(bf16[4,128,256]{2,1,0:T(8,128)(2,1)S(1)} %get-tuple-element.98.first_mid), channel_id=1, source_target_pairs={{8,16},{16,24},{9,17},{17,25},{10,18},{18,26},{11,19},{19,27},{12,... | collective-permute-start | bytes 786440 | tf_op jit(solution)/shard_map/ppermute | solution.py:238
  86.5 11.2 %collective-permute-start.21 = (bf16[4,128,256]{2,1,0:T(8,128)(2,1)S(1)}, bf16[4,128,256]{2,1,0:T(8,128)(2,1)S(1)}, u32[]{:S(2)}, u32[]{:S(2)}) collective-permute-start(bf16[4,128,256]{2,1,0:T(8,128)(2,1)S(1)} %shard_map.66), channel_id=1, source_target_pairs={{8,16},{16,24},{9,17},{17,25},{10,18},{18,26},{11,19},{19,27},{12,... | collective-permute-start | bytes 786440 | tf_op jit(solution)/shard_map/ppermute | solution.py:238
  88.5 9.3 %collective-permute-start.22 = (bf16[4,128,256]{2,1,0:T(8,128)(2,1)S(1)}, bf16[4,128,256]{2,1,0:T(8,128)(2,1)S(1)}, u32[]{:S(2)}, u32[]{:S(2)}) collective-permute-start(bf16[4,128,256]{2,1,0:T(8,128)(2,1)S(1)} %collective-permute-done.15), channel_id=1, source_target_pairs={{8,24},{9,25},{10,26},{11,27},{12,28},{13,29},{14,30},{15,31}} | collective-permute-start | bytes 786440 | tf_op jit(solution)/shard_map/ppermute | solution.py:238
  97.9 7.3 %collective-permute-start.24 = (bf16[3,128,256]{2,1,0:T(8,128)(2,1)S(1)}, bf16[3,128,256]{2,1,0:T(8,128)(2,1)S(1)}, u32[]{:S(2)}, u32[]{:S(2)}) collective-permute-start(bf16[3,128,256]{2,1,0:T(8,128)(2,1)S(1)} %pad_maximum_fusion.9), channel_id=1, source_target_pairs={{1,2},{2,1},{3,4},{4,3},{5,6},{6,5},{9,10},{10,9},{11,12},{12,11},... | collective-permute-start | bytes 589832 | tf_op jit(solution)/shard_map/ppermute | solution.py:202
  101.8 3.5 %collective-permute-start.23 = (bf16[3,128,256]{2,1,0:T(8,128)(2,1)S(1)}, bf16[3,128,256]{2,1,0:T(8,128)(2,1)S(1)}, u32[]{:S(2)}, u32[]{:S(2)}) collective-permute-start(bf16[3,128,256]{2,1,0:T(8,128)(2,1)S(1)} %pad_maximum_fusion.8), channel_id=1, source_target_pairs={{0,1},{1,0},{2,3},{3,2},{4,5},{5,4},{6,7},{7,6},{8,9},{9,8},{10,11... | collective-permute-start | bytes 589832 | tf_op jit(solution)/shard_map/ppermute | solution.py:202
